TPU v7x, 32 devices: a whole 2x2x4 slice. The times are simulated.
32 devices in a mesh: grp: 4 (over y, x), seq: 4 (over z), rep: 2 (over core).
Axes of the slice: x: 2, y: 2, z: 4, core: 2. Of those that a mesh axis runs over, the one named last changes fastest.
Arguments:
- query_rows: bfloat16 [2, 4, 512, 2560], P('rep', 'grp', 'seq'), may hold values from -8 to 8
- key_rows: bfloat16 [2, 4, 512, 2560], P('rep', 'grp', 'seq'), may hold values from -8 to 8
- value_rows: bfloat16 [2, 4, 512, 2560], P('rep', 'grp', 'seq'), may hold values from -6 to 6
- view_frame: int32 [2, 4, 512], P('rep', 'grp', 'seq'), may hold values from 0 to 39, never falling along the last dimension, each value on 1 to 16 neighbouring positions
- control_row: int32 [2, 4, 512], P('rep', 'grp', 'seq'), may hold values from 0 to 511, as said below
- control_gate: float32 [2560], P('rep'), may hold values from 0.2 to 1.6
- out_grad: bfloat16 [2, 4, 512, 2560], P('rep', 'grp', 'seq'), may hold values from -6 to 6
Outputs:
- block_out: bfloat16 [2, 4, 512, 2560], P('rep', 'grp', 'seq')
- branch_grad: bfloat16 [2, 512, 2560], P('rep', 'seq')
Inputs may be any that keep to these rules, and one draw needn't show every extreme that they name: `view_frame`: values never fall along a sequence; value // 20 is the camera and value % 20 the frame; one value holds at most 16 positions. `control_row`: position t of a sequence takes a row r with r // 128 == t // 128.
All inputs are finite; a program needn't handle non-finite values.
Results may differ from a plain program's by a relative error of at most 0.0057.
Values may be sent and summed in bfloat16 or wider, within the bound.
No kernel may reach another device: no remote copies, remote signals or barrier semaphores. Data moves between devices by JAX's collectives and lax.ppermute only.
A program may use at most 64 MiB of HBM per device.

v0:
```python
import math

import jax
import jax.numpy as jnp
from jax import lax
from jax.sharding import PartitionSpec as P

HEADS = 32
DH = 80
FRAMES = 20


def shifted(block, axis, distance):
    devices = range(lax.axis_size(axis))
    route = [(i - distance, i) for i in devices if i - distance in devices]
    return lax.ppermute(block, axis, route)


def from_root(value, axis, source):
    kept = jnp.where(lax.axis_index(axis) == source, value, 0).astype(value.dtype)
    return lax.psum(kept, axis)


def attend(queries, keys_pad, values_pad, query_tag, key_tag, frame_count, block_rows):
    length = queries.shape[-1]
    factor = 1.0 / math.sqrt(queries.shape[1])

    def one_block(block_index):
        query_seg = query_tag - 1
        key_seg = key_tag - 1
        allowed = (
            (key_seg[None, :] >= 0)
            & (query_seg[:, None] // frame_count == key_seg[None, :] // frame_count)
            & (jnp.abs(query_seg[:, None] - key_seg[None, :]) <= 1)
        )
        scores = (
            jnp.einsum("hdq,hdk->hqk", queries, keys_pad, preferred_element_type=jnp.float32)
            * factor
        )
        scores = jnp.where(allowed[None], scores, -1e30)
        largest = jnp.max(scores, axis=-1, keepdims=True)
        powers = jnp.exp(scores - largest)
        totals = jnp.sum(powers, axis=-1, keepdims=True)
        weights = (powers / totals).astype(jnp.bfloat16)
        mixed_rows = jnp.einsum(
            "hqk,hdk->hdq", weights, values_pad, preferred_element_type=jnp.float32
        )
        return mixed_rows.astype(jnp.bfloat16)

    blocks = lax.map(one_block, jnp.arange(length // block_rows, dtype=jnp.int32))
    heads_count = queries.shape[0]
    return jnp.moveaxis(blocks, 0, 2).reshape(heads_count, queries.shape[1], length)


def local(query_rows, key_rows, value_rows, view_frame, control_row, control_gate, out_grad):
    queries = query_rows[0, 0]
    token_count = queries.shape[0]
    width = queries.shape[1]
    length = token_count * lax.axis_size("seq")
    reach = 2 * (length // 32)
    full_gate = lax.all_gather(control_gate, "rep", axis=0, tiled=True)
    tags = lax.all_gather(view_frame[0, 0] + 1, "seq", axis=0, tiled=True)
    shaped = (token_count, HEADS, DH)

    def head_major(rows_in):
        return rows_in.reshape(shaped).transpose(1, 2, 0)

    paired = jnp.stack((head_major(key_rows[0, 0]), head_major(value_rows[0, 0])), axis=0)
    hops = (reach + token_count - 1) // token_count
    lower_list = []
    upper_list = []
    moving_low = paired
    moving_high = paired
    for hop in range(hops):
        moving_low = shifted(moving_low, "seq", 1)
        moving_high = shifted(moving_high, "seq", -1)
        lower_list.insert(0, moving_low)
        upper_list.append(moving_high)
    window_rows = jnp.concatenate(lower_list + [paired] + upper_list, axis=3)
    position = lax.axis_index("seq")
    tag_pad = jnp.pad(tags, (hops * token_count, hops * token_count))
    key_tag = lax.dynamic_slice_in_dim(
        tag_pad, position * token_count, (2 * hops + 1) * token_count, 0
    )
    query_tag = lax.dynamic_slice_in_dim(tags, position * token_count, token_count, 0)
    group_size = 8
    group_count = HEADS // group_size
    window_len = window_rows.shape[3]
    grouped_query = head_major(queries).reshape(group_count, group_size, DH, token_count)
    grouped_key = window_rows[0].reshape(group_count, group_size, DH, window_len)
    grouped_value = window_rows[1].reshape(group_count, group_size, DH, window_len)

    def one_group(packed):
        group_query, group_key, group_value = packed
        return attend(group_query, group_key, group_value, query_tag, key_tag, FRAMES, token_count)

    attended = lax.map(one_group, (grouped_query, grouped_key, grouped_value))
    own_rows = (
        attended.reshape(HEADS, DH, token_count).transpose(2, 0, 1).reshape(token_count, width)
    )
    branch_rows = from_root(own_rows, "grp", 0)
    local_rows = control_row[0, 0] % token_count
    selector = (local_rows[:, None] == jnp.arange(token_count, dtype=jnp.int32)[None, :]).astype(
        jnp.bfloat16
    )
    relayed = jnp.dot(selector, branch_rows, preferred_element_type=jnp.float32)
    block_out = (own_rows.astype(jnp.float32) + full_gate * relayed).astype(jnp.bfloat16)
    grads = out_grad[0, 0]
    summed = jnp.dot(selector.T, grads, preferred_element_type=jnp.float32)
    own_term = jnp.where(lax.axis_index("grp") == 0, grads.astype(jnp.float32), 0.0)
    branch_sum = lax.psum(full_gate * summed + own_term, "grp")
    return (block_out[None, None], branch_sum.astype(jnp.bfloat16)[None])


def solution(mesh):
    placed = (
        P("rep", "grp", "seq", None),
        P("rep", "grp", "seq", None),
        P("rep", "grp", "seq", None),
        P("rep", "grp", "seq"),
        P("rep", "grp", "seq"),
        P("rep"),
        P("rep", "grp", "seq", None),
    )
    return jax.shard_map(
        local,
        mesh=mesh,
        in_specs=placed,
        out_specs=(P("rep", "grp", "seq", None), P("rep", "seq", None)),
        check_vma=False,
    )
```

profile of v0, /device:TPU:0, one launch (start us, length us, event | category | flops | bytes accessed | tf_op | source)
XLA Modules:
  0.0 142.3 jit_solution(12181802161598561534)
XLA Ops:
  7.2 1.5 %copy.17 = bf16[1,1,128,2560]{2,3,1,0:T(8,128)(2,1)S(1)} copy(bf16[1,1,128,2560]{3,2,1,0:T(8,128)(2,1)} %param.10) | data formatting | bytes 1310720 | tf_op args[1]
  8.7 0.3 copy.18
  9.1 1.2 pad_maximum_fusion.1
  10.3 6.0 %collective-permute-start = (bf16[2,32,80,128]{3,2,1,0:T(8,128)(2,1)}, bf16[2,32,80,128]{3,2,1,0:T(8,128)(2,1)}, u32[]{:S(2)}, u32[]{:S(2)}) collective-permute-start(bf16[2,32,80,128]{3,2,1,0:T(8,128)(2,1)} %pad_maximum_fusion.1), channel_id=1, source_target_pairs={{0,2},{2,4},{4,6},{1,3},{3,5},{5,7},{8,10},{10,12},{12,14},{9,11},... | collective-permute-start | bytes 3932168 | tf_op jit(solution)/shard_map/ppermute | solution.py:16
  16.3 1.3 collective-permute-start.1
  17.6 1.1 copy.19
  18.7 1.8 %all-gather.1 = f32[2,1,1280]{2,1,0:T(1,128)S(1)} all-gather(f32[1,1,1280]{2,1,0:T(1,128)S(1)} %reshape.178), channel_id=1, replica_groups=mesh['grp'=4,'seq'=4,'rep'=2] {'rep'}, dimensions={0}, use_global_device_ids=true | all-gather | bytes 15360 | tf_op jit(solution)/shard_map/all_gather | solution.py:61
  20.6 0.4 fusion.45
  21.0 29.8 %all-gather = s32[1,1,512]{2,1,0:T(1,128)S(1)} all-gather(s32[1,1,128]{2,1,0:T(1,128)S(1)} %broadcast_add_fusion.2), channel_id=2, replica_groups=mesh['grp'=4,'seq'=4,'rep'=2] {'seq'}, dimensions={2}, use_global_device_ids=true | all-gather | bytes 2560 | tf_op jit(solution)/shard_map/all_gather | solution.py:62
  50.9 2.0 %pad_maximum_fusion = bf16[2,32,80,384]{3,2,1,0:T(8,128)(2,1)S(1)} fusion(bf16[2,32,80,128]{3,2,1,0:T(8,128)(2,1)} %collective-permute-done.1, bf16[1,32,80,128]{3,2,1,0:T(8,128)(2,1)S(1)} %bitcast.97, bf16[1,32,80,128]{3,2,1,0:T(8,128)(2,1)S(1)} %bitcast.95, bf16[2,32,80,128]{3,2,1,0:T(8,128)(2,1)} %collective-permute-done), kind=kLoop, calls=%fused_computation.35 | loop fusion | flops 15728640 | bytes 7864320 | tf_op jit(solution)/shard_map/concatenate | solution.py:79
  52.9 1.7 %fusion.58 = (bf16[1,32,80,384]{3,2,1,0:T(8,128)(2,1)S(1)}, bf16[1,32,80,384]{3,2,1,0:T(8,128)(2,1)}) fusion(bf16[2,32,80,384]{3,2,1,0:T(8,128)(2,1)S(1)} %pad_maximum_fusion), kind=kLoop, calls=%fused_computation.58 | loop fusion | bytes 7864320 | tf_op jit(solution)/shard_map/slice | solution.py:90
  54.6 18.6 %while.18 = (s32[]{:T(128)}, bf16[4,8,80,128]{3,2,1,0:T(8,128)(2,1)}, bf16[4,8,80,384]{3,2,1,0:T(8,128)(2,1)}, s32[384]{0:T(512)S(1)}, s32[128]{0:T(128)S(1)}, /...) while((s32[]{:T(128)}, bf16[4,8,80,128]{3,2,1,0:T(8,128)(2,1)}, ...), condition=%wide.region_3.4_spmd.clone, body=%wide.region_0.3_spmd.sunk.clone | while | flops 192666624 | bytes 2137421 | solution.py:97
  54.8 1.7 %fusion.82 = f32[8,128]{1,0:T(8,128)S(1)} fusion(pred[128,384]{1,0:T(8,128)(4,1)S(1)} %fusion.81, bf16[4,8,80,384]{3,2,1,0:T(8,128)(2,1)S(1)} %get-tuple-element.251, s32[]{:T(128)} %get-tuple-element.238, bf16[4,8,80,128]{3,2,1,0:T(8,128)(2,1)} %get-tuple-element.250), kind=kOutput, calls=%fused_computation.57.clone.1.clone | convolution fusion | flops 64487808 | bytes 709632 | tf_op jit(solution)/shard_map/while/body/eval_jaxpr/while/body/eval_jaxpr/sub | solution.py:42
  56.5 2.8 %fusion.83 = bf16[4,8,80,128]{3,2,1,0:T(8,128)(2,1)} fusion(bf16[4,8,80,128]{3,2,1,0:T(8,128)(2,1)} %get-tuple-element.239, s32[]{:T(128)} %get-tuple-element.238, f32[8,128]{1,0:T(8,128)S(1)} %fusion.82, bf16[4,8,80,384]{3,2,1,0:T(8,128)(2,1)} %get-tuple-element.247, pred[128,384]{1,0:T(8,128)(4,1)S(1)} %fusion.81, ...), kind=kOutput, calls=%fused_computation.7.clone.1.clone | convolution fusion | flops 127878528 | bytes 1366016 | tf_op jit(solution)/shard_map/while/body/eval_jaxpr/while/body/eval_jaxpr/hqk,hdk->hdq/dot_general | solution.py:45
  59.4 1.7 %fusion.82 = f32[8,128]{1,0:T(8,128)S(1)} fusion(pred[128,384]{1,0:T(8,128)(4,1)S(1)} %fusion.81, bf16[4,8,80,384]{3,2,1,0:T(8,128)(2,1)S(1)} %get-tuple-element.251, s32[]{:T(128)} %get-tuple-element.238, bf16[4,8,80,128]{3,2,1,0:T(8,128)(2,1)} %get-tuple-element.250), kind=kOutput, calls=%fused_computation.57.clone.1.clone | convolution fusion | flops 64487808 | bytes 709632 | tf_op jit(solution)/shard_map/while/body/eval_jaxpr/while/body/eval_jaxpr/sub | solution.py:42
  61.1 2.8 %fusion.83 = bf16[4,8,80,128]{3,2,1,0:T(8,128)(2,1)} fusion(bf16[4,8,80,128]{3,2,1,0:T(8,128)(2,1)} %get-tuple-element.239, s32[]{:T(128)} %get-tuple-element.238, f32[8,128]{1,0:T(8,128)S(1)} %fusion.82, bf16[4,8,80,384]{3,2,1,0:T(8,128)(2,1)} %get-tuple-element.247, pred[128,384]{1,0:T(8,128)(4,1)S(1)} %fusion.81, ...), kind=kOutput, calls=%fused_computation.7.clone.1.clone | convolution fusion | flops 127878528 | bytes 1366016 | tf_op jit(solution)/shard_map/while/body/eval_jaxpr/while/body/eval_jaxpr/hqk,hdk->hdq/dot_general | solution.py:45
  64.1 1.7 %fusion.82 = f32[8,128]{1,0:T(8,128)S(1)} fusion(pred[128,384]{1,0:T(8,128)(4,1)S(1)} %fusion.81, bf16[4,8,80,384]{3,2,1,0:T(8,128)(2,1)S(1)} %get-tuple-element.251, s32[]{:T(128)} %get-tuple-element.238, bf16[4,8,80,128]{3,2,1,0:T(8,128)(2,1)} %get-tuple-element.250), kind=kOutput, calls=%fused_computation.57.clone.1.clone | convolution fusion | flops 64487808 | bytes 709632 | tf_op jit(solution)/shard_map/while/body/eval_jaxpr/while/body/eval_jaxpr/sub | solution.py:42
  65.8 2.8 %fusion.83 = bf16[4,8,80,128]{3,2,1,0:T(8,128)(2,1)} fusion(bf16[4,8,80,128]{3,2,1,0:T(8,128)(2,1)} %get-tuple-element.239, s32[]{:T(128)} %get-tuple-element.238, f32[8,128]{1,0:T(8,128)S(1)} %fusion.82, bf16[4,8,80,384]{3,2,1,0:T(8,128)(2,1)} %get-tuple-element.247, pred[128,384]{1,0:T(8,128)(4,1)S(1)} %fusion.81, ...), kind=kOutput, calls=%fused_computation.7.clone.1.clone | convolution fusion | flops 127878528 | bytes 1366016 | tf_op jit(solution)/shard_map/while/body/eval_jaxpr/while/body/eval_jaxpr/hqk,hdk->hdq/dot_general | solution.py:45
  68.7 1.7 %fusion.82 = f32[8,128]{1,0:T(8,128)S(1)} fusion(pred[128,384]{1,0:T(8,128)(4,1)S(1)} %fusion.81, bf16[4,8,80,384]{3,2,1,0:T(8,128)(2,1)S(1)} %get-tuple-element.251, s32[]{:T(128)} %get-tuple-element.238, bf16[4,8,80,128]{3,2,1,0:T(8,128)(2,1)} %get-tuple-element.250), kind=kOutput, calls=%fused_computation.57.clone.1.clone | convolution fusion | flops 64487808 | bytes 709632 | tf_op jit(solution)/shard_map/while/body/eval_jaxpr/while/body/eval_jaxpr/sub | solution.py:42
  70.4 2.8 %fusion.83 = bf16[4,8,80,128]{3,2,1,0:T(8,128)(2,1)} fusion(bf16[4,8,80,128]{3,2,1,0:T(8,128)(2,1)} %get-tuple-element.239, s32[]{:T(128)} %get-tuple-element.238, f32[8,128]{1,0:T(8,128)S(1)} %fusion.82, bf16[4,8,80,384]{3,2,1,0:T(8,128)(2,1)} %get-tuple-element.247, pred[128,384]{1,0:T(8,128)(4,1)S(1)} %fusion.81, ...), kind=kOutput, calls=%fused_computation.7.clone.1.clone | convolution fusion | flops 127878528 | bytes 1366016 | tf_op jit(solution)/shard_map/while/body/eval_jaxpr/while/body/eval_jaxpr/hqk,hdk->hdq/dot_general | solution.py:45
  73.2 2.1 %broadcast_select_fusion = (bf16[4,8,80,128]{3,2,1,0:T(8,128)(2,1)}, f32[32,80,128]{2,1,0:T(8,128)S(1)}) fusion(bf16[4,8,80,128]{3,2,1,0:T(8,128)(2,1)} %get-tuple-element.137, pred[]{:T(512)S(6)} %eq.50), kind=kLoop, calls=%fused_computation.46 | loop fusion | flops 655360 | bytes 2621441 | tf_op jit(solution)/shard_map/jit(_where)/select_n | solution.py:20
  75.2 57.5 %all-reduce.5 = bf16[128,2560]{1,0:T(8,128)(2,1)} all-reduce(f32[128,2560]{1,0:T(8,128)S(1)} %fusion.45), channel_id=1, replica_groups=mesh['grp'=4,'seq'=4,'rep'=2] {'grp'}, use_global_device_ids=true, to_apply=%region_5.6 | all-reduce | flops 327680 | bytes 1966080 | tf_op jit(solution)/shard_map/psum | solution.py:111
  132.7 0.4 copy.20
  133.1 2.3 %fusion.48 = bf16[1,1,128,2560]{3,2,1,0:T(8,128)(2,1)} fusion(f32[128,2560]{1,0:T(8,128)S(1)} %copy.20, bf16[128,2560]{0,1:T(8,128)(2,1)} %all-reduce.4.cloned.1.call-done, f32[2560]{0:T(1024)S(1)} %reshape.179, s32[128]{0:T(128)S(1)} %and_select_fusion.1), kind=kOutput, calls=%fused_computation.41 | convolution fusion | flops 84885504 | bytes 2632192 | tf_op jit(solution)/shard_map/dot_general | solution.py:106
  (41 shorter events, 1.0 us)
Async XLA Ops:
  7.2 1.5 %copy-start.1 = (bf16[1,1,128,2560]{3,2,1,0:T(8,128)(2,1)S(1)}, bf16[1,1,128,2560]{3,2,1,0:T(8,128)(2,1)}, u32[]{:S(2)}) copy-start(bf16[1,1,128,2560]{3,2,1,0:T(8,128)(2,1)} %param.11) | copy-start | bytes 1966084
  7.2 125.9 %all-reduce.4.cloned.1.call-start = ((), (), s32[]{:S(2)}) async-start(), calls=%async_computation | async-start | bytes 1310720 | tf_op jit(solution)/shard_map/psum | solution.py:21
  9.0 8.5 %copy-start.2 = (bf16[1,1,128,2560]{3,2,1,0:T(8,128)(2,1)S(1)}, bf16[1,1,128,2560]{3,2,1,0:T(8,128)(2,1)}, u32[]{:S(2)}) copy-start(bf16[1,1,128,2560]{3,2,1,0:T(8,128)(2,1)} %param.9) | copy-start | bytes 1966084
  9.0 9.6 %copy-start.3 = (f32[1280]{0:T(1024)S(1)}, f32[1280]{0:T(1024)}, u32[]{:S(2)}) copy-start(f32[1280]{0:T(1024)} %param.14) | copy-start | bytes 15364
  9.1 11.5 %copy-start.4 = (s32[1,1,128]{2,1,0:T(1,128)S(1)}, s32[1,1,128]{2,1,0:T(1,128)}, u32[]{:S(2)}) copy-start(s32[1,1,128]{2,1,0:T(1,128)} %param.13) | copy-start | bytes 1540
  9.1 11.5 %copy-start = (bf16[1,1,128,2560]{3,2,1,0:T(8,128)(2,1)S(1)}, bf16[1,1,128,2560]{3,2,1,0:T(8,128)(2,1)}, u32[]{:S(2)}) copy-start(bf16[1,1,128,2560]{3,2,1,0:T(8,128)(2,1)} %param.15) | copy-start | bytes 1966084
  10.3 40.7 %collective-permute-start = (bf16[2,32,80,128]{3,2,1,0:T(8,128)(2,1)}, bf16[2,32,80,128]{3,2,1,0:T(8,128)(2,1)}, u32[]{:S(2)}, u32[]{:S(2)}) collective-permute-start(bf16[2,32,80,128]{3,2,1,0:T(8,128)(2,1)} %pad_maximum_fusion.1), channel_id=1, source_target_pairs={{0,2},{2,4},{4,6},{1,3},{3,5},{5,7},{8,10},{10,12},{12,14},{9,11},... | collective-permute-start | bytes 3932168 | tf_op jit(solution)/shard_map/ppermute | solution.py:16
  16.3 34.7 %collective-permute-start.1 = (bf16[2,32,80,128]{3,2,1,0:T(8,128)(2,1)}, bf16[2,32,80,128]{3,2,1,0:T(8,128)(2,1)}, u32[]{:S(2)}, u32[]{:S(2)}) collective-permute-start(bf16[2,32,80,128]{3,2,1,0:T(8,128)(2,1)} %pad_maximum_fusion.1), channel_id=1, source_target_pairs={{2,0},{4,2},{6,4},{3,1},{5,3},{7,5},{10,8},{12,10},{14,12},{11,9},... | collective-permute-start | bytes 3932168 | tf_op jit(solution)/shard_map/ppermute | solution.py:16
  17.6 3.4 %copy-start.5 = (s32[1,1,128]{2,1,0:T(1,128)S(1)}, s32[1,1,128]{2,1,0:T(1,128)}, u32[]{:S(2)}) copy-start(s32[1,1,128]{2,1,0:T(1,128)} %param.12) | copy-start | bytes 1540
Sparse Core Ops, SparseCore 0:
  75.3 54.1 all-reduce.3
where the time goes:
time: 143 us; the launch traced here: 142 us
  blocking collectives  89.1 us (62%)
  matrix products  20.5 us (14%)
  between operations  14.2 us (10%)
  starting transfers between devices  7.33 us (5%)
  other arithmetic  5.98 us (4%)
  local copies, waits for them, and re-layouts  5.07 us (4%)
    psum x1, blocking collectives, local(): branch_sum = lax.psum(full_gate * summed + own_term, 'grp')  57.5 us
    all_gather x1, blocking collectives, local(): tags = lax.all_gather(view_frame[0, 0] + 1, 'seq', axis=0, tiled=True)  29.8 us
    dot_general x4, matrix products, one_block(): jnp.einsum('hqk,hdk->hdq', weights, values_pad, preferred_element_type=jn...  11 us
    ppermute x2, starting transfers between devices, shifted(): return lax.ppermute(block, axis, route)  7.29 us
    sub x4, matrix products, one_block(): powers = jnp.exp(scores - largest)  6.73 us
    unnamed x17, local copies, waits for them, and re-layouts  2.92 us
  transfers between devices with their start and end apart: 3, of which 0 were waited for; matrix products, arithmetic and copies ran while one was open for 1% of the time, Pallas kernels for 0%

commit v1 on v0

v1 whole, which is shorter than its diff:
```python
import functools
import math

import jax
import jax.numpy as jnp
from jax import lax
from jax.experimental import pallas as pl
from jax.experimental.pallas import tpu as pltpu
from jax.sharding import PartitionSpec as P

HEADS = 32
DH = 80
FRAMES = 20
LANES = 128
VMEM_LIMIT = 48 * 1024 * 1024


def shifted(block, axis, distance):
    devices = range(lax.axis_size(axis))
    route = [(i - distance, i) for i in devices if i - distance in devices]
    return lax.ppermute(block, axis, route)


def lane_windows(heads):
    windows = []
    for head in range(heads):
        first, last = head * DH, (head + 1) * DH
        if windows and last <= windows[-1][0] + 2 * LANES:
            windows[-1][1].append(head)
        else:
            windows.append((first // LANES * LANES, [head]))
    out = []
    for start, members in windows:
        start = min(start, heads * DH - 2 * LANES)
        out.append((start, members))
    return out


def attend_kernel(hops, block_rows, reach, *refs):
    q_ref, k_ref, v_ref = refs[:3]
    lows = refs[3 : 3 + hops]
    highs = refs[3 + hops : 3 + 2 * hops]
    code_ref, window_code_ref, out_ref, keys, values, mask = refs[3 + 2 * hops :]
    tokens, width = q_ref.shape
    span = block_rows + 2 * reach
    blocks = tokens // block_rows
    factor = math.log2(math.e) / math.sqrt(DH)

    @pl.when(pl.program_id(0) == 0)
    def _():
        column = jnp.broadcast_to(code_ref[...], (tokens, tokens)).T
        for b in range(blocks):
            row = window_code_ref[:, pl.ds(b * block_rows, span)]
            mine = column[b * block_rows : (b + 1) * block_rows, :1]
            near = jnp.abs(mine - row) <= 1.5
            mask[b] = jnp.where(near, 0.0, -1e30)

    at = 0
    for piece in (*lows, None, *highs):
        if piece is None:
            keys[pl.ds(at, tokens), :] = k_ref[...]
            values[pl.ds(at, tokens), :] = v_ref[...]
            at += tokens
        else:
            rows = piece.shape[1]
            keys[pl.ds(at, rows), :] = piece[0]
            values[pl.ds(at, rows), :] = piece[1]
            at += rows

    for b in range(blocks):
        bias = mask[b]
        top = b * block_rows
        for start, members in lane_windows(width // DH):
            wide = slice(start, start + 2 * LANES)
            lane = lax.broadcasted_iota(jnp.int32, (block_rows, 2 * LANES), 1) + start
            inside = [(lane >= h * DH) & (lane < (h + 1) * DH) for h in members]
            query = q_ref[pl.ds(top, block_rows), wide]
            picked = [jnp.where(m, query, jnp.zeros_like(query)) for m in inside]
            key = keys[pl.ds(top, span), wide]
            value = values[pl.ds(top, span), wide]
            scores = lax.dot_general(
                jnp.concatenate(picked, axis=0),
                key,
                (((1,), (1,)), ((), ())),
                preferred_element_type=jnp.float32,
            )
            powers = []
            totals = []
            for n in range(len(members)):
                part = scores[n * block_rows : (n + 1) * block_rows] + bias
                largest = jnp.max(part, axis=-1, keepdims=True)
                power = jnp.exp2((part - largest) * factor)
                totals.append(jnp.sum(power, axis=-1, keepdims=True))
                powers.append(power.astype(jnp.bfloat16))
            mixed = jnp.dot(
                jnp.concatenate(powers, axis=0), value, preferred_element_type=jnp.float32
            )
            merged = mixed[:block_rows] / totals[0]
            for n in range(1, len(members)):
                merged = jnp.where(
                    inside[n], mixed[n * block_rows : (n + 1) * block_rows] / totals[n], merged
                )
            first, last = members[0] * DH, (members[-1] + 1) * DH
            for tile in range(2):
                low = start + tile * LANES
                lanes = slice(low, low + LANES)
                piece = merged[:, tile * LANES : (tile + 1) * LANES].astype(jnp.bfloat16)
                if first > low:
                    before = out_ref[pl.ds(top, block_rows), lanes]
                    piece = jnp.where(lane[:, tile * LANES : (tile + 1) * LANES] >= first, piece, before)
                out_ref[pl.ds(top, block_rows), lanes] = piece


def attend(queries, keys, values, lows, highs, code, window_code, reach):
    tokens, width = queries.shape
    period = math.lcm(DH, LANES)
    block_rows = tokens
    for rows in range(64, tokens, 16):
        if tokens % rows == 0 and (rows + 2 * reach) % LANES == 0:
            block_rows = rows
            break
    span = block_rows + 2 * reach
    window = tokens + 2 * reach
    rows_spec = pl.BlockSpec((tokens, period), lambda g: (0, g))
    pair_specs = [pl.BlockSpec((2, p.shape[1], period), lambda g: (0, 0, g)) for p in (*lows, *highs)]
    whole = lambda a: pl.BlockSpec(a.shape, lambda g: (0, 0))
    return pl.pallas_call(
        functools.partial(attend_kernel, len(lows), block_rows, reach),
        grid=(width // period,),
        in_specs=[rows_spec] * 3 + pair_specs + [whole(code), whole(window_code)],
        out_specs=rows_spec,
        out_shape=jax.ShapeDtypeStruct((tokens, width), jnp.bfloat16),
        scratch_shapes=[
            pltpu.VMEM((window, period), jnp.bfloat16),
            pltpu.VMEM((window, period), jnp.bfloat16),
            pltpu.VMEM((tokens // block_rows, block_rows, span), jnp.float32),
        ],
        compiler_params=pltpu.CompilerParams(vmem_limit_bytes=VMEM_LIMIT),
        cost_estimate=pl.CostEstimate(
            flops=HEADS * tokens * span * 2 * LANES * 4,
            bytes_accessed=12 * tokens * width,
            transcendentals=HEADS * tokens * span,
        ),
        name="attend",
    )(queries, keys, values, *lows, *highs, code, window_code)


def term_kernel(half, row_ref, root_ref, grad_ref, gate_ref, first_ref, second_ref):
    tokens = grad_ref.shape[0]
    wanted = lax.broadcasted_iota(jnp.int32, (tokens, tokens), 0)
    selector = jnp.where(wanted == row_ref[...], 1.0, 0.0).astype(jnp.bfloat16)
    grads = grad_ref[...]
    summed = jnp.dot(selector, grads, preferred_element_type=jnp.float32)
    term = gate_ref[...] * summed + root_ref[0] * grads.astype(jnp.float32)
    term = term.astype(jnp.bfloat16)
    first_ref[...] = term[:, :half]
    second_ref[...] = term[:, half:]


def grad_terms(local_rows, root, grads, gate):
    tokens, width = grads.shape
    half = width // 2
    vmem = pl.BlockSpec(memory_space=pltpu.VMEM)
    return pl.pallas_call(
        functools.partial(term_kernel, half),
        in_specs=[vmem, pl.BlockSpec(memory_space=pltpu.SMEM), vmem, vmem],
        out_specs=[vmem, vmem],
        out_shape=[jax.ShapeDtypeStruct((tokens, half), jnp.bfloat16)] * 2,
        compiler_params=pltpu.CompilerParams(vmem_limit_bytes=VMEM_LIMIT),
        cost_estimate=pl.CostEstimate(
            flops=2 * tokens * tokens * width, bytes_accessed=4 * tokens * width, transcendentals=0
        ),
        name="grad_terms",
    )(local_rows, root, grads, gate)


def add_kernel(a_ref, b_ref, c_ref, d_ref, first_ref, second_ref):
    first_ref[...] = (a_ref[...].astype(jnp.float32) + b_ref[...].astype(jnp.float32)).astype(
        jnp.bfloat16
    )
    second_ref[...] = (c_ref[...].astype(jnp.float32) + d_ref[...].astype(jnp.float32)).astype(
        jnp.bfloat16
    )


def add_pairs(a, b, c, d):
    vmem = pl.BlockSpec(memory_space=pltpu.VMEM)
    return pl.pallas_call(
        add_kernel,
        in_specs=[vmem] * 4,
        out_specs=[vmem] * 2,
        out_shape=[jax.ShapeDtypeStruct(a.shape, a.dtype), jax.ShapeDtypeStruct(c.shape, c.dtype)],
        compiler_params=pltpu.CompilerParams(vmem_limit_bytes=VMEM_LIMIT),
        cost_estimate=pl.CostEstimate(flops=2 * a.size, bytes_accessed=12 * a.size, transcendentals=0),
        name="add_pairs",
    )(a, b, c, d)


def join_kernel(a_ref, b_ref, c_ref, d_ref, out_ref):
    half = a_ref.shape[1]
    out_ref[:, :half] = (a_ref[...].astype(jnp.float32) + b_ref[...].astype(jnp.float32)).astype(
        jnp.bfloat16
    )
    out_ref[:, half:] = (c_ref[...].astype(jnp.float32) + d_ref[...].astype(jnp.float32)).astype(
        jnp.bfloat16
    )


def join_pairs(a, b, c, d):
    vmem = pl.BlockSpec(memory_space=pltpu.VMEM)
    return pl.pallas_call(
        join_kernel,
        in_specs=[vmem] * 4,
        out_specs=vmem,
        out_shape=jax.ShapeDtypeStruct((a.shape[0], 2 * a.shape[1]), a.dtype),
        compiler_params=pltpu.CompilerParams(vmem_limit_bytes=VMEM_LIMIT),
        cost_estimate=pl.CostEstimate(flops=2 * a.size, bytes_accessed=12 * a.size, transcendentals=0),
        name="join_pairs",
    )(a, b, c, d)


def relay_kernel(half, row_ref, own_ref, gate_ref, first_ref, second_ref, out_ref):
    tokens = own_ref.shape[0]
    wanted = lax.broadcasted_iota(jnp.int32, (tokens, tokens), 0)
    selector = jnp.where(wanted == row_ref[...], 1.0, 0.0).T.astype(jnp.bfloat16)
    for lanes, branch_ref in ((slice(0, half), first_ref), (slice(half, 2 * half), second_ref)):
        relayed = jnp.dot(selector, branch_ref[...], preferred_element_type=jnp.float32)
        out_ref[:, lanes] = (
            own_ref[:, lanes].astype(jnp.float32) + gate_ref[:, lanes] * relayed
        ).astype(jnp.bfloat16)


def relay(local_rows, own, gate, first, second):
    tokens, width = own.shape
    half = width // 2
    vmem = pl.BlockSpec(memory_space=pltpu.VMEM)
    return pl.pallas_call(
        functools.partial(relay_kernel, half),
        in_specs=[vmem] * 5,
        out_specs=vmem,
        out_shape=jax.ShapeDtypeStruct((tokens, width), jnp.bfloat16),
        compiler_params=pltpu.CompilerParams(vmem_limit_bytes=VMEM_LIMIT),
        cost_estimate=pl.CostEstimate(
            flops=2 * tokens * tokens * width, bytes_accessed=6 * tokens * width, transcendentals=0
        ),
        name="relay",
    )(local_rows, own, gate, first, second)


def whole_gate(gate):
    ranks = lax.axis_size("rep")
    if ranks != 2:
        return lax.all_gather(gate, "rep", axis=0, tiled=True)
    other = lax.ppermute(gate, "rep", [(0, 1), (1, 0)])
    first = lax.axis_index("rep") == 0
    return jnp.concatenate([jnp.where(first, gate, other), jnp.where(first, other, gate)])


def local(query_rows, key_rows, value_rows, view_frame, control_row, control_gate, out_grad):
    queries, keys, values = query_rows[0, 0], key_rows[0, 0], value_rows[0, 0]
    tokens, width = queries.shape
    length = tokens * lax.axis_size("seq")
    reach = 2 * (length // 32)
    hops = (reach + tokens - 1) // tokens
    half = width // 2
    group = lax.axis_index("grp")

    gate = whole_gate(control_gate)[None]
    tag = view_frame[0, 0]
    code = (tag + 8 * (tag // FRAMES) + 16).astype(jnp.float32)[None]
    lows, highs, low_codes, high_codes = [], [], [], []
    for hop in range(1, hops + 1):
        rows = min(tokens, reach - (hop - 1) * tokens)
        tail = jnp.stack((keys[tokens - rows :], values[tokens - rows :]))
        head = jnp.stack((keys[:rows], values[:rows]))
        lows.insert(0, shifted(tail, "seq", hop))
        highs.append(shifted(head, "seq", -hop))
        low_codes.insert(0, shifted(code[:, tokens - rows :], "seq", hop))
        high_codes.append(shifted(code[:, :rows], "seq", -hop))
    window_code = jnp.concatenate(low_codes + [code] + high_codes, axis=1)

    local_rows = (control_row[0] % tokens).astype(jnp.int32)
    root = (group == 0).astype(jnp.float32)[None]
    term_a, term_b = grad_terms(local_rows, root, out_grad[0, 0], gate)
    swap_x = [(0, 1), (1, 0), (2, 3), (3, 2)]
    swap_y = [(0, 2), (2, 0), (1, 3), (3, 1)]
    sum_a, sum_b = add_pairs(
        term_a, lax.ppermute(term_a, "grp", swap_x), term_b, lax.ppermute(term_b, "grp", swap_y)
    )
    branch_grad = join_pairs(
        sum_a, lax.ppermute(sum_a, "grp", swap_y), sum_b, lax.ppermute(sum_b, "grp", swap_x)
    )

    own = attend(queries, keys, values, lows, highs, code, window_code, reach)
    own_a, own_b = own[:, :half], own[:, half:]
    got_a = lax.ppermute(own_a, "grp", [(0, 1)])
    got_b = lax.ppermute(own_b, "grp", [(0, 2)])
    hold_a = jnp.where(group == 1, got_a, own_a)
    hold_b = jnp.where(group == 2, got_b, own_b)
    last_a = lax.ppermute(hold_a, "grp", [(0, 2), (1, 3)])
    last_b = lax.ppermute(hold_b, "grp", [(0, 1), (2, 3)])
    branch_a = jnp.where(group <= 1, hold_a, last_a)
    branch_b = jnp.where((group == 0) | (group == 2), hold_b, last_b)
    block_out = relay(local_rows, own, gate, branch_a, branch_b)
    return (block_out[None, None], branch_grad[None])


def solution(mesh):
    placed = (
        P("rep", "grp", "seq", None),
        P("rep", "grp", "seq", None),
        P("rep", "grp", "seq", None),
        P("rep", "grp", "seq"),
        P("rep", "grp", "seq"),
        P("rep"),
        P("rep", "grp", "seq", None),
    )
    return jax.shard_map(
        local,
        mesh=mesh,
        in_specs=placed,
        out_specs=(P("rep", "grp", "seq", None), P("rep", "seq", None)),
        check_vma=False,
    )
```

time: 143 us -> 54.9 us (0.38)
  blocking collectives: 89.1 us -> 0 us
  matrix products: 20.5 us -> 0 us
  starting transfers between devices: 7.33 us -> 27.1 us
  between operations: 14.2 us -> 0.93 us
  waiting for transfers between devices: 0.04 us -> 12.7 us
  Pallas kernels: 0 us -> 10.6 us
  other arithmetic: 5.98 us -> 1.76 us
  local copies, waits for them, and re-layouts: 5.07 us -> 1.43 us
    psum x1 -> x0, blocking collectives: 57.5 us -> none  [local(): branch_sum = lax.psum(full_gate * summed + own_term, 'grp')]
    all_gather x2 -> x0, blocking collectives: 31.6 us -> none  [the longest x1 29.8 us: local(): tags = lax.all_gather(view_frame[0, 0] + 1, 'seq', axis=0, tiled=True)]
    ppermute x0 -> x9, starting transfers between devices: none -> 14.5 us  [the longest x1 3.7 us: local(): last_b = lax.ppermute(hold_b, 'grp', [(0, 1), (2, 3)])]
    dot_general x6 -> x0, matrix products: 13.8 us -> none  [the longest x4 11 us: one_block(): jnp.einsum('hqk,hdk->hdq', weights, values_pad, preferred_element_type=jn...]
    pallas_call x0 -> x5, Pallas kernels: none -> 10.6 us  [the longest x1 5.82 us: attend(): pl.pallas_call(functools.partial(attend_kernel, len(lows), block_rows, re...]
    ppermute x0 -> x9, waiting for transfers between devices: none -> 9.36 us  [the longest x1 4.52 us: local(): got_b = lax.ppermute(own_b, 'grp', [(0, 2)])]
    sub x4 -> x0, matrix products: 6.73 us -> none  [one_block(): powers = jnp.exp(scores - largest)]
    ppermute x2 -> x4, starting transfers between devices: 7.29 us -> 12.7 us  [shifted(): return lax.ppermute(block, axis, route)]
  transfers between devices with their start and end apart: 3 -> 13, of which waited for: 0 -> 5; matrix products, arithmetic and copies ran while one was open for 1% -> 2% of each run, Pallas kernels for 0% -> 17%
where the time goes in v1:
time: 54.9 us; the launch traced here: 54.5 us
  starting transfers between devices  27.1 us (49%)
  waiting for transfers between devices  12.7 us (23%)
  Pallas kernels  10.6 us (19%)
  other arithmetic  1.76 us (3%)
  local copies, waits for them, and re-layouts  1.43 us (3%)
  between operations  0.93 us (2%)
    ppermute x4, starting transfers between devices, shifted(): return lax.ppermute(block, axis, route)  12.7 us
    pallas_call x1, Pallas kernels, attend(): pl.pallas_call(functools.partial(attend_kernel, len(lows), block_rows, re...  5.82 us
    ppermute x1, waiting for transfers between devices, local(): got_b = lax.ppermute(own_b, 'grp', [(0, 2)])  4.52 us
    ppermute x1, starting transfers between devices, local(): last_b = lax.ppermute(hold_b, 'grp', [(0, 1), (2, 3)])  3.7 us
    ppermute x4, waiting for transfers between devices, shifted(): return lax.ppermute(block, axis, route)  3.34 us
    ppermute x1, starting transfers between devices, local(): last_a = lax.ppermute(hold_a, 'grp', [(0, 2), (1, 3)])  3.09 us
    ppermute x1, starting transfers between devices, local(): got_b = lax.ppermute(own_b, 'grp', [(0, 2)])  2.43 us
    ppermute x1, starting transfers between devices, local(): got_a = lax.ppermute(own_a, 'grp', [(0, 1)])  2.02 us
  transfers between devices with their start and end apart: 13, of which 5 were waited for; matrix products, arithmetic and copies ran while one was open for 2% of the time, Pallas kernels for 17%

profile of v1, /device:TPU:0, one launch (start us, length us, event | category | flops | bytes accessed | tf_op | source)
XLA Modules:
  0.0 54.5 jit_solution(14555417854570467830)
XLA Ops:
  0.6 1.3 %slice_bitcast_fusion = (bf16[1,32,2560]{2,1,0:T(8,128)(2,1)S(1)}, bf16[1,32,2560]{2,1,0:T(8,128)(2,1)S(1)}, bf16[1,32,2560]{2,1,0:T(8,128)(2,1)S(1)}, bf16[1,32,2560]{2,1,0:T(8,128)(2,1)S(1)}) fusion(bf16[1,1,128,2560]{3,2,1,0:T(8,128)(2,1)} %param.9, bf16[1,1,128,2560]{3,2,1,0:T(8,128)(2,1)} %param.8), kind=kLoop, calls=%fused_computation.6 | loop fusion | bytes 1310720 | tf_op jit(solution)/shard_map/stack | solution.py:275
  2.0 0.8 %pad_maximum_fusion = bf16[2,32,2560]{2,1,0:T(8,128)(2,1)} fusion(bf16[1,32,2560]{2,1,0:T(8,128)(2,1)S(1)} %get-tuple-element.17, bf16[1,32,2560]{2,1,0:T(8,128)(2,1)S(1)} %get-tuple-element.22), kind=kLoop, calls=%fused_computation | loop fusion | flops 163840 | bytes 655360 | tf_op jit(solution)/shard_map/stack | solution.py:274
  2.7 4.9 %collective-permute-start = (bf16[2,32,2560]{2,1,0:T(8,128)(2,1)}, bf16[2,32,2560]{2,1,0:T(8,128)(2,1)S(1)}, u32[]{:S(2)}, u32[]{:S(2)}) collective-permute-start(bf16[2,32,2560]{2,1,0:T(8,128)(2,1)} %pad_maximum_fusion), channel_id=1, source_target_pairs={{0,2},{2,4},{4,6},{1,3},{3,5},{5,7},{8,10},{10,12},{12,14},{9,11},... | collective-permute-start | bytes 983048 | tf_op jit(solution)/shard_map/ppermute | solution.py:21
  7.7 0.8 %pad_maximum_fusion.1 = bf16[2,32,2560]{2,1,0:T(8,128)(2,1)} fusion(bf16[1,32,2560]{2,1,0:T(8,128)(2,1)S(1)} %get-tuple-element.16, bf16[1,32,2560]{2,1,0:T(8,128)(2,1)S(1)} %get-tuple-element.23), kind=kLoop, calls=%fused_computation.1 | loop fusion | flops 163840 | bytes 655360 | tf_op jit(solution)/shard_map/stack | solution.py:275
  8.4 1.3 %collective-permute-start.1 = (bf16[2,32,2560]{2,1,0:T(8,128)(2,1)}, bf16[2,32,2560]{2,1,0:T(8,128)(2,1)S(1)}, u32[]{:S(2)}, u32[]{:S(2)}) collective-permute-start(bf16[2,32,2560]{2,1,0:T(8,128)(2,1)} %pad_maximum_fusion.1), channel_id=1, source_target_pairs={{2,0},{4,2},{6,4},{3,1},{5,3},{7,5},{10,8},{12,10},{14,12},{11,9},... | collective-permute-start | bytes 983048 | tf_op jit(solution)/shard_map/ppermute | solution.py:21
  9.8 1.3 %collective-permute-start.3 = (f32[1,32]{1,0:T(1,128)S(1)}, f32[1,32]{1,0:T(1,128)S(1)}, u32[]{:S(2)}, u32[]{:S(2)}) collective-permute-start(f32[1,32]{1,0:T(1,128)S(1)} %get-tuple-element.21), channel_id=1, source_target_pairs={{2,0},{4,2},{6,4},{3,1},{5,3},{7,5},{10,8},{12,10},{14,12},{11,9},... | collective-permute-start | bytes 392 | tf_op jit(solution)/shard_map/ppermute | solution.py:21
  11.1 5.2 %collective-permute-start.2 = (f32[1,32]{1,0:T(1,128)S(1)}, f32[1,32]{1,0:T(1,128)S(1)}, u32[]{:S(2)}, u32[]{:S(2)}) collective-permute-start(f32[1,32]{1,0:T(1,128)S(1)} %get-tuple-element.20), channel_id=1, source_target_pairs={{0,2},{2,4},{4,6},{1,3},{3,5},{5,7},{8,10},{10,12},{12,14},{9,11},... | collective-permute-start | bytes 392 | tf_op jit(solution)/shard_map/ppermute | solution.py:21
  16.4 3.3 %collective-permute-done.3 = f32[1,32]{1,0:T(1,128)S(1)} collective-permute-done((f32[1,32]{1,0:T(1,128)S(1)}, f32[1,32]{1,0:T(1,128)S(1)}, u32[]{:S(2)}, u32[]{:S(2)}) %collective-permute-start.3) | collective-permute-done | bytes 160 | tf_op jit(solution)/shard_map/ppermute | solution.py:21
  19.8 0.1 pad_maximum_fusion.3.refs_6_
  19.9 1.1 %grad_terms.1 = (bf16[128,1280]{1,0:T(8,128)(2,1)}, bf16[128,1280]{1,0:T(8,128)(2,1)}) custom-call(s32[1,128]{1,0:T(1,128)S(1)} %and_select_fusion.1.row_ref, f32[1]{0:T(128)} %bitcast.10.root_ref, bf16[128,2560]{1,0:T(8,128)(2,1)S(1)} %bitcast.37, f32[1,2560]{1,0:T(1,128)S(1)} %broadcast_in_dim.15.gate_ref), custom_call_target="tpu_custom_call" | custom-call | flops 83886080 | bytes 1310720 | tf_op jit(solution)/shard_map/grad_terms/pallas_call | solution.py:164
  21.0 1.5 %collective-permute-start.9 = (bf16[128,1280]{1,0:T(8,128)(2,1)}, bf16[128,1280]{1,0:T(8,128)(2,1)}, u32[]{:S(2)}, u32[]{:S(2)}) collective-permute-start(bf16[128,1280]{1,0:T(8,128)(2,1)} %get-tuple-element.6.a_ref), channel_id=1, source_target_pairs={{0,8},{8,0},{16,24},{24,16},{1,9},{9,1},{17,25},{25,17},{2,10},{10... | collective-permute-start | bytes 983048 | tf_op jit(solution)/shard_map/ppermute | solution.py:288
  22.5 1.5 %collective-permute-start.10 = (bf16[128,1280]{1,0:T(8,128)(2,1)}, bf16[128,1280]{1,0:T(8,128)(2,1)}, u32[]{:S(2)}, u32[]{:S(2)}) collective-permute-start(bf16[128,1280]{1,0:T(8,128)(2,1)} %get-tuple-element.7.c_ref), channel_id=1, source_target_pairs={{0,16},{16,0},{8,24},{24,8},{1,17},{17,1},{9,25},{25,9},{2,18},{18... | collective-permute-start | bytes 983048 | tf_op jit(solution)/shard_map/ppermute | solution.py:288
  24.0 5.8 %attend.1.own_ref = bf16[128,2560]{1,0:T(8,128)(2,1)S(1)} custom-call(bf16[128,2560]{1,0:T(8,128)(2,1)S(1)} %bitcast.36, bf16[128,2560]{1,0:T(8,128)(2,1)S(1)} %bitcast.34, bf16[128,2560]{1,0:T(8,128)(2,1)S(1)} %bitcast.35, bf16[2,32,2560]{2,1,0:T(8,128)(2,1)S(1)} %collective-permute-done.refs_3_, bf16[2,32,2560]{2,1,0:T(8,128)(2,1)S(1)} %collective-permute-done.1.refs_4_, ...), custom_call_target="tpu_custom_call" | custom-call | flops 536870912 | bytes 3932160 | tf_op jit(solution)/shard_map/attend/pallas_call | solution.py:127
  29.9 2.4 %collective-permute-start.7 = (bf16[128,1280]{1,0:T(8,128)(2,1)S(1)}, bf16[128,1280]{1,0:T(8,128)(2,1)S(1)}, u32[]{:S(2)}, u32[]{:S(2)}) collective-permute-start(bf16[128,1280]{1,0:T(8,128)(2,1)S(1)} %get-tuple-element.12), channel_id=1, source_target_pairs={{0,16},{1,17},{2,18},{3,19},{4,20},{5,21},{6,22},{7,23}} | collective-permute-start | bytes 983048 | tf_op jit(solution)/shard_map/ppermute | solution.py:297
  32.4 2.0 %collective-permute-start.5 = (bf16[128,1280]{1,0:T(8,128)(2,1)S(1)}, bf16[128,1280]{1,0:T(8,128)(2,1)}, u32[]{:S(2)}, u32[]{:S(2)}) collective-permute-start(bf16[128,1280]{1,0:T(8,128)(2,1)S(1)} %get-tuple-element.13), channel_id=1, source_target_pairs={{0,8},{1,9},{2,10},{3,11},{4,12},{5,13},{6,14},{7,15}} | collective-permute-start | bytes 983048 | tf_op jit(solution)/shard_map/ppermute | solution.py:296
  34.4 1.4 %add_pairs.1 = (bf16[128,1280]{1,0:T(8,128)(2,1)S(1)}, bf16[128,1280]{1,0:T(8,128)(2,1)S(1)}) custom-call(bf16[128,1280]{1,0:T(8,128)(2,1)} %get-tuple-element.6.a_ref, bf16[128,1280]{1,0:T(8,128)(2,1)} %collective-permute-done.9.b_ref, bf16[128,1280]{1,0:T(8,128)(2,1)} %get-tuple-element.7.c_ref, bf16[128,1280]{1,0:T(8,128)(2,1)} %collective-permute-done.10.d_ref), custom_call_target="tpu_custom_call" | custom-call | flops 327680 | bytes 1966080 | tf_op jit(solution)/shard_map/add_pairs/pallas_call | solution.py:188
  36.0 4.5 %collective-permute-done.7 = bf16[128,1280]{1,0:T(8,128)(2,1)S(1)} collective-permute-done((bf16[128,1280]{1,0:T(8,128)(2,1)S(1)}, bf16[128,1280]{1,0:T(8,128)(2,1)S(1)}, u32[]{:S(2)}, u32[]{:S(2)}) %collective-permute-start.7) | collective-permute-done | bytes 327712 | tf_op jit(solution)/shard_map/ppermute | solution.py:297
  40.5 1.3 %collective-permute-done.5 = bf16[128,1280]{1,0:T(8,128)(2,1)} collective-permute-done((bf16[128,1280]{1,0:T(8,128)(2,1)S(1)}, bf16[128,1280]{1,0:T(8,128)(2,1)}, u32[]{:S(2)}, u32[]{:S(2)}) %collective-permute-start.5) | collective-permute-done | bytes 327712 | tf_op jit(solution)/shard_map/ppermute | solution.py:296
  41.9 3.1 %collective-permute-start.6 = (bf16[128,1280]{1,0:T(8,128)(2,1)S(1)}, bf16[128,1280]{1,0:T(8,128)(2,1)S(1)}, u32[]{:S(2)}, u32[]{:S(2)}) collective-permute-start(bf16[128,1280]{1,0:T(8,128)(2,1)S(1)} %get-tuple-element.11), channel_id=1, source_target_pairs={{0,16},{8,24},{1,17},{9,25},{2,18},{10,26},{3,19},{11,27},{4,20},{... | collective-permute-start | bytes 983048 | tf_op jit(solution)/shard_map/ppermute | solution.py:300
  45.0 3.7 %collective-permute-start.8 = (bf16[128,1280]{1,0:T(8,128)(2,1)S(1)}, bf16[128,1280]{1,0:T(8,128)(2,1)S(1)}, u32[]{:S(2)}, u32[]{:S(2)}) collective-permute-start(bf16[128,1280]{1,0:T(8,128)(2,1)S(1)} %get-tuple-element.10), channel_id=1, source_target_pairs={{0,8},{16,24},{1,9},{17,25},{2,10},{18,26},{3,11},{19,27},{4,12},{... | collective-permute-start | bytes 983048 | tf_op jit(solution)/shard_map/ppermute | solution.py:301
  48.7 1.0 %join_pairs.1 = bf16[128,2560]{1,0:T(8,128)(2,1)} custom-call(bf16[128,1280]{1,0:T(8,128)(2,1)S(1)} %get-tuple-element.8.a_ref, bf16[128,1280]{1,0:T(8,128)(2,1)S(1)} %collective-permute-done.11.b_ref, bf16[128,1280]{1,0:T(8,128)(2,1)S(1)} %get-tuple-element.9.c_ref, bf16[128,1280]{1,0:T(8,128)(2,1)S(1)} %collective-permute-done.12.d_ref), custom_call_target="tpu_custom_call" | custom-call | flops 327680 | bytes 1966080 | tf_op jit(solution)/shard_map/join_pairs/pallas_call | solution.py:211
  49.7 1.8 %collective-permute-done.6 = bf16[128,1280]{1,0:T(8,128)(2,1)S(1)} collective-permute-done((bf16[128,1280]{1,0:T(8,128)(2,1)S(1)}, bf16[128,1280]{1,0:T(8,128)(2,1)S(1)}, u32[]{:S(2)}, u32[]{:S(2)}) %collective-permute-start.6) | collective-permute-done | bytes 327712 | tf_op jit(solution)/shard_map/ppermute | solution.py:300
  51.6 1.7 %collective-permute-done.8 = bf16[128,1280]{1,0:T(8,128)(2,1)S(1)} collective-permute-done((bf16[128,1280]{1,0:T(8,128)(2,1)S(1)}, bf16[128,1280]{1,0:T(8,128)(2,1)S(1)}, u32[]{:S(2)}, u32[]{:S(2)}) %collective-permute-start.8) | collective-permute-done | bytes 327712 | tf_op jit(solution)/shard_map/ppermute | solution.py:301
  53.3 1.2 %relay.1 = bf16[128,2560]{1,0:T(8,128)(2,1)} custom-call(s32[1,128]{1,0:T(1,128)S(1)} %and_select_fusion.1.row_ref, bf16[128,2560]{1,0:T(8,128)(2,1)S(1)} %attend.1.own_ref, f32[1,2560]{1,0:T(1,128)S(1)} %broadcast_in_dim.15.gate_ref, bf16[128,1280]{1,0:T(8,128)(2,1)S(1)} %broadcast_select_fusion.3.first_ref, ...), custom_call_target="tpu_custom_call" | custom-call | flops 83886080 | bytes 1966080 | tf_op jit(solution)/shard_map/relay/pallas_call | solution.py:237
  (35 shorter events, 0.6 us)
Async XLA Ops:
  0.6 19.3 %copy-start.3 = (bf16[1,1,128,2560]{3,2,1,0:T(8,128)(2,1)S(1)}, bf16[1,1,128,2560]{3,2,1,0:T(8,128)(2,1)}, u32[]{:S(2)}) copy-start(bf16[1,1,128,2560]{3,2,1,0:T(8,128)(2,1)} %param.13) | copy-start | bytes 1966084
  1.9 7.8 %copy-start.5 = (s32[1,1,128]{2,1,0:T(1,128)S(1)}, s32[1,1,128]{2,1,0:T(1,128)}, u32[]{:S(2)}) copy-start(s32[1,1,128]{2,1,0:T(1,128)} %param.10) | copy-start | bytes 1540
  1.9 14.4 %copy-start.4 = (f32[1280]{0:T(1024)S(1)}, f32[1280]{0:T(1024)}, u32[]{:S(2)}) copy-start(f32[1280]{0:T(1024)} %param.12) | copy-start | bytes 15364
  1.9 14.5 %copy-start.6 = (s32[1,1,128]{2,1,0:T(1,128)S(1)}, s32[1,1,128]{2,1,0:T(1,128)}, u32[]{:S(2)}) copy-start(s32[1,1,128]{2,1,0:T(1,128)} %param.11) | copy-start | bytes 1540
  1.9 22.1 %copy-start.2 = (bf16[1,1,128,2560]{3,2,1,0:T(8,128)(2,1)S(1)}, bf16[1,1,128,2560]{3,2,1,0:T(8,128)(2,1)}, u32[]{:S(2)}) copy-start(bf16[1,1,128,2560]{3,2,1,0:T(8,128)(2,1)} %param.7) | copy-start | bytes 1966084
  2.7 21.3 %collective-permute-start = (bf16[2,32,2560]{2,1,0:T(8,128)(2,1)}, bf16[2,32,2560]{2,1,0:T(8,128)(2,1)S(1)}, u32[]{:S(2)}, u32[]{:S(2)}) collective-permute-start(bf16[2,32,2560]{2,1,0:T(8,128)(2,1)} %pad_maximum_fusion), channel_id=1, source_target_pairs={{0,2},{2,4},{4,6},{1,3},{3,5},{5,7},{8,10},{10,12},{12,14},{9,11},... | collective-permute-start | bytes 983048 | tf_op jit(solution)/shard_map/ppermute | solution.py:21
  7.7 16.4 %copy-start = (bf16[1,1,128,2560]{3,2,1,0:T(8,128)(2,1)S(1)}, bf16[1,1,128,2560]{3,2,1,0:T(8,128)(2,1)}, u32[]{:S(2)}) copy-start(bf16[1,1,128,2560]{3,2,1,0:T(8,128)(2,1)} %param.8) | copy-start | bytes 1966084
  7.7 16.4 %copy-start.1 = (bf16[1,1,128,2560]{3,2,1,0:T(8,128)(2,1)S(1)}, bf16[1,1,128,2560]{3,2,1,0:T(8,128)(2,1)}, u32[]{:S(2)}) copy-start(bf16[1,1,128,2560]{3,2,1,0:T(8,128)(2,1)} %param.9) | copy-start | bytes 1966084
  8.4 15.6 %collective-permute-start.1 = (bf16[2,32,2560]{2,1,0:T(8,128)(2,1)}, bf16[2,32,2560]{2,1,0:T(8,128)(2,1)S(1)}, u32[]{:S(2)}, u32[]{:S(2)}) collective-permute-start(bf16[2,32,2560]{2,1,0:T(8,128)(2,1)} %pad_maximum_fusion.1), channel_id=1, source_target_pairs={{2,0},{4,2},{6,4},{3,1},{5,3},{7,5},{10,8},{12,10},{14,12},{11,9},... | collective-permute-start | bytes 983048 | tf_op jit(solution)/shard_map/ppermute | solution.py:21
  9.8 9.9 %collective-permute-start.3 = (f32[1,32]{1,0:T(1,128)S(1)}, f32[1,32]{1,0:T(1,128)S(1)}, u32[]{:S(2)}, u32[]{:S(2)}) collective-permute-start(f32[1,32]{1,0:T(1,128)S(1)} %get-tuple-element.21), channel_id=1, source_target_pairs={{2,0},{4,2},{6,4},{3,1},{5,3},{7,5},{10,8},{12,10},{14,12},{11,9},... | collective-permute-start | bytes 392 | tf_op jit(solution)/shard_map/ppermute | solution.py:21
  11.1 8.7 %collective-permute-start.2 = (f32[1,32]{1,0:T(1,128)S(1)}, f32[1,32]{1,0:T(1,128)S(1)}, u32[]{:S(2)}, u32[]{:S(2)}) collective-permute-start(f32[1,32]{1,0:T(1,128)S(1)} %get-tuple-element.20), channel_id=1, source_target_pairs={{0,2},{2,4},{4,6},{1,3},{3,5},{5,7},{8,10},{10,12},{12,14},{9,11},... | collective-permute-start | bytes 392 | tf_op jit(solution)/shard_map/ppermute | solution.py:21
  16.3 3.5 %collective-permute-start.4 = (f32[1280]{0:T(1024)S(1)}, f32[1280]{0:T(1024)S(1)}, u32[]{:S(2)}, u32[]{:S(2)}) collective-permute-start(f32[1280]{0:T(1024)S(1)} %copy-done.4), channel_id=1, source_target_pairs={{0,1},{1,0},{2,3},{3,2},{4,5},{5,4},{6,7},{7,6},{8,9},{9,8},{10,11... | collective-permute-start | bytes 15368 | tf_op jit(solution)/shard_map/ppermute | solution.py:254
  21.0 13.4 %collective-permute-start.9 = (bf16[128,1280]{1,0:T(8,128)(2,1)}, bf16[128,1280]{1,0:T(8,128)(2,1)}, u32[]{:S(2)}, u32[]{:S(2)}) collective-permute-start(bf16[128,1280]{1,0:T(8,128)(2,1)} %get-tuple-element.6.a_ref), channel_id=1, source_target_pairs={{0,8},{8,0},{16,24},{24,16},{1,9},{9,1},{17,25},{25,17},{2,10},{10... | collective-permute-start | bytes 983048 | tf_op jit(solution)/shard_map/ppermute | solution.py:288
  22.5 11.9 %collective-permute-start.10 = (bf16[128,1280]{1,0:T(8,128)(2,1)}, bf16[128,1280]{1,0:T(8,128)(2,1)}, u32[]{:S(2)}, u32[]{:S(2)}) collective-permute-start(bf16[128,1280]{1,0:T(8,128)(2,1)} %get-tuple-element.7.c_ref), channel_id=1, source_target_pairs={{0,16},{16,0},{8,24},{24,8},{1,17},{17,1},{9,25},{25,9},{2,18},{18... | collective-permute-start | bytes 983048 | tf_op jit(solution)/shard_map/ppermute | solution.py:288
  29.9 10.6 %collective-permute-start.7 = (bf16[128,1280]{1,0:T(8,128)(2,1)S(1)}, bf16[128,1280]{1,0:T(8,128)(2,1)S(1)}, u32[]{:S(2)}, u32[]{:S(2)}) collective-permute-start(bf16[128,1280]{1,0:T(8,128)(2,1)S(1)} %get-tuple-element.12), channel_id=1, source_target_pairs={{0,16},{1,17},{2,18},{3,19},{4,20},{5,21},{6,22},{7,23}} | collective-permute-start | bytes 983048 | tf_op jit(solution)/shard_map/ppermute | solution.py:297
  32.4 9.4 %collective-permute-start.5 = (bf16[128,1280]{1,0:T(8,128)(2,1)S(1)}, bf16[128,1280]{1,0:T(8,128)(2,1)}, u32[]{:S(2)}, u32[]{:S(2)}) collective-permute-start(bf16[128,1280]{1,0:T(8,128)(2,1)S(1)} %get-tuple-element.13), channel_id=1, source_target_pairs={{0,8},{1,9},{2,10},{3,11},{4,12},{5,13},{6,14},{7,15}} | collective-permute-start | bytes 983048 | tf_op jit(solution)/shard_map/ppermute | solution.py:296
  35.8 12.9 %collective-permute-start.11 = (bf16[128,1280]{1,0:T(8,128)(2,1)S(1)}, bf16[128,1280]{1,0:T(8,128)(2,1)S(1)}, u32[]{:S(2)}, u32[]{:S(2)}) collective-permute-start(bf16[128,1280]{1,0:T(8,128)(2,1)S(1)} %get-tuple-element.8.a_ref), channel_id=1, source_target_pairs={{0,16},{16,0},{8,24},{24,8},{1,17},{17,1},{9,25},{25,9},{2,18},{18... | collective-permute-start | bytes 983048 | tf_op jit(solution)/shard_map/ppermute | solution.py:291
  35.9 12.8 %collective-permute-start.12 = (bf16[128,1280]{1,0:T(8,128)(2,1)S(1)}, bf16[128,1280]{1,0:T(8,128)(2,1)S(1)}, u32[]{:S(2)}, u32[]{:S(2)}) collective-permute-start(bf16[128,1280]{1,0:T(8,128)(2,1)S(1)} %get-tuple-element.9.c_ref), channel_id=1, source_target_pairs={{0,8},{8,0},{16,24},{24,16},{1,9},{9,1},{17,25},{25,17},{2,10},{10... | collective-permute-start | bytes 983048 | tf_op jit(solution)/shard_map/ppermute | solution.py:291
  41.9 9.6 %collective-permute-start.6 = (bf16[128,1280]{1,0:T(8,128)(2,1)S(1)}, bf16[128,1280]{1,0:T(8,128)(2,1)S(1)}, u32[]{:S(2)}, u32[]{:S(2)}) collective-permute-start(bf16[128,1280]{1,0:T(8,128)(2,1)S(1)} %get-tuple-element.11), channel_id=1, source_target_pairs={{0,16},{8,24},{1,17},{9,25},{2,18},{10,26},{3,19},{11,27},{4,20},{... | collective-permute-start | bytes 983048 | tf_op jit(solution)/shard_map/ppermute | solution.py:300
  45.0 8.3 %collective-permute-start.8 = (bf16[128,1280]{1,0:T(8,128)(2,1)S(1)}, bf16[128,1280]{1,0:T(8,128)(2,1)S(1)}, u32[]{:S(2)}, u32[]{:S(2)}) collective-permute-start(bf16[128,1280]{1,0:T(8,128)(2,1)S(1)} %get-tuple-element.10), channel_id=1, source_target_pairs={{0,8},{16,24},{1,9},{17,25},{2,10},{18,26},{3,11},{19,27},{4,12},{... | collective-permute-start | bytes 983048 | tf_op jit(solution)/shard_map/ppermute | solution.py:301

commit v2 on v0

v2 whole, which is shorter than its diff:
```python
import functools
import math

import jax
import jax.numpy as jnp
from jax import lax
from jax.experimental import pallas as pl
from jax.experimental.pallas import tpu as pltpu
from jax.sharding import PartitionSpec as P

HEADS = 32
DH = 80
FRAMES = 20
LANES = 128
VMEM_LIMIT = 48 * 1024 * 1024


def shifted(block, axis, distance):
    devices = range(lax.axis_size(axis))
    route = [(i - distance, i) for i in devices if i - distance in devices]
    return lax.ppermute(block, axis, route)


def lane_windows(heads):
    windows = []
    for head in range(heads):
        first, last = head * DH, (head + 1) * DH
        if windows and last <= windows[-1][0] + 2 * LANES:
            windows[-1][1].append(head)
        else:
            windows.append((first // LANES * LANES, [head]))
    out = []
    for start, members in windows:
        start = min(start, heads * DH - 2 * LANES)
        out.append((start, members))
    return out


def head_masks(rows, period):
    masks = {}
    for start, members in lane_windows(period // DH):
        lane = lax.broadcasted_iota(jnp.int32, (rows, 2 * LANES), 1) + start
        for h in members:
            inside = (lane >= h * DH) & (lane < (h + 1) * DH)
            masks[h] = jnp.where(inside, 1.0, 0.0).astype(jnp.bfloat16)
    return masks


def mixed_period(base, bias, query, key, value, masks, period):
    rows = bias.shape[0]
    factor = math.log2(math.e) / math.sqrt(DH)
    windows = lane_windows(period // DH)
    scores = []
    for start, members in windows:
        lanes = slice(base + start, base + start + 2 * LANES)
        part = query(lanes)
        stacked = jnp.concatenate([part * masks[h] for h in members], axis=0)
        scores.append(
            lax.dot_general(
                stacked, key(lanes), (((1,), (1,)), ((), ())), preferred_element_type=jnp.float32
            )
        )
    weights = []
    for part, (start, members) in zip(scores, windows):
        part = part.reshape(len(members), rows, -1) + bias[None]
        largest = jnp.max(part, axis=-1, keepdims=True)
        powers = jnp.exp2((part - largest) * factor)
        totals = jnp.sum(powers, axis=-1, keepdims=True)
        weight = (powers * (1.0 / totals)).astype(jnp.bfloat16)
        weights.append(weight.reshape(len(members) * rows, -1))
    tiles = {}
    for weight, (start, members) in zip(weights, windows):
        lanes = slice(base + start, base + start + 2 * LANES)
        mixed = jnp.dot(weight, value(lanes), preferred_element_type=jnp.float32)
        for n, h in enumerate(members):
            for t in range(2):
                low = start + t * LANES
                if h * DH >= low + LANES or (h + 1) * DH <= low:
                    continue
                piece = mixed[n * rows : (n + 1) * rows, t * LANES : (t + 1) * LANES]
                if low in tiles:
                    lane = lax.broadcasted_iota(jnp.int32, (rows, LANES), 1) + low
                    tiles[low] = jnp.where(lane >= h * DH, piece, tiles[low])
                else:
                    tiles[low] = piece
    return {low: tile.astype(jnp.bfloat16) for low, tile in tiles.items()}


def columns(code):
    return jnp.broadcast_to(code, (LANES, code.shape[1])).T


def attend_blocks(blocks, q_ref, keys, values, own_code, key_code, out_ref):
    width = q_ref.shape[1]
    period = math.lcm(DH, LANES)
    work = []
    masks = {}
    for top, first, rows, span, at in blocks:
        mine = own_code[top : top + rows, :1]
        theirs = key_code[first : first + span].T[:rows]
        bias = jnp.where(jnp.abs(mine - theirs) <= 1.5, 0.0, -1e30)
        if rows not in masks:
            masks[rows] = head_masks(rows, period)
        work.append((top, first, rows, span, at, bias))
    for base in range(0, width, period):
        for top, first, rows, span, at, bias in work:
            tiles = mixed_period(
                base,
                bias,
                lambda lanes: q_ref[top : top + rows, lanes],
                lambda lanes: keys[first : first + span, lanes],
                lambda lanes: values[first : first + span, lanes],
                masks[rows],
                period,
            )
            for low, tile in tiles.items():
                out_ref[at : at + rows, base + low : base + low + LANES] = tile


def middle_kernel(reach, q_ref, k_ref, v_ref, code_ref, out_ref):
    tokens = q_ref.shape[0]
    code = columns(code_ref[...])
    attend_blocks(
        [(reach, 0, tokens - 2 * reach, tokens, 0)], q_ref, k_ref, v_ref, code, code, out_ref
    )


def edge_kernel(hops, blocks, *refs):
    q_ref, k_ref, v_ref, code_ref = refs[:4]
    lows = refs[4 : 4 + hops]
    highs = refs[4 + hops : 4 + 2 * hops]
    out_ref, keys, values, codes = refs[4 + 2 * hops :]
    tokens, width = q_ref.shape
    code = columns(code_ref[...])
    at = 0
    for piece in (*lows, None, *highs):
        if piece is None:
            keys[at : at + tokens] = k_ref[...]
            values[at : at + tokens] = v_ref[...]
            codes[at : at + tokens] = code
            at += tokens
        else:
            rows = piece.shape[0]
            keys[at : at + rows] = piece[:, :width]
            values[at : at + rows] = piece[:, width : 2 * width]
            codes[at : at + rows] = piece[:, 2 * width :].astype(jnp.float32)
            at += rows
    attend_blocks(blocks, q_ref, keys, values, code, codes[...], out_ref)


def attend_cost(tokens, span, width):
    return pl.CostEstimate(
        flops=HEADS * tokens * span * 2 * LANES * 4,
        bytes_accessed=12 * tokens * width,
        transcendentals=HEADS * tokens * span,
    )


VMEM = pl.BlockSpec(memory_space=pltpu.VMEM)
PARAMS = pltpu.CompilerParams(vmem_limit_bytes=VMEM_LIMIT)


def attend_middle(queries, keys, values, code, reach):
    tokens, width = queries.shape
    return pl.pallas_call(
        functools.partial(middle_kernel, reach),
        in_specs=[VMEM] * 4,
        out_specs=VMEM,
        out_shape=jax.ShapeDtypeStruct((tokens - 2 * reach, width), jnp.bfloat16),
        compiler_params=PARAMS,
        cost_estimate=attend_cost(tokens - 2 * reach, tokens, width),
        name="attend_middle",
    )(queries, keys, values, code)


def attend_edges(queries, keys, values, code, lows, highs, reach):
    tokens, width = queries.shape
    window = tokens + 2 * reach
    if tokens > 2 * reach:
        span = min(tokens, -(-3 * reach // LANES) * LANES)
        blocks = [(0, 0, reach, span, 0), (tokens - reach, window - span, reach, span, reach)]
    else:
        blocks = [(0, 0, tokens, window, 0)]
    rows = sum(b[2] for b in blocks)
    return pl.pallas_call(
        functools.partial(edge_kernel, len(lows), blocks),
        in_specs=[VMEM] * (4 + 2 * len(lows)),
        out_specs=VMEM,
        out_shape=jax.ShapeDtypeStruct((rows, width), jnp.bfloat16),
        scratch_shapes=[
            pltpu.VMEM((window, width), jnp.bfloat16),
            pltpu.VMEM((window, width), jnp.bfloat16),
            pltpu.VMEM((window, LANES), jnp.float32),
        ],
        compiler_params=PARAMS,
        cost_estimate=attend_cost(rows, blocks[0][3], width),
        name="attend_edges",
    )(queries, keys, values, code, *lows, *highs)


def pack_kernel(rows, k_ref, v_ref, code_ref, tail_ref, head_ref):
    tokens, width = k_ref.shape
    code = columns(code_ref[...]).astype(jnp.bfloat16)
    for ref, part in ((tail_ref, slice(tokens - rows, tokens)), (head_ref, slice(0, rows))):
        ref[:, :width] = k_ref[part]
        ref[:, width : 2 * width] = v_ref[part]
        ref[:, 2 * width :] = code[part]


def pack_ends(keys, values, code, rows):
    width = keys.shape[1]
    return pl.pallas_call(
        functools.partial(pack_kernel, rows),
        in_specs=[VMEM] * 3,
        out_specs=[VMEM] * 2,
        out_shape=[jax.ShapeDtypeStruct((rows, 2 * width + LANES), jnp.bfloat16)] * 2,
        compiler_params=PARAMS,
        cost_estimate=pl.CostEstimate(flops=0, bytes_accessed=16 * rows * width, transcendentals=0),
        name="pack_ends",
    )(keys, values, code)


def term_kernel(row_ref, root_ref, grad_ref, gate_ref, out_ref):
    tokens = grad_ref.shape[0]
    wanted = lax.broadcasted_iota(jnp.int32, (tokens, tokens), 0)
    selector = jnp.where(wanted == row_ref[...], 1.0, 0.0).astype(jnp.bfloat16)
    grads = grad_ref[...]
    summed = jnp.dot(selector, grads, preferred_element_type=jnp.float32)
    term = gate_ref[...] * summed + root_ref[0] * grads.astype(jnp.float32)
    out_ref[...] = term.astype(jnp.bfloat16)


def grad_terms(local_rows, root, grads, gate):
    tokens, width = grads.shape
    return pl.pallas_call(
        term_kernel,
        in_specs=[VMEM, pl.BlockSpec(memory_space=pltpu.SMEM), VMEM, VMEM],
        out_specs=VMEM,
        out_shape=jax.ShapeDtypeStruct((tokens, width), jnp.bfloat16),
        compiler_params=PARAMS,
        cost_estimate=pl.CostEstimate(
            flops=2 * tokens * tokens * width, bytes_accessed=4 * tokens * width, transcendentals=0
        ),
        name="grad_terms",
    )(local_rows, root, grads, gate)


def relay_kernel(reach, row_ref, gate_ref, *refs):
    out_ref = refs[-1]
    count = (len(refs) - 1) // 2
    tokens = out_ref.shape[0]
    rows = row_ref[...]
    if count == 2:
        spots = [(reach, tokens - 2 * reach, 0, 0), (0, reach, 1, 0), (tokens - reach, reach, 1, reach)]
        low, high = rows < reach, rows >= tokens - reach
        place = jnp.where(low, rows + tokens - 2 * reach, jnp.where(high, rows, rows - reach))
    else:
        spots = [(0, tokens, 0, 0)]
        place = rows
    wanted = lax.broadcasted_iota(jnp.int32, (tokens, tokens), 0)
    selector = jnp.where(wanted == place, 1.0, 0.0).T.astype(jnp.bfloat16)
    branch = jnp.concatenate([ref[...] for ref in refs[count : 2 * count]], axis=0)
    relayed = gate_ref[...] * jnp.dot(selector, branch, preferred_element_type=jnp.float32)
    for top, size, piece, at in spots:
        own = refs[piece][at : at + size].astype(jnp.float32)
        out_ref[top : top + size] = (own + relayed[top : top + size]).astype(jnp.bfloat16)


def relay(local_rows, gate, own, branch, reach):
    tokens = sum(p.shape[0] for p in own)
    width = own[0].shape[1]
    return pl.pallas_call(
        functools.partial(relay_kernel, reach),
        in_specs=[VMEM] * (2 + 2 * len(own)),
        out_specs=VMEM,
        out_shape=jax.ShapeDtypeStruct((tokens, width), jnp.bfloat16),
        compiler_params=PARAMS,
        cost_estimate=pl.CostEstimate(
            flops=2 * tokens * tokens * width, bytes_accessed=6 * tokens * width, transcendentals=0
        ),
        name="relay",
    )(local_rows, gate, *own, *branch)


def whole_gate(gate):
    ranks = lax.axis_size("rep")
    if ranks != 2:
        return lax.all_gather(gate, "rep", axis=0, tiled=True)
    other = lax.ppermute(gate, "rep", [(0, 1), (1, 0)])
    first = lax.axis_index("rep") == 0
    return jnp.concatenate([jnp.where(first, gate, other), jnp.where(first, other, gate)])


def from_branch(rows, group):
    if lax.axis_size("grp") != 4:
        return lax.psum(jnp.where(group == 0, rows, jnp.zeros_like(rows)), "grp")
    got = lax.ppermute(rows, "grp", [(0, 1)])
    hold = jnp.where(group == 1, got, rows)
    last = lax.ppermute(hold, "grp", [(0, 2), (1, 3)])
    return jnp.where(group <= 1, hold, last)


def local(query_rows, key_rows, value_rows, view_frame, control_row, control_gate, out_grad):
    queries, keys, values = query_rows[0, 0], key_rows[0, 0], value_rows[0, 0]
    tokens, width = queries.shape
    length = tokens * lax.axis_size("seq")
    reach = 2 * (length // 32)
    hops = (reach + tokens - 1) // tokens
    group = lax.axis_index("grp")

    gate = whole_gate(control_gate)[None]
    tag = view_frame[0, 0]
    code = (tag + 8 * (tag // FRAMES) + 16).astype(jnp.float32)[None]
    most = min(tokens, reach)
    tail, head = pack_ends(keys, values, code, most)
    lows, highs = [], []
    for hop in range(1, hops + 1):
        rows = min(tokens, reach - (hop - 1) * tokens)
        lows.insert(0, shifted(tail[most - rows :], "seq", hop))
        highs.append(shifted(head[:rows], "seq", -hop))

    local_rows = (control_row[0] % tokens).astype(jnp.int32)
    root = (group == 0).astype(jnp.float32)[None]
    terms = grad_terms(local_rows, root, out_grad[0, 0], gate)
    branch_grad = lax.psum(terms, "grp")

    own = [attend_edges(queries, keys, values, code, lows, highs, reach)]
    if tokens > 2 * reach:
        own.insert(0, attend_middle(queries, keys, values, code, reach))
    branch = [from_branch(piece, group) for piece in own]
    block_out = relay(local_rows, gate, own, branch, reach)
    return (block_out[None, None], branch_grad[None])


def solution(mesh):
    placed = (
        P("rep", "grp", "seq", None),
        P("rep", "grp", "seq", None),
        P("rep", "grp", "seq", None),
        P("rep", "grp", "seq"),
        P("rep", "grp", "seq"),
        P("rep"),
        P("rep", "grp", "seq", None),
    )
    return jax.shard_map(
        local,
        mesh=mesh,
        in_specs=placed,
        out_specs=(P("rep", "grp", "seq", None), P("rep", "seq", None)),
        check_vma=False,
    )
```

time: 143 us -> 85.8 us (0.60)
  blocking collectives: 89.1 us -> 0 us
  waiting for transfers between devices: 0.04 us -> 41.4 us
  matrix products: 20.5 us -> 0 us
  starting transfers between devices: 7.33 us -> 16.4 us
  Pallas kernels: 0 us -> 8.35 us
  other arithmetic: 5.98 us -> 0.85 us
    psum x1 -> x0, blocking collectives: 57.5 us -> none  [local(): branch_sum = lax.psum(full_gate * summed + own_term, 'grp')]
    all_gather x2 -> x0, blocking collectives: 31.6 us -> none  [the longest x1 29.8 us: local(): tags = lax.all_gather(view_frame[0, 0] + 1, 'seq', axis=0, tiled=True)]
    psum x1, waiting for transfers between devices: 0.02 us -> 23.6 us  [local(): branch_grad = lax.psum(terms, 'grp')]
    ppermute x0 -> x5, waiting for transfers between devices: none -> 16.3 us  [the longest x2 8.39 us: from_branch(): last = lax.ppermute(hold, 'grp', [(0, 2), (1, 3)])]
    dot_general x6 -> x0, matrix products: 13.8 us -> none  [the longest x4 11 us: one_block(): jnp.einsum('hqk,hdk->hdq', weights, values_pad, preferred_element_type=jn...]
    ppermute x0 -> x5, starting transfers between devices: none -> 10.2 us  [the longest x2 7.55 us: from_branch(): got = lax.ppermute(rows, 'grp', [(0, 1)])]
    pallas_call x0 -> x5, Pallas kernels: none -> 8.35 us  [the longest x1 3.28 us: attend_edges(): pl.pallas_call(functools.partial(edge_kernel, len(lows), blocks), in_spec...]
    sub x4 -> x0, matrix products: 6.73 us -> none  [one_block(): powers = jnp.exp(scores - largest)]
  transfers between devices with their start and end apart: 3 -> 8, of which waited for: 0 -> 5; matrix products, arithmetic and copies ran while one was open for 1% -> 0% of each run, Pallas kernels for 0% -> 9%
where the time goes in v2:
time: 85.8 us; the launch traced here: 85.4 us
  waiting for transfers between devices  41.4 us (48%)
  starting transfers between devices  16.4 us (19%)
  between operations  14.2 us (17%)
  Pallas kernels  8.35 us (10%)
  local copies, waits for them, and re-layouts  4.17 us (5%)
    psum x1, waiting for transfers between devices, local(): branch_grad = lax.psum(terms, 'grp')  23.6 us
    ppermute x2, waiting for transfers between devices, from_branch(): last = lax.ppermute(hold, 'grp', [(0, 2), (1, 3)])  8.39 us
    ppermute x2, starting transfers between devices, from_branch(): got = lax.ppermute(rows, 'grp', [(0, 1)])  7.55 us
    ppermute x2, waiting for transfers between devices, from_branch(): got = lax.ppermute(rows, 'grp', [(0, 1)])  6.78 us
    ppermute x2, starting transfers between devices, shifted(): return lax.ppermute(block, axis, route)  6.23 us
    unnamed x17, local copies, waits for them, and re-layouts  4.16 us
    pallas_call x1, Pallas kernels, attend_edges(): pl.pallas_call(functools.partial(edge_kernel, len(lows), blocks), in_spec...  3.28 us
    ppermute x2, starting transfers between devices, from_branch(): last = lax.ppermute(hold, 'grp', [(0, 2), (1, 3)])  2.62 us
  transfers between devices with their start and end apart: 8, of which 5 were waited for; matrix products, arithmetic and copies ran while one was open for 0% of the time, Pallas kernels for 9%

profile of v2, /device:TPU:0, one launch (start us, length us, event | category | flops | bytes accessed | tf_op | source)
XLA Modules:
  0.0 85.4 jit_solution(5962984000356585332)
XLA Ops:
  7.2 0.0 all-reduce.2.cloned.1.call-start
  7.2 0.7 fusion.2.code_ref.refs_3_
  7.9 1.1 %copy-done = bf16[1,1,128,2560]{3,2,1,0:T(8,128)(2,1)S(1)} copy-done((bf16[1,1,128,2560]{3,2,1,0:T(8,128)(2,1)S(1)}, bf16[1,1,128,2560]{3,2,1,0:T(8,128)(2,1)}, u32[]{:S(2)}) %copy-start) | copy-done | bytes 655384
  9.0 1.1 %copy-done.2 = bf16[1,1,128,2560]{3,2,1,0:T(8,128)(2,1)S(1)} copy-done((bf16[1,1,128,2560]{3,2,1,0:T(8,128)(2,1)S(1)}, bf16[1,1,128,2560]{3,2,1,0:T(8,128)(2,1)}, u32[]{:S(2)}) %copy-start.2) | copy-done | bytes 655384
  10.1 0.8 pack_ends.1
  10.9 4.9 %collective-permute-start.1 = (bf16[32,5248]{1,0:T(8,128)(2,1)}, bf16[32,5248]{1,0:T(8,128)(2,1)S(1)}, u32[]{:S(2)}, u32[]{:S(2)}) collective-permute-start(bf16[32,5248]{1,0:T(8,128)(2,1)} %get-tuple-element.4), channel_id=1, source_target_pairs={{0,2},{2,4},{4,6},{1,3},{3,5},{5,7},{8,10},{10,12},{12,14},{9,11},... | collective-permute-start | bytes 1007624 | tf_op jit(solution)/shard_map/ppermute | solution.py:21
  15.8 1.3 %collective-permute-start.2 = (bf16[32,5248]{1,0:T(8,128)(2,1)S(1)}, bf16[32,5248]{1,0:T(8,128)(2,1)S(1)}, u32[]{:S(2)}, u32[]{:S(2)}) collective-permute-start(bf16[32,5248]{1,0:T(8,128)(2,1)S(1)} %get-tuple-element.5), channel_id=1, source_target_pairs={{2,0},{4,2},{6,4},{3,1},{5,3},{7,5},{10,8},{12,10},{14,12},{11,9},... | collective-permute-start | bytes 1007624 | tf_op jit(solution)/shard_map/ppermute | solution.py:21
  17.2 0.0 copy-start.7
  17.2 0.0 copy-start.5
  17.2 1.9 %attend_middle.1.refs_0_ = bf16[64,2560]{1,0:T(8,128)(2,1)S(1)} custom-call(bf16[128,2560]{1,0:T(8,128)(2,1)S(1)} %bitcast.32, bf16[128,2560]{1,0:T(8,128)(2,1)S(1)} %bitcast.27, bf16[128,2560]{1,0:T(8,128)(2,1)S(1)} %bitcast.30, f32[1,128]{1,0:T(1,128)S(1)} %fusion.2.code_ref.refs_3_), custom_call_target="tpu_custom_call" | custom-call | flops 268435456 | bytes 1966080 | tf_op jit(solution)/shard_map/attend_middle/pallas_call | solution.py:165
  19.1 4.1 %collective-permute-start.3 = (bf16[64,2560]{1,0:T(8,128)(2,1)S(1)}, bf16[64,2560]{1,0:T(8,128)(2,1)}, u32[]{:S(2)}, u32[]{:S(2)}) collective-permute-start(bf16[64,2560]{1,0:T(8,128)(2,1)S(1)} %attend_middle.1.refs_0_), channel_id=1, source_target_pairs={{0,8},{1,9},{2,10},{3,11},{4,12},{5,13},{6,14},{7,15}} | collective-permute-start | bytes 983048 | tf_op jit(solution)/shard_map/ppermute | solution.py:297
  23.2 1.1 %collective-permute-done = f32[1280]{0:T(1024)S(1)} collective-permute-done((f32[1280]{0:T(1024)S(1)}, f32[1280]{0:T(1024)S(1)}, u32[]{:S(2)}, u32[]{:S(2)}) %collective-permute-start) | collective-permute-done | bytes 5152 | tf_op jit(solution)/shard_map/ppermute | solution.py:289
  24.4 1.2 %grad_terms.1 = bf16[128,2560]{1,0:T(8,128)(2,1)} custom-call(s32[1,128]{1,0:T(1,128)S(1)} %and_select_fusion.1.row_ref, f32[1]{0:T(128)} %bitcast.6.root_ref, bf16[128,2560]{1,0:T(8,128)(2,1)S(1)} %bitcast.34, f32[1,2560]{1,0:T(1,128)S(1)} %broadcast_in_dim.15.gate_ref), custom_call_target="tpu_custom_call" | custom-call | flops 83886080 | bytes 1310720 | tf_op jit(solution)/shard_map/grad_terms/pallas_call | solution.py:235
  25.6 0.0 all-reduce.2.cloned.1.call-update
  25.6 1.5 %collective-permute-done.2.refs_5_ = bf16[32,5248]{1,0:T(8,128)(2,1)S(1)} collective-permute-done((bf16[32,5248]{1,0:T(8,128)(2,1)S(1)}, bf16[32,5248]{1,0:T(8,128)(2,1)S(1)}, u32[]{:S(2)}, u32[]{:S(2)}) %collective-permute-start.2) | collective-permute-done | bytes 335904 | tf_op jit(solution)/shard_map/ppermute | solution.py:21
  27.1 3.3 %attend_edges.1.refs_1_ = bf16[64,2560]{1,0:T(8,128)(2,1)S(1)} custom-call(bf16[128,2560]{1,0:T(8,128)(2,1)S(1)} %bitcast.33, bf16[128,2560]{1,0:T(8,128)(2,1)S(1)} %bitcast.28, bf16[128,2560]{1,0:T(8,128)(2,1)S(1)} %bitcast.31, f32[1,128]{1,0:T(1,128)S(1)} %fusion.2.code_ref.refs_3_, bf16[32,5248]{1,0:T(8,128)(2,1)S(1)} %collective-permute-done.1.refs_4_, ...), custom_call_target="tpu_custom_call" | custom-call | flops 268435456 | bytes 1966080 | tf_op jit(solution)/shard_map/attend_edges/pallas_call | solution.py:185
  30.4 3.4 %collective-permute-start.5 = (bf16[64,2560]{1,0:T(8,128)(2,1)S(1)}, bf16[64,2560]{1,0:T(8,128)(2,1)S(1)}, u32[]{:S(2)}, u32[]{:S(2)}) collective-permute-start(bf16[64,2560]{1,0:T(8,128)(2,1)S(1)} %attend_edges.1.refs_1_), channel_id=1, source_target_pairs={{0,8},{1,9},{2,10},{3,11},{4,12},{5,13},{6,14},{7,15}} | collective-permute-start | bytes 983048 | tf_op jit(solution)/shard_map/ppermute | solution.py:297
  33.8 1.3 %collective-permute-start.4 = (bf16[64,2560]{1,0:T(8,128)(2,1)S(1)}, bf16[64,2560]{1,0:T(8,128)(2,1)S(1)}, u32[]{:S(2)}, u32[]{:S(2)}) collective-permute-start(bf16[64,2560]{1,0:T(8,128)(2,1)S(1)} %broadcast_select_fusion.1), channel_id=1, source_target_pairs={{0,16},{8,24},{1,17},{9,25},{2,18},{10,26},{3,19},{11,27},{4,20},{... | collective-permute-start | bytes 983048 | tf_op jit(solution)/shard_map/ppermute | solution.py:299
  35.2 6.8 %collective-permute-done.5 = bf16[64,2560]{1,0:T(8,128)(2,1)S(1)} collective-permute-done((bf16[64,2560]{1,0:T(8,128)(2,1)S(1)}, bf16[64,2560]{1,0:T(8,128)(2,1)S(1)}, u32[]{:S(2)}, u32[]{:S(2)}) %collective-permute-start.5) | collective-permute-done | bytes 327712 | tf_op jit(solution)/shard_map/ppermute | solution.py:297
  42.0 1.3 %collective-permute-start.6 = (bf16[64,2560]{1,0:T(8,128)(2,1)S(1)}, bf16[64,2560]{1,0:T(8,128)(2,1)S(1)}, u32[]{:S(2)}, u32[]{:S(2)}) collective-permute-start(bf16[64,2560]{1,0:T(8,128)(2,1)S(1)} %broadcast_select_fusion), channel_id=1, source_target_pairs={{0,16},{8,24},{1,17},{9,25},{2,18},{10,26},{3,19},{11,27},{4,20},{... | collective-permute-start | bytes 983048 | tf_op jit(solution)/shard_map/ppermute | solution.py:299
  43.4 8.4 %collective-permute-done.6 = bf16[64,2560]{1,0:T(8,128)(2,1)S(1)} collective-permute-done((bf16[64,2560]{1,0:T(8,128)(2,1)S(1)}, bf16[64,2560]{1,0:T(8,128)(2,1)S(1)}, u32[]{:S(2)}, u32[]{:S(2)}) %collective-permute-start.6) | collective-permute-done | bytes 327712 | tf_op jit(solution)/shard_map/ppermute | solution.py:299
  51.8 1.2 %relay.1 = bf16[128,2560]{1,0:T(8,128)(2,1)} custom-call(s32[1,128]{1,0:T(1,128)S(1)} %and_select_fusion.1.row_ref, f32[1,2560]{1,0:T(1,128)S(1)} %broadcast_in_dim.15.gate_ref, bf16[64,2560]{1,0:T(8,128)(2,1)S(1)} %attend_middle.1.refs_0_, bf16[64,2560]{1,0:T(8,128)(2,1)S(1)} %attend_edges.1.refs_1_, bf16[64,2560]{1,0:T(8,128)(2,1)S(1)} %broadcast_select_fusion.3.refs_2_, ...), custom_call_target="tpu_custom_call" | custom-call | flops 83886080 | bytes 1966080 | tf_op jit(solution)/shard_map/relay/pallas_call | solution.py:272
  53.0 23.6 %all-reduce.2.cloned.1.call-done = bf16[1,128,2560]{2,1,0:T(8,128)(2,1)} async-done(((bf16[1,128,2560]{2,1,0:T(8,128)(2,1)}), bf16[1,128,2560]{2,1,0:T(8,128)(2,1)}) %all-reduce.2.cloned.1.call-update) | async-done | bytes 655376 | tf_op jit(solution)/shard_map/psum | solution.py:325
  76.6 2.0 %copy.10 = bf16[1,128,2560]{2,1,0:T(8,128)(2,1)} copy(bf16[1,128,2560]{2,1,0:T(8,128)(2,1)} %all-reduce.2.cloned.1.call-done) | data formatting | bytes 1310720
  (24 shorter events, 0.2 us)
Async XLA Ops:
  7.2 69.4 %all-reduce.2.cloned.1.call-start = ((), (), s32[]{:S(2)}) async-start(), calls=%async_computation | async-start | bytes 1310720 | tf_op jit(solution)/shard_map/psum | solution.py:325
  7.9 1.1 %copy-start = (bf16[1,1,128,2560]{3,2,1,0:T(8,128)(2,1)S(1)}, bf16[1,1,128,2560]{3,2,1,0:T(8,128)(2,1)}, u32[]{:S(2)}) copy-start(bf16[1,1,128,2560]{3,2,1,0:T(8,128)(2,1)} %param.8) | copy-start | bytes 1966084
  9.0 1.1 %copy-start.2 = (bf16[1,1,128,2560]{3,2,1,0:T(8,128)(2,1)S(1)}, bf16[1,1,128,2560]{3,2,1,0:T(8,128)(2,1)}, u32[]{:S(2)}) copy-start(bf16[1,1,128,2560]{3,2,1,0:T(8,128)(2,1)} %param.9) | copy-start | bytes 1966084
  10.1 7.1 %copy-start.1 = (bf16[1,1,128,2560]{3,2,1,0:T(8,128)(2,1)S(1)}, bf16[1,1,128,2560]{3,2,1,0:T(8,128)(2,1)}, u32[]{:S(2)}) copy-start(bf16[1,1,128,2560]{3,2,1,0:T(8,128)(2,1)} %param.8) | copy-start | bytes 1966084
  10.1 7.1 %copy-start.4 = (bf16[1,1,128,2560]{3,2,1,0:T(8,128)(2,1)S(1)}, bf16[1,1,128,2560]{3,2,1,0:T(8,128)(2,1)}, u32[]{:S(2)}) copy-start(bf16[1,1,128,2560]{3,2,1,0:T(8,128)(2,1)} %param.7) | copy-start | bytes 1966084
  10.9 14.7 %collective-permute-start.1 = (bf16[32,5248]{1,0:T(8,128)(2,1)}, bf16[32,5248]{1,0:T(8,128)(2,1)S(1)}, u32[]{:S(2)}, u32[]{:S(2)}) collective-permute-start(bf16[32,5248]{1,0:T(8,128)(2,1)} %get-tuple-element.4), channel_id=1, source_target_pairs={{0,2},{2,4},{4,6},{1,3},{3,5},{5,7},{8,10},{10,12},{12,14},{9,11},... | collective-permute-start | bytes 1007624 | tf_op jit(solution)/shard_map/ppermute | solution.py:21
  15.8 11.2 %collective-permute-start.2 = (bf16[32,5248]{1,0:T(8,128)(2,1)S(1)}, bf16[32,5248]{1,0:T(8,128)(2,1)S(1)}, u32[]{:S(2)}, u32[]{:S(2)}) collective-permute-start(bf16[32,5248]{1,0:T(8,128)(2,1)S(1)} %get-tuple-element.5), channel_id=1, source_target_pairs={{2,0},{4,2},{6,4},{3,1},{5,3},{7,5},{10,8},{12,10},{14,12},{11,9},... | collective-permute-start | bytes 1007624 | tf_op jit(solution)/shard_map/ppermute | solution.py:21
  17.2 6.0 %copy-start.6 = (f32[1280]{0:T(1024)S(1)}, f32[1280]{0:T(1024)}, u32[]{:S(2)}) copy-start(f32[1280]{0:T(1024)} %param.12) | copy-start | bytes 15364
  17.2 6.0 %copy-start.7 = (s32[1,1,128]{2,1,0:T(1,128)S(1)}, s32[1,1,128]{2,1,0:T(1,128)}, u32[]{:S(2)}) copy-start(s32[1,1,128]{2,1,0:T(1,128)} %param.11) | copy-start | bytes 1540
  17.2 7.2 %copy-start.5 = (bf16[1,1,128,2560]{3,2,1,0:T(8,128)(2,1)S(1)}, bf16[1,1,128,2560]{3,2,1,0:T(8,128)(2,1)}, u32[]{:S(2)}) copy-start(bf16[1,1,128,2560]{3,2,1,0:T(8,128)(2,1)} %param.13) | copy-start | bytes 1966084
  19.1 14.7 %collective-permute-start.3 = (bf16[64,2560]{1,0:T(8,128)(2,1)S(1)}, bf16[64,2560]{1,0:T(8,128)(2,1)}, u32[]{:S(2)}, u32[]{:S(2)}) collective-permute-start(bf16[64,2560]{1,0:T(8,128)(2,1)S(1)} %attend_middle.1.refs_0_), channel_id=1, source_target_pairs={{0,8},{1,9},{2,10},{3,11},{4,12},{5,13},{6,14},{7,15}} | collective-permute-start | bytes 983048 | tf_op jit(solution)/shard_map/ppermute | solution.py:297
  23.2 1.2 %collective-permute-start = (f32[1280]{0:T(1024)S(1)}, f32[1280]{0:T(1024)S(1)}, u32[]{:S(2)}, u32[]{:S(2)}) collective-permute-start(f32[1280]{0:T(1024)S(1)} %copy-done.6), channel_id=1, source_target_pairs={{0,1},{1,0},{2,3},{3,2},{4,5},{5,4},{6,7},{7,6},{8,9},{9,8},{10,11... | collective-permute-start | bytes 15368 | tf_op jit(solution)/shard_map/ppermute | solution.py:289
  25.6 1.5 %copy-start.3 = (bf16[1,1,128,2560]{3,2,1,0:T(8,128)(2,1)S(1)}, bf16[1,1,128,2560]{3,2,1,0:T(8,128)(2,1)}, u32[]{:S(2)}) copy-start(bf16[1,1,128,2560]{3,2,1,0:T(8,128)(2,1)} %param.9) | copy-start | bytes 1966084
  30.4 11.6 %collective-permute-start.5 = (bf16[64,2560]{1,0:T(8,128)(2,1)S(1)}, bf16[64,2560]{1,0:T(8,128)(2,1)S(1)}, u32[]{:S(2)}, u32[]{:S(2)}) collective-permute-start(bf16[64,2560]{1,0:T(8,128)(2,1)S(1)} %attend_edges.1.refs_1_), channel_id=1, source_target_pairs={{0,8},{1,9},{2,10},{3,11},{4,12},{5,13},{6,14},{7,15}} | collective-permute-start | bytes 983048 | tf_op jit(solution)/shard_map/ppermute | solution.py:297
  33.8 9.5 %collective-permute-start.4 = (bf16[64,2560]{1,0:T(8,128)(2,1)S(1)}, bf16[64,2560]{1,0:T(8,128)(2,1)S(1)}, u32[]{:S(2)}, u32[]{:S(2)}) collective-permute-start(bf16[64,2560]{1,0:T(8,128)(2,1)S(1)} %broadcast_select_fusion.1), channel_id=1, source_target_pairs={{0,16},{8,24},{1,17},{9,25},{2,18},{10,26},{3,19},{11,27},{4,20},{... | collective-permute-start | bytes 983048 | tf_op jit(solution)/shard_map/ppermute | solution.py:299
  42.0 9.8 %collective-permute-start.6 = (bf16[64,2560]{1,0:T(8,128)(2,1)S(1)}, bf16[64,2560]{1,0:T(8,128)(2,1)S(1)}, u32[]{:S(2)}, u32[]{:S(2)}) collective-permute-start(bf16[64,2560]{1,0:T(8,128)(2,1)S(1)} %broadcast_select_fusion), channel_id=1, source_target_pairs={{0,16},{8,24},{1,17},{9,25},{2,18},{10,26},{3,19},{11,27},{4,20},{... | collective-permute-start | bytes 983048 | tf_op jit(solution)/shard_map/ppermute | solution.py:299
Sparse Core Ops, SparseCore 0:
  25.7 50.8 all-reduce.1

commit v3 on v2

v3 whole, which is shorter than its diff:
```python
import functools
import math

import jax
import jax.numpy as jnp
from jax import lax
from jax.experimental import pallas as pl
from jax.experimental.pallas import tpu as pltpu
from jax.sharding import PartitionSpec as P

HEADS = 32
DH = 80
FRAMES = 20
LANES = 128
VMEM_LIMIT = 48 * 1024 * 1024


def shifted(block, axis, distance):
    devices = range(lax.axis_size(axis))
    route = [(i - distance, i) for i in devices if i - distance in devices]
    return lax.ppermute(block, axis, route)


def lane_windows(heads):
    windows = []
    for head in range(heads):
        first, last = head * DH, (head + 1) * DH
        if windows and last <= windows[-1][0] + 2 * LANES:
            windows[-1][1].append(head)
        else:
            windows.append((first // LANES * LANES, [head]))
    out = []
    for start, members in windows:
        start = min(start, heads * DH - 2 * LANES)
        out.append((start, members))
    return out


def head_masks(rows, period):
    masks = {}
    for start, members in lane_windows(period // DH):
        lane = lax.broadcasted_iota(jnp.int32, (rows, 2 * LANES), 1) + start
        for h in members:
            inside = (lane >= h * DH) & (lane < (h + 1) * DH)
            masks[h] = jnp.where(inside, 1.0, 0.0).astype(jnp.bfloat16)
    return masks


def mixed_period(base, bias, query, key, value, masks, period):
    rows = bias.shape[0]
    factor = math.log2(math.e) / math.sqrt(DH)
    windows = lane_windows(period // DH)
    scores = []
    for start, members in windows:
        lanes = slice(base + start, base + start + 2 * LANES)
        part = query(lanes)
        stacked = jnp.concatenate([part * masks[h] for h in members], axis=0)
        scores.append(
            lax.dot_general(
                stacked, key(lanes), (((1,), (1,)), ((), ())), preferred_element_type=jnp.float32
            )
        )
    weights = []
    for part, (start, members) in zip(scores, windows):
        part = part.reshape(len(members), rows, -1) + bias[None]
        largest = jnp.max(part, axis=-1, keepdims=True)
        powers = jnp.exp2((part - largest) * factor)
        totals = jnp.sum(powers, axis=-1, keepdims=True)
        weight = (powers * (1.0 / totals)).astype(jnp.bfloat16)
        weights.append(weight.reshape(len(members) * rows, -1))
    tiles = {}
    for weight, (start, members) in zip(weights, windows):
        lanes = slice(base + start, base + start + 2 * LANES)
        mixed = jnp.dot(weight, value(lanes), preferred_element_type=jnp.float32)
        for n, h in enumerate(members):
            for t in range(2):
                low = start + t * LANES
                if h * DH >= low + LANES or (h + 1) * DH <= low:
                    continue
                piece = mixed[n * rows : (n + 1) * rows, t * LANES : (t + 1) * LANES]
                if low in tiles:
                    lane = lax.broadcasted_iota(jnp.int32, (rows, LANES), 1) + low
                    tiles[low] = jnp.where(lane >= h * DH, piece, tiles[low])
                else:
                    tiles[low] = piece
    return {low: tile.astype(jnp.bfloat16) for low, tile in tiles.items()}


def frame_code(tag_ref):
    tag = tag_ref[...].astype(jnp.float32)
    return tag + 8.0 * jnp.floor((tag + 0.5) * (1.0 / FRAMES)) + 16.0


def columns(row):
    return jnp.broadcast_to(row, (LANES, row.shape[1])).T


def attend_blocks(blocks, q_ref, out_ref):
    width = q_ref.shape[1]
    period = math.lcm(DH, LANES)
    masks = {}
    work = []
    for top, rows, at, mine, theirs, key, value in blocks:
        if rows not in masks:
            masks[rows] = head_masks(rows, period)
        bias = jnp.where(jnp.abs(mine[:, :1] - theirs.T[:rows]) <= 1.5, 0.0, -1e30)
        work.append((top, rows, at, bias, key, value))
    for base in range(0, width, period):
        for top, rows, at, bias, key, value in work:
            tiles = mixed_period(
                base, bias, lambda lanes: q_ref[top : top + rows, lanes], key, value, masks[rows], period
            )
            for low, tile in tiles.items():
                out_ref[at : at + rows, base + low : base + low + LANES] = tile


def middle_kernel(reach, q_ref, k_ref, v_ref, tag_ref, out_ref):
    rows = q_ref.shape[0] - 2 * reach
    code = columns(frame_code(tag_ref))
    key = lambda lanes: k_ref[:, lanes]
    value = lambda lanes: v_ref[:, lanes]
    attend_blocks(
        [(reach, rows, 0, code[reach : reach + rows], code, key, value)], q_ref, out_ref
    )


def edge_kernel(hops, reach, *refs):
    q_ref, k_ref, v_ref, tag_ref = refs[:4]
    lows = refs[4 : 4 + hops]
    highs = refs[4 + hops : 4 + 2 * hops]
    out_ref = refs[-1]
    tokens, width = q_ref.shape
    code = columns(frame_code(tag_ref))

    def joined(before, first, last, after):
        def lanes_of(ref, own, shift):
            def take(lanes):
                moved = slice(lanes.start + shift, lanes.stop + shift)
                parts = [piece[:, moved] for piece in before]
                parts.append(own[first:last, lanes])
                parts.extend(piece[:, moved] for piece in after)
                return jnp.concatenate(parts, axis=0)

            return take

        parts = [piece[:, 2 * width :].astype(jnp.float32) for piece in before]
        parts.append(code[first:last])
        parts.extend(piece[:, 2 * width :].astype(jnp.float32) for piece in after)
        codes = jnp.concatenate(parts, axis=0)
        return codes, lanes_of(None, k_ref, 0), lanes_of(None, v_ref, width)

    if tokens > 2 * reach:
        last = tokens - reach
        blocks = [
            (0, reach, 0, code[:reach], *joined(lows, 0, 2 * reach, ())),
            (last, reach, reach, code[last:], *joined((), tokens - 2 * reach, tokens, highs)),
        ]
    else:
        blocks = [(0, tokens, 0, code, *joined(lows, 0, tokens, highs))]
    attend_blocks(blocks, q_ref, out_ref)


def attend_cost(tokens, span, width):
    return pl.CostEstimate(
        flops=HEADS * tokens * span * 2 * LANES * 4,
        bytes_accessed=12 * tokens * width,
        transcendentals=HEADS * tokens * span,
    )


VMEM = pl.BlockSpec(memory_space=pltpu.VMEM)
PARAMS = pltpu.CompilerParams(vmem_limit_bytes=VMEM_LIMIT)


def attend_middle(queries, keys, values, tags, reach):
    tokens, width = queries.shape
    return pl.pallas_call(
        functools.partial(middle_kernel, reach),
        in_specs=[VMEM] * 4,
        out_specs=VMEM,
        out_shape=jax.ShapeDtypeStruct((tokens - 2 * reach, width), jnp.bfloat16),
        compiler_params=PARAMS,
        cost_estimate=attend_cost(tokens - 2 * reach, tokens, width),
        name="attend_middle",
    )(queries, keys, values, tags)


def attend_edges(queries, keys, values, tags, lows, highs, reach):
    tokens, width = queries.shape
    rows = min(tokens, 2 * reach)
    return pl.pallas_call(
        functools.partial(edge_kernel, len(lows), reach),
        in_specs=[VMEM] * (4 + 2 * len(lows)),
        out_specs=VMEM,
        out_shape=jax.ShapeDtypeStruct((rows, width), jnp.bfloat16),
        compiler_params=PARAMS,
        cost_estimate=attend_cost(rows, LANES, width),
        name="attend_edges",
    )(queries, keys, values, tags, *lows, *highs)


def pack_kernel(most, k_ref, v_ref, grad_ref, tag_ref, row_ref, sent_ref, tail_ref, head_ref, sems):
    tokens, width = k_ref.shape
    ends = ((tail_ref, tokens - most), (head_ref, 0))
    copies = [pltpu.make_async_copy(grad_ref, sent_ref.at[:, pl.ds(0, width)], sems.at[0])]
    for n, (ref, first) in enumerate(ends):
        for m, source in enumerate((k_ref, v_ref)):
            copies.append(
                pltpu.make_async_copy(
                    source.at[pl.ds(first, most)],
                    ref.at[:, pl.ds(m * width, width)],
                    sems.at[1 + 2 * n + m],
                )
            )
    for copy in copies:
        copy.start()
    code = columns(frame_code(tag_ref)).astype(jnp.bfloat16)
    for ref, first in ends:
        ref[:, 2 * width :] = code[first : first + most]
    row = row_ref[...].astype(jnp.float32)
    place = row - tokens * jnp.floor((row + 0.5) * (1.0 / tokens))
    sent_ref[:, width:] = columns(place).astype(jnp.bfloat16)
    for copy in copies:
        copy.wait()


def pack(keys, values, grads, tags, rows, most):
    tokens, width = keys.shape
    anywhere = pl.BlockSpec(memory_space=pl.ANY)
    ends = jax.ShapeDtypeStruct((most, 2 * width + LANES), jnp.bfloat16)
    return pl.pallas_call(
        functools.partial(pack_kernel, most),
        in_specs=[anywhere] * 3 + [VMEM] * 2,
        out_specs=[VMEM] * 3,
        out_shape=[jax.ShapeDtypeStruct((tokens, width + LANES), jnp.bfloat16), ends, ends],
        scratch_shapes=[pltpu.SemaphoreType.DMA((5,))],
        compiler_params=PARAMS,
        cost_estimate=pl.CostEstimate(
            flops=0, bytes_accessed=4 * tokens * width + 16 * most * width, transcendentals=0
        ),
        name="pack",
    )(keys, values, grads, tags, rows)


def selector(row):
    tokens = row.shape[1]
    wanted = lax.broadcasted_iota(jnp.int32, (tokens, tokens), 0).astype(jnp.float32)
    return jnp.where(wanted == row, 1.0, 0.0)


def sums_kernel(sizes, flag_ref, mine_ref, theirs_ref, gate_ref, *out_refs):
    tokens = mine_ref.shape[0]
    width = gate_ref.shape[1]
    picks, rows = [], []
    for ref in (mine_ref, theirs_ref):
        place = ref[:, width : width + LANES].astype(jnp.float32).T[:1]
        picks.append(selector(place).astype(jnp.bfloat16))
        rows.append(ref[:, :width])
    summed = jnp.dot(
        jnp.concatenate(picks, axis=1),
        jnp.concatenate(rows, axis=0),
        preferred_element_type=jnp.float32,
    )
    term = gate_ref[...] * summed + flag_ref[0] * rows[1].astype(jnp.float32)
    term = term.astype(jnp.bfloat16)
    at = 0
    for ref, size in zip(out_refs, sizes):
        ref[...] = term[at : at + size]
        at += size


def pair_sums(flag, mine, theirs, gate, sizes):
    tokens, width = mine.shape[0], gate.shape[1]
    return pl.pallas_call(
        functools.partial(sums_kernel, sizes),
        in_specs=[pl.BlockSpec(memory_space=pltpu.SMEM)] + [VMEM] * 3,
        out_specs=[VMEM] * len(sizes),
        out_shape=[jax.ShapeDtypeStruct((size, width), jnp.bfloat16) for size in sizes],
        compiler_params=PARAMS,
        cost_estimate=pl.CostEstimate(
            flops=4 * tokens * tokens * width, bytes_accessed=6 * tokens * width, transcendentals=0
        ),
        name="pair_sums",
    )(flag, mine, theirs, gate)


def relay_kernel(reach, row_ref, gate_ref, *refs):
    out_ref = refs[-1]
    count = (len(refs) - 1) // 2
    tokens = out_ref.shape[0]
    row = row_ref[...].astype(jnp.float32)
    rows = row - tokens * jnp.floor((row + 0.5) * (1.0 / tokens))
    if count == 2:
        spots = [(reach, tokens - 2 * reach, 0, 0), (0, reach, 1, 0), (tokens - reach, reach, 1, reach)]
        low, high = rows < reach, rows >= tokens - reach
        place = jnp.where(low, rows + tokens - 2 * reach, jnp.where(high, rows, rows - reach))
    else:
        spots = [(0, tokens, 0, 0)]
        place = rows
    picks = selector(place).T.astype(jnp.bfloat16)
    branch = jnp.concatenate([ref[...] for ref in refs[count : 2 * count]], axis=0)
    relayed = gate_ref[...] * jnp.dot(picks, branch, preferred_element_type=jnp.float32)
    for top, size, piece, at in spots:
        own = refs[piece][at : at + size].astype(jnp.float32)
        out_ref[top : top + size] = (own + relayed[top : top + size]).astype(jnp.bfloat16)


def relay(rows, gate, own, branch, reach):
    tokens = sum(p.shape[0] for p in own)
    width = own[0].shape[1]
    return pl.pallas_call(
        functools.partial(relay_kernel, reach),
        in_specs=[VMEM] * (2 + 2 * len(own)),
        out_specs=VMEM,
        out_shape=jax.ShapeDtypeStruct((tokens, width), jnp.bfloat16),
        compiler_params=PARAMS,
        cost_estimate=pl.CostEstimate(
            flops=2 * tokens * tokens * width, bytes_accessed=6 * tokens * width, transcendentals=0
        ),
        name="relay",
    )(rows, gate, *own, *branch)


def whole_gate(gate):
    ranks = lax.axis_size("rep")
    if ranks != 2:
        return lax.all_gather(gate, "rep", axis=0, tiled=True)
    other = lax.ppermute(gate, "rep", [(0, 1), (1, 0)])
    first = lax.axis_index("rep") == 0
    return jnp.concatenate([jnp.where(first, gate, other), jnp.where(first, other, gate)])


def over_square(block, even, odd):
    ranks = lax.axis_size("rep")
    route = []
    for rank in range(ranks):
        for source, target in odd if rank % 2 else even:
            route.append((source * ranks + rank, target * ranks + rank))
    return lax.ppermute(block, ("grp", "rep"), route)


FIRST_EVEN = [(0, 2), (1, 3)]
FIRST_ODD = [(0, 1), (2, 3)]
SECOND_EVEN = [(0, 1), (2, 3), (3, 2)]
SECOND_ODD = [(0, 2), (1, 3), (3, 1)]
THIRD_EVEN = [(0, 2), (2, 0), (1, 3), (3, 1)]
THIRD_ODD = [(0, 1), (1, 0), (2, 3), (3, 2)]


def local(query_rows, key_rows, value_rows, view_frame, control_row, control_gate, out_grad):
    queries, keys, values = query_rows[0, 0], key_rows[0, 0], value_rows[0, 0]
    tags, rows = view_frame[0], control_row[0]
    tokens, width = queries.shape
    length = tokens * lax.axis_size("seq")
    reach = 2 * (length // 32)
    hops = (reach + tokens - 1) // tokens
    group = lax.axis_index("grp")
    odd = lax.axis_index("rep") % 2
    source = group == 0
    relaying = group == 1 + odd
    root_partner = group == 2 - odd

    gate = whole_gate(control_gate)[None]
    most = min(tokens, reach)
    sent, tail, head = pack(keys, values, out_grad[0, 0], tags, rows, most)
    got = over_square(sent, FIRST_EVEN, FIRST_ODD)
    lows, highs = [], []
    for hop in range(1, hops + 1):
        count = min(tokens, reach - (hop - 1) * tokens)
        lows.insert(0, shifted(tail[most - count :], "seq", hop))
        highs.append(shifted(head[:count], "seq", -hop))

    own = [attend_edges(queries, keys, values, tags, lows, highs, reach)]
    if tokens > 2 * reach:
        own.insert(0, attend_middle(queries, keys, values, tags, reach))
    sizes = [piece.shape[0] for piece in own]
    sums = pair_sums(root_partner.astype(jnp.float32)[None], sent, got, gate, sizes)
    branch, totals = [], []
    for piece, part in zip(own, sums):
        first = over_square(jnp.where(source, piece, part), SECOND_EVEN, SECOND_ODD)
        total = (part.astype(jnp.float32) + first.astype(jnp.float32)).astype(jnp.bfloat16)
        held = jnp.where(source, piece, first)
        last = over_square(jnp.where(source | relaying, held, total), THIRD_EVEN, THIRD_ODD)
        branch.append(jnp.where(source | relaying, held, last))
        totals.append(jnp.where(source | relaying, last, total))
    branch_grad = jnp.concatenate(totals, axis=0)
    block_out = relay(rows, gate, own, branch, reach)
    return (block_out[None, None], branch_grad[None])


def solution(mesh):
    placed = (
        P("rep", "grp", "seq", None),
        P("rep", "grp", "seq", None),
        P("rep", "grp", "seq", None),
        P("rep", "grp", "seq"),
        P("rep", "grp", "seq"),
        P("rep"),
        P("rep", "grp", "seq", None),
    )
    return jax.shard_map(
        local,
        mesh=mesh,
        in_specs=placed,
        out_specs=(P("rep", "grp", "seq", None), P("rep", "seq", None)),
        check_vma=False,
    )
```

time: 85.8 us -> 57.2 us (0.67)
  waiting for transfers between devices: 41.4 us -> 20.8 us
  between operations: 14.2 us -> 0.85 us
  starting transfers between devices: 16.4 us -> 18.9 us
  Pallas kernels: 8.35 us -> 9.89 us
    psum x1 -> x0, waiting for transfers between devices: 23.6 us -> none  [local(): branch_grad = lax.psum(terms, 'grp')]
    ppermute x2, waiting for transfers between devices: 1.47 us -> 8.93 us  [shifted(): return lax.ppermute(block, axis, route)]
    ppermute x4 -> x5, starting transfers between devices: 10.2 us -> 14.2 us  [over_square(): return lax.ppermute(block, ('grp', 'rep'), route)]
    ppermute x4 -> x5, waiting for transfers between devices: 15.2 us -> 11.9 us  [over_square(): return lax.ppermute(block, ('grp', 'rep'), route)]
    pallas_call x3, Pallas kernels: 5.27 us -> 6.8 us  [the longest x1 4.04 us: attend_edges(): pl.pallas_call(functools.partial(edge_kernel, len(lows), reach), in_specs...]
    ppermute x2, starting transfers between devices: 6.23 us -> 4.78 us  [shifted(): return lax.ppermute(block, axis, route)]
    ppermute x1, waiting for transfers between devices: 1.14 us -> 0.01 us  [whole_gate(): other = lax.ppermute(gate, 'rep', [(0, 1), (1, 0)])]
    broadcast_in_dim x0 -> x1, other arithmetic: none -> 0.88 us  [local(): return (block_out[None, None], branch_grad[None])]
  transfers between devices with their start and end apart: 8 -> 8, of which waited for: 5 -> 5; matrix products, arithmetic and copies ran while one was open for 0% -> 1% of each run, Pallas kernels for 9% -> 10%
where the time goes in v3:
time: 57.2 us; the launch traced here: 56.7 us
  waiting for transfers between devices  20.8 us (36%)
  starting transfers between devices  18.9 us (33%)
  Pallas kernels  9.89 us (17%)
  local copies, waits for them, and re-layouts  4.6 us (8%)
  other arithmetic  1.63 us (3%)
  between operations  0.85 us (1%)
    ppermute x5, starting transfers between devices, over_square(): return lax.ppermute(block, ('grp', 'rep'), route)  14.2 us
    ppermute x5, waiting for transfers between devices, over_square(): return lax.ppermute(block, ('grp', 'rep'), route)  11.9 us
    ppermute x2, waiting for transfers between devices, shifted(): return lax.ppermute(block, axis, route)  8.93 us
    ppermute x2, starting transfers between devices, shifted(): return lax.ppermute(block, axis, route)  4.78 us
    unnamed x22, local copies, waits for them, and re-layouts  4.59 us
    pallas_call x1, Pallas kernels, attend_edges(): pl.pallas_call(functools.partial(edge_kernel, len(lows), reach), in_specs...  4.04 us
    pallas_call x1, Pallas kernels, attend_middle(): pl.pallas_call(functools.partial(middle_kernel, reach), in_specs=[VMEM] *...  1.87 us
    pallas_call x1, Pallas kernels, pair_sums(): pl.pallas_call(functools.partial(sums_kernel, sizes), in_specs=[pl.BlockS...  1.5 us
  transfers between devices with their start and end apart: 8, of which 5 were waited for; matrix products, arithmetic and copies ran while one was open for 1% of the time, Pallas kernels for 10%

profile of v3, /device:TPU:0, one launch (start us, length us, event | category | flops | bytes accessed | tf_op | source)
XLA Modules:
  0.0 56.7 jit_solution(13069201851143584330)
XLA Ops:
  0.6 1.1 %copy-done = bf16[1,1,128,2560]{3,2,1,0:T(8,128)(2,1)S(1)} copy-done((bf16[1,1,128,2560]{3,2,1,0:T(8,128)(2,1)S(1)}, bf16[1,1,128,2560]{3,2,1,0:T(8,128)(2,1)}, u32[]{:S(2)}) %copy-start) | copy-done | bytes 655384
  1.7 1.1 %copy-done.2 = bf16[1,1,128,2560]{3,2,1,0:T(8,128)(2,1)S(1)} copy-done((bf16[1,1,128,2560]{3,2,1,0:T(8,128)(2,1)S(1)}, bf16[1,1,128,2560]{3,2,1,0:T(8,128)(2,1)}, u32[]{:S(2)}) %copy-start.2) | copy-done | bytes 655384
  2.8 1.1 %copy-done.5 = bf16[1,1,128,2560]{3,2,1,0:T(8,128)(2,1)S(1)} copy-done((bf16[1,1,128,2560]{3,2,1,0:T(8,128)(2,1)S(1)}, bf16[1,1,128,2560]{3,2,1,0:T(8,128)(2,1)}, u32[]{:S(2)}) %copy-start.5) | copy-done | bytes 655384
  3.9 0.7 %copy-done.6 = s32[1,1,128]{2,1,0:T(1,128)S(1)} copy-done((s32[1,1,128]{2,1,0:T(1,128)S(1)}, s32[1,1,128]{2,1,0:T(1,128)}, u32[]{:S(2)}) %copy-start.6) | copy-done | bytes 536
  4.6 0.7 %copy-done.8 = s32[1,1,128]{2,1,0:T(1,128)S(1)} copy-done((s32[1,1,128]{2,1,0:T(1,128)S(1)}, s32[1,1,128]{2,1,0:T(1,128)}, u32[]{:S(2)}) %copy-start.8) | copy-done | bytes 536
  5.2 1.3 %pack.1 = (bf16[128,2688]{1,0:T(8,128)(2,1)S(1)}, bf16[32,5248]{1,0:T(8,128)(2,1)}, bf16[32,5248]{1,0:T(8,128)(2,1)}) custom-call(bf16[128,2560]{1,0:T(8,128)(2,1)S(1)} %bitcast.10, bf16[128,2560]{1,0:T(8,128)(2,1)S(1)} %bitcast.13, bf16[128,2560]{1,0:T(8,128)(2,1)S(1)} %bitcast.18, s32[1,128]{1,0:T(1,128)S(1)} %bitcast.19, s32[1,128]{1,0:T(1,128)S(1)} %bitcast.22), custom_call_target="tpu_custom_call" | custom-call | bytes 2621440 | tf_op jit(solution)/shard_map/pack/pallas_call | solution.py:231
  6.5 5.7 %collective-permute-start.3 = (bf16[128,2688]{1,0:T(8,128)(2,1)S(1)}, bf16[128,2688]{1,0:T(8,128)(2,1)}, u32[]{:S(2)}, u32[]{:S(2)}) collective-permute-start(bf16[128,2688]{1,0:T(8,128)(2,1)S(1)} %get-tuple-element.9.mine_ref), channel_id=1, source_target_pairs={{0,16},{8,24},{1,9},{17,25},{2,18},{10,26},{3,11},{19,27},{4,20},{... | collective-permute-start | bytes 2064392 | tf_op jit(solution)/shard_map/ppermute | solution.py:339
  12.2 3.5 %collective-permute-start.1 = (bf16[32,5248]{1,0:T(8,128)(2,1)}, bf16[32,5248]{1,0:T(8,128)(2,1)S(1)}, u32[]{:S(2)}, u32[]{:S(2)}) collective-permute-start(bf16[32,5248]{1,0:T(8,128)(2,1)} %get-tuple-element.7), channel_id=1, source_target_pairs={{0,2},{2,4},{4,6},{1,3},{3,5},{5,7},{8,10},{10,12},{12,14},{9,11},... | collective-permute-start | bytes 1007624 | tf_op jit(solution)/shard_map/ppermute | solution.py:21
  15.7 1.3 %collective-permute-start.2 = (bf16[32,5248]{1,0:T(8,128)(2,1)}, bf16[32,5248]{1,0:T(8,128)(2,1)}, u32[]{:S(2)}, u32[]{:S(2)}) collective-permute-start(bf16[32,5248]{1,0:T(8,128)(2,1)} %get-tuple-element.8), channel_id=1, source_target_pairs={{2,0},{4,2},{6,4},{3,1},{5,3},{7,5},{10,8},{12,10},{14,12},{11,9},... | collective-permute-start | bytes 1007624 | tf_op jit(solution)/shard_map/ppermute | solution.py:21
  17.1 1.9 %attend_middle.1.refs_0_ = bf16[64,2560]{1,0:T(8,128)(2,1)S(1)} custom-call(bf16[128,2560]{1,0:T(8,128)(2,1)S(1)} %bitcast.16, bf16[128,2560]{1,0:T(8,128)(2,1)S(1)} %bitcast.11, bf16[128,2560]{1,0:T(8,128)(2,1)S(1)} %bitcast.14, s32[1,128]{1,0:T(1,128)S(1)} %bitcast.20), custom_call_target="tpu_custom_call" | custom-call | flops 268435456 | bytes 1966080 | tf_op jit(solution)/shard_map/attend_middle/pallas_call | solution.py:177
  19.0 4.8 %collective-permute-done.1.refs_4_ = bf16[32,5248]{1,0:T(8,128)(2,1)S(1)} collective-permute-done((bf16[32,5248]{1,0:T(8,128)(2,1)}, bf16[32,5248]{1,0:T(8,128)(2,1)S(1)}, u32[]{:S(2)}, u32[]{:S(2)}) %collective-permute-start.1) | collective-permute-done | bytes 335904 | tf_op jit(solution)/shard_map/ppermute | solution.py:21
  23.8 4.1 %collective-permute-done.2.refs_5_ = bf16[32,5248]{1,0:T(8,128)(2,1)} collective-permute-done((bf16[32,5248]{1,0:T(8,128)(2,1)}, bf16[32,5248]{1,0:T(8,128)(2,1)}, u32[]{:S(2)}, u32[]{:S(2)}) %collective-permute-start.2) | collective-permute-done | bytes 335904 | tf_op jit(solution)/shard_map/ppermute | solution.py:21
  28.0 4.0 %attend_edges.1.refs_1_ = bf16[64,2560]{1,0:T(8,128)(2,1)S(1)} custom-call(bf16[128,2560]{1,0:T(8,128)(2,1)S(1)} %bitcast.17, bf16[128,2560]{1,0:T(8,128)(2,1)S(1)} %bitcast.12, bf16[128,2560]{1,0:T(8,128)(2,1)S(1)} %bitcast.15, s32[1,128]{1,0:T(1,128)S(1)} %bitcast.21, bf16[32,5248]{1,0:T(8,128)(2,1)S(1)} %collective-permute-done.1.refs_4_, ...), custom_call_target="tpu_custom_call" | custom-call | flops 268435456 | bytes 1966080 | tf_op jit(solution)/shard_map/attend_edges/pallas_call | solution.py:191
  32.0 1.5 %pair_sums.1 = (bf16[64,2560]{1,0:T(8,128)(2,1)S(1)}, bf16[64,2560]{1,0:T(8,128)(2,1)S(1)}) custom-call(f32[1]{0:T(128)} %bitcast.6.flag_ref, bf16[128,2688]{1,0:T(8,128)(2,1)S(1)} %get-tuple-element.9.mine_ref, bf16[128,2688]{1,0:T(8,128)(2,1)} %collective-permute-done.3.theirs_ref, f32[1,2560]{1,0:T(1,128)S(1)} %broadcast_in_dim.14.gate_ref), custom_call_target="tpu_custom_call" | custom-call | flops 167772160 | bytes 1966080 | tf_op jit(solution)/shard_map/pair_sums/pallas_call | solution.py:274
  33.6 3.4 %collective-permute-start.6 = (bf16[64,2560]{1,0:T(8,128)(2,1)S(1)}, bf16[64,2560]{1,0:T(8,128)(2,1)S(1)}, u32[]{:S(2)}, u32[]{:S(2)}) collective-permute-start(bf16[64,2560]{1,0:T(8,128)(2,1)S(1)} %broadcast_select_fusion.1), channel_id=1, source_target_pairs={{0,8},{16,24},{24,16},{1,17},{9,25},{25,9},{2,10},{18,26},{26,18},... | collective-permute-start | bytes 983048 | tf_op jit(solution)/shard_map/ppermute | solution.py:339
  37.0 1.3 %collective-permute-start.4 = (bf16[64,2560]{1,0:T(8,128)(2,1)S(1)}, bf16[64,2560]{1,0:T(8,128)(2,1)S(1)}, u32[]{:S(2)}, u32[]{:S(2)}) collective-permute-start(bf16[64,2560]{1,0:T(8,128)(2,1)S(1)} %broadcast_select_fusion.3), channel_id=1, source_target_pairs={{0,8},{16,24},{24,16},{1,17},{9,25},{25,9},{2,10},{18,26},{26,18},... | collective-permute-start | bytes 983048 | tf_op jit(solution)/shard_map/ppermute | solution.py:339
  38.4 3.2 %collective-permute-done.6 = bf16[64,2560]{1,0:T(8,128)(2,1)S(1)} collective-permute-done((bf16[64,2560]{1,0:T(8,128)(2,1)S(1)}, bf16[64,2560]{1,0:T(8,128)(2,1)S(1)}, u32[]{:S(2)}, u32[]{:S(2)}) %collective-permute-start.6) | collective-permute-done | bytes 327712 | tf_op jit(solution)/shard_map/ppermute | solution.py:339
  41.7 1.6 %collective-permute-start.7 = (bf16[64,2560]{1,0:T(8,128)(2,1)S(1)}, bf16[64,2560]{1,0:T(8,128)(2,1)S(1)}, u32[]{:S(2)}, u32[]{:S(2)}) collective-permute-start(bf16[64,2560]{1,0:T(8,128)(2,1)S(1)} %broadcast_select_fusion.7), channel_id=1, source_target_pairs={{0,16},{16,0},{8,24},{24,8},{1,9},{9,1},{17,25},{25,17},{2,18},{18... | collective-permute-start | bytes 983048 | tf_op jit(solution)/shard_map/ppermute | solution.py:339
  43.3 3.9 %collective-permute-done.4 = bf16[64,2560]{1,0:T(8,128)(2,1)S(1)} collective-permute-done((bf16[64,2560]{1,0:T(8,128)(2,1)S(1)}, bf16[64,2560]{1,0:T(8,128)(2,1)S(1)}, u32[]{:S(2)}, u32[]{:S(2)}) %collective-permute-start.4) | collective-permute-done | bytes 327712 | tf_op jit(solution)/shard_map/ppermute | solution.py:339
  47.3 2.1 %collective-permute-start.5 = (bf16[64,2560]{1,0:T(8,128)(2,1)S(1)}, bf16[64,2560]{1,0:T(8,128)(2,1)S(1)}, u32[]{:S(2)}, u32[]{:S(2)}) collective-permute-start(bf16[64,2560]{1,0:T(8,128)(2,1)S(1)} %broadcast_select_fusion.9), channel_id=1, source_target_pairs={{0,16},{16,0},{8,24},{24,8},{1,9},{9,1},{17,25},{25,17},{2,18},{18... | collective-permute-start | bytes 983048 | tf_op jit(solution)/shard_map/ppermute | solution.py:339
  49.4 0.2 broadcast_select_fusion.4
  49.6 4.8 %collective-permute-done.5 = bf16[64,2560]{1,0:T(8,128)(2,1)S(1)} collective-permute-done((bf16[64,2560]{1,0:T(8,128)(2,1)S(1)}, bf16[64,2560]{1,0:T(8,128)(2,1)S(1)}, u32[]{:S(2)}, u32[]{:S(2)}) %collective-permute-start.5) | collective-permute-done | bytes 327712 | tf_op jit(solution)/shard_map/ppermute | solution.py:339
  54.6 1.2 %relay.1 = bf16[128,2560]{1,0:T(8,128)(2,1)} custom-call(s32[1,128]{1,0:T(1,128)S(1)} %bitcast.23, f32[1,2560]{1,0:T(1,128)S(1)} %broadcast_in_dim.14.gate_ref, bf16[64,2560]{1,0:T(8,128)(2,1)S(1)} %attend_middle.1.refs_0_, bf16[64,2560]{1,0:T(8,128)(2,1)S(1)} %attend_edges.1.refs_1_, bf16[64,2560]{1,0:T(8,128)(2,1)S(1)} %get-tuple-element.13.refs_2_, ...), custom_call_target="tpu_custom_call" | custom-call | flops 83886080 | bytes 1966080 | tf_op jit(solution)/shard_map/relay/pallas_call | solution.py:311
  55.9 0.9 %maximum_bitcast_fusion = bf16[1,128,2560]{2,1,0:T(8,128)(2,1)} fusion(bf16[64,2560]{1,0:T(8,128)(2,1)S(1)} %get-tuple-element.14, bf16[64,2560]{1,0:T(8,128)(2,1)S(1)} %get-tuple-element.12), kind=kLoop, calls=%fused_computation | loop fusion | flops 1310720 | bytes 1310720 | tf_op jit(solution)/shard_map/broadcast_in_dim | solution.py:388
  (29 shorter events, 0.6 us)
Async XLA Ops:
  0.6 1.1 %copy-start = (bf16[1,1,128,2560]{3,2,1,0:T(8,128)(2,1)S(1)}, bf16[1,1,128,2560]{3,2,1,0:T(8,128)(2,1)}, u32[]{:S(2)}) copy-start(bf16[1,1,128,2560]{3,2,1,0:T(8,128)(2,1)} %param.8) | copy-start | bytes 1966084
  1.7 1.1 %copy-start.2 = (bf16[1,1,128,2560]{3,2,1,0:T(8,128)(2,1)S(1)}, bf16[1,1,128,2560]{3,2,1,0:T(8,128)(2,1)}, u32[]{:S(2)}) copy-start(bf16[1,1,128,2560]{3,2,1,0:T(8,128)(2,1)} %param.9) | copy-start | bytes 1966084
  2.8 1.1 %copy-start.5 = (bf16[1,1,128,2560]{3,2,1,0:T(8,128)(2,1)S(1)}, bf16[1,1,128,2560]{3,2,1,0:T(8,128)(2,1)}, u32[]{:S(2)}) copy-start(bf16[1,1,128,2560]{3,2,1,0:T(8,128)(2,1)} %param.13) | copy-start | bytes 1966084
  3.9 0.7 %copy-start.6 = (s32[1,1,128]{2,1,0:T(1,128)S(1)}, s32[1,1,128]{2,1,0:T(1,128)}, u32[]{:S(2)}) copy-start(s32[1,1,128]{2,1,0:T(1,128)} %param.10) | copy-start | bytes 1540
  4.6 0.7 %copy-start.8 = (s32[1,1,128]{2,1,0:T(1,128)S(1)}, s32[1,1,128]{2,1,0:T(1,128)}, u32[]{:S(2)}) copy-start(s32[1,1,128]{2,1,0:T(1,128)} %param.11) | copy-start | bytes 1540
  5.2 7.0 %copy-start.10 = (f32[1280]{0:T(1024)S(1)}, f32[1280]{0:T(1024)}, u32[]{:S(2)}) copy-start(f32[1280]{0:T(1024)} %param.12) | copy-start | bytes 15364
  5.2 11.8 %copy-start.1 = (bf16[1,1,128,2560]{3,2,1,0:T(8,128)(2,1)S(1)}, bf16[1,1,128,2560]{3,2,1,0:T(8,128)(2,1)}, u32[]{:S(2)}) copy-start(bf16[1,1,128,2560]{3,2,1,0:T(8,128)(2,1)} %param.8) | copy-start | bytes 1966084
  5.2 11.8 %copy-start.4 = (bf16[1,1,128,2560]{3,2,1,0:T(8,128)(2,1)S(1)}, bf16[1,1,128,2560]{3,2,1,0:T(8,128)(2,1)}, u32[]{:S(2)}) copy-start(bf16[1,1,128,2560]{3,2,1,0:T(8,128)(2,1)} %param.7) | copy-start | bytes 1966084
  6.5 25.5 %collective-permute-start.3 = (bf16[128,2688]{1,0:T(8,128)(2,1)S(1)}, bf16[128,2688]{1,0:T(8,128)(2,1)}, u32[]{:S(2)}, u32[]{:S(2)}) collective-permute-start(bf16[128,2688]{1,0:T(8,128)(2,1)S(1)} %get-tuple-element.9.mine_ref), channel_id=1, source_target_pairs={{0,16},{8,24},{1,9},{17,25},{2,18},{10,26},{3,11},{19,27},{4,20},{... | collective-permute-start | bytes 2064392 | tf_op jit(solution)/shard_map/ppermute | solution.py:339
  12.2 6.7 %collective-permute-start = (f32[1280]{0:T(1024)S(1)}, f32[1280]{0:T(1024)S(1)}, u32[]{:S(2)}, u32[]{:S(2)}) collective-permute-start(f32[1280]{0:T(1024)S(1)} %copy-done.10), channel_id=1, source_target_pairs={{0,1},{1,0},{2,3},{3,2},{4,5},{5,4},{6,7},{7,6},{8,9},{9,8},{10,11... | collective-permute-start | bytes 15368 | tf_op jit(solution)/shard_map/ppermute | solution.py:328
  12.2 11.6 %collective-permute-start.1 = (bf16[32,5248]{1,0:T(8,128)(2,1)}, bf16[32,5248]{1,0:T(8,128)(2,1)S(1)}, u32[]{:S(2)}, u32[]{:S(2)}) collective-permute-start(bf16[32,5248]{1,0:T(8,128)(2,1)} %get-tuple-element.7), channel_id=1, source_target_pairs={{0,2},{2,4},{4,6},{1,3},{3,5},{5,7},{8,10},{10,12},{12,14},{9,11},... | collective-permute-start | bytes 1007624 | tf_op jit(solution)/shard_map/ppermute | solution.py:21
  15.7 12.2 %collective-permute-start.2 = (bf16[32,5248]{1,0:T(8,128)(2,1)}, bf16[32,5248]{1,0:T(8,128)(2,1)}, u32[]{:S(2)}, u32[]{:S(2)}) collective-permute-start(bf16[32,5248]{1,0:T(8,128)(2,1)} %get-tuple-element.8), channel_id=1, source_target_pairs={{2,0},{4,2},{6,4},{3,1},{5,3},{7,5},{10,8},{12,10},{14,12},{11,9},... | collective-permute-start | bytes 1007624 | tf_op jit(solution)/shard_map/ppermute | solution.py:21
  17.0 10.9 %copy-start.3 = (bf16[1,1,128,2560]{3,2,1,0:T(8,128)(2,1)S(1)}, bf16[1,1,128,2560]{3,2,1,0:T(8,128)(2,1)}, u32[]{:S(2)}) copy-start(bf16[1,1,128,2560]{3,2,1,0:T(8,128)(2,1)} %param.9) | copy-start | bytes 1966084
  17.1 10.9 %copy-start.7 = (s32[1,1,128]{2,1,0:T(1,128)S(1)}, s32[1,1,128]{2,1,0:T(1,128)}, u32[]{:S(2)}) copy-start(s32[1,1,128]{2,1,0:T(1,128)} %param.10) | copy-start | bytes 1540
  33.6 8.0 %collective-permute-start.6 = (bf16[64,2560]{1,0:T(8,128)(2,1)S(1)}, bf16[64,2560]{1,0:T(8,128)(2,1)S(1)}, u32[]{:S(2)}, u32[]{:S(2)}) collective-permute-start(bf16[64,2560]{1,0:T(8,128)(2,1)S(1)} %broadcast_select_fusion.1), channel_id=1, source_target_pairs={{0,8},{16,24},{24,16},{1,17},{9,25},{25,9},{2,10},{18,26},{26,18},... | collective-permute-start | bytes 983048 | tf_op jit(solution)/shard_map/ppermute | solution.py:339
  37.0 10.1 %collective-permute-start.4 = (bf16[64,2560]{1,0:T(8,128)(2,1)S(1)}, bf16[64,2560]{1,0:T(8,128)(2,1)S(1)}, u32[]{:S(2)}, u32[]{:S(2)}) collective-permute-start(bf16[64,2560]{1,0:T(8,128)(2,1)S(1)} %broadcast_select_fusion.3), channel_id=1, source_target_pairs={{0,8},{16,24},{24,16},{1,17},{9,25},{25,9},{2,10},{18,26},{26,18},... | collective-permute-start | bytes 983048 | tf_op jit(solution)/shard_map/ppermute | solution.py:339
  41.7 7.7 %collective-permute-start.7 = (bf16[64,2560]{1,0:T(8,128)(2,1)S(1)}, bf16[64,2560]{1,0:T(8,128)(2,1)S(1)}, u32[]{:S(2)}, u32[]{:S(2)}) collective-permute-start(bf16[64,2560]{1,0:T(8,128)(2,1)S(1)} %broadcast_select_fusion.7), channel_id=1, source_target_pairs={{0,16},{16,0},{8,24},{24,8},{1,9},{9,1},{17,25},{25,17},{2,18},{18... | collective-permute-start | bytes 983048 | tf_op jit(solution)/shard_map/ppermute | solution.py:339
  47.3 7.1 %collective-permute-start.5 = (bf16[64,2560]{1,0:T(8,128)(2,1)S(1)}, bf16[64,2560]{1,0:T(8,128)(2,1)S(1)}, u32[]{:S(2)}, u32[]{:S(2)}) collective-permute-start(bf16[64,2560]{1,0:T(8,128)(2,1)S(1)} %broadcast_select_fusion.9), channel_id=1, source_target_pairs={{0,16},{16,0},{8,24},{24,8},{1,9},{9,1},{17,25},{25,17},{2,18},{18... | collective-permute-start | bytes 983048 | tf_op jit(solution)/shard_map/ppermute | solution.py:339
  49.6 5.1 %copy-start.9 = (s32[1,1,128]{2,1,0:T(1,128)S(1)}, s32[1,1,128]{2,1,0:T(1,128)}, u32[]{:S(2)}) copy-start(s32[1,1,128]{2,1,0:T(1,128)} %param.11) | copy-start | bytes 1540

commit v4 on v3

--- a/solution.py
+++ b/solution.py
@@ -13,6 +13,7 @@
 FRAMES = 20
 LANES = 128
 VMEM_LIMIT = 48 * 1024 * 1024
+PACK_LIMIT = 62 * 1024 * 1024
 
 
 def shifted(block, axis, distance):
@@ -91,6 +92,12 @@
     return tag + 8.0 * jnp.floor((tag + 0.5) * (1.0 / FRAMES)) + 16.0
 
 
+def placed(row_ref):
+    tokens = row_ref.shape[1]
+    row = row_ref[...].astype(jnp.float32)
+    return row - tokens * jnp.floor((row + 0.5) * (1.0 / tokens))
+
+
 def columns(row):
     return jnp.broadcast_to(row, (LANES, row.shape[1])).T
 
@@ -151,9 +158,10 @@
 
     if tokens > 2 * reach:
         last = tokens - reach
+        held = min(tokens, -(-3 * reach // LANES) * LANES - reach)
         blocks = [
-            (0, reach, 0, code[:reach], *joined(lows, 0, 2 * reach, ())),
-            (last, reach, reach, code[last:], *joined((), tokens - 2 * reach, tokens, highs)),
+            (0, reach, 0, code[:reach], *joined(lows, 0, held, ())),
+            (last, reach, reach, code[last:], *joined((), tokens - held, tokens, highs)),
         ]
     else:
         blocks = [(0, tokens, 0, code, *joined(lows, 0, tokens, highs))]
@@ -199,42 +207,72 @@
     )(queries, keys, values, tags, *lows, *highs)
 
 
-def pack_kernel(most, k_ref, v_ref, grad_ref, tag_ref, row_ref, sent_ref, tail_ref, head_ref, sems):
+def pack_kernel(most, k_ref, v_ref, grad_ref, tag_ref, row_ref, *refs):
+    first_ref, second_ref, tail_ref, head_ref, tags, rows, codes, places, sems, small_sems = refs
     tokens, width = k_ref.shape
+    half = width // 2
     ends = ((tail_ref, tokens - most), (head_ref, 0))
-    copies = [pltpu.make_async_copy(grad_ref, sent_ref.at[:, pl.ds(0, width)], sems.at[0])]
+    small = [
+        pltpu.make_async_copy(tag_ref, tags, small_sems.at[0]),
+        pltpu.make_async_copy(row_ref, rows, small_sems.at[1]),
+    ]
+    copies = []
     for n, (ref, first) in enumerate(ends):
         for m, source in enumerate((k_ref, v_ref)):
             copies.append(
                 pltpu.make_async_copy(
                     source.at[pl.ds(first, most)],
                     ref.at[:, pl.ds(m * width, width)],
-                    sems.at[1 + 2 * n + m],
+                    sems.at[2 * n + m],
                 )
             )
-    for copy in copies:
+    for n, ref in enumerate((first_ref, second_ref)):
+        copies.append(
+            pltpu.make_async_copy(
+                grad_ref.at[:, pl.ds(n * half, half)], ref.at[:, pl.ds(0, half)], sems.at[4 + n]
+            )
+        )
+    for copy in small + copies:
         copy.start()
-    code = columns(frame_code(tag_ref)).astype(jnp.bfloat16)
-    for ref, first in ends:
-        ref[:, 2 * width :] = code[first : first + most]
-    row = row_ref[...].astype(jnp.float32)
-    place = row - tokens * jnp.floor((row + 0.5) * (1.0 / tokens))
-    sent_ref[:, width:] = columns(place).astype(jnp.bfloat16)
-    for copy in copies:
+    for copy in small:
+        copy.wait()
+    codes[...] = columns(frame_code(tags)).astype(jnp.bfloat16)
+    places[...] = columns(placed(rows)).astype(jnp.bfloat16)
+    marks = []
+    for n, (ref, first) in enumerate(ends):
+        marks.append(
+            pltpu.make_async_copy(
+                codes.at[pl.ds(first, most)], ref.at[:, pl.ds(2 * width, LANES)], sems.at[6 + n]
+            )
+        )
+    for n, ref in enumerate((first_ref, second_ref)):
+        marks.append(
+            pltpu.make_async_copy(places, ref.at[:, pl.ds(half, LANES)], sems.at[8 + n])
+        )
+    for copy in marks:
+        copy.start()
+    for copy in copies + marks:
         copy.wait()
 
 
 def pack(keys, values, grads, tags, rows, most):
     tokens, width = keys.shape
-    anywhere = pl.BlockSpec(memory_space=pl.ANY)
     ends = jax.ShapeDtypeStruct((most, 2 * width + LANES), jnp.bfloat16)
+    halves = jax.ShapeDtypeStruct((tokens, width // 2 + LANES), jnp.bfloat16)
     return pl.pallas_call(
         functools.partial(pack_kernel, most),
-        in_specs=[anywhere] * 3 + [VMEM] * 2,
-        out_specs=[VMEM] * 3,
-        out_shape=[jax.ShapeDtypeStruct((tokens, width + LANES), jnp.bfloat16), ends, ends],
-        scratch_shapes=[pltpu.SemaphoreType.DMA((5,))],
-        compiler_params=PARAMS,
+        in_specs=[pl.BlockSpec(memory_space=pltpu.HBM)] * 5,
+        out_specs=[pl.BlockSpec(memory_space=pltpu.HBM)] * 4,
+        out_shape=[halves, halves, ends, ends],
+        scratch_shapes=[
+            pltpu.VMEM((1, tokens), jnp.int32),
+            pltpu.VMEM((1, tokens), jnp.int32),
+            pltpu.VMEM((tokens, LANES), jnp.bfloat16),
+            pltpu.VMEM((tokens, LANES), jnp.bfloat16),
+            pltpu.SemaphoreType.DMA((10,)),
+            pltpu.SemaphoreType.DMA((2,)),
+        ],
+        compiler_params=pltpu.CompilerParams(vmem_limit_bytes=PACK_LIMIT),
         cost_estimate=pl.CostEstimate(
             flops=0, bytes_accessed=4 * tokens * width + 16 * most * width, transcendentals=0
         ),
@@ -248,77 +286,78 @@
     return jnp.where(wanted == row, 1.0, 0.0)
 
 
-def sums_kernel(sizes, flag_ref, mine_ref, theirs_ref, gate_ref, *out_refs):
-    tokens = mine_ref.shape[0]
-    width = gate_ref.shape[1]
-    picks, rows = [], []
-    for ref in (mine_ref, theirs_ref):
-        place = ref[:, width : width + LANES].astype(jnp.float32).T[:1]
-        picks.append(selector(place).astype(jnp.bfloat16))
-        rows.append(ref[:, :width])
-    summed = jnp.dot(
-        jnp.concatenate(picks, axis=1),
-        jnp.concatenate(rows, axis=0),
-        preferred_element_type=jnp.float32,
-    )
-    term = gate_ref[...] * summed + flag_ref[0] * rows[1].astype(jnp.float32)
-    term = term.astype(jnp.bfloat16)
-    at = 0
-    for ref, size in zip(out_refs, sizes):
-        ref[...] = term[at : at + size]
-        at += size
-
-
-def pair_sums(flag, mine, theirs, gate, sizes):
-    tokens, width = mine.shape[0], gate.shape[1]
+def sums_kernel(sizes, flag_ref, gate_ref, *refs):
+    half = gate_ref.shape[1] // 2
+    count = len(sizes)
+    for n in range(2):
+        mine_ref, theirs_ref = refs[2 * n : 2 * n + 2]
+        picks, rows = [], []
+        for ref in (mine_ref, theirs_ref):
+            place = ref[:, half : half + LANES].astype(jnp.float32).T[:1]
+            picks.append(selector(place).astype(jnp.bfloat16))
+            rows.append(ref[:, :half])
+        summed = jnp.dot(
+            jnp.concatenate(picks, axis=1),
+            jnp.concatenate(rows, axis=0),
+            preferred_element_type=jnp.float32,
+        )
+        term = gate_ref[:, n * half : (n + 1) * half] * summed
+        term = (term + flag_ref[n] * rows[1].astype(jnp.float32)).astype(jnp.bfloat16)
+        at = 0
+        for ref, size in zip(refs[4 + n * count : 4 + (n + 1) * count], sizes):
+            ref[...] = term[at : at + size]
+            at += size
+
+
+def pair_sums(flags, gate, parts, sizes):
+    tokens, width = parts[0].shape[0], gate.shape[1]
+    outs = [jax.ShapeDtypeStruct((size, width // 2), jnp.bfloat16) for size in sizes] * 2
     return pl.pallas_call(
         functools.partial(sums_kernel, sizes),
-        in_specs=[pl.BlockSpec(memory_space=pltpu.SMEM)] + [VMEM] * 3,
-        out_specs=[VMEM] * len(sizes),
-        out_shape=[jax.ShapeDtypeStruct((size, width), jnp.bfloat16) for size in sizes],
+        in_specs=[pl.BlockSpec(memory_space=pltpu.SMEM)] + [VMEM] * 5,
+        out_specs=[VMEM] * len(outs),
+        out_shape=outs,
         compiler_params=PARAMS,
         cost_estimate=pl.CostEstimate(
             flops=4 * tokens * tokens * width, bytes_accessed=6 * tokens * width, transcendentals=0
         ),
         name="pair_sums",
-    )(flag, mine, theirs, gate)
-
-
-def relay_kernel(reach, row_ref, gate_ref, *refs):
-    out_ref = refs[-1]
-    count = (len(refs) - 1) // 2
-    tokens = out_ref.shape[0]
-    row = row_ref[...].astype(jnp.float32)
-    rows = row - tokens * jnp.floor((row + 0.5) * (1.0 / tokens))
-    if count == 2:
-        spots = [(reach, tokens - 2 * reach, 0, 0), (0, reach, 1, 0), (tokens - reach, reach, 1, reach)]
-        low, high = rows < reach, rows >= tokens - reach
-        place = jnp.where(low, rows + tokens - 2 * reach, jnp.where(high, rows, rows - reach))
-    else:
-        spots = [(0, tokens, 0, 0)]
-        place = rows
-    picks = selector(place).T.astype(jnp.bfloat16)
-    branch = jnp.concatenate([ref[...] for ref in refs[count : 2 * count]], axis=0)
-    relayed = gate_ref[...] * jnp.dot(picks, branch, preferred_element_type=jnp.float32)
-    for top, size, piece, at in spots:
-        own = refs[piece][at : at + size].astype(jnp.float32)
-        out_ref[top : top + size] = (own + relayed[top : top + size]).astype(jnp.bfloat16)
-
-
-def relay(rows, gate, own, branch, reach):
-    tokens = sum(p.shape[0] for p in own)
-    width = own[0].shape[1]
+    )(flags, gate, *parts)
+
+
+def piece_spots(tokens, reach, piece):
+    if tokens <= 2 * reach:
+        return [(0, tokens, 0)]
+    if piece == 0:
+        return [(reach, tokens - 2 * reach, 0)]
+    return [(0, reach, 0), (tokens - reach, reach, reach)]
+
+
+def relay_kernel(spots, row_ref, gate_ref, first_ref, second_ref, base_ref, out_ref):
+    tokens, width = out_ref.shape
+    half = width // 2
+    picks = selector(placed(row_ref)).T.astype(jnp.bfloat16)
+    picks = jnp.concatenate([picks[:, top : top + size] for top, size, at in spots], axis=1)
+    for n, ref in enumerate((first_ref, second_ref)):
+        lanes = slice(n * half, (n + 1) * half)
+        relayed = jnp.dot(picks, ref[...], preferred_element_type=jnp.float32)
+        total = base_ref[:, lanes].astype(jnp.float32) + gate_ref[:, lanes] * relayed
+        out_ref[:, lanes] = total.astype(out_ref.dtype)
+
+
+def relay(rows, gate, first, second, base, spots, dtype):
+    tokens, width = base.shape
     return pl.pallas_call(
-        functools.partial(relay_kernel, reach),
-        in_specs=[VMEM] * (2 + 2 * len(own)),
+        functools.partial(relay_kernel, spots),
+        in_specs=[VMEM] * 5,
         out_specs=VMEM,
-        out_shape=jax.ShapeDtypeStruct((tokens, width), jnp.bfloat16),
+        out_shape=jax.ShapeDtypeStruct((tokens, width), dtype),
         compiler_params=PARAMS,
         cost_estimate=pl.CostEstimate(
-            flops=2 * tokens * tokens * width, bytes_accessed=6 * tokens * width, transcendentals=0
+            flops=2 * tokens * tokens * width, bytes_accessed=24 * tokens * width, transcendentals=0
         ),
         name="relay",
-    )(rows, gate, *own, *branch)
+    )(rows, gate, first, second, base)
 
 
 def whole_gate(gate):
@@ -330,61 +369,79 @@
     return jnp.concatenate([jnp.where(first, gate, other), jnp.where(first, other, gate)])
 
 
-def over_square(block, even, odd):
-    ranks = lax.axis_size("rep")
-    route = []
-    for rank in range(ranks):
-        for source, target in odd if rank % 2 else even:
-            route.append((source * ranks + rank, target * ranks + rank))
-    return lax.ppermute(block, ("grp", "rep"), route)
-
-
-FIRST_EVEN = [(0, 2), (1, 3)]
-FIRST_ODD = [(0, 1), (2, 3)]
-SECOND_EVEN = [(0, 1), (2, 3), (3, 2)]
-SECOND_ODD = [(0, 2), (1, 3), (3, 1)]
-THIRD_EVEN = [(0, 2), (2, 0), (1, 3), (3, 1)]
-THIRD_ODD = [(0, 1), (1, 0), (2, 3), (3, 2)]
+FIRST_A, FIRST_B = [(0, 1), (2, 3)], [(0, 2), (1, 3)]
+SECOND_A, SECOND_B = [(0, 1), (1, 3), (3, 2)], [(0, 2), (2, 3), (3, 1)]
+SWAP_X, SWAP_Y = [(0, 1), (1, 0), (2, 3), (3, 2)], [(0, 2), (2, 0), (1, 3), (3, 1)]
+
+
+def added(a, b):
+    return (a.astype(jnp.float32) + b.astype(jnp.float32)).astype(a.dtype)
 
 
 def local(query_rows, key_rows, value_rows, view_frame, control_row, control_gate, out_grad):
     queries, keys, values = query_rows[0, 0], key_rows[0, 0], value_rows[0, 0]
     tags, rows = view_frame[0], control_row[0]
     tokens, width = queries.shape
+    half = width // 2
     length = tokens * lax.axis_size("seq")
     reach = 2 * (length // 32)
     hops = (reach + tokens - 1) // tokens
     group = lax.axis_index("grp")
-    odd = lax.axis_index("rep") % 2
-    source = group == 0
-    relaying = group == 1 + odd
-    root_partner = group == 2 - odd
-
-    gate = whole_gate(control_gate)[None]
+    send = lambda block, route: lax.ppermute(block, "grp", route)
+
     most = min(tokens, reach)
-    sent, tail, head = pack(keys, values, out_grad[0, 0], tags, rows, most)
-    got = over_square(sent, FIRST_EVEN, FIRST_ODD)
+    sent_a, sent_b, tail, head = pack(keys, values, out_grad[0, 0], tags, rows, most)
+    got_a, got_b = send(sent_a, FIRST_A), send(sent_b, FIRST_B)
     lows, highs = [], []
     for hop in range(1, hops + 1):
         count = min(tokens, reach - (hop - 1) * tokens)
         lows.insert(0, shifted(tail[most - count :], "seq", hop))
         highs.append(shifted(head[:count], "seq", -hop))
-
-    own = [attend_edges(queries, keys, values, tags, lows, highs, reach)]
+    gate = whole_gate(control_gate)[None]
+
+    own = []
+    sizes = [min(tokens, 2 * reach)]
     if tokens > 2 * reach:
-        own.insert(0, attend_middle(queries, keys, values, tags, reach))
-    sizes = [piece.shape[0] for piece in own]
-    sums = pair_sums(root_partner.astype(jnp.float32)[None], sent, got, gate, sizes)
-    branch, totals = [], []
-    for piece, part in zip(own, sums):
-        first = over_square(jnp.where(source, piece, part), SECOND_EVEN, SECOND_ODD)
-        total = (part.astype(jnp.float32) + first.astype(jnp.float32)).astype(jnp.bfloat16)
-        held = jnp.where(source, piece, first)
-        last = over_square(jnp.where(source | relaying, held, total), THIRD_EVEN, THIRD_ODD)
-        branch.append(jnp.where(source | relaying, held, last))
-        totals.append(jnp.where(source | relaying, last, total))
+        own.append(attend_middle(queries, keys, values, tags, reach))
+        sizes.insert(0, tokens - 2 * reach)
+    flags = jnp.stack([group == 1, group == 2]).astype(jnp.float32)
+    sums = pair_sums(flags, gate, (sent_a, got_a, sent_b, got_b), sizes)
+    tags, *sums = lax.optimization_barrier((tags, *sums))
+    own.append(attend_edges(queries, keys, values, tags, lows, highs, reach))
+
+    count = len(own)
+    spots = [piece_spots(tokens, reach, n) for n in range(count)]
+    order = [
+        own[n][at : at + size] for top, size, n, at in sorted(
+            (top, size, n, at) for n in range(count) for top, size, at in spots[n]
+        )
+    ]
+    block_out = jnp.concatenate(order, axis=0)
+    totals = []
+    for n, (piece, sum_a, sum_b) in enumerate(zip(own, sums[:count], sums[count:])):
+        piece_a, piece_b = piece[:, :half], piece[:, half:]
+        one = send(jnp.where(group == 0, piece_a, jnp.where(group == 1, sum_a, sum_b)), SECOND_A)
+        two = send(jnp.where(group == 0, piece_b, jnp.where(group == 2, sum_b, sum_a)), SECOND_B)
+        total_a = added(sum_a, jnp.where(group == 1, two, one))
+        total_b = added(sum_b, jnp.where(group == 2, one, two))
+        held_a = jnp.where(group == 0, piece_a, one)
+        held_b = jnp.where(group == 0, piece_b, two)
+        across = send(jnp.where((group == 0) | (group == 2), held_b, total_a), SWAP_X)
+        down = send(jnp.where(group <= 1, held_a, total_b), SWAP_Y)
+        branch_a = jnp.where(group <= 1, held_a, down)
+        branch_b = jnp.where((group == 0) | (group == 2), held_b, across)
+        dtype = jnp.bfloat16 if n == count - 1 else jnp.float32
+        block_out = relay(rows, gate, branch_a, branch_b, block_out, spots[n], dtype)
+        totals.append(
+            jnp.concatenate(
+                (
+                    jnp.where((group == 0) | (group == 2), across, total_a),
+                    jnp.where(group <= 1, down, total_b),
+                ),
+                axis=1,
+            )
+        )
     branch_grad = jnp.concatenate(totals, axis=0)
-    block_out = relay(rows, gate, own, branch, reach)
     return (block_out[None, None], branch_grad[None])
 
 

time: 57.2 us -> 90.3 us (1.58)
  Pallas kernels: 9.89 us -> 50.4 us
  waiting for transfers between devices: 20.8 us -> 5.67 us
  starting transfers between devices: 18.9 us -> 31.2 us
  local copies, waits for them, and re-layouts: 4.6 us -> 0.07 us
    pallas_call x2 -> x3, Pallas kernels: 2.48 us -> 42.7 us  [the longest x1 40.9 us: pack(): pl.pallas_call(functools.partial(pack_kernel, most), in_specs=[pl.BlockSp...]
    ppermute x5 -> x10, starting transfers between devices: 14.2 us -> 25.7 us  [local(): send = lambda block, route: lax.ppermute(block, 'grp', route)]
    ppermute x5 -> x10, waiting for transfers between devices: 11.9 us -> 3.47 us  [local(): send = lambda block, route: lax.ppermute(block, 'grp', route)]
    ppermute x2, waiting for transfers between devices: 8.93 us -> 2.19 us  [shifted(): return lax.ppermute(block, axis, route)]
    unnamed x22 -> x16, local copies, waits for them, and re-layouts: 4.59 us -> 0.04 us
  transfers between devices with their start and end apart: 8 -> 13, of which waited for: 5 -> 4; matrix products, arithmetic and copies ran while one was open for 1% -> 1% of each run, Pallas kernels for 10% -> 9%
where the time goes in v4:
time: 90.3 us; the launch traced here: 89.9 us
  Pallas kernels  50.4 us (56%)
  starting transfers between devices  31.2 us (35%)
  waiting for transfers between devices  5.67 us (6%)
  other arithmetic  1.66 us (2%)
  between operations  0.95 us (1%)
    pallas_call x1, Pallas kernels, pack(): pl.pallas_call(functools.partial(pack_kernel, most), in_specs=[pl.BlockSp...  40.9 us
    ppermute x10, starting transfers between devices, local(): send = lambda block, route: lax.ppermute(block, 'grp', route)  25.7 us
    ppermute x2, starting transfers between devices, shifted(): return lax.ppermute(block, axis, route)  5.49 us
    pallas_call x1, Pallas kernels, attend_edges(): pl.pallas_call(functools.partial(edge_kernel, len(lows), reach), in_specs...  4.34 us
    ppermute x10, waiting for transfers between devices, local(): send = lambda block, route: lax.ppermute(block, 'grp', route)  3.47 us
    ppermute x2, waiting for transfers between devices, shifted(): return lax.ppermute(block, axis, route)  2.19 us
    pallas_call x1, Pallas kernels, attend_middle(): pl.pallas_call(functools.partial(middle_kernel, reach), in_specs=[VMEM] *...  1.88 us
  transfers between devices with their start and end apart: 13, of which 4 were waited for; matrix products, arithmetic and copies ran while one was open for 1% of the time, Pallas kernels for 9%

profile of v4, /device:TPU:0, one launch (start us, length us, event | category | flops | bytes accessed | tf_op | source)
XLA Modules:
  0.0 89.9 jit_solution(4677293662882703214)
XLA Ops:
  0.7 40.9 %pack.1 = (bf16[128,1408]{1,0:T(8,128)(2,1)}, bf16[128,1408]{1,0:T(8,128)(2,1)}, bf16[32,5248]{1,0:T(8,128)(2,1)}, bf16[32,5248]{1,0:T(8,128)(2,1)}) custom-call(bf16[128,2560]{1,0:T(8,128)(2,1)} %bitcast.11, bf16[128,2560]{1,0:T(8,128)(2,1)} %bitcast.14, bf16[128,2560]{1,0:T(8,128)(2,1)} %bitcast.25, s32[1,128]{1,0:T(1,128)} %bitcast.19, s32[1,128]{1,0:T(1,128)} %bitcast.22), custom_call_target="tpu_custom_call" | custom-call | bytes 2621440 | tf_op jit(solution)/shard_map/pack/pallas_call | solution.py:262
  41.6 5.7 %collective-permute-start.1 = (bf16[128,1408]{1,0:T(8,128)(2,1)}, bf16[128,1408]{1,0:T(8,128)(2,1)}, u32[]{:S(2)}, u32[]{:S(2)}) collective-permute-start(bf16[128,1408]{1,0:T(8,128)(2,1)} %get-tuple-element.15.refs_0_), channel_id=1, source_target_pairs={{0,8},{16,24},{1,9},{17,25},{2,10},{18,26},{3,11},{19,27},{4,12},{... | collective-permute-start | bytes 1081352 | tf_op jit(solution)/shard_map/ppermute | solution.py:390
  47.4 4.1 %collective-permute-start.2 = (bf16[128,1408]{1,0:T(8,128)(2,1)}, bf16[128,1408]{1,0:T(8,128)(2,1)}, u32[]{:S(2)}, u32[]{:S(2)}) collective-permute-start(bf16[128,1408]{1,0:T(8,128)(2,1)} %get-tuple-element.16.refs_2_), channel_id=1, source_target_pairs={{0,16},{8,24},{1,17},{9,25},{2,18},{10,26},{3,19},{11,27},{4,20},{... | collective-permute-start | bytes 1081352 | tf_op jit(solution)/shard_map/ppermute | solution.py:390
  51.5 4.2 %collective-permute-start.3 = (bf16[32,5248]{1,0:T(8,128)(2,1)}, bf16[32,5248]{1,0:T(8,128)(2,1)}, u32[]{:S(2)}, u32[]{:S(2)}) collective-permute-start(bf16[32,5248]{1,0:T(8,128)(2,1)} %get-tuple-element.22), channel_id=1, source_target_pairs={{0,2},{2,4},{4,6},{1,3},{3,5},{5,7},{8,10},{10,12},{12,14},{9,11},... | collective-permute-start | bytes 1007624 | tf_op jit(solution)/shard_map/ppermute | solution.py:22
  55.7 1.3 %collective-permute-start.4 = (bf16[32,5248]{1,0:T(8,128)(2,1)}, bf16[32,5248]{1,0:T(8,128)(2,1)}, u32[]{:S(2)}, u32[]{:S(2)}) collective-permute-start(bf16[32,5248]{1,0:T(8,128)(2,1)} %get-tuple-element.23), channel_id=1, source_target_pairs={{2,0},{4,2},{6,4},{3,1},{5,3},{7,5},{10,8},{12,10},{14,12},{11,9},... | collective-permute-start | bytes 1007624 | tf_op jit(solution)/shard_map/ppermute | solution.py:22
  57.1 1.9 %attend_middle.1 = bf16[64,2560]{1,0:T(8,128)(2,1)S(1)} custom-call(bf16[128,2560]{1,0:T(8,128)(2,1)S(1)} %bitcast.17, bf16[128,2560]{1,0:T(8,128)(2,1)S(1)} %bitcast.12, bf16[128,2560]{1,0:T(8,128)(2,1)S(1)} %bitcast.15, s32[1,128]{1,0:T(1,128)S(1)} %bitcast.20), custom_call_target="tpu_custom_call" | custom-call | flops 268435456 | bytes 1966080 | tf_op jit(solution)/shard_map/attend_middle/pallas_call | solution.py:185
  59.1 1.5 %pair_sums.1 = (bf16[64,1280]{1,0:T(8,128)(2,1)S(1)}, bf16[64,1280]{1,0:T(8,128)(2,1)S(1)}, bf16[64,1280]{1,0:T(8,128)(2,1)S(1)}, bf16[64,1280]{1,0:T(8,128)(2,1)S(1)}) custom-call(f32[2]{0:T(128)S(1)} %add_convert_fusion.4.flag_ref, f32[1,2560]{1,0:T(1,128)S(1)} %broadcast_in_dim.9.gate_ref, bf16[128,1408]{1,0:T(8,128)(2,1)S(1)} %copy-done.3, ...), custom_call_target="tpu_custom_call" | custom-call | flops 167772160 | bytes 1966080 | tf_op jit(solution)/shard_map/pair_sums/pallas_call | solution.py:315
  60.7 3.8 %collective-permute-start.10 = (bf16[64,1280]{1,0:T(8,128)(2,1)S(1)}, bf16[64,1280]{1,0:T(8,128)(2,1)S(1)}, u32[]{:S(2)}, u32[]{:S(2)}) collective-permute-start(bf16[64,1280]{1,0:T(8,128)(2,1)S(1)} %get-tuple-element.38), channel_id=1, source_target_pairs={{0,16},{16,24},{24,8},{1,17},{17,25},{25,9},{2,18},{18,26},{26,10}... | collective-permute-start | bytes 491528 | tf_op jit(solution)/shard_map/ppermute | solution.py:390
  64.4 1.3 %collective-permute-start.9 = (bf16[64,1280]{1,0:T(8,128)(2,1)S(1)}, bf16[64,1280]{1,0:T(8,128)(2,1)S(1)}, u32[]{:S(2)}, u32[]{:S(2)}) collective-permute-start(bf16[64,1280]{1,0:T(8,128)(2,1)S(1)} %get-tuple-element.39), channel_id=1, source_target_pairs={{0,8},{8,24},{24,16},{1,9},{9,25},{25,17},{2,10},{10,26},{26,18},{... | collective-permute-start | bytes 491528 | tf_op jit(solution)/shard_map/ppermute | solution.py:390
  65.8 2.2 %collective-permute-done.4.refs_5_ = bf16[32,5248]{1,0:T(8,128)(2,1)} collective-permute-done((bf16[32,5248]{1,0:T(8,128)(2,1)}, bf16[32,5248]{1,0:T(8,128)(2,1)}, u32[]{:S(2)}, u32[]{:S(2)}) %collective-permute-start.4) | collective-permute-done | bytes 335904 | tf_op jit(solution)/shard_map/ppermute | solution.py:22
  67.9 4.3 %attend_edges.1 = bf16[64,2560]{1,0:T(8,128)(2,1)S(1)} custom-call(bf16[128,2560]{1,0:T(8,128)(2,1)S(1)} %bitcast.18, bf16[128,2560]{1,0:T(8,128)(2,1)S(1)} %bitcast.13, bf16[128,2560]{1,0:T(8,128)(2,1)S(1)} %bitcast.16, s32[1,128]{1,0:T(1,128)S(1)} %bitcast.21, bf16[32,5248]{1,0:T(8,128)(2,1)} %collective-permute-done.3.refs_4_, ...), custom_call_target="tpu_custom_call" | custom-call | flops 268435456 | bytes 1966080 | tf_op jit(solution)/shard_map/attend_edges/pallas_call | solution.py:199
  72.4 1.3 %collective-permute-start.5 = (bf16[64,1280]{1,0:T(8,128)(2,1)S(1)}, bf16[64,1280]{1,0:T(8,128)(2,1)S(1)}, u32[]{:S(2)}, u32[]{:S(2)}) collective-permute-start(bf16[64,1280]{1,0:T(8,128)(2,1)S(1)} %get-tuple-element.43), channel_id=1, source_target_pairs={{0,8},{8,24},{24,16},{1,9},{9,25},{25,17},{2,10},{10,26},{26,18},{... | collective-permute-start | bytes 491528 | tf_op jit(solution)/shard_map/ppermute | solution.py:390
  73.7 1.3 %collective-permute-start.6 = (bf16[64,1280]{1,0:T(8,128)(2,1)S(1)}, bf16[64,1280]{1,0:T(8,128)(2,1)S(1)}, u32[]{:S(2)}, u32[]{:S(2)}) collective-permute-start(bf16[64,1280]{1,0:T(8,128)(2,1)S(1)} %get-tuple-element.42), channel_id=1, source_target_pairs={{0,16},{16,24},{24,8},{1,17},{17,25},{25,9},{2,18},{18,26},{26,10}... | collective-permute-start | bytes 491528 | tf_op jit(solution)/shard_map/ppermute | solution.py:390
  75.2 2.0 %collective-permute-start.11 = (bf16[64,1280]{1,0:T(8,128)(2,1)S(1)}, bf16[64,1280]{1,0:T(8,128)(2,1)S(1)}, u32[]{:S(2)}, u32[]{:S(2)}) collective-permute-start(bf16[64,1280]{1,0:T(8,128)(2,1)S(1)} %get-tuple-element.36), channel_id=1, source_target_pairs={{0,16},{16,0},{8,24},{24,8},{1,17},{17,1},{9,25},{25,9},{2,18},{18... | collective-permute-start | bytes 491528 | tf_op jit(solution)/shard_map/ppermute | solution.py:390
  77.3 1.7 %collective-permute-start.12 = (bf16[64,1280]{1,0:T(8,128)(2,1)S(1)}, bf16[64,1280]{1,0:T(8,128)(2,1)S(1)}, u32[]{:S(2)}, u32[]{:S(2)}) collective-permute-start(bf16[64,1280]{1,0:T(8,128)(2,1)S(1)} %get-tuple-element.28), channel_id=1, source_target_pairs={{0,8},{8,0},{16,24},{24,16},{1,9},{9,1},{17,25},{25,17},{2,10},{10... | collective-permute-start | bytes 491528 | tf_op jit(solution)/shard_map/ppermute | solution.py:390
  79.0 0.6 collective-permute-done.6
  79.6 0.2 broadcast_select_fusion.5
  79.8 2.5 %collective-permute-start.7 = (bf16[64,1280]{1,0:T(8,128)(2,1)S(1)}, bf16[64,1280]{1,0:T(8,128)(2,1)S(1)}, u32[]{:S(2)}, u32[]{:S(2)}) collective-permute-start(bf16[64,1280]{1,0:T(8,128)(2,1)S(1)} %get-tuple-element.40), channel_id=1, source_target_pairs={{0,16},{16,0},{8,24},{24,8},{1,17},{17,1},{9,25},{25,9},{2,18},{18... | collective-permute-start | bytes 491528 | tf_op jit(solution)/shard_map/ppermute | solution.py:390
  82.3 1.9 %collective-permute-start.8 = (bf16[64,1280]{1,0:T(8,128)(2,1)S(1)}, bf16[64,1280]{1,0:T(8,128)(2,1)S(1)}, u32[]{:S(2)}, u32[]{:S(2)}) collective-permute-start(bf16[64,1280]{1,0:T(8,128)(2,1)S(1)} %get-tuple-element.32), channel_id=1, source_target_pairs={{0,8},{8,0},{16,24},{24,16},{1,9},{9,1},{17,25},{25,17},{2,10},{10... | collective-permute-start | bytes 491528 | tf_op jit(solution)/shard_map/ppermute | solution.py:390
  84.3 0.4 relay.2.base_ref
  84.8 0.9 collective-permute-done.7
  85.6 2.0 %collective-permute-done.8 = bf16[64,1280]{1,0:T(8,128)(2,1)S(1)} collective-permute-done((bf16[64,1280]{1,0:T(8,128)(2,1)S(1)}, bf16[64,1280]{1,0:T(8,128)(2,1)S(1)}, u32[]{:S(2)}, u32[]{:S(2)}) %collective-permute-start.8) | collective-permute-done | bytes 163872 | tf_op jit(solution)/shard_map/ppermute | solution.py:390
  87.8 1.3 %relay.3 = bf16[128,2560]{1,0:T(8,128)(2,1)} custom-call(s32[1,128]{1,0:T(1,128)S(1)} %bitcast.24, f32[1,2560]{1,0:T(1,128)S(1)} %broadcast_in_dim.9.gate_ref, bf16[64,1280]{1,0:T(8,128)(2,1)S(1)} %get-tuple-element.49.first_ref, bf16[64,1280]{1,0:T(8,128)(2,1)S(1)} %get-tuple-element.48.second_ref, f32[128,2560]{1,0:T(8,128)S(1)} %relay.2.base_ref), custom_call_target="tpu_custom_call" | custom-call | flops 83886080 | bytes 7864320 | tf_op jit(solution)/shard_map/relay/pallas_call | solution.py:350
  89.0 0.9 maximum_bitcast_fusion
  (37 shorter events, 0.7 us)
Async XLA Ops:
  0.6 56.5 %copy-start = (bf16[1,1,128,2560]{3,2,1,0:T(8,128)(2,1)S(1)}, bf16[1,1,128,2560]{3,2,1,0:T(8,128)(2,1)}, u32[]{:S(2)}) copy-start(bf16[1,1,128,2560]{3,2,1,0:T(8,128)(2,1)} %param.8) | copy-start | bytes 1966084
  0.6 56.5 %copy-start.1 = (bf16[1,1,128,2560]{3,2,1,0:T(8,128)(2,1)S(1)}, bf16[1,1,128,2560]{3,2,1,0:T(8,128)(2,1)}, u32[]{:S(2)}) copy-start(bf16[1,1,128,2560]{3,2,1,0:T(8,128)(2,1)} %param.9) | copy-start | bytes 1966084
  0.7 56.5 %copy-start.5 = (s32[1,1,128]{2,1,0:T(1,128)S(1)}, s32[1,1,128]{2,1,0:T(1,128)}, u32[]{:S(2)}) copy-start(s32[1,1,128]{2,1,0:T(1,128)} %param.10) | copy-start | bytes 1540
  0.7 50.8 %copy-start.7 = (f32[1280]{0:T(1024)S(1)}, f32[1280]{0:T(1024)}, u32[]{:S(2)}) copy-start(f32[1280]{0:T(1024)} %param.12) | copy-start | bytes 15364
  0.7 56.4 %copy-start.2 = (bf16[1,1,128,2560]{3,2,1,0:T(8,128)(2,1)S(1)}, bf16[1,1,128,2560]{3,2,1,0:T(8,128)(2,1)}, u32[]{:S(2)}) copy-start(bf16[1,1,128,2560]{3,2,1,0:T(8,128)(2,1)} %param.7) | copy-start | bytes 1966084
  41.6 17.5 %copy-start.3 = (bf16[128,1408]{1,0:T(8,128)(2,1)S(1)}, bf16[128,1408]{1,0:T(8,128)(2,1)}, u32[]{:S(2)}) copy-start(bf16[128,1408]{1,0:T(8,128)(2,1)} %get-tuple-element.15.refs_0_) | copy-start | bytes 1081348
  41.6 17.5 %copy-start.4 = (bf16[128,1408]{1,0:T(8,128)(2,1)S(1)}, bf16[128,1408]{1,0:T(8,128)(2,1)}, u32[]{:S(2)}) copy-start(bf16[128,1408]{1,0:T(8,128)(2,1)} %get-tuple-element.16.refs_2_) | copy-start | bytes 1081348
  41.6 17.4 %collective-permute-start.1 = (bf16[128,1408]{1,0:T(8,128)(2,1)}, bf16[128,1408]{1,0:T(8,128)(2,1)}, u32[]{:S(2)}, u32[]{:S(2)}) collective-permute-start(bf16[128,1408]{1,0:T(8,128)(2,1)} %get-tuple-element.15.refs_0_), channel_id=1, source_target_pairs={{0,8},{16,24},{1,9},{17,25},{2,10},{18,26},{3,11},{19,27},{4,12},{... | collective-permute-start | bytes 1081352 | tf_op jit(solution)/shard_map/ppermute | solution.py:390
  47.4 11.7 %collective-permute-start.2 = (bf16[128,1408]{1,0:T(8,128)(2,1)}, bf16[128,1408]{1,0:T(8,128)(2,1)}, u32[]{:S(2)}, u32[]{:S(2)}) collective-permute-start(bf16[128,1408]{1,0:T(8,128)(2,1)} %get-tuple-element.16.refs_2_), channel_id=1, source_target_pairs={{0,16},{8,24},{1,17},{9,25},{2,18},{10,26},{3,19},{11,27},{4,20},{... | collective-permute-start | bytes 1081352 | tf_op jit(solution)/shard_map/ppermute | solution.py:390
  51.5 7.5 %collective-permute-start = (f32[1280]{0:T(1024)S(1)}, f32[1280]{0:T(1024)S(1)}, u32[]{:S(2)}, u32[]{:S(2)}) collective-permute-start(f32[1280]{0:T(1024)S(1)} %copy-done.7), channel_id=1, source_target_pairs={{0,1},{1,0},{2,3},{3,2},{4,5},{5,4},{6,7},{7,6},{8,9},{9,8},{10,11... | collective-permute-start | bytes 15368 | tf_op jit(solution)/shard_map/ppermute | solution.py:367
  51.5 14.2 %collective-permute-start.3 = (bf16[32,5248]{1,0:T(8,128)(2,1)}, bf16[32,5248]{1,0:T(8,128)(2,1)}, u32[]{:S(2)}, u32[]{:S(2)}) collective-permute-start(bf16[32,5248]{1,0:T(8,128)(2,1)} %get-tuple-element.22), channel_id=1, source_target_pairs={{0,2},{2,4},{4,6},{1,3},{3,5},{5,7},{8,10},{10,12},{12,14},{9,11},... | collective-permute-start | bytes 1007624 | tf_op jit(solution)/shard_map/ppermute | solution.py:22
  55.7 12.2 %collective-permute-start.4 = (bf16[32,5248]{1,0:T(8,128)(2,1)}, bf16[32,5248]{1,0:T(8,128)(2,1)}, u32[]{:S(2)}, u32[]{:S(2)}) collective-permute-start(bf16[32,5248]{1,0:T(8,128)(2,1)} %get-tuple-element.23), channel_id=1, source_target_pairs={{2,0},{4,2},{6,4},{3,1},{5,3},{7,5},{10,8},{12,10},{14,12},{11,9},... | collective-permute-start | bytes 1007624 | tf_op jit(solution)/shard_map/ppermute | solution.py:22
  60.7 14.4 %collective-permute-start.10 = (bf16[64,1280]{1,0:T(8,128)(2,1)S(1)}, bf16[64,1280]{1,0:T(8,128)(2,1)S(1)}, u32[]{:S(2)}, u32[]{:S(2)}) collective-permute-start(bf16[64,1280]{1,0:T(8,128)(2,1)S(1)} %get-tuple-element.38), channel_id=1, source_target_pairs={{0,16},{16,24},{24,8},{1,17},{17,25},{25,9},{2,18},{18,26},{26,10}... | collective-permute-start | bytes 491528 | tf_op jit(solution)/shard_map/ppermute | solution.py:390
  64.4 10.6 %collective-permute-start.9 = (bf16[64,1280]{1,0:T(8,128)(2,1)S(1)}, bf16[64,1280]{1,0:T(8,128)(2,1)S(1)}, u32[]{:S(2)}, u32[]{:S(2)}) collective-permute-start(bf16[64,1280]{1,0:T(8,128)(2,1)S(1)} %get-tuple-element.39), channel_id=1, source_target_pairs={{0,8},{8,24},{24,16},{1,9},{9,25},{25,17},{2,10},{10,26},{26,18},{... | collective-permute-start | bytes 491528 | tf_op jit(solution)/shard_map/ppermute | solution.py:390
  72.4 6.7 %collective-permute-start.5 = (bf16[64,1280]{1,0:T(8,128)(2,1)S(1)}, bf16[64,1280]{1,0:T(8,128)(2,1)S(1)}, u32[]{:S(2)}, u32[]{:S(2)}) collective-permute-start(bf16[64,1280]{1,0:T(8,128)(2,1)S(1)} %get-tuple-element.43), channel_id=1, source_target_pairs={{0,8},{8,24},{24,16},{1,9},{9,25},{25,17},{2,10},{10,26},{26,18},{... | collective-permute-start | bytes 491528 | tf_op jit(solution)/shard_map/ppermute | solution.py:390
  73.7 5.9 %collective-permute-start.6 = (bf16[64,1280]{1,0:T(8,128)(2,1)S(1)}, bf16[64,1280]{1,0:T(8,128)(2,1)S(1)}, u32[]{:S(2)}, u32[]{:S(2)}) collective-permute-start(bf16[64,1280]{1,0:T(8,128)(2,1)S(1)} %get-tuple-element.42), channel_id=1, source_target_pairs={{0,16},{16,24},{24,8},{1,17},{17,25},{25,9},{2,18},{18,26},{26,10}... | collective-permute-start | bytes 491528 | tf_op jit(solution)/shard_map/ppermute | solution.py:390
  75.2 9.0 %collective-permute-start.11 = (bf16[64,1280]{1,0:T(8,128)(2,1)S(1)}, bf16[64,1280]{1,0:T(8,128)(2,1)S(1)}, u32[]{:S(2)}, u32[]{:S(2)}) collective-permute-start(bf16[64,1280]{1,0:T(8,128)(2,1)S(1)} %get-tuple-element.36), channel_id=1, source_target_pairs={{0,16},{16,0},{8,24},{24,8},{1,17},{17,1},{9,25},{25,9},{2,18},{18... | collective-permute-start | bytes 491528 | tf_op jit(solution)/shard_map/ppermute | solution.py:390
  77.3 6.9 %collective-permute-start.12 = (bf16[64,1280]{1,0:T(8,128)(2,1)S(1)}, bf16[64,1280]{1,0:T(8,128)(2,1)S(1)}, u32[]{:S(2)}, u32[]{:S(2)}) collective-permute-start(bf16[64,1280]{1,0:T(8,128)(2,1)S(1)} %get-tuple-element.28), channel_id=1, source_target_pairs={{0,8},{8,0},{16,24},{24,16},{1,9},{9,1},{17,25},{25,17},{2,10},{10... | collective-permute-start | bytes 491528 | tf_op jit(solution)/shard_map/ppermute | solution.py:390
  79.8 4.5 %copy-start.6 = (s32[1,1,128]{2,1,0:T(1,128)S(1)}, s32[1,1,128]{2,1,0:T(1,128)}, u32[]{:S(2)}) copy-start(s32[1,1,128]{2,1,0:T(1,128)} %param.11) | copy-start | bytes 1540
  79.8 5.8 %collective-permute-start.7 = (bf16[64,1280]{1,0:T(8,128)(2,1)S(1)}, bf16[64,1280]{1,0:T(8,128)(2,1)S(1)}, u32[]{:S(2)}, u32[]{:S(2)}) collective-permute-start(bf16[64,1280]{1,0:T(8,128)(2,1)S(1)} %get-tuple-element.40), channel_id=1, source_target_pairs={{0,16},{16,0},{8,24},{24,8},{1,17},{17,1},{9,25},{25,9},{2,18},{18... | collective-permute-start | bytes 491528 | tf_op jit(solution)/shard_map/ppermute | solution.py:390
  82.3 5.3 %collective-permute-start.8 = (bf16[64,1280]{1,0:T(8,128)(2,1)S(1)}, bf16[64,1280]{1,0:T(8,128)(2,1)S(1)}, u32[]{:S(2)}, u32[]{:S(2)}) collective-permute-start(bf16[64,1280]{1,0:T(8,128)(2,1)S(1)} %get-tuple-element.32), channel_id=1, source_target_pairs={{0,8},{8,0},{16,24},{24,16},{1,9},{9,1},{17,25},{25,17},{2,10},{10... | collective-permute-start | bytes 491528 | tf_op jit(solution)/shard_map/ppermute | solution.py:390

commit v5 on v4

v5 whole, which is shorter than its diff:
```python
import functools
import math

import jax
import jax.numpy as jnp
from jax import lax
from jax.experimental import pallas as pl
from jax.experimental.pallas import tpu as pltpu
from jax.sharding import PartitionSpec as P

HEADS = 32
DH = 80
FRAMES = 20
LANES = 128
VMEM_LIMIT = 48 * 1024 * 1024
PACK_LIMIT = 52 * 1024 * 1024


def shifted(block, axis, distance):
    devices = range(lax.axis_size(axis))
    route = [(i - distance, i) for i in devices if i - distance in devices]
    return lax.ppermute(block, axis, route)


def paired(block, axis, first):
    size = lax.axis_size(axis)
    route = []
    for i in range(size):
        other = i + 1 if (i - first) % 2 == 0 else i - 1
        route.append((i, other if 0 <= other < size else i))
    return lax.ppermute(block, axis, route)


def lane_windows(heads):
    windows = []
    for head in range(heads):
        first, last = head * DH, (head + 1) * DH
        if windows and last <= windows[-1][0] + 2 * LANES:
            windows[-1][1].append(head)
        else:
            windows.append((first // LANES * LANES, [head]))
    out = []
    for start, members in windows:
        start = min(start, heads * DH - 2 * LANES)
        out.append((start, members))
    return out


def head_masks(rows, period):
    masks = {}
    for start, members in lane_windows(period // DH):
        lane = lax.broadcasted_iota(jnp.int32, (rows, 2 * LANES), 1) + start
        for h in members:
            inside = (lane >= h * DH) & (lane < (h + 1) * DH)
            masks[h] = jnp.where(inside, 1.0, 0.0).astype(jnp.bfloat16)
    return masks


def mixed_period(base, query, sets, masks, period):
    rows = sets[0][0].shape[0]
    factor = math.log2(math.e) / math.sqrt(DH)
    windows = lane_windows(period // DH)
    scores = []
    for start, members in windows:
        lanes = slice(base + start, base + start + 2 * LANES)
        part = query(lanes)
        stacked = jnp.concatenate([part * masks[h] for h in members], axis=0)
        scores.append(
            [
                lax.dot_general(
                    stacked, key(lanes), (((1,), (1,)), ((), ())), preferred_element_type=jnp.float32
                )
                for bias, key, value in sets
            ]
        )
    weights = []
    for parts, (start, members) in zip(scores, windows):
        parts = [
            part.reshape(len(members), rows, -1) + bias[None]
            for part, (bias, key, value) in zip(parts, sets)
        ]
        largest = row_reduce(jnp.maximum, jnp.max, parts)
        powers = [jnp.exp2((part - largest) * factor) for part in parts]
        scale = 1.0 / row_reduce(jnp.add, jnp.sum, powers)
        weights.append(
            [(p * scale).astype(jnp.bfloat16).reshape(len(members) * rows, -1) for p in powers]
        )
    tiles = {}
    for parts, (start, members) in zip(weights, windows):
        lanes = slice(base + start, base + start + 2 * LANES)
        mixed = sum(
            jnp.dot(part, value(lanes), preferred_element_type=jnp.float32)
            for part, (bias, key, value) in zip(parts, sets)
        )
        for n, h in enumerate(members):
            for t in range(2):
                low = start + t * LANES
                if h * DH >= low + LANES or (h + 1) * DH <= low:
                    continue
                piece = mixed[n * rows : (n + 1) * rows, t * LANES : (t + 1) * LANES]
                if low in tiles:
                    lane = lax.broadcasted_iota(jnp.int32, (rows, LANES), 1) + low
                    tiles[low] = jnp.where(lane >= h * DH, piece, tiles[low])
                else:
                    tiles[low] = piece
    return {low: tile.astype(jnp.bfloat16) for low, tile in tiles.items()}


def row_reduce(pair, reduce, parts):
    if all(part.shape == parts[0].shape for part in parts):
        return reduce(functools.reduce(pair, parts), axis=-1, keepdims=True)
    return functools.reduce(pair, [reduce(part, axis=-1, keepdims=True) for part in parts])


def columns(row):
    return jnp.broadcast_to(row, (LANES, row.shape[1])).T


def link_bias(mine, theirs):
    return jnp.where(jnp.abs(mine[:, :1] - theirs.T[: mine.shape[0]]) <= 1.5, 0.0, -1e30)


def attend_block(query, sets, out_ref):
    rows, width = out_ref.shape
    period = math.lcm(DH, LANES)
    masks = head_masks(rows, period)
    for base in range(0, width, period):
        tiles = mixed_period(base, query, sets, masks, period)
        for low, tile in tiles.items():
            out_ref[:, base + low : base + low + LANES] = tile


def middle_kernel(reach, q_ref, k_ref, v_ref, code_ref, out_ref):
    rows = out_ref.shape[0]
    code = columns(code_ref[...])
    bias = link_bias(code[reach : reach + rows], code)
    own = (bias, lambda lanes: k_ref[:, lanes], lambda lanes: v_ref[:, lanes])
    attend_block(lambda lanes: q_ref[reach : reach + rows, lanes], [own], out_ref)


def edge_kernel(reach, valid_ref, q_ref, k_ref, v_ref, code_ref, *refs):
    halos = refs[:-4]
    out_ref, keys, values, codes = refs[-4:]
    tokens, width = q_ref.shape
    code = columns(code_ref[...])
    at = 0
    for n, piece in enumerate(halos):
        rows = piece.shape[0]
        keys[at : at + rows] = piece[:, :width]
        values[at : at + rows] = piece[:, width : 2 * width]
        there = valid_ref[n] if n < 2 else 1.0
        codes[at : at + rows] = piece[:, 2 * width :].astype(jnp.float32) * there
        at += rows
    if at < keys.shape[0]:
        spare = keys.shape[0] - at
        keys[at:] = jnp.zeros((spare, width), keys.dtype)
        values[at:] = jnp.zeros((spare, width), values.dtype)
        codes[at:] = jnp.zeros((spare, LANES), codes.dtype)
    if tokens > 2 * reach:
        last = tokens - reach
        mine = jnp.concatenate((code[:reach], code[last:]), axis=0)
        query = lambda lanes: jnp.concatenate((q_ref[:reach, lanes], q_ref[last:, lanes]), axis=0)
    else:
        mine = code
        query = lambda lanes: q_ref[:, lanes]
    own = (link_bias(mine, code), lambda lanes: k_ref[:, lanes], lambda lanes: v_ref[:, lanes])
    halo = (
        link_bias(mine, codes[...]),
        lambda lanes: keys[:, lanes],
        lambda lanes: values[:, lanes],
    )
    attend_block(query, [own, halo], out_ref)


def attend_cost(tokens, span, width):
    return pl.CostEstimate(
        flops=HEADS * tokens * span * 2 * LANES * 4,
        bytes_accessed=12 * tokens * width,
        transcendentals=HEADS * tokens * span,
    )


VMEM = pl.BlockSpec(memory_space=pltpu.VMEM)
SMEM = pl.BlockSpec(memory_space=pltpu.SMEM)
PARAMS = pltpu.CompilerParams(vmem_limit_bytes=VMEM_LIMIT)


def attend_middle(queries, keys, values, code, reach):
    tokens, width = queries.shape
    return pl.pallas_call(
        functools.partial(middle_kernel, reach),
        in_specs=[VMEM] * 4,
        out_specs=VMEM,
        out_shape=jax.ShapeDtypeStruct((tokens - 2 * reach, width), jnp.bfloat16),
        compiler_params=PARAMS,
        cost_estimate=attend_cost(tokens - 2 * reach, tokens, width),
        name="attend_middle",
    )(queries, keys, values, code)


def attend_edges(valid, queries, keys, values, code, halos, reach):
    tokens, width = queries.shape
    rows = min(tokens, 2 * reach)
    held = -(-2 * reach // LANES) * LANES
    return pl.pallas_call(
        functools.partial(edge_kernel, reach),
        in_specs=[SMEM] + [VMEM] * (4 + len(halos)),
        out_specs=VMEM,
        out_shape=jax.ShapeDtypeStruct((rows, width), jnp.bfloat16),
        scratch_shapes=[
            pltpu.VMEM((held, width), jnp.bfloat16),
            pltpu.VMEM((held, width), jnp.bfloat16),
            pltpu.VMEM((held, LANES), jnp.float32),
        ],
        compiler_params=PARAMS,
        cost_estimate=attend_cost(rows, LANES, width),
        name="attend_edges",
    )(valid, queries, keys, values, code, *halos)


def pack_kernel(most, first_ref, k_ref, v_ref, grad_ref, mark_ref, *refs):
    half_refs, end_refs, sems = refs[:2], refs[2:4], refs[4]
    width = k_ref.shape[1]
    half = width // 2
    copies = []
    for n, ref in enumerate(half_refs):
        copies.append(
            pltpu.make_async_copy(
                grad_ref.at[:, pl.ds(n * half, half)], ref.at[:, pl.ds(0, half)], sems.at[n]
            )
        )
    for n, ref in enumerate(end_refs):
        first = pl.multiple_of(first_ref[n], most)
        for m, source in enumerate((k_ref, v_ref)):
            copies.append(
                pltpu.make_async_copy(
                    source.at[pl.ds(first, most)],
                    ref.at[:, pl.ds(m * width, width)],
                    sems.at[2 + 2 * n + m],
                )
            )
    for copy in copies:
        copy.start()
    tokens = grad_ref.shape[0]
    code = columns(mark_ref[:1])
    for n, ref in enumerate(end_refs):
        here = jnp.where(first_ref[n] == 0, code[:most], code[tokens - most :])
        ref[:, 2 * width :] = here.astype(jnp.bfloat16)
    place = columns(mark_ref[1:2]).astype(jnp.bfloat16)
    for ref in half_refs:
        ref[:, half:] = place
    for copy in copies:
        copy.wait()


def pack(firsts, keys, values, grads, marks, most):
    tokens, width = keys.shape
    ends = jax.ShapeDtypeStruct((most, 2 * width + LANES), jnp.bfloat16)
    halves = jax.ShapeDtypeStruct((tokens, width // 2 + LANES), jnp.bfloat16)
    return pl.pallas_call(
        functools.partial(pack_kernel, most),
        in_specs=[SMEM] + [pl.BlockSpec(memory_space=pltpu.HBM)] * 3 + [VMEM],
        out_specs=[VMEM] * 4,
        out_shape=[halves, halves, ends, ends],
        scratch_shapes=[pltpu.SemaphoreType.DMA((6,))],
        compiler_params=pltpu.CompilerParams(vmem_limit_bytes=PACK_LIMIT),
        cost_estimate=pl.CostEstimate(
            flops=0, bytes_accessed=4 * tokens * width + 16 * most * width, transcendentals=0
        ),
        name="pack",
    )(firsts, keys, values, grads, marks)


def selector(row):
    tokens = row.shape[1]
    wanted = lax.broadcasted_iota(jnp.int32, (tokens, tokens), 0).astype(jnp.float32)
    return jnp.where(wanted == row, 1.0, 0.0)


def sums_kernel(sizes, flag_ref, gate_ref, *refs):
    half = gate_ref.shape[1] // 2
    count = len(sizes)
    for n in range(2):
        mine_ref, theirs_ref = refs[2 * n : 2 * n + 2]
        picks, rows = [], []
        for ref in (mine_ref, theirs_ref):
            place = ref[:, half : half + LANES].astype(jnp.float32).T[:1]
            picks.append(selector(place).astype(jnp.bfloat16))
            rows.append(ref[:, :half])
        summed = jnp.dot(
            jnp.concatenate(picks, axis=1),
            jnp.concatenate(rows, axis=0),
            preferred_element_type=jnp.float32,
        )
        term = gate_ref[:, n * half : (n + 1) * half] * summed
        term = (term + flag_ref[n] * rows[1].astype(jnp.float32)).astype(jnp.bfloat16)
        at = 0
        for ref, size in zip(refs[4 + n * count : 4 + (n + 1) * count], sizes):
            ref[...] = term[at : at + size]
            at += size


def pair_sums(flags, gate, parts, sizes):
    tokens, width = parts[0].shape[0], gate.shape[1]
    outs = [jax.ShapeDtypeStruct((size, width // 2), jnp.bfloat16) for size in sizes] * 2
    return pl.pallas_call(
        functools.partial(sums_kernel, sizes),
        in_specs=[SMEM] + [VMEM] * 5,
        out_specs=[VMEM] * len(outs),
        out_shape=outs,
        compiler_params=PARAMS,
        cost_estimate=pl.CostEstimate(
            flops=4 * tokens * tokens * width, bytes_accessed=6 * tokens * width, transcendentals=0
        ),
        name="pair_sums",
    )(flags, gate, *parts)


def piece_spots(tokens, reach, piece):
    if tokens <= 2 * reach:
        return [(0, tokens, 0)]
    if piece == 0:
        return [(reach, tokens - 2 * reach, 0)]
    return [(0, reach, 0), (tokens - reach, reach, reach)]


def relay_kernel(spots, row_ref, gate_ref, first_ref, second_ref, base_ref, out_ref):
    tokens, width = out_ref.shape
    half = width // 2
    picks = selector(row_ref[...]).T.astype(jnp.bfloat16)
    picks = jnp.concatenate([picks[:, top : top + size] for top, size, at in spots], axis=1)
    for n, ref in enumerate((first_ref, second_ref)):
        lanes = slice(n * half, (n + 1) * half)
        relayed = jnp.dot(picks, ref[...], preferred_element_type=jnp.float32)
        total = base_ref[:, lanes].astype(jnp.float32) + gate_ref[:, lanes] * relayed
        out_ref[:, lanes] = total.astype(out_ref.dtype)


def relay(rows, gate, first, second, base, spots, dtype):
    tokens, width = base.shape
    return pl.pallas_call(
        functools.partial(relay_kernel, spots),
        in_specs=[VMEM] * 5,
        out_specs=VMEM,
        out_shape=jax.ShapeDtypeStruct((tokens, width), dtype),
        compiler_params=PARAMS,
        cost_estimate=pl.CostEstimate(
            flops=2 * tokens * tokens * width, bytes_accessed=24 * tokens * width, transcendentals=0
        ),
        name="relay",
    )(rows, gate, first, second, base)


def whole_gate(gate):
    ranks = lax.axis_size("rep")
    if ranks != 2:
        return lax.all_gather(gate, "rep", axis=0, tiled=True)
    other = lax.ppermute(gate, "rep", [(0, 1), (1, 0)])
    first = lax.axis_index("rep") == 0
    return jnp.concatenate([jnp.where(first, gate, other), jnp.where(first, other, gate)])


SWAP_X, SWAP_Y = [(0, 1), (1, 0), (2, 3), (3, 2)], [(0, 2), (2, 0), (1, 3), (3, 1)]
ROUND_A, ROUND_B = [(0, 1), (1, 3), (3, 2), (2, 0)], [(0, 2), (2, 3), (3, 1), (1, 0)]


def added(a, b):
    return (a.astype(jnp.float32) + b.astype(jnp.float32)).astype(a.dtype)


def local(query_rows, key_rows, value_rows, view_frame, control_row, control_gate, out_grad):
    queries, keys, values = query_rows[0, 0], key_rows[0, 0], value_rows[0, 0]
    tokens, width = queries.shape
    half = width // 2
    ranks = lax.axis_size("seq")
    reach = 2 * (tokens * ranks // 32)
    hops = (reach + tokens - 1) // tokens
    group, rank = lax.axis_index("grp"), lax.axis_index("seq")
    send = lambda block, route: lax.ppermute(block, "grp", route)

    tag = view_frame[0, 0]
    code = tag + 8 * (tag // FRAMES) + 16
    marks = jnp.stack((code, control_row[0, 0] % tokens)).astype(jnp.float32)
    code, rows = marks[:1], marks[1:]
    most = min(tokens, reach)
    even = rank % 2 == 0
    firsts = jnp.where(jnp.stack((even, ~even)), tokens - most, 0).astype(jnp.int32)
    sent_a, sent_b, end_one, end_two = pack(firsts, keys, values, out_grad[0, 0], marks, most)
    got_a, got_b = send(sent_a, SWAP_X), send(sent_b, SWAP_Y)
    halos = [paired(end_one, "seq", 0), paired(end_two, "seq", 1)]
    above, below = rank < ranks - 1, rank > 0
    valid = jnp.where(jnp.stack((even, ~even)), above, below).astype(jnp.float32)
    for hop in range(2, hops + 1):
        count = min(tokens, reach - (hop - 1) * tokens)
        tail, head = jnp.where(even, end_one, end_two), jnp.where(even, end_two, end_one)
        halos.append(shifted(tail[most - count :], "seq", hop))
        halos.append(shifted(head[:count], "seq", -hop))
    gate = whole_gate(control_gate)[None]

    own = []
    sizes = [min(tokens, 2 * reach)]
    if tokens > 2 * reach:
        own.append(attend_middle(queries, keys, values, code, reach))
        sizes.insert(0, tokens - 2 * reach)
    flags = jnp.stack([group == 1, group == 2]).astype(jnp.float32)
    sums = pair_sums(flags, gate, (sent_a, got_a, sent_b, got_b), sizes)
    valid, *sums = lax.optimization_barrier((valid, *sums))
    own.append(attend_edges(valid, queries, keys, values, code, halos, reach))

    count = len(own)
    spots = [piece_spots(tokens, reach, n) for n in range(count)]
    order = [
        own[n][at : at + size] for top, size, n, at in sorted(
            (top, size, n, at) for n in range(count) for top, size, at in spots[n]
        )
    ]
    block_out = jnp.concatenate(order, axis=0)
    totals = []
    for n, (piece, sum_a, sum_b) in enumerate(zip(own, sums[:count], sums[count:])):
        piece_a, piece_b = piece[:, :half], piece[:, half:]
        one = send(jnp.where(group == 0, piece_a, jnp.where(group == 1, sum_a, sum_b)), ROUND_A)
        two = send(jnp.where(group == 0, piece_b, jnp.where(group == 2, sum_b, sum_a)), ROUND_B)
        total_a = added(sum_a, jnp.where(group == 1, two, one))
        total_b = added(sum_b, jnp.where(group == 2, one, two))
        held_a = jnp.where(group == 0, piece_a, one)
        held_b = jnp.where(group == 0, piece_b, two)
        across = send(jnp.where((group == 0) | (group == 2), held_b, total_a), SWAP_X)
        down = send(jnp.where(group <= 1, held_a, total_b), SWAP_Y)
        branch_a = jnp.where(group <= 1, held_a, down)
        branch_b = jnp.where((group == 0) | (group == 2), held_b, across)
        dtype = jnp.bfloat16 if n == count - 1 else jnp.float32
        block_out = relay(rows, gate, branch_a, branch_b, block_out, spots[n], dtype)
        totals.append(
            jnp.concatenate(
                (
                    jnp.where((group == 0) | (group == 2), across, total_a),
                    jnp.where(group <= 1, down, total_b),
                ),
                axis=1,
            )
        )
    branch_grad = jnp.concatenate(totals, axis=0)
    return (block_out[None, None], branch_grad[None])


def solution(mesh):
    placed = (
        P("rep", "grp", "seq", None),
        P("rep", "grp", "seq", None),
        P("rep", "grp", "seq", None),
        P("rep", "grp", "seq"),
        P("rep", "grp", "seq"),
        P("rep"),
        P("rep", "grp", "seq", None),
    )
    return jax.shard_map(
        local,
        mesh=mesh,
        in_specs=placed,
        out_specs=(P("rep", "grp", "seq", None), P("rep", "seq", None)),
        check_vma=False,
    )
```

time: 90.3 us -> 42.3 us (0.47)
  Pallas kernels: 50.4 us -> 11.3 us
  starting transfers between devices: 31.2 us -> 19.1 us
  waiting for transfers between devices: 5.67 us -> 7.69 us
  other arithmetic: 1.66 us -> 2.61 us
    pallas_call x3, Pallas kernels: 46.8 us -> 7.68 us  [the longest x1 3.6 us: attend_edges(): pl.pallas_call(functools.partial(edge_kernel, reach), in_specs=[SMEM] + [...]
    ppermute x10, starting transfers between devices: 25.7 us -> 13.2 us  [local(): send = lambda block, route: lax.ppermute(block, 'grp', route)]
    ppermute x10, waiting for transfers between devices: 3.47 us -> 7.68 us  [local(): send = lambda block, route: lax.ppermute(block, 'grp', route)]
    ppermute x2, waiting for transfers between devices: 2.19 us -> 0.01 us  [paired(): return lax.ppermute(block, axis, route)]
  transfers between devices with their start and end apart: 13 -> 13, of which waited for: 4 -> 6; matrix products, arithmetic and copies ran while one was open for 1% -> 2% of each run, Pallas kernels for 9% -> 18%
where the time goes in v5:
time: 42.3 us; the launch traced here: 41.5 us
  starting transfers between devices  19.1 us (45%)
  Pallas kernels  11.3 us (27%)
  waiting for transfers between devices  7.69 us (18%)
  other arithmetic  2.61 us (6%)
  between operations  0.85 us (2%)
    ppermute x10, starting transfers between devices, local(): send = lambda block, route: lax.ppermute(block, 'grp', route)  13.2 us
    ppermute x10, waiting for transfers between devices, local(): send = lambda block, route: lax.ppermute(block, 'grp', route)  7.68 us
    ppermute x2, starting transfers between devices, paired(): return lax.ppermute(block, axis, route)  5.88 us
    pallas_call x1, Pallas kernels, attend_edges(): pl.pallas_call(functools.partial(edge_kernel, reach), in_specs=[SMEM] + [...  3.6 us
    pallas_call x1, Pallas kernels, pack(): pl.pallas_call(functools.partial(pack_kernel, most), in_specs=[SMEM] + [p...  2.69 us
    pallas_call x1, Pallas kernels, attend_middle(): pl.pallas_call(functools.partial(middle_kernel, reach), in_specs=[VMEM] *...  1.86 us
    pallas_call x2, Pallas kernels, relay(): pl.pallas_call(functools.partial(relay_kernel, spots), in_specs=[VMEM] *...  1.72 us
    pallas_call x1, Pallas kernels, pair_sums(): pl.pallas_call(functools.partial(sums_kernel, sizes), in_specs=[SMEM] + [...  1.39 us
  transfers between devices with their start and end apart: 13, of which 6 were waited for; matrix products, arithmetic and copies ran while one was open for 2% of the time, Pallas kernels for 18%

profile of v5, /device:TPU:0, one launch (start us, length us, event | category | flops | bytes accessed | tf_op | source)
XLA Modules:
  0.0 41.5 jit_solution(1887418377011099151)
XLA Ops:
  0.8 0.8 %and_select_fusion = (s32[1,128]{1,0:T(1,128)S(1)}, s32[1,128]{1,0:T(1,128)S(1)}) fusion(s32[1,1,128]{2,1,0:T(1,128)} %param.11, s32[1,1,128]{2,1,0:T(1,128)} %param.10), kind=kLoop, calls=%fused_computation.34 | loop fusion | flops 2816 | bytes 2048 | tf_op jit(solution)/shard_map/jit(remainder)/select_n | solution.py:383
  1.6 2.7 %pack.1 = (bf16[128,1408]{1,0:T(8,128)(2,1)S(1)}, bf16[128,1408]{1,0:T(8,128)(2,1)S(1)}, bf16[32,5248]{1,0:T(8,128)(2,1)}, bf16[32,5248]{1,0:T(8,128)(2,1)}) custom-call(s32[2]{0:T(128)S(1)} %broadcast_select_fusion.18.first_ref, bf16[128,2560]{1,0:T(8,128)(2,1)} %bitcast.28, bf16[128,2560]{1,0:T(8,128)(2,1)} %bitcast.31, bf16[128,2560]{1,0:T(8,128)(2,1)} %bitcast.36, ...), custom_call_target="tpu_custom_call" | custom-call | bytes 2621440 | tf_op jit(solution)/shard_map/pack/pallas_call | solution.py:260
  4.3 3.0 %collective-permute-start.1 = (bf16[128,1408]{1,0:T(8,128)(2,1)S(1)}, bf16[128,1408]{1,0:T(8,128)(2,1)S(1)}, u32[]{:S(2)}, u32[]{:S(2)}) collective-permute-start(bf16[128,1408]{1,0:T(8,128)(2,1)S(1)} %get-tuple-element.15.refs_0_), channel_id=1, source_target_pairs={{0,8},{8,0},{16,24},{24,16},{1,9},{9,1},{17,25},{25,17},{2,10},{10... | collective-permute-start | bytes 1081352 | tf_op jit(solution)/shard_map/ppermute | solution.py:379
  7.3 1.5 %collective-permute-start.2 = (bf16[128,1408]{1,0:T(8,128)(2,1)S(1)}, bf16[128,1408]{1,0:T(8,128)(2,1)}, u32[]{:S(2)}, u32[]{:S(2)}) collective-permute-start(bf16[128,1408]{1,0:T(8,128)(2,1)S(1)} %get-tuple-element.16.refs_2_), channel_id=1, source_target_pairs={{0,16},{16,0},{8,24},{24,8},{1,17},{17,1},{9,25},{25,9},{2,18},{18... | collective-permute-start | bytes 1081352 | tf_op jit(solution)/shard_map/ppermute | solution.py:379
  8.8 1.6 %collective-permute-start.3 = (bf16[32,5248]{1,0:T(8,128)(2,1)}, bf16[32,5248]{1,0:T(8,128)(2,1)}, u32[]{:S(2)}, u32[]{:S(2)}) collective-permute-start(bf16[32,5248]{1,0:T(8,128)(2,1)} %get-tuple-element.22), channel_id=1, source_target_pairs={{0,2},{2,0},{4,6},{6,4},{1,3},{3,1},{5,7},{7,5},{8,10},{10,8},{12,... | collective-permute-start | bytes 1007624 | tf_op jit(solution)/shard_map/ppermute | solution.py:31
  10.4 4.3 %collective-permute-start.4 = (bf16[32,5248]{1,0:T(8,128)(2,1)}, bf16[32,5248]{1,0:T(8,128)(2,1)}, u32[]{:S(2)}, u32[]{:S(2)}) collective-permute-start(bf16[32,5248]{1,0:T(8,128)(2,1)} %get-tuple-element.23), channel_id=1, source_target_pairs={{0,0},{2,4},{4,2},{6,6},{1,1},{3,5},{5,3},{7,7},{8,8},{10,12},{12,... | collective-permute-start | bytes 1007624 | tf_op jit(solution)/shard_map/ppermute | solution.py:31
  14.9 1.9 %attend_middle.1 = bf16[64,2560]{1,0:T(8,128)(2,1)S(1)} custom-call(bf16[128,2560]{1,0:T(8,128)(2,1)S(1)} %bitcast.34, bf16[128,2560]{1,0:T(8,128)(2,1)S(1)} %bitcast.29, bf16[128,2560]{1,0:T(8,128)(2,1)S(1)} %bitcast.32, f32[1,128]{1,0:T(1,128)S(1)} %get-tuple-element.56.code_ref), custom_call_target="tpu_custom_call" | custom-call | flops 268435456 | bytes 1966080 | tf_op jit(solution)/shard_map/attend_middle/pallas_call | solution.py:190
  16.8 0.5 %collective-permute-done.2.refs_3_ = bf16[128,1408]{1,0:T(8,128)(2,1)} collective-permute-done((bf16[128,1408]{1,0:T(8,128)(2,1)S(1)}, bf16[128,1408]{1,0:T(8,128)(2,1)}, u32[]{:S(2)}, u32[]{:S(2)}) %collective-permute-start.2) | collective-permute-done | bytes 360480 | tf_op jit(solution)/shard_map/ppermute | solution.py:379
  17.3 1.4 %pair_sums.1 = (bf16[64,1280]{1,0:T(8,128)(2,1)S(1)}, bf16[64,1280]{1,0:T(8,128)(2,1)S(1)}, bf16[64,1280]{1,0:T(8,128)(2,1)S(1)}, bf16[64,1280]{1,0:T(8,128)(2,1)S(1)}) custom-call(f32[2]{0:T(128)S(1)} %add_convert_fusion.4.flag_ref, f32[1,2560]{1,0:T(1,128)S(1)} %broadcast_in_dim.25.gate_ref, bf16[128,1408]{1,0:T(8,128)(2,1)S(1)} %get-tuple-element.15.refs_0_, ...), custom_call_target="tpu_custom_call" | custom-call | flops 167772160 | bytes 1966080 | tf_op jit(solution)/shard_map/pair_sums/pallas_call | solution.py:306
  18.7 1.6 %collective-permute-start.10 = (bf16[64,1280]{1,0:T(8,128)(2,1)S(1)}, bf16[64,1280]{1,0:T(8,128)(2,1)S(1)}, u32[]{:S(2)}, u32[]{:S(2)}) collective-permute-start(bf16[64,1280]{1,0:T(8,128)(2,1)S(1)} %get-tuple-element.38), channel_id=1, source_target_pairs={{0,16},{16,24},{24,8},{8,0},{1,17},{17,25},{25,9},{9,1},{2,18},{18... | collective-permute-start | bytes 491528 | tf_op jit(solution)/shard_map/ppermute | solution.py:379
  20.3 0.5 %collective-permute-start.9 = (bf16[64,1280]{1,0:T(8,128)(2,1)S(1)}, bf16[64,1280]{1,0:T(8,128)(2,1)S(1)}, u32[]{:S(2)}, u32[]{:S(2)}) collective-permute-start(bf16[64,1280]{1,0:T(8,128)(2,1)S(1)} %get-tuple-element.39), channel_id=1, source_target_pairs={{0,8},{8,24},{24,16},{16,0},{1,9},{9,25},{25,17},{17,1},{2,10},{10... | collective-permute-start | bytes 491528 | tf_op jit(solution)/shard_map/ppermute | solution.py:379
  20.8 3.6 %attend_edges.1 = bf16[64,2560]{1,0:T(8,128)(2,1)S(1)} custom-call(f32[2]{0:T(128)S(1)} %select_convert_fusion.valid_ref, bf16[128,2560]{1,0:T(8,128)(2,1)S(1)} %bitcast.35, bf16[128,2560]{1,0:T(8,128)(2,1)S(1)} %bitcast.30, bf16[128,2560]{1,0:T(8,128)(2,1)S(1)} %bitcast.33, f32[1,128]{1,0:T(1,128)S(1)} %get-tuple-element.56.code_ref, ...), custom_call_target="tpu_custom_call" | custom-call | flops 268435456 | bytes 1966080 | tf_op jit(solution)/shard_map/attend_edges/pallas_call | solution.py:205
  24.9 1.7 %collective-permute-start.6 = (bf16[64,1280]{1,0:T(8,128)(2,1)S(1)}, bf16[64,1280]{1,0:T(8,128)(2,1)S(1)}, u32[]{:S(2)}, u32[]{:S(2)}) collective-permute-start(bf16[64,1280]{1,0:T(8,128)(2,1)S(1)} %get-tuple-element.42), channel_id=1, source_target_pairs={{0,16},{16,24},{24,8},{8,0},{1,17},{17,25},{25,9},{9,1},{2,18},{18... | collective-permute-start | bytes 491528 | tf_op jit(solution)/shard_map/ppermute | solution.py:379
  26.8 1.6 %collective-permute-start.11 = (bf16[64,1280]{1,0:T(8,128)(2,1)S(1)}, bf16[64,1280]{1,0:T(8,128)(2,1)S(1)}, u32[]{:S(2)}, u32[]{:S(2)}) collective-permute-start(bf16[64,1280]{1,0:T(8,128)(2,1)S(1)} %get-tuple-element.36), channel_id=1, source_target_pairs={{0,16},{16,0},{8,24},{24,8},{1,17},{17,1},{9,25},{25,9},{2,18},{18... | collective-permute-start | bytes 491528 | tf_op jit(solution)/shard_map/ppermute | solution.py:379
  28.4 0.5 %collective-permute-start.12 = (bf16[64,1280]{1,0:T(8,128)(2,1)S(1)}, bf16[64,1280]{1,0:T(8,128)(2,1)S(1)}, u32[]{:S(2)}, u32[]{:S(2)}) collective-permute-start(bf16[64,1280]{1,0:T(8,128)(2,1)S(1)} %get-tuple-element.28), channel_id=1, source_target_pairs={{0,8},{8,0},{16,24},{24,16},{1,9},{9,1},{17,25},{25,17},{2,10},{10... | collective-permute-start | bytes 491528 | tf_op jit(solution)/shard_map/ppermute | solution.py:379
  28.9 2.7 %collective-permute-done.5 = bf16[64,1280]{1,0:T(8,128)(2,1)S(1)} collective-permute-done((bf16[64,1280]{1,0:T(8,128)(2,1)S(1)}, bf16[64,1280]{1,0:T(8,128)(2,1)S(1)}, u32[]{:S(2)}, u32[]{:S(2)}) %collective-permute-start.5) | collective-permute-done | bytes 163872 | tf_op jit(solution)/shard_map/ppermute | solution.py:379
  32.1 1.9 %collective-permute-start.7 = (bf16[64,1280]{1,0:T(8,128)(2,1)S(1)}, bf16[64,1280]{1,0:T(8,128)(2,1)S(1)}, u32[]{:S(2)}, u32[]{:S(2)}) collective-permute-start(bf16[64,1280]{1,0:T(8,128)(2,1)S(1)} %get-tuple-element.40), channel_id=1, source_target_pairs={{0,16},{16,0},{8,24},{24,8},{1,17},{17,1},{9,25},{25,9},{2,18},{18... | collective-permute-start | bytes 491528 | tf_op jit(solution)/shard_map/ppermute | solution.py:379
  34.0 0.5 %collective-permute-start.8 = (bf16[64,1280]{1,0:T(8,128)(2,1)S(1)}, bf16[64,1280]{1,0:T(8,128)(2,1)S(1)}, u32[]{:S(2)}, u32[]{:S(2)}) collective-permute-start(bf16[64,1280]{1,0:T(8,128)(2,1)S(1)} %get-tuple-element.32), channel_id=1, source_target_pairs={{0,8},{8,0},{16,24},{24,16},{1,9},{9,1},{17,25},{25,17},{2,10},{10... | collective-permute-start | bytes 491528 | tf_op jit(solution)/shard_map/ppermute | solution.py:379
  34.5 0.6 %collective-permute-done.11 = bf16[64,1280]{1,0:T(8,128)(2,1)S(1)} collective-permute-done((bf16[64,1280]{1,0:T(8,128)(2,1)S(1)}, bf16[64,1280]{1,0:T(8,128)(2,1)S(1)}, u32[]{:S(2)}, u32[]{:S(2)}) %collective-permute-start.11) | collective-permute-done | bytes 163872 | tf_op jit(solution)/shard_map/ppermute | solution.py:379
  35.2 0.4 %relay.2.base_ref = f32[128,2560]{1,0:T(8,128)S(1)} custom-call(f32[1,128]{1,0:T(1,128)S(1)} %get-tuple-element.57.row_ref, f32[1,2560]{1,0:T(1,128)S(1)} %broadcast_in_dim.25.gate_ref, bf16[64,1280]{1,0:T(8,128)(2,1)S(1)} %get-tuple-element.47.first_ref, bf16[64,1280]{1,0:T(8,128)(2,1)S(1)} %get-tuple-element.46.second_ref, ...), custom_call_target="tpu_custom_call" | custom-call | flops 83886080 | bytes 7864320 | tf_op jit(solution)/shard_map/relay/pallas_call | solution.py:341
  35.6 1.8 %collective-permute-done.7 = bf16[64,1280]{1,0:T(8,128)(2,1)S(1)} collective-permute-done((bf16[64,1280]{1,0:T(8,128)(2,1)S(1)}, bf16[64,1280]{1,0:T(8,128)(2,1)S(1)}, u32[]{:S(2)}, u32[]{:S(2)}) %collective-permute-start.7) | collective-permute-done | bytes 163872 | tf_op jit(solution)/shard_map/ppermute | solution.py:379
  37.5 1.8 %collective-permute-done.8 = bf16[64,1280]{1,0:T(8,128)(2,1)S(1)} collective-permute-done((bf16[64,1280]{1,0:T(8,128)(2,1)S(1)}, bf16[64,1280]{1,0:T(8,128)(2,1)S(1)}, u32[]{:S(2)}, u32[]{:S(2)}) %collective-permute-start.8) | collective-permute-done | bytes 163872 | tf_op jit(solution)/shard_map/ppermute | solution.py:379
  39.4 1.3 %relay.3 = bf16[128,2560]{1,0:T(8,128)(2,1)} custom-call(f32[1,128]{1,0:T(1,128)S(1)} %get-tuple-element.57.row_ref, f32[1,2560]{1,0:T(1,128)S(1)} %broadcast_in_dim.25.gate_ref, bf16[64,1280]{1,0:T(8,128)(2,1)S(1)} %get-tuple-element.49.first_ref, bf16[64,1280]{1,0:T(8,128)(2,1)S(1)} %get-tuple-element.48.second_ref, f32[128,2560]{1,0:T(8,128)S(1)} %relay.2.base_ref), custom_call_target="tpu_custom_call" | custom-call | flops 83886080 | bytes 7864320 | tf_op jit(solution)/shard_map/relay/pallas_call | solution.py:341
  40.7 0.9 %maximum_bitcast_fusion = bf16[1,128,2560]{2,1,0:T(8,128)(2,1)} fusion(bf16[64,1280]{1,0:T(8,128)(2,1)S(1)} %get-tuple-element.50, bf16[64,1280]{1,0:T(8,128)(2,1)S(1)} %get-tuple-element.53, bf16[64,1280]{1,0:T(8,128)(2,1)S(1)} %get-tuple-element.51, bf16[64,1280]{1,0:T(8,128)(2,1)S(1)} %get-tuple-element.52), kind=kLoop, calls=%fused_computation.1 | loop fusion | flops 2621440 | bytes 1310720 | tf_op jit(solution)/shard_map/broadcast_in_dim | solution.py:443
  (34 shorter events, 1.7 us)
Async XLA Ops:
  0.6 14.2 %copy-start = (bf16[1,1,128,2560]{3,2,1,0:T(8,128)(2,1)S(1)}, bf16[1,1,128,2560]{3,2,1,0:T(8,128)(2,1)}, u32[]{:S(2)}) copy-start(bf16[1,1,128,2560]{3,2,1,0:T(8,128)(2,1)} %param.8) | copy-start | bytes 1966084
  0.6 14.2 %copy-start.1 = (bf16[1,1,128,2560]{3,2,1,0:T(8,128)(2,1)S(1)}, bf16[1,1,128,2560]{3,2,1,0:T(8,128)(2,1)}, u32[]{:S(2)}) copy-start(bf16[1,1,128,2560]{3,2,1,0:T(8,128)(2,1)} %param.9) | copy-start | bytes 1966084
  0.7 8.2 %copy-start.3 = (f32[1280]{0:T(1024)S(1)}, f32[1280]{0:T(1024)}, u32[]{:S(2)}) copy-start(f32[1280]{0:T(1024)} %param.12) | copy-start | bytes 15364
  0.7 14.2 %copy-start.2 = (bf16[1,1,128,2560]{3,2,1,0:T(8,128)(2,1)S(1)}, bf16[1,1,128,2560]{3,2,1,0:T(8,128)(2,1)}, u32[]{:S(2)}) copy-start(bf16[1,1,128,2560]{3,2,1,0:T(8,128)(2,1)} %param.7) | copy-start | bytes 1966084
  4.3 12.5 %collective-permute-start.1 = (bf16[128,1408]{1,0:T(8,128)(2,1)S(1)}, bf16[128,1408]{1,0:T(8,128)(2,1)S(1)}, u32[]{:S(2)}, u32[]{:S(2)}) collective-permute-start(bf16[128,1408]{1,0:T(8,128)(2,1)S(1)} %get-tuple-element.15.refs_0_), channel_id=1, source_target_pairs={{0,8},{8,0},{16,24},{24,16},{1,9},{9,1},{17,25},{25,17},{2,10},{10... | collective-permute-start | bytes 1081352 | tf_op jit(solution)/shard_map/ppermute | solution.py:379
  7.3 10.0 %collective-permute-start.2 = (bf16[128,1408]{1,0:T(8,128)(2,1)S(1)}, bf16[128,1408]{1,0:T(8,128)(2,1)}, u32[]{:S(2)}, u32[]{:S(2)}) collective-permute-start(bf16[128,1408]{1,0:T(8,128)(2,1)S(1)} %get-tuple-element.16.refs_2_), channel_id=1, source_target_pairs={{0,16},{16,0},{8,24},{24,8},{1,17},{17,1},{9,25},{25,9},{2,18},{18... | collective-permute-start | bytes 1081352 | tf_op jit(solution)/shard_map/ppermute | solution.py:379
  8.8 7.9 %collective-permute-start = (f32[1280]{0:T(1024)S(1)}, f32[1280]{0:T(1024)S(1)}, u32[]{:S(2)}, u32[]{:S(2)}) collective-permute-start(f32[1280]{0:T(1024)S(1)} %copy-done.3), channel_id=1, source_target_pairs={{0,1},{1,0},{2,3},{3,2},{4,5},{5,4},{6,7},{7,6},{8,9},{9,8},{10,11... | collective-permute-start | bytes 15368 | tf_op jit(solution)/shard_map/ppermute | solution.py:358
  8.8 12.0 %collective-permute-start.3 = (bf16[32,5248]{1,0:T(8,128)(2,1)}, bf16[32,5248]{1,0:T(8,128)(2,1)}, u32[]{:S(2)}, u32[]{:S(2)}) collective-permute-start(bf16[32,5248]{1,0:T(8,128)(2,1)} %get-tuple-element.22), channel_id=1, source_target_pairs={{0,2},{2,0},{4,6},{6,4},{1,3},{3,1},{5,7},{7,5},{8,10},{10,8},{12,... | collective-permute-start | bytes 1007624 | tf_op jit(solution)/shard_map/ppermute | solution.py:31
  10.4 10.4 %collective-permute-start.4 = (bf16[32,5248]{1,0:T(8,128)(2,1)}, bf16[32,5248]{1,0:T(8,128)(2,1)}, u32[]{:S(2)}, u32[]{:S(2)}) collective-permute-start(bf16[32,5248]{1,0:T(8,128)(2,1)} %get-tuple-element.23), channel_id=1, source_target_pairs={{0,0},{2,4},{4,2},{6,6},{1,1},{3,5},{5,3},{7,7},{8,8},{10,12},{12,... | collective-permute-start | bytes 1007624 | tf_op jit(solution)/shard_map/ppermute | solution.py:31
  18.7 7.9 %collective-permute-start.10 = (bf16[64,1280]{1,0:T(8,128)(2,1)S(1)}, bf16[64,1280]{1,0:T(8,128)(2,1)S(1)}, u32[]{:S(2)}, u32[]{:S(2)}) collective-permute-start(bf16[64,1280]{1,0:T(8,128)(2,1)S(1)} %get-tuple-element.38), channel_id=1, source_target_pairs={{0,16},{16,24},{24,8},{8,0},{1,17},{17,25},{25,9},{9,1},{2,18},{18... | collective-permute-start | bytes 491528 | tf_op jit(solution)/shard_map/ppermute | solution.py:379
  20.3 6.3 %collective-permute-start.9 = (bf16[64,1280]{1,0:T(8,128)(2,1)S(1)}, bf16[64,1280]{1,0:T(8,128)(2,1)S(1)}, u32[]{:S(2)}, u32[]{:S(2)}) collective-permute-start(bf16[64,1280]{1,0:T(8,128)(2,1)S(1)} %get-tuple-element.39), channel_id=1, source_target_pairs={{0,8},{8,24},{24,16},{16,0},{1,9},{9,25},{25,17},{17,1},{2,10},{10... | collective-permute-start | bytes 491528 | tf_op jit(solution)/shard_map/ppermute | solution.py:379
  24.5 7.1 %collective-permute-start.5 = (bf16[64,1280]{1,0:T(8,128)(2,1)S(1)}, bf16[64,1280]{1,0:T(8,128)(2,1)S(1)}, u32[]{:S(2)}, u32[]{:S(2)}) collective-permute-start(bf16[64,1280]{1,0:T(8,128)(2,1)S(1)} %get-tuple-element.43), channel_id=1, source_target_pairs={{0,8},{8,24},{24,16},{16,0},{1,9},{9,25},{25,17},{17,1},{2,10},{10... | collective-permute-start | bytes 491528 | tf_op jit(solution)/shard_map/ppermute | solution.py:379
  24.9 7.0 %collective-permute-start.6 = (bf16[64,1280]{1,0:T(8,128)(2,1)S(1)}, bf16[64,1280]{1,0:T(8,128)(2,1)S(1)}, u32[]{:S(2)}, u32[]{:S(2)}) collective-permute-start(bf16[64,1280]{1,0:T(8,128)(2,1)S(1)} %get-tuple-element.42), channel_id=1, source_target_pairs={{0,16},{16,24},{24,8},{8,0},{1,17},{17,25},{25,9},{9,1},{2,18},{18... | collective-permute-start | bytes 491528 | tf_op jit(solution)/shard_map/ppermute | solution.py:379
  26.8 8.3 %collective-permute-start.11 = (bf16[64,1280]{1,0:T(8,128)(2,1)S(1)}, bf16[64,1280]{1,0:T(8,128)(2,1)S(1)}, u32[]{:S(2)}, u32[]{:S(2)}) collective-permute-start(bf16[64,1280]{1,0:T(8,128)(2,1)S(1)} %get-tuple-element.36), channel_id=1, source_target_pairs={{0,16},{16,0},{8,24},{24,8},{1,17},{17,1},{9,25},{25,9},{2,18},{18... | collective-permute-start | bytes 491528 | tf_op jit(solution)/shard_map/ppermute | solution.py:379
  28.4 6.7 %collective-permute-start.12 = (bf16[64,1280]{1,0:T(8,128)(2,1)S(1)}, bf16[64,1280]{1,0:T(8,128)(2,1)S(1)}, u32[]{:S(2)}, u32[]{:S(2)}) collective-permute-start(bf16[64,1280]{1,0:T(8,128)(2,1)S(1)} %get-tuple-element.28), channel_id=1, source_target_pairs={{0,8},{8,0},{16,24},{24,16},{1,9},{9,1},{17,25},{25,17},{2,10},{10... | collective-permute-start | bytes 491528 | tf_op jit(solution)/shard_map/ppermute | solution.py:379
  32.1 5.4 %collective-permute-start.7 = (bf16[64,1280]{1,0:T(8,128)(2,1)S(1)}, bf16[64,1280]{1,0:T(8,128)(2,1)S(1)}, u32[]{:S(2)}, u32[]{:S(2)}) collective-permute-start(bf16[64,1280]{1,0:T(8,128)(2,1)S(1)} %get-tuple-element.40), channel_id=1, source_target_pairs={{0,16},{16,0},{8,24},{24,8},{1,17},{17,1},{9,25},{25,9},{2,18},{18... | collective-permute-start | bytes 491528 | tf_op jit(solution)/shard_map/ppermute | solution.py:379
  34.0 5.3 %collective-permute-start.8 = (bf16[64,1280]{1,0:T(8,128)(2,1)S(1)}, bf16[64,1280]{1,0:T(8,128)(2,1)S(1)}, u32[]{:S(2)}, u32[]{:S(2)}) collective-permute-start(bf16[64,1280]{1,0:T(8,128)(2,1)S(1)} %get-tuple-element.32), channel_id=1, source_target_pairs={{0,8},{8,0},{16,24},{24,16},{1,9},{9,1},{17,25},{25,17},{2,10},{10... | collective-permute-start | bytes 491528 | tf_op jit(solution)/shard_map/ppermute | solution.py:379

commit v6 on v5

--- a/solution.py
+++ b/solution.py
@@ -13,7 +13,8 @@
 FRAMES = 20
 LANES = 128
 VMEM_LIMIT = 48 * 1024 * 1024
-PACK_LIMIT = 52 * 1024 * 1024
+PACK_LIMIT = 53 * 1024 * 1024
+ENDS_LIMIT = 53 * 1024 * 1024
 
 
 def shifted(block, axis, distance):
@@ -79,11 +80,12 @@
             part.reshape(len(members), rows, -1) + bias[None]
             for part, (bias, key, value) in zip(parts, sets)
         ]
-        largest = row_reduce(jnp.maximum, jnp.max, parts)
-        powers = [jnp.exp2((part - largest) * factor) for part in parts]
-        scale = 1.0 / row_reduce(jnp.add, jnp.sum, powers)
+        largest = row_max(parts)
         weights.append(
-            [(p * scale).astype(jnp.bfloat16).reshape(len(members) * rows, -1) for p in powers]
+            [
+                jnp.exp2((part - largest) * factor).astype(jnp.bfloat16).reshape(len(members) * rows, -1)
+                for part in parts
+            ]
         )
     tiles = {}
     for parts, (start, members) in zip(weights, windows):
@@ -92,12 +94,18 @@
             jnp.dot(part, value(lanes), preferred_element_type=jnp.float32)
             for part, (bias, key, value) in zip(parts, sets)
         )
+        totals = sum(
+            jnp.dot(part, jnp.ones((part.shape[1], LANES), part.dtype), preferred_element_type=jnp.float32)
+            for part in parts
+        )
+        scale = 1.0 / totals
         for n, h in enumerate(members):
             for t in range(2):
                 low = start + t * LANES
                 if h * DH >= low + LANES or (h + 1) * DH <= low:
                     continue
-                piece = mixed[n * rows : (n + 1) * rows, t * LANES : (t + 1) * LANES]
+                mine = slice(n * rows, (n + 1) * rows)
+                piece = mixed[mine, t * LANES : (t + 1) * LANES] * scale[mine]
                 if low in tiles:
                     lane = lax.broadcasted_iota(jnp.int32, (rows, LANES), 1) + low
                     tiles[low] = jnp.where(lane >= h * DH, piece, tiles[low])
@@ -106,10 +114,10 @@
     return {low: tile.astype(jnp.bfloat16) for low, tile in tiles.items()}
 
 
-def row_reduce(pair, reduce, parts):
+def row_max(parts):
     if all(part.shape == parts[0].shape for part in parts):
-        return reduce(functools.reduce(pair, parts), axis=-1, keepdims=True)
-    return functools.reduce(pair, [reduce(part, axis=-1, keepdims=True) for part in parts])
+        return jnp.max(functools.reduce(jnp.maximum, parts), axis=-1, keepdims=True)
+    return functools.reduce(jnp.maximum, [jnp.max(part, axis=-1, keepdims=True) for part in parts])
 
 
 def columns(row):
@@ -218,17 +226,42 @@
     )(valid, queries, keys, values, code, *halos)
 
 
-def pack_kernel(most, first_ref, k_ref, v_ref, grad_ref, mark_ref, *refs):
-    half_refs, end_refs, sems = refs[:2], refs[2:4], refs[4]
-    width = k_ref.shape[1]
-    half = width // 2
+def pack_grads_kernel(grad_ref, mark_ref, first_ref, second_ref, sems):
+    half = grad_ref.shape[1] // 2
     copies = []
-    for n, ref in enumerate(half_refs):
+    for n, ref in enumerate((first_ref, second_ref)):
         copies.append(
             pltpu.make_async_copy(
                 grad_ref.at[:, pl.ds(n * half, half)], ref.at[:, pl.ds(0, half)], sems.at[n]
             )
         )
+    for copy in copies:
+        copy.start()
+    place = columns(mark_ref[1:2]).astype(jnp.bfloat16)
+    for ref in (first_ref, second_ref):
+        ref[:, half:] = place
+    for copy in copies:
+        copy.wait()
+
+
+def pack_grads(grads, marks):
+    tokens, width = grads.shape
+    return pl.pallas_call(
+        pack_grads_kernel,
+        in_specs=[pl.BlockSpec(memory_space=pltpu.HBM), VMEM],
+        out_specs=[VMEM] * 2,
+        out_shape=[jax.ShapeDtypeStruct((tokens, width // 2 + LANES), jnp.bfloat16)] * 2,
+        scratch_shapes=[pltpu.SemaphoreType.DMA((2,))],
+        compiler_params=pltpu.CompilerParams(vmem_limit_bytes=PACK_LIMIT),
+        cost_estimate=pl.CostEstimate(flops=0, bytes_accessed=4 * tokens * width, transcendentals=0),
+        name="pack_grads",
+    )(grads, marks)
+
+
+def pack_ends_kernel(most, first_ref, k_ref, v_ref, mark_ref, gate_ref, *refs):
+    end_refs, sems = refs[:2], refs[2]
+    tokens, width = k_ref.shape
+    copies = []
     for n, ref in enumerate(end_refs):
         first = pl.multiple_of(first_ref[n], most)
         for m, source in enumerate((k_ref, v_ref)):
@@ -236,39 +269,34 @@
                 pltpu.make_async_copy(
                     source.at[pl.ds(first, most)],
                     ref.at[:, pl.ds(m * width, width)],
-                    sems.at[2 + 2 * n + m],
+                    sems.at[2 * n + m],
                 )
             )
     for copy in copies:
         copy.start()
-    tokens = grad_ref.shape[0]
     code = columns(mark_ref[:1])
     for n, ref in enumerate(end_refs):
         here = jnp.where(first_ref[n] == 0, code[:most], code[tokens - most :])
         ref[:, 2 * width :] = here.astype(jnp.bfloat16)
-    place = columns(mark_ref[1:2]).astype(jnp.bfloat16)
-    for ref in half_refs:
-        ref[:, half:] = place
     for copy in copies:
         copy.wait()
 
 
-def pack(firsts, keys, values, grads, marks, most):
+def pack_ends(firsts, keys, values, marks, gate, most):
     tokens, width = keys.shape
     ends = jax.ShapeDtypeStruct((most, 2 * width + LANES), jnp.bfloat16)
-    halves = jax.ShapeDtypeStruct((tokens, width // 2 + LANES), jnp.bfloat16)
     return pl.pallas_call(
-        functools.partial(pack_kernel, most),
-        in_specs=[SMEM] + [pl.BlockSpec(memory_space=pltpu.HBM)] * 3 + [VMEM],
-        out_specs=[VMEM] * 4,
-        out_shape=[halves, halves, ends, ends],
-        scratch_shapes=[pltpu.SemaphoreType.DMA((6,))],
-        compiler_params=pltpu.CompilerParams(vmem_limit_bytes=PACK_LIMIT),
+        functools.partial(pack_ends_kernel, most),
+        in_specs=[SMEM] + [pl.BlockSpec(memory_space=pltpu.HBM)] * 2 + [VMEM] * 2,
+        out_specs=[VMEM] * 2,
+        out_shape=[ends, ends],
+        scratch_shapes=[pltpu.SemaphoreType.DMA((4,))],
+        compiler_params=pltpu.CompilerParams(vmem_limit_bytes=ENDS_LIMIT),
         cost_estimate=pl.CostEstimate(
-            flops=0, bytes_accessed=4 * tokens * width + 16 * most * width, transcendentals=0
+            flops=0, bytes_accessed=16 * most * width, transcendentals=0
         ),
-        name="pack",
-    )(firsts, keys, values, grads, marks)
+        name="pack_ends",
+    )(firsts, keys, values, marks, gate)
 
 
 def selector(row):
@@ -324,31 +352,80 @@
     return [(0, reach, 0), (tokens - reach, reach, reach)]
 
 
-def relay_kernel(spots, row_ref, gate_ref, first_ref, second_ref, base_ref, out_ref):
-    tokens, width = out_ref.shape
+def relay_kernel(spots, first_row, chunks, row_ref, gate_ref, branch_refs, base_ref, total_refs, *refs):
+    grad_ref, out_ref, staged, sems, grad_sems = refs[-5:]
+    tokens, width = base_ref.shape
     half = width // 2
+    copies = []
+    for n, ref in enumerate(total_refs):
+        copies.append(
+            pltpu.make_async_copy(
+                ref,
+                grad_ref.at[pl.ds(first_row, ref.shape[0]), pl.ds(n * half, half)],
+                grad_sems.at[n],
+            )
+        )
+    for copy in copies:
+        copy.start()
     picks = selector(row_ref[...]).T.astype(jnp.bfloat16)
     picks = jnp.concatenate([picks[:, top : top + size] for top, size, at in spots], axis=1)
-    for n, ref in enumerate((first_ref, second_ref)):
-        lanes = slice(n * half, (n + 1) * half)
-        relayed = jnp.dot(picks, ref[...], preferred_element_type=jnp.float32)
-        total = base_ref[:, lanes].astype(jnp.float32) + gate_ref[:, lanes] * relayed
-        out_ref[:, lanes] = total.astype(out_ref.dtype)
-
-
-def relay(rows, gate, first, second, base, spots, dtype):
+    step = half // chunks
+    for n, ref in enumerate(branch_refs):
+        for c in range(chunks):
+            lanes = slice(n * half + c * step, n * half + (c + 1) * step)
+            relayed = jnp.dot(
+                picks, ref[:, c * step : (c + 1) * step], preferred_element_type=jnp.float32
+            )
+            total = base_ref[:, lanes].astype(jnp.float32) + gate_ref[:, lanes] * relayed
+            staged[:, lanes] = total.astype(staged.dtype)
+            if sems is not None:
+                part = pl.ds(n * half + c * step, step)
+                copy = pltpu.make_async_copy(
+                    staged.at[:, part], out_ref.at[:, part], sems.at[n * chunks + c]
+                )
+                copy.start()
+                copies.append(copy)
+    for copy in copies:
+        copy.wait()
+
+
+def relay(rows, gate, branch, base, totals, spots, first_row, grads, last):
     tokens, width = base.shape
+    chunks = 2 if width // 2 % (2 * LANES) == 0 else 1
+    far = pl.BlockSpec(memory_space=pltpu.HBM)
+    whole = jax.ShapeDtypeStruct((tokens, width), jnp.bfloat16)
+
+    def kernel(row_ref, gate_ref, a_ref, b_ref, base_ref, c_ref, d_ref, *refs):
+        if grads is not None:
+            refs = refs[1:]
+        if last:
+            grad_ref, out_ref, staged, sems, grad_sems = refs
+        else:
+            grad_ref, out_ref, grad_sems = refs
+            staged, sems = out_ref, None
+        relay_kernel(
+            spots, first_row, chunks, row_ref, gate_ref, (a_ref, b_ref), base_ref, (c_ref, d_ref),
+            grad_ref, out_ref, staged, sems, grad_sems,
+        )
+
+    out = whole if last else jax.ShapeDtypeStruct((tokens, width), jnp.float32)
+    scratch = [pltpu.VMEM((tokens, width), jnp.bfloat16), pltpu.SemaphoreType.DMA((2 * chunks,))]
+    operands = [rows, gate, *branch, base, *totals] + ([] if grads is None else [grads])
     return pl.pallas_call(
-        functools.partial(relay_kernel, spots),
-        in_specs=[VMEM] * 5,
-        out_specs=VMEM,
-        out_shape=jax.ShapeDtypeStruct((tokens, width), dtype),
+        kernel,
+        in_specs=[VMEM] * 7 + ([] if grads is None else [far]),
+        out_specs=[far, far if last else VMEM],
+        out_shape=[whole, out],
+        input_output_aliases={} if grads is None else {7: 0},
+        scratch_shapes=(scratch if last else []) + [pltpu.SemaphoreType.DMA((2,))],
         compiler_params=PARAMS,
         cost_estimate=pl.CostEstimate(
-            flops=2 * tokens * tokens * width, bytes_accessed=24 * tokens * width, transcendentals=0
+            flops=2 * tokens * tokens * width,
+            bytes_accessed=24 * tokens * width,
+            transcendentals=0,
         ),
         name="relay",
-    )(rows, gate, first, second, base)
+    )(*operands)
 
 
 def whole_gate(gate):
@@ -385,8 +462,10 @@
     most = min(tokens, reach)
     even = rank % 2 == 0
     firsts = jnp.where(jnp.stack((even, ~even)), tokens - most, 0).astype(jnp.int32)
-    sent_a, sent_b, end_one, end_two = pack(firsts, keys, values, out_grad[0, 0], marks, most)
+    sent_a, sent_b = pack_grads(out_grad[0, 0], marks)
     got_a, got_b = send(sent_a, SWAP_X), send(sent_b, SWAP_Y)
+    gate = whole_gate(control_gate)[None]
+    end_one, end_two = pack_ends(firsts, keys, values, marks, gate, most)
     halos = [paired(end_one, "seq", 0), paired(end_two, "seq", 1)]
     above, below = rank < ranks - 1, rank > 0
     valid = jnp.where(jnp.stack((even, ~even)), above, below).astype(jnp.float32)
@@ -395,7 +474,6 @@
         tail, head = jnp.where(even, end_one, end_two), jnp.where(even, end_two, end_one)
         halos.append(shifted(tail[most - count :], "seq", hop))
         halos.append(shifted(head[:count], "seq", -hop))
-    gate = whole_gate(control_gate)[None]
 
     own = []
     sizes = [min(tokens, 2 * reach)]
@@ -404,10 +482,21 @@
         sizes.insert(0, tokens - 2 * reach)
     flags = jnp.stack([group == 1, group == 2]).astype(jnp.float32)
     sums = pair_sums(flags, gate, (sent_a, got_a, sent_b, got_b), sizes)
-    valid, *sums = lax.optimization_barrier((valid, *sums))
+    count = len(sizes)
+
+    def outgoing(piece, sum_a, sum_b):
+        to_a = jnp.where(group == 0, piece[:, :half], jnp.where(group == 1, sum_a, sum_b))
+        to_b = jnp.where(group == 0, piece[:, half:], jnp.where(group == 2, sum_b, sum_a))
+        return to_a, to_b
+
+    going = [outgoing(own[0], sums[0], sums[count])] if own else []
+    valid, *ready = lax.optimization_barrier((valid, *sums, *(going[0] if going else ())))
+    sums = ready[: 2 * count]
+    if going:
+        going = [ready[2 * count :]]
     own.append(attend_edges(valid, queries, keys, values, code, halos, reach))
 
-    count = len(own)
+    going.append(outgoing(own[-1], sums[count - 1], sums[2 * count - 1]))
     spots = [piece_spots(tokens, reach, n) for n in range(count)]
     order = [
         own[n][at : at + size] for top, size, n, at in sorted(
@@ -415,11 +504,10 @@
         )
     ]
     block_out = jnp.concatenate(order, axis=0)
-    totals = []
+    branch_grad, first_row = None, 0
     for n, (piece, sum_a, sum_b) in enumerate(zip(own, sums[:count], sums[count:])):
         piece_a, piece_b = piece[:, :half], piece[:, half:]
-        one = send(jnp.where(group == 0, piece_a, jnp.where(group == 1, sum_a, sum_b)), ROUND_A)
-        two = send(jnp.where(group == 0, piece_b, jnp.where(group == 2, sum_b, sum_a)), ROUND_B)
+        one, two = send(going[n][0], ROUND_A), send(going[n][1], ROUND_B)
         total_a = added(sum_a, jnp.where(group == 1, two, one))
         total_b = added(sum_b, jnp.where(group == 2, one, two))
         held_a = jnp.where(group == 0, piece_a, one)
@@ -428,18 +516,15 @@
         down = send(jnp.where(group <= 1, held_a, total_b), SWAP_Y)
         branch_a = jnp.where(group <= 1, held_a, down)
         branch_b = jnp.where((group == 0) | (group == 2), held_b, across)
-        dtype = jnp.bfloat16 if n == count - 1 else jnp.float32
-        block_out = relay(rows, gate, branch_a, branch_b, block_out, spots[n], dtype)
-        totals.append(
-            jnp.concatenate(
-                (
-                    jnp.where((group == 0) | (group == 2), across, total_a),
-                    jnp.where(group <= 1, down, total_b),
-                ),
-                axis=1,
-            )
-        )
-    branch_grad = jnp.concatenate(totals, axis=0)
+        totals = (
+            jnp.where((group == 0) | (group == 2), across, total_a),
+            jnp.where(group <= 1, down, total_b),
+        )
+        branch_grad, block_out = relay(
+            rows, gate, (branch_a, branch_b), block_out, totals, spots[n], first_row, branch_grad,
+            n == count - 1,
+        )
+        first_row += piece.shape[0]
     return (block_out[None, None], branch_grad[None])
 
 

time: 42.3 us -> 44.7 us (1.057)
  the two profiles are of different devices: /device:TPU:0 before, /device:TPU:8 now
where the time goes in v6:
time: 44.7 us; the launch traced here: 44.4 us
  starting transfers between devices  15.9 us (36%)
  waiting for transfers between devices  12.5 us (28%)
  Pallas kernels  10.2 us (23%)
  local copies, waits for them, and re-layouts  3.32 us (7%)
  other arithmetic  1.59 us (4%)
  between operations  0.87 us (2%)
    ppermute x10, starting transfers between devices, local(): send = lambda block, route: lax.ppermute(block, 'grp', route)  10.7 us
    ppermute x10, waiting for transfers between devices, local(): send = lambda block, route: lax.ppermute(block, 'grp', route)  7.87 us
    ppermute x2, starting transfers between devices, paired(): return lax.ppermute(block, axis, route)  5.1 us
    ppermute x2, waiting for transfers between devices, paired(): return lax.ppermute(block, axis, route)  4.6 us
    unnamed x14, local copies, waits for them, and re-layouts  3.29 us
    pallas_call x1, Pallas kernels, attend_edges(): pl.pallas_call(functools.partial(edge_kernel, reach), in_specs=[SMEM] + [...  2.74 us
    pallas_call x2, Pallas kernels, relay(): pl.pallas_call(kernel, in_specs=[VMEM] * 7 + ([] if grads is None else [f...  2.11 us
    pallas_call x1, Pallas kernels, pack_ends(): pl.pallas_call(functools.partial(pack_ends_kernel, most), in_specs=[SMEM]...  1.73 us
  transfers between devices with their start and end apart: 13, of which 7 were waited for; matrix products, arithmetic and copies ran while one was open for 3% of the time, Pallas kernels for 20%

profile of v6, /device:TPU:8, one launch (start us, length us, event | category | flops | bytes accessed | tf_op | source)
XLA Modules:
  0.0 44.4 jit_solution(9194535312523435646)
XLA Ops:
  0.7 0.7 %and_select_fusion = (s32[1,128]{1,0:T(1,128)S(1)}, s32[1,128]{1,0:T(1,128)S(1)}) fusion(s32[1,1,128]{2,1,0:T(1,128)} %param.11, s32[1,1,128]{2,1,0:T(1,128)} %param.10), kind=kLoop, calls=%fused_computation.33 | loop fusion | flops 2816 | bytes 2048 | tf_op jit(solution)/shard_map/jit(remainder)/select_n | solution.py:460
  1.4 1.1 %pack_grads.1 = (bf16[128,1408]{1,0:T(8,128)(2,1)S(1)}, bf16[128,1408]{1,0:T(8,128)(2,1)S(1)}) custom-call(bf16[128,2560]{1,0:T(8,128)(2,1)} %bitcast.35, f32[2,128]{1,0:T(2,128)S(1)} %add_convert_fusion.5.mark_ref), custom_call_target="tpu_custom_call" | custom-call | bytes 1310720 | tf_op jit(solution)/shard_map/pack_grads/pallas_call | solution.py:249
  2.5 1.6 %collective-permute-start.1 = (bf16[128,1408]{1,0:T(8,128)(2,1)S(1)}, bf16[128,1408]{1,0:T(8,128)(2,1)S(1)}, u32[]{:S(2)}, u32[]{:S(2)}) collective-permute-start(bf16[128,1408]{1,0:T(8,128)(2,1)S(1)} %get-tuple-element.21.refs_0_), channel_id=1, source_target_pairs={{0,8},{8,0},{16,24},{24,16},{1,9},{9,1},{17,25},{25,17},{2,10},{10... | collective-permute-start | bytes 1081352 | tf_op jit(solution)/shard_map/ppermute | solution.py:456
  4.1 1.5 %collective-permute-start.2 = (bf16[128,1408]{1,0:T(8,128)(2,1)S(1)}, bf16[128,1408]{1,0:T(8,128)(2,1)S(1)}, u32[]{:S(2)}, u32[]{:S(2)}) collective-permute-start(bf16[128,1408]{1,0:T(8,128)(2,1)S(1)} %get-tuple-element.22.refs_2_), channel_id=1, source_target_pairs={{0,16},{16,0},{8,24},{24,8},{1,17},{17,1},{9,25},{25,9},{2,18},{18... | collective-permute-start | bytes 1081352 | tf_op jit(solution)/shard_map/ppermute | solution.py:456
  5.8 1.1 %copy-done = bf16[1,1,128,2560]{3,2,1,0:T(8,128)(2,1)S(1)} copy-done((bf16[1,1,128,2560]{3,2,1,0:T(8,128)(2,1)S(1)}, bf16[1,1,128,2560]{3,2,1,0:T(8,128)(2,1)}, u32[]{:S(2)}) %copy-start) | copy-done | bytes 655384
  6.9 1.1 %copy-done.2 = bf16[1,1,128,2560]{3,2,1,0:T(8,128)(2,1)S(1)} copy-done((bf16[1,1,128,2560]{3,2,1,0:T(8,128)(2,1)S(1)}, bf16[1,1,128,2560]{3,2,1,0:T(8,128)(2,1)}, u32[]{:S(2)}) %copy-start.2) | copy-done | bytes 655384
  8.0 1.1 %copy-done.4 = bf16[1,1,128,2560]{3,2,1,0:T(8,128)(2,1)S(1)} copy-done((bf16[1,1,128,2560]{3,2,1,0:T(8,128)(2,1)S(1)}, bf16[1,1,128,2560]{3,2,1,0:T(8,128)(2,1)}, u32[]{:S(2)}) %copy-start.4) | copy-done | bytes 655384
  9.1 1.6 %attend_middle.1 = bf16[64,2560]{1,0:T(8,128)(2,1)S(1)} custom-call(bf16[128,2560]{1,0:T(8,128)(2,1)S(1)} %bitcast.33, bf16[128,2560]{1,0:T(8,128)(2,1)S(1)} %bitcast.28, bf16[128,2560]{1,0:T(8,128)(2,1)S(1)} %bitcast.31, f32[1,128]{1,0:T(1,128)S(1)} %get-tuple-element.68.code_ref), custom_call_target="tpu_custom_call" | custom-call | flops 268435456 | bytes 1966080 | tf_op jit(solution)/shard_map/attend_middle/pallas_call | solution.py:198
  10.8 1.7 %pack_ends.1 = (bf16[32,5248]{1,0:T(8,128)(2,1)S(1)}, bf16[32,5248]{1,0:T(8,128)(2,1)S(1)}) custom-call(s32[2]{0:T(128)S(1)} %broadcast_select_fusion.18.first_ref, bf16[128,2560]{1,0:T(8,128)(2,1)} %bitcast.27, bf16[128,2560]{1,0:T(8,128)(2,1)} %bitcast.30, f32[2,128]{1,0:T(2,128)S(1)} %add_convert_fusion.5.mark_ref, f32[1,2560]{1,0:T(1,128)S(1)} %broadcast_in_dim.25.gate_ref), custom_call_target="tpu_custom_call" | custom-call | bytes 1310720 | tf_op jit(solution)/shard_map/pack_ends/pallas_call | solution.py:288
  13.1 4.6 %collective-permute-start.4 = (bf16[32,5248]{1,0:T(8,128)(2,1)S(1)}, bf16[32,5248]{1,0:T(8,128)(2,1)S(1)}, u32[]{:S(2)}, u32[]{:S(2)}) collective-permute-start(bf16[32,5248]{1,0:T(8,128)(2,1)S(1)} %get-tuple-element.29), channel_id=1, source_target_pairs={{0,0},{2,4},{4,2},{6,6},{1,1},{3,5},{5,3},{7,7},{8,8},{10,12},{12,... | collective-permute-start | bytes 1007624 | tf_op jit(solution)/shard_map/ppermute | solution.py:32
  17.7 1.0 %pair_sums.1 = (bf16[64,1280]{1,0:T(8,128)(2,1)S(1)}, bf16[64,1280]{1,0:T(8,128)(2,1)S(1)}, bf16[64,1280]{1,0:T(8,128)(2,1)S(1)}, bf16[64,1280]{1,0:T(8,128)(2,1)S(1)}) custom-call(f32[2]{0:T(128)S(1)} %add_convert_fusion.4.flag_ref, f32[1,2560]{1,0:T(1,128)S(1)} %broadcast_in_dim.25.gate_ref, bf16[128,1408]{1,0:T(8,128)(2,1)S(1)} %get-tuple-element.21.refs_0_, ...), custom_call_target="tpu_custom_call" | custom-call | flops 167772160 | bytes 1966080 | tf_op jit(solution)/shard_map/pair_sums/pallas_call | solution.py:334
  18.7 0.6 %collective-permute-start.9 = (bf16[64,1280]{1,0:T(8,128)(2,1)S(1)}, bf16[64,1280]{1,0:T(8,128)(2,1)S(1)}, u32[]{:S(2)}, u32[]{:S(2)}) collective-permute-start(bf16[64,1280]{1,0:T(8,128)(2,1)S(1)} %get-tuple-element.32), channel_id=1, source_target_pairs={{0,8},{8,24},{24,16},{16,0},{1,9},{9,25},{25,17},{17,1},{2,10},{10... | collective-permute-start | bytes 491528 | tf_op jit(solution)/shard_map/ppermute | solution.py:456
  19.3 1.5 %collective-permute-start.10 = (bf16[64,1280]{1,0:T(8,128)(2,1)S(1)}, bf16[64,1280]{1,0:T(8,128)(2,1)S(1)}, u32[]{:S(2)}, u32[]{:S(2)}) collective-permute-start(bf16[64,1280]{1,0:T(8,128)(2,1)S(1)} %get-tuple-element.34), channel_id=1, source_target_pairs={{0,16},{16,24},{24,8},{8,0},{1,17},{17,25},{25,9},{9,1},{2,18},{18... | collective-permute-start | bytes 491528 | tf_op jit(solution)/shard_map/ppermute | solution.py:456
  20.8 1.6 %collective-permute-done.3.refs_0_ = bf16[32,5248]{1,0:T(8,128)(2,1)S(1)} collective-permute-done((bf16[32,5248]{1,0:T(8,128)(2,1)S(1)}, bf16[32,5248]{1,0:T(8,128)(2,1)S(1)}, u32[]{:S(2)}, u32[]{:S(2)}) %collective-permute-start.3) | collective-permute-done | bytes 335904 | tf_op jit(solution)/shard_map/ppermute | solution.py:32
  22.4 3.0 %collective-permute-done.4.refs_1_ = bf16[32,5248]{1,0:T(8,128)(2,1)S(1)} collective-permute-done((bf16[32,5248]{1,0:T(8,128)(2,1)S(1)}, bf16[32,5248]{1,0:T(8,128)(2,1)S(1)}, u32[]{:S(2)}, u32[]{:S(2)}) %collective-permute-start.4) | collective-permute-done | bytes 335904 | tf_op jit(solution)/shard_map/ppermute | solution.py:32
  25.4 2.7 %attend_edges.1 = bf16[64,2560]{1,0:T(8,128)(2,1)S(1)} custom-call(f32[2]{0:T(128)S(1)} %select_convert_fusion.valid_ref, bf16[128,2560]{1,0:T(8,128)(2,1)S(1)} %bitcast.34, bf16[128,2560]{1,0:T(8,128)(2,1)S(1)} %bitcast.29, bf16[128,2560]{1,0:T(8,128)(2,1)S(1)} %bitcast.32, f32[1,128]{1,0:T(1,128)S(1)} %get-tuple-element.68.code_ref, ...), custom_call_target="tpu_custom_call" | custom-call | flops 268435456 | bytes 1966080 | tf_op jit(solution)/shard_map/attend_edges/pallas_call | solution.py:213
  28.8 1.5 %collective-permute-start.5 = (bf16[64,1280]{1,0:T(8,128)(2,1)S(1)}, bf16[64,1280]{1,0:T(8,128)(2,1)S(1)}, u32[]{:S(2)}, u32[]{:S(2)}) collective-permute-start(bf16[64,1280]{1,0:T(8,128)(2,1)S(1)} %get-tuple-element.53), channel_id=1, source_target_pairs={{0,8},{8,24},{24,16},{16,0},{1,9},{9,25},{25,17},{17,1},{2,10},{10... | collective-permute-start | bytes 491528 | tf_op jit(solution)/shard_map/ppermute | solution.py:456
  31.6 3.7 %collective-permute-done.6 = bf16[64,1280]{1,0:T(8,128)(2,1)S(1)} collective-permute-done((bf16[64,1280]{1,0:T(8,128)(2,1)S(1)}, bf16[64,1280]{1,0:T(8,128)(2,1)S(1)}, u32[]{:S(2)}, u32[]{:S(2)}) %collective-permute-start.6) | collective-permute-done | bytes 163872 | tf_op jit(solution)/shard_map/ppermute | solution.py:456
  35.6 2.1 %collective-permute-start.8 = (bf16[64,1280]{1,0:T(8,128)(2,1)S(1)}, bf16[64,1280]{1,0:T(8,128)(2,1)S(1)}, u32[]{:S(2)}, u32[]{:S(2)}) collective-permute-start(bf16[64,1280]{1,0:T(8,128)(2,1)S(1)} %get-tuple-element.44), channel_id=1, source_target_pairs={{0,8},{8,0},{16,24},{24,16},{1,9},{9,1},{17,25},{25,17},{2,10},{10... | collective-permute-start | bytes 491528 | tf_op jit(solution)/shard_map/ppermute | solution.py:456
  38.0 0.7 %collective-permute-done.12 = bf16[64,1280]{1,0:T(8,128)(2,1)S(1)} collective-permute-done((bf16[64,1280]{1,0:T(8,128)(2,1)S(1)}, bf16[64,1280]{1,0:T(8,128)(2,1)S(1)}, u32[]{:S(2)}, u32[]{:S(2)}) %collective-permute-start.12) | collective-permute-done | bytes 163872 | tf_op jit(solution)/shard_map/ppermute | solution.py:456
  38.8 0.8 %relay.2 = (bf16[128,2560]{1,0:T(8,128)(2,1)}, f32[128,2560]{1,0:T(8,128)S(1)}) custom-call(f32[1,128]{1,0:T(1,128)S(1)} %get-tuple-element.69.row_ref, f32[1,2560]{1,0:T(1,128)S(1)} %broadcast_in_dim.25.gate_ref, bf16[64,1280]{1,0:T(8,128)(2,1)S(1)} %get-tuple-element.59.a_ref, bf16[64,1280]{1,0:T(8,128)(2,1)S(1)} %get-tuple-element.58.b_ref, ...), custom_call_target="tpu_custom_call" | custom-call | flops 83886080 | bytes 7864320 | tf_op jit(solution)/shard_map/relay/pallas_call | solution.py:414
  39.7 1.3 %collective-permute-done.8 = bf16[64,1280]{1,0:T(8,128)(2,1)S(1)} collective-permute-done((bf16[64,1280]{1,0:T(8,128)(2,1)S(1)}, bf16[64,1280]{1,0:T(8,128)(2,1)S(1)}, u32[]{:S(2)}, u32[]{:S(2)}) %collective-permute-start.8) | collective-permute-done | bytes 163872 | tf_op jit(solution)/shard_map/ppermute | solution.py:456
  41.0 2.0 %collective-permute-done.7 = bf16[64,1280]{1,0:T(8,128)(2,1)S(1)} collective-permute-done((bf16[64,1280]{1,0:T(8,128)(2,1)S(1)}, bf16[64,1280]{1,0:T(8,128)(2,1)S(1)}, u32[]{:S(2)}, u32[]{:S(2)}) %collective-permute-start.7) | collective-permute-done | bytes 163872 | tf_op jit(solution)/shard_map/ppermute | solution.py:456
  43.1 1.3 %relay.3 = (bf16[128,2560]{1,0:T(8,128)(2,1)}, bf16[128,2560]{1,0:T(8,128)(2,1)}) custom-call(f32[1,128]{1,0:T(1,128)S(1)} %get-tuple-element.69.row_ref, f32[1,2560]{1,0:T(1,128)S(1)} %broadcast_in_dim.25.gate_ref, bf16[64,1280]{1,0:T(8,128)(2,1)S(1)} %get-tuple-element.61.a_ref, ...), custom_call_target="tpu_custom_call", output_to_operand_aliasing={{0}: (7, {})} | custom-call | flops 83886080 | bytes 7864320 | tf_op jit(solution)/shard_map/relay/pallas_call | solution.py:414
  (40 shorter events, 3.7 us)
Async XLA Ops:
  0.6 10.1 %collective-permute-start = (f32[1280]{0:T(1024)}, f32[1280]{0:T(1024)S(1)}, u32[]{:S(2)}, u32[]{:S(2)}) collective-permute-start(f32[1280]{0:T(1024)} %param.12), channel_id=1, source_target_pairs={{0,1},{1,0},{2,3},{3,2},{4,5},{5,4},{6,7},{7,6},{8,9},{9,8},{10,11... | collective-permute-start | bytes 15368 | tf_op jit(solution)/shard_map/ppermute | solution.py:435
  2.5 8.2 %copy-start.6 = (f32[1280]{0:T(1024)S(1)}, f32[1280]{0:T(1024)}, u32[]{:S(2)}) copy-start(f32[1280]{0:T(1024)} %param.12) | copy-start | bytes 15364
  2.5 15.2 %collective-permute-start.1 = (bf16[128,1408]{1,0:T(8,128)(2,1)S(1)}, bf16[128,1408]{1,0:T(8,128)(2,1)S(1)}, u32[]{:S(2)}, u32[]{:S(2)}) collective-permute-start(bf16[128,1408]{1,0:T(8,128)(2,1)S(1)} %get-tuple-element.21.refs_0_), channel_id=1, source_target_pairs={{0,8},{8,0},{16,24},{24,16},{1,9},{9,1},{17,25},{25,17},{2,10},{10... | collective-permute-start | bytes 1081352 | tf_op jit(solution)/shard_map/ppermute | solution.py:456
  4.1 13.6 %collective-permute-start.2 = (bf16[128,1408]{1,0:T(8,128)(2,1)S(1)}, bf16[128,1408]{1,0:T(8,128)(2,1)S(1)}, u32[]{:S(2)}, u32[]{:S(2)}) collective-permute-start(bf16[128,1408]{1,0:T(8,128)(2,1)S(1)} %get-tuple-element.22.refs_2_), channel_id=1, source_target_pairs={{0,16},{16,0},{8,24},{24,8},{1,17},{17,1},{9,25},{25,9},{2,18},{18... | collective-permute-start | bytes 1081352 | tf_op jit(solution)/shard_map/ppermute | solution.py:456
  5.8 1.1 %copy-start = (bf16[1,1,128,2560]{3,2,1,0:T(8,128)(2,1)S(1)}, bf16[1,1,128,2560]{3,2,1,0:T(8,128)(2,1)}, u32[]{:S(2)}) copy-start(bf16[1,1,128,2560]{3,2,1,0:T(8,128)(2,1)} %param.8) | copy-start | bytes 1966084
  6.9 1.1 %copy-start.2 = (bf16[1,1,128,2560]{3,2,1,0:T(8,128)(2,1)S(1)}, bf16[1,1,128,2560]{3,2,1,0:T(8,128)(2,1)}, u32[]{:S(2)}) copy-start(bf16[1,1,128,2560]{3,2,1,0:T(8,128)(2,1)} %param.9) | copy-start | bytes 1966084
  8.0 1.1 %copy-start.4 = (bf16[1,1,128,2560]{3,2,1,0:T(8,128)(2,1)S(1)}, bf16[1,1,128,2560]{3,2,1,0:T(8,128)(2,1)}, u32[]{:S(2)}) copy-start(bf16[1,1,128,2560]{3,2,1,0:T(8,128)(2,1)} %param.7) | copy-start | bytes 1966084
  12.5 12.9 %copy-start.1 = (bf16[1,1,128,2560]{3,2,1,0:T(8,128)(2,1)S(1)}, bf16[1,1,128,2560]{3,2,1,0:T(8,128)(2,1)}, u32[]{:S(2)}) copy-start(bf16[1,1,128,2560]{3,2,1,0:T(8,128)(2,1)} %param.8) | copy-start | bytes 1966084
  12.5 12.8 %copy-start.3 = (bf16[1,1,128,2560]{3,2,1,0:T(8,128)(2,1)S(1)}, bf16[1,1,128,2560]{3,2,1,0:T(8,128)(2,1)}, u32[]{:S(2)}) copy-start(bf16[1,1,128,2560]{3,2,1,0:T(8,128)(2,1)} %param.9) | copy-start | bytes 1966084
  12.6 12.8 %copy-start.5 = (bf16[1,1,128,2560]{3,2,1,0:T(8,128)(2,1)S(1)}, bf16[1,1,128,2560]{3,2,1,0:T(8,128)(2,1)}, u32[]{:S(2)}) copy-start(bf16[1,1,128,2560]{3,2,1,0:T(8,128)(2,1)} %param.7) | copy-start | bytes 1966084
  12.6 9.8 %collective-permute-start.3 = (bf16[32,5248]{1,0:T(8,128)(2,1)S(1)}, bf16[32,5248]{1,0:T(8,128)(2,1)S(1)}, u32[]{:S(2)}, u32[]{:S(2)}) collective-permute-start(bf16[32,5248]{1,0:T(8,128)(2,1)S(1)} %get-tuple-element.28), channel_id=1, source_target_pairs={{0,2},{2,0},{4,6},{6,4},{1,3},{3,1},{5,7},{7,5},{8,10},{10,8},{12,... | collective-permute-start | bytes 1007624 | tf_op jit(solution)/shard_map/ppermute | solution.py:32
  13.1 12.3 %collective-permute-start.4 = (bf16[32,5248]{1,0:T(8,128)(2,1)S(1)}, bf16[32,5248]{1,0:T(8,128)(2,1)S(1)}, u32[]{:S(2)}, u32[]{:S(2)}) collective-permute-start(bf16[32,5248]{1,0:T(8,128)(2,1)S(1)} %get-tuple-element.29), channel_id=1, source_target_pairs={{0,0},{2,4},{4,2},{6,6},{1,1},{3,5},{5,3},{7,7},{8,8},{10,12},{12,... | collective-permute-start | bytes 1007624 | tf_op jit(solution)/shard_map/ppermute | solution.py:32
  18.7 11.6 %collective-permute-start.9 = (bf16[64,1280]{1,0:T(8,128)(2,1)S(1)}, bf16[64,1280]{1,0:T(8,128)(2,1)S(1)}, u32[]{:S(2)}, u32[]{:S(2)}) collective-permute-start(bf16[64,1280]{1,0:T(8,128)(2,1)S(1)} %get-tuple-element.32), channel_id=1, source_target_pairs={{0,8},{8,24},{24,16},{16,0},{1,9},{9,25},{25,17},{17,1},{2,10},{10... | collective-permute-start | bytes 491528 | tf_op jit(solution)/shard_map/ppermute | solution.py:456
  19.3 11.1 %collective-permute-start.10 = (bf16[64,1280]{1,0:T(8,128)(2,1)S(1)}, bf16[64,1280]{1,0:T(8,128)(2,1)S(1)}, u32[]{:S(2)}, u32[]{:S(2)}) collective-permute-start(bf16[64,1280]{1,0:T(8,128)(2,1)S(1)} %get-tuple-element.34), channel_id=1, source_target_pairs={{0,16},{16,24},{24,8},{8,0},{1,17},{17,25},{25,9},{9,1},{2,18},{18... | collective-permute-start | bytes 491528 | tf_op jit(solution)/shard_map/ppermute | solution.py:456
  28.2 7.1 %collective-permute-start.6 = (bf16[64,1280]{1,0:T(8,128)(2,1)S(1)}, bf16[64,1280]{1,0:T(8,128)(2,1)S(1)}, u32[]{:S(2)}, u32[]{:S(2)}) collective-permute-start(bf16[64,1280]{1,0:T(8,128)(2,1)S(1)} %get-tuple-element.52), channel_id=1, source_target_pairs={{0,16},{16,24},{24,8},{8,0},{1,17},{17,25},{25,9},{9,1},{2,18},{18... | collective-permute-start | bytes 491528 | tf_op jit(solution)/shard_map/ppermute | solution.py:456
  28.8 6.6 %collective-permute-start.5 = (bf16[64,1280]{1,0:T(8,128)(2,1)S(1)}, bf16[64,1280]{1,0:T(8,128)(2,1)S(1)}, u32[]{:S(2)}, u32[]{:S(2)}) collective-permute-start(bf16[64,1280]{1,0:T(8,128)(2,1)S(1)} %get-tuple-element.53), channel_id=1, source_target_pairs={{0,8},{8,24},{24,16},{16,0},{1,9},{9,25},{25,17},{17,1},{2,10},{10... | collective-permute-start | bytes 491528 | tf_op jit(solution)/shard_map/ppermute | solution.py:456
  30.6 8.2 %collective-permute-start.12 = (bf16[64,1280]{1,0:T(8,128)(2,1)S(1)}, bf16[64,1280]{1,0:T(8,128)(2,1)S(1)}, u32[]{:S(2)}, u32[]{:S(2)}) collective-permute-start(bf16[64,1280]{1,0:T(8,128)(2,1)S(1)} %get-tuple-element.40), channel_id=1, source_target_pairs={{0,8},{8,0},{16,24},{24,16},{1,9},{9,1},{17,25},{25,17},{2,10},{10... | collective-permute-start | bytes 491528 | tf_op jit(solution)/shard_map/ppermute | solution.py:456
  31.1 7.6 %collective-permute-start.11 = (bf16[64,1280]{1,0:T(8,128)(2,1)S(1)}, bf16[64,1280]{1,0:T(8,128)(2,1)S(1)}, u32[]{:S(2)}, u32[]{:S(2)}) collective-permute-start(bf16[64,1280]{1,0:T(8,128)(2,1)S(1)} %get-tuple-element.48), channel_id=1, source_target_pairs={{0,16},{16,0},{8,24},{24,8},{1,17},{17,1},{9,25},{25,9},{2,18},{18... | collective-permute-start | bytes 491528 | tf_op jit(solution)/shard_map/ppermute | solution.py:456
  35.6 5.4 %collective-permute-start.8 = (bf16[64,1280]{1,0:T(8,128)(2,1)S(1)}, bf16[64,1280]{1,0:T(8,128)(2,1)S(1)}, u32[]{:S(2)}, u32[]{:S(2)}) collective-permute-start(bf16[64,1280]{1,0:T(8,128)(2,1)S(1)} %get-tuple-element.44), channel_id=1, source_target_pairs={{0,8},{8,0},{16,24},{24,16},{1,9},{9,1},{17,25},{25,17},{2,10},{10... | collective-permute-start | bytes 491528 | tf_op jit(solution)/shard_map/ppermute | solution.py:456
  37.7 5.3 %collective-permute-start.7 = (bf16[64,1280]{1,0:T(8,128)(2,1)S(1)}, bf16[64,1280]{1,0:T(8,128)(2,1)S(1)}, u32[]{:S(2)}, u32[]{:S(2)}) collective-permute-start(bf16[64,1280]{1,0:T(8,128)(2,1)S(1)} %get-tuple-element.50), channel_id=1, source_target_pairs={{0,16},{16,0},{8,24},{24,8},{1,17},{17,1},{9,25},{25,9},{2,18},{18... | collective-permute-start | bytes 491528 | tf_op jit(solution)/shard_map/ppermute | solution.py:456

commit v7 on v6

--- a/solution.py
+++ b/solution.py
@@ -258,7 +258,7 @@
     )(grads, marks)
 
 
-def pack_ends_kernel(most, first_ref, k_ref, v_ref, mark_ref, gate_ref, *refs):
+def pack_ends_kernel(most, first_ref, k_ref, v_ref, mark_ref, *refs):
     end_refs, sems = refs[:2], refs[2]
     tokens, width = k_ref.shape
     copies = []
@@ -282,12 +282,12 @@
         copy.wait()
 
 
-def pack_ends(firsts, keys, values, marks, gate, most):
+def pack_ends(firsts, keys, values, marks, most):
     tokens, width = keys.shape
     ends = jax.ShapeDtypeStruct((most, 2 * width + LANES), jnp.bfloat16)
     return pl.pallas_call(
         functools.partial(pack_ends_kernel, most),
-        in_specs=[SMEM] + [pl.BlockSpec(memory_space=pltpu.HBM)] * 2 + [VMEM] * 2,
+        in_specs=[SMEM] + [pl.BlockSpec(memory_space=pltpu.HBM)] * 2 + [VMEM],
         out_specs=[VMEM] * 2,
         out_shape=[ends, ends],
         scratch_shapes=[pltpu.SemaphoreType.DMA((4,))],
@@ -296,7 +296,7 @@
             flops=0, bytes_accessed=16 * most * width, transcendentals=0
         ),
         name="pack_ends",
-    )(firsts, keys, values, marks, gate)
+    )(firsts, keys, values, marks)
 
 
 def selector(row):
@@ -463,9 +463,11 @@
     even = rank % 2 == 0
     firsts = jnp.where(jnp.stack((even, ~even)), tokens - most, 0).astype(jnp.int32)
     sent_a, sent_b = pack_grads(out_grad[0, 0], marks)
+    marks, sent_a, sent_b = lax.optimization_barrier((marks, sent_a, sent_b))
     got_a, got_b = send(sent_a, SWAP_X), send(sent_b, SWAP_Y)
+    end_one, end_two = pack_ends(firsts, keys, values, marks, most)
+    code, end_one, end_two = lax.optimization_barrier((code, end_one, end_two))
     gate = whole_gate(control_gate)[None]
-    end_one, end_two = pack_ends(firsts, keys, values, marks, gate, most)
     halos = [paired(end_one, "seq", 0), paired(end_two, "seq", 1)]
     above, below = rank < ranks - 1, rank > 0
     valid = jnp.where(jnp.stack((even, ~even)), above, below).astype(jnp.float32)

time: 44.7 us -> 41.2 us (0.922)
  the two profiles are of different devices: /device:TPU:8 before, /device:TPU:0 now
where the time goes in v7:
time: 41.2 us; the launch traced here: 40.7 us
  starting transfers between devices  18.2 us (44%)
  Pallas kernels  12 us (29%)
  waiting for transfers between devices  7.84 us (19%)
  other arithmetic  1.63 us (4%)
  between operations  0.86 us (2%)
    ppermute x10, starting transfers between devices, local(): send = lambda block, route: lax.ppermute(block, 'grp', route)  11.8 us
    ppermute x10, waiting for transfers between devices, local(): send = lambda block, route: lax.ppermute(block, 'grp', route)  7.83 us
    ppermute x2, starting transfers between devices, paired(): return lax.ppermute(block, axis, route)  5.96 us
    pallas_call x1, Pallas kernels, attend_edges(): pl.pallas_call(functools.partial(edge_kernel, reach), in_specs=[SMEM] + [...  3.27 us
    pallas_call x1, Pallas kernels, pack_ends(): pl.pallas_call(functools.partial(pack_ends_kernel, most), in_specs=[SMEM]...  2.57 us
    pallas_call x2, Pallas kernels, relay(): pl.pallas_call(kernel, in_specs=[VMEM] * 7 + ([] if grads is None else [f...  2.11 us
    pallas_call x1, Pallas kernels, attend_middle(): pl.pallas_call(functools.partial(middle_kernel, reach), in_specs=[VMEM] *...  1.6 us
    pallas_call x1, Pallas kernels, pair_sums(): pl.pallas_call(functools.partial(sums_kernel, sizes), in_specs=[SMEM] + [...  1.39 us
  transfers between devices with their start and end apart: 13, of which 4 were waited for; matrix products, arithmetic and copies ran while one was open for 4% of the time, Pallas kernels for 26%

profile of v7, /device:TPU:0, one launch (start us, length us, event | category | flops | bytes accessed | tf_op | source)
XLA Modules:
  0.0 40.7 jit_solution(1805914821631756620)
XLA Ops:
  0.7 0.5 %collective-permute-start = (f32[1280]{0:T(1024)}, f32[1280]{0:T(1024)S(1)}, u32[]{:S(2)}, u32[]{:S(2)}) collective-permute-start(f32[1280]{0:T(1024)} %param.12), channel_id=1, source_target_pairs={{0,1},{1,0},{2,3},{3,2},{4,5},{5,4},{6,7},{7,6},{8,9},{9,8},{10,11... | collective-permute-start | bytes 15368 | tf_op jit(solution)/shard_map/ppermute | solution.py:435
  1.2 0.7 %and_select_fusion = (s32[1,128]{1,0:T(1,128)S(1)}, s32[1,128]{1,0:T(1,128)S(1)}) fusion(s32[1,1,128]{2,1,0:T(1,128)} %param.11, s32[1,1,128]{2,1,0:T(1,128)} %param.10), kind=kLoop, calls=%fused_computation.33 | loop fusion | flops 2816 | bytes 2048 | tf_op jit(solution)/shard_map/jit(remainder)/select_n | solution.py:460
  1.9 1.1 %pack_grads.1 = (bf16[128,1408]{1,0:T(8,128)(2,1)S(1)}, bf16[128,1408]{1,0:T(8,128)(2,1)S(1)}) custom-call(bf16[128,2560]{1,0:T(8,128)(2,1)} %bitcast.35, f32[2,128]{1,0:T(2,128)S(1)} %add_convert_fusion.5.mark_ref), custom_call_target="tpu_custom_call" | custom-call | bytes 1310720 | tf_op jit(solution)/shard_map/pack_grads/pallas_call | solution.py:249
  3.0 2.7 %collective-permute-start.1 = (bf16[128,1408]{1,0:T(8,128)(2,1)S(1)}, bf16[128,1408]{1,0:T(8,128)(2,1)S(1)}, u32[]{:S(2)}, u32[]{:S(2)}) collective-permute-start(bf16[128,1408]{1,0:T(8,128)(2,1)S(1)} %get-tuple-element.29.refs_0_), channel_id=1, source_target_pairs={{0,8},{8,0},{16,24},{24,16},{1,9},{9,1},{17,25},{25,17},{2,10},{10... | collective-permute-start | bytes 1081352 | tf_op jit(solution)/shard_map/ppermute | solution.py:456
  5.7 1.5 %collective-permute-start.2 = (bf16[128,1408]{1,0:T(8,128)(2,1)S(1)}, bf16[128,1408]{1,0:T(8,128)(2,1)}, u32[]{:S(2)}, u32[]{:S(2)}) collective-permute-start(bf16[128,1408]{1,0:T(8,128)(2,1)S(1)} %get-tuple-element.30.refs_2_), channel_id=1, source_target_pairs={{0,16},{16,0},{8,24},{24,8},{1,17},{17,1},{9,25},{25,9},{2,18},{18... | collective-permute-start | bytes 1081352 | tf_op jit(solution)/shard_map/ppermute | solution.py:456
  7.3 2.6 %pack_ends.1 = (bf16[32,5248]{1,0:T(8,128)(2,1)}, bf16[32,5248]{1,0:T(8,128)(2,1)}) custom-call(s32[2]{0:T(128)S(1)} %broadcast_select_fusion.18.first_ref, bf16[128,2560]{1,0:T(8,128)(2,1)} %bitcast.27, bf16[128,2560]{1,0:T(8,128)(2,1)} %bitcast.30, f32[2,128]{1,0:T(2,128)S(1)} %add_convert_fusion.5.mark_ref), custom_call_target="tpu_custom_call" | custom-call | bytes 1310720 | tf_op jit(solution)/shard_map/pack_ends/pallas_call | solution.py:288
  9.9 1.6 %collective-permute-start.3 = (bf16[32,5248]{1,0:T(8,128)(2,1)}, bf16[32,5248]{1,0:T(8,128)(2,1)}, u32[]{:S(2)}, u32[]{:S(2)}) collective-permute-start(bf16[32,5248]{1,0:T(8,128)(2,1)} %get-tuple-element.40), channel_id=1, source_target_pairs={{0,2},{2,0},{4,6},{6,4},{1,3},{3,1},{5,7},{7,5},{8,10},{10,8},{12,... | collective-permute-start | bytes 1007624 | tf_op jit(solution)/shard_map/ppermute | solution.py:32
  11.5 4.3 %collective-permute-start.4 = (bf16[32,5248]{1,0:T(8,128)(2,1)}, bf16[32,5248]{1,0:T(8,128)(2,1)}, u32[]{:S(2)}, u32[]{:S(2)}) collective-permute-start(bf16[32,5248]{1,0:T(8,128)(2,1)} %get-tuple-element.41), channel_id=1, source_target_pairs={{0,0},{2,4},{4,2},{6,6},{1,1},{3,5},{5,3},{7,7},{8,8},{10,12},{12,... | collective-permute-start | bytes 1007624 | tf_op jit(solution)/shard_map/ppermute | solution.py:32
  16.0 1.6 %attend_middle.1 = bf16[64,2560]{1,0:T(8,128)(2,1)S(1)} custom-call(bf16[128,2560]{1,0:T(8,128)(2,1)S(1)} %bitcast.33, bf16[128,2560]{1,0:T(8,128)(2,1)S(1)} %bitcast.28, bf16[128,2560]{1,0:T(8,128)(2,1)S(1)} %bitcast.31, f32[1,128]{1,0:T(1,128)S(1)} %get-tuple-element.38.code_ref), custom_call_target="tpu_custom_call" | custom-call | flops 268435456 | bytes 1966080 | tf_op jit(solution)/shard_map/attend_middle/pallas_call | solution.py:198
  17.7 1.4 %pair_sums.1 = (bf16[64,1280]{1,0:T(8,128)(2,1)S(1)}, bf16[64,1280]{1,0:T(8,128)(2,1)S(1)}, bf16[64,1280]{1,0:T(8,128)(2,1)S(1)}, bf16[64,1280]{1,0:T(8,128)(2,1)S(1)}) custom-call(f32[2]{0:T(128)S(1)} %add_convert_fusion.4.flag_ref, f32[1,2560]{1,0:T(1,128)S(1)} %broadcast_in_dim.25.gate_ref, bf16[128,1408]{1,0:T(8,128)(2,1)S(1)} %get-tuple-element.29.refs_0_, ...), custom_call_target="tpu_custom_call" | custom-call | flops 167772160 | bytes 1966080 | tf_op jit(solution)/shard_map/pair_sums/pallas_call | solution.py:334
  19.2 0.6 %collective-permute-start.9 = (bf16[64,1280]{1,0:T(8,128)(2,1)S(1)}, bf16[64,1280]{1,0:T(8,128)(2,1)S(1)}, u32[]{:S(2)}, u32[]{:S(2)}) collective-permute-start(bf16[64,1280]{1,0:T(8,128)(2,1)S(1)} %get-tuple-element.44), channel_id=1, source_target_pairs={{0,8},{8,24},{24,16},{16,0},{1,9},{9,25},{25,17},{17,1},{2,10},{10... | collective-permute-start | bytes 491528 | tf_op jit(solution)/shard_map/ppermute | solution.py:456
  19.8 1.5 %collective-permute-start.10 = (bf16[64,1280]{1,0:T(8,128)(2,1)S(1)}, bf16[64,1280]{1,0:T(8,128)(2,1)S(1)}, u32[]{:S(2)}, u32[]{:S(2)}) collective-permute-start(bf16[64,1280]{1,0:T(8,128)(2,1)S(1)} %get-tuple-element.46), channel_id=1, source_target_pairs={{0,16},{16,24},{24,8},{8,0},{1,17},{17,25},{25,9},{9,1},{2,18},{18... | collective-permute-start | bytes 491528 | tf_op jit(solution)/shard_map/ppermute | solution.py:456
  21.2 3.3 %attend_edges.1 = bf16[64,2560]{1,0:T(8,128)(2,1)S(1)} custom-call(f32[2]{0:T(128)S(1)} %select_convert_fusion.valid_ref, bf16[128,2560]{1,0:T(8,128)(2,1)S(1)} %bitcast.34, bf16[128,2560]{1,0:T(8,128)(2,1)S(1)} %bitcast.29, bf16[128,2560]{1,0:T(8,128)(2,1)S(1)} %bitcast.32, f32[1,128]{1,0:T(1,128)S(1)} %get-tuple-element.38.code_ref, ...), custom_call_target="tpu_custom_call" | custom-call | flops 268435456 | bytes 1966080 | tf_op jit(solution)/shard_map/attend_edges/pallas_call | solution.py:213
  24.6 0.5 %collective-permute-start.6 = (bf16[64,1280]{1,0:T(8,128)(2,1)S(1)}, bf16[64,1280]{1,0:T(8,128)(2,1)S(1)}, u32[]{:S(2)}, u32[]{:S(2)}) collective-permute-start(bf16[64,1280]{1,0:T(8,128)(2,1)S(1)} %get-tuple-element.64), channel_id=1, source_target_pairs={{0,16},{16,24},{24,8},{8,0},{1,17},{17,25},{25,9},{9,1},{2,18},{18... | collective-permute-start | bytes 491528 | tf_op jit(solution)/shard_map/ppermute | solution.py:456
  25.1 1.5 %collective-permute-start.5 = (bf16[64,1280]{1,0:T(8,128)(2,1)S(1)}, bf16[64,1280]{1,0:T(8,128)(2,1)S(1)}, u32[]{:S(2)}, u32[]{:S(2)}) collective-permute-start(bf16[64,1280]{1,0:T(8,128)(2,1)S(1)} %get-tuple-element.65), channel_id=1, source_target_pairs={{0,8},{8,24},{24,16},{16,0},{1,9},{9,25},{25,17},{17,1},{2,10},{10... | collective-permute-start | bytes 491528 | tf_op jit(solution)/shard_map/ppermute | solution.py:456
  26.9 0.6 %collective-permute-start.12 = (bf16[64,1280]{1,0:T(8,128)(2,1)S(1)}, bf16[64,1280]{1,0:T(8,128)(2,1)S(1)}, u32[]{:S(2)}, u32[]{:S(2)}) collective-permute-start(bf16[64,1280]{1,0:T(8,128)(2,1)S(1)} %get-tuple-element.52), channel_id=1, source_target_pairs={{0,8},{8,0},{16,24},{24,16},{1,9},{9,1},{17,25},{25,17},{2,10},{10... | collective-permute-start | bytes 491528 | tf_op jit(solution)/shard_map/ppermute | solution.py:456
  27.6 0.5 %collective-permute-start.11 = (bf16[64,1280]{1,0:T(8,128)(2,1)S(1)}, bf16[64,1280]{1,0:T(8,128)(2,1)S(1)}, u32[]{:S(2)}, u32[]{:S(2)}) collective-permute-start(bf16[64,1280]{1,0:T(8,128)(2,1)S(1)} %get-tuple-element.60), channel_id=1, source_target_pairs={{0,16},{16,0},{8,24},{24,8},{1,17},{17,1},{9,25},{25,9},{2,18},{18... | collective-permute-start | bytes 491528 | tf_op jit(solution)/shard_map/ppermute | solution.py:456
  28.0 3.7 %collective-permute-done.6 = bf16[64,1280]{1,0:T(8,128)(2,1)S(1)} collective-permute-done((bf16[64,1280]{1,0:T(8,128)(2,1)S(1)}, bf16[64,1280]{1,0:T(8,128)(2,1)S(1)}, u32[]{:S(2)}, u32[]{:S(2)}) %collective-permute-start.6) | collective-permute-done | bytes 163872 | tf_op jit(solution)/shard_map/ppermute | solution.py:456
  32.0 2.0 %collective-permute-start.8 = (bf16[64,1280]{1,0:T(8,128)(2,1)S(1)}, bf16[64,1280]{1,0:T(8,128)(2,1)S(1)}, u32[]{:S(2)}, u32[]{:S(2)}) collective-permute-start(bf16[64,1280]{1,0:T(8,128)(2,1)S(1)} %get-tuple-element.56), channel_id=1, source_target_pairs={{0,8},{8,0},{16,24},{24,16},{1,9},{9,1},{17,25},{25,17},{2,10},{10... | collective-permute-start | bytes 491528 | tf_op jit(solution)/shard_map/ppermute | solution.py:456
  34.3 0.7 %collective-permute-done.12 = bf16[64,1280]{1,0:T(8,128)(2,1)S(1)} collective-permute-done((bf16[64,1280]{1,0:T(8,128)(2,1)S(1)}, bf16[64,1280]{1,0:T(8,128)(2,1)S(1)}, u32[]{:S(2)}, u32[]{:S(2)}) %collective-permute-start.12) | collective-permute-done | bytes 163872 | tf_op jit(solution)/shard_map/ppermute | solution.py:456
  35.1 0.8 %relay.2 = (bf16[128,2560]{1,0:T(8,128)(2,1)}, f32[128,2560]{1,0:T(8,128)S(1)}) custom-call(f32[1,128]{1,0:T(1,128)S(1)} %get-tuple-element.81.row_ref, f32[1,2560]{1,0:T(1,128)S(1)} %broadcast_in_dim.25.gate_ref, bf16[64,1280]{1,0:T(8,128)(2,1)S(1)} %get-tuple-element.71.a_ref, bf16[64,1280]{1,0:T(8,128)(2,1)S(1)} %get-tuple-element.70.b_ref, ...), custom_call_target="tpu_custom_call" | custom-call | flops 83886080 | bytes 7864320 | tf_op jit(solution)/shard_map/relay/pallas_call | solution.py:414
  36.0 1.4 %collective-permute-done.8 = bf16[64,1280]{1,0:T(8,128)(2,1)S(1)} collective-permute-done((bf16[64,1280]{1,0:T(8,128)(2,1)S(1)}, bf16[64,1280]{1,0:T(8,128)(2,1)S(1)}, u32[]{:S(2)}, u32[]{:S(2)}) %collective-permute-start.8) | collective-permute-done | bytes 163872 | tf_op jit(solution)/shard_map/ppermute | solution.py:456
  37.3 2.0 %collective-permute-done.7 = bf16[64,1280]{1,0:T(8,128)(2,1)S(1)} collective-permute-done((bf16[64,1280]{1,0:T(8,128)(2,1)S(1)}, bf16[64,1280]{1,0:T(8,128)(2,1)S(1)}, u32[]{:S(2)}, u32[]{:S(2)}) %collective-permute-start.7) | collective-permute-done | bytes 163872 | tf_op jit(solution)/shard_map/ppermute | solution.py:456
  39.4 1.3 %relay.3 = (bf16[128,2560]{1,0:T(8,128)(2,1)}, bf16[128,2560]{1,0:T(8,128)(2,1)}) custom-call(f32[1,128]{1,0:T(1,128)S(1)} %get-tuple-element.81.row_ref, f32[1,2560]{1,0:T(1,128)S(1)} %broadcast_in_dim.25.gate_ref, bf16[64,1280]{1,0:T(8,128)(2,1)S(1)} %get-tuple-element.73.a_ref, ...), custom_call_target="tpu_custom_call", output_to_operand_aliasing={{0}: (7, {})} | custom-call | flops 83886080 | bytes 7864320 | tf_op jit(solution)/shard_map/relay/pallas_call | solution.py:414
  (34 shorter events, 1.3 us)
Async XLA Ops:
  0.6 15.4 %copy-start.1 = (bf16[1,1,128,2560]{3,2,1,0:T(8,128)(2,1)S(1)}, bf16[1,1,128,2560]{3,2,1,0:T(8,128)(2,1)}, u32[]{:S(2)}) copy-start(bf16[1,1,128,2560]{3,2,1,0:T(8,128)(2,1)} %param.9) | copy-start | bytes 1966084
  0.6 15.3 %copy-start = (bf16[1,1,128,2560]{3,2,1,0:T(8,128)(2,1)S(1)}, bf16[1,1,128,2560]{3,2,1,0:T(8,128)(2,1)}, u32[]{:S(2)}) copy-start(bf16[1,1,128,2560]{3,2,1,0:T(8,128)(2,1)} %param.8) | copy-start | bytes 1966084
  0.7 15.3 %copy-start.2 = (bf16[1,1,128,2560]{3,2,1,0:T(8,128)(2,1)S(1)}, bf16[1,1,128,2560]{3,2,1,0:T(8,128)(2,1)}, u32[]{:S(2)}) copy-start(bf16[1,1,128,2560]{3,2,1,0:T(8,128)(2,1)} %param.7) | copy-start | bytes 1966084
  0.7 17.0 %collective-permute-start = (f32[1280]{0:T(1024)}, f32[1280]{0:T(1024)S(1)}, u32[]{:S(2)}, u32[]{:S(2)}) collective-permute-start(f32[1280]{0:T(1024)} %param.12), channel_id=1, source_target_pairs={{0,1},{1,0},{2,3},{3,2},{4,5},{5,4},{6,7},{7,6},{8,9},{9,8},{10,11... | collective-permute-start | bytes 15368 | tf_op jit(solution)/shard_map/ppermute | solution.py:435
  3.0 14.7 %collective-permute-start.1 = (bf16[128,1408]{1,0:T(8,128)(2,1)S(1)}, bf16[128,1408]{1,0:T(8,128)(2,1)S(1)}, u32[]{:S(2)}, u32[]{:S(2)}) collective-permute-start(bf16[128,1408]{1,0:T(8,128)(2,1)S(1)} %get-tuple-element.29.refs_0_), channel_id=1, source_target_pairs={{0,8},{8,0},{16,24},{24,16},{1,9},{9,1},{17,25},{25,17},{2,10},{10... | collective-permute-start | bytes 1081352 | tf_op jit(solution)/shard_map/ppermute | solution.py:456
  5.7 12.0 %collective-permute-start.2 = (bf16[128,1408]{1,0:T(8,128)(2,1)S(1)}, bf16[128,1408]{1,0:T(8,128)(2,1)}, u32[]{:S(2)}, u32[]{:S(2)}) collective-permute-start(bf16[128,1408]{1,0:T(8,128)(2,1)S(1)} %get-tuple-element.30.refs_2_), channel_id=1, source_target_pairs={{0,16},{16,0},{8,24},{24,8},{1,17},{17,1},{9,25},{25,9},{2,18},{18... | collective-permute-start | bytes 1081352 | tf_op jit(solution)/shard_map/ppermute | solution.py:456
  9.9 7.8 %copy-start.3 = (f32[1280]{0:T(1024)S(1)}, f32[1280]{0:T(1024)}, u32[]{:S(2)}) copy-start(f32[1280]{0:T(1024)} %param.12) | copy-start | bytes 15364
  9.9 11.4 %collective-permute-start.3 = (bf16[32,5248]{1,0:T(8,128)(2,1)}, bf16[32,5248]{1,0:T(8,128)(2,1)}, u32[]{:S(2)}, u32[]{:S(2)}) collective-permute-start(bf16[32,5248]{1,0:T(8,128)(2,1)} %get-tuple-element.40), channel_id=1, source_target_pairs={{0,2},{2,0},{4,6},{6,4},{1,3},{3,1},{5,7},{7,5},{8,10},{10,8},{12,... | collective-permute-start | bytes 1007624 | tf_op jit(solution)/shard_map/ppermute | solution.py:32
  11.5 9.7 %collective-permute-start.4 = (bf16[32,5248]{1,0:T(8,128)(2,1)}, bf16[32,5248]{1,0:T(8,128)(2,1)}, u32[]{:S(2)}, u32[]{:S(2)}) collective-permute-start(bf16[32,5248]{1,0:T(8,128)(2,1)} %get-tuple-element.41), channel_id=1, source_target_pairs={{0,0},{2,4},{4,2},{6,6},{1,1},{3,5},{5,3},{7,7},{8,8},{10,12},{12,... | collective-permute-start | bytes 1007624 | tf_op jit(solution)/shard_map/ppermute | solution.py:32
  19.2 7.6 %collective-permute-start.9 = (bf16[64,1280]{1,0:T(8,128)(2,1)S(1)}, bf16[64,1280]{1,0:T(8,128)(2,1)S(1)}, u32[]{:S(2)}, u32[]{:S(2)}) collective-permute-start(bf16[64,1280]{1,0:T(8,128)(2,1)S(1)} %get-tuple-element.44), channel_id=1, source_target_pairs={{0,8},{8,24},{24,16},{16,0},{1,9},{9,25},{25,17},{17,1},{2,10},{10... | collective-permute-start | bytes 491528 | tf_op jit(solution)/shard_map/ppermute | solution.py:456
  19.8 7.0 %collective-permute-start.10 = (bf16[64,1280]{1,0:T(8,128)(2,1)S(1)}, bf16[64,1280]{1,0:T(8,128)(2,1)S(1)}, u32[]{:S(2)}, u32[]{:S(2)}) collective-permute-start(bf16[64,1280]{1,0:T(8,128)(2,1)S(1)} %get-tuple-element.46), channel_id=1, source_target_pairs={{0,16},{16,24},{24,8},{8,0},{1,17},{17,25},{25,9},{9,1},{2,18},{18... | collective-permute-start | bytes 491528 | tf_op jit(solution)/shard_map/ppermute | solution.py:456
  24.6 7.1 %collective-permute-start.6 = (bf16[64,1280]{1,0:T(8,128)(2,1)S(1)}, bf16[64,1280]{1,0:T(8,128)(2,1)S(1)}, u32[]{:S(2)}, u32[]{:S(2)}) collective-permute-start(bf16[64,1280]{1,0:T(8,128)(2,1)S(1)} %get-tuple-element.64), channel_id=1, source_target_pairs={{0,16},{16,24},{24,8},{8,0},{1,17},{17,25},{25,9},{9,1},{2,18},{18... | collective-permute-start | bytes 491528 | tf_op jit(solution)/shard_map/ppermute | solution.py:456
  25.1 6.6 %collective-permute-start.5 = (bf16[64,1280]{1,0:T(8,128)(2,1)S(1)}, bf16[64,1280]{1,0:T(8,128)(2,1)S(1)}, u32[]{:S(2)}, u32[]{:S(2)}) collective-permute-start(bf16[64,1280]{1,0:T(8,128)(2,1)S(1)} %get-tuple-element.65), channel_id=1, source_target_pairs={{0,8},{8,24},{24,16},{16,0},{1,9},{9,25},{25,17},{17,1},{2,10},{10... | collective-permute-start | bytes 491528 | tf_op jit(solution)/shard_map/ppermute | solution.py:456
  26.9 8.1 %collective-permute-start.12 = (bf16[64,1280]{1,0:T(8,128)(2,1)S(1)}, bf16[64,1280]{1,0:T(8,128)(2,1)S(1)}, u32[]{:S(2)}, u32[]{:S(2)}) collective-permute-start(bf16[64,1280]{1,0:T(8,128)(2,1)S(1)} %get-tuple-element.52), channel_id=1, source_target_pairs={{0,8},{8,0},{16,24},{24,16},{1,9},{9,1},{17,25},{25,17},{2,10},{10... | collective-permute-start | bytes 491528 | tf_op jit(solution)/shard_map/ppermute | solution.py:456
  27.6 7.5 %collective-permute-start.11 = (bf16[64,1280]{1,0:T(8,128)(2,1)S(1)}, bf16[64,1280]{1,0:T(8,128)(2,1)S(1)}, u32[]{:S(2)}, u32[]{:S(2)}) collective-permute-start(bf16[64,1280]{1,0:T(8,128)(2,1)S(1)} %get-tuple-element.60), channel_id=1, source_target_pairs={{0,16},{16,0},{8,24},{24,8},{1,17},{17,1},{9,25},{25,9},{2,18},{18... | collective-permute-start | bytes 491528 | tf_op jit(solution)/shard_map/ppermute | solution.py:456
  32.0 5.4 %collective-permute-start.8 = (bf16[64,1280]{1,0:T(8,128)(2,1)S(1)}, bf16[64,1280]{1,0:T(8,128)(2,1)S(1)}, u32[]{:S(2)}, u32[]{:S(2)}) collective-permute-start(bf16[64,1280]{1,0:T(8,128)(2,1)S(1)} %get-tuple-element.56), channel_id=1, source_target_pairs={{0,8},{8,0},{16,24},{24,16},{1,9},{9,1},{17,25},{25,17},{2,10},{10... | collective-permute-start | bytes 491528 | tf_op jit(solution)/shard_map/ppermute | solution.py:456
  34.0 5.3 %collective-permute-start.7 = (bf16[64,1280]{1,0:T(8,128)(2,1)S(1)}, bf16[64,1280]{1,0:T(8,128)(2,1)S(1)}, u32[]{:S(2)}, u32[]{:S(2)}) collective-permute-start(bf16[64,1280]{1,0:T(8,128)(2,1)S(1)} %get-tuple-element.62), channel_id=1, source_target_pairs={{0,16},{16,0},{8,24},{24,8},{1,17},{17,1},{9,25},{25,9},{2,18},{18... | collective-permute-start | bytes 491528 | tf_op jit(solution)/shard_map/ppermute | solution.py:456

commit v8 on v6

--- a/solution.py
+++ b/solution.py
@@ -12,9 +12,8 @@
 DH = 80
 FRAMES = 20
 LANES = 128
-VMEM_LIMIT = 48 * 1024 * 1024
+VMEM_LIMIT = 32 * 1024 * 1024
 PACK_LIMIT = 53 * 1024 * 1024
-ENDS_LIMIT = 53 * 1024 * 1024
 
 
 def shifted(block, axis, distance):
@@ -28,7 +27,8 @@
     route = []
     for i in range(size):
         other = i + 1 if (i - first) % 2 == 0 else i - 1
-        route.append((i, other if 0 <= other < size else i))
+        if 0 <= other < size:
+            route.append((i, other))
     return lax.ppermute(block, axis, route)
 
 
@@ -138,26 +138,39 @@
             out_ref[:, base + low : base + low + LANES] = tile
 
 
-def middle_kernel(reach, q_ref, k_ref, v_ref, code_ref, out_ref):
+def pack_ends(first_ref, k_ref, v_ref, code, end_refs):
+    tokens, width = k_ref.shape
+    for n, ref in enumerate(end_refs):
+        most = ref.shape[0]
+        first = pl.multiple_of(first_ref[n], most)
+        ref[:, :width] = k_ref[pl.ds(first, most), :]
+        ref[:, width : 2 * width] = v_ref[pl.ds(first, most), :]
+        here = jnp.where(first == 0, code[:most], code[tokens - most :])
+        ref[:, 2 * width :] = here.astype(jnp.bfloat16)
+
+
+def middle_kernel(reach, first_ref, q_ref, k_ref, v_ref, code_ref, one_ref, two_ref, out_ref=None):
+    code = columns(code_ref[...])
+    pack_ends(first_ref, k_ref, v_ref, code, (one_ref, two_ref))
+    if out_ref is None:
+        return
     rows = out_ref.shape[0]
-    code = columns(code_ref[...])
     bias = link_bias(code[reach : reach + rows], code)
     own = (bias, lambda lanes: k_ref[:, lanes], lambda lanes: v_ref[:, lanes])
     attend_block(lambda lanes: q_ref[reach : reach + rows, lanes], [own], out_ref)
 
 
-def edge_kernel(reach, valid_ref, q_ref, k_ref, v_ref, code_ref, *refs):
+def edge_kernel(reach, q_ref, k_ref, v_ref, code_ref, *refs):
     halos = refs[:-4]
     out_ref, keys, values, codes = refs[-4:]
     tokens, width = q_ref.shape
     code = columns(code_ref[...])
     at = 0
-    for n, piece in enumerate(halos):
+    for piece in halos:
         rows = piece.shape[0]
         keys[at : at + rows] = piece[:, :width]
         values[at : at + rows] = piece[:, width : 2 * width]
-        there = valid_ref[n] if n < 2 else 1.0
-        codes[at : at + rows] = piece[:, 2 * width :].astype(jnp.float32) * there
+        codes[at : at + rows] = piece[:, 2 * width :].astype(jnp.float32)
         at += rows
     if at < keys.shape[0]:
         spare = keys.shape[0] - at
@@ -193,26 +206,30 @@
 PARAMS = pltpu.CompilerParams(vmem_limit_bytes=VMEM_LIMIT)
 
 
-def attend_middle(queries, keys, values, code, reach):
+def attend_middle(firsts, queries, keys, values, code, reach):
     tokens, width = queries.shape
+    ends = jax.ShapeDtypeStruct((min(tokens, reach), 2 * width + LANES), jnp.bfloat16)
+    outs = [ends, ends]
+    if tokens > 2 * reach:
+        outs.append(jax.ShapeDtypeStruct((tokens - 2 * reach, width), jnp.bfloat16))
     return pl.pallas_call(
         functools.partial(middle_kernel, reach),
-        in_specs=[VMEM] * 4,
-        out_specs=VMEM,
-        out_shape=jax.ShapeDtypeStruct((tokens - 2 * reach, width), jnp.bfloat16),
+        in_specs=[SMEM] + [VMEM] * 4,
+        out_specs=[VMEM] * len(outs),
+        out_shape=outs,
         compiler_params=PARAMS,
-        cost_estimate=attend_cost(tokens - 2 * reach, tokens, width),
+        cost_estimate=attend_cost(tokens, tokens, width),
         name="attend_middle",
-    )(queries, keys, values, code)
-
-
-def attend_edges(valid, queries, keys, values, code, halos, reach):
+    )(firsts, queries, keys, values, code)
+
+
+def attend_edges(queries, keys, values, code, halos, reach):
     tokens, width = queries.shape
     rows = min(tokens, 2 * reach)
     held = -(-2 * reach // LANES) * LANES
     return pl.pallas_call(
         functools.partial(edge_kernel, reach),
-        in_specs=[SMEM] + [VMEM] * (4 + len(halos)),
+        in_specs=[VMEM] * (4 + len(halos)),
         out_specs=VMEM,
         out_shape=jax.ShapeDtypeStruct((rows, width), jnp.bfloat16),
         scratch_shapes=[
@@ -223,10 +240,11 @@
         compiler_params=PARAMS,
         cost_estimate=attend_cost(rows, LANES, width),
         name="attend_edges",
-    )(valid, queries, keys, values, code, *halos)
-
-
-def pack_grads_kernel(grad_ref, mark_ref, first_ref, second_ref, sems):
+    )(queries, keys, values, code, *halos)
+
+
+def pack_grads_kernel(grad_ref, mark_ref, *refs):
+    first_ref, second_ref, sems = refs[-3:]
     half = grad_ref.shape[1] // 2
     copies = []
     for n, ref in enumerate((first_ref, second_ref)):
@@ -244,59 +262,19 @@
         copy.wait()
 
 
-def pack_grads(grads, marks):
+def pack_grads(grads, marks, *others):
     tokens, width = grads.shape
+    far = pl.BlockSpec(memory_space=pltpu.HBM)
     return pl.pallas_call(
         pack_grads_kernel,
-        in_specs=[pl.BlockSpec(memory_space=pltpu.HBM), VMEM],
+        in_specs=[far, VMEM] + [far] * len(others),
         out_specs=[VMEM] * 2,
         out_shape=[jax.ShapeDtypeStruct((tokens, width // 2 + LANES), jnp.bfloat16)] * 2,
         scratch_shapes=[pltpu.SemaphoreType.DMA((2,))],
         compiler_params=pltpu.CompilerParams(vmem_limit_bytes=PACK_LIMIT),
         cost_estimate=pl.CostEstimate(flops=0, bytes_accessed=4 * tokens * width, transcendentals=0),
         name="pack_grads",
-    )(grads, marks)
-
-
-def pack_ends_kernel(most, first_ref, k_ref, v_ref, mark_ref, gate_ref, *refs):
-    end_refs, sems = refs[:2], refs[2]
-    tokens, width = k_ref.shape
-    copies = []
-    for n, ref in enumerate(end_refs):
-        first = pl.multiple_of(first_ref[n], most)
-        for m, source in enumerate((k_ref, v_ref)):
-            copies.append(
-                pltpu.make_async_copy(
-                    source.at[pl.ds(first, most)],
-                    ref.at[:, pl.ds(m * width, width)],
-                    sems.at[2 * n + m],
-                )
-            )
-    for copy in copies:
-        copy.start()
-    code = columns(mark_ref[:1])
-    for n, ref in enumerate(end_refs):
-        here = jnp.where(first_ref[n] == 0, code[:most], code[tokens - most :])
-        ref[:, 2 * width :] = here.astype(jnp.bfloat16)
-    for copy in copies:
-        copy.wait()
-
-
-def pack_ends(firsts, keys, values, marks, gate, most):
-    tokens, width = keys.shape
-    ends = jax.ShapeDtypeStruct((most, 2 * width + LANES), jnp.bfloat16)
-    return pl.pallas_call(
-        functools.partial(pack_ends_kernel, most),
-        in_specs=[SMEM] + [pl.BlockSpec(memory_space=pltpu.HBM)] * 2 + [VMEM] * 2,
-        out_specs=[VMEM] * 2,
-        out_shape=[ends, ends],
-        scratch_shapes=[pltpu.SemaphoreType.DMA((4,))],
-        compiler_params=pltpu.CompilerParams(vmem_limit_bytes=ENDS_LIMIT),
-        cost_estimate=pl.CostEstimate(
-            flops=0, bytes_accessed=16 * most * width, transcendentals=0
-        ),
-        name="pack_ends",
-    )(firsts, keys, values, marks, gate)
+    )(grads, marks, *others)
 
 
 def selector(row):
@@ -462,24 +440,18 @@
     most = min(tokens, reach)
     even = rank % 2 == 0
     firsts = jnp.where(jnp.stack((even, ~even)), tokens - most, 0).astype(jnp.int32)
-    sent_a, sent_b = pack_grads(out_grad[0, 0], marks)
+    sent_a, sent_b = pack_grads(out_grad[0, 0], marks, queries, keys, values)
+    code, sent_a, sent_b = lax.optimization_barrier((code, sent_a, sent_b))
     got_a, got_b = send(sent_a, SWAP_X), send(sent_b, SWAP_Y)
+    end_one, end_two, *own = attend_middle(firsts, queries, keys, values, code, reach)
     gate = whole_gate(control_gate)[None]
-    end_one, end_two = pack_ends(firsts, keys, values, marks, gate, most)
     halos = [paired(end_one, "seq", 0), paired(end_two, "seq", 1)]
-    above, below = rank < ranks - 1, rank > 0
-    valid = jnp.where(jnp.stack((even, ~even)), above, below).astype(jnp.float32)
     for hop in range(2, hops + 1):
         count = min(tokens, reach - (hop - 1) * tokens)
         tail, head = jnp.where(even, end_one, end_two), jnp.where(even, end_two, end_one)
         halos.append(shifted(tail[most - count :], "seq", hop))
         halos.append(shifted(head[:count], "seq", -hop))
-
-    own = []
-    sizes = [min(tokens, 2 * reach)]
-    if tokens > 2 * reach:
-        own.append(attend_middle(queries, keys, values, code, reach))
-        sizes.insert(0, tokens - 2 * reach)
+    sizes = [piece.shape[0] for piece in own] + [min(tokens, 2 * reach)]
     flags = jnp.stack([group == 1, group == 2]).astype(jnp.float32)
     sums = pair_sums(flags, gate, (sent_a, got_a, sent_b, got_b), sizes)
     count = len(sizes)
@@ -490,11 +462,11 @@
         return to_a, to_b
 
     going = [outgoing(own[0], sums[0], sums[count])] if own else []
-    valid, *ready = lax.optimization_barrier((valid, *sums, *(going[0] if going else ())))
+    code, *ready = lax.optimization_barrier((code, *sums, *(going[0] if going else ())))
     sums = ready[: 2 * count]
     if going:
         going = [ready[2 * count :]]
-    own.append(attend_edges(valid, queries, keys, values, code, halos, reach))
+    own.append(attend_edges(queries, keys, values, code, halos, reach))
 
     going.append(outgoing(own[-1], sums[count - 1], sums[2 * count - 1]))
     spots = [piece_spots(tokens, reach, n) for n in range(count)]

time: 44.7 us -> 41.6 us (0.931)
  local copies, waits for them, and re-layouts: 3.32 us -> 0.06 us
  Pallas kernels: 10.2 us -> 10.9 us
    unnamed x14 -> x8, local copies, waits for them, and re-layouts: 3.29 us -> 0.03 us
    ppermute x2, waiting for transfers between devices: 4.6 us -> 3.43 us  [paired(): return lax.ppermute(block, axis, route)]
    ppermute x10, waiting for transfers between devices: 7.87 us -> 8.84 us  [local(): send = lambda block, route: lax.ppermute(block, 'grp', route)]
    pallas_call x4 -> x3, Pallas kernels: 7.17 us -> 7.4 us  [the longest x1 3.23 us: attend_edges(): pl.pallas_call(functools.partial(edge_kernel, reach), in_specs=[VMEM] * (...]
  transfers between devices with their start and end apart: 13 -> 13, of which waited for: 7 -> 8; matrix products, arithmetic and copies ran while one was open for 3% -> 4% of each run, Pallas kernels for 20% -> 23%
where the time goes in v8:
time: 41.6 us; the launch traced here: 41.3 us
  starting transfers between devices  15.8 us (38%)
  waiting for transfers between devices  12.3 us (30%)
  Pallas kernels  10.9 us (26%)
  other arithmetic  1.51 us (4%)
  between operations  0.83 us (2%)
    ppermute x10, starting transfers between devices, local(): send = lambda block, route: lax.ppermute(block, 'grp', route)  10.6 us
    ppermute x10, waiting for transfers between devices, local(): send = lambda block, route: lax.ppermute(block, 'grp', route)  8.84 us
    ppermute x2, starting transfers between devices, paired(): return lax.ppermute(block, axis, route)  5.06 us
    ppermute x2, waiting for transfers between devices, paired(): return lax.ppermute(block, axis, route)  3.43 us
    pallas_call x1, Pallas kernels, attend_edges(): pl.pallas_call(functools.partial(edge_kernel, reach), in_specs=[VMEM] * (...  3.23 us
    pallas_call x1, Pallas kernels, attend_middle(): pl.pallas_call(functools.partial(middle_kernel, reach), in_specs=[SMEM] +...  2.94 us
    pallas_call x2, Pallas kernels, relay(): pl.pallas_call(kernel, in_specs=[VMEM] * 7 + ([] if grads is None else [f...  2.11 us
    pallas_call x1, Pallas kernels, pair_sums(): pl.pallas_call(functools.partial(sums_kernel, sizes), in_specs=[SMEM] + [...  1.39 us
  transfers between devices with their start and end apart: 13, of which 8 were waited for; matrix products, arithmetic and copies ran while one was open for 4% of the time, Pallas kernels for 23%

profile of v8, /device:TPU:8, one launch (start us, length us, event | category | flops | bytes accessed | tf_op | source)
XLA Modules:
  0.0 41.3 jit_solution(3675619716381333276)
XLA Ops:
  0.7 0.7 %and_select_fusion = (s32[1,128]{1,0:T(1,128)S(1)}, s32[1,128]{1,0:T(1,128)S(1)}) fusion(s32[1,1,128]{2,1,0:T(1,128)} %param.11, s32[1,1,128]{2,1,0:T(1,128)} %param.10), kind=kLoop, calls=%fused_computation.32 | loop fusion | flops 2816 | bytes 2048 | tf_op jit(solution)/shard_map/jit(remainder)/select_n | solution.py:438
  1.5 1.2 %pack_grads.1 = (bf16[128,1408]{1,0:T(8,128)(2,1)S(1)}, bf16[128,1408]{1,0:T(8,128)(2,1)S(1)}) custom-call(bf16[128,2560]{1,0:T(8,128)(2,1)} %bitcast.36, f32[2,128]{1,0:T(2,128)S(1)} %add_convert_fusion.5.mark_ref, bf16[128,2560]{1,0:T(8,128)(2,1)} %bitcast.27, bf16[128,2560]{1,0:T(8,128)(2,1)} %bitcast.30, bf16[128,2560]{1,0:T(8,128)(2,1)} %bitcast.33), custom_call_target="tpu_custom_call" | custom-call | bytes 1310720 | tf_op jit(solution)/shard_map/pack_grads/pallas_call | solution.py:268
  2.7 1.6 %collective-permute-start.1 = (bf16[128,1408]{1,0:T(8,128)(2,1)S(1)}, bf16[128,1408]{1,0:T(8,128)(2,1)S(1)}, u32[]{:S(2)}, u32[]{:S(2)}) collective-permute-start(bf16[128,1408]{1,0:T(8,128)(2,1)S(1)} %get-tuple-element.28.refs_0_), channel_id=1, source_target_pairs={{0,8},{8,0},{16,24},{24,16},{1,9},{9,1},{17,25},{25,17},{2,10},{10... | collective-permute-start | bytes 1081352 | tf_op jit(solution)/shard_map/ppermute | solution.py:434
  4.3 1.5 %collective-permute-start.2 = (bf16[128,1408]{1,0:T(8,128)(2,1)S(1)}, bf16[128,1408]{1,0:T(8,128)(2,1)}, u32[]{:S(2)}, u32[]{:S(2)}) collective-permute-start(bf16[128,1408]{1,0:T(8,128)(2,1)S(1)} %get-tuple-element.29.refs_2_), channel_id=1, source_target_pairs={{0,16},{16,0},{8,24},{24,8},{1,17},{17,1},{9,25},{25,9},{2,18},{18... | collective-permute-start | bytes 1081352 | tf_op jit(solution)/shard_map/ppermute | solution.py:434
  5.9 2.9 %attend_middle.1 = (bf16[32,5248]{1,0:T(8,128)(2,1)}, bf16[32,5248]{1,0:T(8,128)(2,1)}, bf16[64,2560]{1,0:T(8,128)(2,1)S(1)}) custom-call(s32[2]{0:T(128)S(1)} %add_select_fusion.first_ref, bf16[128,2560]{1,0:T(8,128)(2,1)S(1)} %bitcast.28, bf16[128,2560]{1,0:T(8,128)(2,1)S(1)} %bitcast.31, bf16[128,2560]{1,0:T(8,128)(2,1)S(1)} %bitcast.34, ...), custom_call_target="tpu_custom_call" | custom-call | flops 536870912 | bytes 3932160 | tf_op jit(solution)/shard_map/attend_middle/pallas_call | solution.py:215
  8.8 0.5 %collective-permute-start.3 = (bf16[32,5248]{1,0:T(8,128)(2,1)}, bf16[32,5248]{1,0:T(8,128)(2,1)}, u32[]{:S(2)}, u32[]{:S(2)}) collective-permute-start(bf16[32,5248]{1,0:T(8,128)(2,1)} %get-tuple-element.36), channel_id=1, source_target_pairs={{0,2},{2,0},{4,6},{6,4},{1,3},{3,1},{5,7},{7,5},{8,10},{10,8},{12,... | collective-permute-start | bytes 1007624 | tf_op jit(solution)/shard_map/ppermute | solution.py:32
  9.3 4.6 %collective-permute-start.4 = (bf16[32,5248]{1,0:T(8,128)(2,1)}, bf16[32,5248]{1,0:T(8,128)(2,1)}, u32[]{:S(2)}, u32[]{:S(2)}) collective-permute-start(bf16[32,5248]{1,0:T(8,128)(2,1)} %get-tuple-element.37), channel_id=1, source_target_pairs={{2,4},{4,2},{3,5},{5,3},{10,12},{12,10},{11,13},{13,11},{18,20},{2... | collective-permute-start | bytes 1007624 | tf_op jit(solution)/shard_map/ppermute | solution.py:32
  14.0 0.9 %collective-permute-done.2.refs_3_ = bf16[128,1408]{1,0:T(8,128)(2,1)} collective-permute-done((bf16[128,1408]{1,0:T(8,128)(2,1)S(1)}, bf16[128,1408]{1,0:T(8,128)(2,1)}, u32[]{:S(2)}, u32[]{:S(2)}) %collective-permute-start.2) | collective-permute-done | bytes 360480 | tf_op jit(solution)/shard_map/ppermute | solution.py:434
  14.9 1.4 %pair_sums.1 = (bf16[64,1280]{1,0:T(8,128)(2,1)S(1)}, bf16[64,1280]{1,0:T(8,128)(2,1)S(1)}, bf16[64,1280]{1,0:T(8,128)(2,1)S(1)}, bf16[64,1280]{1,0:T(8,128)(2,1)S(1)}) custom-call(f32[2]{0:T(128)S(1)} %add_convert_fusion.4.flag_ref, f32[1,2560]{1,0:T(1,128)S(1)} %broadcast_in_dim.17.gate_ref, bf16[128,1408]{1,0:T(8,128)(2,1)S(1)} %get-tuple-element.28.refs_0_, ...), custom_call_target="tpu_custom_call" | custom-call | flops 167772160 | bytes 1966080 | tf_op jit(solution)/shard_map/pair_sums/pallas_call | solution.py:312
  16.3 0.6 %collective-permute-start.9 = (bf16[64,1280]{1,0:T(8,128)(2,1)S(1)}, bf16[64,1280]{1,0:T(8,128)(2,1)S(1)}, u32[]{:S(2)}, u32[]{:S(2)}) collective-permute-start(bf16[64,1280]{1,0:T(8,128)(2,1)S(1)} %get-tuple-element.40), channel_id=1, source_target_pairs={{0,8},{8,24},{24,16},{16,0},{1,9},{9,25},{25,17},{17,1},{2,10},{10... | collective-permute-start | bytes 491528 | tf_op jit(solution)/shard_map/ppermute | solution.py:434
  16.9 1.5 %collective-permute-start.10 = (bf16[64,1280]{1,0:T(8,128)(2,1)S(1)}, bf16[64,1280]{1,0:T(8,128)(2,1)S(1)}, u32[]{:S(2)}, u32[]{:S(2)}) collective-permute-start(bf16[64,1280]{1,0:T(8,128)(2,1)S(1)} %get-tuple-element.42), channel_id=1, source_target_pairs={{0,16},{16,24},{24,8},{8,0},{1,17},{17,25},{25,9},{9,1},{2,18},{18... | collective-permute-start | bytes 491528 | tf_op jit(solution)/shard_map/ppermute | solution.py:434
  18.9 3.0 %collective-permute-done.4.refs_1_ = bf16[32,5248]{1,0:T(8,128)(2,1)} collective-permute-done((bf16[32,5248]{1,0:T(8,128)(2,1)}, bf16[32,5248]{1,0:T(8,128)(2,1)}, u32[]{:S(2)}, u32[]{:S(2)}) %collective-permute-start.4) | collective-permute-done | bytes 335904 | tf_op jit(solution)/shard_map/ppermute | solution.py:32
  21.9 3.2 %attend_edges.1 = bf16[64,2560]{1,0:T(8,128)(2,1)S(1)} custom-call(bf16[128,2560]{1,0:T(8,128)(2,1)S(1)} %bitcast.29, bf16[128,2560]{1,0:T(8,128)(2,1)S(1)} %bitcast.32, bf16[128,2560]{1,0:T(8,128)(2,1)S(1)} %bitcast.35, f32[1,128]{1,0:T(1,128)S(1)} %get-tuple-element.35.code_ref, bf16[32,5248]{1,0:T(8,128)(2,1)} %collective-permute-done.3.refs_0_, ...), custom_call_target="tpu_custom_call" | custom-call | flops 268435456 | bytes 1966080 | tf_op jit(solution)/shard_map/attend_edges/pallas_call | solution.py:230
  25.2 0.6 %collective-permute-start.6 = (bf16[64,1280]{1,0:T(8,128)(2,1)S(1)}, bf16[64,1280]{1,0:T(8,128)(2,1)S(1)}, u32[]{:S(2)}, u32[]{:S(2)}) collective-permute-start(bf16[64,1280]{1,0:T(8,128)(2,1)S(1)} %get-tuple-element.60), channel_id=1, source_target_pairs={{0,16},{16,24},{24,8},{8,0},{1,17},{17,25},{25,9},{9,1},{2,18},{18... | collective-permute-start | bytes 491528 | tf_op jit(solution)/shard_map/ppermute | solution.py:434
  25.8 1.5 %collective-permute-start.5 = (bf16[64,1280]{1,0:T(8,128)(2,1)S(1)}, bf16[64,1280]{1,0:T(8,128)(2,1)S(1)}, u32[]{:S(2)}, u32[]{:S(2)}) collective-permute-start(bf16[64,1280]{1,0:T(8,128)(2,1)S(1)} %get-tuple-element.61), channel_id=1, source_target_pairs={{0,8},{8,24},{24,16},{16,0},{1,9},{9,25},{25,17},{17,1},{2,10},{10... | collective-permute-start | bytes 491528 | tf_op jit(solution)/shard_map/ppermute | solution.py:434
  27.5 0.6 %collective-permute-start.12 = (bf16[64,1280]{1,0:T(8,128)(2,1)S(1)}, bf16[64,1280]{1,0:T(8,128)(2,1)S(1)}, u32[]{:S(2)}, u32[]{:S(2)}) collective-permute-start(bf16[64,1280]{1,0:T(8,128)(2,1)S(1)} %get-tuple-element.48), channel_id=1, source_target_pairs={{0,8},{8,0},{16,24},{24,16},{1,9},{9,1},{17,25},{25,17},{2,10},{10... | collective-permute-start | bytes 491528 | tf_op jit(solution)/shard_map/ppermute | solution.py:434
  28.1 0.5 %collective-permute-start.11 = (bf16[64,1280]{1,0:T(8,128)(2,1)S(1)}, bf16[64,1280]{1,0:T(8,128)(2,1)S(1)}, u32[]{:S(2)}, u32[]{:S(2)}) collective-permute-start(bf16[64,1280]{1,0:T(8,128)(2,1)S(1)} %get-tuple-element.56), channel_id=1, source_target_pairs={{0,16},{16,0},{8,24},{24,8},{1,17},{17,1},{9,25},{25,9},{2,18},{18... | collective-permute-start | bytes 491528 | tf_op jit(solution)/shard_map/ppermute | solution.py:434
  28.6 3.7 %collective-permute-done.6 = bf16[64,1280]{1,0:T(8,128)(2,1)S(1)} collective-permute-done((bf16[64,1280]{1,0:T(8,128)(2,1)S(1)}, bf16[64,1280]{1,0:T(8,128)(2,1)S(1)}, u32[]{:S(2)}, u32[]{:S(2)}) %collective-permute-start.6) | collective-permute-done | bytes 163872 | tf_op jit(solution)/shard_map/ppermute | solution.py:434
  32.7 2.0 %collective-permute-start.8 = (bf16[64,1280]{1,0:T(8,128)(2,1)S(1)}, bf16[64,1280]{1,0:T(8,128)(2,1)S(1)}, u32[]{:S(2)}, u32[]{:S(2)}) collective-permute-start(bf16[64,1280]{1,0:T(8,128)(2,1)S(1)} %get-tuple-element.52), channel_id=1, source_target_pairs={{0,8},{8,0},{16,24},{24,16},{1,9},{9,1},{17,25},{25,17},{2,10},{10... | collective-permute-start | bytes 491528 | tf_op jit(solution)/shard_map/ppermute | solution.py:434
  34.9 0.8 %collective-permute-done.12 = bf16[64,1280]{1,0:T(8,128)(2,1)S(1)} collective-permute-done((bf16[64,1280]{1,0:T(8,128)(2,1)S(1)}, bf16[64,1280]{1,0:T(8,128)(2,1)S(1)}, u32[]{:S(2)}, u32[]{:S(2)}) %collective-permute-start.12) | collective-permute-done | bytes 163872 | tf_op jit(solution)/shard_map/ppermute | solution.py:434
  35.8 0.8 %relay.2 = (bf16[128,2560]{1,0:T(8,128)(2,1)}, f32[128,2560]{1,0:T(8,128)S(1)}) custom-call(f32[1,128]{1,0:T(1,128)S(1)} %get-tuple-element.77.row_ref, f32[1,2560]{1,0:T(1,128)S(1)} %broadcast_in_dim.17.gate_ref, bf16[64,1280]{1,0:T(8,128)(2,1)S(1)} %get-tuple-element.67.a_ref, bf16[64,1280]{1,0:T(8,128)(2,1)S(1)} %get-tuple-element.66.b_ref, ...), custom_call_target="tpu_custom_call" | custom-call | flops 83886080 | bytes 7864320 | tf_op jit(solution)/shard_map/relay/pallas_call | solution.py:392
  36.6 1.4 %collective-permute-done.8 = bf16[64,1280]{1,0:T(8,128)(2,1)S(1)} collective-permute-done((bf16[64,1280]{1,0:T(8,128)(2,1)S(1)}, bf16[64,1280]{1,0:T(8,128)(2,1)S(1)}, u32[]{:S(2)}, u32[]{:S(2)}) %collective-permute-start.8) | collective-permute-done | bytes 163872 | tf_op jit(solution)/shard_map/ppermute | solution.py:434
  38.0 1.9 %collective-permute-done.7 = bf16[64,1280]{1,0:T(8,128)(2,1)S(1)} collective-permute-done((bf16[64,1280]{1,0:T(8,128)(2,1)S(1)}, bf16[64,1280]{1,0:T(8,128)(2,1)S(1)}, u32[]{:S(2)}, u32[]{:S(2)}) %collective-permute-start.7) | collective-permute-done | bytes 163872 | tf_op jit(solution)/shard_map/ppermute | solution.py:434
  40.1 1.3 %relay.3 = (bf16[128,2560]{1,0:T(8,128)(2,1)}, bf16[128,2560]{1,0:T(8,128)(2,1)}) custom-call(f32[1,128]{1,0:T(1,128)S(1)} %get-tuple-element.77.row_ref, f32[1,2560]{1,0:T(1,128)S(1)} %broadcast_in_dim.17.gate_ref, bf16[64,1280]{1,0:T(8,128)(2,1)S(1)} %get-tuple-element.69.a_ref, ...), custom_call_target="tpu_custom_call", output_to_operand_aliasing={{0}: (7, {})} | custom-call | flops 83886080 | bytes 7864320 | tf_op jit(solution)/shard_map/relay/pallas_call | solution.py:392
  (32 shorter events, 1.8 us)
Async XLA Ops:
  0.6 13.3 %collective-permute-start = (f32[1280]{0:T(1024)}, f32[1280]{0:T(1024)S(1)}, u32[]{:S(2)}, u32[]{:S(2)}) collective-permute-start(f32[1280]{0:T(1024)} %param.12), channel_id=1, source_target_pairs={{0,1},{1,0},{2,3},{3,2},{4,5},{5,4},{6,7},{7,6},{8,9},{9,8},{10,11... | collective-permute-start | bytes 15368 | tf_op jit(solution)/shard_map/ppermute | solution.py:413
  1.4 4.4 %copy-start = (bf16[1,1,128,2560]{3,2,1,0:T(8,128)(2,1)S(1)}, bf16[1,1,128,2560]{3,2,1,0:T(8,128)(2,1)}, u32[]{:S(2)}) copy-start(bf16[1,1,128,2560]{3,2,1,0:T(8,128)(2,1)} %param.7) | copy-start | bytes 1966084
  1.4 4.4 %copy-start.1 = (bf16[1,1,128,2560]{3,2,1,0:T(8,128)(2,1)S(1)}, bf16[1,1,128,2560]{3,2,1,0:T(8,128)(2,1)}, u32[]{:S(2)}) copy-start(bf16[1,1,128,2560]{3,2,1,0:T(8,128)(2,1)} %param.8) | copy-start | bytes 1966084
  1.4 4.4 %copy-start.2 = (bf16[1,1,128,2560]{3,2,1,0:T(8,128)(2,1)S(1)}, bf16[1,1,128,2560]{3,2,1,0:T(8,128)(2,1)}, u32[]{:S(2)}) copy-start(bf16[1,1,128,2560]{3,2,1,0:T(8,128)(2,1)} %param.9) | copy-start | bytes 1966084
  2.7 11.3 %copy-start.3 = (f32[1280]{0:T(1024)S(1)}, f32[1280]{0:T(1024)}, u32[]{:S(2)}) copy-start(f32[1280]{0:T(1024)} %param.12) | copy-start | bytes 15364
  2.7 11.3 %collective-permute-start.1 = (bf16[128,1408]{1,0:T(8,128)(2,1)S(1)}, bf16[128,1408]{1,0:T(8,128)(2,1)S(1)}, u32[]{:S(2)}, u32[]{:S(2)}) collective-permute-start(bf16[128,1408]{1,0:T(8,128)(2,1)S(1)} %get-tuple-element.28.refs_0_), channel_id=1, source_target_pairs={{0,8},{8,0},{16,24},{24,16},{1,9},{9,1},{17,25},{25,17},{2,10},{10... | collective-permute-start | bytes 1081352 | tf_op jit(solution)/shard_map/ppermute | solution.py:434
  4.3 10.6 %collective-permute-start.2 = (bf16[128,1408]{1,0:T(8,128)(2,1)S(1)}, bf16[128,1408]{1,0:T(8,128)(2,1)}, u32[]{:S(2)}, u32[]{:S(2)}) collective-permute-start(bf16[128,1408]{1,0:T(8,128)(2,1)S(1)} %get-tuple-element.29.refs_2_), channel_id=1, source_target_pairs={{0,16},{16,0},{8,24},{24,8},{1,17},{17,1},{9,25},{25,9},{2,18},{18... | collective-permute-start | bytes 1081352 | tf_op jit(solution)/shard_map/ppermute | solution.py:434
  8.8 10.1 %collective-permute-start.3 = (bf16[32,5248]{1,0:T(8,128)(2,1)}, bf16[32,5248]{1,0:T(8,128)(2,1)}, u32[]{:S(2)}, u32[]{:S(2)}) collective-permute-start(bf16[32,5248]{1,0:T(8,128)(2,1)} %get-tuple-element.36), channel_id=1, source_target_pairs={{0,2},{2,0},{4,6},{6,4},{1,3},{3,1},{5,7},{7,5},{8,10},{10,8},{12,... | collective-permute-start | bytes 1007624 | tf_op jit(solution)/shard_map/ppermute | solution.py:32
  9.3 12.6 %collective-permute-start.4 = (bf16[32,5248]{1,0:T(8,128)(2,1)}, bf16[32,5248]{1,0:T(8,128)(2,1)}, u32[]{:S(2)}, u32[]{:S(2)}) collective-permute-start(bf16[32,5248]{1,0:T(8,128)(2,1)} %get-tuple-element.37), channel_id=1, source_target_pairs={{2,4},{4,2},{3,5},{5,3},{10,12},{12,10},{11,13},{13,11},{18,20},{2... | collective-permute-start | bytes 1007624 | tf_op jit(solution)/shard_map/ppermute | solution.py:32
  16.3 11.0 %collective-permute-start.9 = (bf16[64,1280]{1,0:T(8,128)(2,1)S(1)}, bf16[64,1280]{1,0:T(8,128)(2,1)S(1)}, u32[]{:S(2)}, u32[]{:S(2)}) collective-permute-start(bf16[64,1280]{1,0:T(8,128)(2,1)S(1)} %get-tuple-element.40), channel_id=1, source_target_pairs={{0,8},{8,24},{24,16},{16,0},{1,9},{9,25},{25,17},{17,1},{2,10},{10... | collective-permute-start | bytes 491528 | tf_op jit(solution)/shard_map/ppermute | solution.py:434
  16.9 10.4 %collective-permute-start.10 = (bf16[64,1280]{1,0:T(8,128)(2,1)S(1)}, bf16[64,1280]{1,0:T(8,128)(2,1)S(1)}, u32[]{:S(2)}, u32[]{:S(2)}) collective-permute-start(bf16[64,1280]{1,0:T(8,128)(2,1)S(1)} %get-tuple-element.42), channel_id=1, source_target_pairs={{0,16},{16,24},{24,8},{8,0},{1,17},{17,25},{25,9},{9,1},{2,18},{18... | collective-permute-start | bytes 491528 | tf_op jit(solution)/shard_map/ppermute | solution.py:434
  25.2 7.1 %collective-permute-start.6 = (bf16[64,1280]{1,0:T(8,128)(2,1)S(1)}, bf16[64,1280]{1,0:T(8,128)(2,1)S(1)}, u32[]{:S(2)}, u32[]{:S(2)}) collective-permute-start(bf16[64,1280]{1,0:T(8,128)(2,1)S(1)} %get-tuple-element.60), channel_id=1, source_target_pairs={{0,16},{16,24},{24,8},{8,0},{1,17},{17,25},{25,9},{9,1},{2,18},{18... | collective-permute-start | bytes 491528 | tf_op jit(solution)/shard_map/ppermute | solution.py:434
  25.8 6.7 %collective-permute-start.5 = (bf16[64,1280]{1,0:T(8,128)(2,1)S(1)}, bf16[64,1280]{1,0:T(8,128)(2,1)S(1)}, u32[]{:S(2)}, u32[]{:S(2)}) collective-permute-start(bf16[64,1280]{1,0:T(8,128)(2,1)S(1)} %get-tuple-element.61), channel_id=1, source_target_pairs={{0,8},{8,24},{24,16},{16,0},{1,9},{9,25},{25,17},{17,1},{2,10},{10... | collective-permute-start | bytes 491528 | tf_op jit(solution)/shard_map/ppermute | solution.py:434
  27.5 8.2 %collective-permute-start.12 = (bf16[64,1280]{1,0:T(8,128)(2,1)S(1)}, bf16[64,1280]{1,0:T(8,128)(2,1)S(1)}, u32[]{:S(2)}, u32[]{:S(2)}) collective-permute-start(bf16[64,1280]{1,0:T(8,128)(2,1)S(1)} %get-tuple-element.48), channel_id=1, source_target_pairs={{0,8},{8,0},{16,24},{24,16},{1,9},{9,1},{17,25},{25,17},{2,10},{10... | collective-permute-start | bytes 491528 | tf_op jit(solution)/shard_map/ppermute | solution.py:434
  28.1 7.6 %collective-permute-start.11 = (bf16[64,1280]{1,0:T(8,128)(2,1)S(1)}, bf16[64,1280]{1,0:T(8,128)(2,1)S(1)}, u32[]{:S(2)}, u32[]{:S(2)}) collective-permute-start(bf16[64,1280]{1,0:T(8,128)(2,1)S(1)} %get-tuple-element.56), channel_id=1, source_target_pairs={{0,16},{16,0},{8,24},{24,8},{1,17},{17,1},{9,25},{25,9},{2,18},{18... | collective-permute-start | bytes 491528 | tf_op jit(solution)/shard_map/ppermute | solution.py:434
  32.7 5.4 %collective-permute-start.8 = (bf16[64,1280]{1,0:T(8,128)(2,1)S(1)}, bf16[64,1280]{1,0:T(8,128)(2,1)S(1)}, u32[]{:S(2)}, u32[]{:S(2)}) collective-permute-start(bf16[64,1280]{1,0:T(8,128)(2,1)S(1)} %get-tuple-element.52), channel_id=1, source_target_pairs={{0,8},{8,0},{16,24},{24,16},{1,9},{9,1},{17,25},{25,17},{2,10},{10... | collective-permute-start | bytes 491528 | tf_op jit(solution)/shard_map/ppermute | solution.py:434
  34.7 5.3 %collective-permute-start.7 = (bf16[64,1280]{1,0:T(8,128)(2,1)S(1)}, bf16[64,1280]{1,0:T(8,128)(2,1)S(1)}, u32[]{:S(2)}, u32[]{:S(2)}) collective-permute-start(bf16[64,1280]{1,0:T(8,128)(2,1)S(1)} %get-tuple-element.58), channel_id=1, source_target_pairs={{0,16},{16,0},{8,24},{24,8},{1,17},{17,1},{9,25},{25,9},{2,18},{18... | collective-permute-start | bytes 491528 | tf_op jit(solution)/shard_map/ppermute | solution.py:434

commit v9 on v8

--- a/solution.py
+++ b/solution.py
@@ -13,7 +13,7 @@
 FRAMES = 20
 LANES = 128
 VMEM_LIMIT = 32 * 1024 * 1024
-PACK_LIMIT = 53 * 1024 * 1024
+PACK_LIMIT = 52 * 1024 * 1024
 
 
 def shifted(block, axis, distance):

time: 41.6 us -> 41.6 us (level)
  local copies, waits for them, and re-layouts: 0.06 us -> 1.14 us
  Pallas kernels: 10.9 us -> 9.86 us
  waiting for transfers between devices: 12.3 us -> 11.8 us
    unnamed x8 -> x10, local copies, waits for them, and re-layouts: 0.03 us -> 1.1 us
    pallas_call x1, Pallas kernels: 1.23 us -> 0.17 us  [pack_grads(): pl.pallas_call(pack_grads_kernel, in_specs=[far, VMEM] + [far] * len(othe...]
    ppermute x10, starting transfers between devices: 10.6 us -> 11.1 us  [local(): send = lambda block, route: lax.ppermute(block, 'grp', route)]
    ppermute x10, waiting for transfers between devices: 8.84 us -> 8.33 us  [local(): send = lambda block, route: lax.ppermute(block, 'grp', route)]
  transfers between devices with their start and end apart: 13 -> 13, of which waited for: 8 -> 8; matrix products, arithmetic and copies ran while one was open for 4% -> 4% of each run, Pallas kernels for 23% -> 21%
where the time goes in v9:
time: 41.6 us; the launch traced here: 41.3 us
  starting transfers between devices  16.2 us (39%)
  waiting for transfers between devices  11.8 us (28%)
  Pallas kernels  9.86 us (24%)
  other arithmetic  1.51 us (4%)
  local copies, waits for them, and re-layouts  1.14 us (3%)
  between operations  0.82 us (2%)
    ppermute x10, starting transfers between devices, local(): send = lambda block, route: lax.ppermute(block, 'grp', route)  11.1 us
    ppermute x10, waiting for transfers between devices, local(): send = lambda block, route: lax.ppermute(block, 'grp', route)  8.33 us
    ppermute x2, starting transfers between devices, paired(): return lax.ppermute(block, axis, route)  5.04 us
    ppermute x2, waiting for transfers between devices, paired(): return lax.ppermute(block, axis, route)  3.44 us
    pallas_call x1, Pallas kernels, attend_edges(): pl.pallas_call(functools.partial(edge_kernel, reach), in_specs=[VMEM] * (...  3.23 us
    pallas_call x1, Pallas kernels, attend_middle(): pl.pallas_call(functools.partial(middle_kernel, reach), in_specs=[SMEM] +...  2.95 us
    pallas_call x2, Pallas kernels, relay(): pl.pallas_call(kernel, in_specs=[VMEM] * 7 + ([] if grads is None else [f...  2.11 us
    pallas_call x1, Pallas kernels, pair_sums(): pl.pallas_call(functools.partial(sums_kernel, sizes), in_specs=[SMEM] + [...  1.4 us
  transfers between devices with their start and end apart: 13, of which 8 were waited for; matrix products, arithmetic and copies ran while one was open for 4% of the time, Pallas kernels for 21%

profile of v9, /device:TPU:8, one launch (start us, length us, event | category | flops | bytes accessed | tf_op | source)
XLA Modules:
  0.0 41.3 jit_solution(5510142192412451227)
XLA Ops:
  0.7 0.7 %and_select_fusion = (s32[1,128]{1,0:T(1,128)S(1)}, s32[1,128]{1,0:T(1,128)S(1)}) fusion(s32[1,1,128]{2,1,0:T(1,128)} %param.11, s32[1,1,128]{2,1,0:T(1,128)} %param.10), kind=kLoop, calls=%fused_computation.32 | loop fusion | flops 2816 | bytes 2048 | tf_op jit(solution)/shard_map/jit(remainder)/select_n | solution.py:438
  1.4 1.1 %copy-done.3 = bf16[1,1,128,2560]{3,2,1,0:T(8,128)(2,1)S(1)} copy-done((bf16[1,1,128,2560]{3,2,1,0:T(8,128)(2,1)S(1)}, bf16[1,1,128,2560]{3,2,1,0:T(8,128)(2,1)}, u32[]{:S(2)}) %copy-start.3) | copy-done | bytes 655384
  2.7 1.6 %collective-permute-start.1 = (bf16[128,1408]{1,0:T(8,128)(2,1)S(1)}, bf16[128,1408]{1,0:T(8,128)(2,1)S(1)}, u32[]{:S(2)}, u32[]{:S(2)}) collective-permute-start(bf16[128,1408]{1,0:T(8,128)(2,1)S(1)} %get-tuple-element.28.refs_0_), channel_id=1, source_target_pairs={{0,8},{8,0},{16,24},{24,16},{1,9},{9,1},{17,25},{25,17},{2,10},{10... | collective-permute-start | bytes 1081352 | tf_op jit(solution)/shard_map/ppermute | solution.py:434
  4.3 1.5 %collective-permute-start.2 = (bf16[128,1408]{1,0:T(8,128)(2,1)S(1)}, bf16[128,1408]{1,0:T(8,128)(2,1)}, u32[]{:S(2)}, u32[]{:S(2)}) collective-permute-start(bf16[128,1408]{1,0:T(8,128)(2,1)S(1)} %get-tuple-element.29.refs_2_), channel_id=1, source_target_pairs={{0,16},{16,0},{8,24},{24,8},{1,17},{17,1},{9,25},{25,9},{2,18},{18... | collective-permute-start | bytes 1081352 | tf_op jit(solution)/shard_map/ppermute | solution.py:434
  5.9 3.0 %attend_middle.1 = (bf16[32,5248]{1,0:T(8,128)(2,1)}, bf16[32,5248]{1,0:T(8,128)(2,1)}, bf16[64,2560]{1,0:T(8,128)(2,1)S(1)}) custom-call(s32[2]{0:T(128)S(1)} %add_select_fusion.first_ref, bf16[128,2560]{1,0:T(8,128)(2,1)S(1)} %bitcast.28, bf16[128,2560]{1,0:T(8,128)(2,1)S(1)} %bitcast.31, bf16[128,2560]{1,0:T(8,128)(2,1)S(1)} %bitcast.34, ...), custom_call_target="tpu_custom_call" | custom-call | flops 536870912 | bytes 3932160 | tf_op jit(solution)/shard_map/attend_middle/pallas_call | solution.py:215
  9.2 4.6 %collective-permute-start.4 = (bf16[32,5248]{1,0:T(8,128)(2,1)}, bf16[32,5248]{1,0:T(8,128)(2,1)}, u32[]{:S(2)}, u32[]{:S(2)}) collective-permute-start(bf16[32,5248]{1,0:T(8,128)(2,1)} %get-tuple-element.37), channel_id=1, source_target_pairs={{2,4},{4,2},{3,5},{5,3},{10,12},{12,10},{11,13},{13,11},{18,20},{2... | collective-permute-start | bytes 1007624 | tf_op jit(solution)/shard_map/ppermute | solution.py:32
  14.0 0.9 %collective-permute-done.2.refs_3_ = bf16[128,1408]{1,0:T(8,128)(2,1)} collective-permute-done((bf16[128,1408]{1,0:T(8,128)(2,1)S(1)}, bf16[128,1408]{1,0:T(8,128)(2,1)}, u32[]{:S(2)}, u32[]{:S(2)}) %collective-permute-start.2) | collective-permute-done | bytes 360480 | tf_op jit(solution)/shard_map/ppermute | solution.py:434
  14.9 1.4 %pair_sums.1 = (bf16[64,1280]{1,0:T(8,128)(2,1)S(1)}, bf16[64,1280]{1,0:T(8,128)(2,1)S(1)}, bf16[64,1280]{1,0:T(8,128)(2,1)S(1)}, bf16[64,1280]{1,0:T(8,128)(2,1)S(1)}) custom-call(f32[2]{0:T(128)S(1)} %add_convert_fusion.4.flag_ref, f32[1,2560]{1,0:T(1,128)S(1)} %broadcast_in_dim.17.gate_ref, bf16[128,1408]{1,0:T(8,128)(2,1)S(1)} %get-tuple-element.28.refs_0_, ...), custom_call_target="tpu_custom_call" | custom-call | flops 167772160 | bytes 1966080 | tf_op jit(solution)/shard_map/pair_sums/pallas_call | solution.py:312
  16.4 0.6 %collective-permute-start.9 = (bf16[64,1280]{1,0:T(8,128)(2,1)S(1)}, bf16[64,1280]{1,0:T(8,128)(2,1)S(1)}, u32[]{:S(2)}, u32[]{:S(2)}) collective-permute-start(bf16[64,1280]{1,0:T(8,128)(2,1)S(1)} %get-tuple-element.40), channel_id=1, source_target_pairs={{0,8},{8,24},{24,16},{16,0},{1,9},{9,25},{25,17},{17,1},{2,10},{10... | collective-permute-start | bytes 491528 | tf_op jit(solution)/shard_map/ppermute | solution.py:434
  16.9 1.5 %collective-permute-start.10 = (bf16[64,1280]{1,0:T(8,128)(2,1)S(1)}, bf16[64,1280]{1,0:T(8,128)(2,1)S(1)}, u32[]{:S(2)}, u32[]{:S(2)}) collective-permute-start(bf16[64,1280]{1,0:T(8,128)(2,1)S(1)} %get-tuple-element.42), channel_id=1, source_target_pairs={{0,16},{16,24},{24,8},{8,0},{1,17},{17,25},{25,9},{9,1},{2,18},{18... | collective-permute-start | bytes 491528 | tf_op jit(solution)/shard_map/ppermute | solution.py:434
  18.4 0.4 %collective-permute-done.3.refs_0_ = bf16[32,5248]{1,0:T(8,128)(2,1)} collective-permute-done((bf16[32,5248]{1,0:T(8,128)(2,1)}, bf16[32,5248]{1,0:T(8,128)(2,1)}, u32[]{:S(2)}, u32[]{:S(2)}) %collective-permute-start.3) | collective-permute-done | bytes 335904 | tf_op jit(solution)/shard_map/ppermute | solution.py:32
  18.9 3.0 %collective-permute-done.4.refs_1_ = bf16[32,5248]{1,0:T(8,128)(2,1)} collective-permute-done((bf16[32,5248]{1,0:T(8,128)(2,1)}, bf16[32,5248]{1,0:T(8,128)(2,1)}, u32[]{:S(2)}, u32[]{:S(2)}) %collective-permute-start.4) | collective-permute-done | bytes 335904 | tf_op jit(solution)/shard_map/ppermute | solution.py:32
  21.9 3.2 %attend_edges.1 = bf16[64,2560]{1,0:T(8,128)(2,1)S(1)} custom-call(bf16[128,2560]{1,0:T(8,128)(2,1)S(1)} %bitcast.29, bf16[128,2560]{1,0:T(8,128)(2,1)S(1)} %bitcast.32, bf16[128,2560]{1,0:T(8,128)(2,1)S(1)} %bitcast.35, f32[1,128]{1,0:T(1,128)S(1)} %get-tuple-element.35.code_ref, bf16[32,5248]{1,0:T(8,128)(2,1)} %collective-permute-done.3.refs_0_, ...), custom_call_target="tpu_custom_call" | custom-call | flops 268435456 | bytes 1966080 | tf_op jit(solution)/shard_map/attend_edges/pallas_call | solution.py:230
  25.2 0.5 %collective-permute-start.6 = (bf16[64,1280]{1,0:T(8,128)(2,1)S(1)}, bf16[64,1280]{1,0:T(8,128)(2,1)S(1)}, u32[]{:S(2)}, u32[]{:S(2)}) collective-permute-start(bf16[64,1280]{1,0:T(8,128)(2,1)S(1)} %get-tuple-element.60), channel_id=1, source_target_pairs={{0,16},{16,24},{24,8},{8,0},{1,17},{17,25},{25,9},{9,1},{2,18},{18... | collective-permute-start | bytes 491528 | tf_op jit(solution)/shard_map/ppermute | solution.py:434
  25.7 1.5 %collective-permute-start.5 = (bf16[64,1280]{1,0:T(8,128)(2,1)S(1)}, bf16[64,1280]{1,0:T(8,128)(2,1)S(1)}, u32[]{:S(2)}, u32[]{:S(2)}) collective-permute-start(bf16[64,1280]{1,0:T(8,128)(2,1)S(1)} %get-tuple-element.61), channel_id=1, source_target_pairs={{0,8},{8,24},{24,16},{16,0},{1,9},{9,25},{25,17},{17,1},{2,10},{10... | collective-permute-start | bytes 491528 | tf_op jit(solution)/shard_map/ppermute | solution.py:434
  27.5 0.6 %collective-permute-start.12 = (bf16[64,1280]{1,0:T(8,128)(2,1)S(1)}, bf16[64,1280]{1,0:T(8,128)(2,1)S(1)}, u32[]{:S(2)}, u32[]{:S(2)}) collective-permute-start(bf16[64,1280]{1,0:T(8,128)(2,1)S(1)} %get-tuple-element.48), channel_id=1, source_target_pairs={{0,8},{8,0},{16,24},{24,16},{1,9},{9,1},{17,25},{25,17},{2,10},{10... | collective-permute-start | bytes 491528 | tf_op jit(solution)/shard_map/ppermute | solution.py:434
  28.1 1.2 %collective-permute-start.11 = (bf16[64,1280]{1,0:T(8,128)(2,1)S(1)}, bf16[64,1280]{1,0:T(8,128)(2,1)S(1)}, u32[]{:S(2)}, u32[]{:S(2)}) collective-permute-start(bf16[64,1280]{1,0:T(8,128)(2,1)S(1)} %get-tuple-element.56), channel_id=1, source_target_pairs={{0,16},{16,0},{8,24},{24,8},{1,17},{17,1},{9,25},{25,9},{2,18},{18... | collective-permute-start | bytes 491528 | tf_op jit(solution)/shard_map/ppermute | solution.py:434
  29.3 3.0 %collective-permute-done.6 = bf16[64,1280]{1,0:T(8,128)(2,1)S(1)} collective-permute-done((bf16[64,1280]{1,0:T(8,128)(2,1)S(1)}, bf16[64,1280]{1,0:T(8,128)(2,1)S(1)}, u32[]{:S(2)}, u32[]{:S(2)}) %collective-permute-start.6) | collective-permute-done | bytes 163872 | tf_op jit(solution)/shard_map/ppermute | solution.py:434
  32.8 1.9 %collective-permute-start.8 = (bf16[64,1280]{1,0:T(8,128)(2,1)S(1)}, bf16[64,1280]{1,0:T(8,128)(2,1)S(1)}, u32[]{:S(2)}, u32[]{:S(2)}) collective-permute-start(bf16[64,1280]{1,0:T(8,128)(2,1)S(1)} %get-tuple-element.52), channel_id=1, source_target_pairs={{0,8},{8,0},{16,24},{24,16},{1,9},{9,1},{17,25},{25,17},{2,10},{10... | collective-permute-start | bytes 491528 | tf_op jit(solution)/shard_map/ppermute | solution.py:434
  34.9 0.8 %collective-permute-done.12 = bf16[64,1280]{1,0:T(8,128)(2,1)S(1)} collective-permute-done((bf16[64,1280]{1,0:T(8,128)(2,1)S(1)}, bf16[64,1280]{1,0:T(8,128)(2,1)S(1)}, u32[]{:S(2)}, u32[]{:S(2)}) %collective-permute-start.12) | collective-permute-done | bytes 163872 | tf_op jit(solution)/shard_map/ppermute | solution.py:434
  35.8 0.8 %relay.2 = (bf16[128,2560]{1,0:T(8,128)(2,1)}, f32[128,2560]{1,0:T(8,128)S(1)}) custom-call(f32[1,128]{1,0:T(1,128)S(1)} %get-tuple-element.77.row_ref, f32[1,2560]{1,0:T(1,128)S(1)} %broadcast_in_dim.17.gate_ref, bf16[64,1280]{1,0:T(8,128)(2,1)S(1)} %get-tuple-element.67.a_ref, bf16[64,1280]{1,0:T(8,128)(2,1)S(1)} %get-tuple-element.66.b_ref, ...), custom_call_target="tpu_custom_call" | custom-call | flops 83886080 | bytes 7864320 | tf_op jit(solution)/shard_map/relay/pallas_call | solution.py:392
  36.6 1.6 %collective-permute-done.8 = bf16[64,1280]{1,0:T(8,128)(2,1)S(1)} collective-permute-done((bf16[64,1280]{1,0:T(8,128)(2,1)S(1)}, bf16[64,1280]{1,0:T(8,128)(2,1)S(1)}, u32[]{:S(2)}, u32[]{:S(2)}) %collective-permute-start.8) | collective-permute-done | bytes 163872 | tf_op jit(solution)/shard_map/ppermute | solution.py:434
  38.2 1.8 %collective-permute-done.7 = bf16[64,1280]{1,0:T(8,128)(2,1)S(1)} collective-permute-done((bf16[64,1280]{1,0:T(8,128)(2,1)S(1)}, bf16[64,1280]{1,0:T(8,128)(2,1)S(1)}, u32[]{:S(2)}, u32[]{:S(2)}) %collective-permute-start.7) | collective-permute-done | bytes 163872 | tf_op jit(solution)/shard_map/ppermute | solution.py:434
  40.1 1.3 %relay.3 = (bf16[128,2560]{1,0:T(8,128)(2,1)}, bf16[128,2560]{1,0:T(8,128)(2,1)}) custom-call(f32[1,128]{1,0:T(1,128)S(1)} %get-tuple-element.77.row_ref, f32[1,2560]{1,0:T(1,128)S(1)} %broadcast_in_dim.17.gate_ref, bf16[64,1280]{1,0:T(8,128)(2,1)S(1)} %get-tuple-element.69.a_ref, ...), custom_call_target="tpu_custom_call", output_to_operand_aliasing={{0}: (7, {})} | custom-call | flops 83886080 | bytes 7864320 | tf_op jit(solution)/shard_map/relay/pallas_call | solution.py:392
  (34 shorter events, 2.1 us)
Async XLA Ops:
  0.6 13.3 %collective-permute-start = (f32[1280]{0:T(1024)}, f32[1280]{0:T(1024)S(1)}, u32[]{:S(2)}, u32[]{:S(2)}) collective-permute-start(f32[1280]{0:T(1024)} %param.12), channel_id=1, source_target_pairs={{0,1},{1,0},{2,3},{3,2},{4,5},{5,4},{6,7},{7,6},{8,9},{9,8},{10,11... | collective-permute-start | bytes 15368 | tf_op jit(solution)/shard_map/ppermute | solution.py:413
  1.4 1.1 %copy-start.3 = (bf16[1,1,128,2560]{3,2,1,0:T(8,128)(2,1)S(1)}, bf16[1,1,128,2560]{3,2,1,0:T(8,128)(2,1)}, u32[]{:S(2)}) copy-start(bf16[1,1,128,2560]{3,2,1,0:T(8,128)(2,1)} %param.13) | copy-start | bytes 1966084
  2.5 3.3 %copy-start = (bf16[1,1,128,2560]{3,2,1,0:T(8,128)(2,1)S(1)}, bf16[1,1,128,2560]{3,2,1,0:T(8,128)(2,1)}, u32[]{:S(2)}) copy-start(bf16[1,1,128,2560]{3,2,1,0:T(8,128)(2,1)} %param.7) | copy-start | bytes 1966084
  2.5 3.3 %copy-start.1 = (bf16[1,1,128,2560]{3,2,1,0:T(8,128)(2,1)S(1)}, bf16[1,1,128,2560]{3,2,1,0:T(8,128)(2,1)}, u32[]{:S(2)}) copy-start(bf16[1,1,128,2560]{3,2,1,0:T(8,128)(2,1)} %param.8) | copy-start | bytes 1966084
  2.5 3.3 %copy-start.2 = (bf16[1,1,128,2560]{3,2,1,0:T(8,128)(2,1)S(1)}, bf16[1,1,128,2560]{3,2,1,0:T(8,128)(2,1)}, u32[]{:S(2)}) copy-start(bf16[1,1,128,2560]{3,2,1,0:T(8,128)(2,1)} %param.9) | copy-start | bytes 1966084
  2.7 11.3 %copy-start.4 = (f32[1280]{0:T(1024)S(1)}, f32[1280]{0:T(1024)}, u32[]{:S(2)}) copy-start(f32[1280]{0:T(1024)} %param.12) | copy-start | bytes 15364
  2.7 11.3 %collective-permute-start.1 = (bf16[128,1408]{1,0:T(8,128)(2,1)S(1)}, bf16[128,1408]{1,0:T(8,128)(2,1)S(1)}, u32[]{:S(2)}, u32[]{:S(2)}) collective-permute-start(bf16[128,1408]{1,0:T(8,128)(2,1)S(1)} %get-tuple-element.28.refs_0_), channel_id=1, source_target_pairs={{0,8},{8,0},{16,24},{24,16},{1,9},{9,1},{17,25},{25,17},{2,10},{10... | collective-permute-start | bytes 1081352 | tf_op jit(solution)/shard_map/ppermute | solution.py:434
  4.3 10.6 %collective-permute-start.2 = (bf16[128,1408]{1,0:T(8,128)(2,1)S(1)}, bf16[128,1408]{1,0:T(8,128)(2,1)}, u32[]{:S(2)}, u32[]{:S(2)}) collective-permute-start(bf16[128,1408]{1,0:T(8,128)(2,1)S(1)} %get-tuple-element.29.refs_2_), channel_id=1, source_target_pairs={{0,16},{16,0},{8,24},{24,8},{1,17},{17,1},{9,25},{25,9},{2,18},{18... | collective-permute-start | bytes 1081352 | tf_op jit(solution)/shard_map/ppermute | solution.py:434
  8.8 10.0 %collective-permute-start.3 = (bf16[32,5248]{1,0:T(8,128)(2,1)}, bf16[32,5248]{1,0:T(8,128)(2,1)}, u32[]{:S(2)}, u32[]{:S(2)}) collective-permute-start(bf16[32,5248]{1,0:T(8,128)(2,1)} %get-tuple-element.36), channel_id=1, source_target_pairs={{0,2},{2,0},{4,6},{6,4},{1,3},{3,1},{5,7},{7,5},{8,10},{10,8},{12,... | collective-permute-start | bytes 1007624 | tf_op jit(solution)/shard_map/ppermute | solution.py:32
  9.2 12.6 %collective-permute-start.4 = (bf16[32,5248]{1,0:T(8,128)(2,1)}, bf16[32,5248]{1,0:T(8,128)(2,1)}, u32[]{:S(2)}, u32[]{:S(2)}) collective-permute-start(bf16[32,5248]{1,0:T(8,128)(2,1)} %get-tuple-element.37), channel_id=1, source_target_pairs={{2,4},{4,2},{3,5},{5,3},{10,12},{12,10},{11,13},{13,11},{18,20},{2... | collective-permute-start | bytes 1007624 | tf_op jit(solution)/shard_map/ppermute | solution.py:32
  16.4 11.0 %collective-permute-start.9 = (bf16[64,1280]{1,0:T(8,128)(2,1)S(1)}, bf16[64,1280]{1,0:T(8,128)(2,1)S(1)}, u32[]{:S(2)}, u32[]{:S(2)}) collective-permute-start(bf16[64,1280]{1,0:T(8,128)(2,1)S(1)} %get-tuple-element.40), channel_id=1, source_target_pairs={{0,8},{8,24},{24,16},{16,0},{1,9},{9,25},{25,17},{17,1},{2,10},{10... | collective-permute-start | bytes 491528 | tf_op jit(solution)/shard_map/ppermute | solution.py:434
  16.9 10.4 %collective-permute-start.10 = (bf16[64,1280]{1,0:T(8,128)(2,1)S(1)}, bf16[64,1280]{1,0:T(8,128)(2,1)S(1)}, u32[]{:S(2)}, u32[]{:S(2)}) collective-permute-start(bf16[64,1280]{1,0:T(8,128)(2,1)S(1)} %get-tuple-element.42), channel_id=1, source_target_pairs={{0,16},{16,24},{24,8},{8,0},{1,17},{17,25},{25,9},{9,1},{2,18},{18... | collective-permute-start | bytes 491528 | tf_op jit(solution)/shard_map/ppermute | solution.py:434
  25.2 7.1 %collective-permute-start.6 = (bf16[64,1280]{1,0:T(8,128)(2,1)S(1)}, bf16[64,1280]{1,0:T(8,128)(2,1)S(1)}, u32[]{:S(2)}, u32[]{:S(2)}) collective-permute-start(bf16[64,1280]{1,0:T(8,128)(2,1)S(1)} %get-tuple-element.60), channel_id=1, source_target_pairs={{0,16},{16,24},{24,8},{8,0},{1,17},{17,25},{25,9},{9,1},{2,18},{18... | collective-permute-start | bytes 491528 | tf_op jit(solution)/shard_map/ppermute | solution.py:434
  25.7 6.9 %collective-permute-start.5 = (bf16[64,1280]{1,0:T(8,128)(2,1)S(1)}, bf16[64,1280]{1,0:T(8,128)(2,1)S(1)}, u32[]{:S(2)}, u32[]{:S(2)}) collective-permute-start(bf16[64,1280]{1,0:T(8,128)(2,1)S(1)} %get-tuple-element.61), channel_id=1, source_target_pairs={{0,8},{8,24},{24,16},{16,0},{1,9},{9,25},{25,17},{17,1},{2,10},{10... | collective-permute-start | bytes 491528 | tf_op jit(solution)/shard_map/ppermute | solution.py:434
  27.5 8.2 %collective-permute-start.12 = (bf16[64,1280]{1,0:T(8,128)(2,1)S(1)}, bf16[64,1280]{1,0:T(8,128)(2,1)S(1)}, u32[]{:S(2)}, u32[]{:S(2)}) collective-permute-start(bf16[64,1280]{1,0:T(8,128)(2,1)S(1)} %get-tuple-element.48), channel_id=1, source_target_pairs={{0,8},{8,0},{16,24},{24,16},{1,9},{9,1},{17,25},{25,17},{2,10},{10... | collective-permute-start | bytes 491528 | tf_op jit(solution)/shard_map/ppermute | solution.py:434
  28.1 7.6 %collective-permute-start.11 = (bf16[64,1280]{1,0:T(8,128)(2,1)S(1)}, bf16[64,1280]{1,0:T(8,128)(2,1)S(1)}, u32[]{:S(2)}, u32[]{:S(2)}) collective-permute-start(bf16[64,1280]{1,0:T(8,128)(2,1)S(1)} %get-tuple-element.56), channel_id=1, source_target_pairs={{0,16},{16,0},{8,24},{24,8},{1,17},{17,1},{9,25},{25,9},{2,18},{18... | collective-permute-start | bytes 491528 | tf_op jit(solution)/shard_map/ppermute | solution.py:434
  32.8 5.4 %collective-permute-start.8 = (bf16[64,1280]{1,0:T(8,128)(2,1)S(1)}, bf16[64,1280]{1,0:T(8,128)(2,1)S(1)}, u32[]{:S(2)}, u32[]{:S(2)}) collective-permute-start(bf16[64,1280]{1,0:T(8,128)(2,1)S(1)} %get-tuple-element.52), channel_id=1, source_target_pairs={{0,8},{8,0},{16,24},{24,16},{1,9},{9,1},{17,25},{25,17},{2,10},{10... | collective-permute-start | bytes 491528 | tf_op jit(solution)/shard_map/ppermute | solution.py:434
  34.7 5.3 %collective-permute-start.7 = (bf16[64,1280]{1,0:T(8,128)(2,1)S(1)}, bf16[64,1280]{1,0:T(8,128)(2,1)S(1)}, u32[]{:S(2)}, u32[]{:S(2)}) collective-permute-start(bf16[64,1280]{1,0:T(8,128)(2,1)S(1)} %get-tuple-element.58), channel_id=1, source_target_pairs={{0,16},{16,0},{8,24},{24,8},{1,17},{17,1},{9,25},{25,9},{2,18},{18... | collective-permute-start | bytes 491528 | tf_op jit(solution)/shard_map/ppermute | solution.py:434

commit v10 on v8

--- a/solution.py
+++ b/solution.py
@@ -57,12 +57,9 @@
     return masks
 
 
-def mixed_period(base, query, sets, masks, period):
-    rows = sets[0][0].shape[0]
-    factor = math.log2(math.e) / math.sqrt(DH)
-    windows = lane_windows(period // DH)
+def period_scores(base, query, keys, masks, period):
     scores = []
-    for start, members in windows:
+    for start, members in lane_windows(period // DH):
         lanes = slice(base + start, base + start + 2 * LANES)
         part = query(lanes)
         stacked = jnp.concatenate([part * masks[h] for h in members], axis=0)
@@ -71,14 +68,21 @@
                 lax.dot_general(
                     stacked, key(lanes), (((1,), (1,)), ((), ())), preferred_element_type=jnp.float32
                 )
-                for bias, key, value in sets
+                for key in keys
             ]
         )
+    return scores
+
+
+def mixed_period(base, scores, sets, period):
+    rows = sets[0][0].shape[0]
+    factor = math.log2(math.e) / math.sqrt(DH)
+    windows = lane_windows(period // DH)
     weights = []
     for parts, (start, members) in zip(scores, windows):
         parts = [
             part.reshape(len(members), rows, -1) + bias[None]
-            for part, (bias, key, value) in zip(parts, sets)
+            for part, (bias, value) in zip(parts, sets)
         ]
         largest = row_max(parts)
         weights.append(
@@ -92,7 +96,7 @@
         lanes = slice(base + start, base + start + 2 * LANES)
         mixed = sum(
             jnp.dot(part, value(lanes), preferred_element_type=jnp.float32)
-            for part, (bias, key, value) in zip(parts, sets)
+            for part, (bias, value) in zip(parts, sets)
         )
         totals = sum(
             jnp.dot(part, jnp.ones((part.shape[1], LANES), part.dtype), preferred_element_type=jnp.float32)
@@ -128,18 +132,14 @@
     return jnp.where(jnp.abs(mine[:, :1] - theirs.T[: mine.shape[0]]) <= 1.5, 0.0, -1e30)
 
 
-def attend_block(query, sets, out_ref):
-    rows, width = out_ref.shape
-    period = math.lcm(DH, LANES)
-    masks = head_masks(rows, period)
-    for base in range(0, width, period):
-        tiles = mixed_period(base, query, sets, masks, period)
-        for low, tile in tiles.items():
-            out_ref[:, base + low : base + low + LANES] = tile
-
-
-def pack_ends(first_ref, k_ref, v_ref, code, end_refs):
+def store_period(base, tiles, out_ref):
+    for low, tile in tiles.items():
+        out_ref[:, base + low : base + low + LANES] = tile
+
+
+def ends_kernel(first_ref, k_ref, v_ref, code_ref, *end_refs):
     tokens, width = k_ref.shape
+    code = columns(code_ref[...])
     for n, ref in enumerate(end_refs):
         most = ref.shape[0]
         first = pl.multiple_of(first_ref[n], most)
@@ -149,34 +149,40 @@
         ref[:, 2 * width :] = here.astype(jnp.bfloat16)
 
 
-def middle_kernel(reach, first_ref, q_ref, k_ref, v_ref, code_ref, one_ref, two_ref, out_ref=None):
+def middle_kernel(reach, q_ref, k_ref, v_ref, code_ref, out_ref):
+    rows = out_ref.shape[0]
     code = columns(code_ref[...])
-    pack_ends(first_ref, k_ref, v_ref, code, (one_ref, two_ref))
-    if out_ref is None:
-        return
-    rows = out_ref.shape[0]
     bias = link_bias(code[reach : reach + rows], code)
-    own = (bias, lambda lanes: k_ref[:, lanes], lambda lanes: v_ref[:, lanes])
-    attend_block(lambda lanes: q_ref[reach : reach + rows, lanes], [own], out_ref)
+    period = math.lcm(DH, LANES)
+    masks = head_masks(rows, period)
+    query = lambda lanes: q_ref[reach : reach + rows, lanes]
+    for base in range(0, out_ref.shape[1], period):
+        scores = period_scores(base, query, [lambda lanes: k_ref[:, lanes]], masks, period)
+        sets = [(bias, lambda lanes: v_ref[:, lanes])]
+        store_period(base, mixed_period(base, scores, sets, period), out_ref)
 
 
 def edge_kernel(reach, q_ref, k_ref, v_ref, code_ref, *refs):
-    halos = refs[:-4]
-    out_ref, keys, values, codes = refs[-4:]
+    halos = refs[:-6]
+    out_ref, keys, values, codes, near, sems = refs[-6:]
     tokens, width = q_ref.shape
+    copies = []
+    at = 0
+    for n, piece in enumerate(halos):
+        rows = piece.shape[0]
+        for m, (ref, size) in enumerate(((keys, width), (values, width), (codes, LANES))):
+            copies.append(
+                pltpu.make_async_copy(
+                    piece.at[:, pl.ds(m * width, size)], ref.at[pl.ds(at, rows)], sems.at[n, m]
+                )
+            )
+        at += rows
+    for copy in copies:
+        copy.start()
+    if at < keys.shape[0]:
+        for ref in (keys, values, codes):
+            ref[at:] = jnp.zeros((ref.shape[0] - at, ref.shape[1]), ref.dtype)
     code = columns(code_ref[...])
-    at = 0
-    for piece in halos:
-        rows = piece.shape[0]
-        keys[at : at + rows] = piece[:, :width]
-        values[at : at + rows] = piece[:, width : 2 * width]
-        codes[at : at + rows] = piece[:, 2 * width :].astype(jnp.float32)
-        at += rows
-    if at < keys.shape[0]:
-        spare = keys.shape[0] - at
-        keys[at:] = jnp.zeros((spare, width), keys.dtype)
-        values[at:] = jnp.zeros((spare, width), values.dtype)
-        codes[at:] = jnp.zeros((spare, LANES), codes.dtype)
     if tokens > 2 * reach:
         last = tokens - reach
         mine = jnp.concatenate((code[:reach], code[last:]), axis=0)
@@ -184,13 +190,32 @@
     else:
         mine = code
         query = lambda lanes: q_ref[:, lanes]
-    own = (link_bias(mine, code), lambda lanes: k_ref[:, lanes], lambda lanes: v_ref[:, lanes])
-    halo = (
-        link_bias(mine, codes[...]),
-        lambda lanes: keys[:, lanes],
-        lambda lanes: values[:, lanes],
-    )
-    attend_block(query, [own, halo], out_ref)
+    period = math.lcm(DH, LANES)
+    rows = out_ref.shape[0]
+    masks = head_masks(rows, period)
+    place = {}
+    at = 0
+    for base in range(0, width, period):
+        scores = period_scores(base, query, [lambda lanes: k_ref[:, lanes]], masks, period)
+        place[base] = []
+        for (part,) in scores:
+            near[at : at + part.shape[0]] = part
+            place[base].append((at, part.shape[0]))
+            at += part.shape[0]
+    own_bias = link_bias(mine, code)
+    for copy in copies:
+        copy.wait()
+    sets = [
+        (own_bias, lambda lanes: v_ref[:, lanes]),
+        (link_bias(mine, codes[...].astype(jnp.float32)), lambda lanes: values[:, lanes]),
+    ]
+    for base in range(0, width, period):
+        scores = period_scores(base, query, [lambda lanes: keys[:, lanes]], masks, period)
+        scores = [
+            [near[first : first + size], *parts]
+            for (first, size), parts in zip(place[base], scores)
+        ]
+        store_period(base, mixed_period(base, scores, sets, period), out_ref)
 
 
 def attend_cost(tokens, span, width):
@@ -206,21 +231,31 @@
 PARAMS = pltpu.CompilerParams(vmem_limit_bytes=VMEM_LIMIT)
 
 
-def attend_middle(firsts, queries, keys, values, code, reach):
+def pack_ends(firsts, keys, values, code, most):
+    width = keys.shape[1]
+    ends = jax.ShapeDtypeStruct((most, 2 * width + LANES), jnp.bfloat16)
+    return pl.pallas_call(
+        ends_kernel,
+        in_specs=[SMEM] + [VMEM] * 3,
+        out_specs=[VMEM] * 2,
+        out_shape=[ends, ends],
+        compiler_params=PARAMS,
+        cost_estimate=pl.CostEstimate(flops=0, bytes_accessed=16 * most * width, transcendentals=0),
+        name="pack_ends",
+    )(firsts, keys, values, code)
+
+
+def attend_middle(queries, keys, values, code, reach):
     tokens, width = queries.shape
-    ends = jax.ShapeDtypeStruct((min(tokens, reach), 2 * width + LANES), jnp.bfloat16)
-    outs = [ends, ends]
-    if tokens > 2 * reach:
-        outs.append(jax.ShapeDtypeStruct((tokens - 2 * reach, width), jnp.bfloat16))
     return pl.pallas_call(
         functools.partial(middle_kernel, reach),
-        in_specs=[SMEM] + [VMEM] * 4,
-        out_specs=[VMEM] * len(outs),
-        out_shape=outs,
+        in_specs=[VMEM] * 4,
+        out_specs=VMEM,
+        out_shape=jax.ShapeDtypeStruct((tokens - 2 * reach, width), jnp.bfloat16),
         compiler_params=PARAMS,
-        cost_estimate=attend_cost(tokens, tokens, width),
+        cost_estimate=attend_cost(tokens - 2 * reach, tokens, width),
         name="attend_middle",
-    )(firsts, queries, keys, values, code)
+    )(queries, keys, values, code)
 
 
 def attend_edges(queries, keys, values, code, halos, reach):
@@ -229,13 +264,15 @@
     held = -(-2 * reach // LANES) * LANES
     return pl.pallas_call(
         functools.partial(edge_kernel, reach),
-        in_specs=[VMEM] * (4 + len(halos)),
+        in_specs=[VMEM] * 4 + [pl.BlockSpec(memory_space=pltpu.HBM)] * len(halos),
         out_specs=VMEM,
         out_shape=jax.ShapeDtypeStruct((rows, width), jnp.bfloat16),
         scratch_shapes=[
             pltpu.VMEM((held, width), jnp.bfloat16),
             pltpu.VMEM((held, width), jnp.bfloat16),
-            pltpu.VMEM((held, LANES), jnp.float32),
+            pltpu.VMEM((held, LANES), jnp.bfloat16),
+            pltpu.VMEM((rows * (width // DH), tokens), jnp.float32),
+            pltpu.SemaphoreType.DMA((len(halos), 3)),
         ],
         compiler_params=PARAMS,
         cost_estimate=attend_cost(rows, LANES, width),
@@ -369,7 +406,7 @@
 
 def relay(rows, gate, branch, base, totals, spots, first_row, grads, last):
     tokens, width = base.shape
-    chunks = 2 if width // 2 % (2 * LANES) == 0 else 1
+    chunks = width // 2 // (2 * LANES) if width // 2 % (2 * LANES) == 0 else 1
     far = pl.BlockSpec(memory_space=pltpu.HBM)
     whole = jax.ShapeDtypeStruct((tokens, width), jnp.bfloat16)
 
@@ -443,7 +480,9 @@
     sent_a, sent_b = pack_grads(out_grad[0, 0], marks, queries, keys, values)
     code, sent_a, sent_b = lax.optimization_barrier((code, sent_a, sent_b))
     got_a, got_b = send(sent_a, SWAP_X), send(sent_b, SWAP_Y)
-    end_one, end_two, *own = attend_middle(firsts, queries, keys, values, code, reach)
+    end_one, end_two = pack_ends(firsts, keys, values, code, most)
+    code, end_one, end_two = lax.optimization_barrier((code, end_one, end_two))
+    own = [attend_middle(queries, keys, values, code, reach)] if tokens > 2 * reach else []
     gate = whole_gate(control_gate)[None]
     halos = [paired(end_one, "seq", 0), paired(end_two, "seq", 1)]
     for hop in range(2, hops + 1):

time: 41.6 us -> 40.5 us (0.974)
  waiting for transfers between devices: 12.3 us -> 10.6 us
  Pallas kernels: 10.9 us -> 11.4 us
    ppermute x2, waiting for transfers between devices: 3.43 us -> 1.99 us  [paired(): return lax.ppermute(block, axis, route)]
    pallas_call x2 -> x3, Pallas kernels: 6.17 us -> 6.68 us  [the longest x1 3.59 us: attend_edges(): pl.pallas_call(functools.partial(edge_kernel, reach), in_specs=[VMEM] * 4...]
  transfers between devices with their start and end apart: 13 -> 13, of which waited for: 8 -> 7; matrix products, arithmetic and copies ran while one was open for 4% -> 4% of each run, Pallas kernels for 23% -> 25%
where the time goes in v10:
time: 40.5 us; the launch traced here: 40.3 us
  starting transfers between devices  15.8 us (39%)
  Pallas kernels  11.4 us (28%)
  waiting for transfers between devices  10.6 us (26%)
  other arithmetic  1.52 us (4%)
  between operations  0.86 us (2%)
    ppermute x10, starting transfers between devices, local(): send = lambda block, route: lax.ppermute(block, 'grp', route)  10.7 us
    ppermute x10, waiting for transfers between devices, local(): send = lambda block, route: lax.ppermute(block, 'grp', route)  8.62 us
    ppermute x2, starting transfers between devices, paired(): return lax.ppermute(block, axis, route)  5.05 us
    pallas_call x1, Pallas kernels, attend_edges(): pl.pallas_call(functools.partial(edge_kernel, reach), in_specs=[VMEM] * 4...  3.59 us
    pallas_call x2, Pallas kernels, relay(): pl.pallas_call(kernel, in_specs=[VMEM] * 7 + ([] if grads is None else [f...  2.19 us
    ppermute x2, waiting for transfers between devices, paired(): return lax.ppermute(block, axis, route)  1.99 us
    pallas_call x1, Pallas kernels, attend_middle(): pl.pallas_call(functools.partial(middle_kernel, reach), in_specs=[VMEM] *...  1.61 us
    pallas_call x1, Pallas kernels, pack_ends(): pl.pallas_call(ends_kernel, in_specs=[SMEM] + [VMEM] * 3, out_specs=[VMEM...  1.48 us
  transfers between devices with their start and end apart: 13, of which 7 were waited for; matrix products, arithmetic and copies ran while one was open for 4% of the time, Pallas kernels for 25%

profile of v10, /device:TPU:8, one launch (start us, length us, event | category | flops | bytes accessed | tf_op | source)
XLA Modules:
  0.0 40.3 jit_solution(3027874598953958846)
XLA Ops:
  0.7 0.7 %and_select_fusion = (s32[1,128]{1,0:T(1,128)S(1)}, s32[1,128]{1,0:T(1,128)S(1)}) fusion(s32[1,1,128]{2,1,0:T(1,128)} %param.11, s32[1,1,128]{2,1,0:T(1,128)} %param.10), kind=kLoop, calls=%fused_computation.32 | loop fusion | flops 2816 | bytes 2048 | tf_op jit(solution)/shard_map/jit(remainder)/select_n | solution.py:475
  1.4 1.2 %pack_grads.1 = (bf16[128,1408]{1,0:T(8,128)(2,1)S(1)}, bf16[128,1408]{1,0:T(8,128)(2,1)S(1)}) custom-call(bf16[128,2560]{1,0:T(8,128)(2,1)} %bitcast.38, f32[2,128]{1,0:T(2,128)S(1)} %add_convert_fusion.5.mark_ref, bf16[128,2560]{1,0:T(8,128)(2,1)} %bitcast.35, bf16[128,2560]{1,0:T(8,128)(2,1)} %bitcast.27, bf16[128,2560]{1,0:T(8,128)(2,1)} %bitcast.31), custom_call_target="tpu_custom_call" | custom-call | bytes 1310720 | tf_op jit(solution)/shard_map/pack_grads/pallas_call | solution.py:305
  2.7 1.6 %collective-permute-start.1 = (bf16[128,1408]{1,0:T(8,128)(2,1)S(1)}, bf16[128,1408]{1,0:T(8,128)(2,1)S(1)}, u32[]{:S(2)}, u32[]{:S(2)}) collective-permute-start(bf16[128,1408]{1,0:T(8,128)(2,1)S(1)} %get-tuple-element.33.refs_0_), channel_id=1, source_target_pairs={{0,8},{8,0},{16,24},{24,16},{1,9},{9,1},{17,25},{25,17},{2,10},{10... | collective-permute-start | bytes 1081352 | tf_op jit(solution)/shard_map/ppermute | solution.py:471
  4.2 1.5 %collective-permute-start.2 = (bf16[128,1408]{1,0:T(8,128)(2,1)S(1)}, bf16[128,1408]{1,0:T(8,128)(2,1)}, u32[]{:S(2)}, u32[]{:S(2)}) collective-permute-start(bf16[128,1408]{1,0:T(8,128)(2,1)S(1)} %get-tuple-element.34.refs_2_), channel_id=1, source_target_pairs={{0,16},{16,0},{8,24},{24,8},{1,17},{17,1},{9,25},{25,9},{2,18},{18... | collective-permute-start | bytes 1081352 | tf_op jit(solution)/shard_map/ppermute | solution.py:471
  5.8 1.5 %pack_ends.1 = (bf16[32,5248]{1,0:T(8,128)(2,1)}, bf16[32,5248]{1,0:T(8,128)(2,1)}) custom-call(s32[2]{0:T(128)S(1)} %add_select_fusion.first_ref, bf16[128,2560]{1,0:T(8,128)(2,1)S(1)} %bitcast.28, bf16[128,2560]{1,0:T(8,128)(2,1)S(1)} %bitcast.32, f32[1,128]{1,0:T(1,128)S(1)} %get-tuple-element.39.code_ref), custom_call_target="tpu_custom_call" | custom-call | bytes 1310720 | tf_op jit(solution)/shard_map/pack_ends/pallas_call | solution.py:237
  7.8 4.6 %collective-permute-start.4 = (bf16[32,5248]{1,0:T(8,128)(2,1)}, bf16[32,5248]{1,0:T(8,128)(2,1)}, u32[]{:S(2)}, u32[]{:S(2)}) collective-permute-start(bf16[32,5248]{1,0:T(8,128)(2,1)} %get-tuple-element.41), channel_id=1, source_target_pairs={{2,4},{4,2},{3,5},{5,3},{10,12},{12,10},{11,13},{13,11},{18,20},{2... | collective-permute-start | bytes 1007624 | tf_op jit(solution)/shard_map/ppermute | solution.py:32
  12.4 1.6 %attend_middle.1 = bf16[64,2560]{1,0:T(8,128)(2,1)S(1)} custom-call(bf16[128,2560]{1,0:T(8,128)(2,1)S(1)} %bitcast.36, bf16[128,2560]{1,0:T(8,128)(2,1)S(1)} %bitcast.29, bf16[128,2560]{1,0:T(8,128)(2,1)S(1)} %bitcast.33, f32[1,128]{1,0:T(1,128)S(1)} %get-tuple-element.39.code_ref), custom_call_target="tpu_custom_call" | custom-call | flops 268435456 | bytes 1966080 | tf_op jit(solution)/shard_map/attend_middle/pallas_call | solution.py:250
  14.2 0.7 %collective-permute-done.2.refs_3_ = bf16[128,1408]{1,0:T(8,128)(2,1)} collective-permute-done((bf16[128,1408]{1,0:T(8,128)(2,1)S(1)}, bf16[128,1408]{1,0:T(8,128)(2,1)}, u32[]{:S(2)}, u32[]{:S(2)}) %collective-permute-start.2) | collective-permute-done | bytes 360480 | tf_op jit(solution)/shard_map/ppermute | solution.py:471
  14.9 1.4 %pair_sums.1 = (bf16[64,1280]{1,0:T(8,128)(2,1)S(1)}, bf16[64,1280]{1,0:T(8,128)(2,1)S(1)}, bf16[64,1280]{1,0:T(8,128)(2,1)S(1)}, bf16[64,1280]{1,0:T(8,128)(2,1)S(1)}) custom-call(f32[2]{0:T(128)S(1)} %add_convert_fusion.4.flag_ref, f32[1,2560]{1,0:T(1,128)S(1)} %broadcast_in_dim.17.gate_ref, bf16[128,1408]{1,0:T(8,128)(2,1)S(1)} %get-tuple-element.33.refs_0_, ...), custom_call_target="tpu_custom_call" | custom-call | flops 167772160 | bytes 1966080 | tf_op jit(solution)/shard_map/pair_sums/pallas_call | solution.py:349
  16.3 0.6 %collective-permute-start.9 = (bf16[64,1280]{1,0:T(8,128)(2,1)S(1)}, bf16[64,1280]{1,0:T(8,128)(2,1)S(1)}, u32[]{:S(2)}, u32[]{:S(2)}) collective-permute-start(bf16[64,1280]{1,0:T(8,128)(2,1)S(1)} %get-tuple-element.44), channel_id=1, source_target_pairs={{0,8},{8,24},{24,16},{16,0},{1,9},{9,25},{25,17},{17,1},{2,10},{10... | collective-permute-start | bytes 491528 | tf_op jit(solution)/shard_map/ppermute | solution.py:471
  16.9 1.5 %collective-permute-start.10 = (bf16[64,1280]{1,0:T(8,128)(2,1)S(1)}, bf16[64,1280]{1,0:T(8,128)(2,1)S(1)}, u32[]{:S(2)}, u32[]{:S(2)}) collective-permute-start(bf16[64,1280]{1,0:T(8,128)(2,1)S(1)} %get-tuple-element.46), channel_id=1, source_target_pairs={{0,16},{16,24},{24,8},{8,0},{1,17},{17,25},{25,9},{9,1},{2,18},{18... | collective-permute-start | bytes 491528 | tf_op jit(solution)/shard_map/ppermute | solution.py:471
  18.4 2.0 %collective-permute-done.4.refs_1_ = bf16[32,5248]{1,0:T(8,128)(2,1)} collective-permute-done((bf16[32,5248]{1,0:T(8,128)(2,1)}, bf16[32,5248]{1,0:T(8,128)(2,1)}, u32[]{:S(2)}, u32[]{:S(2)}) %collective-permute-start.4) | collective-permute-done | bytes 335904 | tf_op jit(solution)/shard_map/ppermute | solution.py:32
  20.4 3.6 %attend_edges.1 = bf16[64,2560]{1,0:T(8,128)(2,1)S(1)} custom-call(bf16[128,2560]{1,0:T(8,128)(2,1)S(1)} %bitcast.37, bf16[128,2560]{1,0:T(8,128)(2,1)S(1)} %bitcast.30, bf16[128,2560]{1,0:T(8,128)(2,1)S(1)} %bitcast.34, f32[1,128]{1,0:T(1,128)S(1)} %get-tuple-element.39.code_ref, bf16[32,5248]{1,0:T(8,128)(2,1)} %collective-permute-done.3.refs_0_, ...), custom_call_target="tpu_custom_call" | custom-call | flops 268435456 | bytes 1966080 | tf_op jit(solution)/shard_map/attend_edges/pallas_call | solution.py:265
  24.0 0.6 %collective-permute-start.6 = (bf16[64,1280]{1,0:T(8,128)(2,1)S(1)}, bf16[64,1280]{1,0:T(8,128)(2,1)S(1)}, u32[]{:S(2)}, u32[]{:S(2)}) collective-permute-start(bf16[64,1280]{1,0:T(8,128)(2,1)S(1)} %get-tuple-element.64), channel_id=1, source_target_pairs={{0,16},{16,24},{24,8},{8,0},{1,17},{17,25},{25,9},{9,1},{2,18},{18... | collective-permute-start | bytes 491528 | tf_op jit(solution)/shard_map/ppermute | solution.py:471
  24.6 1.5 %collective-permute-start.5 = (bf16[64,1280]{1,0:T(8,128)(2,1)S(1)}, bf16[64,1280]{1,0:T(8,128)(2,1)S(1)}, u32[]{:S(2)}, u32[]{:S(2)}) collective-permute-start(bf16[64,1280]{1,0:T(8,128)(2,1)S(1)} %get-tuple-element.65), channel_id=1, source_target_pairs={{0,8},{8,24},{24,16},{16,0},{1,9},{9,25},{25,17},{17,1},{2,10},{10... | collective-permute-start | bytes 491528 | tf_op jit(solution)/shard_map/ppermute | solution.py:471
  26.4 0.6 %collective-permute-start.12 = (bf16[64,1280]{1,0:T(8,128)(2,1)S(1)}, bf16[64,1280]{1,0:T(8,128)(2,1)S(1)}, u32[]{:S(2)}, u32[]{:S(2)}) collective-permute-start(bf16[64,1280]{1,0:T(8,128)(2,1)S(1)} %get-tuple-element.52), channel_id=1, source_target_pairs={{0,8},{8,0},{16,24},{24,16},{1,9},{9,1},{17,25},{25,17},{2,10},{10... | collective-permute-start | bytes 491528 | tf_op jit(solution)/shard_map/ppermute | solution.py:471
  27.0 0.5 %collective-permute-start.11 = (bf16[64,1280]{1,0:T(8,128)(2,1)S(1)}, bf16[64,1280]{1,0:T(8,128)(2,1)S(1)}, u32[]{:S(2)}, u32[]{:S(2)}) collective-permute-start(bf16[64,1280]{1,0:T(8,128)(2,1)S(1)} %get-tuple-element.60), channel_id=1, source_target_pairs={{0,16},{16,0},{8,24},{24,8},{1,17},{17,1},{9,25},{25,9},{2,18},{18... | collective-permute-start | bytes 491528 | tf_op jit(solution)/shard_map/ppermute | solution.py:471
  27.5 3.7 %collective-permute-done.6 = bf16[64,1280]{1,0:T(8,128)(2,1)S(1)} collective-permute-done((bf16[64,1280]{1,0:T(8,128)(2,1)S(1)}, bf16[64,1280]{1,0:T(8,128)(2,1)S(1)}, u32[]{:S(2)}, u32[]{:S(2)}) %collective-permute-start.6) | collective-permute-done | bytes 163872 | tf_op jit(solution)/shard_map/ppermute | solution.py:471
  31.5 2.0 %collective-permute-start.8 = (bf16[64,1280]{1,0:T(8,128)(2,1)S(1)}, bf16[64,1280]{1,0:T(8,128)(2,1)S(1)}, u32[]{:S(2)}, u32[]{:S(2)}) collective-permute-start(bf16[64,1280]{1,0:T(8,128)(2,1)S(1)} %get-tuple-element.56), channel_id=1, source_target_pairs={{0,8},{8,0},{16,24},{24,16},{1,9},{9,1},{17,25},{25,17},{2,10},{10... | collective-permute-start | bytes 491528 | tf_op jit(solution)/shard_map/ppermute | solution.py:471
  33.8 0.8 %collective-permute-done.12 = bf16[64,1280]{1,0:T(8,128)(2,1)S(1)} collective-permute-done((bf16[64,1280]{1,0:T(8,128)(2,1)S(1)}, bf16[64,1280]{1,0:T(8,128)(2,1)S(1)}, u32[]{:S(2)}, u32[]{:S(2)}) %collective-permute-start.12) | collective-permute-done | bytes 163872 | tf_op jit(solution)/shard_map/ppermute | solution.py:471
  34.7 0.8 %relay.2 = (bf16[128,2560]{1,0:T(8,128)(2,1)}, f32[128,2560]{1,0:T(8,128)S(1)}) custom-call(f32[1,128]{1,0:T(1,128)S(1)} %get-tuple-element.81.row_ref, f32[1,2560]{1,0:T(1,128)S(1)} %broadcast_in_dim.17.gate_ref, bf16[64,1280]{1,0:T(8,128)(2,1)S(1)} %get-tuple-element.71.a_ref, bf16[64,1280]{1,0:T(8,128)(2,1)S(1)} %get-tuple-element.70.b_ref, ...), custom_call_target="tpu_custom_call" | custom-call | flops 83886080 | bytes 7864320 | tf_op jit(solution)/shard_map/relay/pallas_call | solution.py:429
  35.5 1.4 %collective-permute-done.8 = bf16[64,1280]{1,0:T(8,128)(2,1)S(1)} collective-permute-done((bf16[64,1280]{1,0:T(8,128)(2,1)S(1)}, bf16[64,1280]{1,0:T(8,128)(2,1)S(1)}, u32[]{:S(2)}, u32[]{:S(2)}) %collective-permute-start.8) | collective-permute-done | bytes 163872 | tf_op jit(solution)/shard_map/ppermute | solution.py:471
  36.9 1.9 %collective-permute-done.7 = bf16[64,1280]{1,0:T(8,128)(2,1)S(1)} collective-permute-done((bf16[64,1280]{1,0:T(8,128)(2,1)S(1)}, bf16[64,1280]{1,0:T(8,128)(2,1)S(1)}, u32[]{:S(2)}, u32[]{:S(2)}) %collective-permute-start.7) | collective-permute-done | bytes 163872 | tf_op jit(solution)/shard_map/ppermute | solution.py:471
  38.9 1.3 %relay.3 = (bf16[128,2560]{1,0:T(8,128)(2,1)}, bf16[128,2560]{1,0:T(8,128)(2,1)}) custom-call(f32[1,128]{1,0:T(1,128)S(1)} %get-tuple-element.81.row_ref, f32[1,2560]{1,0:T(1,128)S(1)} %broadcast_in_dim.17.gate_ref, bf16[64,1280]{1,0:T(8,128)(2,1)S(1)} %get-tuple-element.73.a_ref, ...), custom_call_target="tpu_custom_call", output_to_operand_aliasing={{0}: (7, {})} | custom-call | flops 83886080 | bytes 7864320 | tf_op jit(solution)/shard_map/relay/pallas_call | solution.py:429
  (33 shorter events, 1.9 us)
Async XLA Ops:
  0.6 13.5 %collective-permute-start = (f32[1280]{0:T(1024)}, f32[1280]{0:T(1024)S(1)}, u32[]{:S(2)}, u32[]{:S(2)}) collective-permute-start(f32[1280]{0:T(1024)} %param.12), channel_id=1, source_target_pairs={{0,1},{1,0},{2,3},{3,2},{4,5},{5,4},{6,7},{7,6},{8,9},{9,8},{10,11... | collective-permute-start | bytes 15368 | tf_op jit(solution)/shard_map/ppermute | solution.py:450
  1.4 4.4 %copy-start = (bf16[1,1,128,2560]{3,2,1,0:T(8,128)(2,1)S(1)}, bf16[1,1,128,2560]{3,2,1,0:T(8,128)(2,1)}, u32[]{:S(2)}) copy-start(bf16[1,1,128,2560]{3,2,1,0:T(8,128)(2,1)} %param.8) | copy-start | bytes 1966084
  1.4 4.4 %copy-start.1 = (bf16[1,1,128,2560]{3,2,1,0:T(8,128)(2,1)S(1)}, bf16[1,1,128,2560]{3,2,1,0:T(8,128)(2,1)}, u32[]{:S(2)}) copy-start(bf16[1,1,128,2560]{3,2,1,0:T(8,128)(2,1)} %param.9) | copy-start | bytes 1966084
  2.6 9.8 %copy-start.2 = (bf16[1,1,128,2560]{3,2,1,0:T(8,128)(2,1)S(1)}, bf16[1,1,128,2560]{3,2,1,0:T(8,128)(2,1)}, u32[]{:S(2)}) copy-start(bf16[1,1,128,2560]{3,2,1,0:T(8,128)(2,1)} %param.7) | copy-start | bytes 1966084
  2.7 11.5 %collective-permute-start.1 = (bf16[128,1408]{1,0:T(8,128)(2,1)S(1)}, bf16[128,1408]{1,0:T(8,128)(2,1)S(1)}, u32[]{:S(2)}, u32[]{:S(2)}) collective-permute-start(bf16[128,1408]{1,0:T(8,128)(2,1)S(1)} %get-tuple-element.33.refs_0_), channel_id=1, source_target_pairs={{0,8},{8,0},{16,24},{24,16},{1,9},{9,1},{17,25},{25,17},{2,10},{10... | collective-permute-start | bytes 1081352 | tf_op jit(solution)/shard_map/ppermute | solution.py:471
  4.2 10.6 %collective-permute-start.2 = (bf16[128,1408]{1,0:T(8,128)(2,1)S(1)}, bf16[128,1408]{1,0:T(8,128)(2,1)}, u32[]{:S(2)}, u32[]{:S(2)}) collective-permute-start(bf16[128,1408]{1,0:T(8,128)(2,1)S(1)} %get-tuple-element.34.refs_2_), channel_id=1, source_target_pairs={{0,16},{16,0},{8,24},{24,8},{1,17},{17,1},{9,25},{25,9},{2,18},{18... | collective-permute-start | bytes 1081352 | tf_op jit(solution)/shard_map/ppermute | solution.py:471
  7.3 6.8 %copy-start.3 = (f32[1280]{0:T(1024)S(1)}, f32[1280]{0:T(1024)}, u32[]{:S(2)}) copy-start(f32[1280]{0:T(1024)} %param.12) | copy-start | bytes 15364
  7.3 11.1 %collective-permute-start.3 = (bf16[32,5248]{1,0:T(8,128)(2,1)}, bf16[32,5248]{1,0:T(8,128)(2,1)}, u32[]{:S(2)}, u32[]{:S(2)}) collective-permute-start(bf16[32,5248]{1,0:T(8,128)(2,1)} %get-tuple-element.40), channel_id=1, source_target_pairs={{0,2},{2,0},{4,6},{6,4},{1,3},{3,1},{5,7},{7,5},{8,10},{10,8},{12,... | collective-permute-start | bytes 1007624 | tf_op jit(solution)/shard_map/ppermute | solution.py:32
  7.8 12.6 %collective-permute-start.4 = (bf16[32,5248]{1,0:T(8,128)(2,1)}, bf16[32,5248]{1,0:T(8,128)(2,1)}, u32[]{:S(2)}, u32[]{:S(2)}) collective-permute-start(bf16[32,5248]{1,0:T(8,128)(2,1)} %get-tuple-element.41), channel_id=1, source_target_pairs={{2,4},{4,2},{3,5},{5,3},{10,12},{12,10},{11,13},{13,11},{18,20},{2... | collective-permute-start | bytes 1007624 | tf_op jit(solution)/shard_map/ppermute | solution.py:32
  16.3 9.9 %collective-permute-start.9 = (bf16[64,1280]{1,0:T(8,128)(2,1)S(1)}, bf16[64,1280]{1,0:T(8,128)(2,1)S(1)}, u32[]{:S(2)}, u32[]{:S(2)}) collective-permute-start(bf16[64,1280]{1,0:T(8,128)(2,1)S(1)} %get-tuple-element.44), channel_id=1, source_target_pairs={{0,8},{8,24},{24,16},{16,0},{1,9},{9,25},{25,17},{17,1},{2,10},{10... | collective-permute-start | bytes 491528 | tf_op jit(solution)/shard_map/ppermute | solution.py:471
  16.9 9.3 %collective-permute-start.10 = (bf16[64,1280]{1,0:T(8,128)(2,1)S(1)}, bf16[64,1280]{1,0:T(8,128)(2,1)S(1)}, u32[]{:S(2)}, u32[]{:S(2)}) collective-permute-start(bf16[64,1280]{1,0:T(8,128)(2,1)S(1)} %get-tuple-element.46), channel_id=1, source_target_pairs={{0,16},{16,24},{24,8},{8,0},{1,17},{17,25},{25,9},{9,1},{2,18},{18... | collective-permute-start | bytes 491528 | tf_op jit(solution)/shard_map/ppermute | solution.py:471
  24.0 7.1 %collective-permute-start.6 = (bf16[64,1280]{1,0:T(8,128)(2,1)S(1)}, bf16[64,1280]{1,0:T(8,128)(2,1)S(1)}, u32[]{:S(2)}, u32[]{:S(2)}) collective-permute-start(bf16[64,1280]{1,0:T(8,128)(2,1)S(1)} %get-tuple-element.64), channel_id=1, source_target_pairs={{0,16},{16,24},{24,8},{8,0},{1,17},{17,25},{25,9},{9,1},{2,18},{18... | collective-permute-start | bytes 491528 | tf_op jit(solution)/shard_map/ppermute | solution.py:471
  24.6 6.7 %collective-permute-start.5 = (bf16[64,1280]{1,0:T(8,128)(2,1)S(1)}, bf16[64,1280]{1,0:T(8,128)(2,1)S(1)}, u32[]{:S(2)}, u32[]{:S(2)}) collective-permute-start(bf16[64,1280]{1,0:T(8,128)(2,1)S(1)} %get-tuple-element.65), channel_id=1, source_target_pairs={{0,8},{8,24},{24,16},{16,0},{1,9},{9,25},{25,17},{17,1},{2,10},{10... | collective-permute-start | bytes 491528 | tf_op jit(solution)/shard_map/ppermute | solution.py:471
  26.4 8.2 %collective-permute-start.12 = (bf16[64,1280]{1,0:T(8,128)(2,1)S(1)}, bf16[64,1280]{1,0:T(8,128)(2,1)S(1)}, u32[]{:S(2)}, u32[]{:S(2)}) collective-permute-start(bf16[64,1280]{1,0:T(8,128)(2,1)S(1)} %get-tuple-element.52), channel_id=1, source_target_pairs={{0,8},{8,0},{16,24},{24,16},{1,9},{9,1},{17,25},{25,17},{2,10},{10... | collective-permute-start | bytes 491528 | tf_op jit(solution)/shard_map/ppermute | solution.py:471
  27.0 7.6 %collective-permute-start.11 = (bf16[64,1280]{1,0:T(8,128)(2,1)S(1)}, bf16[64,1280]{1,0:T(8,128)(2,1)S(1)}, u32[]{:S(2)}, u32[]{:S(2)}) collective-permute-start(bf16[64,1280]{1,0:T(8,128)(2,1)S(1)} %get-tuple-element.60), channel_id=1, source_target_pairs={{0,16},{16,0},{8,24},{24,8},{1,17},{17,1},{9,25},{25,9},{2,18},{18... | collective-permute-start | bytes 491528 | tf_op jit(solution)/shard_map/ppermute | solution.py:471
  31.5 5.4 %collective-permute-start.8 = (bf16[64,1280]{1,0:T(8,128)(2,1)S(1)}, bf16[64,1280]{1,0:T(8,128)(2,1)S(1)}, u32[]{:S(2)}, u32[]{:S(2)}) collective-permute-start(bf16[64,1280]{1,0:T(8,128)(2,1)S(1)} %get-tuple-element.56), channel_id=1, source_target_pairs={{0,8},{8,0},{16,24},{24,16},{1,9},{9,1},{17,25},{25,17},{2,10},{10... | collective-permute-start | bytes 491528 | tf_op jit(solution)/shard_map/ppermute | solution.py:471
  33.5 5.3 %collective-permute-start.7 = (bf16[64,1280]{1,0:T(8,128)(2,1)S(1)}, bf16[64,1280]{1,0:T(8,128)(2,1)S(1)}, u32[]{:S(2)}, u32[]{:S(2)}) collective-permute-start(bf16[64,1280]{1,0:T(8,128)(2,1)S(1)} %get-tuple-element.62), channel_id=1, source_target_pairs={{0,16},{16,0},{8,24},{24,8},{1,17},{17,1},{9,25},{25,9},{2,18},{18... | collective-permute-start | bytes 491528 | tf_op jit(solution)/shard_map/ppermute | solution.py:471

commit v11 on v10

--- a/solution.py
+++ b/solution.py
@@ -163,21 +163,36 @@
 
 
 def edge_kernel(reach, q_ref, k_ref, v_ref, code_ref, *refs):
-    halos = refs[:-6]
-    out_ref, keys, values, codes, near, sems = refs[-6:]
+    halos = refs[:-5]
+    out_ref, keys, values, codes, sems = refs[-5:]
     tokens, width = q_ref.shape
-    copies = []
+    period = math.lcm(DH, LANES)
+    bases = list(range(0, width, period))
+    waits = {base: [] for base in bases}
+    code_waits = []
     at = 0
     for n, piece in enumerate(halos):
-        rows = piece.shape[0]
-        for m, (ref, size) in enumerate(((keys, width), (values, width), (codes, LANES))):
-            copies.append(
-                pltpu.make_async_copy(
-                    piece.at[:, pl.ds(m * width, size)], ref.at[pl.ds(at, rows)], sems.at[n, m]
+        rows = pl.ds(at, piece.shape[0])
+        code_waits.append(
+            pltpu.make_async_copy(
+                piece.at[:, pl.ds(2 * width, LANES)], codes.at[rows], sems.at[n, 2 * len(bases)]
+            )
+        )
+        at += piece.shape[0]
+    for c, base in enumerate(bases):
+        at = 0
+        for n, piece in enumerate(halos):
+            rows = pl.ds(at, piece.shape[0])
+            for m, ref in enumerate((keys, values)):
+                waits[base].append(
+                    pltpu.make_async_copy(
+                        piece.at[:, pl.ds(m * width + base, period)],
+                        ref.at[rows, pl.ds(base, period)],
+                        sems.at[n, 2 * c + m],
+                    )
                 )
-            )
-        at += rows
-    for copy in copies:
+            at += piece.shape[0]
+    for copy in code_waits + [copy for base in bases for copy in waits[base]]:
         copy.start()
     if at < keys.shape[0]:
         for ref in (keys, values, codes):
@@ -190,31 +205,24 @@
     else:
         mine = code
         query = lambda lanes: q_ref[:, lanes]
-    period = math.lcm(DH, LANES)
-    rows = out_ref.shape[0]
-    masks = head_masks(rows, period)
-    place = {}
-    at = 0
-    for base in range(0, width, period):
-        scores = period_scores(base, query, [lambda lanes: k_ref[:, lanes]], masks, period)
-        place[base] = []
-        for (part,) in scores:
-            near[at : at + part.shape[0]] = part
-            place[base].append((at, part.shape[0]))
-            at += part.shape[0]
+    masks = head_masks(out_ref.shape[0], period)
     own_bias = link_bias(mine, code)
-    for copy in copies:
-        copy.wait()
-    sets = [
-        (own_bias, lambda lanes: v_ref[:, lanes]),
-        (link_bias(mine, codes[...].astype(jnp.float32)), lambda lanes: values[:, lanes]),
-    ]
-    for base in range(0, width, period):
-        scores = period_scores(base, query, [lambda lanes: keys[:, lanes]], masks, period)
-        scores = [
-            [near[first : first + size], *parts]
-            for (first, size), parts in zip(place[base], scores)
-        ]
+    own_key, halo_key = lambda lanes: k_ref[:, lanes], lambda lanes: keys[:, lanes]
+    own_value, halo_value = lambda lanes: v_ref[:, lanes], lambda lanes: values[:, lanes]
+    halo_bias = None
+    for base in bases:
+        if halo_bias is None:
+            early = period_scores(base, query, [own_key], masks, period)
+            for copy in code_waits + waits[base]:
+                copy.wait()
+            halo_bias = link_bias(mine, codes[...].astype(jnp.float32))
+            late = period_scores(base, query, [halo_key], masks, period)
+            scores = [first + second for first, second in zip(early, late)]
+        else:
+            for copy in waits[base]:
+                copy.wait()
+            scores = period_scores(base, query, [own_key, halo_key], masks, period)
+        sets = [(own_bias, own_value), (halo_bias, halo_value)]
         store_period(base, mixed_period(base, scores, sets, period), out_ref)
 
 
@@ -271,8 +279,7 @@
             pltpu.VMEM((held, width), jnp.bfloat16),
             pltpu.VMEM((held, width), jnp.bfloat16),
             pltpu.VMEM((held, LANES), jnp.bfloat16),
-            pltpu.VMEM((rows * (width // DH), tokens), jnp.float32),
-            pltpu.SemaphoreType.DMA((len(halos), 3)),
+            pltpu.SemaphoreType.DMA((len(halos), 2 * width // math.lcm(DH, LANES) + 1)),
         ],
         compiler_params=PARAMS,
         cost_estimate=attend_cost(rows, LANES, width),
@@ -323,8 +330,14 @@
 def sums_kernel(sizes, flag_ref, gate_ref, *refs):
     half = gate_ref.shape[1] // 2
     count = len(sizes)
+    second, sem = refs[-2:]
+    copy = pltpu.make_async_copy(refs[3], second, sem)
+    copy.start()
     for n in range(2):
         mine_ref, theirs_ref = refs[2 * n : 2 * n + 2]
+        if n == 1:
+            theirs_ref = second
+            copy.wait()
         picks, rows = [], []
         for ref in (mine_ref, theirs_ref):
             place = ref[:, half : half + LANES].astype(jnp.float32).T[:1]
@@ -348,7 +361,8 @@
     outs = [jax.ShapeDtypeStruct((size, width // 2), jnp.bfloat16) for size in sizes] * 2
     return pl.pallas_call(
         functools.partial(sums_kernel, sizes),
-        in_specs=[SMEM] + [VMEM] * 5,
+        in_specs=[SMEM] + [VMEM] * 4 + [pl.BlockSpec(memory_space=pltpu.HBM)],
+        scratch_shapes=[pltpu.VMEM(parts[3].shape, jnp.bfloat16), pltpu.SemaphoreType.DMA],
         out_specs=[VMEM] * len(outs),
         out_shape=outs,
         compiler_params=PARAMS,
@@ -406,7 +420,7 @@
 
 def relay(rows, gate, branch, base, totals, spots, first_row, grads, last):
     tokens, width = base.shape
-    chunks = width // 2 // (2 * LANES) if width // 2 % (2 * LANES) == 0 else 1
+    chunks = 2 if width // 2 % (2 * LANES) == 0 else 1
     far = pl.BlockSpec(memory_space=pltpu.HBM)
     whole = jax.ShapeDtypeStruct((tokens, width), jnp.bfloat16)
 

time: 40.5 us -> 40.5 us (level)
  the two profiles are of different devices: /device:TPU:8 before, /device:TPU:0 now
where the time goes in v11:
time: 40.5 us; the launch traced here: 40 us
  starting transfers between devices  15 us (37%)
  Pallas kernels  11.9 us (29%)
  waiting for transfers between devices  10.7 us (26%)
  other arithmetic  1.51 us (4%)
  between operations  0.83 us (2%)
    ppermute x10, starting transfers between devices, local(): send = lambda block, route: lax.ppermute(block, 'grp', route)  11.5 us
    ppermute x10, waiting for transfers between devices, local(): send = lambda block, route: lax.ppermute(block, 'grp', route)  10.6 us
    pallas_call x1, Pallas kernels, attend_edges(): pl.pallas_call(functools.partial(edge_kernel, reach), in_specs=[VMEM] * 4...  3.67 us
    ppermute x2, starting transfers between devices, paired(): return lax.ppermute(block, axis, route)  2.98 us
    pallas_call x2, Pallas kernels, relay(): pl.pallas_call(kernel, in_specs=[VMEM] * 7 + ([] if grads is None else [f...  2.11 us
    pallas_call x1, Pallas kernels, pair_sums(): pl.pallas_call(functools.partial(sums_kernel, sizes), in_specs=[SMEM] + [...  1.86 us
    pallas_call x1, Pallas kernels, attend_middle(): pl.pallas_call(functools.partial(middle_kernel, reach), in_specs=[VMEM] *...  1.63 us
    pallas_call x1, Pallas kernels, pack_ends(): pl.pallas_call(ends_kernel, in_specs=[SMEM] + [VMEM] * 3, out_specs=[VMEM...  1.48 us
  transfers between devices with their start and end apart: 13, of which 7 were waited for; matrix products, arithmetic and copies ran while one was open for 4% of the time, Pallas kernels for 27%

profile of v11, /device:TPU:0, one launch (start us, length us, event | category | flops | bytes accessed | tf_op | source)
XLA Modules:
  0.0 40.0 jit_solution(11542691405441656655)
XLA Ops:
  0.6 0.5 %collective-permute-start = (f32[1280]{0:T(1024)}, f32[1280]{0:T(1024)S(1)}, u32[]{:S(2)}, u32[]{:S(2)}) collective-permute-start(f32[1280]{0:T(1024)} %param.12), channel_id=1, source_target_pairs={{0,1},{1,0},{2,3},{3,2},{4,5},{5,4},{6,7},{7,6},{8,9},{9,8},{10,11... | collective-permute-start | bytes 15368 | tf_op jit(solution)/shard_map/ppermute | solution.py:464
  1.1 0.7 %and_select_fusion = (s32[1,128]{1,0:T(1,128)S(1)}, s32[1,128]{1,0:T(1,128)S(1)}) fusion(s32[1,1,128]{2,1,0:T(1,128)} %param.11, s32[1,1,128]{2,1,0:T(1,128)} %param.10), kind=kLoop, calls=%fused_computation.32 | loop fusion | flops 2816 | bytes 2048 | tf_op jit(solution)/shard_map/jit(remainder)/select_n | solution.py:489
  1.9 1.2 %pack_grads.1 = (bf16[128,1408]{1,0:T(8,128)(2,1)S(1)}, bf16[128,1408]{1,0:T(8,128)(2,1)S(1)}) custom-call(bf16[128,2560]{1,0:T(8,128)(2,1)} %bitcast.38, f32[2,128]{1,0:T(2,128)S(1)} %add_convert_fusion.5.mark_ref, bf16[128,2560]{1,0:T(8,128)(2,1)} %bitcast.35, bf16[128,2560]{1,0:T(8,128)(2,1)} %bitcast.27, bf16[128,2560]{1,0:T(8,128)(2,1)} %bitcast.31), custom_call_target="tpu_custom_call" | custom-call | bytes 1310720 | tf_op jit(solution)/shard_map/pack_grads/pallas_call | solution.py:312
  3.1 2.6 %collective-permute-start.1 = (bf16[128,1408]{1,0:T(8,128)(2,1)S(1)}, bf16[128,1408]{1,0:T(8,128)(2,1)S(1)}, u32[]{:S(2)}, u32[]{:S(2)}) collective-permute-start(bf16[128,1408]{1,0:T(8,128)(2,1)S(1)} %get-tuple-element.33.refs_0_), channel_id=1, source_target_pairs={{0,8},{8,0},{16,24},{24,16},{1,9},{9,1},{17,25},{25,17},{2,10},{10... | collective-permute-start | bytes 1081352 | tf_op jit(solution)/shard_map/ppermute | solution.py:485
  5.7 1.5 %collective-permute-start.2 = (bf16[128,1408]{1,0:T(8,128)(2,1)S(1)}, bf16[128,1408]{1,0:T(8,128)(2,1)}, u32[]{:S(2)}, u32[]{:S(2)}) collective-permute-start(bf16[128,1408]{1,0:T(8,128)(2,1)S(1)} %get-tuple-element.34.refs_2_), channel_id=1, source_target_pairs={{0,16},{16,0},{8,24},{24,8},{1,17},{17,1},{9,25},{25,9},{2,18},{18... | collective-permute-start | bytes 1081352 | tf_op jit(solution)/shard_map/ppermute | solution.py:485
  7.3 1.5 %pack_ends.1 = (bf16[32,5248]{1,0:T(8,128)(2,1)}, bf16[32,5248]{1,0:T(8,128)(2,1)}) custom-call(s32[2]{0:T(128)S(1)} %add_select_fusion.first_ref, bf16[128,2560]{1,0:T(8,128)(2,1)S(1)} %bitcast.28, bf16[128,2560]{1,0:T(8,128)(2,1)S(1)} %bitcast.32, f32[1,128]{1,0:T(1,128)S(1)} %get-tuple-element.39.code_ref), custom_call_target="tpu_custom_call" | custom-call | bytes 1310720 | tf_op jit(solution)/shard_map/pack_ends/pallas_call | solution.py:245
  8.7 1.6 %collective-permute-start.3 = (bf16[32,5248]{1,0:T(8,128)(2,1)}, bf16[32,5248]{1,0:T(8,128)(2,1)}, u32[]{:S(2)}, u32[]{:S(2)}) collective-permute-start(bf16[32,5248]{1,0:T(8,128)(2,1)} %get-tuple-element.40), channel_id=1, source_target_pairs={{0,2},{2,0},{4,6},{6,4},{1,3},{3,1},{5,7},{7,5},{8,10},{10,8},{12,... | collective-permute-start | bytes 1007624 | tf_op jit(solution)/shard_map/ppermute | solution.py:32
  10.3 1.4 %collective-permute-start.4 = (bf16[32,5248]{1,0:T(8,128)(2,1)}, bf16[32,5248]{1,0:T(8,128)(2,1)}, u32[]{:S(2)}, u32[]{:S(2)}) collective-permute-start(bf16[32,5248]{1,0:T(8,128)(2,1)} %get-tuple-element.41), channel_id=1, source_target_pairs={{2,4},{4,2},{3,5},{5,3},{10,12},{12,10},{11,13},{13,11},{18,20},{2... | collective-permute-start | bytes 1007624 | tf_op jit(solution)/shard_map/ppermute | solution.py:32
  11.8 1.6 %attend_middle.1 = bf16[64,2560]{1,0:T(8,128)(2,1)S(1)} custom-call(bf16[128,2560]{1,0:T(8,128)(2,1)S(1)} %bitcast.36, bf16[128,2560]{1,0:T(8,128)(2,1)S(1)} %bitcast.29, bf16[128,2560]{1,0:T(8,128)(2,1)S(1)} %bitcast.33, f32[1,128]{1,0:T(1,128)S(1)} %get-tuple-element.39.code_ref), custom_call_target="tpu_custom_call" | custom-call | flops 268435456 | bytes 1966080 | tf_op jit(solution)/shard_map/attend_middle/pallas_call | solution.py:258
  13.5 1.2 %collective-permute-done.1.refs_1_ = bf16[128,1408]{1,0:T(8,128)(2,1)S(1)} collective-permute-done((bf16[128,1408]{1,0:T(8,128)(2,1)S(1)}, bf16[128,1408]{1,0:T(8,128)(2,1)S(1)}, u32[]{:S(2)}, u32[]{:S(2)}) %collective-permute-start.1) | collective-permute-done | bytes 360480 | tf_op jit(solution)/shard_map/ppermute | solution.py:485
  14.7 1.6 %collective-permute-done.2.refs_3_ = bf16[128,1408]{1,0:T(8,128)(2,1)} collective-permute-done((bf16[128,1408]{1,0:T(8,128)(2,1)S(1)}, bf16[128,1408]{1,0:T(8,128)(2,1)}, u32[]{:S(2)}, u32[]{:S(2)}) %collective-permute-start.2) | collective-permute-done | bytes 360480 | tf_op jit(solution)/shard_map/ppermute | solution.py:485
  16.3 1.9 %pair_sums.1 = (bf16[64,1280]{1,0:T(8,128)(2,1)S(1)}, bf16[64,1280]{1,0:T(8,128)(2,1)S(1)}, bf16[64,1280]{1,0:T(8,128)(2,1)S(1)}, bf16[64,1280]{1,0:T(8,128)(2,1)S(1)}) custom-call(f32[2]{0:T(128)S(1)} %add_convert_fusion.4.flag_ref, f32[1,2560]{1,0:T(1,128)S(1)} %broadcast_in_dim.17.gate_ref, bf16[128,1408]{1,0:T(8,128)(2,1)S(1)} %get-tuple-element.33.refs_0_, ...), custom_call_target="tpu_custom_call" | custom-call | flops 167772160 | bytes 1966080 | tf_op jit(solution)/shard_map/pair_sums/pallas_call | solution.py:362
  18.6 1.7 %collective-permute-start.10 = (bf16[64,1280]{1,0:T(8,128)(2,1)S(1)}, bf16[64,1280]{1,0:T(8,128)(2,1)S(1)}, u32[]{:S(2)}, u32[]{:S(2)}) collective-permute-start(bf16[64,1280]{1,0:T(8,128)(2,1)S(1)} %get-tuple-element.46), channel_id=1, source_target_pairs={{0,16},{16,24},{24,8},{8,0},{1,17},{17,25},{25,9},{9,1},{2,18},{18... | collective-permute-start | bytes 491528 | tf_op jit(solution)/shard_map/ppermute | solution.py:485
  20.3 3.7 %attend_edges.1 = bf16[64,2560]{1,0:T(8,128)(2,1)S(1)} custom-call(bf16[128,2560]{1,0:T(8,128)(2,1)S(1)} %bitcast.37, bf16[128,2560]{1,0:T(8,128)(2,1)S(1)} %bitcast.30, bf16[128,2560]{1,0:T(8,128)(2,1)S(1)} %bitcast.34, f32[1,128]{1,0:T(1,128)S(1)} %get-tuple-element.39.code_ref, bf16[32,5248]{1,0:T(8,128)(2,1)} %collective-permute-done.3.refs_0_, ...), custom_call_target="tpu_custom_call" | custom-call | flops 268435456 | bytes 1966080 | tf_op jit(solution)/shard_map/attend_edges/pallas_call | solution.py:273
  24.1 1.6 %collective-permute-start.6 = (bf16[64,1280]{1,0:T(8,128)(2,1)S(1)}, bf16[64,1280]{1,0:T(8,128)(2,1)S(1)}, u32[]{:S(2)}, u32[]{:S(2)}) collective-permute-start(bf16[64,1280]{1,0:T(8,128)(2,1)S(1)} %get-tuple-element.64), channel_id=1, source_target_pairs={{0,16},{16,24},{24,8},{8,0},{1,17},{17,25},{25,9},{9,1},{2,18},{18... | collective-permute-start | bytes 491528 | tf_op jit(solution)/shard_map/ppermute | solution.py:485
  26.8 1.7 %collective-permute-start.11 = (bf16[64,1280]{1,0:T(8,128)(2,1)S(1)}, bf16[64,1280]{1,0:T(8,128)(2,1)S(1)}, u32[]{:S(2)}, u32[]{:S(2)}) collective-permute-start(bf16[64,1280]{1,0:T(8,128)(2,1)S(1)} %get-tuple-element.60), channel_id=1, source_target_pairs={{0,16},{16,0},{8,24},{24,8},{1,17},{17,1},{9,25},{25,9},{2,18},{18... | collective-permute-start | bytes 491528 | tf_op jit(solution)/shard_map/ppermute | solution.py:485
  28.5 2.3 %collective-permute-done.6 = bf16[64,1280]{1,0:T(8,128)(2,1)S(1)} collective-permute-done((bf16[64,1280]{1,0:T(8,128)(2,1)S(1)}, bf16[64,1280]{1,0:T(8,128)(2,1)S(1)}, u32[]{:S(2)}, u32[]{:S(2)}) %collective-permute-start.6) | collective-permute-done | bytes 163872 | tf_op jit(solution)/shard_map/ppermute | solution.py:485
  30.8 1.5 %collective-permute-done.5 = bf16[64,1280]{1,0:T(8,128)(2,1)S(1)} collective-permute-done((bf16[64,1280]{1,0:T(8,128)(2,1)S(1)}, bf16[64,1280]{1,0:T(8,128)(2,1)S(1)}, u32[]{:S(2)}, u32[]{:S(2)}) %collective-permute-start.5) | collective-permute-done | bytes 163872 | tf_op jit(solution)/shard_map/ppermute | solution.py:485
  32.5 0.8 %collective-permute-start.8 = (bf16[64,1280]{1,0:T(8,128)(2,1)S(1)}, bf16[64,1280]{1,0:T(8,128)(2,1)S(1)}, u32[]{:S(2)}, u32[]{:S(2)}) collective-permute-start(bf16[64,1280]{1,0:T(8,128)(2,1)S(1)} %get-tuple-element.56), channel_id=1, source_target_pairs={{0,8},{8,0},{16,24},{24,16},{1,9},{9,1},{17,25},{25,17},{2,10},{10... | collective-permute-start | bytes 491528 | tf_op jit(solution)/shard_map/ppermute | solution.py:485
  33.6 1.9 %collective-permute-done.11 = bf16[64,1280]{1,0:T(8,128)(2,1)S(1)} collective-permute-done((bf16[64,1280]{1,0:T(8,128)(2,1)S(1)}, bf16[64,1280]{1,0:T(8,128)(2,1)S(1)}, u32[]{:S(2)}, u32[]{:S(2)}) %collective-permute-start.11) | collective-permute-done | bytes 163872 | tf_op jit(solution)/shard_map/ppermute | solution.py:485
  35.6 0.8 %relay.2 = (bf16[128,2560]{1,0:T(8,128)(2,1)}, f32[128,2560]{1,0:T(8,128)S(1)}) custom-call(f32[1,128]{1,0:T(1,128)S(1)} %get-tuple-element.81.row_ref, f32[1,2560]{1,0:T(1,128)S(1)} %broadcast_in_dim.17.gate_ref, bf16[64,1280]{1,0:T(8,128)(2,1)S(1)} %get-tuple-element.71.a_ref, bf16[64,1280]{1,0:T(8,128)(2,1)S(1)} %get-tuple-element.70.b_ref, ...), custom_call_target="tpu_custom_call" | custom-call | flops 83886080 | bytes 7864320 | tf_op jit(solution)/shard_map/relay/pallas_call | solution.py:443
  36.5 1.4 %collective-permute-done.8 = bf16[64,1280]{1,0:T(8,128)(2,1)S(1)} collective-permute-done((bf16[64,1280]{1,0:T(8,128)(2,1)S(1)}, bf16[64,1280]{1,0:T(8,128)(2,1)S(1)}, u32[]{:S(2)}, u32[]{:S(2)}) %collective-permute-start.8) | collective-permute-done | bytes 163872 | tf_op jit(solution)/shard_map/ppermute | solution.py:485
  37.9 0.7 %collective-permute-done.7 = bf16[64,1280]{1,0:T(8,128)(2,1)S(1)} collective-permute-done((bf16[64,1280]{1,0:T(8,128)(2,1)S(1)}, bf16[64,1280]{1,0:T(8,128)(2,1)S(1)}, u32[]{:S(2)}, u32[]{:S(2)}) %collective-permute-start.7) | collective-permute-done | bytes 163872 | tf_op jit(solution)/shard_map/ppermute | solution.py:485
  38.7 1.3 %relay.3 = (bf16[128,2560]{1,0:T(8,128)(2,1)}, bf16[128,2560]{1,0:T(8,128)(2,1)}) custom-call(f32[1,128]{1,0:T(1,128)S(1)} %get-tuple-element.81.row_ref, f32[1,2560]{1,0:T(1,128)S(1)} %broadcast_in_dim.17.gate_ref, bf16[64,1280]{1,0:T(8,128)(2,1)S(1)} %get-tuple-element.73.a_ref, ...), custom_call_target="tpu_custom_call", output_to_operand_aliasing={{0}: (7, {})} | custom-call | flops 83886080 | bytes 7864320 | tf_op jit(solution)/shard_map/relay/pallas_call | solution.py:443
  (33 shorter events, 2.6 us)
Async XLA Ops:
  0.6 12.8 %collective-permute-start = (f32[1280]{0:T(1024)}, f32[1280]{0:T(1024)S(1)}, u32[]{:S(2)}, u32[]{:S(2)}) collective-permute-start(f32[1280]{0:T(1024)} %param.12), channel_id=1, source_target_pairs={{0,1},{1,0},{2,3},{3,2},{4,5},{5,4},{6,7},{7,6},{8,9},{9,8},{10,11... | collective-permute-start | bytes 15368 | tf_op jit(solution)/shard_map/ppermute | solution.py:464
  1.9 5.4 %copy-start = (bf16[1,1,128,2560]{3,2,1,0:T(8,128)(2,1)S(1)}, bf16[1,1,128,2560]{3,2,1,0:T(8,128)(2,1)}, u32[]{:S(2)}) copy-start(bf16[1,1,128,2560]{3,2,1,0:T(8,128)(2,1)} %param.8) | copy-start | bytes 1966084
  1.9 5.4 %copy-start.1 = (bf16[1,1,128,2560]{3,2,1,0:T(8,128)(2,1)S(1)}, bf16[1,1,128,2560]{3,2,1,0:T(8,128)(2,1)}, u32[]{:S(2)}) copy-start(bf16[1,1,128,2560]{3,2,1,0:T(8,128)(2,1)} %param.9) | copy-start | bytes 1966084
  3.1 8.7 %copy-start.2 = (bf16[1,1,128,2560]{3,2,1,0:T(8,128)(2,1)S(1)}, bf16[1,1,128,2560]{3,2,1,0:T(8,128)(2,1)}, u32[]{:S(2)}) copy-start(bf16[1,1,128,2560]{3,2,1,0:T(8,128)(2,1)} %param.7) | copy-start | bytes 1966084
  3.1 11.6 %collective-permute-start.1 = (bf16[128,1408]{1,0:T(8,128)(2,1)S(1)}, bf16[128,1408]{1,0:T(8,128)(2,1)S(1)}, u32[]{:S(2)}, u32[]{:S(2)}) collective-permute-start(bf16[128,1408]{1,0:T(8,128)(2,1)S(1)} %get-tuple-element.33.refs_0_), channel_id=1, source_target_pairs={{0,8},{8,0},{16,24},{24,16},{1,9},{9,1},{17,25},{25,17},{2,10},{10... | collective-permute-start | bytes 1081352 | tf_op jit(solution)/shard_map/ppermute | solution.py:485
  5.7 10.6 %collective-permute-start.2 = (bf16[128,1408]{1,0:T(8,128)(2,1)S(1)}, bf16[128,1408]{1,0:T(8,128)(2,1)}, u32[]{:S(2)}, u32[]{:S(2)}) collective-permute-start(bf16[128,1408]{1,0:T(8,128)(2,1)S(1)} %get-tuple-element.34.refs_2_), channel_id=1, source_target_pairs={{0,16},{16,0},{8,24},{24,8},{1,17},{17,1},{9,25},{25,9},{2,18},{18... | collective-permute-start | bytes 1081352 | tf_op jit(solution)/shard_map/ppermute | solution.py:485
  8.7 4.7 %copy-start.3 = (f32[1280]{0:T(1024)S(1)}, f32[1280]{0:T(1024)}, u32[]{:S(2)}) copy-start(f32[1280]{0:T(1024)} %param.12) | copy-start | bytes 15364
  8.7 11.5 %collective-permute-start.3 = (bf16[32,5248]{1,0:T(8,128)(2,1)}, bf16[32,5248]{1,0:T(8,128)(2,1)}, u32[]{:S(2)}, u32[]{:S(2)}) collective-permute-start(bf16[32,5248]{1,0:T(8,128)(2,1)} %get-tuple-element.40), channel_id=1, source_target_pairs={{0,2},{2,0},{4,6},{6,4},{1,3},{3,1},{5,7},{7,5},{8,10},{10,8},{12,... | collective-permute-start | bytes 1007624 | tf_op jit(solution)/shard_map/ppermute | solution.py:32
  10.3 10.0 %collective-permute-start.4 = (bf16[32,5248]{1,0:T(8,128)(2,1)}, bf16[32,5248]{1,0:T(8,128)(2,1)}, u32[]{:S(2)}, u32[]{:S(2)}) collective-permute-start(bf16[32,5248]{1,0:T(8,128)(2,1)} %get-tuple-element.41), channel_id=1, source_target_pairs={{2,4},{4,2},{3,5},{5,3},{10,12},{12,10},{11,13},{13,11},{18,20},{2... | collective-permute-start | bytes 1007624 | tf_op jit(solution)/shard_map/ppermute | solution.py:32
  18.2 8.0 %collective-permute-start.9 = (bf16[64,1280]{1,0:T(8,128)(2,1)S(1)}, bf16[64,1280]{1,0:T(8,128)(2,1)S(1)}, u32[]{:S(2)}, u32[]{:S(2)}) collective-permute-start(bf16[64,1280]{1,0:T(8,128)(2,1)S(1)} %get-tuple-element.44), channel_id=1, source_target_pairs={{0,8},{8,24},{24,16},{16,0},{1,9},{9,25},{25,17},{17,1},{2,10},{10... | collective-permute-start | bytes 491528 | tf_op jit(solution)/shard_map/ppermute | solution.py:485
  18.6 7.6 %collective-permute-start.10 = (bf16[64,1280]{1,0:T(8,128)(2,1)S(1)}, bf16[64,1280]{1,0:T(8,128)(2,1)S(1)}, u32[]{:S(2)}, u32[]{:S(2)}) collective-permute-start(bf16[64,1280]{1,0:T(8,128)(2,1)S(1)} %get-tuple-element.46), channel_id=1, source_target_pairs={{0,16},{16,24},{24,8},{8,0},{1,17},{17,25},{25,9},{9,1},{2,18},{18... | collective-permute-start | bytes 491528 | tf_op jit(solution)/shard_map/ppermute | solution.py:485
  24.1 6.8 %collective-permute-start.6 = (bf16[64,1280]{1,0:T(8,128)(2,1)S(1)}, bf16[64,1280]{1,0:T(8,128)(2,1)S(1)}, u32[]{:S(2)}, u32[]{:S(2)}) collective-permute-start(bf16[64,1280]{1,0:T(8,128)(2,1)S(1)} %get-tuple-element.64), channel_id=1, source_target_pairs={{0,16},{16,24},{24,8},{8,0},{1,17},{17,25},{25,9},{9,1},{2,18},{18... | collective-permute-start | bytes 491528 | tf_op jit(solution)/shard_map/ppermute | solution.py:485
  25.6 6.7 %collective-permute-start.5 = (bf16[64,1280]{1,0:T(8,128)(2,1)S(1)}, bf16[64,1280]{1,0:T(8,128)(2,1)S(1)}, u32[]{:S(2)}, u32[]{:S(2)}) collective-permute-start(bf16[64,1280]{1,0:T(8,128)(2,1)S(1)} %get-tuple-element.65), channel_id=1, source_target_pairs={{0,8},{8,24},{24,16},{16,0},{1,9},{9,25},{25,17},{17,1},{2,10},{10... | collective-permute-start | bytes 491528 | tf_op jit(solution)/shard_map/ppermute | solution.py:485
  26.4 7.2 %collective-permute-start.12 = (bf16[64,1280]{1,0:T(8,128)(2,1)S(1)}, bf16[64,1280]{1,0:T(8,128)(2,1)S(1)}, u32[]{:S(2)}, u32[]{:S(2)}) collective-permute-start(bf16[64,1280]{1,0:T(8,128)(2,1)S(1)} %get-tuple-element.52), channel_id=1, source_target_pairs={{0,8},{8,0},{16,24},{24,16},{1,9},{9,1},{17,25},{25,17},{2,10},{10... | collective-permute-start | bytes 491528 | tf_op jit(solution)/shard_map/ppermute | solution.py:485
  26.8 8.8 %collective-permute-start.11 = (bf16[64,1280]{1,0:T(8,128)(2,1)S(1)}, bf16[64,1280]{1,0:T(8,128)(2,1)S(1)}, u32[]{:S(2)}, u32[]{:S(2)}) collective-permute-start(bf16[64,1280]{1,0:T(8,128)(2,1)S(1)} %get-tuple-element.60), channel_id=1, source_target_pairs={{0,16},{16,0},{8,24},{24,8},{1,17},{17,1},{9,25},{25,9},{2,18},{18... | collective-permute-start | bytes 491528 | tf_op jit(solution)/shard_map/ppermute | solution.py:485
  32.5 5.4 %collective-permute-start.8 = (bf16[64,1280]{1,0:T(8,128)(2,1)S(1)}, bf16[64,1280]{1,0:T(8,128)(2,1)S(1)}, u32[]{:S(2)}, u32[]{:S(2)}) collective-permute-start(bf16[64,1280]{1,0:T(8,128)(2,1)S(1)} %get-tuple-element.56), channel_id=1, source_target_pairs={{0,8},{8,0},{16,24},{24,16},{1,9},{9,1},{17,25},{25,17},{2,10},{10... | collective-permute-start | bytes 491528 | tf_op jit(solution)/shard_map/ppermute | solution.py:485
  33.3 5.3 %collective-permute-start.7 = (bf16[64,1280]{1,0:T(8,128)(2,1)S(1)}, bf16[64,1280]{1,0:T(8,128)(2,1)S(1)}, u32[]{:S(2)}, u32[]{:S(2)}) collective-permute-start(bf16[64,1280]{1,0:T(8,128)(2,1)S(1)} %get-tuple-element.62), channel_id=1, source_target_pairs={{0,16},{16,0},{8,24},{24,8},{1,17},{17,1},{9,25},{25,9},{2,18},{18... | collective-permute-start | bytes 491528 | tf_op jit(solution)/shard_map/ppermute | solution.py:485

commit v12 on v10

--- a/solution.py
+++ b/solution.py
@@ -162,59 +162,68 @@
         store_period(base, mixed_period(base, scores, sets, period), out_ref)
 
 
+def sides_kernel(reach, even_ref, q_ref, k_ref, v_ref, code_ref, one_ref, two_ref, *refs):
+    out_ref, keys, values, codes = refs
+    tokens, width = q_ref.shape
+    near = 2 * reach
+    code = columns(code_ref[...])
+    even = even_ref[0] == 1
+    period = math.lcm(DH, LANES)
+    masks = head_masks(reach, period)
+    blocks = []
+    for side, first in ((0, 0), (1, tokens - near)):
+        own = slice(first, first + near)
+        use_two = even if side == 0 else jnp.logical_not(even)
+        halo = jnp.where(use_two, two_ref[...], one_ref[...])
+        keys[side, :near] = k_ref[own]
+        values[side, :near] = v_ref[own]
+        codes[side, :near] = code[own]
+        keys[side, near : near + reach] = halo[:, :width]
+        values[side, near : near + reach] = halo[:, width : 2 * width]
+        codes[side, near : near + reach] = halo[:, 2 * width :].astype(jnp.float32)
+        spare = keys.shape[1] - near - reach
+        if spare:
+            for ref in (keys, values, codes):
+                ref[side, near + reach :] = jnp.zeros((spare, ref.shape[2]), ref.dtype)
+        top = side * (tokens - reach)
+        blocks.append((side, top, link_bias(code[top : top + reach], codes[side])))
+    for base in range(0, width, period):
+        scores = []
+        for side, top, bias in blocks:
+            query = lambda lanes: q_ref[top : top + reach, lanes]
+            key = lambda lanes: keys[side, :, lanes]
+            scores.append(period_scores(base, query, [key], masks, period))
+        for (side, top, bias), part in zip(blocks, scores):
+            sets = [(bias, lambda lanes: values[side, :, lanes])]
+            tiles = mixed_period(base, part, sets, period)
+            store_period(base, tiles, out_ref.at[side * reach : (side + 1) * reach])
+
+
 def edge_kernel(reach, q_ref, k_ref, v_ref, code_ref, *refs):
-    halos = refs[:-6]
-    out_ref, keys, values, codes, near, sems = refs[-6:]
-    tokens, width = q_ref.shape
-    copies = []
+    halos = refs[:-4]
+    out_ref, keys, values, codes = refs[-4:]
+    width = q_ref.shape[1]
+    code = columns(code_ref[...])
     at = 0
-    for n, piece in enumerate(halos):
+    for piece in halos:
         rows = piece.shape[0]
-        for m, (ref, size) in enumerate(((keys, width), (values, width), (codes, LANES))):
-            copies.append(
-                pltpu.make_async_copy(
-                    piece.at[:, pl.ds(m * width, size)], ref.at[pl.ds(at, rows)], sems.at[n, m]
-                )
-            )
+        keys[at : at + rows] = piece[:, :width]
+        values[at : at + rows] = piece[:, width : 2 * width]
+        codes[at : at + rows] = piece[:, 2 * width :].astype(jnp.float32)
         at += rows
-    for copy in copies:
-        copy.start()
     if at < keys.shape[0]:
         for ref in (keys, values, codes):
             ref[at:] = jnp.zeros((ref.shape[0] - at, ref.shape[1]), ref.dtype)
-    code = columns(code_ref[...])
-    if tokens > 2 * reach:
-        last = tokens - reach
-        mine = jnp.concatenate((code[:reach], code[last:]), axis=0)
-        query = lambda lanes: jnp.concatenate((q_ref[:reach, lanes], q_ref[last:, lanes]), axis=0)
-    else:
-        mine = code
-        query = lambda lanes: q_ref[:, lanes]
     period = math.lcm(DH, LANES)
-    rows = out_ref.shape[0]
-    masks = head_masks(rows, period)
-    place = {}
-    at = 0
-    for base in range(0, width, period):
-        scores = period_scores(base, query, [lambda lanes: k_ref[:, lanes]], masks, period)
-        place[base] = []
-        for (part,) in scores:
-            near[at : at + part.shape[0]] = part
-            place[base].append((at, part.shape[0]))
-            at += part.shape[0]
-    own_bias = link_bias(mine, code)
-    for copy in copies:
-        copy.wait()
+    masks = head_masks(q_ref.shape[0], period)
+    query = lambda lanes: q_ref[:, lanes]
+    pair = [lambda lanes: k_ref[:, lanes], lambda lanes: keys[:, lanes]]
     sets = [
-        (own_bias, lambda lanes: v_ref[:, lanes]),
-        (link_bias(mine, codes[...].astype(jnp.float32)), lambda lanes: values[:, lanes]),
+        (link_bias(code, code), lambda lanes: v_ref[:, lanes]),
+        (link_bias(code, codes[...]), lambda lanes: values[:, lanes]),
     ]
     for base in range(0, width, period):
-        scores = period_scores(base, query, [lambda lanes: keys[:, lanes]], masks, period)
-        scores = [
-            [near[first : first + size], *parts]
-            for (first, size), parts in zip(place[base], scores)
-        ]
+        scores = period_scores(base, query, pair, masks, period)
         store_period(base, mixed_period(base, scores, sets, period), out_ref)
 
 
@@ -258,26 +267,29 @@
     )(queries, keys, values, code)
 
 
-def attend_edges(queries, keys, values, code, halos, reach):
+def attend_edges(even, queries, keys, values, code, halos, reach):
     tokens, width = queries.shape
     rows = min(tokens, 2 * reach)
-    held = -(-2 * reach // LANES) * LANES
+    if tokens > 2 * reach:
+        kernel, operands = sides_kernel, [even, queries, keys, values, code, *halos]
+        held = (2, -(-3 * reach // LANES) * LANES)
+    else:
+        kernel, operands = edge_kernel, [queries, keys, values, code, *halos]
+        held = (-(-2 * reach // LANES) * LANES,)
     return pl.pallas_call(
-        functools.partial(edge_kernel, reach),
-        in_specs=[VMEM] * 4 + [pl.BlockSpec(memory_space=pltpu.HBM)] * len(halos),
+        functools.partial(kernel, reach),
+        in_specs=[SMEM if operand is even else VMEM for operand in operands],
         out_specs=VMEM,
         out_shape=jax.ShapeDtypeStruct((rows, width), jnp.bfloat16),
         scratch_shapes=[
-            pltpu.VMEM((held, width), jnp.bfloat16),
-            pltpu.VMEM((held, width), jnp.bfloat16),
-            pltpu.VMEM((held, LANES), jnp.bfloat16),
-            pltpu.VMEM((rows * (width // DH), tokens), jnp.float32),
-            pltpu.SemaphoreType.DMA((len(halos), 3)),
+            pltpu.VMEM((*held, width), jnp.bfloat16),
+            pltpu.VMEM((*held, width), jnp.bfloat16),
+            pltpu.VMEM((*held, LANES), jnp.float32),
         ],
         compiler_params=PARAMS,
         cost_estimate=attend_cost(rows, LANES, width),
         name="attend_edges",
-    )(queries, keys, values, code, *halos)
+    )(*operands)
 
 
 def pack_grads_kernel(grad_ref, mark_ref, *refs):
@@ -406,7 +418,7 @@
 
 def relay(rows, gate, branch, base, totals, spots, first_row, grads, last):
     tokens, width = base.shape
-    chunks = width // 2 // (2 * LANES) if width // 2 % (2 * LANES) == 0 else 1
+    chunks = 2 if width // 2 % (2 * LANES) == 0 else 1
     far = pl.BlockSpec(memory_space=pltpu.HBM)
     whole = jax.ShapeDtypeStruct((tokens, width), jnp.bfloat16)
 
@@ -505,7 +517,7 @@
     sums = ready[: 2 * count]
     if going:
         going = [ready[2 * count :]]
-    own.append(attend_edges(queries, keys, values, code, halos, reach))
+    own.append(attend_edges(even.astype(jnp.int32)[None], queries, keys, values, code, halos, reach))
 
     going.append(outgoing(own[-1], sums[count - 1], sums[2 * count - 1]))
     spots = [piece_spots(tokens, reach, n) for n in range(count)]

time: 40.5 us -> 39.9 us (0.985)
  Pallas kernels: 11.4 us -> 10.8 us
    pallas_call x1, Pallas kernels: 3.59 us -> 3.04 us  [attend_edges(): pl.pallas_call(functools.partial(kernel, reach), in_specs=[SMEM if operan...]
  transfers between devices with their start and end apart: 13 -> 13, of which waited for: 7 -> 7; matrix products, arithmetic and copies ran while one was open for 4% -> 4% of each run, Pallas kernels for 25% -> 24%
where the time goes in v12:
time: 39.9 us; the launch traced here: 39.7 us
  starting transfers between devices  15.8 us (40%)
  Pallas kernels  10.8 us (27%)
  waiting for transfers between devices  10.6 us (27%)
  other arithmetic  1.51 us (4%)
  between operations  0.86 us (2%)
    ppermute x10, starting transfers between devices, local(): send = lambda block, route: lax.ppermute(block, 'grp', route)  10.7 us
    ppermute x10, waiting for transfers between devices, local(): send = lambda block, route: lax.ppermute(block, 'grp', route)  8.61 us
    ppermute x2, starting transfers between devices, paired(): return lax.ppermute(block, axis, route)  5.05 us
    pallas_call x1, Pallas kernels, attend_edges(): pl.pallas_call(functools.partial(kernel, reach), in_specs=[SMEM if operan...  3.04 us
    pallas_call x2, Pallas kernels, relay(): pl.pallas_call(kernel, in_specs=[VMEM] * 7 + ([] if grads is None else [f...  2.12 us
    ppermute x2, waiting for transfers between devices, paired(): return lax.ppermute(block, axis, route)  1.98 us
    pallas_call x1, Pallas kernels, attend_middle(): pl.pallas_call(functools.partial(middle_kernel, reach), in_specs=[VMEM] *...  1.61 us
    pallas_call x1, Pallas kernels, pack_ends(): pl.pallas_call(ends_kernel, in_specs=[SMEM] + [VMEM] * 3, out_specs=[VMEM...  1.48 us
  transfers between devices with their start and end apart: 13, of which 7 were waited for; matrix products, arithmetic and copies ran while one was open for 4% of the time, Pallas kernels for 24%

profile of v12, /device:TPU:8, one launch (start us, length us, event | category | flops | bytes accessed | tf_op | source)
XLA Modules:
  0.0 39.7 jit_solution(16594256232669371976)
XLA Ops:
  0.7 0.7 %and_select_fusion = (s32[1,128]{1,0:T(1,128)S(1)}, s32[1,128]{1,0:T(1,128)S(1)}) fusion(s32[1,1,128]{2,1,0:T(1,128)} %param.11, s32[1,1,128]{2,1,0:T(1,128)} %param.10), kind=kLoop, calls=%fused_computation.32 | loop fusion | flops 2816 | bytes 2048 | tf_op jit(solution)/shard_map/jit(remainder)/select_n | solution.py:487
  1.4 1.2 %pack_grads.1 = (bf16[128,1408]{1,0:T(8,128)(2,1)S(1)}, bf16[128,1408]{1,0:T(8,128)(2,1)S(1)}) custom-call(bf16[128,2560]{1,0:T(8,128)(2,1)} %bitcast.38, f32[2,128]{1,0:T(2,128)S(1)} %add_convert_fusion.5.mark_ref, bf16[128,2560]{1,0:T(8,128)(2,1)} %bitcast.35, bf16[128,2560]{1,0:T(8,128)(2,1)} %bitcast.27, bf16[128,2560]{1,0:T(8,128)(2,1)} %bitcast.31), custom_call_target="tpu_custom_call" | custom-call | bytes 1310720 | tf_op jit(solution)/shard_map/pack_grads/pallas_call | solution.py:317
  2.7 1.6 %collective-permute-start.1 = (bf16[128,1408]{1,0:T(8,128)(2,1)S(1)}, bf16[128,1408]{1,0:T(8,128)(2,1)S(1)}, u32[]{:S(2)}, u32[]{:S(2)}) collective-permute-start(bf16[128,1408]{1,0:T(8,128)(2,1)S(1)} %get-tuple-element.33.refs_0_), channel_id=1, source_target_pairs={{0,8},{8,0},{16,24},{24,16},{1,9},{9,1},{17,25},{25,17},{2,10},{10... | collective-permute-start | bytes 1081352 | tf_op jit(solution)/shard_map/ppermute | solution.py:483
  4.2 1.5 %collective-permute-start.2 = (bf16[128,1408]{1,0:T(8,128)(2,1)S(1)}, bf16[128,1408]{1,0:T(8,128)(2,1)}, u32[]{:S(2)}, u32[]{:S(2)}) collective-permute-start(bf16[128,1408]{1,0:T(8,128)(2,1)S(1)} %get-tuple-element.34.refs_2_), channel_id=1, source_target_pairs={{0,16},{16,0},{8,24},{24,8},{1,17},{17,1},{9,25},{25,9},{2,18},{18... | collective-permute-start | bytes 1081352 | tf_op jit(solution)/shard_map/ppermute | solution.py:483
  5.8 1.5 %pack_ends.1 = (bf16[32,5248]{1,0:T(8,128)(2,1)}, bf16[32,5248]{1,0:T(8,128)(2,1)}) custom-call(s32[2]{0:T(128)S(1)} %add_select_fusion.first_ref, bf16[128,2560]{1,0:T(8,128)(2,1)S(1)} %bitcast.28, bf16[128,2560]{1,0:T(8,128)(2,1)S(1)} %bitcast.32, f32[1,128]{1,0:T(1,128)S(1)} %get-tuple-element.39.code_ref), custom_call_target="tpu_custom_call" | custom-call | bytes 1310720 | tf_op jit(solution)/shard_map/pack_ends/pallas_call | solution.py:246
  7.8 4.6 %collective-permute-start.4 = (bf16[32,5248]{1,0:T(8,128)(2,1)}, bf16[32,5248]{1,0:T(8,128)(2,1)}, u32[]{:S(2)}, u32[]{:S(2)}) collective-permute-start(bf16[32,5248]{1,0:T(8,128)(2,1)} %get-tuple-element.41), channel_id=1, source_target_pairs={{2,4},{4,2},{3,5},{5,3},{10,12},{12,10},{11,13},{13,11},{18,20},{2... | collective-permute-start | bytes 1007624 | tf_op jit(solution)/shard_map/ppermute | solution.py:32
  12.4 1.6 %attend_middle.1 = bf16[64,2560]{1,0:T(8,128)(2,1)S(1)} custom-call(bf16[128,2560]{1,0:T(8,128)(2,1)S(1)} %bitcast.36, bf16[128,2560]{1,0:T(8,128)(2,1)S(1)} %bitcast.29, bf16[128,2560]{1,0:T(8,128)(2,1)S(1)} %bitcast.33, f32[1,128]{1,0:T(1,128)S(1)} %get-tuple-element.39.code_ref), custom_call_target="tpu_custom_call" | custom-call | flops 268435456 | bytes 1966080 | tf_op jit(solution)/shard_map/attend_middle/pallas_call | solution.py:259
  14.2 0.7 %collective-permute-done.2.refs_3_ = bf16[128,1408]{1,0:T(8,128)(2,1)} collective-permute-done((bf16[128,1408]{1,0:T(8,128)(2,1)S(1)}, bf16[128,1408]{1,0:T(8,128)(2,1)}, u32[]{:S(2)}, u32[]{:S(2)}) %collective-permute-start.2) | collective-permute-done | bytes 360480 | tf_op jit(solution)/shard_map/ppermute | solution.py:483
  14.9 1.4 %pair_sums.1 = (bf16[64,1280]{1,0:T(8,128)(2,1)S(1)}, bf16[64,1280]{1,0:T(8,128)(2,1)S(1)}, bf16[64,1280]{1,0:T(8,128)(2,1)S(1)}, bf16[64,1280]{1,0:T(8,128)(2,1)S(1)}) custom-call(f32[2]{0:T(128)S(1)} %add_convert_fusion.4.flag_ref, f32[1,2560]{1,0:T(1,128)S(1)} %broadcast_in_dim.22.gate_ref, bf16[128,1408]{1,0:T(8,128)(2,1)S(1)} %get-tuple-element.33.refs_0_, ...), custom_call_target="tpu_custom_call" | custom-call | flops 167772160 | bytes 1966080 | tf_op jit(solution)/shard_map/pair_sums/pallas_call | solution.py:361
  16.3 0.6 %collective-permute-start.9 = (bf16[64,1280]{1,0:T(8,128)(2,1)S(1)}, bf16[64,1280]{1,0:T(8,128)(2,1)S(1)}, u32[]{:S(2)}, u32[]{:S(2)}) collective-permute-start(bf16[64,1280]{1,0:T(8,128)(2,1)S(1)} %get-tuple-element.44), channel_id=1, source_target_pairs={{0,8},{8,24},{24,16},{16,0},{1,9},{9,25},{25,17},{17,1},{2,10},{10... | collective-permute-start | bytes 491528 | tf_op jit(solution)/shard_map/ppermute | solution.py:483
  16.9 1.5 %collective-permute-start.10 = (bf16[64,1280]{1,0:T(8,128)(2,1)S(1)}, bf16[64,1280]{1,0:T(8,128)(2,1)S(1)}, u32[]{:S(2)}, u32[]{:S(2)}) collective-permute-start(bf16[64,1280]{1,0:T(8,128)(2,1)S(1)} %get-tuple-element.46), channel_id=1, source_target_pairs={{0,16},{16,24},{24,8},{8,0},{1,17},{17,25},{25,9},{9,1},{2,18},{18... | collective-permute-start | bytes 491528 | tf_op jit(solution)/shard_map/ppermute | solution.py:483
  18.4 2.0 %collective-permute-done.4.two_ref = bf16[32,5248]{1,0:T(8,128)(2,1)} collective-permute-done((bf16[32,5248]{1,0:T(8,128)(2,1)}, bf16[32,5248]{1,0:T(8,128)(2,1)}, u32[]{:S(2)}, u32[]{:S(2)}) %collective-permute-start.4) | collective-permute-done | bytes 335904 | tf_op jit(solution)/shard_map/ppermute | solution.py:32
  20.4 3.0 %attend_edges.1 = bf16[64,2560]{1,0:T(8,128)(2,1)S(1)} custom-call(s32[1]{0:T(128)S(6)} %broadcast_in_dim.24.even_ref, bf16[128,2560]{1,0:T(8,128)(2,1)S(1)} %bitcast.37, bf16[128,2560]{1,0:T(8,128)(2,1)S(1)} %bitcast.30, bf16[128,2560]{1,0:T(8,128)(2,1)S(1)} %bitcast.34, f32[1,128]{1,0:T(1,128)S(1)} %get-tuple-element.39.code_ref, ...), custom_call_target="tpu_custom_call" | custom-call | flops 268435456 | bytes 1966080 | tf_op jit(solution)/shard_map/attend_edges/pallas_call | solution.py:279
  23.5 0.6 %collective-permute-start.6 = (bf16[64,1280]{1,0:T(8,128)(2,1)S(1)}, bf16[64,1280]{1,0:T(8,128)(2,1)S(1)}, u32[]{:S(2)}, u32[]{:S(2)}) collective-permute-start(bf16[64,1280]{1,0:T(8,128)(2,1)S(1)} %get-tuple-element.64), channel_id=1, source_target_pairs={{0,16},{16,24},{24,8},{8,0},{1,17},{17,25},{25,9},{9,1},{2,18},{18... | collective-permute-start | bytes 491528 | tf_op jit(solution)/shard_map/ppermute | solution.py:483
  24.1 1.5 %collective-permute-start.5 = (bf16[64,1280]{1,0:T(8,128)(2,1)S(1)}, bf16[64,1280]{1,0:T(8,128)(2,1)S(1)}, u32[]{:S(2)}, u32[]{:S(2)}) collective-permute-start(bf16[64,1280]{1,0:T(8,128)(2,1)S(1)} %get-tuple-element.65), channel_id=1, source_target_pairs={{0,8},{8,24},{24,16},{16,0},{1,9},{9,25},{25,17},{17,1},{2,10},{10... | collective-permute-start | bytes 491528 | tf_op jit(solution)/shard_map/ppermute | solution.py:483
  25.8 0.6 %collective-permute-start.12 = (bf16[64,1280]{1,0:T(8,128)(2,1)S(1)}, bf16[64,1280]{1,0:T(8,128)(2,1)S(1)}, u32[]{:S(2)}, u32[]{:S(2)}) collective-permute-start(bf16[64,1280]{1,0:T(8,128)(2,1)S(1)} %get-tuple-element.52), channel_id=1, source_target_pairs={{0,8},{8,0},{16,24},{24,16},{1,9},{9,1},{17,25},{25,17},{2,10},{10... | collective-permute-start | bytes 491528 | tf_op jit(solution)/shard_map/ppermute | solution.py:483
  26.4 0.5 %collective-permute-start.11 = (bf16[64,1280]{1,0:T(8,128)(2,1)S(1)}, bf16[64,1280]{1,0:T(8,128)(2,1)S(1)}, u32[]{:S(2)}, u32[]{:S(2)}) collective-permute-start(bf16[64,1280]{1,0:T(8,128)(2,1)S(1)} %get-tuple-element.60), channel_id=1, source_target_pairs={{0,16},{16,0},{8,24},{24,8},{1,17},{17,1},{9,25},{25,9},{2,18},{18... | collective-permute-start | bytes 491528 | tf_op jit(solution)/shard_map/ppermute | solution.py:483
  26.9 3.7 %collective-permute-done.6 = bf16[64,1280]{1,0:T(8,128)(2,1)S(1)} collective-permute-done((bf16[64,1280]{1,0:T(8,128)(2,1)S(1)}, bf16[64,1280]{1,0:T(8,128)(2,1)S(1)}, u32[]{:S(2)}, u32[]{:S(2)}) %collective-permute-start.6) | collective-permute-done | bytes 163872 | tf_op jit(solution)/shard_map/ppermute | solution.py:483
  31.0 2.0 %collective-permute-start.8 = (bf16[64,1280]{1,0:T(8,128)(2,1)S(1)}, bf16[64,1280]{1,0:T(8,128)(2,1)S(1)}, u32[]{:S(2)}, u32[]{:S(2)}) collective-permute-start(bf16[64,1280]{1,0:T(8,128)(2,1)S(1)} %get-tuple-element.56), channel_id=1, source_target_pairs={{0,8},{8,0},{16,24},{24,16},{1,9},{9,1},{17,25},{25,17},{2,10},{10... | collective-permute-start | bytes 491528 | tf_op jit(solution)/shard_map/ppermute | solution.py:483
  33.3 0.7 %collective-permute-done.12 = bf16[64,1280]{1,0:T(8,128)(2,1)S(1)} collective-permute-done((bf16[64,1280]{1,0:T(8,128)(2,1)S(1)}, bf16[64,1280]{1,0:T(8,128)(2,1)S(1)}, u32[]{:S(2)}, u32[]{:S(2)}) %collective-permute-start.12) | collective-permute-done | bytes 163872 | tf_op jit(solution)/shard_map/ppermute | solution.py:483
  34.1 0.8 %relay.2 = (bf16[128,2560]{1,0:T(8,128)(2,1)}, f32[128,2560]{1,0:T(8,128)S(1)}) custom-call(f32[1,128]{1,0:T(1,128)S(1)} %get-tuple-element.81.row_ref, f32[1,2560]{1,0:T(1,128)S(1)} %broadcast_in_dim.22.gate_ref, bf16[64,1280]{1,0:T(8,128)(2,1)S(1)} %get-tuple-element.71.a_ref, bf16[64,1280]{1,0:T(8,128)(2,1)S(1)} %get-tuple-element.70.b_ref, ...), custom_call_target="tpu_custom_call" | custom-call | flops 83886080 | bytes 7864320 | tf_op jit(solution)/shard_map/relay/pallas_call | solution.py:441
  35.0 1.4 %collective-permute-done.8 = bf16[64,1280]{1,0:T(8,128)(2,1)S(1)} collective-permute-done((bf16[64,1280]{1,0:T(8,128)(2,1)S(1)}, bf16[64,1280]{1,0:T(8,128)(2,1)S(1)}, u32[]{:S(2)}, u32[]{:S(2)}) %collective-permute-start.8) | collective-permute-done | bytes 163872 | tf_op jit(solution)/shard_map/ppermute | solution.py:483
  36.3 1.9 %collective-permute-done.7 = bf16[64,1280]{1,0:T(8,128)(2,1)S(1)} collective-permute-done((bf16[64,1280]{1,0:T(8,128)(2,1)S(1)}, bf16[64,1280]{1,0:T(8,128)(2,1)S(1)}, u32[]{:S(2)}, u32[]{:S(2)}) %collective-permute-start.7) | collective-permute-done | bytes 163872 | tf_op jit(solution)/shard_map/ppermute | solution.py:483
  38.4 1.3 %relay.3 = (bf16[128,2560]{1,0:T(8,128)(2,1)}, bf16[128,2560]{1,0:T(8,128)(2,1)}) custom-call(f32[1,128]{1,0:T(1,128)S(1)} %get-tuple-element.81.row_ref, f32[1,2560]{1,0:T(1,128)S(1)} %broadcast_in_dim.22.gate_ref, bf16[64,1280]{1,0:T(8,128)(2,1)S(1)} %get-tuple-element.73.a_ref, ...), custom_call_target="tpu_custom_call", output_to_operand_aliasing={{0}: (7, {})} | custom-call | flops 83886080 | bytes 7864320 | tf_op jit(solution)/shard_map/relay/pallas_call | solution.py:441
  (33 shorter events, 1.9 us)
Async XLA Ops:
  0.6 13.5 %collective-permute-start = (f32[1280]{0:T(1024)}, f32[1280]{0:T(1024)S(1)}, u32[]{:S(2)}, u32[]{:S(2)}) collective-permute-start(f32[1280]{0:T(1024)} %param.12), channel_id=1, source_target_pairs={{0,1},{1,0},{2,3},{3,2},{4,5},{5,4},{6,7},{7,6},{8,9},{9,8},{10,11... | collective-permute-start | bytes 15368 | tf_op jit(solution)/shard_map/ppermute | solution.py:462
  1.4 4.4 %copy-start = (bf16[1,1,128,2560]{3,2,1,0:T(8,128)(2,1)S(1)}, bf16[1,1,128,2560]{3,2,1,0:T(8,128)(2,1)}, u32[]{:S(2)}) copy-start(bf16[1,1,128,2560]{3,2,1,0:T(8,128)(2,1)} %param.8) | copy-start | bytes 1966084
  1.4 4.4 %copy-start.1 = (bf16[1,1,128,2560]{3,2,1,0:T(8,128)(2,1)S(1)}, bf16[1,1,128,2560]{3,2,1,0:T(8,128)(2,1)}, u32[]{:S(2)}) copy-start(bf16[1,1,128,2560]{3,2,1,0:T(8,128)(2,1)} %param.9) | copy-start | bytes 1966084
  2.6 9.8 %copy-start.2 = (bf16[1,1,128,2560]{3,2,1,0:T(8,128)(2,1)S(1)}, bf16[1,1,128,2560]{3,2,1,0:T(8,128)(2,1)}, u32[]{:S(2)}) copy-start(bf16[1,1,128,2560]{3,2,1,0:T(8,128)(2,1)} %param.7) | copy-start | bytes 1966084
  2.7 11.5 %collective-permute-start.1 = (bf16[128,1408]{1,0:T(8,128)(2,1)S(1)}, bf16[128,1408]{1,0:T(8,128)(2,1)S(1)}, u32[]{:S(2)}, u32[]{:S(2)}) collective-permute-start(bf16[128,1408]{1,0:T(8,128)(2,1)S(1)} %get-tuple-element.33.refs_0_), channel_id=1, source_target_pairs={{0,8},{8,0},{16,24},{24,16},{1,9},{9,1},{17,25},{25,17},{2,10},{10... | collective-permute-start | bytes 1081352 | tf_op jit(solution)/shard_map/ppermute | solution.py:483
  4.2 10.6 %collective-permute-start.2 = (bf16[128,1408]{1,0:T(8,128)(2,1)S(1)}, bf16[128,1408]{1,0:T(8,128)(2,1)}, u32[]{:S(2)}, u32[]{:S(2)}) collective-permute-start(bf16[128,1408]{1,0:T(8,128)(2,1)S(1)} %get-tuple-element.34.refs_2_), channel_id=1, source_target_pairs={{0,16},{16,0},{8,24},{24,8},{1,17},{17,1},{9,25},{25,9},{2,18},{18... | collective-permute-start | bytes 1081352 | tf_op jit(solution)/shard_map/ppermute | solution.py:483
  7.3 6.8 %copy-start.3 = (f32[1280]{0:T(1024)S(1)}, f32[1280]{0:T(1024)}, u32[]{:S(2)}) copy-start(f32[1280]{0:T(1024)} %param.12) | copy-start | bytes 15364
  7.3 11.1 %collective-permute-start.3 = (bf16[32,5248]{1,0:T(8,128)(2,1)}, bf16[32,5248]{1,0:T(8,128)(2,1)}, u32[]{:S(2)}, u32[]{:S(2)}) collective-permute-start(bf16[32,5248]{1,0:T(8,128)(2,1)} %get-tuple-element.40), channel_id=1, source_target_pairs={{0,2},{2,0},{4,6},{6,4},{1,3},{3,1},{5,7},{7,5},{8,10},{10,8},{12,... | collective-permute-start | bytes 1007624 | tf_op jit(solution)/shard_map/ppermute | solution.py:32
  7.8 12.6 %collective-permute-start.4 = (bf16[32,5248]{1,0:T(8,128)(2,1)}, bf16[32,5248]{1,0:T(8,128)(2,1)}, u32[]{:S(2)}, u32[]{:S(2)}) collective-permute-start(bf16[32,5248]{1,0:T(8,128)(2,1)} %get-tuple-element.41), channel_id=1, source_target_pairs={{2,4},{4,2},{3,5},{5,3},{10,12},{12,10},{11,13},{13,11},{18,20},{2... | collective-permute-start | bytes 1007624 | tf_op jit(solution)/shard_map/ppermute | solution.py:32
  16.3 9.3 %collective-permute-start.9 = (bf16[64,1280]{1,0:T(8,128)(2,1)S(1)}, bf16[64,1280]{1,0:T(8,128)(2,1)S(1)}, u32[]{:S(2)}, u32[]{:S(2)}) collective-permute-start(bf16[64,1280]{1,0:T(8,128)(2,1)S(1)} %get-tuple-element.44), channel_id=1, source_target_pairs={{0,8},{8,24},{24,16},{16,0},{1,9},{9,25},{25,17},{17,1},{2,10},{10... | collective-permute-start | bytes 491528 | tf_op jit(solution)/shard_map/ppermute | solution.py:483
  16.9 8.7 %collective-permute-start.10 = (bf16[64,1280]{1,0:T(8,128)(2,1)S(1)}, bf16[64,1280]{1,0:T(8,128)(2,1)S(1)}, u32[]{:S(2)}, u32[]{:S(2)}) collective-permute-start(bf16[64,1280]{1,0:T(8,128)(2,1)S(1)} %get-tuple-element.46), channel_id=1, source_target_pairs={{0,16},{16,24},{24,8},{8,0},{1,17},{17,25},{25,9},{9,1},{2,18},{18... | collective-permute-start | bytes 491528 | tf_op jit(solution)/shard_map/ppermute | solution.py:483
  23.5 7.1 %collective-permute-start.6 = (bf16[64,1280]{1,0:T(8,128)(2,1)S(1)}, bf16[64,1280]{1,0:T(8,128)(2,1)S(1)}, u32[]{:S(2)}, u32[]{:S(2)}) collective-permute-start(bf16[64,1280]{1,0:T(8,128)(2,1)S(1)} %get-tuple-element.64), channel_id=1, source_target_pairs={{0,16},{16,24},{24,8},{8,0},{1,17},{17,25},{25,9},{9,1},{2,18},{18... | collective-permute-start | bytes 491528 | tf_op jit(solution)/shard_map/ppermute | solution.py:483
  24.1 6.7 %collective-permute-start.5 = (bf16[64,1280]{1,0:T(8,128)(2,1)S(1)}, bf16[64,1280]{1,0:T(8,128)(2,1)S(1)}, u32[]{:S(2)}, u32[]{:S(2)}) collective-permute-start(bf16[64,1280]{1,0:T(8,128)(2,1)S(1)} %get-tuple-element.65), channel_id=1, source_target_pairs={{0,8},{8,24},{24,16},{16,0},{1,9},{9,25},{25,17},{17,1},{2,10},{10... | collective-permute-start | bytes 491528 | tf_op jit(solution)/shard_map/ppermute | solution.py:483
  25.8 8.2 %collective-permute-start.12 = (bf16[64,1280]{1,0:T(8,128)(2,1)S(1)}, bf16[64,1280]{1,0:T(8,128)(2,1)S(1)}, u32[]{:S(2)}, u32[]{:S(2)}) collective-permute-start(bf16[64,1280]{1,0:T(8,128)(2,1)S(1)} %get-tuple-element.52), channel_id=1, source_target_pairs={{0,8},{8,0},{16,24},{24,16},{1,9},{9,1},{17,25},{25,17},{2,10},{10... | collective-permute-start | bytes 491528 | tf_op jit(solution)/shard_map/ppermute | solution.py:483
  26.4 7.6 %collective-permute-start.11 = (bf16[64,1280]{1,0:T(8,128)(2,1)S(1)}, bf16[64,1280]{1,0:T(8,128)(2,1)S(1)}, u32[]{:S(2)}, u32[]{:S(2)}) collective-permute-start(bf16[64,1280]{1,0:T(8,128)(2,1)S(1)} %get-tuple-element.60), channel_id=1, source_target_pairs={{0,16},{16,0},{8,24},{24,8},{1,17},{17,1},{9,25},{25,9},{2,18},{18... | collective-permute-start | bytes 491528 | tf_op jit(solution)/shard_map/ppermute | solution.py:483
  31.0 5.4 %collective-permute-start.8 = (bf16[64,1280]{1,0:T(8,128)(2,1)S(1)}, bf16[64,1280]{1,0:T(8,128)(2,1)S(1)}, u32[]{:S(2)}, u32[]{:S(2)}) collective-permute-start(bf16[64,1280]{1,0:T(8,128)(2,1)S(1)} %get-tuple-element.56), channel_id=1, source_target_pairs={{0,8},{8,0},{16,24},{24,16},{1,9},{9,1},{17,25},{25,17},{2,10},{10... | collective-permute-start | bytes 491528 | tf_op jit(solution)/shard_map/ppermute | solution.py:483
  33.0 5.3 %collective-permute-start.7 = (bf16[64,1280]{1,0:T(8,128)(2,1)S(1)}, bf16[64,1280]{1,0:T(8,128)(2,1)S(1)}, u32[]{:S(2)}, u32[]{:S(2)}) collective-permute-start(bf16[64,1280]{1,0:T(8,128)(2,1)S(1)} %get-tuple-element.62), channel_id=1, source_target_pairs={{0,16},{16,0},{8,24},{24,8},{1,17},{17,1},{9,25},{25,9},{2,18},{18... | collective-permute-start | bytes 491528 | tf_op jit(solution)/shard_map/ppermute | solution.py:483

commit v13 on v12

--- a/solution.py
+++ b/solution.py
@@ -379,79 +379,105 @@
     return [(0, reach, 0), (tokens - reach, reach, reach)]
 
 
-def relay_kernel(spots, first_row, chunks, row_ref, gate_ref, branch_refs, base_ref, total_refs, *refs):
-    grad_ref, out_ref, staged, sems, grad_sems = refs[-5:]
-    tokens, width = base_ref.shape
-    half = width // 2
+def relayed_rows(spots, row_ref, branch):
+    picks = selector(row_ref[...]).T.astype(jnp.bfloat16)
+    picks = jnp.concatenate([picks[:, top : top + size] for top, size, at in spots], axis=1)
+    return jnp.dot(picks, branch, preferred_element_type=jnp.float32)
+
+
+def relay_first_kernel(spots, row_ref, gate_ref, a_ref, b_ref, base_ref, c_ref, d_ref, grad_ref, out_ref, sems):
+    half = a_ref.shape[1]
     copies = []
-    for n, ref in enumerate(total_refs):
+    for n, ref in enumerate((c_ref, d_ref)):
+        to = grad_ref.at[pl.ds(0, ref.shape[0]), pl.ds(n * half, half)]
+        copies.append(pltpu.make_async_copy(ref, to, sems.at[n]))
+    for copy in copies:
+        copy.start()
+    for n, ref in enumerate((a_ref, b_ref)):
+        lanes = slice(n * half, (n + 1) * half)
+        relayed = relayed_rows(spots, row_ref, ref[...])
+        out_ref[:, lanes] = base_ref[:, lanes].astype(jnp.float32) + gate_ref[:, lanes] * relayed
+    for copy in copies:
+        copy.wait()
+
+
+def relay_first(rows, gate, branch, base, totals, spots):
+    tokens, width = base.shape
+    return pl.pallas_call(
+        functools.partial(relay_first_kernel, spots),
+        in_specs=[VMEM] * 7,
+        out_specs=[pl.BlockSpec(memory_space=pltpu.HBM), VMEM],
+        out_shape=[
+            jax.ShapeDtypeStruct((tokens, width), jnp.bfloat16),
+            jax.ShapeDtypeStruct((tokens, width), jnp.float32),
+        ],
+        scratch_shapes=[pltpu.SemaphoreType.DMA((2,))],
+        compiler_params=PARAMS,
+        cost_estimate=pl.CostEstimate(
+            flops=2 * tokens * tokens * width, bytes_accessed=24 * tokens * width, transcendentals=0
+        ),
+        name="relay_first",
+    )(rows, gate, *branch, base, *totals)
+
+
+def relay_last_kernel(
+    spots, part, chunks, first_row, holds_ref, row_ref, gate_ref, held_ref, got_ref, base_ref, total_ref, *refs
+):
+    grad_ref, out_ref, staged, summed, sems, grad_sem = refs[-6:]
+    half = held_ref.shape[1]
+    other = 1 - part
+    holds = holds_ref[0] == 1
+    summed[...] = jnp.where(holds, got_ref[...], total_ref[...])
+    to = grad_ref.at[pl.ds(first_row, total_ref.shape[0]), pl.ds(other * half, half)]
+    copies = [pltpu.make_async_copy(summed, to, grad_sem)]
+    copies[0].start()
+    step = half // chunks
+    for c in range(chunks):
+        mine = slice(c * step, (c + 1) * step)
+        lanes = slice(part * half + c * step, part * half + (c + 1) * step)
+        branch = jnp.where(holds, held_ref[:, mine], got_ref[:, mine])
+        relayed = relayed_rows(spots, row_ref, branch)
+        total = base_ref[:, lanes].astype(jnp.float32) + gate_ref[:, lanes] * relayed
+        staged[:, mine] = total.astype(staged.dtype)
         copies.append(
             pltpu.make_async_copy(
-                ref,
-                grad_ref.at[pl.ds(first_row, ref.shape[0]), pl.ds(n * half, half)],
-                grad_sems.at[n],
+                staged.at[:, pl.ds(c * step, step)],
+                out_ref.at[:, pl.ds(part * half + c * step, step)],
+                sems.at[c],
             )
         )
-    for copy in copies:
-        copy.start()
-    picks = selector(row_ref[...]).T.astype(jnp.bfloat16)
-    picks = jnp.concatenate([picks[:, top : top + size] for top, size, at in spots], axis=1)
-    step = half // chunks
-    for n, ref in enumerate(branch_refs):
-        for c in range(chunks):
-            lanes = slice(n * half + c * step, n * half + (c + 1) * step)
-            relayed = jnp.dot(
-                picks, ref[:, c * step : (c + 1) * step], preferred_element_type=jnp.float32
-            )
-            total = base_ref[:, lanes].astype(jnp.float32) + gate_ref[:, lanes] * relayed
-            staged[:, lanes] = total.astype(staged.dtype)
-            if sems is not None:
-                part = pl.ds(n * half + c * step, step)
-                copy = pltpu.make_async_copy(
-                    staged.at[:, part], out_ref.at[:, part], sems.at[n * chunks + c]
-                )
-                copy.start()
-                copies.append(copy)
+        copies[-1].start()
     for copy in copies:
         copy.wait()
 
 
-def relay(rows, gate, branch, base, totals, spots, first_row, grads, last):
+def relay_last(holds, rows, gate, held, got, base, total, spots, part, first_row, grads, out):
     tokens, width = base.shape
     chunks = 2 if width // 2 % (2 * LANES) == 0 else 1
     far = pl.BlockSpec(memory_space=pltpu.HBM)
-    whole = jax.ShapeDtypeStruct((tokens, width), jnp.bfloat16)
-
-    def kernel(row_ref, gate_ref, a_ref, b_ref, base_ref, c_ref, d_ref, *refs):
-        if grads is not None:
-            refs = refs[1:]
-        if last:
-            grad_ref, out_ref, staged, sems, grad_sems = refs
-        else:
-            grad_ref, out_ref, grad_sems = refs
-            staged, sems = out_ref, None
-        relay_kernel(
-            spots, first_row, chunks, row_ref, gate_ref, (a_ref, b_ref), base_ref, (c_ref, d_ref),
-            grad_ref, out_ref, staged, sems, grad_sems,
-        )
-
-    out = whole if last else jax.ShapeDtypeStruct((tokens, width), jnp.float32)
-    scratch = [pltpu.VMEM((tokens, width), jnp.bfloat16), pltpu.SemaphoreType.DMA((2 * chunks,))]
-    operands = [rows, gate, *branch, base, *totals] + ([] if grads is None else [grads])
+    operands = [holds, rows, gate, held, got, base, total]
+    aliases = {}
+    for n, buffer in enumerate((grads, out)):
+        if buffer is not None:
+            aliases[len(operands)] = n
+            operands.append(buffer)
     return pl.pallas_call(
-        kernel,
-        in_specs=[VMEM] * 7 + ([] if grads is None else [far]),
-        out_specs=[far, far if last else VMEM],
-        out_shape=[whole, out],
-        input_output_aliases={} if grads is None else {7: 0},
-        scratch_shapes=(scratch if last else []) + [pltpu.SemaphoreType.DMA((2,))],
+        functools.partial(relay_last_kernel, spots, part, chunks, first_row),
+        in_specs=[SMEM] + [VMEM] * 6 + [far] * len(aliases),
+        out_specs=[far] * 2,
+        out_shape=[jax.ShapeDtypeStruct((tokens, width), jnp.bfloat16)] * 2,
+        input_output_aliases=aliases,
+        scratch_shapes=[
+            pltpu.VMEM((tokens, width // 2), jnp.bfloat16),
+            pltpu.VMEM(total.shape, jnp.bfloat16),
+            pltpu.SemaphoreType.DMA((chunks,)),
+            pltpu.SemaphoreType.DMA,
+        ],
         compiler_params=PARAMS,
         cost_estimate=pl.CostEstimate(
-            flops=2 * tokens * tokens * width,
-            bytes_accessed=24 * tokens * width,
-            transcendentals=0,
+            flops=tokens * tokens * width, bytes_accessed=6 * tokens * width, transcendentals=0
         ),
-        name="relay",
+        name="relay_last",
     )(*operands)
 
 
@@ -543,11 +569,20 @@
             jnp.where((group == 0) | (group == 2), across, total_a),
             jnp.where(group <= 1, down, total_b),
         )
-        branch_grad, block_out = relay(
-            rows, gate, (branch_a, branch_b), block_out, totals, spots[n], first_row, branch_grad,
-            n == count - 1,
-        )
-        first_row += piece.shape[0]
+        if n < count - 1:
+            branch_grad, block_out = relay_first(
+                rows, gate, (branch_a, branch_b), block_out, totals, spots[n]
+            )
+            first_row = piece.shape[0]
+            continue
+        base, block_out = block_out, None
+        ends = ((group <= 1, held_a, down, total_b), ((group == 0) | (group == 2), held_b, across, total_a))
+        for part in (1, 0):
+            holds, held, got, total = ends[part]
+            branch_grad, block_out = relay_last(
+                holds.astype(jnp.int32)[None], rows, gate, held, got, base, total, spots[n], part,
+                first_row, branch_grad, block_out,
+            )
     return (block_out[None, None], branch_grad[None])
 
 

time: 39.9 us -> 39.7 us (level)
  the two profiles are of different devices: /device:TPU:8 before, /device:TPU:0 now
where the time goes in v13:
time: 39.7 us; the launch traced here: 39.1 us
  starting transfers between devices  15 us (38%)
  Pallas kernels  12 us (30%)
  waiting for transfers between devices  9.75 us (25%)
  other arithmetic  1.43 us (4%)
  between operations  0.84 us (2%)
    ppermute x10, starting transfers between devices, local(): send = lambda block, route: lax.ppermute(block, 'grp', route)  11.5 us
    ppermute x10, waiting for transfers between devices, local(): send = lambda block, route: lax.ppermute(block, 'grp', route)  9.75 us
    pallas_call x1, Pallas kernels, attend_edges(): pl.pallas_call(functools.partial(kernel, reach), in_specs=[SMEM if operan...  3.05 us
    ppermute x2, starting transfers between devices, paired(): return lax.ppermute(block, axis, route)  2.98 us
    pallas_call x2, Pallas kernels, relay_last(): pl.pallas_call(functools.partial(relay_last_kernel, spots, part, chunks,...  2.3 us
    pallas_call x1, Pallas kernels, attend_middle(): pl.pallas_call(functools.partial(middle_kernel, reach), in_specs=[VMEM] *...  1.59 us
    pallas_call x1, Pallas kernels, pack_ends(): pl.pallas_call(ends_kernel, in_specs=[SMEM] + [VMEM] * 3, out_specs=[VMEM...  1.48 us
    pallas_call x1, Pallas kernels, pair_sums(): pl.pallas_call(functools.partial(sums_kernel, sizes), in_specs=[SMEM] + [...  1.39 us
  transfers between devices with their start and end apart: 13, of which 6 were waited for; matrix products, arithmetic and copies ran while one was open for 4% of the time, Pallas kernels for 28%

profile of v13, /device:TPU:0, one launch (start us, length us, event | category | flops | bytes accessed | tf_op | source)
XLA Modules:
  0.0 39.1 jit_solution(17649407416974702514)
XLA Ops:
  0.6 0.5 %collective-permute-start = (f32[1280]{0:T(1024)}, f32[1280]{0:T(1024)S(1)}, u32[]{:S(2)}, u32[]{:S(2)}) collective-permute-start(f32[1280]{0:T(1024)} %param.12), channel_id=1, source_target_pairs={{0,1},{1,0},{2,3},{3,2},{4,5},{5,4},{6,7},{7,6},{8,9},{9,8},{10,11... | collective-permute-start | bytes 15368 | tf_op jit(solution)/shard_map/ppermute | solution.py:488
  1.1 0.7 %and_select_fusion = (s32[1,128]{1,0:T(1,128)S(1)}, s32[1,128]{1,0:T(1,128)S(1)}) fusion(s32[1,1,128]{2,1,0:T(1,128)} %param.11, s32[1,1,128]{2,1,0:T(1,128)} %param.10), kind=kLoop, calls=%fused_computation.28 | loop fusion | flops 2816 | bytes 2048 | tf_op jit(solution)/shard_map/jit(remainder)/select_n | solution.py:513
  1.9 1.2 %pack_grads.1 = (bf16[128,1408]{1,0:T(8,128)(2,1)S(1)}, bf16[128,1408]{1,0:T(8,128)(2,1)S(1)}) custom-call(bf16[128,2560]{1,0:T(8,128)(2,1)} %bitcast.42, f32[2,128]{1,0:T(2,128)S(1)} %add_convert_fusion.5.mark_ref, bf16[128,2560]{1,0:T(8,128)(2,1)} %bitcast.37, bf16[128,2560]{1,0:T(8,128)(2,1)} %bitcast.29, bf16[128,2560]{1,0:T(8,128)(2,1)} %bitcast.33), custom_call_target="tpu_custom_call" | custom-call | bytes 1310720 | tf_op jit(solution)/shard_map/pack_grads/pallas_call | solution.py:317
  3.1 2.6 %collective-permute-start.1 = (bf16[128,1408]{1,0:T(8,128)(2,1)S(1)}, bf16[128,1408]{1,0:T(8,128)(2,1)S(1)}, u32[]{:S(2)}, u32[]{:S(2)}) collective-permute-start(bf16[128,1408]{1,0:T(8,128)(2,1)S(1)} %get-tuple-element.35.refs_0_), channel_id=1, source_target_pairs={{0,8},{8,0},{16,24},{24,16},{1,9},{9,1},{17,25},{25,17},{2,10},{10... | collective-permute-start | bytes 1081352 | tf_op jit(solution)/shard_map/ppermute | solution.py:509
  5.7 1.5 %collective-permute-start.2 = (bf16[128,1408]{1,0:T(8,128)(2,1)S(1)}, bf16[128,1408]{1,0:T(8,128)(2,1)}, u32[]{:S(2)}, u32[]{:S(2)}) collective-permute-start(bf16[128,1408]{1,0:T(8,128)(2,1)S(1)} %get-tuple-element.36.refs_2_), channel_id=1, source_target_pairs={{0,16},{16,0},{8,24},{24,8},{1,17},{17,1},{9,25},{25,9},{2,18},{18... | collective-permute-start | bytes 1081352 | tf_op jit(solution)/shard_map/ppermute | solution.py:509
  7.3 1.5 %pack_ends.1 = (bf16[32,5248]{1,0:T(8,128)(2,1)}, bf16[32,5248]{1,0:T(8,128)(2,1)}) custom-call(s32[2]{0:T(128)S(1)} %add_select_fusion.first_ref, bf16[128,2560]{1,0:T(8,128)(2,1)S(1)} %bitcast.30, bf16[128,2560]{1,0:T(8,128)(2,1)S(1)} %bitcast.34, f32[1,128]{1,0:T(1,128)S(1)} %get-tuple-element.41.code_ref), custom_call_target="tpu_custom_call" | custom-call | bytes 1310720 | tf_op jit(solution)/shard_map/pack_ends/pallas_call | solution.py:246
  8.7 1.6 %collective-permute-start.3 = (bf16[32,5248]{1,0:T(8,128)(2,1)}, bf16[32,5248]{1,0:T(8,128)(2,1)}, u32[]{:S(2)}, u32[]{:S(2)}) collective-permute-start(bf16[32,5248]{1,0:T(8,128)(2,1)} %get-tuple-element.42), channel_id=1, source_target_pairs={{0,2},{2,0},{4,6},{6,4},{1,3},{3,1},{5,7},{7,5},{8,10},{10,8},{12,... | collective-permute-start | bytes 1007624 | tf_op jit(solution)/shard_map/ppermute | solution.py:32
  10.3 1.4 %collective-permute-start.4 = (bf16[32,5248]{1,0:T(8,128)(2,1)}, bf16[32,5248]{1,0:T(8,128)(2,1)}, u32[]{:S(2)}, u32[]{:S(2)}) collective-permute-start(bf16[32,5248]{1,0:T(8,128)(2,1)} %get-tuple-element.43), channel_id=1, source_target_pairs={{2,4},{4,2},{3,5},{5,3},{10,12},{12,10},{11,13},{13,11},{18,20},{2... | collective-permute-start | bytes 1007624 | tf_op jit(solution)/shard_map/ppermute | solution.py:32
  11.8 1.6 %attend_middle.1 = bf16[64,2560]{1,0:T(8,128)(2,1)S(1)} custom-call(bf16[128,2560]{1,0:T(8,128)(2,1)S(1)} %bitcast.38, bf16[128,2560]{1,0:T(8,128)(2,1)S(1)} %bitcast.31, bf16[128,2560]{1,0:T(8,128)(2,1)S(1)} %bitcast.35, f32[1,128]{1,0:T(1,128)S(1)} %get-tuple-element.41.code_ref), custom_call_target="tpu_custom_call" | custom-call | flops 268435456 | bytes 1966080 | tf_op jit(solution)/shard_map/attend_middle/pallas_call | solution.py:259
  13.5 1.2 %collective-permute-done.1.refs_1_ = bf16[128,1408]{1,0:T(8,128)(2,1)S(1)} collective-permute-done((bf16[128,1408]{1,0:T(8,128)(2,1)S(1)}, bf16[128,1408]{1,0:T(8,128)(2,1)S(1)}, u32[]{:S(2)}, u32[]{:S(2)}) %collective-permute-start.1) | collective-permute-done | bytes 360480 | tf_op jit(solution)/shard_map/ppermute | solution.py:509
  14.7 1.6 %collective-permute-done.2.refs_3_ = bf16[128,1408]{1,0:T(8,128)(2,1)} collective-permute-done((bf16[128,1408]{1,0:T(8,128)(2,1)S(1)}, bf16[128,1408]{1,0:T(8,128)(2,1)}, u32[]{:S(2)}, u32[]{:S(2)}) %collective-permute-start.2) | collective-permute-done | bytes 360480 | tf_op jit(solution)/shard_map/ppermute | solution.py:509
  16.3 1.4 %pair_sums.1 = (bf16[64,1280]{1,0:T(8,128)(2,1)S(1)}, bf16[64,1280]{1,0:T(8,128)(2,1)S(1)}, bf16[64,1280]{1,0:T(8,128)(2,1)S(1)}, bf16[64,1280]{1,0:T(8,128)(2,1)S(1)}) custom-call(f32[2]{0:T(128)S(1)} %add_convert_fusion.4.flag_ref, f32[1,2560]{1,0:T(1,128)S(1)} %broadcast_in_dim.34.gate_ref, bf16[128,1408]{1,0:T(8,128)(2,1)S(1)} %get-tuple-element.35.refs_0_, ...), custom_call_target="tpu_custom_call" | custom-call | flops 167772160 | bytes 1966080 | tf_op jit(solution)/shard_map/pair_sums/pallas_call | solution.py:361
  18.2 1.7 %collective-permute-start.9 = (bf16[64,1280]{1,0:T(8,128)(2,1)S(1)}, bf16[64,1280]{1,0:T(8,128)(2,1)S(1)}, u32[]{:S(2)}, u32[]{:S(2)}) collective-permute-start(bf16[64,1280]{1,0:T(8,128)(2,1)S(1)} %get-tuple-element.48), channel_id=1, source_target_pairs={{0,16},{16,24},{24,8},{8,0},{1,17},{17,25},{25,9},{9,1},{2,18},{18... | collective-permute-start | bytes 491528 | tf_op jit(solution)/shard_map/ppermute | solution.py:509
  19.8 3.1 %attend_edges.1 = bf16[64,2560]{1,0:T(8,128)(2,1)S(1)} custom-call(s32[1]{0:T(128)S(6)} %broadcast_in_dim.36.even_ref, bf16[128,2560]{1,0:T(8,128)(2,1)S(1)} %bitcast.39, bf16[128,2560]{1,0:T(8,128)(2,1)S(1)} %bitcast.32, bf16[128,2560]{1,0:T(8,128)(2,1)S(1)} %bitcast.36, f32[1,128]{1,0:T(1,128)S(1)} %get-tuple-element.41.code_ref, ...), custom_call_target="tpu_custom_call" | custom-call | flops 268435456 | bytes 1966080 | tf_op jit(solution)/shard_map/attend_edges/pallas_call | solution.py:279
  23.0 1.6 %collective-permute-start.6 = (bf16[64,1280]{1,0:T(8,128)(2,1)S(1)}, bf16[64,1280]{1,0:T(8,128)(2,1)S(1)}, u32[]{:S(2)}, u32[]{:S(2)}) collective-permute-start(bf16[64,1280]{1,0:T(8,128)(2,1)S(1)} %get-tuple-element.71), channel_id=1, source_target_pairs={{0,16},{16,24},{24,8},{8,0},{1,17},{17,25},{25,9},{9,1},{2,18},{18... | collective-permute-start | bytes 491528 | tf_op jit(solution)/shard_map/ppermute | solution.py:509
  25.7 1.7 %collective-permute-start.10 = (bf16[64,1280]{1,0:T(8,128)(2,1)S(1)}, bf16[64,1280]{1,0:T(8,128)(2,1)S(1)}, u32[]{:S(2)}, u32[]{:S(2)}) collective-permute-start(bf16[64,1280]{1,0:T(8,128)(2,1)S(1)} %get-tuple-element.69), channel_id=1, source_target_pairs={{0,16},{16,0},{8,24},{24,8},{1,17},{17,1},{9,25},{25,9},{2,18},{18... | collective-permute-start | bytes 491528 | tf_op jit(solution)/shard_map/ppermute | solution.py:509
  27.4 2.3 %collective-permute-done.6 = bf16[64,1280]{1,0:T(8,128)(2,1)S(1)} collective-permute-done((bf16[64,1280]{1,0:T(8,128)(2,1)S(1)}, bf16[64,1280]{1,0:T(8,128)(2,1)S(1)}, u32[]{:S(2)}, u32[]{:S(2)}) %collective-permute-start.6) | collective-permute-done | bytes 163872 | tf_op jit(solution)/shard_map/ppermute | solution.py:509
  29.7 1.5 %collective-permute-done.5 = bf16[64,1280]{1,0:T(8,128)(2,1)S(1)} collective-permute-done((bf16[64,1280]{1,0:T(8,128)(2,1)S(1)}, bf16[64,1280]{1,0:T(8,128)(2,1)S(1)}, u32[]{:S(2)}, u32[]{:S(2)}) %collective-permute-start.5) | collective-permute-done | bytes 163872 | tf_op jit(solution)/shard_map/ppermute | solution.py:509
  31.4 0.8 %collective-permute-start.12 = (bf16[64,1280]{1,0:T(8,128)(2,1)S(1)}, bf16[64,1280]{1,0:T(8,128)(2,1)S(1)}, u32[]{:S(2)}, u32[]{:S(2)}) collective-permute-start(bf16[64,1280]{1,0:T(8,128)(2,1)S(1)} %get-tuple-element.56), channel_id=1, source_target_pairs={{0,8},{8,0},{16,24},{24,16},{1,9},{9,1},{17,25},{25,17},{2,10},{10... | collective-permute-start | bytes 491528 | tf_op jit(solution)/shard_map/ppermute | solution.py:509
  32.6 1.9 %collective-permute-done.10 = bf16[64,1280]{1,0:T(8,128)(2,1)S(1)} collective-permute-done((bf16[64,1280]{1,0:T(8,128)(2,1)S(1)}, bf16[64,1280]{1,0:T(8,128)(2,1)S(1)}, u32[]{:S(2)}, u32[]{:S(2)}) %collective-permute-start.10) | collective-permute-done | bytes 163872 | tf_op jit(solution)/shard_map/ppermute | solution.py:509
  34.5 1.0 %relay_first.1 = (bf16[128,2560]{1,0:T(8,128)(2,1)}, f32[128,2560]{1,0:T(8,128)S(1)}) custom-call(f32[1,128]{1,0:T(1,128)S(1)} %get-tuple-element.84.row_ref, f32[1,2560]{1,0:T(1,128)S(1)} %broadcast_in_dim.34.gate_ref, bf16[64,1280]{1,0:T(8,128)(2,1)S(1)} %get-tuple-element.78.a_ref, bf16[64,1280]{1,0:T(8,128)(2,1)S(1)} %get-tuple-element.77.b_ref, ...), custom_call_target="tpu_custom_call" | custom-call | flops 83886080 | bytes 7864320 | tf_op jit(solution)/shard_map/relay_first/pallas_call | solution.py:406
  35.5 1.2 %collective-permute-done.12.got_ref = bf16[64,1280]{1,0:T(8,128)(2,1)S(1)} collective-permute-done((bf16[64,1280]{1,0:T(8,128)(2,1)S(1)}, bf16[64,1280]{1,0:T(8,128)(2,1)S(1)}, u32[]{:S(2)}, u32[]{:S(2)}) %collective-permute-start.12) | collective-permute-done | bytes 163872 | tf_op jit(solution)/shard_map/ppermute | solution.py:509
  36.8 1.2 %relay_last.2 = (bf16[128,2560]{1,0:T(8,128)(2,1)}, bf16[128,2560]{1,0:T(8,128)(2,1)}) custom-call(s32[1]{0:T(128)} %bitcast.11.holds_ref, f32[1,128]{1,0:T(1,128)S(1)} %get-tuple-element.84.row_ref, f32[1,2560]{1,0:T(1,128)S(1)} %broadcast_in_dim.34.gate_ref, bf16[64,1280]{1,0:T(8,128)(2,1)S(1)} %get-tuple-element.58.held_ref, ...), custom_call_target="tpu_custom_call", output_to_operand_aliasing={{0}: (7, {})} | custom-call | flops 41943040 | bytes 1966080 | tf_op jit(solution)/shard_map/relay_last/pallas_call | solution.py:464
  37.9 1.1 %relay_last.3 = (bf16[128,2560]{1,0:T(8,128)(2,1)}, bf16[128,2560]{1,0:T(8,128)(2,1)}) custom-call(s32[1]{0:T(128)} %bitcast.holds_ref, f32[1,128]{1,0:T(1,128)S(1)} %get-tuple-element.84.row_ref, f32[1,2560]{1,0:T(1,128)S(1)} %broadcast_in_dim.34.gate_ref, ...), custom_call_target="tpu_custom_call", output_to_operand_aliasing={{0}: (7, {}), {1}: (8, {})} | custom-call | flops 41943040 | bytes 1966080 | tf_op jit(solution)/shard_map/relay_last/pallas_call | solution.py:464
  (33 shorter events, 2.5 us)
Async XLA Ops:
  0.6 12.8 %collective-permute-start = (f32[1280]{0:T(1024)}, f32[1280]{0:T(1024)S(1)}, u32[]{:S(2)}, u32[]{:S(2)}) collective-permute-start(f32[1280]{0:T(1024)} %param.12), channel_id=1, source_target_pairs={{0,1},{1,0},{2,3},{3,2},{4,5},{5,4},{6,7},{7,6},{8,9},{9,8},{10,11... | collective-permute-start | bytes 15368 | tf_op jit(solution)/shard_map/ppermute | solution.py:488
  1.9 5.4 %copy-start = (bf16[1,1,128,2560]{3,2,1,0:T(8,128)(2,1)S(1)}, bf16[1,1,128,2560]{3,2,1,0:T(8,128)(2,1)}, u32[]{:S(2)}) copy-start(bf16[1,1,128,2560]{3,2,1,0:T(8,128)(2,1)} %param.8) | copy-start | bytes 1966084
  1.9 5.4 %copy-start.1 = (bf16[1,1,128,2560]{3,2,1,0:T(8,128)(2,1)S(1)}, bf16[1,1,128,2560]{3,2,1,0:T(8,128)(2,1)}, u32[]{:S(2)}) copy-start(bf16[1,1,128,2560]{3,2,1,0:T(8,128)(2,1)} %param.9) | copy-start | bytes 1966084
  3.1 8.7 %copy-start.2 = (bf16[1,1,128,2560]{3,2,1,0:T(8,128)(2,1)S(1)}, bf16[1,1,128,2560]{3,2,1,0:T(8,128)(2,1)}, u32[]{:S(2)}) copy-start(bf16[1,1,128,2560]{3,2,1,0:T(8,128)(2,1)} %param.7) | copy-start | bytes 1966084
  3.1 11.6 %collective-permute-start.1 = (bf16[128,1408]{1,0:T(8,128)(2,1)S(1)}, bf16[128,1408]{1,0:T(8,128)(2,1)S(1)}, u32[]{:S(2)}, u32[]{:S(2)}) collective-permute-start(bf16[128,1408]{1,0:T(8,128)(2,1)S(1)} %get-tuple-element.35.refs_0_), channel_id=1, source_target_pairs={{0,8},{8,0},{16,24},{24,16},{1,9},{9,1},{17,25},{25,17},{2,10},{10... | collective-permute-start | bytes 1081352 | tf_op jit(solution)/shard_map/ppermute | solution.py:509
  5.7 10.6 %collective-permute-start.2 = (bf16[128,1408]{1,0:T(8,128)(2,1)S(1)}, bf16[128,1408]{1,0:T(8,128)(2,1)}, u32[]{:S(2)}, u32[]{:S(2)}) collective-permute-start(bf16[128,1408]{1,0:T(8,128)(2,1)S(1)} %get-tuple-element.36.refs_2_), channel_id=1, source_target_pairs={{0,16},{16,0},{8,24},{24,8},{1,17},{17,1},{9,25},{25,9},{2,18},{18... | collective-permute-start | bytes 1081352 | tf_op jit(solution)/shard_map/ppermute | solution.py:509
  8.7 4.7 %copy-start.3 = (f32[1280]{0:T(1024)S(1)}, f32[1280]{0:T(1024)}, u32[]{:S(2)}) copy-start(f32[1280]{0:T(1024)} %param.12) | copy-start | bytes 15364
  8.7 11.1 %collective-permute-start.3 = (bf16[32,5248]{1,0:T(8,128)(2,1)}, bf16[32,5248]{1,0:T(8,128)(2,1)}, u32[]{:S(2)}, u32[]{:S(2)}) collective-permute-start(bf16[32,5248]{1,0:T(8,128)(2,1)} %get-tuple-element.42), channel_id=1, source_target_pairs={{0,2},{2,0},{4,6},{6,4},{1,3},{3,1},{5,7},{7,5},{8,10},{10,8},{12,... | collective-permute-start | bytes 1007624 | tf_op jit(solution)/shard_map/ppermute | solution.py:32
  10.3 9.5 %collective-permute-start.4 = (bf16[32,5248]{1,0:T(8,128)(2,1)}, bf16[32,5248]{1,0:T(8,128)(2,1)}, u32[]{:S(2)}, u32[]{:S(2)}) collective-permute-start(bf16[32,5248]{1,0:T(8,128)(2,1)} %get-tuple-element.43), channel_id=1, source_target_pairs={{2,4},{4,2},{3,5},{5,3},{10,12},{12,10},{11,13},{13,11},{18,20},{2... | collective-permute-start | bytes 1007624 | tf_op jit(solution)/shard_map/ppermute | solution.py:32
  17.7 7.4 %collective-permute-start.8 = (bf16[64,1280]{1,0:T(8,128)(2,1)S(1)}, bf16[64,1280]{1,0:T(8,128)(2,1)S(1)}, u32[]{:S(2)}, u32[]{:S(2)}) collective-permute-start(bf16[64,1280]{1,0:T(8,128)(2,1)S(1)} %get-tuple-element.46), channel_id=1, source_target_pairs={{0,8},{8,24},{24,16},{16,0},{1,9},{9,25},{25,17},{17,1},{2,10},{10... | collective-permute-start | bytes 491528 | tf_op jit(solution)/shard_map/ppermute | solution.py:509
  18.2 7.0 %collective-permute-start.9 = (bf16[64,1280]{1,0:T(8,128)(2,1)S(1)}, bf16[64,1280]{1,0:T(8,128)(2,1)S(1)}, u32[]{:S(2)}, u32[]{:S(2)}) collective-permute-start(bf16[64,1280]{1,0:T(8,128)(2,1)S(1)} %get-tuple-element.48), channel_id=1, source_target_pairs={{0,16},{16,24},{24,8},{8,0},{1,17},{17,25},{25,9},{9,1},{2,18},{18... | collective-permute-start | bytes 491528 | tf_op jit(solution)/shard_map/ppermute | solution.py:509
  23.0 6.8 %collective-permute-start.6 = (bf16[64,1280]{1,0:T(8,128)(2,1)S(1)}, bf16[64,1280]{1,0:T(8,128)(2,1)S(1)}, u32[]{:S(2)}, u32[]{:S(2)}) collective-permute-start(bf16[64,1280]{1,0:T(8,128)(2,1)S(1)} %get-tuple-element.71), channel_id=1, source_target_pairs={{0,16},{16,24},{24,8},{8,0},{1,17},{17,25},{25,9},{9,1},{2,18},{18... | collective-permute-start | bytes 491528 | tf_op jit(solution)/shard_map/ppermute | solution.py:509
  24.5 6.7 %collective-permute-start.5 = (bf16[64,1280]{1,0:T(8,128)(2,1)S(1)}, bf16[64,1280]{1,0:T(8,128)(2,1)S(1)}, u32[]{:S(2)}, u32[]{:S(2)}) collective-permute-start(bf16[64,1280]{1,0:T(8,128)(2,1)S(1)} %get-tuple-element.72), channel_id=1, source_target_pairs={{0,8},{8,24},{24,16},{16,0},{1,9},{9,25},{25,17},{17,1},{2,10},{10... | collective-permute-start | bytes 491528 | tf_op jit(solution)/shard_map/ppermute | solution.py:509
  25.3 7.3 %collective-permute-start.11 = (bf16[64,1280]{1,0:T(8,128)(2,1)S(1)}, bf16[64,1280]{1,0:T(8,128)(2,1)S(1)}, u32[]{:S(2)}, u32[]{:S(2)}) collective-permute-start(bf16[64,1280]{1,0:T(8,128)(2,1)S(1)} %get-tuple-element.59), channel_id=1, source_target_pairs={{0,8},{8,0},{16,24},{24,16},{1,9},{9,1},{17,25},{25,17},{2,10},{10... | collective-permute-start | bytes 491528 | tf_op jit(solution)/shard_map/ppermute | solution.py:509
  25.7 8.7 %collective-permute-start.10 = (bf16[64,1280]{1,0:T(8,128)(2,1)S(1)}, bf16[64,1280]{1,0:T(8,128)(2,1)S(1)}, u32[]{:S(2)}, u32[]{:S(2)}) collective-permute-start(bf16[64,1280]{1,0:T(8,128)(2,1)S(1)} %get-tuple-element.69), channel_id=1, source_target_pairs={{0,16},{16,0},{8,24},{24,8},{1,17},{17,1},{9,25},{25,9},{2,18},{18... | collective-permute-start | bytes 491528 | tf_op jit(solution)/shard_map/ppermute | solution.py:509
  31.4 5.4 %collective-permute-start.12 = (bf16[64,1280]{1,0:T(8,128)(2,1)S(1)}, bf16[64,1280]{1,0:T(8,128)(2,1)S(1)}, u32[]{:S(2)}, u32[]{:S(2)}) collective-permute-start(bf16[64,1280]{1,0:T(8,128)(2,1)S(1)} %get-tuple-element.56), channel_id=1, source_target_pairs={{0,8},{8,0},{16,24},{24,16},{1,9},{9,1},{17,25},{25,17},{2,10},{10... | collective-permute-start | bytes 491528 | tf_op jit(solution)/shard_map/ppermute | solution.py:509
  32.2 5.7 %collective-permute-start.7 = (bf16[64,1280]{1,0:T(8,128)(2,1)S(1)}, bf16[64,1280]{1,0:T(8,128)(2,1)S(1)}, u32[]{:S(2)}, u32[]{:S(2)}) collective-permute-start(bf16[64,1280]{1,0:T(8,128)(2,1)S(1)} %get-tuple-element.66), channel_id=1, source_target_pairs={{0,16},{16,0},{8,24},{24,8},{1,17},{17,1},{9,25},{25,9},{2,18},{18... | collective-permute-start | bytes 491528 | tf_op jit(solution)/shard_map/ppermute | solution.py:509

commit v14 on v13

--- a/solution.py
+++ b/solution.py
@@ -137,15 +137,17 @@
         out_ref[:, base + low : base + low + LANES] = tile
 
 
-def ends_kernel(first_ref, k_ref, v_ref, code_ref, *end_refs):
+def ends_kernel(k_ref, v_ref, code_ref, *end_refs):
+    even = lax.axis_index("seq") % 2 == 0
     tokens, width = k_ref.shape
     code = columns(code_ref[...])
     for n, ref in enumerate(end_refs):
         most = ref.shape[0]
-        first = pl.multiple_of(first_ref[n], most)
+        tail = even if n == 0 else jnp.logical_not(even)
+        first = pl.multiple_of(jnp.where(tail, tokens - most, 0), most)
         ref[:, :width] = k_ref[pl.ds(first, most), :]
         ref[:, width : 2 * width] = v_ref[pl.ds(first, most), :]
-        here = jnp.where(first == 0, code[:most], code[tokens - most :])
+        here = jnp.where(tail, code[tokens - most :], code[:most])
         ref[:, 2 * width :] = here.astype(jnp.bfloat16)
 
 
@@ -162,12 +164,12 @@
         store_period(base, mixed_period(base, scores, sets, period), out_ref)
 
 
-def sides_kernel(reach, even_ref, q_ref, k_ref, v_ref, code_ref, one_ref, two_ref, *refs):
+def sides_kernel(reach, q_ref, k_ref, v_ref, code_ref, one_ref, two_ref, *refs):
     out_ref, keys, values, codes = refs
     tokens, width = q_ref.shape
     near = 2 * reach
     code = columns(code_ref[...])
-    even = even_ref[0] == 1
+    even = lax.axis_index("seq") % 2 == 0
     period = math.lcm(DH, LANES)
     masks = head_masks(reach, period)
     blocks = []
@@ -236,22 +238,21 @@
 
 
 VMEM = pl.BlockSpec(memory_space=pltpu.VMEM)
-SMEM = pl.BlockSpec(memory_space=pltpu.SMEM)
 PARAMS = pltpu.CompilerParams(vmem_limit_bytes=VMEM_LIMIT)
 
 
-def pack_ends(firsts, keys, values, code, most):
+def pack_ends(keys, values, code, most):
     width = keys.shape[1]
     ends = jax.ShapeDtypeStruct((most, 2 * width + LANES), jnp.bfloat16)
     return pl.pallas_call(
         ends_kernel,
-        in_specs=[SMEM] + [VMEM] * 3,
+        in_specs=[VMEM] * 3,
         out_specs=[VMEM] * 2,
         out_shape=[ends, ends],
         compiler_params=PARAMS,
         cost_estimate=pl.CostEstimate(flops=0, bytes_accessed=16 * most * width, transcendentals=0),
         name="pack_ends",
-    )(firsts, keys, values, code)
+    )(keys, values, code)
 
 
 def attend_middle(queries, keys, values, code, reach):
@@ -267,18 +268,19 @@
     )(queries, keys, values, code)
 
 
-def attend_edges(even, queries, keys, values, code, halos, reach):
+def attend_edges(queries, keys, values, code, halos, reach):
     tokens, width = queries.shape
     rows = min(tokens, 2 * reach)
     if tokens > 2 * reach:
-        kernel, operands = sides_kernel, [even, queries, keys, values, code, *halos]
+        kernel = sides_kernel
         held = (2, -(-3 * reach // LANES) * LANES)
     else:
-        kernel, operands = edge_kernel, [queries, keys, values, code, *halos]
+        kernel = edge_kernel
         held = (-(-2 * reach // LANES) * LANES,)
+    operands = [queries, keys, values, code, *halos]
     return pl.pallas_call(
         functools.partial(kernel, reach),
-        in_specs=[SMEM if operand is even else VMEM for operand in operands],
+        in_specs=[VMEM] * len(operands),
         out_specs=VMEM,
         out_shape=jax.ShapeDtypeStruct((rows, width), jnp.bfloat16),
         scratch_shapes=[
@@ -332,7 +334,8 @@
     return jnp.where(wanted == row, 1.0, 0.0)
 
 
-def sums_kernel(sizes, flag_ref, gate_ref, *refs):
+def sums_kernel(sizes, gate_ref, *refs):
+    group = lax.axis_index("grp")
     half = gate_ref.shape[1] // 2
     count = len(sizes)
     for n in range(2):
@@ -348,19 +351,20 @@
             preferred_element_type=jnp.float32,
         )
         term = gate_ref[:, n * half : (n + 1) * half] * summed
-        term = (term + flag_ref[n] * rows[1].astype(jnp.float32)).astype(jnp.bfloat16)
+        own = jnp.where(group == n + 1, 1.0, 0.0)
+        term = (term + own * rows[1].astype(jnp.float32)).astype(jnp.bfloat16)
         at = 0
         for ref, size in zip(refs[4 + n * count : 4 + (n + 1) * count], sizes):
             ref[...] = term[at : at + size]
             at += size
 
 
-def pair_sums(flags, gate, parts, sizes):
+def pair_sums(gate, parts, sizes):
     tokens, width = parts[0].shape[0], gate.shape[1]
     outs = [jax.ShapeDtypeStruct((size, width // 2), jnp.bfloat16) for size in sizes] * 2
     return pl.pallas_call(
         functools.partial(sums_kernel, sizes),
-        in_specs=[SMEM] + [VMEM] * 5,
+        in_specs=[VMEM] * 5,
         out_specs=[VMEM] * len(outs),
         out_shape=outs,
         compiler_params=PARAMS,
@@ -368,7 +372,7 @@
             flops=4 * tokens * tokens * width, bytes_accessed=6 * tokens * width, transcendentals=0
         ),
         name="pair_sums",
-    )(flags, gate, *parts)
+    )(gate, *parts)
 
 
 def piece_spots(tokens, reach, piece):
@@ -379,13 +383,14 @@
     return [(0, reach, 0), (tokens - reach, reach, reach)]
 
 
-def relayed_rows(spots, row_ref, branch):
+def picked(spots, row_ref):
     picks = selector(row_ref[...]).T.astype(jnp.bfloat16)
-    picks = jnp.concatenate([picks[:, top : top + size] for top, size, at in spots], axis=1)
-    return jnp.dot(picks, branch, preferred_element_type=jnp.float32)
-
-
-def relay_first_kernel(spots, row_ref, gate_ref, a_ref, b_ref, base_ref, c_ref, d_ref, grad_ref, out_ref, sems):
+    return jnp.concatenate([picks[:, top : top + size] for top, size, at in spots], axis=1)
+
+
+def relay_first_kernel(
+    spots, later, row_ref, gate_ref, a_ref, b_ref, base_ref, c_ref, d_ref, grad_ref, out_ref, picks_ref, sems
+):
     half = a_ref.shape[1]
     copies = []
     for n, ref in enumerate((c_ref, d_ref)):
@@ -393,23 +398,26 @@
         copies.append(pltpu.make_async_copy(ref, to, sems.at[n]))
     for copy in copies:
         copy.start()
+    picks = picked(spots, row_ref)
     for n, ref in enumerate((a_ref, b_ref)):
         lanes = slice(n * half, (n + 1) * half)
-        relayed = relayed_rows(spots, row_ref, ref[...])
+        relayed = jnp.dot(picks, ref[...], preferred_element_type=jnp.float32)
         out_ref[:, lanes] = base_ref[:, lanes].astype(jnp.float32) + gate_ref[:, lanes] * relayed
+    picks_ref[...] = picked(later, row_ref)
     for copy in copies:
         copy.wait()
 
 
-def relay_first(rows, gate, branch, base, totals, spots):
+def relay_first(rows, gate, branch, base, totals, spots, later):
     tokens, width = base.shape
     return pl.pallas_call(
-        functools.partial(relay_first_kernel, spots),
+        functools.partial(relay_first_kernel, spots, later),
         in_specs=[VMEM] * 7,
-        out_specs=[pl.BlockSpec(memory_space=pltpu.HBM), VMEM],
+        out_specs=[pl.BlockSpec(memory_space=pltpu.HBM), VMEM, VMEM],
         out_shape=[
             jax.ShapeDtypeStruct((tokens, width), jnp.bfloat16),
             jax.ShapeDtypeStruct((tokens, width), jnp.float32),
+            jax.ShapeDtypeStruct((tokens, sum(size for top, size, at in later)), jnp.bfloat16),
         ],
         scratch_shapes=[pltpu.SemaphoreType.DMA((2,))],
         compiler_params=PARAMS,
@@ -421,12 +429,13 @@
 
 
 def relay_last_kernel(
-    spots, part, chunks, first_row, holds_ref, row_ref, gate_ref, held_ref, got_ref, base_ref, total_ref, *refs
+    part, chunks, first_row, picks_ref, gate_ref, held_ref, got_ref, base_ref, total_ref, *refs
 ):
     grad_ref, out_ref, staged, summed, sems, grad_sem = refs[-6:]
     half = held_ref.shape[1]
     other = 1 - part
-    holds = holds_ref[0] == 1
+    group = lax.axis_index("grp")
+    holds = group <= 1 if part == 0 else group % 2 == 0
     summed[...] = jnp.where(holds, got_ref[...], total_ref[...])
     to = grad_ref.at[pl.ds(first_row, total_ref.shape[0]), pl.ds(other * half, half)]
     copies = [pltpu.make_async_copy(summed, to, grad_sem)]
@@ -436,7 +445,7 @@
         mine = slice(c * step, (c + 1) * step)
         lanes = slice(part * half + c * step, part * half + (c + 1) * step)
         branch = jnp.where(holds, held_ref[:, mine], got_ref[:, mine])
-        relayed = relayed_rows(spots, row_ref, branch)
+        relayed = jnp.dot(picks_ref[...], branch, preferred_element_type=jnp.float32)
         total = base_ref[:, lanes].astype(jnp.float32) + gate_ref[:, lanes] * relayed
         staged[:, mine] = total.astype(staged.dtype)
         copies.append(
@@ -451,19 +460,19 @@
         copy.wait()
 
 
-def relay_last(holds, rows, gate, held, got, base, total, spots, part, first_row, grads, out):
+def relay_last(picks, gate, held, got, base, total, part, first_row, grads, out):
     tokens, width = base.shape
     chunks = 2 if width // 2 % (2 * LANES) == 0 else 1
     far = pl.BlockSpec(memory_space=pltpu.HBM)
-    operands = [holds, rows, gate, held, got, base, total]
+    operands = [picks, gate, held, got, base, total]
     aliases = {}
     for n, buffer in enumerate((grads, out)):
         if buffer is not None:
             aliases[len(operands)] = n
             operands.append(buffer)
     return pl.pallas_call(
-        functools.partial(relay_last_kernel, spots, part, chunks, first_row),
-        in_specs=[SMEM] + [VMEM] * 6 + [far] * len(aliases),
+        functools.partial(relay_last_kernel, part, chunks, first_row),
+        in_specs=[VMEM] * 6 + [far] * len(aliases),
         out_specs=[far] * 2,
         out_shape=[jax.ShapeDtypeStruct((tokens, width), jnp.bfloat16)] * 2,
         input_output_aliases=aliases,
@@ -514,11 +523,10 @@
     code, rows = marks[:1], marks[1:]
     most = min(tokens, reach)
     even = rank % 2 == 0
-    firsts = jnp.where(jnp.stack((even, ~even)), tokens - most, 0).astype(jnp.int32)
     sent_a, sent_b = pack_grads(out_grad[0, 0], marks, queries, keys, values)
     code, sent_a, sent_b = lax.optimization_barrier((code, sent_a, sent_b))
     got_a, got_b = send(sent_a, SWAP_X), send(sent_b, SWAP_Y)
-    end_one, end_two = pack_ends(firsts, keys, values, code, most)
+    end_one, end_two = pack_ends(keys, values, code, most)
     code, end_one, end_two = lax.optimization_barrier((code, end_one, end_two))
     own = [attend_middle(queries, keys, values, code, reach)] if tokens > 2 * reach else []
     gate = whole_gate(control_gate)[None]
@@ -529,8 +537,7 @@
         halos.append(shifted(tail[most - count :], "seq", hop))
         halos.append(shifted(head[:count], "seq", -hop))
     sizes = [piece.shape[0] for piece in own] + [min(tokens, 2 * reach)]
-    flags = jnp.stack([group == 1, group == 2]).astype(jnp.float32)
-    sums = pair_sums(flags, gate, (sent_a, got_a, sent_b, got_b), sizes)
+    sums = pair_sums(gate, (sent_a, got_a, sent_b, got_b), sizes)
     count = len(sizes)
 
     def outgoing(piece, sum_a, sum_b):
@@ -543,7 +550,7 @@
     sums = ready[: 2 * count]
     if going:
         going = [ready[2 * count :]]
-    own.append(attend_edges(even.astype(jnp.int32)[None], queries, keys, values, code, halos, reach))
+    own.append(attend_edges(queries, keys, values, code, halos, reach))
 
     going.append(outgoing(own[-1], sums[count - 1], sums[2 * count - 1]))
     spots = [piece_spots(tokens, reach, n) for n in range(count)]
@@ -554,6 +561,7 @@
     ]
     block_out = jnp.concatenate(order, axis=0)
     branch_grad, first_row = None, 0
+    picks = (rows[0][:, None] == jnp.arange(tokens)).astype(jnp.bfloat16) if count == 1 else None
     for n, (piece, sum_a, sum_b) in enumerate(zip(own, sums[:count], sums[count:])):
         piece_a, piece_b = piece[:, :half], piece[:, half:]
         one, two = send(going[n][0], ROUND_A), send(going[n][1], ROUND_B)
@@ -570,18 +578,17 @@
             jnp.where(group <= 1, down, total_b),
         )
         if n < count - 1:
-            branch_grad, block_out = relay_first(
-                rows, gate, (branch_a, branch_b), block_out, totals, spots[n]
+            branch_grad, block_out, picks = relay_first(
+                rows, gate, (branch_a, branch_b), block_out, totals, spots[n], spots[n + 1]
             )
             first_row = piece.shape[0]
             continue
         base, block_out = block_out, None
-        ends = ((group <= 1, held_a, down, total_b), ((group == 0) | (group == 2), held_b, across, total_a))
+        ends = ((held_a, down, total_b), (held_b, across, total_a))
         for part in (1, 0):
-            holds, held, got, total = ends[part]
+            held, got, total = ends[part]
             branch_grad, block_out = relay_last(
-                holds.astype(jnp.int32)[None], rows, gate, held, got, base, total, spots[n], part,
-                first_row, branch_grad, block_out,
+                picks, gate, held, got, base, total, part, first_row, branch_grad, block_out
             )
     return (block_out[None, None], branch_grad[None])
 

time: 39.7 us -> 39 us (0.982)
  Pallas kernels: 12 us -> 10.9 us
  waiting for transfers between devices: 9.75 us -> 10.6 us
    pallas_call x6, Pallas kernels: 9.21 us -> 8.11 us  [the longest x1 3.05 us: attend_edges(): pl.pallas_call(functools.partial(kernel, reach), in_specs=[VMEM] * len(op...]
    ppermute x10, waiting for transfers between devices: 9.75 us -> 10.6 us  [local(): send = lambda block, route: lax.ppermute(block, 'grp', route)]
  transfers between devices with their start and end apart: 13 -> 13, of which waited for: 6 -> 6; matrix products, arithmetic and copies ran while one was open for 4% -> 4% of each run, Pallas kernels for 28% -> 26%
where the time goes in v14:
time: 39 us; the launch traced here: 38.8 us
  starting transfers between devices  15 us (38%)
  Pallas kernels  10.9 us (28%)
  waiting for transfers between devices  10.6 us (27%)
  other arithmetic  1.34 us (3%)
  between operations  0.83 us (2%)
    ppermute x10, starting transfers between devices, local(): send = lambda block, route: lax.ppermute(block, 'grp', route)  11.6 us
    ppermute x10, waiting for transfers between devices, local(): send = lambda block, route: lax.ppermute(block, 'grp', route)  10.6 us
    pallas_call x1, Pallas kernels, attend_edges(): pl.pallas_call(functools.partial(kernel, reach), in_specs=[VMEM] * len(op...  3.05 us
    ppermute x2, starting transfers between devices, paired(): return lax.ppermute(block, axis, route)  2.98 us
    pallas_call x2, Pallas kernels, relay_last(): pl.pallas_call(functools.partial(relay_last_kernel, part, chunks, first_r...  1.98 us
    pallas_call x1, Pallas kernels, attend_middle(): pl.pallas_call(functools.partial(middle_kernel, reach), in_specs=[VMEM] *...  1.61 us
    pallas_call x1, Pallas kernels, pair_sums(): pl.pallas_call(functools.partial(sums_kernel, sizes), in_specs=[VMEM] * 5...  1.38 us
    pallas_call x1, Pallas kernels, pack_grads(): pl.pallas_call(pack_grads_kernel, in_specs=[far, VMEM] + [far] * len(othe...  1.19 us
  transfers between devices with their start and end apart: 13, of which 6 were waited for; matrix products, arithmetic and copies ran while one was open for 4% of the time, Pallas kernels for 26%

profile of v14, /device:TPU:0, one launch (start us, length us, event | category | flops | bytes accessed | tf_op | source)
XLA Modules:
  0.0 38.8 jit_solution(8691392296750016735)
XLA Ops:
  0.6 0.5 %collective-permute-start = (f32[1280]{0:T(1024)}, f32[1280]{0:T(1024)S(1)}, u32[]{:S(2)}, u32[]{:S(2)}) collective-permute-start(f32[1280]{0:T(1024)} %param.12), channel_id=1, source_target_pairs={{0,1},{1,0},{2,3},{3,2},{4,5},{5,4},{6,7},{7,6},{8,9},{9,8},{10,11... | collective-permute-start | bytes 15368 | tf_op jit(solution)/shard_map/ppermute | solution.py:497
  1.1 0.7 %and_select_fusion = (s32[1,128]{1,0:T(1,128)S(1)}, s32[1,128]{1,0:T(1,128)S(1)}) fusion(s32[1,1,128]{2,1,0:T(1,128)} %param.11, s32[1,1,128]{2,1,0:T(1,128)} %param.10), kind=kLoop, calls=%fused_computation.26 | loop fusion | flops 2816 | bytes 2048 | tf_op jit(solution)/shard_map/jit(remainder)/select_n | solution.py:522
  1.9 1.2 %pack_grads.1 = (bf16[128,1408]{1,0:T(8,128)(2,1)S(1)}, bf16[128,1408]{1,0:T(8,128)(2,1)S(1)}) custom-call(bf16[128,2560]{1,0:T(8,128)(2,1)} %bitcast.35, f32[2,128]{1,0:T(2,128)S(1)} %add_convert_fusion.4.mark_ref, bf16[128,2560]{1,0:T(8,128)(2,1)} %bitcast.31, bf16[128,2560]{1,0:T(8,128)(2,1)} %bitcast.23, bf16[128,2560]{1,0:T(8,128)(2,1)} %bitcast.27), custom_call_target="tpu_custom_call" | custom-call | bytes 1310720 | tf_op jit(solution)/shard_map/pack_grads/pallas_call | solution.py:319
  3.1 2.6 %collective-permute-start.1 = (bf16[128,1408]{1,0:T(8,128)(2,1)S(1)}, bf16[128,1408]{1,0:T(8,128)(2,1)S(1)}, u32[]{:S(2)}, u32[]{:S(2)}) collective-permute-start(bf16[128,1408]{1,0:T(8,128)(2,1)S(1)} %get-tuple-element.36.refs_0_), channel_id=1, source_target_pairs={{0,8},{8,0},{16,24},{24,16},{1,9},{9,1},{17,25},{25,17},{2,10},{10... | collective-permute-start | bytes 1081352 | tf_op jit(solution)/shard_map/ppermute | solution.py:518
  5.7 1.5 %collective-permute-start.2 = (bf16[128,1408]{1,0:T(8,128)(2,1)S(1)}, bf16[128,1408]{1,0:T(8,128)(2,1)}, u32[]{:S(2)}, u32[]{:S(2)}) collective-permute-start(bf16[128,1408]{1,0:T(8,128)(2,1)S(1)} %get-tuple-element.37.refs_2_), channel_id=1, source_target_pairs={{0,16},{16,0},{8,24},{24,8},{1,17},{17,1},{9,25},{25,9},{2,18},{18... | collective-permute-start | bytes 1081352 | tf_op jit(solution)/shard_map/ppermute | solution.py:518
  7.2 0.9 %pack_ends.1 = (bf16[32,5248]{1,0:T(8,128)(2,1)}, bf16[32,5248]{1,0:T(8,128)(2,1)}) custom-call(bf16[128,2560]{1,0:T(8,128)(2,1)S(1)} %bitcast.24, bf16[128,2560]{1,0:T(8,128)(2,1)S(1)} %bitcast.28, f32[1,128]{1,0:T(1,128)S(1)} %get-tuple-element.46.code_ref), custom_call_target="tpu_custom_call" | custom-call | bytes 1310720 | tf_op jit(solution)/shard_map/pack_ends/pallas_call | solution.py:247
  8.1 1.6 %collective-permute-start.7 = (bf16[32,5248]{1,0:T(8,128)(2,1)}, bf16[32,5248]{1,0:T(8,128)(2,1)}, u32[]{:S(2)}, u32[]{:S(2)}) collective-permute-start(bf16[32,5248]{1,0:T(8,128)(2,1)} %get-tuple-element.47), channel_id=1, source_target_pairs={{0,2},{2,0},{4,6},{6,4},{1,3},{3,1},{5,7},{7,5},{8,10},{10,8},{12,... | collective-permute-start | bytes 1007624 | tf_op jit(solution)/shard_map/ppermute | solution.py:32
  9.7 1.4 %collective-permute-start.8 = (bf16[32,5248]{1,0:T(8,128)(2,1)}, bf16[32,5248]{1,0:T(8,128)(2,1)}, u32[]{:S(2)}, u32[]{:S(2)}) collective-permute-start(bf16[32,5248]{1,0:T(8,128)(2,1)} %get-tuple-element.48), channel_id=1, source_target_pairs={{2,4},{4,2},{3,5},{5,3},{10,12},{12,10},{11,13},{13,11},{18,20},{2... | collective-permute-start | bytes 1007624 | tf_op jit(solution)/shard_map/ppermute | solution.py:32
  11.1 1.6 %attend_middle.1 = bf16[64,2560]{1,0:T(8,128)(2,1)S(1)} custom-call(bf16[128,2560]{1,0:T(8,128)(2,1)S(1)} %bitcast.32, bf16[128,2560]{1,0:T(8,128)(2,1)S(1)} %bitcast.25, bf16[128,2560]{1,0:T(8,128)(2,1)S(1)} %bitcast.29, f32[1,128]{1,0:T(1,128)S(1)} %get-tuple-element.46.code_ref), custom_call_target="tpu_custom_call" | custom-call | flops 268435456 | bytes 1966080 | tf_op jit(solution)/shard_map/attend_middle/pallas_call | solution.py:260
  12.8 1.9 %collective-permute-done.1.refs_1_ = bf16[128,1408]{1,0:T(8,128)(2,1)S(1)} collective-permute-done((bf16[128,1408]{1,0:T(8,128)(2,1)S(1)}, bf16[128,1408]{1,0:T(8,128)(2,1)S(1)}, u32[]{:S(2)}, u32[]{:S(2)}) %collective-permute-start.1) | collective-permute-done | bytes 360480 | tf_op jit(solution)/shard_map/ppermute | solution.py:518
  14.7 1.6 %collective-permute-done.2.refs_3_ = bf16[128,1408]{1,0:T(8,128)(2,1)} collective-permute-done((bf16[128,1408]{1,0:T(8,128)(2,1)S(1)}, bf16[128,1408]{1,0:T(8,128)(2,1)}, u32[]{:S(2)}, u32[]{:S(2)}) %collective-permute-start.2) | collective-permute-done | bytes 360480 | tf_op jit(solution)/shard_map/ppermute | solution.py:518
  16.3 1.4 %pair_sums.1 = (bf16[64,1280]{1,0:T(8,128)(2,1)S(1)}, bf16[64,1280]{1,0:T(8,128)(2,1)S(1)}, bf16[64,1280]{1,0:T(8,128)(2,1)S(1)}, bf16[64,1280]{1,0:T(8,128)(2,1)S(1)}) custom-call(f32[1,2560]{1,0:T(1,128)S(1)} %broadcast_in_dim.9.gate_ref, bf16[128,1408]{1,0:T(8,128)(2,1)S(1)} %get-tuple-element.36.refs_0_, ...), custom_call_target="tpu_custom_call" | custom-call | flops 167772160 | bytes 1966080 | tf_op jit(solution)/shard_map/pair_sums/pallas_call | solution.py:365
  18.2 1.7 %collective-permute-start.4 = (bf16[64,1280]{1,0:T(8,128)(2,1)S(1)}, bf16[64,1280]{1,0:T(8,128)(2,1)S(1)}, u32[]{:S(2)}, u32[]{:S(2)}) collective-permute-start(bf16[64,1280]{1,0:T(8,128)(2,1)S(1)} %get-tuple-element.44), channel_id=1, source_target_pairs={{0,16},{16,24},{24,8},{8,0},{1,17},{17,25},{25,9},{9,1},{2,18},{18... | collective-permute-start | bytes 491528 | tf_op jit(solution)/shard_map/ppermute | solution.py:518
  19.8 3.0 %attend_edges.1 = bf16[64,2560]{1,0:T(8,128)(2,1)S(1)} custom-call(bf16[128,2560]{1,0:T(8,128)(2,1)S(1)} %bitcast.33, bf16[128,2560]{1,0:T(8,128)(2,1)S(1)} %bitcast.26, bf16[128,2560]{1,0:T(8,128)(2,1)S(1)} %bitcast.30, f32[1,128]{1,0:T(1,128)S(1)} %get-tuple-element.46.code_ref, bf16[32,5248]{1,0:T(8,128)(2,1)} %collective-permute-done.7.one_ref, ...), custom_call_target="tpu_custom_call" | custom-call | flops 268435456 | bytes 1966080 | tf_op jit(solution)/shard_map/attend_edges/pallas_call | solution.py:281
  23.0 1.6 %collective-permute-start.10 = (bf16[64,1280]{1,0:T(8,128)(2,1)S(1)}, bf16[64,1280]{1,0:T(8,128)(2,1)S(1)}, u32[]{:S(2)}, u32[]{:S(2)}) collective-permute-start(bf16[64,1280]{1,0:T(8,128)(2,1)S(1)} %get-tuple-element.71), channel_id=1, source_target_pairs={{0,16},{16,24},{24,8},{8,0},{1,17},{17,25},{25,9},{9,1},{2,18},{18... | collective-permute-start | bytes 491528 | tf_op jit(solution)/shard_map/ppermute | solution.py:518
  25.7 1.7 %collective-permute-start.5 = (bf16[64,1280]{1,0:T(8,128)(2,1)S(1)}, bf16[64,1280]{1,0:T(8,128)(2,1)S(1)}, u32[]{:S(2)}, u32[]{:S(2)}) collective-permute-start(bf16[64,1280]{1,0:T(8,128)(2,1)S(1)} %get-tuple-element.73), channel_id=1, source_target_pairs={{0,16},{16,0},{8,24},{24,8},{1,17},{17,1},{9,25},{25,9},{2,18},{18... | collective-permute-start | bytes 491528 | tf_op jit(solution)/shard_map/ppermute | solution.py:518
  27.4 2.3 %collective-permute-done.10 = bf16[64,1280]{1,0:T(8,128)(2,1)S(1)} collective-permute-done((bf16[64,1280]{1,0:T(8,128)(2,1)S(1)}, bf16[64,1280]{1,0:T(8,128)(2,1)S(1)}, u32[]{:S(2)}, u32[]{:S(2)}) %collective-permute-start.10) | collective-permute-done | bytes 163872 | tf_op jit(solution)/shard_map/ppermute | solution.py:518
  29.8 1.4 %collective-permute-done.9 = bf16[64,1280]{1,0:T(8,128)(2,1)S(1)} collective-permute-done((bf16[64,1280]{1,0:T(8,128)(2,1)S(1)}, bf16[64,1280]{1,0:T(8,128)(2,1)S(1)}, u32[]{:S(2)}, u32[]{:S(2)}) %collective-permute-start.9) | collective-permute-done | bytes 163872 | tf_op jit(solution)/shard_map/ppermute | solution.py:518
  31.4 0.8 %collective-permute-start.12 = (bf16[64,1280]{1,0:T(8,128)(2,1)S(1)}, bf16[64,1280]{1,0:T(8,128)(2,1)S(1)}, u32[]{:S(2)}, u32[]{:S(2)}) collective-permute-start(bf16[64,1280]{1,0:T(8,128)(2,1)S(1)} %get-tuple-element.58), channel_id=1, source_target_pairs={{0,8},{8,0},{16,24},{24,16},{1,9},{9,1},{17,25},{25,17},{2,10},{10... | collective-permute-start | bytes 491528 | tf_op jit(solution)/shard_map/ppermute | solution.py:518
  32.6 1.9 %collective-permute-done.5 = bf16[64,1280]{1,0:T(8,128)(2,1)S(1)} collective-permute-done((bf16[64,1280]{1,0:T(8,128)(2,1)S(1)}, bf16[64,1280]{1,0:T(8,128)(2,1)S(1)}, u32[]{:S(2)}, u32[]{:S(2)}) %collective-permute-start.5) | collective-permute-done | bytes 163872 | tf_op jit(solution)/shard_map/ppermute | solution.py:518
  34.6 0.8 %relay_first.1 = (bf16[128,2560]{1,0:T(8,128)(2,1)}, f32[128,2560]{1,0:T(8,128)S(1)}, bf16[128,64]{1,0:T(8,128)(2,1)S(1)}) custom-call(f32[1,128]{1,0:T(1,128)S(1)} %get-tuple-element.86.row_ref, f32[1,2560]{1,0:T(1,128)S(1)} %broadcast_in_dim.9.gate_ref, bf16[64,1280]{1,0:T(8,128)(2,1)S(1)} %get-tuple-element.80.a_ref, ...), custom_call_target="tpu_custom_call" | custom-call | flops 83886080 | bytes 7864320 | tf_op jit(solution)/shard_map/relay_first/pallas_call | solution.py:413
  35.3 1.5 %collective-permute-done.12.got_ref = bf16[64,1280]{1,0:T(8,128)(2,1)S(1)} collective-permute-done((bf16[64,1280]{1,0:T(8,128)(2,1)S(1)}, bf16[64,1280]{1,0:T(8,128)(2,1)S(1)}, u32[]{:S(2)}, u32[]{:S(2)}) %collective-permute-start.12) | collective-permute-done | bytes 163872 | tf_op jit(solution)/shard_map/ppermute | solution.py:518
  36.8 1.0 %relay_last.2 = (bf16[128,2560]{1,0:T(8,128)(2,1)}, bf16[128,2560]{1,0:T(8,128)(2,1)}) custom-call(bf16[128,64]{1,0:T(8,128)(2,1)S(1)} %get-tuple-element.49.picks_ref, f32[1,2560]{1,0:T(1,128)S(1)} %broadcast_in_dim.9.gate_ref, bf16[64,1280]{1,0:T(8,128)(2,1)S(1)} %get-tuple-element.60.held_ref, ...), custom_call_target="tpu_custom_call", output_to_operand_aliasing={{0}: (6, {})} | custom-call | flops 41943040 | bytes 1966080 | tf_op jit(solution)/shard_map/relay_last/pallas_call | solution.py:473
  37.8 1.0 %relay_last.3 = (bf16[128,2560]{1,0:T(8,128)(2,1)}, bf16[128,2560]{1,0:T(8,128)(2,1)}) custom-call(bf16[128,64]{1,0:T(8,128)(2,1)S(1)} %get-tuple-element.49.picks_ref, f32[1,2560]{1,0:T(1,128)S(1)} %broadcast_in_dim.9.gate_ref, bf16[64,1280]{1,0:T(8,128)(2,1)S(1)} %get-tuple-element.70.held_ref, ...), custom_call_target="tpu_custom_call", output_to_operand_aliasing={{0}: (6, {}), {1}: (7, {})} | custom-call | flops 41943040 | bytes 1966080 | tf_op jit(solution)/shard_map/relay_last/pallas_call | solution.py:473
  (31 shorter events, 2.5 us)
Async XLA Ops:
  0.6 12.1 %collective-permute-start = (f32[1280]{0:T(1024)}, f32[1280]{0:T(1024)S(1)}, u32[]{:S(2)}, u32[]{:S(2)}) collective-permute-start(f32[1280]{0:T(1024)} %param.12), channel_id=1, source_target_pairs={{0,1},{1,0},{2,3},{3,2},{4,5},{5,4},{6,7},{7,6},{8,9},{9,8},{10,11... | collective-permute-start | bytes 15368 | tf_op jit(solution)/shard_map/ppermute | solution.py:497
  1.9 5.3 %copy-start = (bf16[1,1,128,2560]{3,2,1,0:T(8,128)(2,1)S(1)}, bf16[1,1,128,2560]{3,2,1,0:T(8,128)(2,1)}, u32[]{:S(2)}) copy-start(bf16[1,1,128,2560]{3,2,1,0:T(8,128)(2,1)} %param.8) | copy-start | bytes 1966084
  1.9 5.3 %copy-start.1 = (bf16[1,1,128,2560]{3,2,1,0:T(8,128)(2,1)S(1)}, bf16[1,1,128,2560]{3,2,1,0:T(8,128)(2,1)}, u32[]{:S(2)}) copy-start(bf16[1,1,128,2560]{3,2,1,0:T(8,128)(2,1)} %param.9) | copy-start | bytes 1966084
  3.1 8.0 %copy-start.2 = (bf16[1,1,128,2560]{3,2,1,0:T(8,128)(2,1)S(1)}, bf16[1,1,128,2560]{3,2,1,0:T(8,128)(2,1)}, u32[]{:S(2)}) copy-start(bf16[1,1,128,2560]{3,2,1,0:T(8,128)(2,1)} %param.7) | copy-start | bytes 1966084
  3.1 11.6 %collective-permute-start.1 = (bf16[128,1408]{1,0:T(8,128)(2,1)S(1)}, bf16[128,1408]{1,0:T(8,128)(2,1)S(1)}, u32[]{:S(2)}, u32[]{:S(2)}) collective-permute-start(bf16[128,1408]{1,0:T(8,128)(2,1)S(1)} %get-tuple-element.36.refs_0_), channel_id=1, source_target_pairs={{0,8},{8,0},{16,24},{24,16},{1,9},{9,1},{17,25},{25,17},{2,10},{10... | collective-permute-start | bytes 1081352 | tf_op jit(solution)/shard_map/ppermute | solution.py:518
  5.7 10.6 %collective-permute-start.2 = (bf16[128,1408]{1,0:T(8,128)(2,1)S(1)}, bf16[128,1408]{1,0:T(8,128)(2,1)}, u32[]{:S(2)}, u32[]{:S(2)}) collective-permute-start(bf16[128,1408]{1,0:T(8,128)(2,1)S(1)} %get-tuple-element.37.refs_2_), channel_id=1, source_target_pairs={{0,16},{16,0},{8,24},{24,8},{1,17},{17,1},{9,25},{25,9},{2,18},{18... | collective-permute-start | bytes 1081352 | tf_op jit(solution)/shard_map/ppermute | solution.py:518
  8.1 4.6 %copy-start.3 = (f32[1280]{0:T(1024)S(1)}, f32[1280]{0:T(1024)}, u32[]{:S(2)}) copy-start(f32[1280]{0:T(1024)} %param.12) | copy-start | bytes 15364
  8.1 11.7 %collective-permute-start.7 = (bf16[32,5248]{1,0:T(8,128)(2,1)}, bf16[32,5248]{1,0:T(8,128)(2,1)}, u32[]{:S(2)}, u32[]{:S(2)}) collective-permute-start(bf16[32,5248]{1,0:T(8,128)(2,1)} %get-tuple-element.47), channel_id=1, source_target_pairs={{0,2},{2,0},{4,6},{6,4},{1,3},{3,1},{5,7},{7,5},{8,10},{10,8},{12,... | collective-permute-start | bytes 1007624 | tf_op jit(solution)/shard_map/ppermute | solution.py:32
  9.7 10.1 %collective-permute-start.8 = (bf16[32,5248]{1,0:T(8,128)(2,1)}, bf16[32,5248]{1,0:T(8,128)(2,1)}, u32[]{:S(2)}, u32[]{:S(2)}) collective-permute-start(bf16[32,5248]{1,0:T(8,128)(2,1)} %get-tuple-element.48), channel_id=1, source_target_pairs={{2,4},{4,2},{3,5},{5,3},{10,12},{12,10},{11,13},{13,11},{18,20},{2... | collective-permute-start | bytes 1007624 | tf_op jit(solution)/shard_map/ppermute | solution.py:32
  17.8 7.4 %collective-permute-start.3 = (bf16[64,1280]{1,0:T(8,128)(2,1)S(1)}, bf16[64,1280]{1,0:T(8,128)(2,1)S(1)}, u32[]{:S(2)}, u32[]{:S(2)}) collective-permute-start(bf16[64,1280]{1,0:T(8,128)(2,1)S(1)} %get-tuple-element.42), channel_id=1, source_target_pairs={{0,8},{8,24},{24,16},{16,0},{1,9},{9,25},{25,17},{17,1},{2,10},{10... | collective-permute-start | bytes 491528 | tf_op jit(solution)/shard_map/ppermute | solution.py:518
  18.2 6.9 %collective-permute-start.4 = (bf16[64,1280]{1,0:T(8,128)(2,1)S(1)}, bf16[64,1280]{1,0:T(8,128)(2,1)S(1)}, u32[]{:S(2)}, u32[]{:S(2)}) collective-permute-start(bf16[64,1280]{1,0:T(8,128)(2,1)S(1)} %get-tuple-element.44), channel_id=1, source_target_pairs={{0,16},{16,24},{24,8},{8,0},{1,17},{17,25},{25,9},{9,1},{2,18},{18... | collective-permute-start | bytes 491528 | tf_op jit(solution)/shard_map/ppermute | solution.py:518
  23.0 6.8 %collective-permute-start.10 = (bf16[64,1280]{1,0:T(8,128)(2,1)S(1)}, bf16[64,1280]{1,0:T(8,128)(2,1)S(1)}, u32[]{:S(2)}, u32[]{:S(2)}) collective-permute-start(bf16[64,1280]{1,0:T(8,128)(2,1)S(1)} %get-tuple-element.71), channel_id=1, source_target_pairs={{0,16},{16,24},{24,8},{8,0},{1,17},{17,25},{25,9},{9,1},{2,18},{18... | collective-permute-start | bytes 491528 | tf_op jit(solution)/shard_map/ppermute | solution.py:518
  24.5 6.6 %collective-permute-start.9 = (bf16[64,1280]{1,0:T(8,128)(2,1)S(1)}, bf16[64,1280]{1,0:T(8,128)(2,1)S(1)}, u32[]{:S(2)}, u32[]{:S(2)}) collective-permute-start(bf16[64,1280]{1,0:T(8,128)(2,1)S(1)} %get-tuple-element.72), channel_id=1, source_target_pairs={{0,8},{8,24},{24,16},{16,0},{1,9},{9,25},{25,17},{17,1},{2,10},{10... | collective-permute-start | bytes 491528 | tf_op jit(solution)/shard_map/ppermute | solution.py:518
  25.3 7.3 %collective-permute-start.6 = (bf16[64,1280]{1,0:T(8,128)(2,1)S(1)}, bf16[64,1280]{1,0:T(8,128)(2,1)S(1)}, u32[]{:S(2)}, u32[]{:S(2)}) collective-permute-start(bf16[64,1280]{1,0:T(8,128)(2,1)S(1)} %get-tuple-element.64), channel_id=1, source_target_pairs={{0,8},{8,0},{16,24},{24,16},{1,9},{9,1},{17,25},{25,17},{2,10},{10... | collective-permute-start | bytes 491528 | tf_op jit(solution)/shard_map/ppermute | solution.py:518
  25.7 8.7 %collective-permute-start.5 = (bf16[64,1280]{1,0:T(8,128)(2,1)S(1)}, bf16[64,1280]{1,0:T(8,128)(2,1)S(1)}, u32[]{:S(2)}, u32[]{:S(2)}) collective-permute-start(bf16[64,1280]{1,0:T(8,128)(2,1)S(1)} %get-tuple-element.73), channel_id=1, source_target_pairs={{0,16},{16,0},{8,24},{24,8},{1,17},{17,1},{9,25},{25,9},{2,18},{18... | collective-permute-start | bytes 491528 | tf_op jit(solution)/shard_map/ppermute | solution.py:518
  31.4 5.4 %collective-permute-start.12 = (bf16[64,1280]{1,0:T(8,128)(2,1)S(1)}, bf16[64,1280]{1,0:T(8,128)(2,1)S(1)}, u32[]{:S(2)}, u32[]{:S(2)}) collective-permute-start(bf16[64,1280]{1,0:T(8,128)(2,1)S(1)} %get-tuple-element.58), channel_id=1, source_target_pairs={{0,8},{8,0},{16,24},{24,16},{1,9},{9,1},{17,25},{25,17},{2,10},{10... | collective-permute-start | bytes 491528 | tf_op jit(solution)/shard_map/ppermute | solution.py:518
  32.2 5.6 %collective-permute-start.11 = (bf16[64,1280]{1,0:T(8,128)(2,1)S(1)}, bf16[64,1280]{1,0:T(8,128)(2,1)S(1)}, u32[]{:S(2)}, u32[]{:S(2)}) collective-permute-start(bf16[64,1280]{1,0:T(8,128)(2,1)S(1)} %get-tuple-element.68), channel_id=1, source_target_pairs={{0,16},{16,0},{8,24},{24,8},{1,17},{17,1},{9,25},{25,9},{2,18},{18... | collective-permute-start | bytes 491528 | tf_op jit(solution)/shard_map/ppermute | solution.py:518

commit v15 on v14

--- a/solution.py
+++ b/solution.py
@@ -334,45 +334,38 @@
     return jnp.where(wanted == row, 1.0, 0.0)
 
 
-def sums_kernel(sizes, gate_ref, *refs):
-    group = lax.axis_index("grp")
+def sums_kernel(part, sizes, gate_ref, row_ref, mine_ref, theirs_ref, *out_refs):
     half = gate_ref.shape[1] // 2
-    count = len(sizes)
-    for n in range(2):
-        mine_ref, theirs_ref = refs[2 * n : 2 * n + 2]
-        picks, rows = [], []
-        for ref in (mine_ref, theirs_ref):
-            place = ref[:, half : half + LANES].astype(jnp.float32).T[:1]
-            picks.append(selector(place).astype(jnp.bfloat16))
-            rows.append(ref[:, :half])
-        summed = jnp.dot(
-            jnp.concatenate(picks, axis=1),
-            jnp.concatenate(rows, axis=0),
-            preferred_element_type=jnp.float32,
-        )
-        term = gate_ref[:, n * half : (n + 1) * half] * summed
-        own = jnp.where(group == n + 1, 1.0, 0.0)
-        term = (term + own * rows[1].astype(jnp.float32)).astype(jnp.bfloat16)
-        at = 0
-        for ref, size in zip(refs[4 + n * count : 4 + (n + 1) * count], sizes):
-            ref[...] = term[at : at + size]
-            at += size
-
-
-def pair_sums(gate, parts, sizes):
-    tokens, width = parts[0].shape[0], gate.shape[1]
-    outs = [jax.ShapeDtypeStruct((size, width // 2), jnp.bfloat16) for size in sizes] * 2
+    place = theirs_ref[:, half:].astype(jnp.float32).T[:1]
+    picks = [selector(row).astype(jnp.bfloat16) for row in (row_ref[...], place)]
+    theirs = theirs_ref[:, :half]
+    summed = jnp.dot(
+        jnp.concatenate(picks, axis=1),
+        jnp.concatenate((mine_ref[:, :half], theirs), axis=0),
+        preferred_element_type=jnp.float32,
+    )
+    own = jnp.where(lax.axis_index("grp") == part + 1, 1.0, 0.0)
+    term = gate_ref[:, part * half : (part + 1) * half] * summed + own * theirs.astype(jnp.float32)
+    term = term.astype(jnp.bfloat16)
+    at = 0
+    for ref, size in zip(out_refs, sizes):
+        ref[...] = term[at : at + size]
+        at += size
+
+
+def pair_sums(part, gate, rows, mine, theirs, sizes):
+    tokens, half = mine.shape[0], gate.shape[1] // 2
     return pl.pallas_call(
-        functools.partial(sums_kernel, sizes),
-        in_specs=[VMEM] * 5,
-        out_specs=[VMEM] * len(outs),
-        out_shape=outs,
+        functools.partial(sums_kernel, part, sizes),
+        in_specs=[VMEM] * 4,
+        out_specs=[VMEM] * len(sizes),
+        out_shape=[jax.ShapeDtypeStruct((size, half), jnp.bfloat16) for size in sizes],
         compiler_params=PARAMS,
         cost_estimate=pl.CostEstimate(
-            flops=4 * tokens * tokens * width, bytes_accessed=6 * tokens * width, transcendentals=0
+            flops=4 * tokens * tokens * half, bytes_accessed=6 * tokens * half, transcendentals=0
         ),
         name="pair_sums",
-    )(gate, *parts)
+    )(gate, rows, mine, theirs)
 
 
 def piece_spots(tokens, reach, piece):
@@ -537,7 +530,10 @@
         halos.append(shifted(tail[most - count :], "seq", hop))
         halos.append(shifted(head[:count], "seq", -hop))
     sizes = [piece.shape[0] for piece in own] + [min(tokens, 2 * reach)]
-    sums = pair_sums(gate, (sent_a, got_a, sent_b, got_b), sizes)
+    sums = [
+        *pair_sums(0, gate, rows, sent_a, got_a, sizes),
+        *pair_sums(1, gate, rows, sent_b, got_b, sizes),
+    ]
     count = len(sizes)
 
     def outgoing(piece, sum_a, sum_b):

time: 39 us -> 38.9 us (level); the launches traced: 38.8 us -> 38.2 us
  waiting for transfers between devices: 10.6 us -> 8.03 us
  starting transfers between devices: 15 us -> 16.8 us
    ppermute x10, waiting for transfers between devices: 10.6 us -> 8.02 us  [local(): send = lambda block, route: lax.ppermute(block, 'grp', route)]
    ppermute x10, starting transfers between devices: 11.6 us -> 13.3 us  [local(): send = lambda block, route: lax.ppermute(block, 'grp', route)]
    pallas_call x1 -> x2, Pallas kernels: 1.38 us -> 1.57 us  [pair_sums(): pl.pallas_call(functools.partial(sums_kernel, part, sizes), in_specs=[VME...]
  transfers between devices with their start and end apart: 13 -> 13, of which waited for: 6 -> 6; matrix products, arithmetic and copies ran while one was open for 4% -> 3% of each run, Pallas kernels for 26% -> 26%
where the time goes in v15:
time: 38.9 us; the launch traced here: 38.2 us
  starting transfers between devices  16.8 us (43%)
  Pallas kernels  11.1 us (29%)
  waiting for transfers between devices  8.03 us (21%)
  other arithmetic  1.3 us (3%)
  between operations  0.84 us (2%)
    ppermute x10, starting transfers between devices, local(): send = lambda block, route: lax.ppermute(block, 'grp', route)  13.3 us
    ppermute x10, waiting for transfers between devices, local(): send = lambda block, route: lax.ppermute(block, 'grp', route)  8.02 us
    pallas_call x1, Pallas kernels, attend_edges(): pl.pallas_call(functools.partial(kernel, reach), in_specs=[VMEM] * len(op...  3.05 us
    ppermute x2, starting transfers between devices, paired(): return lax.ppermute(block, axis, route)  2.98 us
    pallas_call x2, Pallas kernels, relay_last(): pl.pallas_call(functools.partial(relay_last_kernel, part, chunks, first_r...  1.99 us
    pallas_call x1, Pallas kernels, attend_middle(): pl.pallas_call(functools.partial(middle_kernel, reach), in_specs=[VMEM] *...  1.6 us
    pallas_call x2, Pallas kernels, pair_sums(): pl.pallas_call(functools.partial(sums_kernel, part, sizes), in_specs=[VME...  1.57 us
    pallas_call x1, Pallas kernels, pack_grads(): pl.pallas_call(pack_grads_kernel, in_specs=[far, VMEM] + [far] * len(othe...  1.19 us
  transfers between devices with their start and end apart: 13, of which 6 were waited for; matrix products, arithmetic and copies ran while one was open for 3% of the time, Pallas kernels for 26%

profile of v15, /device:TPU:0, one launch (start us, length us, event | category | flops | bytes accessed | tf_op | source)
XLA Modules:
  0.0 38.2 jit_solution(17650849148769296011)
XLA Ops:
  0.6 0.5 %collective-permute-start = (f32[1280]{0:T(1024)}, f32[1280]{0:T(1024)S(1)}, u32[]{:S(2)}, u32[]{:S(2)}) collective-permute-start(f32[1280]{0:T(1024)} %param.12), channel_id=1, source_target_pairs={{0,1},{1,0},{2,3},{3,2},{4,5},{5,4},{6,7},{7,6},{8,9},{9,8},{10,11... | collective-permute-start | bytes 15368 | tf_op jit(solution)/shard_map/ppermute | solution.py:490
  1.1 0.7 %and_select_fusion = (s32[1,128]{1,0:T(1,128)S(1)}, s32[1,128]{1,0:T(1,128)S(1)}) fusion(s32[1,1,128]{2,1,0:T(1,128)} %param.11, s32[1,1,128]{2,1,0:T(1,128)} %param.10), kind=kLoop, calls=%fused_computation.26 | loop fusion | flops 2816 | bytes 2048 | tf_op jit(solution)/shard_map/jit(remainder)/select_n | solution.py:515
  1.9 1.2 %pack_grads.1 = (bf16[128,1408]{1,0:T(8,128)(2,1)S(1)}, bf16[128,1408]{1,0:T(8,128)(2,1)S(1)}) custom-call(bf16[128,2560]{1,0:T(8,128)(2,1)} %bitcast.35, f32[2,128]{1,0:T(2,128)S(1)} %add_convert_fusion.4.mark_ref, bf16[128,2560]{1,0:T(8,128)(2,1)} %bitcast.31, bf16[128,2560]{1,0:T(8,128)(2,1)} %bitcast.23, bf16[128,2560]{1,0:T(8,128)(2,1)} %bitcast.27), custom_call_target="tpu_custom_call" | custom-call | bytes 1310720 | tf_op jit(solution)/shard_map/pack_grads/pallas_call | solution.py:319
  3.1 2.6 %collective-permute-start.1 = (bf16[128,1408]{1,0:T(8,128)(2,1)S(1)}, bf16[128,1408]{1,0:T(8,128)(2,1)}, u32[]{:S(2)}, u32[]{:S(2)}) collective-permute-start(bf16[128,1408]{1,0:T(8,128)(2,1)S(1)} %get-tuple-element.36.mine_ref), channel_id=1, source_target_pairs={{0,8},{8,0},{16,24},{24,16},{1,9},{9,1},{17,25},{25,17},{2,10},{10... | collective-permute-start | bytes 1081352 | tf_op jit(solution)/shard_map/ppermute | solution.py:511
  5.7 1.5 %collective-permute-start.2 = (bf16[128,1408]{1,0:T(8,128)(2,1)S(1)}, bf16[128,1408]{1,0:T(8,128)(2,1)S(1)}, u32[]{:S(2)}, u32[]{:S(2)}) collective-permute-start(bf16[128,1408]{1,0:T(8,128)(2,1)S(1)} %get-tuple-element.39.mine_ref), channel_id=1, source_target_pairs={{0,16},{16,0},{8,24},{24,8},{1,17},{17,1},{9,25},{25,9},{2,18},{18... | collective-permute-start | bytes 1081352 | tf_op jit(solution)/shard_map/ppermute | solution.py:511
  7.2 0.9 %pack_ends.1 = (bf16[32,5248]{1,0:T(8,128)(2,1)}, bf16[32,5248]{1,0:T(8,128)(2,1)}) custom-call(bf16[128,2560]{1,0:T(8,128)(2,1)S(1)} %bitcast.24, bf16[128,2560]{1,0:T(8,128)(2,1)S(1)} %bitcast.28, f32[1,128]{1,0:T(1,128)S(1)} %get-tuple-element.46.code_ref), custom_call_target="tpu_custom_call" | custom-call | bytes 1310720 | tf_op jit(solution)/shard_map/pack_ends/pallas_call | solution.py:247
  8.1 1.6 %collective-permute-start.7 = (bf16[32,5248]{1,0:T(8,128)(2,1)}, bf16[32,5248]{1,0:T(8,128)(2,1)}, u32[]{:S(2)}, u32[]{:S(2)}) collective-permute-start(bf16[32,5248]{1,0:T(8,128)(2,1)} %get-tuple-element.47), channel_id=1, source_target_pairs={{0,2},{2,0},{4,6},{6,4},{1,3},{3,1},{5,7},{7,5},{8,10},{10,8},{12,... | collective-permute-start | bytes 1007624 | tf_op jit(solution)/shard_map/ppermute | solution.py:32
  9.7 1.4 %collective-permute-start.8 = (bf16[32,5248]{1,0:T(8,128)(2,1)}, bf16[32,5248]{1,0:T(8,128)(2,1)}, u32[]{:S(2)}, u32[]{:S(2)}) collective-permute-start(bf16[32,5248]{1,0:T(8,128)(2,1)} %get-tuple-element.48), channel_id=1, source_target_pairs={{2,4},{4,2},{3,5},{5,3},{10,12},{12,10},{11,13},{13,11},{18,20},{2... | collective-permute-start | bytes 1007624 | tf_op jit(solution)/shard_map/ppermute | solution.py:32
  11.1 1.6 %attend_middle.1 = bf16[64,2560]{1,0:T(8,128)(2,1)S(1)} custom-call(bf16[128,2560]{1,0:T(8,128)(2,1)S(1)} %bitcast.32, bf16[128,2560]{1,0:T(8,128)(2,1)S(1)} %bitcast.25, bf16[128,2560]{1,0:T(8,128)(2,1)S(1)} %bitcast.29, f32[1,128]{1,0:T(1,128)S(1)} %get-tuple-element.46.code_ref), custom_call_target="tpu_custom_call" | custom-call | flops 268435456 | bytes 1966080 | tf_op jit(solution)/shard_map/attend_middle/pallas_call | solution.py:260
  12.8 2.0 %collective-permute-done.1.theirs_ref = bf16[128,1408]{1,0:T(8,128)(2,1)} collective-permute-done((bf16[128,1408]{1,0:T(8,128)(2,1)S(1)}, bf16[128,1408]{1,0:T(8,128)(2,1)}, u32[]{:S(2)}, u32[]{:S(2)}) %collective-permute-start.1) | collective-permute-done | bytes 360480 | tf_op jit(solution)/shard_map/ppermute | solution.py:511
  14.8 1.3 %pair_sums.2 = (bf16[64,1280]{1,0:T(8,128)(2,1)S(1)}, bf16[64,1280]{1,0:T(8,128)(2,1)S(1)}) custom-call(f32[1,2560]{1,0:T(1,128)S(1)} %broadcast_in_dim.9.gate_ref, f32[1,128]{1,0:T(1,128)S(1)} %get-tuple-element.86.row_ref, bf16[128,1408]{1,0:T(8,128)(2,1)S(1)} %get-tuple-element.36.mine_ref, bf16[128,1408]{1,0:T(8,128)(2,1)} %collective-permute-done.1.theirs_ref), custom_call_target="tpu_custom_call" | custom-call | flops 83886080 | bytes 983040 | tf_op jit(solution)/shard_map/pair_sums/pallas_call | solution.py:358
  16.5 1.7 %collective-permute-start.3 = (bf16[64,1280]{1,0:T(8,128)(2,1)S(1)}, bf16[64,1280]{1,0:T(8,128)(2,1)S(1)}, u32[]{:S(2)}, u32[]{:S(2)}) collective-permute-start(bf16[64,1280]{1,0:T(8,128)(2,1)S(1)} %get-tuple-element.42), channel_id=1, source_target_pairs={{0,8},{8,24},{24,16},{16,0},{1,9},{9,25},{25,17},{17,1},{2,10},{10... | collective-permute-start | bytes 491528 | tf_op jit(solution)/shard_map/ppermute | solution.py:511
  18.6 3.0 %attend_edges.1 = bf16[64,2560]{1,0:T(8,128)(2,1)S(1)} custom-call(bf16[128,2560]{1,0:T(8,128)(2,1)S(1)} %bitcast.33, bf16[128,2560]{1,0:T(8,128)(2,1)S(1)} %bitcast.26, bf16[128,2560]{1,0:T(8,128)(2,1)S(1)} %bitcast.30, f32[1,128]{1,0:T(1,128)S(1)} %get-tuple-element.46.code_ref, bf16[32,5248]{1,0:T(8,128)(2,1)} %collective-permute-done.7.one_ref, ...), custom_call_target="tpu_custom_call" | custom-call | flops 268435456 | bytes 1966080 | tf_op jit(solution)/shard_map/attend_edges/pallas_call | solution.py:281
  21.8 1.8 %collective-permute-start.10 = (bf16[64,1280]{1,0:T(8,128)(2,1)S(1)}, bf16[64,1280]{1,0:T(8,128)(2,1)S(1)}, u32[]{:S(2)}, u32[]{:S(2)}) collective-permute-start(bf16[64,1280]{1,0:T(8,128)(2,1)S(1)} %get-tuple-element.71), channel_id=1, source_target_pairs={{0,16},{16,24},{24,8},{8,0},{1,17},{17,25},{25,9},{9,1},{2,18},{18... | collective-permute-start | bytes 491528 | tf_op jit(solution)/shard_map/ppermute | solution.py:511
  24.1 1.7 %collective-permute-start.6 = (bf16[64,1280]{1,0:T(8,128)(2,1)S(1)}, bf16[64,1280]{1,0:T(8,128)(2,1)S(1)}, u32[]{:S(2)}, u32[]{:S(2)}) collective-permute-start(bf16[64,1280]{1,0:T(8,128)(2,1)S(1)} %get-tuple-element.64), channel_id=1, source_target_pairs={{0,8},{8,0},{16,24},{24,16},{1,9},{9,1},{17,25},{25,17},{2,10},{10... | collective-permute-start | bytes 491528 | tf_op jit(solution)/shard_map/ppermute | solution.py:511
  25.8 1.5 %collective-permute-start.5 = (bf16[64,1280]{1,0:T(8,128)(2,1)S(1)}, bf16[64,1280]{1,0:T(8,128)(2,1)S(1)}, u32[]{:S(2)}, u32[]{:S(2)}) collective-permute-start(bf16[64,1280]{1,0:T(8,128)(2,1)S(1)} %get-tuple-element.73), channel_id=1, source_target_pairs={{0,16},{16,0},{8,24},{24,8},{1,17},{17,1},{9,25},{25,9},{2,18},{18... | collective-permute-start | bytes 491528 | tf_op jit(solution)/shard_map/ppermute | solution.py:511
  27.4 1.6 %collective-permute-done.10 = bf16[64,1280]{1,0:T(8,128)(2,1)S(1)} collective-permute-done((bf16[64,1280]{1,0:T(8,128)(2,1)S(1)}, bf16[64,1280]{1,0:T(8,128)(2,1)S(1)}, u32[]{:S(2)}, u32[]{:S(2)}) %collective-permute-start.10) | collective-permute-done | bytes 163872 | tf_op jit(solution)/shard_map/ppermute | solution.py:511
  29.0 1.6 %collective-permute-done.9 = bf16[64,1280]{1,0:T(8,128)(2,1)S(1)} collective-permute-done((bf16[64,1280]{1,0:T(8,128)(2,1)S(1)}, bf16[64,1280]{1,0:T(8,128)(2,1)S(1)}, u32[]{:S(2)}, u32[]{:S(2)}) %collective-permute-start.9) | collective-permute-done | bytes 163872 | tf_op jit(solution)/shard_map/ppermute | solution.py:511
  31.3 1.3 %collective-permute-start.11 = (bf16[64,1280]{1,0:T(8,128)(2,1)S(1)}, bf16[64,1280]{1,0:T(8,128)(2,1)S(1)}, u32[]{:S(2)}, u32[]{:S(2)}) collective-permute-start(bf16[64,1280]{1,0:T(8,128)(2,1)S(1)} %get-tuple-element.68), channel_id=1, source_target_pairs={{0,16},{16,0},{8,24},{24,8},{1,17},{17,1},{9,25},{25,9},{2,18},{18... | collective-permute-start | bytes 491528 | tf_op jit(solution)/shard_map/ppermute | solution.py:511
  32.6 1.2 %collective-permute-done.5 = bf16[64,1280]{1,0:T(8,128)(2,1)S(1)} collective-permute-done((bf16[64,1280]{1,0:T(8,128)(2,1)S(1)}, bf16[64,1280]{1,0:T(8,128)(2,1)S(1)}, u32[]{:S(2)}, u32[]{:S(2)}) %collective-permute-start.5) | collective-permute-done | bytes 163872 | tf_op jit(solution)/shard_map/ppermute | solution.py:511
  33.9 0.8 %relay_first.1 = (bf16[128,2560]{1,0:T(8,128)(2,1)}, f32[128,2560]{1,0:T(8,128)S(1)}, bf16[128,64]{1,0:T(8,128)(2,1)S(1)}) custom-call(f32[1,128]{1,0:T(1,128)S(1)} %get-tuple-element.86.row_ref, f32[1,2560]{1,0:T(1,128)S(1)} %broadcast_in_dim.9.gate_ref, bf16[64,1280]{1,0:T(8,128)(2,1)S(1)} %get-tuple-element.80.a_ref, ...), custom_call_target="tpu_custom_call" | custom-call | flops 83886080 | bytes 7864320 | tf_op jit(solution)/shard_map/relay_first/pallas_call | solution.py:406
  34.6 1.5 %collective-permute-done.12.got_ref = bf16[64,1280]{1,0:T(8,128)(2,1)S(1)} collective-permute-done((bf16[64,1280]{1,0:T(8,128)(2,1)S(1)}, bf16[64,1280]{1,0:T(8,128)(2,1)S(1)}, u32[]{:S(2)}, u32[]{:S(2)}) %collective-permute-start.12) | collective-permute-done | bytes 163872 | tf_op jit(solution)/shard_map/ppermute | solution.py:511
  36.1 1.0 %relay_last.2 = (bf16[128,2560]{1,0:T(8,128)(2,1)}, bf16[128,2560]{1,0:T(8,128)(2,1)}) custom-call(bf16[128,64]{1,0:T(8,128)(2,1)S(1)} %get-tuple-element.49.picks_ref, f32[1,2560]{1,0:T(1,128)S(1)} %broadcast_in_dim.9.gate_ref, bf16[64,1280]{1,0:T(8,128)(2,1)S(1)} %get-tuple-element.60.held_ref, ...), custom_call_target="tpu_custom_call", output_to_operand_aliasing={{0}: (6, {})} | custom-call | flops 41943040 | bytes 1966080 | tf_op jit(solution)/shard_map/relay_last/pallas_call | solution.py:466
  37.2 1.0 %relay_last.3 = (bf16[128,2560]{1,0:T(8,128)(2,1)}, bf16[128,2560]{1,0:T(8,128)(2,1)}) custom-call(bf16[128,64]{1,0:T(8,128)(2,1)S(1)} %get-tuple-element.49.picks_ref, f32[1,2560]{1,0:T(1,128)S(1)} %broadcast_in_dim.9.gate_ref, bf16[64,1280]{1,0:T(8,128)(2,1)S(1)} %get-tuple-element.70.held_ref, ...), custom_call_target="tpu_custom_call", output_to_operand_aliasing={{0}: (6, {}), {1}: (7, {})} | custom-call | flops 41943040 | bytes 1966080 | tf_op jit(solution)/shard_map/relay_last/pallas_call | solution.py:466
  (32 shorter events, 2.2 us)
Async XLA Ops:
  0.6 12.1 %collective-permute-start = (f32[1280]{0:T(1024)}, f32[1280]{0:T(1024)S(1)}, u32[]{:S(2)}, u32[]{:S(2)}) collective-permute-start(f32[1280]{0:T(1024)} %param.12), channel_id=1, source_target_pairs={{0,1},{1,0},{2,3},{3,2},{4,5},{5,4},{6,7},{7,6},{8,9},{9,8},{10,11... | collective-permute-start | bytes 15368 | tf_op jit(solution)/shard_map/ppermute | solution.py:490
  1.9 5.3 %copy-start = (bf16[1,1,128,2560]{3,2,1,0:T(8,128)(2,1)S(1)}, bf16[1,1,128,2560]{3,2,1,0:T(8,128)(2,1)}, u32[]{:S(2)}) copy-start(bf16[1,1,128,2560]{3,2,1,0:T(8,128)(2,1)} %param.8) | copy-start | bytes 1966084
  1.9 5.3 %copy-start.1 = (bf16[1,1,128,2560]{3,2,1,0:T(8,128)(2,1)S(1)}, bf16[1,1,128,2560]{3,2,1,0:T(8,128)(2,1)}, u32[]{:S(2)}) copy-start(bf16[1,1,128,2560]{3,2,1,0:T(8,128)(2,1)} %param.9) | copy-start | bytes 1966084
  3.1 8.0 %copy-start.2 = (bf16[1,1,128,2560]{3,2,1,0:T(8,128)(2,1)S(1)}, bf16[1,1,128,2560]{3,2,1,0:T(8,128)(2,1)}, u32[]{:S(2)}) copy-start(bf16[1,1,128,2560]{3,2,1,0:T(8,128)(2,1)} %param.7) | copy-start | bytes 1966084
  3.1 11.7 %collective-permute-start.1 = (bf16[128,1408]{1,0:T(8,128)(2,1)S(1)}, bf16[128,1408]{1,0:T(8,128)(2,1)}, u32[]{:S(2)}, u32[]{:S(2)}) collective-permute-start(bf16[128,1408]{1,0:T(8,128)(2,1)S(1)} %get-tuple-element.36.mine_ref), channel_id=1, source_target_pairs={{0,8},{8,0},{16,24},{24,16},{1,9},{9,1},{17,25},{25,17},{2,10},{10... | collective-permute-start | bytes 1081352 | tf_op jit(solution)/shard_map/ppermute | solution.py:511
  5.7 10.5 %collective-permute-start.2 = (bf16[128,1408]{1,0:T(8,128)(2,1)S(1)}, bf16[128,1408]{1,0:T(8,128)(2,1)S(1)}, u32[]{:S(2)}, u32[]{:S(2)}) collective-permute-start(bf16[128,1408]{1,0:T(8,128)(2,1)S(1)} %get-tuple-element.39.mine_ref), channel_id=1, source_target_pairs={{0,16},{16,0},{8,24},{24,8},{1,17},{17,1},{9,25},{25,9},{2,18},{18... | collective-permute-start | bytes 1081352 | tf_op jit(solution)/shard_map/ppermute | solution.py:511
  8.1 4.6 %copy-start.3 = (f32[1280]{0:T(1024)S(1)}, f32[1280]{0:T(1024)}, u32[]{:S(2)}) copy-start(f32[1280]{0:T(1024)} %param.12) | copy-start | bytes 15364
  8.1 10.5 %collective-permute-start.7 = (bf16[32,5248]{1,0:T(8,128)(2,1)}, bf16[32,5248]{1,0:T(8,128)(2,1)}, u32[]{:S(2)}, u32[]{:S(2)}) collective-permute-start(bf16[32,5248]{1,0:T(8,128)(2,1)} %get-tuple-element.47), channel_id=1, source_target_pairs={{0,2},{2,0},{4,6},{6,4},{1,3},{3,1},{5,7},{7,5},{8,10},{10,8},{12,... | collective-permute-start | bytes 1007624 | tf_op jit(solution)/shard_map/ppermute | solution.py:32
  9.7 8.9 %collective-permute-start.8 = (bf16[32,5248]{1,0:T(8,128)(2,1)}, bf16[32,5248]{1,0:T(8,128)(2,1)}, u32[]{:S(2)}, u32[]{:S(2)}) collective-permute-start(bf16[32,5248]{1,0:T(8,128)(2,1)} %get-tuple-element.48), channel_id=1, source_target_pairs={{2,4},{4,2},{3,5},{5,3},{10,12},{12,10},{11,13},{13,11},{18,20},{2... | collective-permute-start | bytes 1007624 | tf_op jit(solution)/shard_map/ppermute | solution.py:32
  16.5 7.3 %collective-permute-start.3 = (bf16[64,1280]{1,0:T(8,128)(2,1)S(1)}, bf16[64,1280]{1,0:T(8,128)(2,1)S(1)}, u32[]{:S(2)}, u32[]{:S(2)}) collective-permute-start(bf16[64,1280]{1,0:T(8,128)(2,1)S(1)} %get-tuple-element.42), channel_id=1, source_target_pairs={{0,8},{8,24},{24,16},{16,0},{1,9},{9,25},{25,17},{17,1},{2,10},{10... | collective-permute-start | bytes 491528 | tf_op jit(solution)/shard_map/ppermute | solution.py:511
  18.3 5.6 %collective-permute-start.4 = (bf16[64,1280]{1,0:T(8,128)(2,1)S(1)}, bf16[64,1280]{1,0:T(8,128)(2,1)S(1)}, u32[]{:S(2)}, u32[]{:S(2)}) collective-permute-start(bf16[64,1280]{1,0:T(8,128)(2,1)S(1)} %get-tuple-element.44), channel_id=1, source_target_pairs={{0,16},{16,24},{24,8},{8,0},{1,17},{17,25},{25,9},{9,1},{2,18},{18... | collective-permute-start | bytes 491528 | tf_op jit(solution)/shard_map/ppermute | solution.py:511
  21.8 7.2 %collective-permute-start.10 = (bf16[64,1280]{1,0:T(8,128)(2,1)S(1)}, bf16[64,1280]{1,0:T(8,128)(2,1)S(1)}, u32[]{:S(2)}, u32[]{:S(2)}) collective-permute-start(bf16[64,1280]{1,0:T(8,128)(2,1)S(1)} %get-tuple-element.71), channel_id=1, source_target_pairs={{0,16},{16,24},{24,8},{8,0},{1,17},{17,25},{25,9},{9,1},{2,18},{18... | collective-permute-start | bytes 491528 | tf_op jit(solution)/shard_map/ppermute | solution.py:511
  23.5 7.0 %collective-permute-start.9 = (bf16[64,1280]{1,0:T(8,128)(2,1)S(1)}, bf16[64,1280]{1,0:T(8,128)(2,1)S(1)}, u32[]{:S(2)}, u32[]{:S(2)}) collective-permute-start(bf16[64,1280]{1,0:T(8,128)(2,1)S(1)} %get-tuple-element.72), channel_id=1, source_target_pairs={{0,8},{8,24},{24,16},{16,0},{1,9},{9,25},{25,17},{17,1},{2,10},{10... | collective-permute-start | bytes 491528 | tf_op jit(solution)/shard_map/ppermute | solution.py:511
  24.1 8.5 %collective-permute-start.6 = (bf16[64,1280]{1,0:T(8,128)(2,1)S(1)}, bf16[64,1280]{1,0:T(8,128)(2,1)S(1)}, u32[]{:S(2)}, u32[]{:S(2)}) collective-permute-start(bf16[64,1280]{1,0:T(8,128)(2,1)S(1)} %get-tuple-element.64), channel_id=1, source_target_pairs={{0,8},{8,0},{16,24},{24,16},{1,9},{9,1},{17,25},{25,17},{2,10},{10... | collective-permute-start | bytes 491528 | tf_op jit(solution)/shard_map/ppermute | solution.py:511
  25.8 7.9 %collective-permute-start.5 = (bf16[64,1280]{1,0:T(8,128)(2,1)S(1)}, bf16[64,1280]{1,0:T(8,128)(2,1)S(1)}, u32[]{:S(2)}, u32[]{:S(2)}) collective-permute-start(bf16[64,1280]{1,0:T(8,128)(2,1)S(1)} %get-tuple-element.73), channel_id=1, source_target_pairs={{0,16},{16,0},{8,24},{24,8},{1,17},{17,1},{9,25},{25,9},{2,18},{18... | collective-permute-start | bytes 491528 | tf_op jit(solution)/shard_map/ppermute | solution.py:511
  30.8 5.4 %collective-permute-start.12 = (bf16[64,1280]{1,0:T(8,128)(2,1)S(1)}, bf16[64,1280]{1,0:T(8,128)(2,1)S(1)}, u32[]{:S(2)}, u32[]{:S(2)}) collective-permute-start(bf16[64,1280]{1,0:T(8,128)(2,1)S(1)} %get-tuple-element.58), channel_id=1, source_target_pairs={{0,8},{8,0},{16,24},{24,16},{1,9},{9,1},{17,25},{25,17},{2,10},{10... | collective-permute-start | bytes 491528 | tf_op jit(solution)/shard_map/ppermute | solution.py:511
  31.3 5.9 %collective-permute-start.11 = (bf16[64,1280]{1,0:T(8,128)(2,1)S(1)}, bf16[64,1280]{1,0:T(8,128)(2,1)S(1)}, u32[]{:S(2)}, u32[]{:S(2)}) collective-permute-start(bf16[64,1280]{1,0:T(8,128)(2,1)S(1)} %get-tuple-element.68), channel_id=1, source_target_pairs={{0,16},{16,0},{8,24},{24,8},{1,17},{17,1},{9,25},{25,9},{2,18},{18... | collective-permute-start | bytes 491528 | tf_op jit(solution)/shard_map/ppermute | solution.py:511

commit v16 on v15

--- a/solution.py
+++ b/solution.py
@@ -164,7 +164,7 @@
         store_period(base, mixed_period(base, scores, sets, period), out_ref)
 
 
-def sides_kernel(reach, q_ref, k_ref, v_ref, code_ref, one_ref, two_ref, *refs):
+def sides_kernel(reach, q_ref, k_ref, v_ref, code_ref, two_ref, one_ref, *refs):
     out_ref, keys, values, codes = refs
     tokens, width = q_ref.shape
     near = 2 * reach
@@ -523,7 +523,8 @@
     code, end_one, end_two = lax.optimization_barrier((code, end_one, end_two))
     own = [attend_middle(queries, keys, values, code, reach)] if tokens > 2 * reach else []
     gate = whole_gate(control_gate)[None]
-    halos = [paired(end_one, "seq", 0), paired(end_two, "seq", 1)]
+    inner = paired(end_two, "seq", 1)
+    halos = [inner, paired(end_one, "seq", 0)]
     for hop in range(2, hops + 1):
         count = min(tokens, reach - (hop - 1) * tokens)
         tail, head = jnp.where(even, end_one, end_two), jnp.where(even, end_two, end_one)

time: 38.9 us -> 40.6 us (1.044); the launches traced: 38.2 us -> 40.3 us
  waiting for transfers between devices: 8.03 us -> 9.63 us
  starting transfers between devices: 16.8 us -> 17.4 us
    ppermute x2, waiting for transfers between devices: 0.01 us -> 2.58 us  [paired(): return lax.ppermute(block, axis, route)]
    ppermute x2, starting transfers between devices: 2.98 us -> 5.25 us  [paired(): return lax.ppermute(block, axis, route)]
    ppermute x10, starting transfers between devices: 13.3 us -> 11.6 us  [local(): send = lambda block, route: lax.ppermute(block, 'grp', route)]
    ppermute x10, waiting for transfers between devices: 8.02 us -> 7.04 us  [local(): send = lambda block, route: lax.ppermute(block, 'grp', route)]
  transfers between devices with their start and end apart: 13 -> 13, of which waited for: 6 -> 6; matrix products, arithmetic and copies ran while one was open for 3% -> 3% of each run, Pallas kernels for 26% -> 25%
where the time goes in v16:
time: 40.6 us; the launch traced here: 40.3 us
  starting transfers between devices  17.4 us (43%)
  Pallas kernels  11.1 us (27%)
  waiting for transfers between devices  9.63 us (24%)
  other arithmetic  1.3 us (3%)
  between operations  0.85 us (2%)
    ppermute x10, starting transfers between devices, local(): send = lambda block, route: lax.ppermute(block, 'grp', route)  11.6 us
    ppermute x10, waiting for transfers between devices, local(): send = lambda block, route: lax.ppermute(block, 'grp', route)  7.04 us
    ppermute x2, starting transfers between devices, paired(): return lax.ppermute(block, axis, route)  5.25 us
    pallas_call x1, Pallas kernels, attend_edges(): pl.pallas_call(functools.partial(kernel, reach), in_specs=[VMEM] * len(op...  3.05 us
    ppermute x2, waiting for transfers between devices, paired(): return lax.ppermute(block, axis, route)  2.58 us
    pallas_call x2, Pallas kernels, relay_last(): pl.pallas_call(functools.partial(relay_last_kernel, part, chunks, first_r...  1.98 us
    pallas_call x1, Pallas kernels, attend_middle(): pl.pallas_call(functools.partial(middle_kernel, reach), in_specs=[VMEM] *...  1.61 us
    pallas_call x2, Pallas kernels, pair_sums(): pl.pallas_call(functools.partial(sums_kernel, part, sizes), in_specs=[VME...  1.57 us
  transfers between devices with their start and end apart: 13, of which 6 were waited for; matrix products, arithmetic and copies ran while one was open for 3% of the time, Pallas kernels for 25%

profile of v16, /device:TPU:0, one launch (start us, length us, event | category | flops | bytes accessed | tf_op | source)
XLA Modules:
  0.0 40.3 jit_solution(5731221223708510325)
XLA Ops:
  1.1 0.7 %and_select_fusion = (s32[1,128]{1,0:T(1,128)S(1)}, s32[1,128]{1,0:T(1,128)S(1)}) fusion(s32[1,1,128]{2,1,0:T(1,128)} %param.11, s32[1,1,128]{2,1,0:T(1,128)} %param.10), kind=kLoop, calls=%fused_computation.26 | loop fusion | flops 2816 | bytes 2048 | tf_op jit(solution)/shard_map/jit(remainder)/select_n | solution.py:515
  1.9 1.2 %pack_grads.1 = (bf16[128,1408]{1,0:T(8,128)(2,1)S(1)}, bf16[128,1408]{1,0:T(8,128)(2,1)S(1)}) custom-call(bf16[128,2560]{1,0:T(8,128)(2,1)} %bitcast.35, f32[2,128]{1,0:T(2,128)S(1)} %add_convert_fusion.4.mark_ref, bf16[128,2560]{1,0:T(8,128)(2,1)} %bitcast.31, bf16[128,2560]{1,0:T(8,128)(2,1)} %bitcast.23, bf16[128,2560]{1,0:T(8,128)(2,1)} %bitcast.27), custom_call_target="tpu_custom_call" | custom-call | bytes 1310720 | tf_op jit(solution)/shard_map/pack_grads/pallas_call | solution.py:319
  3.1 2.6 %collective-permute-start.1 = (bf16[128,1408]{1,0:T(8,128)(2,1)S(1)}, bf16[128,1408]{1,0:T(8,128)(2,1)}, u32[]{:S(2)}, u32[]{:S(2)}) collective-permute-start(bf16[128,1408]{1,0:T(8,128)(2,1)S(1)} %get-tuple-element.36.mine_ref), channel_id=1, source_target_pairs={{0,8},{8,0},{16,24},{24,16},{1,9},{9,1},{17,25},{25,17},{2,10},{10... | collective-permute-start | bytes 1081352 | tf_op jit(solution)/shard_map/ppermute | solution.py:511
  5.7 1.5 %collective-permute-start.2 = (bf16[128,1408]{1,0:T(8,128)(2,1)S(1)}, bf16[128,1408]{1,0:T(8,128)(2,1)S(1)}, u32[]{:S(2)}, u32[]{:S(2)}) collective-permute-start(bf16[128,1408]{1,0:T(8,128)(2,1)S(1)} %get-tuple-element.39.mine_ref), channel_id=1, source_target_pairs={{0,16},{16,0},{8,24},{24,8},{1,17},{17,1},{9,25},{25,9},{2,18},{18... | collective-permute-start | bytes 1081352 | tf_op jit(solution)/shard_map/ppermute | solution.py:511
  7.2 0.9 %pack_ends.1 = (bf16[32,5248]{1,0:T(8,128)(2,1)}, bf16[32,5248]{1,0:T(8,128)(2,1)}) custom-call(bf16[128,2560]{1,0:T(8,128)(2,1)S(1)} %bitcast.24, bf16[128,2560]{1,0:T(8,128)(2,1)S(1)} %bitcast.28, f32[1,128]{1,0:T(1,128)S(1)} %get-tuple-element.46.code_ref), custom_call_target="tpu_custom_call" | custom-call | bytes 1310720 | tf_op jit(solution)/shard_map/pack_ends/pallas_call | solution.py:247
  8.1 1.5 %collective-permute-start.7 = (bf16[32,5248]{1,0:T(8,128)(2,1)}, bf16[32,5248]{1,0:T(8,128)(2,1)}, u32[]{:S(2)}, u32[]{:S(2)}) collective-permute-start(bf16[32,5248]{1,0:T(8,128)(2,1)} %get-tuple-element.47), channel_id=1, source_target_pairs={{2,4},{4,2},{3,5},{5,3},{10,12},{12,10},{11,13},{13,11},{18,20},{2... | collective-permute-start | bytes 1007624 | tf_op jit(solution)/shard_map/ppermute | solution.py:32
  9.7 3.7 %collective-permute-start.8 = (bf16[32,5248]{1,0:T(8,128)(2,1)}, bf16[32,5248]{1,0:T(8,128)(2,1)}, u32[]{:S(2)}, u32[]{:S(2)}) collective-permute-start(bf16[32,5248]{1,0:T(8,128)(2,1)} %get-tuple-element.48), channel_id=1, source_target_pairs={{0,2},{2,0},{4,6},{6,4},{1,3},{3,1},{5,7},{7,5},{8,10},{10,8},{12,... | collective-permute-start | bytes 1007624 | tf_op jit(solution)/shard_map/ppermute | solution.py:32
  13.4 1.6 %attend_middle.1 = bf16[64,2560]{1,0:T(8,128)(2,1)S(1)} custom-call(bf16[128,2560]{1,0:T(8,128)(2,1)S(1)} %bitcast.32, bf16[128,2560]{1,0:T(8,128)(2,1)S(1)} %bitcast.25, bf16[128,2560]{1,0:T(8,128)(2,1)S(1)} %bitcast.29, f32[1,128]{1,0:T(1,128)S(1)} %get-tuple-element.46.code_ref), custom_call_target="tpu_custom_call" | custom-call | flops 268435456 | bytes 1966080 | tf_op jit(solution)/shard_map/attend_middle/pallas_call | solution.py:260
  15.1 1.3 %pair_sums.2 = (bf16[64,1280]{1,0:T(8,128)(2,1)S(1)}, bf16[64,1280]{1,0:T(8,128)(2,1)S(1)}) custom-call(f32[1,2560]{1,0:T(1,128)S(1)} %broadcast_in_dim.9.gate_ref, f32[1,128]{1,0:T(1,128)S(1)} %get-tuple-element.86.row_ref, bf16[128,1408]{1,0:T(8,128)(2,1)S(1)} %get-tuple-element.36.mine_ref, bf16[128,1408]{1,0:T(8,128)(2,1)} %collective-permute-done.1.theirs_ref), custom_call_target="tpu_custom_call" | custom-call | flops 83886080 | bytes 983040 | tf_op jit(solution)/shard_map/pair_sums/pallas_call | solution.py:358
  16.7 1.5 %collective-permute-start.3 = (bf16[64,1280]{1,0:T(8,128)(2,1)S(1)}, bf16[64,1280]{1,0:T(8,128)(2,1)S(1)}, u32[]{:S(2)}, u32[]{:S(2)}) collective-permute-start(bf16[64,1280]{1,0:T(8,128)(2,1)S(1)} %get-tuple-element.42), channel_id=1, source_target_pairs={{0,8},{8,24},{24,16},{16,0},{1,9},{9,25},{25,17},{17,1},{2,10},{10... | collective-permute-start | bytes 491528 | tf_op jit(solution)/shard_map/ppermute | solution.py:511
  18.3 0.5 %collective-permute-start.4 = (bf16[64,1280]{1,0:T(8,128)(2,1)S(1)}, bf16[64,1280]{1,0:T(8,128)(2,1)S(1)}, u32[]{:S(2)}, u32[]{:S(2)}) collective-permute-start(bf16[64,1280]{1,0:T(8,128)(2,1)S(1)} %get-tuple-element.44), channel_id=1, source_target_pairs={{0,16},{16,24},{24,8},{8,0},{1,17},{17,25},{25,9},{9,1},{2,18},{18... | collective-permute-start | bytes 491528 | tf_op jit(solution)/shard_map/ppermute | solution.py:511
  18.8 2.6 %collective-permute-done.8.one_ref = bf16[32,5248]{1,0:T(8,128)(2,1)} collective-permute-done((bf16[32,5248]{1,0:T(8,128)(2,1)}, bf16[32,5248]{1,0:T(8,128)(2,1)}, u32[]{:S(2)}, u32[]{:S(2)}) %collective-permute-start.8) | collective-permute-done | bytes 335904 | tf_op jit(solution)/shard_map/ppermute | solution.py:32
  21.4 3.0 %attend_edges.1 = bf16[64,2560]{1,0:T(8,128)(2,1)S(1)} custom-call(bf16[128,2560]{1,0:T(8,128)(2,1)S(1)} %bitcast.33, bf16[128,2560]{1,0:T(8,128)(2,1)S(1)} %bitcast.26, bf16[128,2560]{1,0:T(8,128)(2,1)S(1)} %bitcast.30, f32[1,128]{1,0:T(1,128)S(1)} %get-tuple-element.46.code_ref, bf16[32,5248]{1,0:T(8,128)(2,1)} %collective-permute-done.7.two_ref, ...), custom_call_target="tpu_custom_call" | custom-call | flops 268435456 | bytes 1966080 | tf_op jit(solution)/shard_map/attend_edges/pallas_call | solution.py:281
  24.5 0.6 %collective-permute-start.10 = (bf16[64,1280]{1,0:T(8,128)(2,1)S(1)}, bf16[64,1280]{1,0:T(8,128)(2,1)S(1)}, u32[]{:S(2)}, u32[]{:S(2)}) collective-permute-start(bf16[64,1280]{1,0:T(8,128)(2,1)S(1)} %get-tuple-element.71), channel_id=1, source_target_pairs={{0,16},{16,24},{24,8},{8,0},{1,17},{17,25},{25,9},{9,1},{2,18},{18... | collective-permute-start | bytes 491528 | tf_op jit(solution)/shard_map/ppermute | solution.py:511
  25.1 1.5 %collective-permute-start.9 = (bf16[64,1280]{1,0:T(8,128)(2,1)S(1)}, bf16[64,1280]{1,0:T(8,128)(2,1)S(1)}, u32[]{:S(2)}, u32[]{:S(2)}) collective-permute-start(bf16[64,1280]{1,0:T(8,128)(2,1)S(1)} %get-tuple-element.72), channel_id=1, source_target_pairs={{0,8},{8,24},{24,16},{16,0},{1,9},{9,25},{25,17},{17,1},{2,10},{10... | collective-permute-start | bytes 491528 | tf_op jit(solution)/shard_map/ppermute | solution.py:511
  26.9 0.6 %collective-permute-start.6 = (bf16[64,1280]{1,0:T(8,128)(2,1)S(1)}, bf16[64,1280]{1,0:T(8,128)(2,1)S(1)}, u32[]{:S(2)}, u32[]{:S(2)}) collective-permute-start(bf16[64,1280]{1,0:T(8,128)(2,1)S(1)} %get-tuple-element.64), channel_id=1, source_target_pairs={{0,8},{8,0},{16,24},{24,16},{1,9},{9,1},{17,25},{25,17},{2,10},{10... | collective-permute-start | bytes 491528 | tf_op jit(solution)/shard_map/ppermute | solution.py:511
  28.0 3.7 %collective-permute-done.10 = bf16[64,1280]{1,0:T(8,128)(2,1)S(1)} collective-permute-done((bf16[64,1280]{1,0:T(8,128)(2,1)S(1)}, bf16[64,1280]{1,0:T(8,128)(2,1)S(1)}, u32[]{:S(2)}, u32[]{:S(2)}) %collective-permute-start.10) | collective-permute-done | bytes 163872 | tf_op jit(solution)/shard_map/ppermute | solution.py:511
  32.0 2.0 %collective-permute-start.12 = (bf16[64,1280]{1,0:T(8,128)(2,1)S(1)}, bf16[64,1280]{1,0:T(8,128)(2,1)S(1)}, u32[]{:S(2)}, u32[]{:S(2)}) collective-permute-start(bf16[64,1280]{1,0:T(8,128)(2,1)S(1)} %get-tuple-element.58), channel_id=1, source_target_pairs={{0,8},{8,0},{16,24},{24,16},{1,9},{9,1},{17,25},{25,17},{2,10},{10... | collective-permute-start | bytes 491528 | tf_op jit(solution)/shard_map/ppermute | solution.py:511
  34.3 0.8 %collective-permute-done.6 = bf16[64,1280]{1,0:T(8,128)(2,1)S(1)} collective-permute-done((bf16[64,1280]{1,0:T(8,128)(2,1)S(1)}, bf16[64,1280]{1,0:T(8,128)(2,1)S(1)}, u32[]{:S(2)}, u32[]{:S(2)}) %collective-permute-start.6) | collective-permute-done | bytes 163872 | tf_op jit(solution)/shard_map/ppermute | solution.py:511
  35.1 0.8 %relay_first.1 = (bf16[128,2560]{1,0:T(8,128)(2,1)}, f32[128,2560]{1,0:T(8,128)S(1)}, bf16[128,64]{1,0:T(8,128)(2,1)S(1)}) custom-call(f32[1,128]{1,0:T(1,128)S(1)} %get-tuple-element.86.row_ref, f32[1,2560]{1,0:T(1,128)S(1)} %broadcast_in_dim.9.gate_ref, bf16[64,1280]{1,0:T(8,128)(2,1)S(1)} %get-tuple-element.80.a_ref, ...), custom_call_target="tpu_custom_call" | custom-call | flops 83886080 | bytes 7864320 | tf_op jit(solution)/shard_map/relay_first/pallas_call | solution.py:406
  35.9 1.5 %collective-permute-done.12.got_ref = bf16[64,1280]{1,0:T(8,128)(2,1)S(1)} collective-permute-done((bf16[64,1280]{1,0:T(8,128)(2,1)S(1)}, bf16[64,1280]{1,0:T(8,128)(2,1)S(1)}, u32[]{:S(2)}, u32[]{:S(2)}) %collective-permute-start.12) | collective-permute-done | bytes 163872 | tf_op jit(solution)/shard_map/ppermute | solution.py:511
  37.4 1.0 %relay_last.2 = (bf16[128,2560]{1,0:T(8,128)(2,1)}, bf16[128,2560]{1,0:T(8,128)(2,1)}) custom-call(bf16[128,64]{1,0:T(8,128)(2,1)S(1)} %get-tuple-element.49.picks_ref, f32[1,2560]{1,0:T(1,128)S(1)} %broadcast_in_dim.9.gate_ref, bf16[64,1280]{1,0:T(8,128)(2,1)S(1)} %get-tuple-element.60.held_ref, ...), custom_call_target="tpu_custom_call", output_to_operand_aliasing={{0}: (6, {})} | custom-call | flops 41943040 | bytes 1966080 | tf_op jit(solution)/shard_map/relay_last/pallas_call | solution.py:466
  38.4 0.9 %collective-permute-done.11.got_ref = bf16[64,1280]{1,0:T(8,128)(2,1)S(1)} collective-permute-done((bf16[64,1280]{1,0:T(8,128)(2,1)S(1)}, bf16[64,1280]{1,0:T(8,128)(2,1)S(1)}, u32[]{:S(2)}, u32[]{:S(2)}) %collective-permute-start.11) | collective-permute-done | bytes 163872 | tf_op jit(solution)/shard_map/ppermute | solution.py:511
  39.4 1.0 %relay_last.3 = (bf16[128,2560]{1,0:T(8,128)(2,1)}, bf16[128,2560]{1,0:T(8,128)(2,1)}) custom-call(bf16[128,64]{1,0:T(8,128)(2,1)S(1)} %get-tuple-element.49.picks_ref, f32[1,2560]{1,0:T(1,128)S(1)} %broadcast_in_dim.9.gate_ref, bf16[64,1280]{1,0:T(8,128)(2,1)S(1)} %get-tuple-element.70.held_ref, ...), custom_call_target="tpu_custom_call", output_to_operand_aliasing={{0}: (6, {}), {1}: (7, {})} | custom-call | flops 41943040 | bytes 1966080 | tf_op jit(solution)/shard_map/relay_last/pallas_call | solution.py:466
  (32 shorter events, 2.4 us)
Async XLA Ops:
  0.6 14.4 %collective-permute-start = (f32[1280]{0:T(1024)}, f32[1280]{0:T(1024)S(1)}, u32[]{:S(2)}, u32[]{:S(2)}) collective-permute-start(f32[1280]{0:T(1024)} %param.12), channel_id=1, source_target_pairs={{0,1},{1,0},{2,3},{3,2},{4,5},{5,4},{6,7},{7,6},{8,9},{9,8},{10,11... | collective-permute-start | bytes 15368 | tf_op jit(solution)/shard_map/ppermute | solution.py:490
  1.9 5.3 %copy-start = (bf16[1,1,128,2560]{3,2,1,0:T(8,128)(2,1)S(1)}, bf16[1,1,128,2560]{3,2,1,0:T(8,128)(2,1)}, u32[]{:S(2)}) copy-start(bf16[1,1,128,2560]{3,2,1,0:T(8,128)(2,1)} %param.8) | copy-start | bytes 1966084
  1.9 5.3 %copy-start.1 = (bf16[1,1,128,2560]{3,2,1,0:T(8,128)(2,1)S(1)}, bf16[1,1,128,2560]{3,2,1,0:T(8,128)(2,1)}, u32[]{:S(2)}) copy-start(bf16[1,1,128,2560]{3,2,1,0:T(8,128)(2,1)} %param.9) | copy-start | bytes 1966084
  3.1 10.3 %copy-start.2 = (bf16[1,1,128,2560]{3,2,1,0:T(8,128)(2,1)S(1)}, bf16[1,1,128,2560]{3,2,1,0:T(8,128)(2,1)}, u32[]{:S(2)}) copy-start(bf16[1,1,128,2560]{3,2,1,0:T(8,128)(2,1)} %param.7) | copy-start | bytes 1966084
  3.1 12.0 %collective-permute-start.1 = (bf16[128,1408]{1,0:T(8,128)(2,1)S(1)}, bf16[128,1408]{1,0:T(8,128)(2,1)}, u32[]{:S(2)}, u32[]{:S(2)}) collective-permute-start(bf16[128,1408]{1,0:T(8,128)(2,1)S(1)} %get-tuple-element.36.mine_ref), channel_id=1, source_target_pairs={{0,8},{8,0},{16,24},{24,16},{1,9},{9,1},{17,25},{25,17},{2,10},{10... | collective-permute-start | bytes 1081352 | tf_op jit(solution)/shard_map/ppermute | solution.py:511
  5.7 10.7 %collective-permute-start.2 = (bf16[128,1408]{1,0:T(8,128)(2,1)S(1)}, bf16[128,1408]{1,0:T(8,128)(2,1)S(1)}, u32[]{:S(2)}, u32[]{:S(2)}) collective-permute-start(bf16[128,1408]{1,0:T(8,128)(2,1)S(1)} %get-tuple-element.39.mine_ref), channel_id=1, source_target_pairs={{0,16},{16,0},{8,24},{24,8},{1,17},{17,1},{9,25},{25,9},{2,18},{18... | collective-permute-start | bytes 1081352 | tf_op jit(solution)/shard_map/ppermute | solution.py:511
  8.1 6.9 %copy-start.3 = (f32[1280]{0:T(1024)S(1)}, f32[1280]{0:T(1024)}, u32[]{:S(2)}) copy-start(f32[1280]{0:T(1024)} %param.12) | copy-start | bytes 15364
  8.1 10.7 %collective-permute-start.7 = (bf16[32,5248]{1,0:T(8,128)(2,1)}, bf16[32,5248]{1,0:T(8,128)(2,1)}, u32[]{:S(2)}, u32[]{:S(2)}) collective-permute-start(bf16[32,5248]{1,0:T(8,128)(2,1)} %get-tuple-element.47), channel_id=1, source_target_pairs={{2,4},{4,2},{3,5},{5,3},{10,12},{12,10},{11,13},{13,11},{18,20},{2... | collective-permute-start | bytes 1007624 | tf_op jit(solution)/shard_map/ppermute | solution.py:32
  9.7 11.8 %collective-permute-start.8 = (bf16[32,5248]{1,0:T(8,128)(2,1)}, bf16[32,5248]{1,0:T(8,128)(2,1)}, u32[]{:S(2)}, u32[]{:S(2)}) collective-permute-start(bf16[32,5248]{1,0:T(8,128)(2,1)} %get-tuple-element.48), channel_id=1, source_target_pairs={{0,2},{2,0},{4,6},{6,4},{1,3},{3,1},{5,7},{7,5},{8,10},{10,8},{12,... | collective-permute-start | bytes 1007624 | tf_op jit(solution)/shard_map/ppermute | solution.py:32
  16.7 9.9 %collective-permute-start.3 = (bf16[64,1280]{1,0:T(8,128)(2,1)S(1)}, bf16[64,1280]{1,0:T(8,128)(2,1)S(1)}, u32[]{:S(2)}, u32[]{:S(2)}) collective-permute-start(bf16[64,1280]{1,0:T(8,128)(2,1)S(1)} %get-tuple-element.42), channel_id=1, source_target_pairs={{0,8},{8,24},{24,16},{16,0},{1,9},{9,25},{25,17},{17,1},{2,10},{10... | collective-permute-start | bytes 491528 | tf_op jit(solution)/shard_map/ppermute | solution.py:511
  18.3 8.4 %collective-permute-start.4 = (bf16[64,1280]{1,0:T(8,128)(2,1)S(1)}, bf16[64,1280]{1,0:T(8,128)(2,1)S(1)}, u32[]{:S(2)}, u32[]{:S(2)}) collective-permute-start(bf16[64,1280]{1,0:T(8,128)(2,1)S(1)} %get-tuple-element.44), channel_id=1, source_target_pairs={{0,16},{16,24},{24,8},{8,0},{1,17},{17,25},{25,9},{9,1},{2,18},{18... | collective-permute-start | bytes 491528 | tf_op jit(solution)/shard_map/ppermute | solution.py:511
  24.5 7.1 %collective-permute-start.10 = (bf16[64,1280]{1,0:T(8,128)(2,1)S(1)}, bf16[64,1280]{1,0:T(8,128)(2,1)S(1)}, u32[]{:S(2)}, u32[]{:S(2)}) collective-permute-start(bf16[64,1280]{1,0:T(8,128)(2,1)S(1)} %get-tuple-element.71), channel_id=1, source_target_pairs={{0,16},{16,24},{24,8},{8,0},{1,17},{17,25},{25,9},{9,1},{2,18},{18... | collective-permute-start | bytes 491528 | tf_op jit(solution)/shard_map/ppermute | solution.py:511
  25.1 6.7 %collective-permute-start.9 = (bf16[64,1280]{1,0:T(8,128)(2,1)S(1)}, bf16[64,1280]{1,0:T(8,128)(2,1)S(1)}, u32[]{:S(2)}, u32[]{:S(2)}) collective-permute-start(bf16[64,1280]{1,0:T(8,128)(2,1)S(1)} %get-tuple-element.72), channel_id=1, source_target_pairs={{0,8},{8,24},{24,16},{16,0},{1,9},{9,25},{25,17},{17,1},{2,10},{10... | collective-permute-start | bytes 491528 | tf_op jit(solution)/shard_map/ppermute | solution.py:511
  26.9 8.2 %collective-permute-start.6 = (bf16[64,1280]{1,0:T(8,128)(2,1)S(1)}, bf16[64,1280]{1,0:T(8,128)(2,1)S(1)}, u32[]{:S(2)}, u32[]{:S(2)}) collective-permute-start(bf16[64,1280]{1,0:T(8,128)(2,1)S(1)} %get-tuple-element.64), channel_id=1, source_target_pairs={{0,8},{8,0},{16,24},{24,16},{1,9},{9,1},{17,25},{25,17},{2,10},{10... | collective-permute-start | bytes 491528 | tf_op jit(solution)/shard_map/ppermute | solution.py:511
  27.5 7.6 %collective-permute-start.5 = (bf16[64,1280]{1,0:T(8,128)(2,1)S(1)}, bf16[64,1280]{1,0:T(8,128)(2,1)S(1)}, u32[]{:S(2)}, u32[]{:S(2)}) collective-permute-start(bf16[64,1280]{1,0:T(8,128)(2,1)S(1)} %get-tuple-element.73), channel_id=1, source_target_pairs={{0,16},{16,0},{8,24},{24,8},{1,17},{17,1},{9,25},{25,9},{2,18},{18... | collective-permute-start | bytes 491528 | tf_op jit(solution)/shard_map/ppermute | solution.py:511
  32.0 5.4 %collective-permute-start.12 = (bf16[64,1280]{1,0:T(8,128)(2,1)S(1)}, bf16[64,1280]{1,0:T(8,128)(2,1)S(1)}, u32[]{:S(2)}, u32[]{:S(2)}) collective-permute-start(bf16[64,1280]{1,0:T(8,128)(2,1)S(1)} %get-tuple-element.58), channel_id=1, source_target_pairs={{0,8},{8,0},{16,24},{24,16},{1,9},{9,1},{17,25},{25,17},{2,10},{10... | collective-permute-start | bytes 491528 | tf_op jit(solution)/shard_map/ppermute | solution.py:511
  34.0 5.3 %collective-permute-start.11 = (bf16[64,1280]{1,0:T(8,128)(2,1)S(1)}, bf16[64,1280]{1,0:T(8,128)(2,1)S(1)}, u32[]{:S(2)}, u32[]{:S(2)}) collective-permute-start(bf16[64,1280]{1,0:T(8,128)(2,1)S(1)} %get-tuple-element.68), channel_id=1, source_target_pairs={{0,16},{16,0},{8,24},{24,8},{1,17},{17,1},{9,25},{25,9},{2,18},{18... | collective-permute-start | bytes 491528 | tf_op jit(solution)/shard_map/ppermute | solution.py:511

commit v17 on v15

--- a/solution.py
+++ b/solution.py
@@ -165,29 +165,38 @@
 
 
 def sides_kernel(reach, q_ref, k_ref, v_ref, code_ref, one_ref, two_ref, *refs):
-    out_ref, keys, values, codes = refs
+    out_ref, keys, values, codes, one, two, sems = refs
+    copies = [
+        pltpu.make_async_copy(one_ref, one, sems.at[0]),
+        pltpu.make_async_copy(two_ref, two, sems.at[1]),
+    ]
+    for copy in copies:
+        copy.start()
     tokens, width = q_ref.shape
     near = 2 * reach
     code = columns(code_ref[...])
     even = lax.axis_index("seq") % 2 == 0
     period = math.lcm(DH, LANES)
     masks = head_masks(reach, period)
-    blocks = []
-    for side, first in ((0, 0), (1, tokens - near)):
+    spare = keys.shape[1] - near - reach
+    sides = ((0, 0, 0), (1, tokens - near, tokens - reach))
+    for side, first, top in sides:
         own = slice(first, first + near)
-        use_two = even if side == 0 else jnp.logical_not(even)
-        halo = jnp.where(use_two, two_ref[...], one_ref[...])
         keys[side, :near] = k_ref[own]
         values[side, :near] = v_ref[own]
         codes[side, :near] = code[own]
+        if spare:
+            for ref in (keys, values, codes):
+                ref[side, near + reach :] = jnp.zeros((spare, ref.shape[2]), ref.dtype)
+    for copy in copies:
+        copy.wait()
+    blocks = []
+    for side, first, top in sides:
+        use_two = even if side == 0 else jnp.logical_not(even)
+        halo = jnp.where(use_two, two[...], one[...])
         keys[side, near : near + reach] = halo[:, :width]
         values[side, near : near + reach] = halo[:, width : 2 * width]
         codes[side, near : near + reach] = halo[:, 2 * width :].astype(jnp.float32)
-        spare = keys.shape[1] - near - reach
-        if spare:
-            for ref in (keys, values, codes):
-                ref[side, near + reach :] = jnp.zeros((spare, ref.shape[2]), ref.dtype)
-        top = side * (tokens - reach)
         blocks.append((side, top, link_bias(code[top : top + reach], codes[side])))
     for base in range(0, width, period):
         scores = []
@@ -278,16 +287,20 @@
         kernel = edge_kernel
         held = (-(-2 * reach // LANES) * LANES,)
     operands = [queries, keys, values, code, *halos]
+    far = pl.BlockSpec(memory_space=pltpu.HBM)
+    landing = [pltpu.VMEM(halo.shape, jnp.bfloat16) for halo in halos[:2]]
+    landing.append(pltpu.SemaphoreType.DMA((2,)))
     return pl.pallas_call(
         functools.partial(kernel, reach),
-        in_specs=[VMEM] * len(operands),
+        in_specs=[VMEM] * 4 + [VMEM if kernel is edge_kernel else far] * len(halos),
         out_specs=VMEM,
         out_shape=jax.ShapeDtypeStruct((rows, width), jnp.bfloat16),
         scratch_shapes=[
             pltpu.VMEM((*held, width), jnp.bfloat16),
             pltpu.VMEM((*held, width), jnp.bfloat16),
             pltpu.VMEM((*held, LANES), jnp.float32),
-        ],
+        ]
+        + (landing if kernel is sides_kernel else []),
         compiler_params=PARAMS,
         cost_estimate=attend_cost(rows, LANES, width),
         name="attend_edges",

time: 38.9 us -> 38.9 us (level)
  transfers between devices with their start and end apart: 13 -> 13, of which waited for: 6 -> 7; matrix products, arithmetic and copies ran while one was open for 3% -> 3% of each run, Pallas kernels for 26% -> 26%
where the time goes in v17:
time: 38.9 us; the launch traced here: 38.1 us
  starting transfers between devices  16.8 us (43%)
  Pallas kernels  11 us (28%)
  waiting for transfers between devices  8.08 us (21%)
  other arithmetic  1.29 us (3%)
  between operations  0.83 us (2%)
    ppermute x10, starting transfers between devices, local(): send = lambda block, route: lax.ppermute(block, 'grp', route)  13.3 us
    ppermute x10, waiting for transfers between devices, local(): send = lambda block, route: lax.ppermute(block, 'grp', route)  8.07 us
    pallas_call x1, Pallas kernels, attend_edges(): pl.pallas_call(functools.partial(kernel, reach), in_specs=[VMEM] * 4 + [V...  2.99 us
    ppermute x2, starting transfers between devices, paired(): return lax.ppermute(block, axis, route)  2.98 us
    pallas_call x2, Pallas kernels, relay_last(): pl.pallas_call(functools.partial(relay_last_kernel, part, chunks, first_r...  1.99 us
    pallas_call x1, Pallas kernels, attend_middle(): pl.pallas_call(functools.partial(middle_kernel, reach), in_specs=[VMEM] *...  1.6 us
    pallas_call x2, Pallas kernels, pair_sums(): pl.pallas_call(functools.partial(sums_kernel, part, sizes), in_specs=[VME...  1.57 us
    pallas_call x1, Pallas kernels, pack_grads(): pl.pallas_call(pack_grads_kernel, in_specs=[far, VMEM] + [far] * len(othe...  1.19 us
  transfers between devices with their start and end apart: 13, of which 7 were waited for; matrix products, arithmetic and copies ran while one was open for 3% of the time, Pallas kernels for 26%

profile of v17, /device:TPU:0, one launch (start us, length us, event | category | flops | bytes accessed | tf_op | source)
XLA Modules:
  0.0 38.1 jit_solution(15571864206193277057)
XLA Ops:
  0.6 0.5 %collective-permute-start = (f32[1280]{0:T(1024)}, f32[1280]{0:T(1024)S(1)}, u32[]{:S(2)}, u32[]{:S(2)}) collective-permute-start(f32[1280]{0:T(1024)} %param.12), channel_id=1, source_target_pairs={{0,1},{1,0},{2,3},{3,2},{4,5},{5,4},{6,7},{7,6},{8,9},{9,8},{10,11... | collective-permute-start | bytes 15368 | tf_op jit(solution)/shard_map/ppermute | solution.py:503
  1.1 0.7 %and_select_fusion = (s32[1,128]{1,0:T(1,128)S(1)}, s32[1,128]{1,0:T(1,128)S(1)}) fusion(s32[1,1,128]{2,1,0:T(1,128)} %param.11, s32[1,1,128]{2,1,0:T(1,128)} %param.10), kind=kLoop, calls=%fused_computation.26 | loop fusion | flops 2816 | bytes 2048 | tf_op jit(solution)/shard_map/jit(remainder)/select_n | solution.py:528
  1.9 1.2 %pack_grads.1 = (bf16[128,1408]{1,0:T(8,128)(2,1)S(1)}, bf16[128,1408]{1,0:T(8,128)(2,1)S(1)}) custom-call(bf16[128,2560]{1,0:T(8,128)(2,1)} %bitcast.35, f32[2,128]{1,0:T(2,128)S(1)} %add_convert_fusion.4.mark_ref, bf16[128,2560]{1,0:T(8,128)(2,1)} %bitcast.31, bf16[128,2560]{1,0:T(8,128)(2,1)} %bitcast.23, bf16[128,2560]{1,0:T(8,128)(2,1)} %bitcast.27), custom_call_target="tpu_custom_call" | custom-call | bytes 1310720 | tf_op jit(solution)/shard_map/pack_grads/pallas_call | solution.py:332
  3.1 2.6 %collective-permute-start.1 = (bf16[128,1408]{1,0:T(8,128)(2,1)S(1)}, bf16[128,1408]{1,0:T(8,128)(2,1)}, u32[]{:S(2)}, u32[]{:S(2)}) collective-permute-start(bf16[128,1408]{1,0:T(8,128)(2,1)S(1)} %get-tuple-element.36.mine_ref), channel_id=1, source_target_pairs={{0,8},{8,0},{16,24},{24,16},{1,9},{9,1},{17,25},{25,17},{2,10},{10... | collective-permute-start | bytes 1081352 | tf_op jit(solution)/shard_map/ppermute | solution.py:524
  5.7 1.5 %collective-permute-start.2 = (bf16[128,1408]{1,0:T(8,128)(2,1)S(1)}, bf16[128,1408]{1,0:T(8,128)(2,1)S(1)}, u32[]{:S(2)}, u32[]{:S(2)}) collective-permute-start(bf16[128,1408]{1,0:T(8,128)(2,1)S(1)} %get-tuple-element.39.mine_ref), channel_id=1, source_target_pairs={{0,16},{16,0},{8,24},{24,8},{1,17},{17,1},{9,25},{25,9},{2,18},{18... | collective-permute-start | bytes 1081352 | tf_op jit(solution)/shard_map/ppermute | solution.py:524
  7.2 0.9 %pack_ends.1 = (bf16[32,5248]{1,0:T(8,128)(2,1)}, bf16[32,5248]{1,0:T(8,128)(2,1)}) custom-call(bf16[128,2560]{1,0:T(8,128)(2,1)S(1)} %bitcast.24, bf16[128,2560]{1,0:T(8,128)(2,1)S(1)} %bitcast.28, f32[1,128]{1,0:T(1,128)S(1)} %get-tuple-element.46.code_ref), custom_call_target="tpu_custom_call" | custom-call | bytes 1310720 | tf_op jit(solution)/shard_map/pack_ends/pallas_call | solution.py:256
  8.1 1.6 %collective-permute-start.7 = (bf16[32,5248]{1,0:T(8,128)(2,1)}, bf16[32,5248]{1,0:T(8,128)(2,1)}, u32[]{:S(2)}, u32[]{:S(2)}) collective-permute-start(bf16[32,5248]{1,0:T(8,128)(2,1)} %get-tuple-element.47), channel_id=1, source_target_pairs={{0,2},{2,0},{4,6},{6,4},{1,3},{3,1},{5,7},{7,5},{8,10},{10,8},{12,... | collective-permute-start | bytes 1007624 | tf_op jit(solution)/shard_map/ppermute | solution.py:32
  9.7 1.4 %collective-permute-start.8 = (bf16[32,5248]{1,0:T(8,128)(2,1)}, bf16[32,5248]{1,0:T(8,128)(2,1)}, u32[]{:S(2)}, u32[]{:S(2)}) collective-permute-start(bf16[32,5248]{1,0:T(8,128)(2,1)} %get-tuple-element.48), channel_id=1, source_target_pairs={{2,4},{4,2},{3,5},{5,3},{10,12},{12,10},{11,13},{13,11},{18,20},{2... | collective-permute-start | bytes 1007624 | tf_op jit(solution)/shard_map/ppermute | solution.py:32
  11.1 1.6 %attend_middle.1 = bf16[64,2560]{1,0:T(8,128)(2,1)S(1)} custom-call(bf16[128,2560]{1,0:T(8,128)(2,1)S(1)} %bitcast.32, bf16[128,2560]{1,0:T(8,128)(2,1)S(1)} %bitcast.25, bf16[128,2560]{1,0:T(8,128)(2,1)S(1)} %bitcast.29, f32[1,128]{1,0:T(1,128)S(1)} %get-tuple-element.46.code_ref), custom_call_target="tpu_custom_call" | custom-call | flops 268435456 | bytes 1966080 | tf_op jit(solution)/shard_map/attend_middle/pallas_call | solution.py:269
  12.8 2.0 %collective-permute-done.1.theirs_ref = bf16[128,1408]{1,0:T(8,128)(2,1)} collective-permute-done((bf16[128,1408]{1,0:T(8,128)(2,1)S(1)}, bf16[128,1408]{1,0:T(8,128)(2,1)}, u32[]{:S(2)}, u32[]{:S(2)}) %collective-permute-start.1) | collective-permute-done | bytes 360480 | tf_op jit(solution)/shard_map/ppermute | solution.py:524
  14.8 1.3 %pair_sums.2 = (bf16[64,1280]{1,0:T(8,128)(2,1)S(1)}, bf16[64,1280]{1,0:T(8,128)(2,1)S(1)}) custom-call(f32[1,2560]{1,0:T(1,128)S(1)} %broadcast_in_dim.9.gate_ref, f32[1,128]{1,0:T(1,128)S(1)} %get-tuple-element.86.row_ref, bf16[128,1408]{1,0:T(8,128)(2,1)S(1)} %get-tuple-element.36.mine_ref, bf16[128,1408]{1,0:T(8,128)(2,1)} %collective-permute-done.1.theirs_ref), custom_call_target="tpu_custom_call" | custom-call | flops 83886080 | bytes 983040 | tf_op jit(solution)/shard_map/pair_sums/pallas_call | solution.py:371
  16.5 1.7 %collective-permute-start.3 = (bf16[64,1280]{1,0:T(8,128)(2,1)S(1)}, bf16[64,1280]{1,0:T(8,128)(2,1)S(1)}, u32[]{:S(2)}, u32[]{:S(2)}) collective-permute-start(bf16[64,1280]{1,0:T(8,128)(2,1)S(1)} %get-tuple-element.42), channel_id=1, source_target_pairs={{0,8},{8,24},{24,16},{16,0},{1,9},{9,25},{25,17},{17,1},{2,10},{10... | collective-permute-start | bytes 491528 | tf_op jit(solution)/shard_map/ppermute | solution.py:524
  18.6 3.0 %attend_edges.1 = bf16[64,2560]{1,0:T(8,128)(2,1)S(1)} custom-call(bf16[128,2560]{1,0:T(8,128)(2,1)S(1)} %bitcast.33, bf16[128,2560]{1,0:T(8,128)(2,1)S(1)} %bitcast.26, bf16[128,2560]{1,0:T(8,128)(2,1)S(1)} %bitcast.30, f32[1,128]{1,0:T(1,128)S(1)} %get-tuple-element.46.code_ref, bf16[32,5248]{1,0:T(8,128)(2,1)} %collective-permute-done.7.one_ref, ...), custom_call_target="tpu_custom_call" | custom-call | flops 268435456 | bytes 1966080 | tf_op jit(solution)/shard_map/attend_edges/pallas_call | solution.py:293
  21.7 1.8 %collective-permute-start.10 = (bf16[64,1280]{1,0:T(8,128)(2,1)S(1)}, bf16[64,1280]{1,0:T(8,128)(2,1)S(1)}, u32[]{:S(2)}, u32[]{:S(2)}) collective-permute-start(bf16[64,1280]{1,0:T(8,128)(2,1)S(1)} %get-tuple-element.71), channel_id=1, source_target_pairs={{0,16},{16,24},{24,8},{8,0},{1,17},{17,25},{25,9},{9,1},{2,18},{18... | collective-permute-start | bytes 491528 | tf_op jit(solution)/shard_map/ppermute | solution.py:524
  24.1 1.7 %collective-permute-start.6 = (bf16[64,1280]{1,0:T(8,128)(2,1)S(1)}, bf16[64,1280]{1,0:T(8,128)(2,1)S(1)}, u32[]{:S(2)}, u32[]{:S(2)}) collective-permute-start(bf16[64,1280]{1,0:T(8,128)(2,1)S(1)} %get-tuple-element.64), channel_id=1, source_target_pairs={{0,8},{8,0},{16,24},{24,16},{1,9},{9,1},{17,25},{25,17},{2,10},{10... | collective-permute-start | bytes 491528 | tf_op jit(solution)/shard_map/ppermute | solution.py:524
  25.8 1.5 %collective-permute-start.5 = (bf16[64,1280]{1,0:T(8,128)(2,1)S(1)}, bf16[64,1280]{1,0:T(8,128)(2,1)S(1)}, u32[]{:S(2)}, u32[]{:S(2)}) collective-permute-start(bf16[64,1280]{1,0:T(8,128)(2,1)S(1)} %get-tuple-element.73), channel_id=1, source_target_pairs={{0,16},{16,0},{8,24},{24,8},{1,17},{17,1},{9,25},{25,9},{2,18},{18... | collective-permute-start | bytes 491528 | tf_op jit(solution)/shard_map/ppermute | solution.py:524
  27.3 1.6 %collective-permute-done.10 = bf16[64,1280]{1,0:T(8,128)(2,1)S(1)} collective-permute-done((bf16[64,1280]{1,0:T(8,128)(2,1)S(1)}, bf16[64,1280]{1,0:T(8,128)(2,1)S(1)}, u32[]{:S(2)}, u32[]{:S(2)}) %collective-permute-start.10) | collective-permute-done | bytes 163872 | tf_op jit(solution)/shard_map/ppermute | solution.py:524
  28.9 1.6 %collective-permute-done.9 = bf16[64,1280]{1,0:T(8,128)(2,1)S(1)} collective-permute-done((bf16[64,1280]{1,0:T(8,128)(2,1)S(1)}, bf16[64,1280]{1,0:T(8,128)(2,1)S(1)}, u32[]{:S(2)}, u32[]{:S(2)}) %collective-permute-start.9) | collective-permute-done | bytes 163872 | tf_op jit(solution)/shard_map/ppermute | solution.py:524
  31.2 1.3 %collective-permute-start.11 = (bf16[64,1280]{1,0:T(8,128)(2,1)S(1)}, bf16[64,1280]{1,0:T(8,128)(2,1)S(1)}, u32[]{:S(2)}, u32[]{:S(2)}) collective-permute-start(bf16[64,1280]{1,0:T(8,128)(2,1)S(1)} %get-tuple-element.68), channel_id=1, source_target_pairs={{0,16},{16,0},{8,24},{24,8},{1,17},{17,1},{9,25},{25,9},{2,18},{18... | collective-permute-start | bytes 491528 | tf_op jit(solution)/shard_map/ppermute | solution.py:524
  32.5 1.2 %collective-permute-done.5 = bf16[64,1280]{1,0:T(8,128)(2,1)S(1)} collective-permute-done((bf16[64,1280]{1,0:T(8,128)(2,1)S(1)}, bf16[64,1280]{1,0:T(8,128)(2,1)S(1)}, u32[]{:S(2)}, u32[]{:S(2)}) %collective-permute-start.5) | collective-permute-done | bytes 163872 | tf_op jit(solution)/shard_map/ppermute | solution.py:524
  33.8 0.8 %relay_first.1 = (bf16[128,2560]{1,0:T(8,128)(2,1)}, f32[128,2560]{1,0:T(8,128)S(1)}, bf16[128,64]{1,0:T(8,128)(2,1)S(1)}) custom-call(f32[1,128]{1,0:T(1,128)S(1)} %get-tuple-element.86.row_ref, f32[1,2560]{1,0:T(1,128)S(1)} %broadcast_in_dim.9.gate_ref, bf16[64,1280]{1,0:T(8,128)(2,1)S(1)} %get-tuple-element.80.a_ref, ...), custom_call_target="tpu_custom_call" | custom-call | flops 83886080 | bytes 7864320 | tf_op jit(solution)/shard_map/relay_first/pallas_call | solution.py:419
  34.6 1.5 %collective-permute-done.12.got_ref = bf16[64,1280]{1,0:T(8,128)(2,1)S(1)} collective-permute-done((bf16[64,1280]{1,0:T(8,128)(2,1)S(1)}, bf16[64,1280]{1,0:T(8,128)(2,1)S(1)}, u32[]{:S(2)}, u32[]{:S(2)}) %collective-permute-start.12) | collective-permute-done | bytes 163872 | tf_op jit(solution)/shard_map/ppermute | solution.py:524
  36.1 1.0 %relay_last.2 = (bf16[128,2560]{1,0:T(8,128)(2,1)}, bf16[128,2560]{1,0:T(8,128)(2,1)}) custom-call(bf16[128,64]{1,0:T(8,128)(2,1)S(1)} %get-tuple-element.49.picks_ref, f32[1,2560]{1,0:T(1,128)S(1)} %broadcast_in_dim.9.gate_ref, bf16[64,1280]{1,0:T(8,128)(2,1)S(1)} %get-tuple-element.60.held_ref, ...), custom_call_target="tpu_custom_call", output_to_operand_aliasing={{0}: (6, {})} | custom-call | flops 41943040 | bytes 1966080 | tf_op jit(solution)/shard_map/relay_last/pallas_call | solution.py:479
  37.1 1.0 %relay_last.3 = (bf16[128,2560]{1,0:T(8,128)(2,1)}, bf16[128,2560]{1,0:T(8,128)(2,1)}) custom-call(bf16[128,64]{1,0:T(8,128)(2,1)S(1)} %get-tuple-element.49.picks_ref, f32[1,2560]{1,0:T(1,128)S(1)} %broadcast_in_dim.9.gate_ref, bf16[64,1280]{1,0:T(8,128)(2,1)S(1)} %get-tuple-element.70.held_ref, ...), custom_call_target="tpu_custom_call", output_to_operand_aliasing={{0}: (6, {}), {1}: (7, {})} | custom-call | flops 41943040 | bytes 1966080 | tf_op jit(solution)/shard_map/relay_last/pallas_call | solution.py:479
  (32 shorter events, 2.3 us)
Async XLA Ops:
  0.6 12.1 %collective-permute-start = (f32[1280]{0:T(1024)}, f32[1280]{0:T(1024)S(1)}, u32[]{:S(2)}, u32[]{:S(2)}) collective-permute-start(f32[1280]{0:T(1024)} %param.12), channel_id=1, source_target_pairs={{0,1},{1,0},{2,3},{3,2},{4,5},{5,4},{6,7},{7,6},{8,9},{9,8},{10,11... | collective-permute-start | bytes 15368 | tf_op jit(solution)/shard_map/ppermute | solution.py:503
  1.9 5.3 %copy-start = (bf16[1,1,128,2560]{3,2,1,0:T(8,128)(2,1)S(1)}, bf16[1,1,128,2560]{3,2,1,0:T(8,128)(2,1)}, u32[]{:S(2)}) copy-start(bf16[1,1,128,2560]{3,2,1,0:T(8,128)(2,1)} %param.8) | copy-start | bytes 1966084
  1.9 5.3 %copy-start.1 = (bf16[1,1,128,2560]{3,2,1,0:T(8,128)(2,1)S(1)}, bf16[1,1,128,2560]{3,2,1,0:T(8,128)(2,1)}, u32[]{:S(2)}) copy-start(bf16[1,1,128,2560]{3,2,1,0:T(8,128)(2,1)} %param.9) | copy-start | bytes 1966084
  3.1 8.0 %copy-start.2 = (bf16[1,1,128,2560]{3,2,1,0:T(8,128)(2,1)S(1)}, bf16[1,1,128,2560]{3,2,1,0:T(8,128)(2,1)}, u32[]{:S(2)}) copy-start(bf16[1,1,128,2560]{3,2,1,0:T(8,128)(2,1)} %param.7) | copy-start | bytes 1966084
  3.1 11.7 %collective-permute-start.1 = (bf16[128,1408]{1,0:T(8,128)(2,1)S(1)}, bf16[128,1408]{1,0:T(8,128)(2,1)}, u32[]{:S(2)}, u32[]{:S(2)}) collective-permute-start(bf16[128,1408]{1,0:T(8,128)(2,1)S(1)} %get-tuple-element.36.mine_ref), channel_id=1, source_target_pairs={{0,8},{8,0},{16,24},{24,16},{1,9},{9,1},{17,25},{25,17},{2,10},{10... | collective-permute-start | bytes 1081352 | tf_op jit(solution)/shard_map/ppermute | solution.py:524
  5.7 10.5 %collective-permute-start.2 = (bf16[128,1408]{1,0:T(8,128)(2,1)S(1)}, bf16[128,1408]{1,0:T(8,128)(2,1)S(1)}, u32[]{:S(2)}, u32[]{:S(2)}) collective-permute-start(bf16[128,1408]{1,0:T(8,128)(2,1)S(1)} %get-tuple-element.39.mine_ref), channel_id=1, source_target_pairs={{0,16},{16,0},{8,24},{24,8},{1,17},{17,1},{9,25},{25,9},{2,18},{18... | collective-permute-start | bytes 1081352 | tf_op jit(solution)/shard_map/ppermute | solution.py:524
  8.1 4.6 %copy-start.3 = (f32[1280]{0:T(1024)S(1)}, f32[1280]{0:T(1024)}, u32[]{:S(2)}) copy-start(f32[1280]{0:T(1024)} %param.12) | copy-start | bytes 15364
  8.1 10.5 %collective-permute-start.7 = (bf16[32,5248]{1,0:T(8,128)(2,1)}, bf16[32,5248]{1,0:T(8,128)(2,1)}, u32[]{:S(2)}, u32[]{:S(2)}) collective-permute-start(bf16[32,5248]{1,0:T(8,128)(2,1)} %get-tuple-element.47), channel_id=1, source_target_pairs={{0,2},{2,0},{4,6},{6,4},{1,3},{3,1},{5,7},{7,5},{8,10},{10,8},{12,... | collective-permute-start | bytes 1007624 | tf_op jit(solution)/shard_map/ppermute | solution.py:32
  9.7 8.9 %collective-permute-start.8 = (bf16[32,5248]{1,0:T(8,128)(2,1)}, bf16[32,5248]{1,0:T(8,128)(2,1)}, u32[]{:S(2)}, u32[]{:S(2)}) collective-permute-start(bf16[32,5248]{1,0:T(8,128)(2,1)} %get-tuple-element.48), channel_id=1, source_target_pairs={{2,4},{4,2},{3,5},{5,3},{10,12},{12,10},{11,13},{13,11},{18,20},{2... | collective-permute-start | bytes 1007624 | tf_op jit(solution)/shard_map/ppermute | solution.py:32
  16.5 7.3 %collective-permute-start.3 = (bf16[64,1280]{1,0:T(8,128)(2,1)S(1)}, bf16[64,1280]{1,0:T(8,128)(2,1)S(1)}, u32[]{:S(2)}, u32[]{:S(2)}) collective-permute-start(bf16[64,1280]{1,0:T(8,128)(2,1)S(1)} %get-tuple-element.42), channel_id=1, source_target_pairs={{0,8},{8,24},{24,16},{16,0},{1,9},{9,25},{25,17},{17,1},{2,10},{10... | collective-permute-start | bytes 491528 | tf_op jit(solution)/shard_map/ppermute | solution.py:524
  18.3 5.6 %collective-permute-start.4 = (bf16[64,1280]{1,0:T(8,128)(2,1)S(1)}, bf16[64,1280]{1,0:T(8,128)(2,1)S(1)}, u32[]{:S(2)}, u32[]{:S(2)}) collective-permute-start(bf16[64,1280]{1,0:T(8,128)(2,1)S(1)} %get-tuple-element.44), channel_id=1, source_target_pairs={{0,16},{16,24},{24,8},{8,0},{1,17},{17,25},{25,9},{9,1},{2,18},{18... | collective-permute-start | bytes 491528 | tf_op jit(solution)/shard_map/ppermute | solution.py:524
  21.7 7.2 %collective-permute-start.10 = (bf16[64,1280]{1,0:T(8,128)(2,1)S(1)}, bf16[64,1280]{1,0:T(8,128)(2,1)S(1)}, u32[]{:S(2)}, u32[]{:S(2)}) collective-permute-start(bf16[64,1280]{1,0:T(8,128)(2,1)S(1)} %get-tuple-element.71), channel_id=1, source_target_pairs={{0,16},{16,24},{24,8},{8,0},{1,17},{17,25},{25,9},{9,1},{2,18},{18... | collective-permute-start | bytes 491528 | tf_op jit(solution)/shard_map/ppermute | solution.py:524
  23.5 7.0 %collective-permute-start.9 = (bf16[64,1280]{1,0:T(8,128)(2,1)S(1)}, bf16[64,1280]{1,0:T(8,128)(2,1)S(1)}, u32[]{:S(2)}, u32[]{:S(2)}) collective-permute-start(bf16[64,1280]{1,0:T(8,128)(2,1)S(1)} %get-tuple-element.72), channel_id=1, source_target_pairs={{0,8},{8,24},{24,16},{16,0},{1,9},{9,25},{25,17},{17,1},{2,10},{10... | collective-permute-start | bytes 491528 | tf_op jit(solution)/shard_map/ppermute | solution.py:524
  24.1 8.5 %collective-permute-start.6 = (bf16[64,1280]{1,0:T(8,128)(2,1)S(1)}, bf16[64,1280]{1,0:T(8,128)(2,1)S(1)}, u32[]{:S(2)}, u32[]{:S(2)}) collective-permute-start(bf16[64,1280]{1,0:T(8,128)(2,1)S(1)} %get-tuple-element.64), channel_id=1, source_target_pairs={{0,8},{8,0},{16,24},{24,16},{1,9},{9,1},{17,25},{25,17},{2,10},{10... | collective-permute-start | bytes 491528 | tf_op jit(solution)/shard_map/ppermute | solution.py:524
  25.8 7.9 %collective-permute-start.5 = (bf16[64,1280]{1,0:T(8,128)(2,1)S(1)}, bf16[64,1280]{1,0:T(8,128)(2,1)S(1)}, u32[]{:S(2)}, u32[]{:S(2)}) collective-permute-start(bf16[64,1280]{1,0:T(8,128)(2,1)S(1)} %get-tuple-element.73), channel_id=1, source_target_pairs={{0,16},{16,0},{8,24},{24,8},{1,17},{17,1},{9,25},{25,9},{2,18},{18... | collective-permute-start | bytes 491528 | tf_op jit(solution)/shard_map/ppermute | solution.py:524
  30.7 5.4 %collective-permute-start.12 = (bf16[64,1280]{1,0:T(8,128)(2,1)S(1)}, bf16[64,1280]{1,0:T(8,128)(2,1)S(1)}, u32[]{:S(2)}, u32[]{:S(2)}) collective-permute-start(bf16[64,1280]{1,0:T(8,128)(2,1)S(1)} %get-tuple-element.58), channel_id=1, source_target_pairs={{0,8},{8,0},{16,24},{24,16},{1,9},{9,1},{17,25},{25,17},{2,10},{10... | collective-permute-start | bytes 491528 | tf_op jit(solution)/shard_map/ppermute | solution.py:524
  31.2 5.9 %collective-permute-start.11 = (bf16[64,1280]{1,0:T(8,128)(2,1)S(1)}, bf16[64,1280]{1,0:T(8,128)(2,1)S(1)}, u32[]{:S(2)}, u32[]{:S(2)}) collective-permute-start(bf16[64,1280]{1,0:T(8,128)(2,1)S(1)} %get-tuple-element.68), channel_id=1, source_target_pairs={{0,16},{16,0},{8,24},{24,8},{1,17},{17,1},{9,25},{25,9},{2,18},{18... | collective-permute-start | bytes 491528 | tf_op jit(solution)/shard_map/ppermute | solution.py:524

commit v18 on v15

--- a/solution.py
+++ b/solution.py
@@ -91,6 +91,12 @@
                 for part in parts
             ]
         )
+    totals = 0.0
+    for n in range(len(sets)):
+        part = jnp.concatenate([parts[n] for parts in weights], axis=0)
+        ones = jnp.ones((part.shape[1], LANES), part.dtype)
+        totals += jnp.dot(part, ones, preferred_element_type=jnp.float32)
+    scales = 1.0 / totals
     tiles = {}
     for parts, (start, members) in zip(weights, windows):
         lanes = slice(base + start, base + start + 2 * LANES)
@@ -98,11 +104,7 @@
             jnp.dot(part, value(lanes), preferred_element_type=jnp.float32)
             for part, (bias, value) in zip(parts, sets)
         )
-        totals = sum(
-            jnp.dot(part, jnp.ones((part.shape[1], LANES), part.dtype), preferred_element_type=jnp.float32)
-            for part in parts
-        )
-        scale = 1.0 / totals
+        scale = scales[members[0] * rows : (members[-1] + 1) * rows]
         for n, h in enumerate(members):
             for t in range(2):
                 low = start + t * LANES

time: 38.9 us -> 38.9 us (level)
  no operation moved by 1% of the time
where the time goes in v18:
time: 38.9 us; the launch traced here: 38.2 us
  starting transfers between devices  16.8 us (43%)
  Pallas kernels  11.1 us (29%)
  waiting for transfers between devices  8.15 us (21%)
  other arithmetic  1.3 us (3%)
  between operations  0.84 us (2%)
    ppermute x10, starting transfers between devices, local(): send = lambda block, route: lax.ppermute(block, 'grp', route)  13.3 us
    ppermute x10, waiting for transfers between devices, local(): send = lambda block, route: lax.ppermute(block, 'grp', route)  8.14 us
    pallas_call x1, Pallas kernels, attend_edges(): pl.pallas_call(functools.partial(kernel, reach), in_specs=[VMEM] * len(op...  3.03 us
    ppermute x2, starting transfers between devices, paired(): return lax.ppermute(block, axis, route)  2.98 us
    pallas_call x2, Pallas kernels, relay_last(): pl.pallas_call(functools.partial(relay_last_kernel, part, chunks, first_r...  1.99 us
    pallas_call x1, Pallas kernels, attend_middle(): pl.pallas_call(functools.partial(middle_kernel, reach), in_specs=[VMEM] *...  1.58 us
    pallas_call x2, Pallas kernels, pair_sums(): pl.pallas_call(functools.partial(sums_kernel, part, sizes), in_specs=[VME...  1.57 us
    pallas_call x1, Pallas kernels, pack_grads(): pl.pallas_call(pack_grads_kernel, in_specs=[far, VMEM] + [far] * len(othe...  1.19 us
  transfers between devices with their start and end apart: 13, of which 6 were waited for; matrix products, arithmetic and copies ran while one was open for 3% of the time, Pallas kernels for 26%

profile of v18, /device:TPU:0, one launch (start us, length us, event | category | flops | bytes accessed | tf_op | source)
XLA Modules:
  0.0 38.2 jit_solution(1268060719426765342)
XLA Ops:
  0.6 0.5 %collective-permute-start = (f32[1280]{0:T(1024)}, f32[1280]{0:T(1024)S(1)}, u32[]{:S(2)}, u32[]{:S(2)}) collective-permute-start(f32[1280]{0:T(1024)} %param.12), channel_id=1, source_target_pairs={{0,1},{1,0},{2,3},{3,2},{4,5},{5,4},{6,7},{7,6},{8,9},{9,8},{10,11... | collective-permute-start | bytes 15368 | tf_op jit(solution)/shard_map/ppermute | solution.py:492
  1.1 0.7 %and_select_fusion = (s32[1,128]{1,0:T(1,128)S(1)}, s32[1,128]{1,0:T(1,128)S(1)}) fusion(s32[1,1,128]{2,1,0:T(1,128)} %param.11, s32[1,1,128]{2,1,0:T(1,128)} %param.10), kind=kLoop, calls=%fused_computation.26 | loop fusion | flops 2816 | bytes 2048 | tf_op jit(solution)/shard_map/jit(remainder)/select_n | solution.py:517
  1.9 1.2 %pack_grads.1 = (bf16[128,1408]{1,0:T(8,128)(2,1)S(1)}, bf16[128,1408]{1,0:T(8,128)(2,1)S(1)}) custom-call(bf16[128,2560]{1,0:T(8,128)(2,1)} %bitcast.35, f32[2,128]{1,0:T(2,128)S(1)} %add_convert_fusion.4.mark_ref, bf16[128,2560]{1,0:T(8,128)(2,1)} %bitcast.31, bf16[128,2560]{1,0:T(8,128)(2,1)} %bitcast.23, bf16[128,2560]{1,0:T(8,128)(2,1)} %bitcast.27), custom_call_target="tpu_custom_call" | custom-call | bytes 1310720 | tf_op jit(solution)/shard_map/pack_grads/pallas_call | solution.py:321
  3.1 2.6 %collective-permute-start.1 = (bf16[128,1408]{1,0:T(8,128)(2,1)S(1)}, bf16[128,1408]{1,0:T(8,128)(2,1)}, u32[]{:S(2)}, u32[]{:S(2)}) collective-permute-start(bf16[128,1408]{1,0:T(8,128)(2,1)S(1)} %get-tuple-element.36.mine_ref), channel_id=1, source_target_pairs={{0,8},{8,0},{16,24},{24,16},{1,9},{9,1},{17,25},{25,17},{2,10},{10... | collective-permute-start | bytes 1081352 | tf_op jit(solution)/shard_map/ppermute | solution.py:513
  5.7 1.5 %collective-permute-start.2 = (bf16[128,1408]{1,0:T(8,128)(2,1)S(1)}, bf16[128,1408]{1,0:T(8,128)(2,1)S(1)}, u32[]{:S(2)}, u32[]{:S(2)}) collective-permute-start(bf16[128,1408]{1,0:T(8,128)(2,1)S(1)} %get-tuple-element.39.mine_ref), channel_id=1, source_target_pairs={{0,16},{16,0},{8,24},{24,8},{1,17},{17,1},{9,25},{25,9},{2,18},{18... | collective-permute-start | bytes 1081352 | tf_op jit(solution)/shard_map/ppermute | solution.py:513
  7.2 0.9 %pack_ends.1 = (bf16[32,5248]{1,0:T(8,128)(2,1)}, bf16[32,5248]{1,0:T(8,128)(2,1)}) custom-call(bf16[128,2560]{1,0:T(8,128)(2,1)S(1)} %bitcast.24, bf16[128,2560]{1,0:T(8,128)(2,1)S(1)} %bitcast.28, f32[1,128]{1,0:T(1,128)S(1)} %get-tuple-element.46.code_ref), custom_call_target="tpu_custom_call" | custom-call | bytes 1310720 | tf_op jit(solution)/shard_map/pack_ends/pallas_call | solution.py:249
  8.1 1.6 %collective-permute-start.7 = (bf16[32,5248]{1,0:T(8,128)(2,1)}, bf16[32,5248]{1,0:T(8,128)(2,1)}, u32[]{:S(2)}, u32[]{:S(2)}) collective-permute-start(bf16[32,5248]{1,0:T(8,128)(2,1)} %get-tuple-element.47), channel_id=1, source_target_pairs={{0,2},{2,0},{4,6},{6,4},{1,3},{3,1},{5,7},{7,5},{8,10},{10,8},{12,... | collective-permute-start | bytes 1007624 | tf_op jit(solution)/shard_map/ppermute | solution.py:32
  9.7 1.4 %collective-permute-start.8 = (bf16[32,5248]{1,0:T(8,128)(2,1)}, bf16[32,5248]{1,0:T(8,128)(2,1)}, u32[]{:S(2)}, u32[]{:S(2)}) collective-permute-start(bf16[32,5248]{1,0:T(8,128)(2,1)} %get-tuple-element.48), channel_id=1, source_target_pairs={{2,4},{4,2},{3,5},{5,3},{10,12},{12,10},{11,13},{13,11},{18,20},{2... | collective-permute-start | bytes 1007624 | tf_op jit(solution)/shard_map/ppermute | solution.py:32
  11.1 1.6 %attend_middle.1 = bf16[64,2560]{1,0:T(8,128)(2,1)S(1)} custom-call(bf16[128,2560]{1,0:T(8,128)(2,1)S(1)} %bitcast.32, bf16[128,2560]{1,0:T(8,128)(2,1)S(1)} %bitcast.25, bf16[128,2560]{1,0:T(8,128)(2,1)S(1)} %bitcast.29, f32[1,128]{1,0:T(1,128)S(1)} %get-tuple-element.46.code_ref), custom_call_target="tpu_custom_call" | custom-call | flops 268435456 | bytes 1966080 | tf_op jit(solution)/shard_map/attend_middle/pallas_call | solution.py:262
  12.8 2.1 %collective-permute-done.1.theirs_ref = bf16[128,1408]{1,0:T(8,128)(2,1)} collective-permute-done((bf16[128,1408]{1,0:T(8,128)(2,1)S(1)}, bf16[128,1408]{1,0:T(8,128)(2,1)}, u32[]{:S(2)}, u32[]{:S(2)}) %collective-permute-start.1) | collective-permute-done | bytes 360480 | tf_op jit(solution)/shard_map/ppermute | solution.py:513
  14.8 1.3 %pair_sums.2 = (bf16[64,1280]{1,0:T(8,128)(2,1)S(1)}, bf16[64,1280]{1,0:T(8,128)(2,1)S(1)}) custom-call(f32[1,2560]{1,0:T(1,128)S(1)} %broadcast_in_dim.9.gate_ref, f32[1,128]{1,0:T(1,128)S(1)} %get-tuple-element.86.row_ref, bf16[128,1408]{1,0:T(8,128)(2,1)S(1)} %get-tuple-element.36.mine_ref, bf16[128,1408]{1,0:T(8,128)(2,1)} %collective-permute-done.1.theirs_ref), custom_call_target="tpu_custom_call" | custom-call | flops 83886080 | bytes 983040 | tf_op jit(solution)/shard_map/pair_sums/pallas_call | solution.py:360
  16.5 1.7 %collective-permute-start.3 = (bf16[64,1280]{1,0:T(8,128)(2,1)S(1)}, bf16[64,1280]{1,0:T(8,128)(2,1)S(1)}, u32[]{:S(2)}, u32[]{:S(2)}) collective-permute-start(bf16[64,1280]{1,0:T(8,128)(2,1)S(1)} %get-tuple-element.42), channel_id=1, source_target_pairs={{0,8},{8,24},{24,16},{16,0},{1,9},{9,25},{25,17},{17,1},{2,10},{10... | collective-permute-start | bytes 491528 | tf_op jit(solution)/shard_map/ppermute | solution.py:513
  18.6 3.0 %attend_edges.1 = bf16[64,2560]{1,0:T(8,128)(2,1)S(1)} custom-call(bf16[128,2560]{1,0:T(8,128)(2,1)S(1)} %bitcast.33, bf16[128,2560]{1,0:T(8,128)(2,1)S(1)} %bitcast.26, bf16[128,2560]{1,0:T(8,128)(2,1)S(1)} %bitcast.30, f32[1,128]{1,0:T(1,128)S(1)} %get-tuple-element.46.code_ref, bf16[32,5248]{1,0:T(8,128)(2,1)} %collective-permute-done.7.one_ref, ...), custom_call_target="tpu_custom_call" | custom-call | flops 268435456 | bytes 1966080 | tf_op jit(solution)/shard_map/attend_edges/pallas_call | solution.py:283
  21.7 1.8 %collective-permute-start.10 = (bf16[64,1280]{1,0:T(8,128)(2,1)S(1)}, bf16[64,1280]{1,0:T(8,128)(2,1)S(1)}, u32[]{:S(2)}, u32[]{:S(2)}) collective-permute-start(bf16[64,1280]{1,0:T(8,128)(2,1)S(1)} %get-tuple-element.71), channel_id=1, source_target_pairs={{0,16},{16,24},{24,8},{8,0},{1,17},{17,25},{25,9},{9,1},{2,18},{18... | collective-permute-start | bytes 491528 | tf_op jit(solution)/shard_map/ppermute | solution.py:513
  24.1 1.7 %collective-permute-start.6 = (bf16[64,1280]{1,0:T(8,128)(2,1)S(1)}, bf16[64,1280]{1,0:T(8,128)(2,1)S(1)}, u32[]{:S(2)}, u32[]{:S(2)}) collective-permute-start(bf16[64,1280]{1,0:T(8,128)(2,1)S(1)} %get-tuple-element.64), channel_id=1, source_target_pairs={{0,8},{8,0},{16,24},{24,16},{1,9},{9,1},{17,25},{25,17},{2,10},{10... | collective-permute-start | bytes 491528 | tf_op jit(solution)/shard_map/ppermute | solution.py:513
  25.8 1.5 %collective-permute-start.5 = (bf16[64,1280]{1,0:T(8,128)(2,1)S(1)}, bf16[64,1280]{1,0:T(8,128)(2,1)S(1)}, u32[]{:S(2)}, u32[]{:S(2)}) collective-permute-start(bf16[64,1280]{1,0:T(8,128)(2,1)S(1)} %get-tuple-element.73), channel_id=1, source_target_pairs={{0,16},{16,0},{8,24},{24,8},{1,17},{17,1},{9,25},{25,9},{2,18},{18... | collective-permute-start | bytes 491528 | tf_op jit(solution)/shard_map/ppermute | solution.py:513
  27.3 1.6 %collective-permute-done.10 = bf16[64,1280]{1,0:T(8,128)(2,1)S(1)} collective-permute-done((bf16[64,1280]{1,0:T(8,128)(2,1)S(1)}, bf16[64,1280]{1,0:T(8,128)(2,1)S(1)}, u32[]{:S(2)}, u32[]{:S(2)}) %collective-permute-start.10) | collective-permute-done | bytes 163872 | tf_op jit(solution)/shard_map/ppermute | solution.py:513
  28.9 1.6 %collective-permute-done.9 = bf16[64,1280]{1,0:T(8,128)(2,1)S(1)} collective-permute-done((bf16[64,1280]{1,0:T(8,128)(2,1)S(1)}, bf16[64,1280]{1,0:T(8,128)(2,1)S(1)}, u32[]{:S(2)}, u32[]{:S(2)}) %collective-permute-start.9) | collective-permute-done | bytes 163872 | tf_op jit(solution)/shard_map/ppermute | solution.py:513
  31.2 1.3 %collective-permute-start.11 = (bf16[64,1280]{1,0:T(8,128)(2,1)S(1)}, bf16[64,1280]{1,0:T(8,128)(2,1)S(1)}, u32[]{:S(2)}, u32[]{:S(2)}) collective-permute-start(bf16[64,1280]{1,0:T(8,128)(2,1)S(1)} %get-tuple-element.68), channel_id=1, source_target_pairs={{0,16},{16,0},{8,24},{24,8},{1,17},{17,1},{9,25},{25,9},{2,18},{18... | collective-permute-start | bytes 491528 | tf_op jit(solution)/shard_map/ppermute | solution.py:513
  32.6 1.2 %collective-permute-done.5 = bf16[64,1280]{1,0:T(8,128)(2,1)S(1)} collective-permute-done((bf16[64,1280]{1,0:T(8,128)(2,1)S(1)}, bf16[64,1280]{1,0:T(8,128)(2,1)S(1)}, u32[]{:S(2)}, u32[]{:S(2)}) %collective-permute-start.5) | collective-permute-done | bytes 163872 | tf_op jit(solution)/shard_map/ppermute | solution.py:513
  33.8 0.8 %relay_first.1 = (bf16[128,2560]{1,0:T(8,128)(2,1)}, f32[128,2560]{1,0:T(8,128)S(1)}, bf16[128,64]{1,0:T(8,128)(2,1)S(1)}) custom-call(f32[1,128]{1,0:T(1,128)S(1)} %get-tuple-element.86.row_ref, f32[1,2560]{1,0:T(1,128)S(1)} %broadcast_in_dim.9.gate_ref, bf16[64,1280]{1,0:T(8,128)(2,1)S(1)} %get-tuple-element.80.a_ref, ...), custom_call_target="tpu_custom_call" | custom-call | flops 83886080 | bytes 7864320 | tf_op jit(solution)/shard_map/relay_first/pallas_call | solution.py:408
  34.6 1.6 %collective-permute-done.12.got_ref = bf16[64,1280]{1,0:T(8,128)(2,1)S(1)} collective-permute-done((bf16[64,1280]{1,0:T(8,128)(2,1)S(1)}, bf16[64,1280]{1,0:T(8,128)(2,1)S(1)}, u32[]{:S(2)}, u32[]{:S(2)}) %collective-permute-start.12) | collective-permute-done | bytes 163872 | tf_op jit(solution)/shard_map/ppermute | solution.py:513
  36.2 1.0 %relay_last.2 = (bf16[128,2560]{1,0:T(8,128)(2,1)}, bf16[128,2560]{1,0:T(8,128)(2,1)}) custom-call(bf16[128,64]{1,0:T(8,128)(2,1)S(1)} %get-tuple-element.49.picks_ref, f32[1,2560]{1,0:T(1,128)S(1)} %broadcast_in_dim.9.gate_ref, bf16[64,1280]{1,0:T(8,128)(2,1)S(1)} %get-tuple-element.60.held_ref, ...), custom_call_target="tpu_custom_call", output_to_operand_aliasing={{0}: (6, {})} | custom-call | flops 41943040 | bytes 1966080 | tf_op jit(solution)/shard_map/relay_last/pallas_call | solution.py:468
  37.2 1.0 %relay_last.3 = (bf16[128,2560]{1,0:T(8,128)(2,1)}, bf16[128,2560]{1,0:T(8,128)(2,1)}) custom-call(bf16[128,64]{1,0:T(8,128)(2,1)S(1)} %get-tuple-element.49.picks_ref, f32[1,2560]{1,0:T(1,128)S(1)} %broadcast_in_dim.9.gate_ref, bf16[64,1280]{1,0:T(8,128)(2,1)S(1)} %get-tuple-element.70.held_ref, ...), custom_call_target="tpu_custom_call", output_to_operand_aliasing={{0}: (6, {}), {1}: (7, {})} | custom-call | flops 41943040 | bytes 1966080 | tf_op jit(solution)/shard_map/relay_last/pallas_call | solution.py:468
  (32 shorter events, 2.2 us)
Async XLA Ops:
  0.6 12.1 %collective-permute-start = (f32[1280]{0:T(1024)}, f32[1280]{0:T(1024)S(1)}, u32[]{:S(2)}, u32[]{:S(2)}) collective-permute-start(f32[1280]{0:T(1024)} %param.12), channel_id=1, source_target_pairs={{0,1},{1,0},{2,3},{3,2},{4,5},{5,4},{6,7},{7,6},{8,9},{9,8},{10,11... | collective-permute-start | bytes 15368 | tf_op jit(solution)/shard_map/ppermute | solution.py:492
  1.9 5.3 %copy-start = (bf16[1,1,128,2560]{3,2,1,0:T(8,128)(2,1)S(1)}, bf16[1,1,128,2560]{3,2,1,0:T(8,128)(2,1)}, u32[]{:S(2)}) copy-start(bf16[1,1,128,2560]{3,2,1,0:T(8,128)(2,1)} %param.8) | copy-start | bytes 1966084
  1.9 5.3 %copy-start.1 = (bf16[1,1,128,2560]{3,2,1,0:T(8,128)(2,1)S(1)}, bf16[1,1,128,2560]{3,2,1,0:T(8,128)(2,1)}, u32[]{:S(2)}) copy-start(bf16[1,1,128,2560]{3,2,1,0:T(8,128)(2,1)} %param.9) | copy-start | bytes 1966084
  3.1 8.0 %copy-start.2 = (bf16[1,1,128,2560]{3,2,1,0:T(8,128)(2,1)S(1)}, bf16[1,1,128,2560]{3,2,1,0:T(8,128)(2,1)}, u32[]{:S(2)}) copy-start(bf16[1,1,128,2560]{3,2,1,0:T(8,128)(2,1)} %param.7) | copy-start | bytes 1966084
  3.1 11.7 %collective-permute-start.1 = (bf16[128,1408]{1,0:T(8,128)(2,1)S(1)}, bf16[128,1408]{1,0:T(8,128)(2,1)}, u32[]{:S(2)}, u32[]{:S(2)}) collective-permute-start(bf16[128,1408]{1,0:T(8,128)(2,1)S(1)} %get-tuple-element.36.mine_ref), channel_id=1, source_target_pairs={{0,8},{8,0},{16,24},{24,16},{1,9},{9,1},{17,25},{25,17},{2,10},{10... | collective-permute-start | bytes 1081352 | tf_op jit(solution)/shard_map/ppermute | solution.py:513
  5.7 10.5 %collective-permute-start.2 = (bf16[128,1408]{1,0:T(8,128)(2,1)S(1)}, bf16[128,1408]{1,0:T(8,128)(2,1)S(1)}, u32[]{:S(2)}, u32[]{:S(2)}) collective-permute-start(bf16[128,1408]{1,0:T(8,128)(2,1)S(1)} %get-tuple-element.39.mine_ref), channel_id=1, source_target_pairs={{0,16},{16,0},{8,24},{24,8},{1,17},{17,1},{9,25},{25,9},{2,18},{18... | collective-permute-start | bytes 1081352 | tf_op jit(solution)/shard_map/ppermute | solution.py:513
  8.1 4.6 %copy-start.3 = (f32[1280]{0:T(1024)S(1)}, f32[1280]{0:T(1024)}, u32[]{:S(2)}) copy-start(f32[1280]{0:T(1024)} %param.12) | copy-start | bytes 15364
  8.1 10.5 %collective-permute-start.7 = (bf16[32,5248]{1,0:T(8,128)(2,1)}, bf16[32,5248]{1,0:T(8,128)(2,1)}, u32[]{:S(2)}, u32[]{:S(2)}) collective-permute-start(bf16[32,5248]{1,0:T(8,128)(2,1)} %get-tuple-element.47), channel_id=1, source_target_pairs={{0,2},{2,0},{4,6},{6,4},{1,3},{3,1},{5,7},{7,5},{8,10},{10,8},{12,... | collective-permute-start | bytes 1007624 | tf_op jit(solution)/shard_map/ppermute | solution.py:32
  9.7 8.9 %collective-permute-start.8 = (bf16[32,5248]{1,0:T(8,128)(2,1)}, bf16[32,5248]{1,0:T(8,128)(2,1)}, u32[]{:S(2)}, u32[]{:S(2)}) collective-permute-start(bf16[32,5248]{1,0:T(8,128)(2,1)} %get-tuple-element.48), channel_id=1, source_target_pairs={{2,4},{4,2},{3,5},{5,3},{10,12},{12,10},{11,13},{13,11},{18,20},{2... | collective-permute-start | bytes 1007624 | tf_op jit(solution)/shard_map/ppermute | solution.py:32
  16.5 7.3 %collective-permute-start.3 = (bf16[64,1280]{1,0:T(8,128)(2,1)S(1)}, bf16[64,1280]{1,0:T(8,128)(2,1)S(1)}, u32[]{:S(2)}, u32[]{:S(2)}) collective-permute-start(bf16[64,1280]{1,0:T(8,128)(2,1)S(1)} %get-tuple-element.42), channel_id=1, source_target_pairs={{0,8},{8,24},{24,16},{16,0},{1,9},{9,25},{25,17},{17,1},{2,10},{10... | collective-permute-start | bytes 491528 | tf_op jit(solution)/shard_map/ppermute | solution.py:513
  18.3 5.6 %collective-permute-start.4 = (bf16[64,1280]{1,0:T(8,128)(2,1)S(1)}, bf16[64,1280]{1,0:T(8,128)(2,1)S(1)}, u32[]{:S(2)}, u32[]{:S(2)}) collective-permute-start(bf16[64,1280]{1,0:T(8,128)(2,1)S(1)} %get-tuple-element.44), channel_id=1, source_target_pairs={{0,16},{16,24},{24,8},{8,0},{1,17},{17,25},{25,9},{9,1},{2,18},{18... | collective-permute-start | bytes 491528 | tf_op jit(solution)/shard_map/ppermute | solution.py:513
  21.7 7.2 %collective-permute-start.10 = (bf16[64,1280]{1,0:T(8,128)(2,1)S(1)}, bf16[64,1280]{1,0:T(8,128)(2,1)S(1)}, u32[]{:S(2)}, u32[]{:S(2)}) collective-permute-start(bf16[64,1280]{1,0:T(8,128)(2,1)S(1)} %get-tuple-element.71), channel_id=1, source_target_pairs={{0,16},{16,24},{24,8},{8,0},{1,17},{17,25},{25,9},{9,1},{2,18},{18... | collective-permute-start | bytes 491528 | tf_op jit(solution)/shard_map/ppermute | solution.py:513
  23.5 7.1 %collective-permute-start.9 = (bf16[64,1280]{1,0:T(8,128)(2,1)S(1)}, bf16[64,1280]{1,0:T(8,128)(2,1)S(1)}, u32[]{:S(2)}, u32[]{:S(2)}) collective-permute-start(bf16[64,1280]{1,0:T(8,128)(2,1)S(1)} %get-tuple-element.72), channel_id=1, source_target_pairs={{0,8},{8,24},{24,16},{16,0},{1,9},{9,25},{25,17},{17,1},{2,10},{10... | collective-permute-start | bytes 491528 | tf_op jit(solution)/shard_map/ppermute | solution.py:513
  24.1 8.5 %collective-permute-start.6 = (bf16[64,1280]{1,0:T(8,128)(2,1)S(1)}, bf16[64,1280]{1,0:T(8,128)(2,1)S(1)}, u32[]{:S(2)}, u32[]{:S(2)}) collective-permute-start(bf16[64,1280]{1,0:T(8,128)(2,1)S(1)} %get-tuple-element.64), channel_id=1, source_target_pairs={{0,8},{8,0},{16,24},{24,16},{1,9},{9,1},{17,25},{25,17},{2,10},{10... | collective-permute-start | bytes 491528 | tf_op jit(solution)/shard_map/ppermute | solution.py:513
  25.8 7.9 %collective-permute-start.5 = (bf16[64,1280]{1,0:T(8,128)(2,1)S(1)}, bf16[64,1280]{1,0:T(8,128)(2,1)S(1)}, u32[]{:S(2)}, u32[]{:S(2)}) collective-permute-start(bf16[64,1280]{1,0:T(8,128)(2,1)S(1)} %get-tuple-element.73), channel_id=1, source_target_pairs={{0,16},{16,0},{8,24},{24,8},{1,17},{17,1},{9,25},{25,9},{2,18},{18... | collective-permute-start | bytes 491528 | tf_op jit(solution)/shard_map/ppermute | solution.py:513
  30.8 5.4 %collective-permute-start.12 = (bf16[64,1280]{1,0:T(8,128)(2,1)S(1)}, bf16[64,1280]{1,0:T(8,128)(2,1)S(1)}, u32[]{:S(2)}, u32[]{:S(2)}) collective-permute-start(bf16[64,1280]{1,0:T(8,128)(2,1)S(1)} %get-tuple-element.58), channel_id=1, source_target_pairs={{0,8},{8,0},{16,24},{24,16},{1,9},{9,1},{17,25},{25,17},{2,10},{10... | collective-permute-start | bytes 491528 | tf_op jit(solution)/shard_map/ppermute | solution.py:513
  31.2 5.9 %collective-permute-start.11 = (bf16[64,1280]{1,0:T(8,128)(2,1)S(1)}, bf16[64,1280]{1,0:T(8,128)(2,1)S(1)}, u32[]{:S(2)}, u32[]{:S(2)}) collective-permute-start(bf16[64,1280]{1,0:T(8,128)(2,1)S(1)} %get-tuple-element.68), channel_id=1, source_target_pairs={{0,16},{16,0},{8,24},{24,8},{1,17},{17,1},{9,25},{25,9},{2,18},{18... | collective-permute-start | bytes 491528 | tf_op jit(solution)/shard_map/ppermute | solution.py:513

commit v19 on v15

--- a/solution.py
+++ b/solution.py
@@ -22,14 +22,22 @@
     return lax.ppermute(block, axis, route)
 
 
-def paired(block, axis, first):
-    size = lax.axis_size(axis)
+def paired(block, first):
+    size, ranks = lax.axis_size("seq"), lax.axis_size("rep")
     route = []
     for i in range(size):
         other = i + 1 if (i - first) % 2 == 0 else i - 1
-        if 0 <= other < size:
-            route.append((i, other))
-    return lax.ppermute(block, axis, route)
+        for rank in range(ranks):
+            if 0 <= other < size:
+                route.append((i * ranks + rank, other * ranks + rank))
+            elif rank ^ 1 < ranks:
+                route.append((i * ranks + rank, i * ranks + (rank ^ 1)))
+    return lax.ppermute(block, ("seq", "rep"), route)
+
+
+def neighbours_there(ranks):
+    rank = lax.axis_index("seq")
+    return jnp.where(rank > 0, 1.0, 0.0), jnp.where(rank < ranks - 1, 1.0, 0.0)
 
 
 def lane_windows(heads):
@@ -164,7 +172,8 @@
         store_period(base, mixed_period(base, scores, sets, period), out_ref)
 
 
-def sides_kernel(reach, q_ref, k_ref, v_ref, code_ref, one_ref, two_ref, *refs):
+def sides_kernel(reach, ranks, q_ref, k_ref, v_ref, code_ref, one_ref, two_ref, *refs):
+    there = neighbours_there(ranks)
     out_ref, keys, values, codes = refs
     tokens, width = q_ref.shape
     near = 2 * reach
@@ -182,7 +191,7 @@
         codes[side, :near] = code[own]
         keys[side, near : near + reach] = halo[:, :width]
         values[side, near : near + reach] = halo[:, width : 2 * width]
-        codes[side, near : near + reach] = halo[:, 2 * width :].astype(jnp.float32)
+        codes[side, near : near + reach] = halo[:, 2 * width :].astype(jnp.float32) * there[side]
         spare = keys.shape[1] - near - reach
         if spare:
             for ref in (keys, values, codes):
@@ -201,17 +210,21 @@
             store_period(base, tiles, out_ref.at[side * reach : (side + 1) * reach])
 
 
-def edge_kernel(reach, q_ref, k_ref, v_ref, code_ref, *refs):
+def edge_kernel(reach, ranks, q_ref, k_ref, v_ref, code_ref, *refs):
+    below, above = neighbours_there(ranks)
+    even = lax.axis_index("seq") % 2 == 0
+    there = [jnp.where(even, above, below), jnp.where(even, below, above)]
     halos = refs[:-4]
     out_ref, keys, values, codes = refs[-4:]
     width = q_ref.shape[1]
     code = columns(code_ref[...])
     at = 0
-    for piece in halos:
+    for n, piece in enumerate(halos):
         rows = piece.shape[0]
+        known = there[n] if n < 2 else 1.0
         keys[at : at + rows] = piece[:, :width]
         values[at : at + rows] = piece[:, width : 2 * width]
-        codes[at : at + rows] = piece[:, 2 * width :].astype(jnp.float32)
+        codes[at : at + rows] = piece[:, 2 * width :].astype(jnp.float32) * known
         at += rows
     if at < keys.shape[0]:
         for ref in (keys, values, codes):
@@ -279,7 +292,7 @@
         held = (-(-2 * reach // LANES) * LANES,)
     operands = [queries, keys, values, code, *halos]
     return pl.pallas_call(
-        functools.partial(kernel, reach),
+        functools.partial(kernel, reach, lax.axis_size("seq")),
         in_specs=[VMEM] * len(operands),
         out_specs=VMEM,
         out_shape=jax.ShapeDtypeStruct((rows, width), jnp.bfloat16),
@@ -523,7 +536,7 @@
     code, end_one, end_two = lax.optimization_barrier((code, end_one, end_two))
     own = [attend_middle(queries, keys, values, code, reach)] if tokens > 2 * reach else []
     gate = whole_gate(control_gate)[None]
-    halos = [paired(end_one, "seq", 0), paired(end_two, "seq", 1)]
+    halos = [paired(end_one, 0), paired(end_two, 1)]
     for hop in range(2, hops + 1):
         count = min(tokens, reach - (hop - 1) * tokens)
         tail, head = jnp.where(even, end_one, end_two), jnp.where(even, end_two, end_one)

time: 38.9 us -> 38.3 us (0.985); the launches traced: 38.2 us -> 38.1 us
  starting transfers between devices: 16.8 us -> 15.4 us
  waiting for transfers between devices: 8.03 us -> 9.4 us
    ppermute x2, starting transfers between devices: 2.98 us -> 1.58 us  [paired(): return lax.ppermute(block, ('seq', 'rep'), route)]
    ppermute x10, waiting for transfers between devices: 8.02 us -> 9.39 us  [local(): send = lambda block, route: lax.ppermute(block, 'grp', route)]
  transfers between devices with their start and end apart: 13 -> 13, of which waited for: 6 -> 6; matrix products, arithmetic and copies ran while one was open for 3% -> 4% of each run, Pallas kernels for 26% -> 27%
where the time goes in v19:
time: 38.3 us; the launch traced here: 38.1 us
  starting transfers between devices  15.4 us (40%)
  Pallas kernels  11.1 us (29%)
  waiting for transfers between devices  9.4 us (25%)
  other arithmetic  1.3 us (3%)
  between operations  0.84 us (2%)
    ppermute x10, starting transfers between devices, local(): send = lambda block, route: lax.ppermute(block, 'grp', route)  13.4 us
    ppermute x10, waiting for transfers between devices, local(): send = lambda block, route: lax.ppermute(block, 'grp', route)  9.39 us
    pallas_call x1, Pallas kernels, attend_edges(): pl.pallas_call(functools.partial(kernel, reach, lax.axis_size('seq')), in...  3.04 us
    pallas_call x2, Pallas kernels, relay_last(): pl.pallas_call(functools.partial(relay_last_kernel, part, chunks, first_r...  1.99 us
    pallas_call x1, Pallas kernels, attend_middle(): pl.pallas_call(functools.partial(middle_kernel, reach), in_specs=[VMEM] *...  1.61 us
    ppermute x2, starting transfers between devices, paired(): return lax.ppermute(block, ('seq', 'rep'), route)  1.58 us
    pallas_call x2, Pallas kernels, pair_sums(): pl.pallas_call(functools.partial(sums_kernel, part, sizes), in_specs=[VME...  1.57 us
    pallas_call x1, Pallas kernels, pack_grads(): pl.pallas_call(pack_grads_kernel, in_specs=[far, VMEM] + [far] * len(othe...  1.19 us
  transfers between devices with their start and end apart: 13, of which 6 were waited for; matrix products, arithmetic and copies ran while one was open for 4% of the time, Pallas kernels for 27%

profile of v19, /device:TPU:0, one launch (start us, length us, event | category | flops | bytes accessed | tf_op | source)
XLA Modules:
  0.0 38.1 jit_solution(5746805717124755146)
XLA Ops:
  0.6 0.5 %collective-permute-start = (f32[1280]{0:T(1024)}, f32[1280]{0:T(1024)S(1)}, u32[]{:S(2)}, u32[]{:S(2)}) collective-permute-start(f32[1280]{0:T(1024)} %param.12), channel_id=1, source_target_pairs={{0,1},{1,0},{2,3},{3,2},{4,5},{5,4},{6,7},{7,6},{8,9},{9,8},{10,11... | collective-permute-start | bytes 15368 | tf_op jit(solution)/shard_map/ppermute | solution.py:503
  1.1 0.7 %and_select_fusion = (s32[1,128]{1,0:T(1,128)S(1)}, s32[1,128]{1,0:T(1,128)S(1)}) fusion(s32[1,1,128]{2,1,0:T(1,128)} %param.11, s32[1,1,128]{2,1,0:T(1,128)} %param.10), kind=kLoop, calls=%fused_computation.26 | loop fusion | flops 2816 | bytes 2048 | tf_op jit(solution)/shard_map/jit(remainder)/select_n | solution.py:528
  1.9 1.2 %pack_grads.1 = (bf16[128,1408]{1,0:T(8,128)(2,1)S(1)}, bf16[128,1408]{1,0:T(8,128)(2,1)S(1)}) custom-call(bf16[128,2560]{1,0:T(8,128)(2,1)} %bitcast.35, f32[2,128]{1,0:T(2,128)S(1)} %add_convert_fusion.4.mark_ref, bf16[128,2560]{1,0:T(8,128)(2,1)} %bitcast.31, bf16[128,2560]{1,0:T(8,128)(2,1)} %bitcast.23, bf16[128,2560]{1,0:T(8,128)(2,1)} %bitcast.27), custom_call_target="tpu_custom_call" | custom-call | bytes 1310720 | tf_op jit(solution)/shard_map/pack_grads/pallas_call | solution.py:332
  3.1 2.6 %collective-permute-start.1 = (bf16[128,1408]{1,0:T(8,128)(2,1)S(1)}, bf16[128,1408]{1,0:T(8,128)(2,1)}, u32[]{:S(2)}, u32[]{:S(2)}) collective-permute-start(bf16[128,1408]{1,0:T(8,128)(2,1)S(1)} %get-tuple-element.36.mine_ref), channel_id=1, source_target_pairs={{0,8},{8,0},{16,24},{24,16},{1,9},{9,1},{17,25},{25,17},{2,10},{10... | collective-permute-start | bytes 1081352 | tf_op jit(solution)/shard_map/ppermute | solution.py:524
  5.7 1.5 %collective-permute-start.2 = (bf16[128,1408]{1,0:T(8,128)(2,1)S(1)}, bf16[128,1408]{1,0:T(8,128)(2,1)S(1)}, u32[]{:S(2)}, u32[]{:S(2)}) collective-permute-start(bf16[128,1408]{1,0:T(8,128)(2,1)S(1)} %get-tuple-element.39.mine_ref), channel_id=1, source_target_pairs={{0,16},{16,0},{8,24},{24,8},{1,17},{17,1},{9,25},{25,9},{2,18},{18... | collective-permute-start | bytes 1081352 | tf_op jit(solution)/shard_map/ppermute | solution.py:524
  7.2 0.9 %pack_ends.1 = (bf16[32,5248]{1,0:T(8,128)(2,1)}, bf16[32,5248]{1,0:T(8,128)(2,1)}) custom-call(bf16[128,2560]{1,0:T(8,128)(2,1)S(1)} %bitcast.24, bf16[128,2560]{1,0:T(8,128)(2,1)S(1)} %bitcast.28, f32[1,128]{1,0:T(1,128)S(1)} %get-tuple-element.46.code_ref), custom_call_target="tpu_custom_call" | custom-call | bytes 1310720 | tf_op jit(solution)/shard_map/pack_ends/pallas_call | solution.py:260
  8.1 1.6 %collective-permute-start.7 = (bf16[32,5248]{1,0:T(8,128)(2,1)}, bf16[32,5248]{1,0:T(8,128)(2,1)}, u32[]{:S(2)}, u32[]{:S(2)}) collective-permute-start(bf16[32,5248]{1,0:T(8,128)(2,1)} %get-tuple-element.47), channel_id=1, source_target_pairs={{0,2},{1,3},{2,0},{3,1},{4,6},{5,7},{6,4},{7,5},{8,10},{9,11},{10,... | collective-permute-start | bytes 1007624 | tf_op jit(solution)/shard_map/ppermute | solution.py:35
  9.7 1.6 %attend_middle.1 = bf16[64,2560]{1,0:T(8,128)(2,1)S(1)} custom-call(bf16[128,2560]{1,0:T(8,128)(2,1)S(1)} %bitcast.32, bf16[128,2560]{1,0:T(8,128)(2,1)S(1)} %bitcast.25, bf16[128,2560]{1,0:T(8,128)(2,1)S(1)} %bitcast.29, f32[1,128]{1,0:T(1,128)S(1)} %get-tuple-element.46.code_ref), custom_call_target="tpu_custom_call" | custom-call | flops 268435456 | bytes 1966080 | tf_op jit(solution)/shard_map/attend_middle/pallas_call | solution.py:273
  11.4 3.4 %collective-permute-done.1.theirs_ref = bf16[128,1408]{1,0:T(8,128)(2,1)} collective-permute-done((bf16[128,1408]{1,0:T(8,128)(2,1)S(1)}, bf16[128,1408]{1,0:T(8,128)(2,1)}, u32[]{:S(2)}, u32[]{:S(2)}) %collective-permute-start.1) | collective-permute-done | bytes 360480 | tf_op jit(solution)/shard_map/ppermute | solution.py:524
  14.8 1.3 %pair_sums.2 = (bf16[64,1280]{1,0:T(8,128)(2,1)S(1)}, bf16[64,1280]{1,0:T(8,128)(2,1)S(1)}) custom-call(f32[1,2560]{1,0:T(1,128)S(1)} %broadcast_in_dim.9.gate_ref, f32[1,128]{1,0:T(1,128)S(1)} %get-tuple-element.86.row_ref, bf16[128,1408]{1,0:T(8,128)(2,1)S(1)} %get-tuple-element.36.mine_ref, bf16[128,1408]{1,0:T(8,128)(2,1)} %collective-permute-done.1.theirs_ref), custom_call_target="tpu_custom_call" | custom-call | flops 83886080 | bytes 983040 | tf_op jit(solution)/shard_map/pair_sums/pallas_call | solution.py:371
  16.5 1.7 %collective-permute-start.3 = (bf16[64,1280]{1,0:T(8,128)(2,1)S(1)}, bf16[64,1280]{1,0:T(8,128)(2,1)S(1)}, u32[]{:S(2)}, u32[]{:S(2)}) collective-permute-start(bf16[64,1280]{1,0:T(8,128)(2,1)S(1)} %get-tuple-element.42), channel_id=1, source_target_pairs={{0,8},{8,24},{24,16},{16,0},{1,9},{9,25},{25,17},{17,1},{2,10},{10... | collective-permute-start | bytes 491528 | tf_op jit(solution)/shard_map/ppermute | solution.py:524
  18.6 3.0 %attend_edges.1 = bf16[64,2560]{1,0:T(8,128)(2,1)S(1)} custom-call(bf16[128,2560]{1,0:T(8,128)(2,1)S(1)} %bitcast.33, bf16[128,2560]{1,0:T(8,128)(2,1)S(1)} %bitcast.26, bf16[128,2560]{1,0:T(8,128)(2,1)S(1)} %bitcast.30, f32[1,128]{1,0:T(1,128)S(1)} %get-tuple-element.46.code_ref, bf16[32,5248]{1,0:T(8,128)(2,1)} %collective-permute-done.7.one_ref, ...), custom_call_target="tpu_custom_call" | custom-call | flops 268435456 | bytes 1966080 | tf_op jit(solution)/shard_map/attend_edges/pallas_call | solution.py:294
  21.8 1.8 %collective-permute-start.10 = (bf16[64,1280]{1,0:T(8,128)(2,1)S(1)}, bf16[64,1280]{1,0:T(8,128)(2,1)S(1)}, u32[]{:S(2)}, u32[]{:S(2)}) collective-permute-start(bf16[64,1280]{1,0:T(8,128)(2,1)S(1)} %get-tuple-element.71), channel_id=1, source_target_pairs={{0,16},{16,24},{24,8},{8,0},{1,17},{17,25},{25,9},{9,1},{2,18},{18... | collective-permute-start | bytes 491528 | tf_op jit(solution)/shard_map/ppermute | solution.py:524
  24.1 1.7 %collective-permute-start.6 = (bf16[64,1280]{1,0:T(8,128)(2,1)S(1)}, bf16[64,1280]{1,0:T(8,128)(2,1)S(1)}, u32[]{:S(2)}, u32[]{:S(2)}) collective-permute-start(bf16[64,1280]{1,0:T(8,128)(2,1)S(1)} %get-tuple-element.64), channel_id=1, source_target_pairs={{0,8},{8,0},{16,24},{24,16},{1,9},{9,1},{17,25},{25,17},{2,10},{10... | collective-permute-start | bytes 491528 | tf_op jit(solution)/shard_map/ppermute | solution.py:524
  25.8 1.5 %collective-permute-start.5 = (bf16[64,1280]{1,0:T(8,128)(2,1)S(1)}, bf16[64,1280]{1,0:T(8,128)(2,1)S(1)}, u32[]{:S(2)}, u32[]{:S(2)}) collective-permute-start(bf16[64,1280]{1,0:T(8,128)(2,1)S(1)} %get-tuple-element.73), channel_id=1, source_target_pairs={{0,16},{16,0},{8,24},{24,8},{1,17},{17,1},{9,25},{25,9},{2,18},{18... | collective-permute-start | bytes 491528 | tf_op jit(solution)/shard_map/ppermute | solution.py:524
  27.4 1.6 %collective-permute-done.10 = bf16[64,1280]{1,0:T(8,128)(2,1)S(1)} collective-permute-done((bf16[64,1280]{1,0:T(8,128)(2,1)S(1)}, bf16[64,1280]{1,0:T(8,128)(2,1)S(1)}, u32[]{:S(2)}, u32[]{:S(2)}) %collective-permute-start.10) | collective-permute-done | bytes 163872 | tf_op jit(solution)/shard_map/ppermute | solution.py:524
  29.0 1.6 %collective-permute-done.9 = bf16[64,1280]{1,0:T(8,128)(2,1)S(1)} collective-permute-done((bf16[64,1280]{1,0:T(8,128)(2,1)S(1)}, bf16[64,1280]{1,0:T(8,128)(2,1)S(1)}, u32[]{:S(2)}, u32[]{:S(2)}) %collective-permute-start.9) | collective-permute-done | bytes 163872 | tf_op jit(solution)/shard_map/ppermute | solution.py:524
  30.7 0.5 %collective-permute-start.12 = (bf16[64,1280]{1,0:T(8,128)(2,1)S(1)}, bf16[64,1280]{1,0:T(8,128)(2,1)S(1)}, u32[]{:S(2)}, u32[]{:S(2)}) collective-permute-start(bf16[64,1280]{1,0:T(8,128)(2,1)S(1)} %get-tuple-element.58), channel_id=1, source_target_pairs={{0,8},{8,0},{16,24},{24,16},{1,9},{9,1},{17,25},{25,17},{2,10},{10... | collective-permute-start | bytes 491528 | tf_op jit(solution)/shard_map/ppermute | solution.py:524
  31.3 1.3 %collective-permute-start.11 = (bf16[64,1280]{1,0:T(8,128)(2,1)S(1)}, bf16[64,1280]{1,0:T(8,128)(2,1)S(1)}, u32[]{:S(2)}, u32[]{:S(2)}) collective-permute-start(bf16[64,1280]{1,0:T(8,128)(2,1)S(1)} %get-tuple-element.68), channel_id=1, source_target_pairs={{0,16},{16,0},{8,24},{24,8},{1,17},{17,1},{9,25},{25,9},{2,18},{18... | collective-permute-start | bytes 491528 | tf_op jit(solution)/shard_map/ppermute | solution.py:524
  32.6 1.2 %collective-permute-done.5 = bf16[64,1280]{1,0:T(8,128)(2,1)S(1)} collective-permute-done((bf16[64,1280]{1,0:T(8,128)(2,1)S(1)}, bf16[64,1280]{1,0:T(8,128)(2,1)S(1)}, u32[]{:S(2)}, u32[]{:S(2)}) %collective-permute-start.5) | collective-permute-done | bytes 163872 | tf_op jit(solution)/shard_map/ppermute | solution.py:524
  33.8 0.8 %relay_first.1 = (bf16[128,2560]{1,0:T(8,128)(2,1)}, f32[128,2560]{1,0:T(8,128)S(1)}, bf16[128,64]{1,0:T(8,128)(2,1)S(1)}) custom-call(f32[1,128]{1,0:T(1,128)S(1)} %get-tuple-element.86.row_ref, f32[1,2560]{1,0:T(1,128)S(1)} %broadcast_in_dim.9.gate_ref, bf16[64,1280]{1,0:T(8,128)(2,1)S(1)} %get-tuple-element.80.a_ref, ...), custom_call_target="tpu_custom_call" | custom-call | flops 83886080 | bytes 7864320 | tf_op jit(solution)/shard_map/relay_first/pallas_call | solution.py:419
  34.6 1.5 %collective-permute-done.12.got_ref = bf16[64,1280]{1,0:T(8,128)(2,1)S(1)} collective-permute-done((bf16[64,1280]{1,0:T(8,128)(2,1)S(1)}, bf16[64,1280]{1,0:T(8,128)(2,1)S(1)}, u32[]{:S(2)}, u32[]{:S(2)}) %collective-permute-start.12) | collective-permute-done | bytes 163872 | tf_op jit(solution)/shard_map/ppermute | solution.py:524
  36.1 1.0 %relay_last.2 = (bf16[128,2560]{1,0:T(8,128)(2,1)}, bf16[128,2560]{1,0:T(8,128)(2,1)}) custom-call(bf16[128,64]{1,0:T(8,128)(2,1)S(1)} %get-tuple-element.49.picks_ref, f32[1,2560]{1,0:T(1,128)S(1)} %broadcast_in_dim.9.gate_ref, bf16[64,1280]{1,0:T(8,128)(2,1)S(1)} %get-tuple-element.60.held_ref, ...), custom_call_target="tpu_custom_call", output_to_operand_aliasing={{0}: (6, {})} | custom-call | flops 41943040 | bytes 1966080 | tf_op jit(solution)/shard_map/relay_last/pallas_call | solution.py:479
  37.1 1.0 %relay_last.3 = (bf16[128,2560]{1,0:T(8,128)(2,1)}, bf16[128,2560]{1,0:T(8,128)(2,1)}) custom-call(bf16[128,64]{1,0:T(8,128)(2,1)S(1)} %get-tuple-element.49.picks_ref, f32[1,2560]{1,0:T(1,128)S(1)} %broadcast_in_dim.9.gate_ref, bf16[64,1280]{1,0:T(8,128)(2,1)S(1)} %get-tuple-element.70.held_ref, ...), custom_call_target="tpu_custom_call", output_to_operand_aliasing={{0}: (6, {}), {1}: (7, {})} | custom-call | flops 41943040 | bytes 1966080 | tf_op jit(solution)/shard_map/relay_last/pallas_call | solution.py:479
  (32 shorter events, 1.7 us)
Async XLA Ops:
  0.6 10.7 %collective-permute-start = (f32[1280]{0:T(1024)}, f32[1280]{0:T(1024)S(1)}, u32[]{:S(2)}, u32[]{:S(2)}) collective-permute-start(f32[1280]{0:T(1024)} %param.12), channel_id=1, source_target_pairs={{0,1},{1,0},{2,3},{3,2},{4,5},{5,4},{6,7},{7,6},{8,9},{9,8},{10,11... | collective-permute-start | bytes 15368 | tf_op jit(solution)/shard_map/ppermute | solution.py:503
  1.9 5.3 %copy-start = (bf16[1,1,128,2560]{3,2,1,0:T(8,128)(2,1)S(1)}, bf16[1,1,128,2560]{3,2,1,0:T(8,128)(2,1)}, u32[]{:S(2)}) copy-start(bf16[1,1,128,2560]{3,2,1,0:T(8,128)(2,1)} %param.8) | copy-start | bytes 1966084
  1.9 5.3 %copy-start.1 = (bf16[1,1,128,2560]{3,2,1,0:T(8,128)(2,1)S(1)}, bf16[1,1,128,2560]{3,2,1,0:T(8,128)(2,1)}, u32[]{:S(2)}) copy-start(bf16[1,1,128,2560]{3,2,1,0:T(8,128)(2,1)} %param.9) | copy-start | bytes 1966084
  3.1 6.6 %copy-start.2 = (bf16[1,1,128,2560]{3,2,1,0:T(8,128)(2,1)S(1)}, bf16[1,1,128,2560]{3,2,1,0:T(8,128)(2,1)}, u32[]{:S(2)}) copy-start(bf16[1,1,128,2560]{3,2,1,0:T(8,128)(2,1)} %param.7) | copy-start | bytes 1966084
  3.1 11.7 %collective-permute-start.1 = (bf16[128,1408]{1,0:T(8,128)(2,1)S(1)}, bf16[128,1408]{1,0:T(8,128)(2,1)}, u32[]{:S(2)}, u32[]{:S(2)}) collective-permute-start(bf16[128,1408]{1,0:T(8,128)(2,1)S(1)} %get-tuple-element.36.mine_ref), channel_id=1, source_target_pairs={{0,8},{8,0},{16,24},{24,16},{1,9},{9,1},{17,25},{25,17},{2,10},{10... | collective-permute-start | bytes 1081352 | tf_op jit(solution)/shard_map/ppermute | solution.py:524
  5.7 10.5 %collective-permute-start.2 = (bf16[128,1408]{1,0:T(8,128)(2,1)S(1)}, bf16[128,1408]{1,0:T(8,128)(2,1)S(1)}, u32[]{:S(2)}, u32[]{:S(2)}) collective-permute-start(bf16[128,1408]{1,0:T(8,128)(2,1)S(1)} %get-tuple-element.39.mine_ref), channel_id=1, source_target_pairs={{0,16},{16,0},{8,24},{24,8},{1,17},{17,1},{9,25},{25,9},{2,18},{18... | collective-permute-start | bytes 1081352 | tf_op jit(solution)/shard_map/ppermute | solution.py:524
  8.1 3.2 %copy-start.3 = (f32[1280]{0:T(1024)S(1)}, f32[1280]{0:T(1024)}, u32[]{:S(2)}) copy-start(f32[1280]{0:T(1024)} %param.12) | copy-start | bytes 15364
  8.1 10.5 %collective-permute-start.7 = (bf16[32,5248]{1,0:T(8,128)(2,1)}, bf16[32,5248]{1,0:T(8,128)(2,1)}, u32[]{:S(2)}, u32[]{:S(2)}) collective-permute-start(bf16[32,5248]{1,0:T(8,128)(2,1)} %get-tuple-element.47), channel_id=1, source_target_pairs={{0,2},{1,3},{2,0},{3,1},{4,6},{5,7},{6,4},{7,5},{8,10},{9,11},{10,... | collective-permute-start | bytes 1007624 | tf_op jit(solution)/shard_map/ppermute | solution.py:35
  9.7 8.9 %collective-permute-start.8 = (bf16[32,5248]{1,0:T(8,128)(2,1)}, bf16[32,5248]{1,0:T(8,128)(2,1)}, u32[]{:S(2)}, u32[]{:S(2)}) collective-permute-start(bf16[32,5248]{1,0:T(8,128)(2,1)} %get-tuple-element.48), channel_id=1, source_target_pairs={{0,1},{1,0},{2,4},{3,5},{4,2},{5,3},{6,7},{7,6},{8,9},{9,8},{10,12... | collective-permute-start | bytes 1007624 | tf_op jit(solution)/shard_map/ppermute | solution.py:35
  16.5 7.3 %collective-permute-start.3 = (bf16[64,1280]{1,0:T(8,128)(2,1)S(1)}, bf16[64,1280]{1,0:T(8,128)(2,1)S(1)}, u32[]{:S(2)}, u32[]{:S(2)}) collective-permute-start(bf16[64,1280]{1,0:T(8,128)(2,1)S(1)} %get-tuple-element.42), channel_id=1, source_target_pairs={{0,8},{8,24},{24,16},{16,0},{1,9},{9,25},{25,17},{17,1},{2,10},{10... | collective-permute-start | bytes 491528 | tf_op jit(solution)/shard_map/ppermute | solution.py:524
  18.3 5.6 %collective-permute-start.4 = (bf16[64,1280]{1,0:T(8,128)(2,1)S(1)}, bf16[64,1280]{1,0:T(8,128)(2,1)S(1)}, u32[]{:S(2)}, u32[]{:S(2)}) collective-permute-start(bf16[64,1280]{1,0:T(8,128)(2,1)S(1)} %get-tuple-element.44), channel_id=1, source_target_pairs={{0,16},{16,24},{24,8},{8,0},{1,17},{17,25},{25,9},{9,1},{2,18},{18... | collective-permute-start | bytes 491528 | tf_op jit(solution)/shard_map/ppermute | solution.py:524
  21.8 7.2 %collective-permute-start.10 = (bf16[64,1280]{1,0:T(8,128)(2,1)S(1)}, bf16[64,1280]{1,0:T(8,128)(2,1)S(1)}, u32[]{:S(2)}, u32[]{:S(2)}) collective-permute-start(bf16[64,1280]{1,0:T(8,128)(2,1)S(1)} %get-tuple-element.71), channel_id=1, source_target_pairs={{0,16},{16,24},{24,8},{8,0},{1,17},{17,25},{25,9},{9,1},{2,18},{18... | collective-permute-start | bytes 491528 | tf_op jit(solution)/shard_map/ppermute | solution.py:524
  23.5 7.0 %collective-permute-start.9 = (bf16[64,1280]{1,0:T(8,128)(2,1)S(1)}, bf16[64,1280]{1,0:T(8,128)(2,1)S(1)}, u32[]{:S(2)}, u32[]{:S(2)}) collective-permute-start(bf16[64,1280]{1,0:T(8,128)(2,1)S(1)} %get-tuple-element.72), channel_id=1, source_target_pairs={{0,8},{8,24},{24,16},{16,0},{1,9},{9,25},{25,17},{17,1},{2,10},{10... | collective-permute-start | bytes 491528 | tf_op jit(solution)/shard_map/ppermute | solution.py:524
  24.1 8.5 %collective-permute-start.6 = (bf16[64,1280]{1,0:T(8,128)(2,1)S(1)}, bf16[64,1280]{1,0:T(8,128)(2,1)S(1)}, u32[]{:S(2)}, u32[]{:S(2)}) collective-permute-start(bf16[64,1280]{1,0:T(8,128)(2,1)S(1)} %get-tuple-element.64), channel_id=1, source_target_pairs={{0,8},{8,0},{16,24},{24,16},{1,9},{9,1},{17,25},{25,17},{2,10},{10... | collective-permute-start | bytes 491528 | tf_op jit(solution)/shard_map/ppermute | solution.py:524
  25.8 7.9 %collective-permute-start.5 = (bf16[64,1280]{1,0:T(8,128)(2,1)S(1)}, bf16[64,1280]{1,0:T(8,128)(2,1)S(1)}, u32[]{:S(2)}, u32[]{:S(2)}) collective-permute-start(bf16[64,1280]{1,0:T(8,128)(2,1)S(1)} %get-tuple-element.73), channel_id=1, source_target_pairs={{0,16},{16,0},{8,24},{24,8},{1,17},{17,1},{9,25},{25,9},{2,18},{18... | collective-permute-start | bytes 491528 | tf_op jit(solution)/shard_map/ppermute | solution.py:524
  30.7 5.4 %collective-permute-start.12 = (bf16[64,1280]{1,0:T(8,128)(2,1)S(1)}, bf16[64,1280]{1,0:T(8,128)(2,1)S(1)}, u32[]{:S(2)}, u32[]{:S(2)}) collective-permute-start(bf16[64,1280]{1,0:T(8,128)(2,1)S(1)} %get-tuple-element.58), channel_id=1, source_target_pairs={{0,8},{8,0},{16,24},{24,16},{1,9},{9,1},{17,25},{25,17},{2,10},{10... | collective-permute-start | bytes 491528 | tf_op jit(solution)/shard_map/ppermute | solution.py:524
  31.3 5.9 %collective-permute-start.11 = (bf16[64,1280]{1,0:T(8,128)(2,1)S(1)}, bf16[64,1280]{1,0:T(8,128)(2,1)S(1)}, u32[]{:S(2)}, u32[]{:S(2)}) collective-permute-start(bf16[64,1280]{1,0:T(8,128)(2,1)S(1)} %get-tuple-element.68), channel_id=1, source_target_pairs={{0,16},{16,0},{8,24},{24,8},{1,17},{17,1},{9,25},{25,9},{2,18},{18... | collective-permute-start | bytes 491528 | tf_op jit(solution)/shard_map/ppermute | solution.py:524

commit v20 on v19

--- a/solution.py
+++ b/solution.py
@@ -434,63 +434,69 @@
     )(rows, gate, *branch, base, *totals)
 
 
-def relay_last_kernel(
-    part, chunks, first_row, picks_ref, gate_ref, held_ref, got_ref, base_ref, total_ref, *refs
-):
-    grad_ref, out_ref, staged, summed, sems, grad_sem = refs[-6:]
-    half = held_ref.shape[1]
-    other = 1 - part
+def relay_last_kernel(chunks, first_row, picks_ref, gate_ref, base_ref, *refs):
+    halves = (refs[:3], refs[3:6])
+    grad_ref, out_ref, staged, summed, sems, grad_sems = refs[-6:]
+    half = refs[0].shape[1]
+    rows = refs[0].shape[0]
     group = lax.axis_index("grp")
-    holds = group <= 1 if part == 0 else group % 2 == 0
-    summed[...] = jnp.where(holds, got_ref[...], total_ref[...])
-    to = grad_ref.at[pl.ds(first_row, total_ref.shape[0]), pl.ds(other * half, half)]
-    copies = [pltpu.make_async_copy(summed, to, grad_sem)]
-    copies[0].start()
+    holds = (group <= 1, group % 2 == 0)
+    copies = []
+    for part in (1, 0):
+        held_ref, got_ref, total_ref = halves[part]
+        other = 1 - part
+        summed[other] = jnp.where(holds[part], got_ref[...], total_ref[...])
+        to = grad_ref.at[pl.ds(first_row, rows), pl.ds(other * half, half)]
+        copies.append(pltpu.make_async_copy(summed.at[other], to, grad_sems.at[other]))
+        copies[-1].start()
     step = half // chunks
-    for c in range(chunks):
-        mine = slice(c * step, (c + 1) * step)
-        lanes = slice(part * half + c * step, part * half + (c + 1) * step)
-        branch = jnp.where(holds, held_ref[:, mine], got_ref[:, mine])
-        relayed = jnp.dot(picks_ref[...], branch, preferred_element_type=jnp.float32)
-        total = base_ref[:, lanes].astype(jnp.float32) + gate_ref[:, lanes] * relayed
-        staged[:, mine] = total.astype(staged.dtype)
-        copies.append(
-            pltpu.make_async_copy(
-                staged.at[:, pl.ds(c * step, step)],
-                out_ref.at[:, pl.ds(part * half + c * step, step)],
-                sems.at[c],
+    for part in (1, 0):
+        held_ref, got_ref, total_ref = halves[part]
+        for c in range(chunks):
+            mine = slice(c * step, (c + 1) * step)
+            first = part * half + c * step
+            lanes = slice(first, first + step)
+            branch = jnp.where(holds[part], held_ref[:, mine], got_ref[:, mine])
+            relayed = jnp.dot(picks_ref[...], branch, preferred_element_type=jnp.float32)
+            total = base_ref[:, lanes].astype(jnp.float32) + gate_ref[:, lanes] * relayed
+            staged[:, lanes] = total.astype(staged.dtype)
+            copies.append(
+                pltpu.make_async_copy(
+                    staged.at[:, pl.ds(first, step)],
+                    out_ref.at[:, pl.ds(first, step)],
+                    sems.at[part * chunks + c],
+                )
             )
-        )
-        copies[-1].start()
+            copies[-1].start()
     for copy in copies:
         copy.wait()
 
 
-def relay_last(picks, gate, held, got, base, total, part, first_row, grads, out):
+def relay_last(picks, gate, base, halves, first_row, grads):
     tokens, width = base.shape
     chunks = 2 if width // 2 % (2 * LANES) == 0 else 1
     far = pl.BlockSpec(memory_space=pltpu.HBM)
-    operands = [picks, gate, held, got, base, total]
+    operands = [picks, gate, base, *halves[0], *halves[1]]
+    known = len(operands)
     aliases = {}
-    for n, buffer in enumerate((grads, out)):
-        if buffer is not None:
-            aliases[len(operands)] = n
-            operands.append(buffer)
+    if grads is not None:
+        aliases[known] = 0
+        operands.append(grads)
     return pl.pallas_call(
-        functools.partial(relay_last_kernel, part, chunks, first_row),
-        in_specs=[VMEM] * 6 + [far] * len(aliases),
+        functools.partial(relay_last_kernel, chunks, first_row),
+        in_specs=[VMEM] * known + [far] * len(aliases),
         out_specs=[far] * 2,
         out_shape=[jax.ShapeDtypeStruct((tokens, width), jnp.bfloat16)] * 2,
         input_output_aliases=aliases,
         scratch_shapes=[
-            pltpu.VMEM((tokens, width // 2), jnp.bfloat16),
-            pltpu.VMEM(total.shape, jnp.bfloat16),
-            pltpu.SemaphoreType.DMA((chunks,)),
-            pltpu.SemaphoreType.DMA,
+            pltpu.VMEM((tokens, width), jnp.bfloat16),
+            pltpu.VMEM((2, *halves[0][0].shape), jnp.bfloat16),
+            pltpu.SemaphoreType.DMA((2 * chunks,)),
+            pltpu.SemaphoreType.DMA((2,)),
         ],
         compiler_params=PARAMS,
         cost_estimate=pl.CostEstimate(
-            flops=tokens * tokens * width, bytes_accessed=6 * tokens * width, transcendentals=0
+            flops=2 * tokens * tokens * width, bytes_accessed=12 * tokens * width, transcendentals=0
         ),
         name="relay_last",
     )(*operands)
@@ -592,13 +598,8 @@
             )
             first_row = piece.shape[0]
             continue
-        base, block_out = block_out, None
-        ends = ((held_a, down, total_b), (held_b, across, total_a))
-        for part in (1, 0):
-            held, got, total = ends[part]
-            branch_grad, block_out = relay_last(
-                picks, gate, held, got, base, total, part, first_row, branch_grad, block_out
-            )
+        halves = ((held_a, down, total_b), (held_b, across, total_a))
+        branch_grad, block_out = relay_last(picks, gate, block_out, halves, first_row, branch_grad)
     return (block_out[None, None], branch_grad[None])
 
 

time: 38.3 us -> 39 us (1.018)
  waiting for transfers between devices: 9.4 us -> 10.7 us
  Pallas kernels: 11.1 us -> 10.3 us
    ppermute x10, waiting for transfers between devices: 9.39 us -> 10.7 us  [local(): send = lambda block, route: lax.ppermute(block, 'grp', route)]
    pallas_call x2 -> x1, Pallas kernels: 1.99 us -> 1.2 us  [relay_last(): pl.pallas_call(functools.partial(relay_last_kernel, chunks, first_row), i...]
  transfers between devices with their start and end apart: 13 -> 13, of which waited for: 6 -> 7; matrix products, arithmetic and copies ran while one was open for 4% -> 3% of each run, Pallas kernels for 27% -> 24%
where the time goes in v20:
time: 39 us; the launch traced here: 38.7 us
  starting transfers between devices  15.6 us (40%)
  waiting for transfers between devices  10.7 us (27%)
  Pallas kernels  10.3 us (26%)
  other arithmetic  1.29 us (3%)
  between operations  0.82 us (2%)
    ppermute x10, starting transfers between devices, local(): send = lambda block, route: lax.ppermute(block, 'grp', route)  13.5 us
    ppermute x10, waiting for transfers between devices, local(): send = lambda block, route: lax.ppermute(block, 'grp', route)  10.7 us
    pallas_call x1, Pallas kernels, attend_edges(): pl.pallas_call(functools.partial(kernel, reach, lax.axis_size('seq')), in...  3.04 us
    pallas_call x1, Pallas kernels, attend_middle(): pl.pallas_call(functools.partial(middle_kernel, reach), in_specs=[VMEM] *...  1.61 us
    ppermute x2, starting transfers between devices, paired(): return lax.ppermute(block, ('seq', 'rep'), route)  1.58 us
    pallas_call x2, Pallas kernels, pair_sums(): pl.pallas_call(functools.partial(sums_kernel, part, sizes), in_specs=[VME...  1.57 us
    pallas_call x1, Pallas kernels, relay_last(): pl.pallas_call(functools.partial(relay_last_kernel, chunks, first_row), i...  1.2 us
    pallas_call x1, Pallas kernels, pack_grads(): pl.pallas_call(pack_grads_kernel, in_specs=[far, VMEM] + [far] * len(othe...  1.19 us
  transfers between devices with their start and end apart: 13, of which 7 were waited for; matrix products, arithmetic and copies ran while one was open for 3% of the time, Pallas kernels for 24%

profile of v20, /device:TPU:0, one launch (start us, length us, event | category | flops | bytes accessed | tf_op | source)
XLA Modules:
  0.0 38.7 jit_solution(1220368932422402177)
XLA Ops:
  0.6 0.5 %collective-permute-start = (f32[1280]{0:T(1024)}, f32[1280]{0:T(1024)S(1)}, u32[]{:S(2)}, u32[]{:S(2)}) collective-permute-start(f32[1280]{0:T(1024)} %param.12), channel_id=1, source_target_pairs={{0,1},{1,0},{2,3},{3,2},{4,5},{5,4},{6,7},{7,6},{8,9},{9,8},{10,11... | collective-permute-start | bytes 15368 | tf_op jit(solution)/shard_map/ppermute | solution.py:509
  1.1 0.7 %and_select_fusion = (s32[1,128]{1,0:T(1,128)S(1)}, s32[1,128]{1,0:T(1,128)S(1)}) fusion(s32[1,1,128]{2,1,0:T(1,128)} %param.11, s32[1,1,128]{2,1,0:T(1,128)} %param.10), kind=kLoop, calls=%fused_computation.26 | loop fusion | flops 2816 | bytes 2048 | tf_op jit(solution)/shard_map/jit(remainder)/select_n | solution.py:534
  1.9 1.2 %pack_grads.1 = (bf16[128,1408]{1,0:T(8,128)(2,1)S(1)}, bf16[128,1408]{1,0:T(8,128)(2,1)S(1)}) custom-call(bf16[128,2560]{1,0:T(8,128)(2,1)} %bitcast.35, f32[2,128]{1,0:T(2,128)S(1)} %add_convert_fusion.4.mark_ref, bf16[128,2560]{1,0:T(8,128)(2,1)} %bitcast.31, bf16[128,2560]{1,0:T(8,128)(2,1)} %bitcast.23, bf16[128,2560]{1,0:T(8,128)(2,1)} %bitcast.27), custom_call_target="tpu_custom_call" | custom-call | bytes 1310720 | tf_op jit(solution)/shard_map/pack_grads/pallas_call | solution.py:332
  3.1 2.6 %collective-permute-start.1 = (bf16[128,1408]{1,0:T(8,128)(2,1)S(1)}, bf16[128,1408]{1,0:T(8,128)(2,1)}, u32[]{:S(2)}, u32[]{:S(2)}) collective-permute-start(bf16[128,1408]{1,0:T(8,128)(2,1)S(1)} %get-tuple-element.34.mine_ref), channel_id=1, source_target_pairs={{0,8},{8,0},{16,24},{24,16},{1,9},{9,1},{17,25},{25,17},{2,10},{10... | collective-permute-start | bytes 1081352 | tf_op jit(solution)/shard_map/ppermute | solution.py:530
  5.7 1.5 %collective-permute-start.2 = (bf16[128,1408]{1,0:T(8,128)(2,1)S(1)}, bf16[128,1408]{1,0:T(8,128)(2,1)S(1)}, u32[]{:S(2)}, u32[]{:S(2)}) collective-permute-start(bf16[128,1408]{1,0:T(8,128)(2,1)S(1)} %get-tuple-element.37.mine_ref), channel_id=1, source_target_pairs={{0,16},{16,0},{8,24},{24,8},{1,17},{17,1},{9,25},{25,9},{2,18},{18... | collective-permute-start | bytes 1081352 | tf_op jit(solution)/shard_map/ppermute | solution.py:530
  7.2 0.9 %pack_ends.1 = (bf16[32,5248]{1,0:T(8,128)(2,1)}, bf16[32,5248]{1,0:T(8,128)(2,1)}) custom-call(bf16[128,2560]{1,0:T(8,128)(2,1)S(1)} %bitcast.24, bf16[128,2560]{1,0:T(8,128)(2,1)S(1)} %bitcast.28, f32[1,128]{1,0:T(1,128)S(1)} %get-tuple-element.44.code_ref), custom_call_target="tpu_custom_call" | custom-call | bytes 1310720 | tf_op jit(solution)/shard_map/pack_ends/pallas_call | solution.py:260
  8.1 1.6 %collective-permute-start.7 = (bf16[32,5248]{1,0:T(8,128)(2,1)}, bf16[32,5248]{1,0:T(8,128)(2,1)}, u32[]{:S(2)}, u32[]{:S(2)}) collective-permute-start(bf16[32,5248]{1,0:T(8,128)(2,1)} %get-tuple-element.45), channel_id=1, source_target_pairs={{0,2},{1,3},{2,0},{3,1},{4,6},{5,7},{6,4},{7,5},{8,10},{9,11},{10,... | collective-permute-start | bytes 1007624 | tf_op jit(solution)/shard_map/ppermute | solution.py:35
  9.7 1.6 %attend_middle.1 = bf16[64,2560]{1,0:T(8,128)(2,1)S(1)} custom-call(bf16[128,2560]{1,0:T(8,128)(2,1)S(1)} %bitcast.32, bf16[128,2560]{1,0:T(8,128)(2,1)S(1)} %bitcast.25, bf16[128,2560]{1,0:T(8,128)(2,1)S(1)} %bitcast.29, f32[1,128]{1,0:T(1,128)S(1)} %get-tuple-element.44.code_ref), custom_call_target="tpu_custom_call" | custom-call | flops 268435456 | bytes 1966080 | tf_op jit(solution)/shard_map/attend_middle/pallas_call | solution.py:273
  11.4 3.4 %collective-permute-done.1.theirs_ref = bf16[128,1408]{1,0:T(8,128)(2,1)} collective-permute-done((bf16[128,1408]{1,0:T(8,128)(2,1)S(1)}, bf16[128,1408]{1,0:T(8,128)(2,1)}, u32[]{:S(2)}, u32[]{:S(2)}) %collective-permute-start.1) | collective-permute-done | bytes 360480 | tf_op jit(solution)/shard_map/ppermute | solution.py:530
  14.8 1.3 %pair_sums.2 = (bf16[64,1280]{1,0:T(8,128)(2,1)S(1)}, bf16[64,1280]{1,0:T(8,128)(2,1)S(1)}) custom-call(f32[1,2560]{1,0:T(1,128)S(1)} %broadcast_in_dim.9.gate_ref, f32[1,128]{1,0:T(1,128)S(1)} %get-tuple-element.82.row_ref, bf16[128,1408]{1,0:T(8,128)(2,1)S(1)} %get-tuple-element.34.mine_ref, bf16[128,1408]{1,0:T(8,128)(2,1)} %collective-permute-done.1.theirs_ref), custom_call_target="tpu_custom_call" | custom-call | flops 83886080 | bytes 983040 | tf_op jit(solution)/shard_map/pair_sums/pallas_call | solution.py:371
  16.5 1.8 %collective-permute-start.4 = (bf16[64,1280]{1,0:T(8,128)(2,1)S(1)}, bf16[64,1280]{1,0:T(8,128)(2,1)S(1)}, u32[]{:S(2)}, u32[]{:S(2)}) collective-permute-start(bf16[64,1280]{1,0:T(8,128)(2,1)S(1)} %get-tuple-element.42), channel_id=1, source_target_pairs={{0,16},{16,24},{24,8},{8,0},{1,17},{17,25},{25,9},{9,1},{2,18},{18... | collective-permute-start | bytes 491528 | tf_op jit(solution)/shard_map/ppermute | solution.py:530
  18.6 3.0 %attend_edges.1 = bf16[64,2560]{1,0:T(8,128)(2,1)S(1)} custom-call(bf16[128,2560]{1,0:T(8,128)(2,1)S(1)} %bitcast.33, bf16[128,2560]{1,0:T(8,128)(2,1)S(1)} %bitcast.26, bf16[128,2560]{1,0:T(8,128)(2,1)S(1)} %bitcast.30, f32[1,128]{1,0:T(1,128)S(1)} %get-tuple-element.44.code_ref, bf16[32,5248]{1,0:T(8,128)(2,1)} %collective-permute-done.7.one_ref, ...), custom_call_target="tpu_custom_call" | custom-call | flops 268435456 | bytes 1966080 | tf_op jit(solution)/shard_map/attend_edges/pallas_call | solution.py:294
  21.8 1.8 %collective-permute-start.10 = (bf16[64,1280]{1,0:T(8,128)(2,1)S(1)}, bf16[64,1280]{1,0:T(8,128)(2,1)S(1)}, u32[]{:S(2)}, u32[]{:S(2)}) collective-permute-start(bf16[64,1280]{1,0:T(8,128)(2,1)S(1)} %get-tuple-element.67), channel_id=1, source_target_pairs={{0,16},{16,24},{24,8},{8,0},{1,17},{17,25},{25,9},{9,1},{2,18},{18... | collective-permute-start | bytes 491528 | tf_op jit(solution)/shard_map/ppermute | solution.py:530
  24.1 1.7 %collective-permute-start.6 = (bf16[64,1280]{1,0:T(8,128)(2,1)S(1)}, bf16[64,1280]{1,0:T(8,128)(2,1)S(1)}, u32[]{:S(2)}, u32[]{:S(2)}) collective-permute-start(bf16[64,1280]{1,0:T(8,128)(2,1)S(1)} %get-tuple-element.60), channel_id=1, source_target_pairs={{0,8},{8,0},{16,24},{24,16},{1,9},{9,1},{17,25},{25,17},{2,10},{10... | collective-permute-start | bytes 491528 | tf_op jit(solution)/shard_map/ppermute | solution.py:530
  25.8 1.5 %collective-permute-start.5 = (bf16[64,1280]{1,0:T(8,128)(2,1)S(1)}, bf16[64,1280]{1,0:T(8,128)(2,1)S(1)}, u32[]{:S(2)}, u32[]{:S(2)}) collective-permute-start(bf16[64,1280]{1,0:T(8,128)(2,1)S(1)} %get-tuple-element.69), channel_id=1, source_target_pairs={{0,16},{16,0},{8,24},{24,8},{1,17},{17,1},{9,25},{25,9},{2,18},{18... | collective-permute-start | bytes 491528 | tf_op jit(solution)/shard_map/ppermute | solution.py:530
  27.4 1.6 %collective-permute-done.10 = bf16[64,1280]{1,0:T(8,128)(2,1)S(1)} collective-permute-done((bf16[64,1280]{1,0:T(8,128)(2,1)S(1)}, bf16[64,1280]{1,0:T(8,128)(2,1)S(1)}, u32[]{:S(2)}, u32[]{:S(2)}) %collective-permute-start.10) | collective-permute-done | bytes 163872 | tf_op jit(solution)/shard_map/ppermute | solution.py:530
  29.0 1.7 %collective-permute-done.9 = bf16[64,1280]{1,0:T(8,128)(2,1)S(1)} collective-permute-done((bf16[64,1280]{1,0:T(8,128)(2,1)S(1)}, bf16[64,1280]{1,0:T(8,128)(2,1)S(1)}, u32[]{:S(2)}, u32[]{:S(2)}) %collective-permute-start.9) | collective-permute-done | bytes 163872 | tf_op jit(solution)/shard_map/ppermute | solution.py:530
  30.9 1.4 %collective-permute-start.11 = (bf16[64,1280]{1,0:T(8,128)(2,1)S(1)}, bf16[64,1280]{1,0:T(8,128)(2,1)S(1)}, u32[]{:S(2)}, u32[]{:S(2)}) collective-permute-start(bf16[64,1280]{1,0:T(8,128)(2,1)S(1)} %get-tuple-element.64), channel_id=1, source_target_pairs={{0,16},{16,0},{8,24},{24,8},{1,17},{17,1},{9,25},{25,9},{2,18},{18... | collective-permute-start | bytes 491528 | tf_op jit(solution)/shard_map/ppermute | solution.py:530
  32.2 0.6 %collective-permute-start.12 = (bf16[64,1280]{1,0:T(8,128)(2,1)S(1)}, bf16[64,1280]{1,0:T(8,128)(2,1)S(1)}, u32[]{:S(2)}, u32[]{:S(2)}) collective-permute-start(bf16[64,1280]{1,0:T(8,128)(2,1)S(1)} %get-tuple-element.54), channel_id=1, source_target_pairs={{0,8},{8,0},{16,24},{24,16},{1,9},{9,1},{17,25},{25,17},{2,10},{10... | collective-permute-start | bytes 491528 | tf_op jit(solution)/shard_map/ppermute | solution.py:530
  32.9 0.9 %collective-permute-done.5 = bf16[64,1280]{1,0:T(8,128)(2,1)S(1)} collective-permute-done((bf16[64,1280]{1,0:T(8,128)(2,1)S(1)}, bf16[64,1280]{1,0:T(8,128)(2,1)S(1)}, u32[]{:S(2)}, u32[]{:S(2)}) %collective-permute-start.5) | collective-permute-done | bytes 163872 | tf_op jit(solution)/shard_map/ppermute | solution.py:530
  33.8 0.8 %relay_first.1 = (bf16[128,2560]{1,0:T(8,128)(2,1)}, f32[128,2560]{1,0:T(8,128)S(1)}, bf16[128,64]{1,0:T(8,128)(2,1)S(1)}) custom-call(f32[1,128]{1,0:T(1,128)S(1)} %get-tuple-element.82.row_ref, f32[1,2560]{1,0:T(1,128)S(1)} %broadcast_in_dim.9.gate_ref, bf16[64,1280]{1,0:T(8,128)(2,1)S(1)} %get-tuple-element.76.a_ref, ...), custom_call_target="tpu_custom_call" | custom-call | flops 83886080 | bytes 7864320 | tf_op jit(solution)/shard_map/relay_first/pallas_call | solution.py:419
  34.6 1.6 %collective-permute-done.11.refs_1_ = bf16[64,1280]{1,0:T(8,128)(2,1)S(1)} collective-permute-done((bf16[64,1280]{1,0:T(8,128)(2,1)S(1)}, bf16[64,1280]{1,0:T(8,128)(2,1)S(1)}, u32[]{:S(2)}, u32[]{:S(2)}) %collective-permute-start.11) | collective-permute-done | bytes 163872 | tf_op jit(solution)/shard_map/ppermute | solution.py:530
  36.2 1.3 %collective-permute-done.12.refs_4_ = bf16[64,1280]{1,0:T(8,128)(2,1)S(1)} collective-permute-done((bf16[64,1280]{1,0:T(8,128)(2,1)S(1)}, bf16[64,1280]{1,0:T(8,128)(2,1)S(1)}, u32[]{:S(2)}, u32[]{:S(2)}) %collective-permute-start.12) | collective-permute-done | bytes 163872 | tf_op jit(solution)/shard_map/ppermute | solution.py:530
  37.6 1.2 %relay_last.1 = (bf16[128,2560]{1,0:T(8,128)(2,1)}, bf16[128,2560]{1,0:T(8,128)(2,1)}) custom-call(bf16[128,64]{1,0:T(8,128)(2,1)S(1)} %get-tuple-element.47.picks_ref, f32[1,2560]{1,0:T(1,128)S(1)} %broadcast_in_dim.9.gate_ref, f32[128,2560]{1,0:T(8,128)S(1)} %get-tuple-element.48.base_ref, ...), custom_call_target="tpu_custom_call", output_to_operand_aliasing={{0}: (9, {})} | custom-call | flops 83886080 | bytes 3932160 | tf_op jit(solution)/shard_map/relay_last/pallas_call | solution.py:485
  (31 shorter events, 1.7 us)
Async XLA Ops:
  0.6 10.7 %collective-permute-start = (f32[1280]{0:T(1024)}, f32[1280]{0:T(1024)S(1)}, u32[]{:S(2)}, u32[]{:S(2)}) collective-permute-start(f32[1280]{0:T(1024)} %param.12), channel_id=1, source_target_pairs={{0,1},{1,0},{2,3},{3,2},{4,5},{5,4},{6,7},{7,6},{8,9},{9,8},{10,11... | collective-permute-start | bytes 15368 | tf_op jit(solution)/shard_map/ppermute | solution.py:509
  1.9 5.3 %copy-start = (bf16[1,1,128,2560]{3,2,1,0:T(8,128)(2,1)S(1)}, bf16[1,1,128,2560]{3,2,1,0:T(8,128)(2,1)}, u32[]{:S(2)}) copy-start(bf16[1,1,128,2560]{3,2,1,0:T(8,128)(2,1)} %param.8) | copy-start | bytes 1966084
  1.9 5.3 %copy-start.1 = (bf16[1,1,128,2560]{3,2,1,0:T(8,128)(2,1)S(1)}, bf16[1,1,128,2560]{3,2,1,0:T(8,128)(2,1)}, u32[]{:S(2)}) copy-start(bf16[1,1,128,2560]{3,2,1,0:T(8,128)(2,1)} %param.9) | copy-start | bytes 1966084
  3.1 6.6 %copy-start.2 = (bf16[1,1,128,2560]{3,2,1,0:T(8,128)(2,1)S(1)}, bf16[1,1,128,2560]{3,2,1,0:T(8,128)(2,1)}, u32[]{:S(2)}) copy-start(bf16[1,1,128,2560]{3,2,1,0:T(8,128)(2,1)} %param.7) | copy-start | bytes 1966084
  3.1 11.7 %collective-permute-start.1 = (bf16[128,1408]{1,0:T(8,128)(2,1)S(1)}, bf16[128,1408]{1,0:T(8,128)(2,1)}, u32[]{:S(2)}, u32[]{:S(2)}) collective-permute-start(bf16[128,1408]{1,0:T(8,128)(2,1)S(1)} %get-tuple-element.34.mine_ref), channel_id=1, source_target_pairs={{0,8},{8,0},{16,24},{24,16},{1,9},{9,1},{17,25},{25,17},{2,10},{10... | collective-permute-start | bytes 1081352 | tf_op jit(solution)/shard_map/ppermute | solution.py:530
  5.7 10.5 %collective-permute-start.2 = (bf16[128,1408]{1,0:T(8,128)(2,1)S(1)}, bf16[128,1408]{1,0:T(8,128)(2,1)S(1)}, u32[]{:S(2)}, u32[]{:S(2)}) collective-permute-start(bf16[128,1408]{1,0:T(8,128)(2,1)S(1)} %get-tuple-element.37.mine_ref), channel_id=1, source_target_pairs={{0,16},{16,0},{8,24},{24,8},{1,17},{17,1},{9,25},{25,9},{2,18},{18... | collective-permute-start | bytes 1081352 | tf_op jit(solution)/shard_map/ppermute | solution.py:530
  8.1 3.2 %copy-start.3 = (f32[1280]{0:T(1024)S(1)}, f32[1280]{0:T(1024)}, u32[]{:S(2)}) copy-start(f32[1280]{0:T(1024)} %param.12) | copy-start | bytes 15364
  8.1 10.5 %collective-permute-start.7 = (bf16[32,5248]{1,0:T(8,128)(2,1)}, bf16[32,5248]{1,0:T(8,128)(2,1)}, u32[]{:S(2)}, u32[]{:S(2)}) collective-permute-start(bf16[32,5248]{1,0:T(8,128)(2,1)} %get-tuple-element.45), channel_id=1, source_target_pairs={{0,2},{1,3},{2,0},{3,1},{4,6},{5,7},{6,4},{7,5},{8,10},{9,11},{10,... | collective-permute-start | bytes 1007624 | tf_op jit(solution)/shard_map/ppermute | solution.py:35
  9.7 8.9 %collective-permute-start.8 = (bf16[32,5248]{1,0:T(8,128)(2,1)}, bf16[32,5248]{1,0:T(8,128)(2,1)}, u32[]{:S(2)}, u32[]{:S(2)}) collective-permute-start(bf16[32,5248]{1,0:T(8,128)(2,1)} %get-tuple-element.46), channel_id=1, source_target_pairs={{0,1},{1,0},{2,4},{3,5},{4,2},{5,3},{6,7},{7,6},{8,9},{9,8},{10,12... | collective-permute-start | bytes 1007624 | tf_op jit(solution)/shard_map/ppermute | solution.py:35
  16.5 7.3 %collective-permute-start.4 = (bf16[64,1280]{1,0:T(8,128)(2,1)S(1)}, bf16[64,1280]{1,0:T(8,128)(2,1)S(1)}, u32[]{:S(2)}, u32[]{:S(2)}) collective-permute-start(bf16[64,1280]{1,0:T(8,128)(2,1)S(1)} %get-tuple-element.42), channel_id=1, source_target_pairs={{0,16},{16,24},{24,8},{8,0},{1,17},{17,25},{25,9},{9,1},{2,18},{18... | collective-permute-start | bytes 491528 | tf_op jit(solution)/shard_map/ppermute | solution.py:530
  18.3 5.6 %collective-permute-start.3 = (bf16[64,1280]{1,0:T(8,128)(2,1)S(1)}, bf16[64,1280]{1,0:T(8,128)(2,1)S(1)}, u32[]{:S(2)}, u32[]{:S(2)}) collective-permute-start(bf16[64,1280]{1,0:T(8,128)(2,1)S(1)} %get-tuple-element.40), channel_id=1, source_target_pairs={{0,8},{8,24},{24,16},{16,0},{1,9},{9,25},{25,17},{17,1},{2,10},{10... | collective-permute-start | bytes 491528 | tf_op jit(solution)/shard_map/ppermute | solution.py:530
  21.8 7.2 %collective-permute-start.10 = (bf16[64,1280]{1,0:T(8,128)(2,1)S(1)}, bf16[64,1280]{1,0:T(8,128)(2,1)S(1)}, u32[]{:S(2)}, u32[]{:S(2)}) collective-permute-start(bf16[64,1280]{1,0:T(8,128)(2,1)S(1)} %get-tuple-element.67), channel_id=1, source_target_pairs={{0,16},{16,24},{24,8},{8,0},{1,17},{17,25},{25,9},{9,1},{2,18},{18... | collective-permute-start | bytes 491528 | tf_op jit(solution)/shard_map/ppermute | solution.py:530
  23.5 7.1 %collective-permute-start.9 = (bf16[64,1280]{1,0:T(8,128)(2,1)S(1)}, bf16[64,1280]{1,0:T(8,128)(2,1)S(1)}, u32[]{:S(2)}, u32[]{:S(2)}) collective-permute-start(bf16[64,1280]{1,0:T(8,128)(2,1)S(1)} %get-tuple-element.68), channel_id=1, source_target_pairs={{0,8},{8,24},{24,16},{16,0},{1,9},{9,25},{25,17},{17,1},{2,10},{10... | collective-permute-start | bytes 491528 | tf_op jit(solution)/shard_map/ppermute | solution.py:530
  24.1 8.8 %collective-permute-start.6 = (bf16[64,1280]{1,0:T(8,128)(2,1)S(1)}, bf16[64,1280]{1,0:T(8,128)(2,1)S(1)}, u32[]{:S(2)}, u32[]{:S(2)}) collective-permute-start(bf16[64,1280]{1,0:T(8,128)(2,1)S(1)} %get-tuple-element.60), channel_id=1, source_target_pairs={{0,8},{8,0},{16,24},{24,16},{1,9},{9,1},{17,25},{25,17},{2,10},{10... | collective-permute-start | bytes 491528 | tf_op jit(solution)/shard_map/ppermute | solution.py:530
  25.8 7.9 %collective-permute-start.5 = (bf16[64,1280]{1,0:T(8,128)(2,1)S(1)}, bf16[64,1280]{1,0:T(8,128)(2,1)S(1)}, u32[]{:S(2)}, u32[]{:S(2)}) collective-permute-start(bf16[64,1280]{1,0:T(8,128)(2,1)S(1)} %get-tuple-element.69), channel_id=1, source_target_pairs={{0,16},{16,0},{8,24},{24,8},{1,17},{17,1},{9,25},{25,9},{2,18},{18... | collective-permute-start | bytes 491528 | tf_op jit(solution)/shard_map/ppermute | solution.py:530
  30.9 5.4 %collective-permute-start.11 = (bf16[64,1280]{1,0:T(8,128)(2,1)S(1)}, bf16[64,1280]{1,0:T(8,128)(2,1)S(1)}, u32[]{:S(2)}, u32[]{:S(2)}) collective-permute-start(bf16[64,1280]{1,0:T(8,128)(2,1)S(1)} %get-tuple-element.64), channel_id=1, source_target_pairs={{0,16},{16,0},{8,24},{24,8},{1,17},{17,1},{9,25},{25,9},{2,18},{18... | collective-permute-start | bytes 491528 | tf_op jit(solution)/shard_map/ppermute | solution.py:530
  32.2 5.3 %collective-permute-start.12 = (bf16[64,1280]{1,0:T(8,128)(2,1)S(1)}, bf16[64,1280]{1,0:T(8,128)(2,1)S(1)}, u32[]{:S(2)}, u32[]{:S(2)}) collective-permute-start(bf16[64,1280]{1,0:T(8,128)(2,1)S(1)} %get-tuple-element.54), channel_id=1, source_target_pairs={{0,8},{8,0},{16,24},{24,16},{1,9},{9,1},{17,25},{25,17},{2,10},{10... | collective-permute-start | bytes 491528 | tf_op jit(solution)/shard_map/ppermute | solution.py:530

commit v21 on v19

--- a/solution.py
+++ b/solution.py
@@ -509,6 +509,22 @@
 ROUND_A, ROUND_B = [(0, 1), (1, 3), (3, 2), (2, 0)], [(0, 2), (2, 3), (3, 1), (1, 0)]
 
 
+def sent_both(to_a, to_b, route_a, route_b):
+    ranks = lax.axis_size("rep")
+    odd = lax.axis_index("rep") % 2 == 1
+
+    def mixed(block, even_route, odd_route):
+        route = []
+        for rank in range(ranks):
+            for source, target in odd_route if rank % 2 else even_route:
+                route.append((source * ranks + rank, target * ranks + rank))
+        return lax.ppermute(block, ("grp", "rep"), route)
+
+    first = mixed(jnp.where(odd, to_b, to_a), route_a, route_b)
+    second = mixed(jnp.where(odd, to_a, to_b), route_b, route_a)
+    return jnp.where(odd, second, first), jnp.where(odd, first, second)
+
+
 def added(a, b):
     return (a.astype(jnp.float32) + b.astype(jnp.float32)).astype(a.dtype)
 
@@ -573,13 +589,17 @@
     picks = (rows[0][:, None] == jnp.arange(tokens)).astype(jnp.bfloat16) if count == 1 else None
     for n, (piece, sum_a, sum_b) in enumerate(zip(own, sums[:count], sums[count:])):
         piece_a, piece_b = piece[:, :half], piece[:, half:]
-        one, two = send(going[n][0], ROUND_A), send(going[n][1], ROUND_B)
+        one, two = sent_both(*going[n], ROUND_A, ROUND_B)
         total_a = added(sum_a, jnp.where(group == 1, two, one))
         total_b = added(sum_b, jnp.where(group == 2, one, two))
         held_a = jnp.where(group == 0, piece_a, one)
         held_b = jnp.where(group == 0, piece_b, two)
-        across = send(jnp.where((group == 0) | (group == 2), held_b, total_a), SWAP_X)
-        down = send(jnp.where(group <= 1, held_a, total_b), SWAP_Y)
+        to_across = jnp.where((group == 0) | (group == 2), held_b, total_a)
+        to_down = jnp.where(group <= 1, held_a, total_b)
+        if n < count - 1:
+            across, down = sent_both(to_across, to_down, SWAP_X, SWAP_Y)
+        else:
+            across, down = send(to_across, SWAP_X), send(to_down, SWAP_Y)
         branch_a = jnp.where(group <= 1, held_a, down)
         branch_b = jnp.where((group == 0) | (group == 2), held_b, across)
         totals = (

time: 38.3 us -> 37.9 us (0.990)
  waiting for transfers between devices: 9.4 us -> 8.47 us
  starting transfers between devices: 15.4 us -> 15.8 us
    ppermute x0 -> x6, starting transfers between devices: none -> 7.41 us  [mixed(): return lax.ppermute(block, ('grp', 'rep'), route)]
    ppermute x10 -> x4, starting transfers between devices: 13.4 us -> 6.25 us  [local(): send = lambda block, route: lax.ppermute(block, 'grp', route)]
    ppermute x10 -> x4, waiting for transfers between devices: 9.39 us -> 5.75 us  [local(): send = lambda block, route: lax.ppermute(block, 'grp', route)]
    ppermute x0 -> x6, waiting for transfers between devices: none -> 2.71 us  [mixed(): return lax.ppermute(block, ('grp', 'rep'), route)]
  transfers between devices with their start and end apart: 13 -> 13, of which waited for: 6 -> 5; matrix products, arithmetic and copies ran while one was open for 4% -> 4% of each run, Pallas kernels for 27% -> 27%
where the time goes in v21:
time: 37.9 us; the launch traced here: 37.7 us
  starting transfers between devices  15.8 us (42%)
  Pallas kernels  11.1 us (29%)
  waiting for transfers between devices  8.47 us (22%)
  other arithmetic  1.44 us (4%)
  between operations  0.87 us (2%)
    ppermute x6, starting transfers between devices, mixed(): return lax.ppermute(block, ('grp', 'rep'), route)  7.41 us
    ppermute x4, starting transfers between devices, local(): send = lambda block, route: lax.ppermute(block, 'grp', route)  6.25 us
    ppermute x4, waiting for transfers between devices, local(): send = lambda block, route: lax.ppermute(block, 'grp', route)  5.75 us
    pallas_call x1, Pallas kernels, attend_edges(): pl.pallas_call(functools.partial(kernel, reach, lax.axis_size('seq')), in...  3.05 us
    ppermute x6, waiting for transfers between devices, mixed(): return lax.ppermute(block, ('grp', 'rep'), route)  2.71 us
    pallas_call x2, Pallas kernels, relay_last(): pl.pallas_call(functools.partial(relay_last_kernel, part, chunks, first_r...  1.99 us
    pallas_call x1, Pallas kernels, attend_middle(): pl.pallas_call(functools.partial(middle_kernel, reach), in_specs=[VMEM] *...  1.61 us
    ppermute x2, starting transfers between devices, paired(): return lax.ppermute(block, ('seq', 'rep'), route)  1.58 us
  transfers between devices with their start and end apart: 13, of which 5 were waited for; matrix products, arithmetic and copies ran while one was open for 4% of the time, Pallas kernels for 27%

profile of v21, /device:TPU:0, one launch (start us, length us, event | category | flops | bytes accessed | tf_op | source)
XLA Modules:
  0.0 37.7 jit_solution(5708176047751241939)
XLA Ops:
  0.6 0.5 %collective-permute-start = (f32[1280]{0:T(1024)}, f32[1280]{0:T(1024)S(1)}, u32[]{:S(2)}, u32[]{:S(2)}) collective-permute-start(f32[1280]{0:T(1024)} %param.12), channel_id=1, source_target_pairs={{0,1},{1,0},{2,3},{3,2},{4,5},{5,4},{6,7},{7,6},{8,9},{9,8},{10,11... | collective-permute-start | bytes 15368 | tf_op jit(solution)/shard_map/ppermute | solution.py:503
  1.1 0.7 %and_select_fusion = (s32[1,128]{1,0:T(1,128)S(1)}, s32[1,128]{1,0:T(1,128)S(1)}) fusion(s32[1,1,128]{2,1,0:T(1,128)} %param.11, s32[1,1,128]{2,1,0:T(1,128)} %param.10), kind=kLoop, calls=%fused_computation.38 | loop fusion | flops 2816 | bytes 2048 | tf_op jit(solution)/shard_map/jit(remainder)/select_n | solution.py:544
  1.9 1.2 %pack_grads.1 = (bf16[128,1408]{1,0:T(8,128)(2,1)S(1)}, bf16[128,1408]{1,0:T(8,128)(2,1)S(1)}) custom-call(bf16[128,2560]{1,0:T(8,128)(2,1)} %bitcast.35, f32[2,128]{1,0:T(2,128)S(1)} %add_convert_fusion.4.mark_ref, bf16[128,2560]{1,0:T(8,128)(2,1)} %bitcast.31, bf16[128,2560]{1,0:T(8,128)(2,1)} %bitcast.23, bf16[128,2560]{1,0:T(8,128)(2,1)} %bitcast.27), custom_call_target="tpu_custom_call" | custom-call | bytes 1310720 | tf_op jit(solution)/shard_map/pack_grads/pallas_call | solution.py:332
  3.1 2.6 %collective-permute-start.1 = (bf16[128,1408]{1,0:T(8,128)(2,1)S(1)}, bf16[128,1408]{1,0:T(8,128)(2,1)}, u32[]{:S(2)}, u32[]{:S(2)}) collective-permute-start(bf16[128,1408]{1,0:T(8,128)(2,1)S(1)} %get-tuple-element.36.mine_ref), channel_id=1, source_target_pairs={{0,8},{8,0},{16,24},{24,16},{1,9},{9,1},{17,25},{25,17},{2,10},{10... | collective-permute-start | bytes 1081352 | tf_op jit(solution)/shard_map/ppermute | solution.py:540
  5.7 1.5 %collective-permute-start.2 = (bf16[128,1408]{1,0:T(8,128)(2,1)S(1)}, bf16[128,1408]{1,0:T(8,128)(2,1)S(1)}, u32[]{:S(2)}, u32[]{:S(2)}) collective-permute-start(bf16[128,1408]{1,0:T(8,128)(2,1)S(1)} %get-tuple-element.39.mine_ref), channel_id=1, source_target_pairs={{0,16},{16,0},{8,24},{24,8},{1,17},{17,1},{9,25},{25,9},{2,18},{18... | collective-permute-start | bytes 1081352 | tf_op jit(solution)/shard_map/ppermute | solution.py:540
  7.2 0.9 %pack_ends.1 = (bf16[32,5248]{1,0:T(8,128)(2,1)}, bf16[32,5248]{1,0:T(8,128)(2,1)}) custom-call(bf16[128,2560]{1,0:T(8,128)(2,1)S(1)} %bitcast.24, bf16[128,2560]{1,0:T(8,128)(2,1)S(1)} %bitcast.28, f32[1,128]{1,0:T(1,128)S(1)} %get-tuple-element.46.code_ref), custom_call_target="tpu_custom_call" | custom-call | bytes 1310720 | tf_op jit(solution)/shard_map/pack_ends/pallas_call | solution.py:260
  8.1 1.6 %collective-permute-start.7 = (bf16[32,5248]{1,0:T(8,128)(2,1)}, bf16[32,5248]{1,0:T(8,128)(2,1)}, u32[]{:S(2)}, u32[]{:S(2)}) collective-permute-start(bf16[32,5248]{1,0:T(8,128)(2,1)} %get-tuple-element.47), channel_id=1, source_target_pairs={{0,2},{1,3},{2,0},{3,1},{4,6},{5,7},{6,4},{7,5},{8,10},{9,11},{10,... | collective-permute-start | bytes 1007624 | tf_op jit(solution)/shard_map/ppermute | solution.py:35
  9.7 1.6 %attend_middle.1 = bf16[64,2560]{1,0:T(8,128)(2,1)S(1)} custom-call(bf16[128,2560]{1,0:T(8,128)(2,1)S(1)} %bitcast.32, bf16[128,2560]{1,0:T(8,128)(2,1)S(1)} %bitcast.25, bf16[128,2560]{1,0:T(8,128)(2,1)S(1)} %bitcast.29, f32[1,128]{1,0:T(1,128)S(1)} %get-tuple-element.46.code_ref), custom_call_target="tpu_custom_call" | custom-call | flops 268435456 | bytes 1966080 | tf_op jit(solution)/shard_map/attend_middle/pallas_call | solution.py:273
  11.4 3.4 %collective-permute-done.1.theirs_ref = bf16[128,1408]{1,0:T(8,128)(2,1)} collective-permute-done((bf16[128,1408]{1,0:T(8,128)(2,1)S(1)}, bf16[128,1408]{1,0:T(8,128)(2,1)}, u32[]{:S(2)}, u32[]{:S(2)}) %collective-permute-start.1) | collective-permute-done | bytes 360480 | tf_op jit(solution)/shard_map/ppermute | solution.py:540
  14.8 1.3 %pair_sums.2 = (bf16[64,1280]{1,0:T(8,128)(2,1)S(1)}, bf16[64,1280]{1,0:T(8,128)(2,1)S(1)}) custom-call(f32[1,2560]{1,0:T(1,128)S(1)} %broadcast_in_dim.9.gate_ref, f32[1,128]{1,0:T(1,128)S(1)} %get-tuple-element.89.row_ref, bf16[128,1408]{1,0:T(8,128)(2,1)S(1)} %get-tuple-element.36.mine_ref, bf16[128,1408]{1,0:T(8,128)(2,1)} %collective-permute-done.1.theirs_ref), custom_call_target="tpu_custom_call" | custom-call | flops 83886080 | bytes 983040 | tf_op jit(solution)/shard_map/pair_sums/pallas_call | solution.py:371
  16.6 1.8 %collective-permute-start.3 = (bf16[64,1280]{1,0:T(8,128)(2,1)S(1)}, bf16[64,1280]{1,0:T(8,128)(2,1)S(1)}, u32[]{:S(2)}, u32[]{:S(2)}) collective-permute-start(bf16[64,1280]{1,0:T(8,128)(2,1)S(1)} %get-tuple-element.84), channel_id=1, source_target_pairs={{0,16},{16,24},{24,8},{8,0},{1,9},{9,25},{25,17},{17,1},{2,18},{18... | collective-permute-start | bytes 491528 | tf_op jit(solution)/shard_map/ppermute | solution.py:521
  18.7 3.1 %attend_edges.1 = bf16[64,2560]{1,0:T(8,128)(2,1)S(1)} custom-call(bf16[128,2560]{1,0:T(8,128)(2,1)S(1)} %bitcast.33, bf16[128,2560]{1,0:T(8,128)(2,1)S(1)} %bitcast.26, bf16[128,2560]{1,0:T(8,128)(2,1)S(1)} %bitcast.30, f32[1,128]{1,0:T(1,128)S(1)} %get-tuple-element.46.code_ref, bf16[32,5248]{1,0:T(8,128)(2,1)} %collective-permute-done.7.one_ref, ...), custom_call_target="tpu_custom_call" | custom-call | flops 268435456 | bytes 1966080 | tf_op jit(solution)/shard_map/attend_edges/pallas_call | solution.py:294
  21.8 1.8 %collective-permute-start.9 = (bf16[64,1280]{1,0:T(8,128)(2,1)S(1)}, bf16[64,1280]{1,0:T(8,128)(2,1)S(1)}, u32[]{:S(2)}, u32[]{:S(2)}) collective-permute-start(bf16[64,1280]{1,0:T(8,128)(2,1)S(1)} %broadcast_select_fusion.7), channel_id=1, source_target_pairs={{0,16},{16,24},{24,8},{8,0},{1,9},{9,25},{25,17},{17,1},{2,18},{18... | collective-permute-start | bytes 491528 | tf_op jit(solution)/shard_map/ppermute | solution.py:521
  23.6 0.3 collective-permute-start.10
  24.3 1.7 %collective-permute-start.5 = (bf16[64,1280]{1,0:T(8,128)(2,1)S(1)}, bf16[64,1280]{1,0:T(8,128)(2,1)S(1)}, u32[]{:S(2)}, u32[]{:S(2)}) collective-permute-start(bf16[64,1280]{1,0:T(8,128)(2,1)S(1)} %broadcast_select_fusion.11), channel_id=1, source_target_pairs={{0,8},{8,0},{16,24},{24,16},{1,17},{17,1},{9,25},{25,9},{2,10},{10... | collective-permute-start | bytes 491528 | tf_op jit(solution)/shard_map/ppermute | solution.py:521
  26.0 1.5 %collective-permute-start.6 = (bf16[64,1280]{1,0:T(8,128)(2,1)S(1)}, bf16[64,1280]{1,0:T(8,128)(2,1)S(1)}, u32[]{:S(2)}, u32[]{:S(2)}) collective-permute-start(bf16[64,1280]{1,0:T(8,128)(2,1)S(1)} %get-tuple-element.69), channel_id=1, source_target_pairs={{0,16},{16,0},{8,24},{24,8},{1,9},{9,1},{17,25},{25,17},{2,18},{18... | collective-permute-start | bytes 491528 | tf_op jit(solution)/shard_map/ppermute | solution.py:521
  27.5 1.3 %collective-permute-done.9 = bf16[64,1280]{1,0:T(8,128)(2,1)S(1)} collective-permute-done((bf16[64,1280]{1,0:T(8,128)(2,1)S(1)}, bf16[64,1280]{1,0:T(8,128)(2,1)S(1)}, u32[]{:S(2)}, u32[]{:S(2)}) %collective-permute-start.9) | collective-permute-done | bytes 163872 | tf_op jit(solution)/shard_map/ppermute | solution.py:521
  28.9 1.4 %collective-permute-done.10 = bf16[64,1280]{1,0:T(8,128)(2,1)S(1)} collective-permute-done((bf16[64,1280]{1,0:T(8,128)(2,1)S(1)}, bf16[64,1280]{1,0:T(8,128)(2,1)S(1)}, u32[]{:S(2)}, u32[]{:S(2)}) %collective-permute-start.10) | collective-permute-done | bytes 163872 | tf_op jit(solution)/shard_map/ppermute | solution.py:521
  30.3 0.4 %collective-permute-start.12 = (bf16[64,1280]{1,0:T(8,128)(2,1)S(1)}, bf16[64,1280]{1,0:T(8,128)(2,1)S(1)}, u32[]{:S(2)}, u32[]{:S(2)}) collective-permute-start(bf16[64,1280]{1,0:T(8,128)(2,1)S(1)} %get-tuple-element.58), channel_id=1, source_target_pairs={{0,8},{8,0},{16,24},{24,16},{1,9},{9,1},{17,25},{25,17},{2,10},{10... | collective-permute-start | bytes 491528 | tf_op jit(solution)/shard_map/ppermute | solution.py:540
  30.8 1.8 %collective-permute-start.11 = (bf16[64,1280]{1,0:T(8,128)(2,1)S(1)}, bf16[64,1280]{1,0:T(8,128)(2,1)S(1)}, u32[]{:S(2)}, u32[]{:S(2)}) collective-permute-start(bf16[64,1280]{1,0:T(8,128)(2,1)S(1)} %get-tuple-element.63), channel_id=1, source_target_pairs={{0,16},{16,0},{8,24},{24,8},{1,17},{17,1},{9,25},{25,9},{2,18},{18... | collective-permute-start | bytes 491528 | tf_op jit(solution)/shard_map/ppermute | solution.py:540
  32.7 0.8 %relay_first.1 = (bf16[128,2560]{1,0:T(8,128)(2,1)}, f32[128,2560]{1,0:T(8,128)S(1)}, bf16[128,64]{1,0:T(8,128)(2,1)S(1)}) custom-call(f32[1,128]{1,0:T(1,128)S(1)} %get-tuple-element.89.row_ref, f32[1,2560]{1,0:T(1,128)S(1)} %broadcast_in_dim.9.gate_ref, bf16[64,1280]{1,0:T(8,128)(2,1)S(1)} %get-tuple-element.79.a_ref, ...), custom_call_target="tpu_custom_call" | custom-call | flops 83886080 | bytes 7864320 | tf_op jit(solution)/shard_map/relay_first/pallas_call | solution.py:419
  33.4 2.3 %collective-permute-done.12.got_ref = bf16[64,1280]{1,0:T(8,128)(2,1)S(1)} collective-permute-done((bf16[64,1280]{1,0:T(8,128)(2,1)S(1)}, bf16[64,1280]{1,0:T(8,128)(2,1)S(1)}, u32[]{:S(2)}, u32[]{:S(2)}) %collective-permute-start.12) | collective-permute-done | bytes 163872 | tf_op jit(solution)/shard_map/ppermute | solution.py:540
  35.7 1.0 %relay_last.2 = (bf16[128,2560]{1,0:T(8,128)(2,1)}, bf16[128,2560]{1,0:T(8,128)(2,1)}) custom-call(bf16[128,64]{1,0:T(8,128)(2,1)S(1)} %get-tuple-element.49.picks_ref, f32[1,2560]{1,0:T(1,128)S(1)} %broadcast_in_dim.9.gate_ref, bf16[64,1280]{1,0:T(8,128)(2,1)S(1)} %get-tuple-element.60.held_ref, ...), custom_call_target="tpu_custom_call", output_to_operand_aliasing={{0}: (6, {})} | custom-call | flops 41943040 | bytes 1966080 | tf_op jit(solution)/shard_map/relay_last/pallas_call | solution.py:479
  36.7 1.0 %relay_last.3 = (bf16[128,2560]{1,0:T(8,128)(2,1)}, bf16[128,2560]{1,0:T(8,128)(2,1)}) custom-call(bf16[128,64]{1,0:T(8,128)(2,1)S(1)} %get-tuple-element.49.picks_ref, f32[1,2560]{1,0:T(1,128)S(1)} %broadcast_in_dim.9.gate_ref, bf16[64,1280]{1,0:T(8,128)(2,1)S(1)} %get-tuple-element.65.held_ref, ...), custom_call_target="tpu_custom_call", output_to_operand_aliasing={{0}: (6, {}), {1}: (7, {})} | custom-call | flops 41943040 | bytes 1966080 | tf_op jit(solution)/shard_map/relay_last/pallas_call | solution.py:479
  (37 shorter events, 1.5 us)
Async XLA Ops:
  0.6 10.7 %collective-permute-start = (f32[1280]{0:T(1024)}, f32[1280]{0:T(1024)S(1)}, u32[]{:S(2)}, u32[]{:S(2)}) collective-permute-start(f32[1280]{0:T(1024)} %param.12), channel_id=1, source_target_pairs={{0,1},{1,0},{2,3},{3,2},{4,5},{5,4},{6,7},{7,6},{8,9},{9,8},{10,11... | collective-permute-start | bytes 15368 | tf_op jit(solution)/shard_map/ppermute | solution.py:503
  1.9 5.3 %copy-start = (bf16[1,1,128,2560]{3,2,1,0:T(8,128)(2,1)S(1)}, bf16[1,1,128,2560]{3,2,1,0:T(8,128)(2,1)}, u32[]{:S(2)}) copy-start(bf16[1,1,128,2560]{3,2,1,0:T(8,128)(2,1)} %param.8) | copy-start | bytes 1966084
  1.9 5.3 %copy-start.1 = (bf16[1,1,128,2560]{3,2,1,0:T(8,128)(2,1)S(1)}, bf16[1,1,128,2560]{3,2,1,0:T(8,128)(2,1)}, u32[]{:S(2)}) copy-start(bf16[1,1,128,2560]{3,2,1,0:T(8,128)(2,1)} %param.9) | copy-start | bytes 1966084
  3.1 6.6 %copy-start.2 = (bf16[1,1,128,2560]{3,2,1,0:T(8,128)(2,1)S(1)}, bf16[1,1,128,2560]{3,2,1,0:T(8,128)(2,1)}, u32[]{:S(2)}) copy-start(bf16[1,1,128,2560]{3,2,1,0:T(8,128)(2,1)} %param.7) | copy-start | bytes 1966084
  3.1 11.7 %collective-permute-start.1 = (bf16[128,1408]{1,0:T(8,128)(2,1)S(1)}, bf16[128,1408]{1,0:T(8,128)(2,1)}, u32[]{:S(2)}, u32[]{:S(2)}) collective-permute-start(bf16[128,1408]{1,0:T(8,128)(2,1)S(1)} %get-tuple-element.36.mine_ref), channel_id=1, source_target_pairs={{0,8},{8,0},{16,24},{24,16},{1,9},{9,1},{17,25},{25,17},{2,10},{10... | collective-permute-start | bytes 1081352 | tf_op jit(solution)/shard_map/ppermute | solution.py:540
  5.7 10.5 %collective-permute-start.2 = (bf16[128,1408]{1,0:T(8,128)(2,1)S(1)}, bf16[128,1408]{1,0:T(8,128)(2,1)S(1)}, u32[]{:S(2)}, u32[]{:S(2)}) collective-permute-start(bf16[128,1408]{1,0:T(8,128)(2,1)S(1)} %get-tuple-element.39.mine_ref), channel_id=1, source_target_pairs={{0,16},{16,0},{8,24},{24,8},{1,17},{17,1},{9,25},{25,9},{2,18},{18... | collective-permute-start | bytes 1081352 | tf_op jit(solution)/shard_map/ppermute | solution.py:540
  8.1 3.2 %copy-start.3 = (f32[1280]{0:T(1024)S(1)}, f32[1280]{0:T(1024)}, u32[]{:S(2)}) copy-start(f32[1280]{0:T(1024)} %param.12) | copy-start | bytes 15364
  8.1 10.5 %collective-permute-start.7 = (bf16[32,5248]{1,0:T(8,128)(2,1)}, bf16[32,5248]{1,0:T(8,128)(2,1)}, u32[]{:S(2)}, u32[]{:S(2)}) collective-permute-start(bf16[32,5248]{1,0:T(8,128)(2,1)} %get-tuple-element.47), channel_id=1, source_target_pairs={{0,2},{1,3},{2,0},{3,1},{4,6},{5,7},{6,4},{7,5},{8,10},{9,11},{10,... | collective-permute-start | bytes 1007624 | tf_op jit(solution)/shard_map/ppermute | solution.py:35
  9.7 9.0 %collective-permute-start.8 = (bf16[32,5248]{1,0:T(8,128)(2,1)}, bf16[32,5248]{1,0:T(8,128)(2,1)}, u32[]{:S(2)}, u32[]{:S(2)}) collective-permute-start(bf16[32,5248]{1,0:T(8,128)(2,1)} %get-tuple-element.48), channel_id=1, source_target_pairs={{0,1},{1,0},{2,4},{3,5},{4,2},{5,3},{6,7},{7,6},{8,9},{9,8},{10,12... | collective-permute-start | bytes 1007624 | tf_op jit(solution)/shard_map/ppermute | solution.py:35
  16.6 7.4 %collective-permute-start.3 = (bf16[64,1280]{1,0:T(8,128)(2,1)S(1)}, bf16[64,1280]{1,0:T(8,128)(2,1)S(1)}, u32[]{:S(2)}, u32[]{:S(2)}) collective-permute-start(bf16[64,1280]{1,0:T(8,128)(2,1)S(1)} %get-tuple-element.84), channel_id=1, source_target_pairs={{0,16},{16,24},{24,8},{8,0},{1,9},{9,25},{25,17},{17,1},{2,18},{18... | collective-permute-start | bytes 491528 | tf_op jit(solution)/shard_map/ppermute | solution.py:521
  18.3 5.6 %collective-permute-start.4 = (bf16[64,1280]{1,0:T(8,128)(2,1)S(1)}, bf16[64,1280]{1,0:T(8,128)(2,1)S(1)}, u32[]{:S(2)}, u32[]{:S(2)}) collective-permute-start(bf16[64,1280]{1,0:T(8,128)(2,1)S(1)} %get-tuple-element.85), channel_id=1, source_target_pairs={{0,8},{8,24},{24,16},{16,0},{1,17},{17,25},{25,9},{9,1},{2,10},{10... | collective-permute-start | bytes 491528 | tf_op jit(solution)/shard_map/ppermute | solution.py:521
  21.8 7.0 %collective-permute-start.9 = (bf16[64,1280]{1,0:T(8,128)(2,1)S(1)}, bf16[64,1280]{1,0:T(8,128)(2,1)S(1)}, u32[]{:S(2)}, u32[]{:S(2)}) collective-permute-start(bf16[64,1280]{1,0:T(8,128)(2,1)S(1)} %broadcast_select_fusion.7), channel_id=1, source_target_pairs={{0,16},{16,24},{24,8},{8,0},{1,9},{9,25},{25,17},{17,1},{2,18},{18... | collective-permute-start | bytes 491528 | tf_op jit(solution)/shard_map/ppermute | solution.py:521
  23.6 6.6 %collective-permute-start.10 = (bf16[64,1280]{1,0:T(8,128)(2,1)S(1)}, bf16[64,1280]{1,0:T(8,128)(2,1)S(1)}, u32[]{:S(2)}, u32[]{:S(2)}) collective-permute-start(bf16[64,1280]{1,0:T(8,128)(2,1)S(1)} %get-tuple-element.66), channel_id=1, source_target_pairs={{0,8},{8,24},{24,16},{16,0},{1,17},{17,25},{25,9},{9,1},{2,10},{10... | collective-permute-start | bytes 491528 | tf_op jit(solution)/shard_map/ppermute | solution.py:521
  24.3 8.3 %collective-permute-start.5 = (bf16[64,1280]{1,0:T(8,128)(2,1)S(1)}, bf16[64,1280]{1,0:T(8,128)(2,1)S(1)}, u32[]{:S(2)}, u32[]{:S(2)}) collective-permute-start(bf16[64,1280]{1,0:T(8,128)(2,1)S(1)} %broadcast_select_fusion.11), channel_id=1, source_target_pairs={{0,8},{8,0},{16,24},{24,16},{1,17},{17,1},{9,25},{25,9},{2,10},{10... | collective-permute-start | bytes 491528 | tf_op jit(solution)/shard_map/ppermute | solution.py:521
  26.0 6.6 %collective-permute-start.6 = (bf16[64,1280]{1,0:T(8,128)(2,1)S(1)}, bf16[64,1280]{1,0:T(8,128)(2,1)S(1)}, u32[]{:S(2)}, u32[]{:S(2)}) collective-permute-start(bf16[64,1280]{1,0:T(8,128)(2,1)S(1)} %get-tuple-element.69), channel_id=1, source_target_pairs={{0,16},{16,0},{8,24},{24,8},{1,9},{9,1},{17,25},{25,17},{2,18},{18... | collective-permute-start | bytes 491528 | tf_op jit(solution)/shard_map/ppermute | solution.py:521
  30.3 5.4 %collective-permute-start.12 = (bf16[64,1280]{1,0:T(8,128)(2,1)S(1)}, bf16[64,1280]{1,0:T(8,128)(2,1)S(1)}, u32[]{:S(2)}, u32[]{:S(2)}) collective-permute-start(bf16[64,1280]{1,0:T(8,128)(2,1)S(1)} %get-tuple-element.58), channel_id=1, source_target_pairs={{0,8},{8,0},{16,24},{24,16},{1,9},{9,1},{17,25},{25,17},{2,10},{10... | collective-permute-start | bytes 491528 | tf_op jit(solution)/shard_map/ppermute | solution.py:540
  30.8 5.9 %collective-permute-start.11 = (bf16[64,1280]{1,0:T(8,128)(2,1)S(1)}, bf16[64,1280]{1,0:T(8,128)(2,1)S(1)}, u32[]{:S(2)}, u32[]{:S(2)}) collective-permute-start(bf16[64,1280]{1,0:T(8,128)(2,1)S(1)} %get-tuple-element.63), channel_id=1, source_target_pairs={{0,16},{16,0},{8,24},{24,8},{1,17},{17,1},{9,25},{25,9},{2,18},{18... | collective-permute-start | bytes 491528 | tf_op jit(solution)/shard_map/ppermute | solution.py:540

commit v22 on v20

--- a/solution.py
+++ b/solution.py
@@ -515,6 +515,22 @@
 ROUND_A, ROUND_B = [(0, 1), (1, 3), (3, 2), (2, 0)], [(0, 2), (2, 3), (3, 1), (1, 0)]
 
 
+def sent_both(to_a, to_b, route_a, route_b):
+    ranks = lax.axis_size("rep")
+    odd = lax.axis_index("rep") % 2 == 1
+
+    def mixed(block, even_route, odd_route):
+        route = []
+        for rank in range(ranks):
+            for source, target in odd_route if rank % 2 else even_route:
+                route.append((source * ranks + rank, target * ranks + rank))
+        return lax.ppermute(block, ("grp", "rep"), route)
+
+    first = mixed(jnp.where(odd, to_b, to_a), route_a, route_b)
+    second = mixed(jnp.where(odd, to_a, to_b), route_b, route_a)
+    return jnp.where(odd, second, first), jnp.where(odd, first, second)
+
+
 def added(a, b):
     return (a.astype(jnp.float32) + b.astype(jnp.float32)).astype(a.dtype)
 
@@ -579,13 +595,14 @@
     picks = (rows[0][:, None] == jnp.arange(tokens)).astype(jnp.bfloat16) if count == 1 else None
     for n, (piece, sum_a, sum_b) in enumerate(zip(own, sums[:count], sums[count:])):
         piece_a, piece_b = piece[:, :half], piece[:, half:]
-        one, two = send(going[n][0], ROUND_A), send(going[n][1], ROUND_B)
+        one, two = sent_both(*going[n], ROUND_A, ROUND_B)
         total_a = added(sum_a, jnp.where(group == 1, two, one))
         total_b = added(sum_b, jnp.where(group == 2, one, two))
         held_a = jnp.where(group == 0, piece_a, one)
         held_b = jnp.where(group == 0, piece_b, two)
-        across = send(jnp.where((group == 0) | (group == 2), held_b, total_a), SWAP_X)
-        down = send(jnp.where(group <= 1, held_a, total_b), SWAP_Y)
+        to_across = jnp.where((group == 0) | (group == 2), held_b, total_a)
+        to_down = jnp.where(group <= 1, held_a, total_b)
+        across, down = sent_both(to_across, to_down, SWAP_X, SWAP_Y)
         branch_a = jnp.where(group <= 1, held_a, down)
         branch_b = jnp.where((group == 0) | (group == 2), held_b, across)
         totals = (

time: 39 us -> 39.3 us (level)
    ppermute x0 -> x8, starting transfers between devices: none -> 9.55 us  [mixed(): return lax.ppermute(block, ('grp', 'rep'), route)]
    ppermute x10 -> x2, starting transfers between devices: 13.5 us -> 4.09 us  [local(): send = lambda block, route: lax.ppermute(block, 'grp', route)]
    ppermute x10 -> x2, waiting for transfers between devices: 10.7 us -> 3.49 us  [local(): send = lambda block, route: lax.ppermute(block, 'grp', route)]
    ppermute x0 -> x8, waiting for transfers between devices: none -> 7.13 us  [mixed(): return lax.ppermute(block, ('grp', 'rep'), route)]
  transfers between devices with their start and end apart: 13 -> 13, of which waited for: 7 -> 6; matrix products, arithmetic and copies ran while one was open for 3% -> 4% of each run, Pallas kernels for 24% -> 23%
where the time goes in v22:
time: 39.3 us; the launch traced here: 39.1 us
  starting transfers between devices  15.7 us (40%)
  waiting for transfers between devices  10.6 us (27%)
  Pallas kernels  10.3 us (26%)
  other arithmetic  1.49 us (4%)
  between operations  0.89 us (2%)
    ppermute x8, starting transfers between devices, mixed(): return lax.ppermute(block, ('grp', 'rep'), route)  9.55 us
    ppermute x8, waiting for transfers between devices, mixed(): return lax.ppermute(block, ('grp', 'rep'), route)  7.13 us
    ppermute x2, starting transfers between devices, local(): send = lambda block, route: lax.ppermute(block, 'grp', route)  4.09 us
    ppermute x2, waiting for transfers between devices, local(): send = lambda block, route: lax.ppermute(block, 'grp', route)  3.49 us
    pallas_call x1, Pallas kernels, attend_edges(): pl.pallas_call(functools.partial(kernel, reach, lax.axis_size('seq')), in...  3.05 us
    pallas_call x1, Pallas kernels, attend_middle(): pl.pallas_call(functools.partial(middle_kernel, reach), in_specs=[VMEM] *...  1.61 us
    ppermute x2, starting transfers between devices, paired(): return lax.ppermute(block, ('seq', 'rep'), route)  1.58 us
    pallas_call x2, Pallas kernels, pair_sums(): pl.pallas_call(functools.partial(sums_kernel, part, sizes), in_specs=[VME...  1.57 us
  transfers between devices with their start and end apart: 13, of which 6 were waited for; matrix products, arithmetic and copies ran while one was open for 4% of the time, Pallas kernels for 23%

profile of v22, /device:TPU:0, one launch (start us, length us, event | category | flops | bytes accessed | tf_op | source)
XLA Modules:
  0.0 39.1 jit_solution(17105238914014215518)
XLA Ops:
  0.6 0.5 %collective-permute-start = (f32[1280]{0:T(1024)}, f32[1280]{0:T(1024)S(1)}, u32[]{:S(2)}, u32[]{:S(2)}) collective-permute-start(f32[1280]{0:T(1024)} %param.12), channel_id=1, source_target_pairs={{0,1},{1,0},{2,3},{3,2},{4,5},{5,4},{6,7},{7,6},{8,9},{9,8},{10,11... | collective-permute-start | bytes 15368 | tf_op jit(solution)/shard_map/ppermute | solution.py:509
  1.1 0.7 %and_select_fusion = (s32[1,128]{1,0:T(1,128)S(1)}, s32[1,128]{1,0:T(1,128)S(1)}) fusion(s32[1,1,128]{2,1,0:T(1,128)} %param.11, s32[1,1,128]{2,1,0:T(1,128)} %param.10), kind=kLoop, calls=%fused_computation.42 | loop fusion | flops 2816 | bytes 2048 | tf_op jit(solution)/shard_map/jit(remainder)/select_n | solution.py:550
  1.9 1.2 %pack_grads.1 = (bf16[128,1408]{1,0:T(8,128)(2,1)S(1)}, bf16[128,1408]{1,0:T(8,128)(2,1)S(1)}) custom-call(bf16[128,2560]{1,0:T(8,128)(2,1)} %bitcast.35, f32[2,128]{1,0:T(2,128)S(1)} %add_convert_fusion.4.mark_ref, bf16[128,2560]{1,0:T(8,128)(2,1)} %bitcast.31, bf16[128,2560]{1,0:T(8,128)(2,1)} %bitcast.23, bf16[128,2560]{1,0:T(8,128)(2,1)} %bitcast.27), custom_call_target="tpu_custom_call" | custom-call | bytes 1310720 | tf_op jit(solution)/shard_map/pack_grads/pallas_call | solution.py:332
  3.1 2.6 %collective-permute-start.1 = (bf16[128,1408]{1,0:T(8,128)(2,1)S(1)}, bf16[128,1408]{1,0:T(8,128)(2,1)}, u32[]{:S(2)}, u32[]{:S(2)}) collective-permute-start(bf16[128,1408]{1,0:T(8,128)(2,1)S(1)} %get-tuple-element.34.mine_ref), channel_id=1, source_target_pairs={{0,8},{8,0},{16,24},{24,16},{1,9},{9,1},{17,25},{25,17},{2,10},{10... | collective-permute-start | bytes 1081352 | tf_op jit(solution)/shard_map/ppermute | solution.py:546
  5.7 1.5 %collective-permute-start.2 = (bf16[128,1408]{1,0:T(8,128)(2,1)S(1)}, bf16[128,1408]{1,0:T(8,128)(2,1)S(1)}, u32[]{:S(2)}, u32[]{:S(2)}) collective-permute-start(bf16[128,1408]{1,0:T(8,128)(2,1)S(1)} %get-tuple-element.37.mine_ref), channel_id=1, source_target_pairs={{0,16},{16,0},{8,24},{24,8},{1,17},{17,1},{9,25},{25,9},{2,18},{18... | collective-permute-start | bytes 1081352 | tf_op jit(solution)/shard_map/ppermute | solution.py:546
  7.2 0.9 %pack_ends.1 = (bf16[32,5248]{1,0:T(8,128)(2,1)}, bf16[32,5248]{1,0:T(8,128)(2,1)}) custom-call(bf16[128,2560]{1,0:T(8,128)(2,1)S(1)} %bitcast.24, bf16[128,2560]{1,0:T(8,128)(2,1)S(1)} %bitcast.28, f32[1,128]{1,0:T(1,128)S(1)} %get-tuple-element.44.code_ref), custom_call_target="tpu_custom_call" | custom-call | bytes 1310720 | tf_op jit(solution)/shard_map/pack_ends/pallas_call | solution.py:260
  8.1 1.6 %collective-permute-start.7 = (bf16[32,5248]{1,0:T(8,128)(2,1)}, bf16[32,5248]{1,0:T(8,128)(2,1)}, u32[]{:S(2)}, u32[]{:S(2)}) collective-permute-start(bf16[32,5248]{1,0:T(8,128)(2,1)} %get-tuple-element.45), channel_id=1, source_target_pairs={{0,2},{1,3},{2,0},{3,1},{4,6},{5,7},{6,4},{7,5},{8,10},{9,11},{10,... | collective-permute-start | bytes 1007624 | tf_op jit(solution)/shard_map/ppermute | solution.py:35
  9.7 1.6 %attend_middle.1 = bf16[64,2560]{1,0:T(8,128)(2,1)S(1)} custom-call(bf16[128,2560]{1,0:T(8,128)(2,1)S(1)} %bitcast.32, bf16[128,2560]{1,0:T(8,128)(2,1)S(1)} %bitcast.25, bf16[128,2560]{1,0:T(8,128)(2,1)S(1)} %bitcast.29, f32[1,128]{1,0:T(1,128)S(1)} %get-tuple-element.44.code_ref), custom_call_target="tpu_custom_call" | custom-call | flops 268435456 | bytes 1966080 | tf_op jit(solution)/shard_map/attend_middle/pallas_call | solution.py:273
  11.4 3.4 %collective-permute-done.1.theirs_ref = bf16[128,1408]{1,0:T(8,128)(2,1)} collective-permute-done((bf16[128,1408]{1,0:T(8,128)(2,1)S(1)}, bf16[128,1408]{1,0:T(8,128)(2,1)}, u32[]{:S(2)}, u32[]{:S(2)}) %collective-permute-start.1) | collective-permute-done | bytes 360480 | tf_op jit(solution)/shard_map/ppermute | solution.py:546
  14.8 1.3 %pair_sums.2 = (bf16[64,1280]{1,0:T(8,128)(2,1)S(1)}, bf16[64,1280]{1,0:T(8,128)(2,1)S(1)}) custom-call(f32[1,2560]{1,0:T(1,128)S(1)} %broadcast_in_dim.9.gate_ref, f32[1,128]{1,0:T(1,128)S(1)} %get-tuple-element.86.row_ref, bf16[128,1408]{1,0:T(8,128)(2,1)S(1)} %get-tuple-element.34.mine_ref, bf16[128,1408]{1,0:T(8,128)(2,1)} %collective-permute-done.1.theirs_ref), custom_call_target="tpu_custom_call" | custom-call | flops 83886080 | bytes 983040 | tf_op jit(solution)/shard_map/pair_sums/pallas_call | solution.py:371
  16.6 1.8 %collective-permute-start.3 = (bf16[64,1280]{1,0:T(8,128)(2,1)S(1)}, bf16[64,1280]{1,0:T(8,128)(2,1)S(1)}, u32[]{:S(2)}, u32[]{:S(2)}) collective-permute-start(bf16[64,1280]{1,0:T(8,128)(2,1)S(1)} %get-tuple-element.81), channel_id=1, source_target_pairs={{0,16},{16,24},{24,8},{8,0},{1,9},{9,25},{25,17},{17,1},{2,18},{18... | collective-permute-start | bytes 491528 | tf_op jit(solution)/shard_map/ppermute | solution.py:527
  18.3 0.3 collective-permute-start.4
  18.7 3.0 %attend_edges.1 = bf16[64,2560]{1,0:T(8,128)(2,1)S(1)} custom-call(bf16[128,2560]{1,0:T(8,128)(2,1)S(1)} %bitcast.33, bf16[128,2560]{1,0:T(8,128)(2,1)S(1)} %bitcast.26, bf16[128,2560]{1,0:T(8,128)(2,1)S(1)} %bitcast.30, f32[1,128]{1,0:T(1,128)S(1)} %get-tuple-element.44.code_ref, bf16[32,5248]{1,0:T(8,128)(2,1)} %collective-permute-done.7.one_ref, ...), custom_call_target="tpu_custom_call" | custom-call | flops 268435456 | bytes 1966080 | tf_op jit(solution)/shard_map/attend_edges/pallas_call | solution.py:294
  21.8 1.8 %collective-permute-start.9 = (bf16[64,1280]{1,0:T(8,128)(2,1)S(1)}, bf16[64,1280]{1,0:T(8,128)(2,1)S(1)}, u32[]{:S(2)}, u32[]{:S(2)}) collective-permute-start(bf16[64,1280]{1,0:T(8,128)(2,1)S(1)} %broadcast_select_fusion.11), channel_id=1, source_target_pairs={{0,16},{16,24},{24,8},{8,0},{1,9},{9,25},{25,17},{17,1},{2,18},{18... | collective-permute-start | bytes 491528 | tf_op jit(solution)/shard_map/ppermute | solution.py:527
  23.6 0.3 collective-permute-start.10
  24.3 1.8 %collective-permute-start.5 = (bf16[64,1280]{1,0:T(8,128)(2,1)S(1)}, bf16[64,1280]{1,0:T(8,128)(2,1)S(1)}, u32[]{:S(2)}, u32[]{:S(2)}) collective-permute-start(bf16[64,1280]{1,0:T(8,128)(2,1)S(1)} %broadcast_select_fusion.15), channel_id=1, source_target_pairs={{0,8},{8,0},{16,24},{24,16},{1,17},{17,1},{9,25},{25,9},{2,10},{10... | collective-permute-start | bytes 491528 | tf_op jit(solution)/shard_map/ppermute | solution.py:527
  26.0 1.5 %collective-permute-start.6 = (bf16[64,1280]{1,0:T(8,128)(2,1)S(1)}, bf16[64,1280]{1,0:T(8,128)(2,1)S(1)}, u32[]{:S(2)}, u32[]{:S(2)}) collective-permute-start(bf16[64,1280]{1,0:T(8,128)(2,1)S(1)} %get-tuple-element.62), channel_id=1, source_target_pairs={{0,16},{16,0},{8,24},{24,8},{1,9},{9,1},{17,25},{25,17},{2,18},{18... | collective-permute-start | bytes 491528 | tf_op jit(solution)/shard_map/ppermute | solution.py:527
  27.5 1.3 %collective-permute-done.9 = bf16[64,1280]{1,0:T(8,128)(2,1)S(1)} collective-permute-done((bf16[64,1280]{1,0:T(8,128)(2,1)S(1)}, bf16[64,1280]{1,0:T(8,128)(2,1)S(1)}, u32[]{:S(2)}, u32[]{:S(2)}) %collective-permute-start.9) | collective-permute-done | bytes 163872 | tf_op jit(solution)/shard_map/ppermute | solution.py:527
  28.9 1.3 %collective-permute-done.10 = bf16[64,1280]{1,0:T(8,128)(2,1)S(1)} collective-permute-done((bf16[64,1280]{1,0:T(8,128)(2,1)S(1)}, bf16[64,1280]{1,0:T(8,128)(2,1)S(1)}, u32[]{:S(2)}, u32[]{:S(2)}) %collective-permute-start.10) | collective-permute-done | bytes 163872 | tf_op jit(solution)/shard_map/ppermute | solution.py:527
  30.5 2.0 %collective-permute-start.12 = (bf16[64,1280]{1,0:T(8,128)(2,1)S(1)}, bf16[64,1280]{1,0:T(8,128)(2,1)S(1)}, u32[]{:S(2)}, u32[]{:S(2)}) collective-permute-start(bf16[64,1280]{1,0:T(8,128)(2,1)S(1)} %get-tuple-element.54), channel_id=1, source_target_pairs={{0,16},{16,0},{8,24},{24,8},{1,9},{9,1},{17,25},{25,17},{2,18},{18... | collective-permute-start | bytes 491528 | tf_op jit(solution)/shard_map/ppermute | solution.py:527
  32.7 0.8 %relay_first.1 = (bf16[128,2560]{1,0:T(8,128)(2,1)}, f32[128,2560]{1,0:T(8,128)S(1)}, bf16[128,64]{1,0:T(8,128)(2,1)S(1)}) custom-call(f32[1,128]{1,0:T(1,128)S(1)} %get-tuple-element.86.row_ref, f32[1,2560]{1,0:T(1,128)S(1)} %broadcast_in_dim.9.gate_ref, bf16[64,1280]{1,0:T(8,128)(2,1)S(1)} %get-tuple-element.76.a_ref, ...), custom_call_target="tpu_custom_call" | custom-call | flops 83886080 | bytes 7864320 | tf_op jit(solution)/shard_map/relay_first/pallas_call | solution.py:419
  33.4 2.4 %collective-permute-done.12 = bf16[64,1280]{1,0:T(8,128)(2,1)S(1)} collective-permute-done((bf16[64,1280]{1,0:T(8,128)(2,1)S(1)}, bf16[64,1280]{1,0:T(8,128)(2,1)S(1)}, u32[]{:S(2)}, u32[]{:S(2)}) %collective-permute-start.12) | collective-permute-done | bytes 163872 | tf_op jit(solution)/shard_map/ppermute | solution.py:527
  35.8 2.0 %collective-permute-done.11 = bf16[64,1280]{1,0:T(8,128)(2,1)S(1)} collective-permute-done((bf16[64,1280]{1,0:T(8,128)(2,1)S(1)}, bf16[64,1280]{1,0:T(8,128)(2,1)S(1)}, u32[]{:S(2)}, u32[]{:S(2)}) %collective-permute-start.11) | collective-permute-done | bytes 163872 | tf_op jit(solution)/shard_map/ppermute | solution.py:527
  37.9 1.2 %relay_last.1 = (bf16[128,2560]{1,0:T(8,128)(2,1)}, bf16[128,2560]{1,0:T(8,128)(2,1)}) custom-call(bf16[128,64]{1,0:T(8,128)(2,1)S(1)} %get-tuple-element.47.picks_ref, f32[1,2560]{1,0:T(1,128)S(1)} %broadcast_in_dim.9.gate_ref, f32[128,2560]{1,0:T(8,128)S(1)} %get-tuple-element.48.base_ref, ...), custom_call_target="tpu_custom_call", output_to_operand_aliasing={{0}: (9, {})} | custom-call | flops 83886080 | bytes 3932160 | tf_op jit(solution)/shard_map/relay_last/pallas_call | solution.py:485
  (38 shorter events, 1.4 us)
Async XLA Ops:
  0.6 10.7 %collective-permute-start = (f32[1280]{0:T(1024)}, f32[1280]{0:T(1024)S(1)}, u32[]{:S(2)}, u32[]{:S(2)}) collective-permute-start(f32[1280]{0:T(1024)} %param.12), channel_id=1, source_target_pairs={{0,1},{1,0},{2,3},{3,2},{4,5},{5,4},{6,7},{7,6},{8,9},{9,8},{10,11... | collective-permute-start | bytes 15368 | tf_op jit(solution)/shard_map/ppermute | solution.py:509
  1.9 5.3 %copy-start = (bf16[1,1,128,2560]{3,2,1,0:T(8,128)(2,1)S(1)}, bf16[1,1,128,2560]{3,2,1,0:T(8,128)(2,1)}, u32[]{:S(2)}) copy-start(bf16[1,1,128,2560]{3,2,1,0:T(8,128)(2,1)} %param.8) | copy-start | bytes 1966084
  1.9 5.3 %copy-start.1 = (bf16[1,1,128,2560]{3,2,1,0:T(8,128)(2,1)S(1)}, bf16[1,1,128,2560]{3,2,1,0:T(8,128)(2,1)}, u32[]{:S(2)}) copy-start(bf16[1,1,128,2560]{3,2,1,0:T(8,128)(2,1)} %param.9) | copy-start | bytes 1966084
  3.1 6.6 %copy-start.2 = (bf16[1,1,128,2560]{3,2,1,0:T(8,128)(2,1)S(1)}, bf16[1,1,128,2560]{3,2,1,0:T(8,128)(2,1)}, u32[]{:S(2)}) copy-start(bf16[1,1,128,2560]{3,2,1,0:T(8,128)(2,1)} %param.7) | copy-start | bytes 1966084
  3.1 11.7 %collective-permute-start.1 = (bf16[128,1408]{1,0:T(8,128)(2,1)S(1)}, bf16[128,1408]{1,0:T(8,128)(2,1)}, u32[]{:S(2)}, u32[]{:S(2)}) collective-permute-start(bf16[128,1408]{1,0:T(8,128)(2,1)S(1)} %get-tuple-element.34.mine_ref), channel_id=1, source_target_pairs={{0,8},{8,0},{16,24},{24,16},{1,9},{9,1},{17,25},{25,17},{2,10},{10... | collective-permute-start | bytes 1081352 | tf_op jit(solution)/shard_map/ppermute | solution.py:546
  5.7 10.5 %collective-permute-start.2 = (bf16[128,1408]{1,0:T(8,128)(2,1)S(1)}, bf16[128,1408]{1,0:T(8,128)(2,1)S(1)}, u32[]{:S(2)}, u32[]{:S(2)}) collective-permute-start(bf16[128,1408]{1,0:T(8,128)(2,1)S(1)} %get-tuple-element.37.mine_ref), channel_id=1, source_target_pairs={{0,16},{16,0},{8,24},{24,8},{1,17},{17,1},{9,25},{25,9},{2,18},{18... | collective-permute-start | bytes 1081352 | tf_op jit(solution)/shard_map/ppermute | solution.py:546
  8.1 3.2 %copy-start.3 = (f32[1280]{0:T(1024)S(1)}, f32[1280]{0:T(1024)}, u32[]{:S(2)}) copy-start(f32[1280]{0:T(1024)} %param.12) | copy-start | bytes 15364
  8.1 10.5 %collective-permute-start.7 = (bf16[32,5248]{1,0:T(8,128)(2,1)}, bf16[32,5248]{1,0:T(8,128)(2,1)}, u32[]{:S(2)}, u32[]{:S(2)}) collective-permute-start(bf16[32,5248]{1,0:T(8,128)(2,1)} %get-tuple-element.45), channel_id=1, source_target_pairs={{0,2},{1,3},{2,0},{3,1},{4,6},{5,7},{6,4},{7,5},{8,10},{9,11},{10,... | collective-permute-start | bytes 1007624 | tf_op jit(solution)/shard_map/ppermute | solution.py:35
  9.7 9.0 %collective-permute-start.8 = (bf16[32,5248]{1,0:T(8,128)(2,1)}, bf16[32,5248]{1,0:T(8,128)(2,1)}, u32[]{:S(2)}, u32[]{:S(2)}) collective-permute-start(bf16[32,5248]{1,0:T(8,128)(2,1)} %get-tuple-element.46), channel_id=1, source_target_pairs={{0,1},{1,0},{2,4},{3,5},{4,2},{5,3},{6,7},{7,6},{8,9},{9,8},{10,12... | collective-permute-start | bytes 1007624 | tf_op jit(solution)/shard_map/ppermute | solution.py:35
  16.6 7.4 %collective-permute-start.3 = (bf16[64,1280]{1,0:T(8,128)(2,1)S(1)}, bf16[64,1280]{1,0:T(8,128)(2,1)S(1)}, u32[]{:S(2)}, u32[]{:S(2)}) collective-permute-start(bf16[64,1280]{1,0:T(8,128)(2,1)S(1)} %get-tuple-element.81), channel_id=1, source_target_pairs={{0,16},{16,24},{24,8},{8,0},{1,9},{9,25},{25,17},{17,1},{2,18},{18... | collective-permute-start | bytes 491528 | tf_op jit(solution)/shard_map/ppermute | solution.py:527
  18.3 5.6 %collective-permute-start.4 = (bf16[64,1280]{1,0:T(8,128)(2,1)S(1)}, bf16[64,1280]{1,0:T(8,128)(2,1)S(1)}, u32[]{:S(2)}, u32[]{:S(2)}) collective-permute-start(bf16[64,1280]{1,0:T(8,128)(2,1)S(1)} %get-tuple-element.82), channel_id=1, source_target_pairs={{0,8},{8,24},{24,16},{16,0},{1,17},{17,25},{25,9},{9,1},{2,10},{10... | collective-permute-start | bytes 491528 | tf_op jit(solution)/shard_map/ppermute | solution.py:527
  21.8 7.0 %collective-permute-start.9 = (bf16[64,1280]{1,0:T(8,128)(2,1)S(1)}, bf16[64,1280]{1,0:T(8,128)(2,1)S(1)}, u32[]{:S(2)}, u32[]{:S(2)}) collective-permute-start(bf16[64,1280]{1,0:T(8,128)(2,1)S(1)} %broadcast_select_fusion.11), channel_id=1, source_target_pairs={{0,16},{16,24},{24,8},{8,0},{1,9},{9,25},{25,17},{17,1},{2,18},{18... | collective-permute-start | bytes 491528 | tf_op jit(solution)/shard_map/ppermute | solution.py:527
  23.6 6.6 %collective-permute-start.10 = (bf16[64,1280]{1,0:T(8,128)(2,1)S(1)}, bf16[64,1280]{1,0:T(8,128)(2,1)S(1)}, u32[]{:S(2)}, u32[]{:S(2)}) collective-permute-start(bf16[64,1280]{1,0:T(8,128)(2,1)S(1)} %get-tuple-element.59), channel_id=1, source_target_pairs={{0,8},{8,24},{24,16},{16,0},{1,17},{17,25},{25,9},{9,1},{2,10},{10... | collective-permute-start | bytes 491528 | tf_op jit(solution)/shard_map/ppermute | solution.py:527
  24.3 8.4 %collective-permute-start.5 = (bf16[64,1280]{1,0:T(8,128)(2,1)S(1)}, bf16[64,1280]{1,0:T(8,128)(2,1)S(1)}, u32[]{:S(2)}, u32[]{:S(2)}) collective-permute-start(bf16[64,1280]{1,0:T(8,128)(2,1)S(1)} %broadcast_select_fusion.15), channel_id=1, source_target_pairs={{0,8},{8,0},{16,24},{24,16},{1,17},{17,1},{9,25},{25,9},{2,10},{10... | collective-permute-start | bytes 491528 | tf_op jit(solution)/shard_map/ppermute | solution.py:527
  26.0 6.6 %collective-permute-start.6 = (bf16[64,1280]{1,0:T(8,128)(2,1)S(1)}, bf16[64,1280]{1,0:T(8,128)(2,1)S(1)}, u32[]{:S(2)}, u32[]{:S(2)}) collective-permute-start(bf16[64,1280]{1,0:T(8,128)(2,1)S(1)} %get-tuple-element.62), channel_id=1, source_target_pairs={{0,16},{16,0},{8,24},{24,8},{1,9},{9,1},{17,25},{25,17},{2,18},{18... | collective-permute-start | bytes 491528 | tf_op jit(solution)/shard_map/ppermute | solution.py:527
  30.5 5.4 %collective-permute-start.12 = (bf16[64,1280]{1,0:T(8,128)(2,1)S(1)}, bf16[64,1280]{1,0:T(8,128)(2,1)S(1)}, u32[]{:S(2)}, u32[]{:S(2)}) collective-permute-start(bf16[64,1280]{1,0:T(8,128)(2,1)S(1)} %get-tuple-element.54), channel_id=1, source_target_pairs={{0,16},{16,0},{8,24},{24,8},{1,9},{9,1},{17,25},{25,17},{2,18},{18... | collective-permute-start | bytes 491528 | tf_op jit(solution)/shard_map/ppermute | solution.py:527
  32.5 5.4 %collective-permute-start.11 = (bf16[64,1280]{1,0:T(8,128)(2,1)S(1)}, bf16[64,1280]{1,0:T(8,128)(2,1)S(1)}, u32[]{:S(2)}, u32[]{:S(2)}) collective-permute-start(bf16[64,1280]{1,0:T(8,128)(2,1)S(1)} %broadcast_select_fusion.7), channel_id=1, source_target_pairs={{0,8},{8,0},{16,24},{24,16},{1,17},{17,1},{9,25},{25,9},{2,10},{10... | collective-permute-start | bytes 491528 | tf_op jit(solution)/shard_map/ppermute | solution.py:527

commit v23 on v21

--- a/solution.py
+++ b/solution.py
@@ -596,10 +596,7 @@
         held_b = jnp.where(group == 0, piece_b, two)
         to_across = jnp.where((group == 0) | (group == 2), held_b, total_a)
         to_down = jnp.where(group <= 1, held_a, total_b)
-        if n < count - 1:
-            across, down = sent_both(to_across, to_down, SWAP_X, SWAP_Y)
-        else:
-            across, down = send(to_across, SWAP_X), send(to_down, SWAP_Y)
+        across, down = send(to_across, SWAP_X), send(to_down, SWAP_Y)
         branch_a = jnp.where(group <= 1, held_a, down)
         branch_b = jnp.where((group == 0) | (group == 2), held_b, across)
         totals = (

time: 37.9 us -> 42.5 us (1.12)
  waiting for transfers between devices: 8.47 us -> 11.7 us
  starting transfers between devices: 15.8 us -> 17.2 us
    ppermute x4 -> x6, starting transfers between devices: 6.25 us -> 10.9 us  [local(): send = lambda block, route: lax.ppermute(block, 'grp', route)]
    ppermute x6 -> x4, starting transfers between devices: 7.41 us -> 4.16 us  [mixed(): return lax.ppermute(block, ('grp', 'rep'), route)]
    ppermute x4 -> x6, waiting for transfers between devices: 5.75 us -> 8.65 us  [local(): send = lambda block, route: lax.ppermute(block, 'grp', route)]
    ppermute x6 -> x4, waiting for transfers between devices: 2.71 us -> 3.07 us  [mixed(): return lax.ppermute(block, ('grp', 'rep'), route)]
  transfers between devices with their start and end apart: 13 -> 13, of which waited for: 5 -> 4; matrix products, arithmetic and copies ran while one was open for 4% -> 3% of each run, Pallas kernels for 27% -> 24%
where the time goes in v23:
time: 42.5 us; the launch traced here: 42.3 us
  starting transfers between devices  17.2 us (40%)
  waiting for transfers between devices  11.7 us (28%)
  Pallas kernels  11.1 us (26%)
  other arithmetic  1.35 us (3%)
  between operations  0.87 us (2%)
    ppermute x6, starting transfers between devices, local(): send = lambda block, route: lax.ppermute(block, 'grp', route)  10.9 us
    ppermute x6, waiting for transfers between devices, local(): send = lambda block, route: lax.ppermute(block, 'grp', route)  8.65 us
    ppermute x4, starting transfers between devices, mixed(): return lax.ppermute(block, ('grp', 'rep'), route)  4.16 us
    ppermute x4, waiting for transfers between devices, mixed(): return lax.ppermute(block, ('grp', 'rep'), route)  3.07 us
    pallas_call x1, Pallas kernels, attend_edges(): pl.pallas_call(functools.partial(kernel, reach, lax.axis_size('seq')), in...  3.04 us
    pallas_call x2, Pallas kernels, relay_last(): pl.pallas_call(functools.partial(relay_last_kernel, part, chunks, first_r...  1.99 us
    pallas_call x1, Pallas kernels, attend_middle(): pl.pallas_call(functools.partial(middle_kernel, reach), in_specs=[VMEM] *...  1.61 us
    ppermute x2, starting transfers between devices, paired(): return lax.ppermute(block, ('seq', 'rep'), route)  1.58 us
  transfers between devices with their start and end apart: 13, of which 4 were waited for; matrix products, arithmetic and copies ran while one was open for 3% of the time, Pallas kernels for 24%

profile of v23, /device:TPU:0, one launch (start us, length us, event | category | flops | bytes accessed | tf_op | source)
XLA Modules:
  0.0 42.3 jit_solution(9049480643632152369)
XLA Ops:
  0.6 0.5 %collective-permute-start = (f32[1280]{0:T(1024)}, f32[1280]{0:T(1024)S(1)}, u32[]{:S(2)}, u32[]{:S(2)}) collective-permute-start(f32[1280]{0:T(1024)} %param.12), channel_id=1, source_target_pairs={{0,1},{1,0},{2,3},{3,2},{4,5},{5,4},{6,7},{7,6},{8,9},{9,8},{10,11... | collective-permute-start | bytes 15368 | tf_op jit(solution)/shard_map/ppermute | solution.py:503
  1.1 0.7 %and_select_fusion = (s32[1,128]{1,0:T(1,128)S(1)}, s32[1,128]{1,0:T(1,128)S(1)}) fusion(s32[1,1,128]{2,1,0:T(1,128)} %param.11, s32[1,1,128]{2,1,0:T(1,128)} %param.10), kind=kLoop, calls=%fused_computation.34 | loop fusion | flops 2816 | bytes 2048 | tf_op jit(solution)/shard_map/jit(remainder)/select_n | solution.py:544
  1.9 1.2 %pack_grads.1 = (bf16[128,1408]{1,0:T(8,128)(2,1)S(1)}, bf16[128,1408]{1,0:T(8,128)(2,1)S(1)}) custom-call(bf16[128,2560]{1,0:T(8,128)(2,1)} %bitcast.35, f32[2,128]{1,0:T(2,128)S(1)} %add_convert_fusion.4.mark_ref, bf16[128,2560]{1,0:T(8,128)(2,1)} %bitcast.31, bf16[128,2560]{1,0:T(8,128)(2,1)} %bitcast.23, bf16[128,2560]{1,0:T(8,128)(2,1)} %bitcast.27), custom_call_target="tpu_custom_call" | custom-call | bytes 1310720 | tf_op jit(solution)/shard_map/pack_grads/pallas_call | solution.py:332
  3.1 2.6 %collective-permute-start.1 = (bf16[128,1408]{1,0:T(8,128)(2,1)S(1)}, bf16[128,1408]{1,0:T(8,128)(2,1)}, u32[]{:S(2)}, u32[]{:S(2)}) collective-permute-start(bf16[128,1408]{1,0:T(8,128)(2,1)S(1)} %get-tuple-element.36.mine_ref), channel_id=1, source_target_pairs={{0,8},{8,0},{16,24},{24,16},{1,9},{9,1},{17,25},{25,17},{2,10},{10... | collective-permute-start | bytes 1081352 | tf_op jit(solution)/shard_map/ppermute | solution.py:540
  5.7 1.5 %collective-permute-start.2 = (bf16[128,1408]{1,0:T(8,128)(2,1)S(1)}, bf16[128,1408]{1,0:T(8,128)(2,1)S(1)}, u32[]{:S(2)}, u32[]{:S(2)}) collective-permute-start(bf16[128,1408]{1,0:T(8,128)(2,1)S(1)} %get-tuple-element.39.mine_ref), channel_id=1, source_target_pairs={{0,16},{16,0},{8,24},{24,8},{1,17},{17,1},{9,25},{25,9},{2,18},{18... | collective-permute-start | bytes 1081352 | tf_op jit(solution)/shard_map/ppermute | solution.py:540
  7.2 0.9 %pack_ends.1 = (bf16[32,5248]{1,0:T(8,128)(2,1)}, bf16[32,5248]{1,0:T(8,128)(2,1)}) custom-call(bf16[128,2560]{1,0:T(8,128)(2,1)S(1)} %bitcast.24, bf16[128,2560]{1,0:T(8,128)(2,1)S(1)} %bitcast.28, f32[1,128]{1,0:T(1,128)S(1)} %get-tuple-element.46.code_ref), custom_call_target="tpu_custom_call" | custom-call | bytes 1310720 | tf_op jit(solution)/shard_map/pack_ends/pallas_call | solution.py:260
  8.1 1.6 %collective-permute-start.7 = (bf16[32,5248]{1,0:T(8,128)(2,1)}, bf16[32,5248]{1,0:T(8,128)(2,1)}, u32[]{:S(2)}, u32[]{:S(2)}) collective-permute-start(bf16[32,5248]{1,0:T(8,128)(2,1)} %get-tuple-element.47), channel_id=1, source_target_pairs={{0,2},{1,3},{2,0},{3,1},{4,6},{5,7},{6,4},{7,5},{8,10},{9,11},{10,... | collective-permute-start | bytes 1007624 | tf_op jit(solution)/shard_map/ppermute | solution.py:35
  9.7 1.6 %attend_middle.1 = bf16[64,2560]{1,0:T(8,128)(2,1)S(1)} custom-call(bf16[128,2560]{1,0:T(8,128)(2,1)S(1)} %bitcast.32, bf16[128,2560]{1,0:T(8,128)(2,1)S(1)} %bitcast.25, bf16[128,2560]{1,0:T(8,128)(2,1)S(1)} %bitcast.29, f32[1,128]{1,0:T(1,128)S(1)} %get-tuple-element.46.code_ref), custom_call_target="tpu_custom_call" | custom-call | flops 268435456 | bytes 1966080 | tf_op jit(solution)/shard_map/attend_middle/pallas_call | solution.py:273
  11.4 3.4 %collective-permute-done.1.theirs_ref = bf16[128,1408]{1,0:T(8,128)(2,1)} collective-permute-done((bf16[128,1408]{1,0:T(8,128)(2,1)S(1)}, bf16[128,1408]{1,0:T(8,128)(2,1)}, u32[]{:S(2)}, u32[]{:S(2)}) %collective-permute-start.1) | collective-permute-done | bytes 360480 | tf_op jit(solution)/shard_map/ppermute | solution.py:540
  14.8 1.3 %pair_sums.2 = (bf16[64,1280]{1,0:T(8,128)(2,1)S(1)}, bf16[64,1280]{1,0:T(8,128)(2,1)S(1)}) custom-call(f32[1,2560]{1,0:T(1,128)S(1)} %broadcast_in_dim.9.gate_ref, f32[1,128]{1,0:T(1,128)S(1)} %get-tuple-element.87.row_ref, bf16[128,1408]{1,0:T(8,128)(2,1)S(1)} %get-tuple-element.36.mine_ref, bf16[128,1408]{1,0:T(8,128)(2,1)} %collective-permute-done.1.theirs_ref), custom_call_target="tpu_custom_call" | custom-call | flops 83886080 | bytes 983040 | tf_op jit(solution)/shard_map/pair_sums/pallas_call | solution.py:371
  16.6 1.8 %collective-permute-start.3 = (bf16[64,1280]{1,0:T(8,128)(2,1)S(1)}, bf16[64,1280]{1,0:T(8,128)(2,1)S(1)}, u32[]{:S(2)}, u32[]{:S(2)}) collective-permute-start(bf16[64,1280]{1,0:T(8,128)(2,1)S(1)} %get-tuple-element.80), channel_id=1, source_target_pairs={{0,16},{16,24},{24,8},{8,0},{1,9},{9,25},{25,17},{17,1},{2,18},{18... | collective-permute-start | bytes 491528 | tf_op jit(solution)/shard_map/ppermute | solution.py:521
  18.4 0.3 collective-permute-start.4
  18.7 3.0 %attend_edges.1 = bf16[64,2560]{1,0:T(8,128)(2,1)S(1)} custom-call(bf16[128,2560]{1,0:T(8,128)(2,1)S(1)} %bitcast.33, bf16[128,2560]{1,0:T(8,128)(2,1)S(1)} %bitcast.26, bf16[128,2560]{1,0:T(8,128)(2,1)S(1)} %bitcast.30, f32[1,128]{1,0:T(1,128)S(1)} %get-tuple-element.46.code_ref, bf16[32,5248]{1,0:T(8,128)(2,1)} %collective-permute-done.7.one_ref, ...), custom_call_target="tpu_custom_call" | custom-call | flops 268435456 | bytes 1966080 | tf_op jit(solution)/shard_map/attend_edges/pallas_call | solution.py:294
  21.8 1.8 %collective-permute-start.9 = (bf16[64,1280]{1,0:T(8,128)(2,1)S(1)}, bf16[64,1280]{1,0:T(8,128)(2,1)S(1)}, u32[]{:S(2)}, u32[]{:S(2)}) collective-permute-start(bf16[64,1280]{1,0:T(8,128)(2,1)S(1)} %broadcast_select_fusion.7), channel_id=1, source_target_pairs={{0,16},{16,24},{24,8},{8,0},{1,9},{9,25},{25,17},{17,1},{2,18},{18... | collective-permute-start | bytes 491528 | tf_op jit(solution)/shard_map/ppermute | solution.py:521
  23.6 0.3 collective-permute-start.10
  24.1 1.8 %collective-permute-start.6 = (bf16[64,1280]{1,0:T(8,128)(2,1)S(1)}, bf16[64,1280]{1,0:T(8,128)(2,1)S(1)}, u32[]{:S(2)}, u32[]{:S(2)}) collective-permute-start(bf16[64,1280]{1,0:T(8,128)(2,1)S(1)} %get-tuple-element.69), channel_id=1, source_target_pairs={{0,8},{8,0},{16,24},{24,16},{1,9},{9,1},{17,25},{25,17},{2,10},{10... | collective-permute-start | bytes 491528 | tf_op jit(solution)/shard_map/ppermute | solution.py:540
  25.9 3.0 %collective-permute-done.9 = bf16[64,1280]{1,0:T(8,128)(2,1)S(1)} collective-permute-done((bf16[64,1280]{1,0:T(8,128)(2,1)S(1)}, bf16[64,1280]{1,0:T(8,128)(2,1)S(1)}, u32[]{:S(2)}, u32[]{:S(2)}) %collective-permute-start.9) | collective-permute-done | bytes 163872 | tf_op jit(solution)/shard_map/ppermute | solution.py:521
  29.0 1.4 %collective-permute-start.12 = (bf16[64,1280]{1,0:T(8,128)(2,1)S(1)}, bf16[64,1280]{1,0:T(8,128)(2,1)S(1)}, u32[]{:S(2)}, u32[]{:S(2)}) collective-permute-start(bf16[64,1280]{1,0:T(8,128)(2,1)S(1)} %get-tuple-element.58), channel_id=1, source_target_pairs={{0,8},{8,0},{16,24},{24,16},{1,9},{9,1},{17,25},{25,17},{2,10},{10... | collective-permute-start | bytes 491528 | tf_op jit(solution)/shard_map/ppermute | solution.py:540
  30.6 2.0 %collective-permute-start.11 = (bf16[64,1280]{1,0:T(8,128)(2,1)S(1)}, bf16[64,1280]{1,0:T(8,128)(2,1)S(1)}, u32[]{:S(2)}, u32[]{:S(2)}) collective-permute-start(bf16[64,1280]{1,0:T(8,128)(2,1)S(1)} %get-tuple-element.63), channel_id=1, source_target_pairs={{0,16},{16,0},{8,24},{24,8},{1,17},{17,1},{9,25},{25,9},{2,18},{18... | collective-permute-start | bytes 491528 | tf_op jit(solution)/shard_map/ppermute | solution.py:540
  32.7 1.6 %collective-permute-start.5 = (bf16[64,1280]{1,0:T(8,128)(2,1)S(1)}, bf16[64,1280]{1,0:T(8,128)(2,1)S(1)}, u32[]{:S(2)}, u32[]{:S(2)}) collective-permute-start(bf16[64,1280]{1,0:T(8,128)(2,1)S(1)} %get-tuple-element.73), channel_id=1, source_target_pairs={{0,16},{16,0},{8,24},{24,8},{1,17},{17,1},{9,25},{25,9},{2,18},{18... | collective-permute-start | bytes 491528 | tf_op jit(solution)/shard_map/ppermute | solution.py:540
  34.3 5.2 %collective-permute-done.5 = bf16[64,1280]{1,0:T(8,128)(2,1)S(1)} collective-permute-done((bf16[64,1280]{1,0:T(8,128)(2,1)S(1)}, bf16[64,1280]{1,0:T(8,128)(2,1)S(1)}, u32[]{:S(2)}, u32[]{:S(2)}) %collective-permute-start.5) | collective-permute-done | bytes 163872 | tf_op jit(solution)/shard_map/ppermute | solution.py:540
  39.5 0.8 %relay_first.1 = (bf16[128,2560]{1,0:T(8,128)(2,1)}, f32[128,2560]{1,0:T(8,128)S(1)}, bf16[128,64]{1,0:T(8,128)(2,1)S(1)}) custom-call(f32[1,128]{1,0:T(1,128)S(1)} %get-tuple-element.87.row_ref, f32[1,2560]{1,0:T(1,128)S(1)} %broadcast_in_dim.9.gate_ref, bf16[64,1280]{1,0:T(8,128)(2,1)S(1)} %get-tuple-element.83.a_ref, ...), custom_call_target="tpu_custom_call" | custom-call | flops 83886080 | bytes 7864320 | tf_op jit(solution)/shard_map/relay_first/pallas_call | solution.py:419
  40.3 1.0 %relay_last.2 = (bf16[128,2560]{1,0:T(8,128)(2,1)}, bf16[128,2560]{1,0:T(8,128)(2,1)}) custom-call(bf16[128,64]{1,0:T(8,128)(2,1)S(1)} %get-tuple-element.49.picks_ref, f32[1,2560]{1,0:T(1,128)S(1)} %broadcast_in_dim.9.gate_ref, bf16[64,1280]{1,0:T(8,128)(2,1)S(1)} %get-tuple-element.60.held_ref, ...), custom_call_target="tpu_custom_call", output_to_operand_aliasing={{0}: (6, {})} | custom-call | flops 41943040 | bytes 1966080 | tf_op jit(solution)/shard_map/relay_last/pallas_call | solution.py:479
  41.3 1.0 %relay_last.3 = (bf16[128,2560]{1,0:T(8,128)(2,1)}, bf16[128,2560]{1,0:T(8,128)(2,1)}) custom-call(bf16[128,64]{1,0:T(8,128)(2,1)S(1)} %get-tuple-element.49.picks_ref, f32[1,2560]{1,0:T(1,128)S(1)} %broadcast_in_dim.9.gate_ref, bf16[64,1280]{1,0:T(8,128)(2,1)S(1)} %get-tuple-element.65.held_ref, ...), custom_call_target="tpu_custom_call", output_to_operand_aliasing={{0}: (6, {}), {1}: (7, {})} | custom-call | flops 41943040 | bytes 1966080 | tf_op jit(solution)/shard_map/relay_last/pallas_call | solution.py:479
  (37 shorter events, 1.2 us)
Async XLA Ops:
  0.6 10.7 %collective-permute-start = (f32[1280]{0:T(1024)}, f32[1280]{0:T(1024)S(1)}, u32[]{:S(2)}, u32[]{:S(2)}) collective-permute-start(f32[1280]{0:T(1024)} %param.12), channel_id=1, source_target_pairs={{0,1},{1,0},{2,3},{3,2},{4,5},{5,4},{6,7},{7,6},{8,9},{9,8},{10,11... | collective-permute-start | bytes 15368 | tf_op jit(solution)/shard_map/ppermute | solution.py:503
  1.9 5.3 %copy-start = (bf16[1,1,128,2560]{3,2,1,0:T(8,128)(2,1)S(1)}, bf16[1,1,128,2560]{3,2,1,0:T(8,128)(2,1)}, u32[]{:S(2)}) copy-start(bf16[1,1,128,2560]{3,2,1,0:T(8,128)(2,1)} %param.8) | copy-start | bytes 1966084
  1.9 5.3 %copy-start.1 = (bf16[1,1,128,2560]{3,2,1,0:T(8,128)(2,1)S(1)}, bf16[1,1,128,2560]{3,2,1,0:T(8,128)(2,1)}, u32[]{:S(2)}) copy-start(bf16[1,1,128,2560]{3,2,1,0:T(8,128)(2,1)} %param.9) | copy-start | bytes 1966084
  3.1 6.6 %copy-start.2 = (bf16[1,1,128,2560]{3,2,1,0:T(8,128)(2,1)S(1)}, bf16[1,1,128,2560]{3,2,1,0:T(8,128)(2,1)}, u32[]{:S(2)}) copy-start(bf16[1,1,128,2560]{3,2,1,0:T(8,128)(2,1)} %param.7) | copy-start | bytes 1966084
  3.1 11.7 %collective-permute-start.1 = (bf16[128,1408]{1,0:T(8,128)(2,1)S(1)}, bf16[128,1408]{1,0:T(8,128)(2,1)}, u32[]{:S(2)}, u32[]{:S(2)}) collective-permute-start(bf16[128,1408]{1,0:T(8,128)(2,1)S(1)} %get-tuple-element.36.mine_ref), channel_id=1, source_target_pairs={{0,8},{8,0},{16,24},{24,16},{1,9},{9,1},{17,25},{25,17},{2,10},{10... | collective-permute-start | bytes 1081352 | tf_op jit(solution)/shard_map/ppermute | solution.py:540
  5.7 10.5 %collective-permute-start.2 = (bf16[128,1408]{1,0:T(8,128)(2,1)S(1)}, bf16[128,1408]{1,0:T(8,128)(2,1)S(1)}, u32[]{:S(2)}, u32[]{:S(2)}) collective-permute-start(bf16[128,1408]{1,0:T(8,128)(2,1)S(1)} %get-tuple-element.39.mine_ref), channel_id=1, source_target_pairs={{0,16},{16,0},{8,24},{24,8},{1,17},{17,1},{9,25},{25,9},{2,18},{18... | collective-permute-start | bytes 1081352 | tf_op jit(solution)/shard_map/ppermute | solution.py:540
  8.1 3.2 %copy-start.3 = (f32[1280]{0:T(1024)S(1)}, f32[1280]{0:T(1024)}, u32[]{:S(2)}) copy-start(f32[1280]{0:T(1024)} %param.12) | copy-start | bytes 15364
  8.1 10.5 %collective-permute-start.7 = (bf16[32,5248]{1,0:T(8,128)(2,1)}, bf16[32,5248]{1,0:T(8,128)(2,1)}, u32[]{:S(2)}, u32[]{:S(2)}) collective-permute-start(bf16[32,5248]{1,0:T(8,128)(2,1)} %get-tuple-element.47), channel_id=1, source_target_pairs={{0,2},{1,3},{2,0},{3,1},{4,6},{5,7},{6,4},{7,5},{8,10},{9,11},{10,... | collective-permute-start | bytes 1007624 | tf_op jit(solution)/shard_map/ppermute | solution.py:35
  9.7 9.0 %collective-permute-start.8 = (bf16[32,5248]{1,0:T(8,128)(2,1)}, bf16[32,5248]{1,0:T(8,128)(2,1)}, u32[]{:S(2)}, u32[]{:S(2)}) collective-permute-start(bf16[32,5248]{1,0:T(8,128)(2,1)} %get-tuple-element.48), channel_id=1, source_target_pairs={{0,1},{1,0},{2,4},{3,5},{4,2},{5,3},{6,7},{7,6},{8,9},{9,8},{10,12... | collective-permute-start | bytes 1007624 | tf_op jit(solution)/shard_map/ppermute | solution.py:35
  16.6 7.4 %collective-permute-start.3 = (bf16[64,1280]{1,0:T(8,128)(2,1)S(1)}, bf16[64,1280]{1,0:T(8,128)(2,1)S(1)}, u32[]{:S(2)}, u32[]{:S(2)}) collective-permute-start(bf16[64,1280]{1,0:T(8,128)(2,1)S(1)} %get-tuple-element.80), channel_id=1, source_target_pairs={{0,16},{16,24},{24,8},{8,0},{1,9},{9,25},{25,17},{17,1},{2,18},{18... | collective-permute-start | bytes 491528 | tf_op jit(solution)/shard_map/ppermute | solution.py:521
  18.4 5.6 %collective-permute-start.4 = (bf16[64,1280]{1,0:T(8,128)(2,1)S(1)}, bf16[64,1280]{1,0:T(8,128)(2,1)S(1)}, u32[]{:S(2)}, u32[]{:S(2)}) collective-permute-start(bf16[64,1280]{1,0:T(8,128)(2,1)S(1)} %get-tuple-element.81), channel_id=1, source_target_pairs={{0,8},{8,24},{24,16},{16,0},{1,17},{17,25},{25,9},{9,1},{2,10},{10... | collective-permute-start | bytes 491528 | tf_op jit(solution)/shard_map/ppermute | solution.py:521
  21.8 7.0 %collective-permute-start.9 = (bf16[64,1280]{1,0:T(8,128)(2,1)S(1)}, bf16[64,1280]{1,0:T(8,128)(2,1)S(1)}, u32[]{:S(2)}, u32[]{:S(2)}) collective-permute-start(bf16[64,1280]{1,0:T(8,128)(2,1)S(1)} %broadcast_select_fusion.7), channel_id=1, source_target_pairs={{0,16},{16,24},{24,8},{8,0},{1,9},{9,25},{25,17},{17,1},{2,18},{18... | collective-permute-start | bytes 491528 | tf_op jit(solution)/shard_map/ppermute | solution.py:521
  23.6 5.3 %collective-permute-start.10 = (bf16[64,1280]{1,0:T(8,128)(2,1)S(1)}, bf16[64,1280]{1,0:T(8,128)(2,1)S(1)}, u32[]{:S(2)}, u32[]{:S(2)}) collective-permute-start(bf16[64,1280]{1,0:T(8,128)(2,1)S(1)} %get-tuple-element.66), channel_id=1, source_target_pairs={{0,8},{8,24},{24,16},{16,0},{1,17},{17,25},{25,9},{9,1},{2,10},{10... | collective-permute-start | bytes 491528 | tf_op jit(solution)/shard_map/ppermute | solution.py:521
  24.1 8.5 %collective-permute-start.6 = (bf16[64,1280]{1,0:T(8,128)(2,1)S(1)}, bf16[64,1280]{1,0:T(8,128)(2,1)S(1)}, u32[]{:S(2)}, u32[]{:S(2)}) collective-permute-start(bf16[64,1280]{1,0:T(8,128)(2,1)S(1)} %get-tuple-element.69), channel_id=1, source_target_pairs={{0,8},{8,0},{16,24},{24,16},{1,9},{9,1},{17,25},{25,17},{2,10},{10... | collective-permute-start | bytes 491528 | tf_op jit(solution)/shard_map/ppermute | solution.py:540
  29.0 11.3 %collective-permute-start.12 = (bf16[64,1280]{1,0:T(8,128)(2,1)S(1)}, bf16[64,1280]{1,0:T(8,128)(2,1)S(1)}, u32[]{:S(2)}, u32[]{:S(2)}) collective-permute-start(bf16[64,1280]{1,0:T(8,128)(2,1)S(1)} %get-tuple-element.58), channel_id=1, source_target_pairs={{0,8},{8,0},{16,24},{24,16},{1,9},{9,1},{17,25},{25,17},{2,10},{10... | collective-permute-start | bytes 491528 | tf_op jit(solution)/shard_map/ppermute | solution.py:540
  30.6 10.7 %collective-permute-start.11 = (bf16[64,1280]{1,0:T(8,128)(2,1)S(1)}, bf16[64,1280]{1,0:T(8,128)(2,1)S(1)}, u32[]{:S(2)}, u32[]{:S(2)}) collective-permute-start(bf16[64,1280]{1,0:T(8,128)(2,1)S(1)} %get-tuple-element.63), channel_id=1, source_target_pairs={{0,16},{16,0},{8,24},{24,8},{1,17},{17,1},{9,25},{25,9},{2,18},{18... | collective-permute-start | bytes 491528 | tf_op jit(solution)/shard_map/ppermute | solution.py:540
  32.7 6.8 %collective-permute-start.5 = (bf16[64,1280]{1,0:T(8,128)(2,1)S(1)}, bf16[64,1280]{1,0:T(8,128)(2,1)S(1)}, u32[]{:S(2)}, u32[]{:S(2)}) collective-permute-start(bf16[64,1280]{1,0:T(8,128)(2,1)S(1)} %get-tuple-element.73), channel_id=1, source_target_pairs={{0,16},{16,0},{8,24},{24,8},{1,17},{17,1},{9,25},{25,9},{2,18},{18... | collective-permute-start | bytes 491528 | tf_op jit(solution)/shard_map/ppermute | solution.py:540
